TPU v7x, 32 devices: a whole 2x2x4 slice. The times are simulated.
32 devices in a mesh: groups: 2 (over x), ctx: 16 (over z, y, core).
Axes of the slice: x: 2, y: 2, z: 4, core: 2. Of those that a mesh axis runs over, the one named last changes fastest.
Arguments:
- tokens: bfloat16 [16384, 8192], P(('groups', 'ctx')), parts along dimension 0, may hold values from -6 to 6
- key_down: bfloat16 [8192, 512], P('ctx'), may hold values from -0.0625 to 0.0625
- value_down: bfloat16 [8192, 512], P('ctx'), may hold values from -0.0625 to 0.0625
- key_up: bfloat16 [512, 1024], replicated, may hold values from -0.25 to 0.25
- value_up: bfloat16 [512, 1024], replicated, may hold values from -0.25 to 0.25
- prompt_lens: int32 [8], P('groups'), parts along dimension 0, may hold values from 1 to 4096, 8192 in all
- queries: bfloat16 [4, 8, 8192], P(None, 'groups'), parts along dimension 1, may hold values from -136 to 136
- new_latent: bfloat16 [4, 8, 1024], P(None, 'groups'), parts along dimension 1, may hold values from -6 to 6
Outputs:
- attention: bfloat16 [4, 8, 8192], P(None, 'groups'), parts along dimension 1
There are 2 independent parts, one for each index of `groups`. A program takes and returns all parts, laid end to end along the dimension named above; an argument that names none is the same for every part. Nothing has to cross between parts.
All inputs are finite; a program needn't handle non-finite values.
Results may differ from a plain program's by a relative error of at most 0.015.
The roundings to bfloat16 on the way count: a program that leaves them out, or rounds other values in their place, can miss the bound.
Values may be sent and summed in bfloat16 or wider, within the bound.
No kernel may reach another device: no remote copies, remote signals or barrier semaphores. Data moves between devices by JAX's collectives and lax.ppermute only.
A program may use at most 192 MiB of HBM per device.

v0:
```python
import jax
import jax.numpy as jnp
from jax import lax
from jax.sharding import PartitionSpec as P

QH = 64
KVH = 8
DH = 128


def merged(x, axis, combine):
    everything = jax.tree.map(lambda part: lax.all_gather(part, axis), x)
    first = jax.tree.map(lambda part: part[0], everything)

    def hop(k, so_far):
        return combine(so_far, jax.tree.map(lambda part: part[k], everything))

    return lax.fori_loop(1, lax.axis_size(axis), hop, first)


def merge_parts(first, second):
    top = jnp.maximum(first[0], second[0])
    scale_one = jnp.exp(first[0] - top)
    scale_two = jnp.exp(second[0] - top)
    total = first[1] * scale_one + second[1] * scale_two
    summed = first[2] * scale_one[..., None] + second[2] * scale_two[..., None]
    return (top, total, summed)


def on_device(tokens, key_down, value_down, key_up, value_up, prompt_lens, queries, new_latent):
    n_ctx = lax.axis_size("ctx")
    device = lax.axis_index("ctx")
    tok_rows = tokens.shape[0]
    piece = tok_rows // n_ctx
    lat_width = key_down.shape[1]
    group = QH // KVH
    scale = 1.0 / DH**0.5

    def add_rows(rows_piece):
        return jnp.dot(tokens, rows_piece, preferred_element_type=jnp.float32)

    key_sum = add_rows(lax.all_gather(key_down, "ctx", axis=0, tiled=True))
    value_sum = add_rows(lax.all_gather(value_down, "ctx", axis=0, tiled=True))
    key_latent = key_sum.astype(jnp.bfloat16)
    value_latent = value_sum.astype(jnp.bfloat16)
    moved_position = (
        jnp.arange(n_ctx, dtype=jnp.int32)[:, None] * tok_rows
        + device * piece
        + jnp.arange(piece, dtype=jnp.int32)[None, :]
    ).reshape(-1)
    sending = jnp.concatenate([key_latent, value_latent], 1).reshape(n_ctx, piece, 2 * lat_width)
    arrived = lax.all_to_all(sending, "ctx", split_axis=0, concat_axis=0, tiled=True).reshape(
        n_ctx * piece, 2 * lat_width
    )
    keys = jnp.dot(arrived[:, :lat_width], key_up, preferred_element_type=jnp.float32).astype(
        jnp.bfloat16
    )
    values = jnp.dot(arrived[:, lat_width:], value_up, preferred_element_type=jnp.float32).astype(
        jnp.bfloat16
    )
    offsets = jnp.cumsum(prompt_lens) - prompt_lens
    member = (moved_position[None, :] >= offsets[:, None]) & (
        moved_position[None, :] < (offsets + prompt_lens)[:, None]
    )
    steps_count, req_count = (queries.shape[0], queries.shape[1])
    query = queries.reshape(steps_count, req_count, KVH, group, DH)
    key_heads = keys.reshape(-1, KVH, DH)
    value_heads = values.reshape(-1, KVH, DH)
    scores = (
        jnp.einsum("srgjd,tgd->srgjt", query, key_heads, preferred_element_type=jnp.float32) * scale
    )
    visible = member[None, :, None, None, :]
    scores = jnp.where(visible, scores, -1e30)
    top = jnp.max(scores, -1)
    weights = jnp.where(visible, jnp.exp(scores - top[..., None]), 0.0)
    total = jnp.sum(weights, -1)
    summed = jnp.einsum(
        "srgjt,tgd->srgjd",
        weights.astype(jnp.bfloat16),
        value_heads,
        preferred_element_type=jnp.float32,
    )
    top, total, summed = merged((top, total, summed), "ctx", merge_parts)
    flat_new = new_latent.reshape(steps_count * req_count, 2 * lat_width)
    new_keys = (
        jnp.dot(flat_new[:, :lat_width], key_up, preferred_element_type=jnp.float32)
        .astype(jnp.bfloat16)
        .reshape(steps_count, req_count, KVH, DH)
    )
    new_values = (
        jnp.dot(flat_new[:, lat_width:], value_up, preferred_element_type=jnp.float32)
        .astype(jnp.bfloat16)
        .reshape(steps_count, req_count, KVH, DH)
    )
    causal = (jnp.arange(steps_count)[:, None] >= jnp.arange(steps_count)[None, :])[
        :, None, None, None, :
    ]
    fresh = (
        jnp.einsum("srgjd,urgd->srgju", query, new_keys, preferred_element_type=jnp.float32) * scale
    )
    fresh = jnp.where(causal, fresh, -1e30)
    overall = jnp.maximum(top, jnp.max(fresh, -1))
    carried = jnp.exp(top - overall)
    fresh_weights = jnp.where(causal, jnp.exp(fresh - overall[..., None]), 0.0)
    total = total * carried + jnp.sum(fresh_weights, -1)
    summed = summed * carried[..., None] + jnp.einsum(
        "srgju,urgd->srgjd",
        fresh_weights.astype(jnp.bfloat16),
        new_values,
        preferred_element_type=jnp.float32,
    )
    result = summed / total[..., None]
    return result.reshape(steps_count, req_count, QH * DH).astype(jnp.bfloat16)


def solution(mesh):
    return jax.shard_map(
        on_device,
        mesh=mesh,
        in_specs=(
            P(("groups", "ctx"), None),
            P("ctx", None),
            P("ctx", None),
            P(),
            P(),
            P("groups"),
            P(None, "groups", None),
            P(None, "groups", None),
        ),
        out_specs=P(None, "groups", None),
        check_vma=False,
    )
```

profile of v0, /device:TPU:0, one launch (start us, length us, event | category | flops | bytes accessed | tf_op | source)
XLA Modules:
  0.0 339.6 jit_solution(9440178313860140618)
XLA Ops:
  6.5 0.7 all-gather.9.cloned.1.call-update
  7.3 0.7 all-gather.7.cloned.1.call-update
  8.0 79.1 %all-gather.9.cloned.1.call-done = bf16[8192,512]{1,0:T(8,128)(2,1)} async-done(((bf16[512,512]{1,0:T(8,128)(2,1)}), bf16[8192,512]{1,0:T(8,128)(2,1)}) %all-gather.9.cloned.1.call-update) | async-done | bytes 8388624 | tf_op jit(solution)/shard_map/all_gather | solution.py:43
  87.2 10.3 %convolution_convert_fusion.2 = bf16[512,512]{0,1:T(8,128)(2,1)S(1)} fusion(bf16[512,8192]{1,0:T(8,128)(2,1)} %param.10, bf16[8192,512]{1,0:T(8,128)(2,1)} %all-gather.9.cloned.1.call-done), kind=kOutput, calls=%fused_computation.19 | convolution fusion | flops 4295229440 | bytes 17301504 | tf_op jit(solution)/shard_map/dot_general | solution.py:40
  97.5 65.0 %all-gather.7.cloned.1.call-done = bf16[8192,512]{1,0:T(8,128)(2,1)} async-done(((bf16[512,512]{1,0:T(8,128)(2,1)}), bf16[8192,512]{1,0:T(8,128)(2,1)}) %all-gather.7.cloned.1.call-update) | async-done | bytes 8388624 | tf_op jit(solution)/shard_map/all_gather | solution.py:42
  162.5 10.3 %convolution_convert_fusion.3 = bf16[512,512]{0,1:T(8,128)(2,1)S(1)} fusion(bf16[512,8192]{1,0:T(8,128)(2,1)} %param.10, bf16[8192,512]{1,0:T(8,128)(2,1)} %all-gather.7.cloned.1.call-done), kind=kOutput, calls=%fused_computation.20 | convolution fusion | flops 4295229440 | bytes 17301504 | tf_op jit(solution)/shard_map/dot_general | solution.py:40
  172.9 1.3 copy.37
  174.2 3.7 %all-to-all-start = ((bf16[16,32,1024]{2,1,0:T(8,128)(2,1)}), bf16[16,32,1024]{2,1,0:T(8,128)(2,1)S(1)}, u32[]{:S(2)}, u32[]{:S(2)}) async-start(bf16[16,32,1024]{2,1,0:T(8,128)(2,1)} %bitcast.5), calls=%async_computation | async-start | bytes 2097152 | tf_op jit(solution)/shard_map/all_to_all | solution.py:52
  177.9 0.2 all-gather.11.cloned.1.call-start
  178.3 1.0 reshape.145
  179.3 0.2 reduce-window.8
  179.5 21.2 %all-to-all-done = bf16[16,32,1024]{2,1,0:T(8,128)(2,1)S(1)} async-done(((bf16[16,32,1024]{2,1,0:T(8,128)(2,1)}), bf16[16,32,1024]{2,1,0:T(8,128)(2,1)S(1)}, u32[]{:S(2)}, u32[]{:S(2)}) %all-to-all-start) | async-done | bytes 1048608 | tf_op jit(solution)/shard_map/all_to_all | solution.py:52
  200.8 0.7 fusion.7
  201.5 0.3 copy.66
  201.8 0.2 copy-done.2
  202.0 0.7 fusion.8
  202.7 0.3 copy.67
  203.0 0.6 fusion.4
  203.6 1.5 convolution_bitcast_fusion.1
  205.2 0.3 fusion.14
  205.5 1.5 fusion.15
  206.9 0.6 copy.69
  207.6 2.2 fusion.45
  209.8 0.7 fusion.6
  210.6 31.1 %all-gather.1 = f32[64,4,8,8]{3,2,1,0:T(8,128)S(1)} all-gather(f32[4,4,8,8]{3,2,1,0:T(8,128)S(1)} %copy.41), channel_id=3, replica_groups=mesh['groups'=2,'ctx'=16] {'ctx'}, dimensions={0}, use_global_device_ids=true | all-gather | bytes 69632 | tf_op jit(solution)/shard_map/all_gather | solution.py:12
  241.7 25.5 %all-gather = f32[64,4,8,8]{3,2,1,0:T(8,128)S(1)} all-gather(f32[4,4,8,8]{3,2,1,0:T(8,128)S(1)} %copy.40), channel_id=2, replica_groups=mesh['groups'=2,'ctx'=16] {'ctx'}, dimensions={0}, use_global_device_ids=true | all-gather | bytes 69632 | tf_op jit(solution)/shard_map/all_gather | solution.py:12
  267.3 1.1 copy-done.1
  268.3 26.0 %all-gather.11.cloned.1.call-done = f32[64,4,8,8,128]{4,3,1,0,2:T(8,128)} async-done(((f32[4,4,8,8,128]{4,3,1,0,2:T(8,128)}), f32[64,4,8,8,128]{4,3,1,0,2:T(8,128)}) %all-gather.11.cloned.1.call-update) | async-done | bytes 8388624 | tf_op jit(solution)/shard_map/all_gather | solution.py:12
  294.3 1.1 slice.35
  295.5 35.7 %while.19 = (s32[]{:T(128)}, f32[4,4,8,8]{3,2,1,0:T(8,128)S(1)}, f32[4,4,8,8]{3,2,1,0:T(8,128)S(1)}, f32[4,4,8,8,128]{4,3,2,1,0:T(8,128)S(1)}, f32[16,4,4,8,8]{4...) while((s32[]{:T(128)}, f32[4,4,8,8]{3,2,1,0:T(8,128)S(1)}, ...), condition=%wide.region_4.5_spmd, body=%wide.region_3.4_spmd.sunk | while | flops 399365 | bytes 1613975 | solution.py:18
  295.5 0.9 fusion.56
  296.4 1.4 fusion.57
  297.9 0.9 fusion.56
  298.8 1.4 fusion.57
  300.3 0.9 fusion.56
  301.2 1.4 fusion.57
  302.6 0.9 fusion.56
  303.6 1.4 fusion.57
  305.0 0.9 fusion.56
  305.9 1.4 fusion.57
  307.4 0.9 fusion.56
  308.3 1.4 fusion.57
  309.8 0.9 fusion.56
  310.7 1.4 fusion.57
  312.2 0.9 fusion.56
  313.1 1.4 fusion.57
  314.6 0.9 fusion.56
  315.5 1.4 fusion.57
  316.9 0.9 fusion.56
  317.9 1.4 fusion.57
  319.3 0.9 fusion.56
  320.2 1.4 fusion.57
  321.7 0.9 fusion.56
  322.6 1.4 fusion.57
  324.1 0.9 fusion.56
  325.0 1.4 fusion.57
  326.5 0.9 fusion.56
  327.4 1.4 fusion.57
  328.9 0.9 fusion.56
  329.8 1.4 fusion.57
  331.3 0.3 fusion.29
  331.6 0.1 fusion.35
  331.7 0.6 fusion.11
  332.3 0.8 convert_element_type.39
  (33 shorter events, 0.6 us)
Async XLA Ops:
  6.5 194.2 %copy-start = (bf16[512,1024]{1,0:T(8,128)(2,1)S(1)}, bf16[512,1024]{1,0:T(8,128)(2,1)}, u32[]{:S(2)}) copy-start(bf16[512,1024]{1,0:T(8,128)(2,1)} %param.13) | copy-start | bytes 3145732
  6.5 80.6 %all-gather.9.cloned.1.call-start = ((), (), s32[]{:S(2)}) async-start(), calls=%async_computation.2 | async-start | bytes 8912896 | tf_op jit(solution)/shard_map/all_gather | solution.py:43
  7.3 155.2 %all-gather.7.cloned.1.call-start = ((), (), s32[]{:S(2)}) async-start(), calls=%async_computation.1 | async-start | bytes 8912896 | tf_op jit(solution)/shard_map/all_gather | solution.py:42
  172.9 5.4 %copy-start.3 = (bf16[4,4,8192]{2,1,0:T(4,128)(2,1)S(1)}, bf16[4,4,8192]{2,1,0:T(4,128)(2,1)}, u32[]{:S(2)}) copy-start(bf16[4,4,8192]{2,1,0:T(4,128)(2,1)} %param.16) | copy-start | bytes 786436
  172.9 6.4 %copy-start.7 = (s32[4]{0:T(128)S(1)}, s32[4]{0:T(128)}, u32[]{:S(2)}) copy-start(s32[4]{0:T(128)} %param.15) | copy-start | bytes 52
  174.2 26.6 %all-to-all-start = ((bf16[16,32,1024]{2,1,0:T(8,128)(2,1)}), bf16[16,32,1024]{2,1,0:T(8,128)(2,1)S(1)}, u32[]{:S(2)}, u32[]{:S(2)}) async-start(bf16[16,32,1024]{2,1,0:T(8,128)(2,1)} %bitcast.5), calls=%async_computation | async-start | bytes 2097152 | tf_op jit(solution)/shard_map/all_to_all | solution.py:52
  177.9 116.5 %all-gather.11.cloned.1.call-start = ((), (), s32[]{:S(2)}) async-start(), calls=%async_computation.3 | async-start | bytes 8912896 | tf_op jit(solution)/shard_map/all_gather | solution.py:12
  200.8 1.2 copy-start.2
  202.0 1.0 copy-start.4
  203.6 1.5 copy-start.5
  267.3 1.1 copy-start.1
  295.5 36.2 %copy-start.6 = (bf16[2,8,8,128]{3,2,1,0:T(8,128)(2,1)S(1)}, bf16[2,8,8,128]{3,2,1,0:T(8,128)(2,1)}, u32[]{:S(2)}) copy-start(bf16[2,8,8,128]{3,2,1,0:T(8,128)(2,1)} %copy.69) | copy-start | bytes 98308
Sparse Core Ops, SparseCore 0:
  9.5 77.5 all-gather.8
  89.3 73.1 all-gather.6
  205.3 89.0 all-gather.10
where the time goes:
time: 341 us; the launch traced here: 340 us
  waiting for transfers between devices  193 us (57%)
  blocking collectives  56.7 us (17%)
  other arithmetic  36.9 us (11%)
  matrix products  28.7 us (8%)
  between operations  13.3 us (4%)
  local copies, waits for them, and re-layouts  6.89 us (2%)
  starting transfers between devices  3.92 us (1%)
    all_gather x1, waiting for transfers between devices, on_device(): value_sum = add_rows(lax.all_gather(value_down, 'ctx', axis=0, tiled=True))  79.1 us
    all_gather x1, waiting for transfers between devices, on_device(): key_sum = add_rows(lax.all_gather(key_down, 'ctx', axis=0, tiled=True))  65 us
    all_gather x2, blocking collectives, merged(): everything = jax.tree.map(lambda part: lax.all_gather(part, axis), x)  56.7 us
    all_gather x1, waiting for transfers between devices, merged(): everything = jax.tree.map(lambda part: lax.all_gather(part, axis), x)  26 us
    add x15, other arithmetic, merge_parts(): summed = first[2] * scale_one[..., None] + second[2] * scale_two[..., None]  21.7 us
    all_to_all x1, waiting for transfers between devices, on_device(): lax.all_to_all(sending, 'ctx', split_axis=0, concat_axis=0, tiled=True)  21.2 us
    dot_general x2, matrix products, add_rows(): return jnp.dot(tokens, rows_piece, preferred_element_type=jnp.float32)  20.6 us
    add x15, other arithmetic, merge_parts(): total = first[1] * scale_one + second[1] * scale_two  13.7 us
  transfers between devices with their start and end apart: 4, of which 4 were waited for; matrix products, arithmetic and copies ran while one was open for 5% of the time, Pallas kernels for 0%

commit v1 on v0

v1 whole, which is shorter than its diff:
```python
import jax
import jax.numpy as jnp
from jax import lax
from jax.sharding import Mesh, PartitionSpec as P

QH = 64
KVH = 8
DH = 128
BF = jnp.bfloat16
F32 = jnp.float32


def mm(a, b):
    return jnp.dot(a, b, preferred_element_type=F32)


def on_device(tokens, key_down, value_down, key_up, value_up, prompt_lens, queries, new_latent):
    chips = lax.axis_size("chip")
    cores = lax.axis_size("core")
    n_ctx = chips * cores
    core = lax.axis_index("core")
    device = lax.axis_index("chip") * cores + core
    tok_rows, width = tokens.shape
    shard, lat_width = key_down.shape
    group = QH // KVH
    scale = 1.0 / DH**0.5
    steps_count, req_count = (queries.shape[0], queries.shape[1])
    pairs = steps_count * req_count
    rows = pairs * QH
    share = rows // n_ctx

    swap = [(0, 1), (1, 0)]
    key_mine = lax.all_gather(key_down, "chip", axis=0, tiled=True)
    value_mine = lax.all_gather(value_down, "chip", axis=0, tiled=True)
    key_other = lax.ppermute(key_mine, "core", swap)
    value_other = lax.ppermute(value_mine, "core", swap)
    by_core = tokens.reshape(tok_rows, chips, cores, shard)
    tokens_mine = lax.dynamic_index_in_dim(by_core, core, 2, keepdims=False).reshape(tok_rows, -1)
    tokens_other = lax.dynamic_index_in_dim(by_core, 1 - core, 2, keepdims=False).reshape(tok_rows, -1)

    query = queries.reshape(steps_count, req_count, KVH, group, DH)
    flat_new = new_latent.reshape(pairs, 2 * lat_width)
    new_keys = mm(flat_new[:, :lat_width], key_up).astype(BF).reshape(steps_count, req_count, KVH, DH)
    new_values = mm(flat_new[:, lat_width:], value_up).astype(BF).reshape(steps_count, req_count, KVH, DH)
    causal = (jnp.arange(steps_count)[:, None] >= jnp.arange(steps_count)[None, :])[:, None, None, None, :]
    fresh = jnp.einsum("srgjd,urgd->srgju", query, new_keys, preferred_element_type=F32) * scale
    fresh = jnp.where(causal, fresh, -1e30)
    fresh_top = jnp.max(fresh, -1)
    fresh_weights = jnp.where(causal, jnp.exp(fresh - fresh_top[..., None]), 0.0)
    fresh_total = jnp.sum(fresh_weights, -1)
    fresh_summed = jnp.einsum("srgju,urgd->srgjd", fresh_weights.astype(BF), new_values, preferred_element_type=F32)

    def my_share(x):
        return lax.dynamic_slice_in_dim(x, device * share, share, 0)

    fresh_top = my_share(fresh_top.reshape(rows))
    fresh_total = my_share(fresh_total.reshape(rows))
    fresh_summed = my_share(fresh_summed.reshape(rows, DH))

    key_latent = (mm(tokens_mine, key_mine) + mm(tokens_other, key_other)).astype(BF)
    keys = mm(key_latent, key_up).astype(BF)
    position = device * tok_rows + jnp.arange(tok_rows, dtype=jnp.int32)
    offsets = jnp.cumsum(prompt_lens) - prompt_lens
    member = (position[None, :] >= offsets[:, None]) & (position[None, :] < (offsets + prompt_lens)[:, None])
    key_heads = keys.reshape(-1, KVH, DH)
    scores = jnp.einsum("srgjd,tgd->srgjt", query, key_heads, preferred_element_type=F32) * scale
    visible = member[None, :, None, None, :]
    scores = jnp.where(visible, scores, -1e30)
    top = jnp.max(scores, -1)
    weights = jnp.where(visible, jnp.exp(scores - top[..., None]), 0.0)
    total = jnp.sum(weights, -1)

    value_latent = (mm(tokens_mine, value_mine) + mm(tokens_other, value_other)).astype(BF)
    values = mm(value_latent, value_up).astype(BF)
    value_heads = values.reshape(-1, KVH, DH)
    summed = jnp.einsum("srgjt,tgd->srgjd", weights.astype(BF), value_heads, preferred_element_type=F32)

    stats = jnp.stack([top.reshape(n_ctx, share), total.reshape(n_ctx, share)], 1).reshape(n_ctx, 1, 2 * share)
    stats = jnp.pad(stats, ((0, 0), (0, 7), (0, DH - 2 * share)))
    sending = jnp.concatenate([summed.reshape(n_ctx, share, DH), stats], 1)
    arrived = lax.all_to_all(sending, ("chip", "core"), split_axis=0, concat_axis=0, tiled=True)
    tops = arrived[:, share, :share]
    totals = arrived[:, share, share : 2 * share]
    overall = jnp.maximum(jnp.max(tops, 0), fresh_top)
    carried = jnp.exp(tops - overall[None])
    fresh_carried = jnp.exp(fresh_top - overall)
    total = jnp.sum(totals * carried, 0) + fresh_total * fresh_carried
    summed = jnp.sum(arrived[:, :share] * carried[..., None], 0) + fresh_summed * fresh_carried[:, None]
    result = (summed / total[:, None]).astype(BF)
    result = lax.all_gather(result, ("chip", "core"), axis=0, tiled=True)
    return result.reshape(steps_count, req_count, QH * DH)


def solution(mesh):
    cores = 2
    groups, n_ctx = mesh.shape["groups"], mesh.shape["ctx"]
    split = Mesh(mesh.devices.reshape(groups, n_ctx // cores, cores), ("groups", "chip", "core"))
    ctx = ("chip", "core")
    return jax.shard_map(
        on_device,
        mesh=split,
        in_specs=(
            P(("groups",) + ctx, None),
            P(ctx, None),
            P(ctx, None),
            P(),
            P(),
            P("groups"),
            P(None, "groups", None),
            P(None, "groups", None),
        ),
        out_specs=P(None, "groups", None),
        check_vma=False,
    )
```

time: 341 us -> 253 us (0.74)
  blocking collectives: 56.7 us -> 20.8 us
  other arithmetic: 36.9 us -> 2.65 us
  waiting for transfers between devices: 193 us -> 165 us
  local copies, waits for them, and re-layouts: 6.89 us -> 23.1 us
  matrix products: 28.7 us -> 23.1 us
    all_gather x2 -> x1, blocking collectives: 56.7 us -> 20.8 us  [on_device(): result = lax.all_gather(result, ('chip', 'core'), axis=0, tiled=True)]
    add x33 -> x2, other arithmetic: 35.5 us -> 0.08 us  [the longest x1 0.08 us: on_device(): total = jnp.sum(totals * carried, 0) + fresh_total * fresh_carried]
    all_gather x3 -> x2, waiting for transfers between devices: 170 us -> 151 us  [the longest x1 77.6 us: on_device(): key_mine = lax.all_gather(key_down, 'chip', axis=0, tiled=True)]
    unnamed x20 -> x19, local copies, waits for them, and re-layouts: 2.47 us -> 15 us
    all_to_all x1, waiting for transfers between devices: 21.2 us -> 12.5 us  [on_device(): lax.all_to_all(sending, ('chip', 'core'), split_axis=0, concat_axis=0, ti...]
    dynamic_slice x0 -> x1, local copies, waits for them, and re-layouts: none -> 6.33 us  [on_device(): lax.dynamic_index_in_dim(by_core, 1 - core, 2, keepdims=False)]
    dot_general x10, matrix products: 28.7 us -> 23.1 us  [the longest x6 20.1 us: mm(): return jnp.dot(a, b, preferred_element_type=F32)]
  transfers between devices with their start and end apart: 4 -> 5, of which waited for: 4 -> 3; matrix products, arithmetic and copies ran while one was open for 5% -> 14% of each run, Pallas kernels for 0% -> 0%
where the time goes in v1:
time: 253 us; the launch traced here: 252 us
  waiting for transfers between devices  165 us (65%)
  local copies, waits for them, and re-layouts  23.1 us (9%)
  matrix products  23.1 us (9%)
  blocking collectives  20.8 us (8%)
  between operations  13.6 us (5%)
  starting transfers between devices  3.81 us (2%)
  other arithmetic  2.65 us (1%)
    all_gather x1, waiting for transfers between devices, on_device(): key_mine = lax.all_gather(key_down, 'chip', axis=0, tiled=True)  77.6 us
    all_gather x1, waiting for transfers between devices, on_device(): value_mine = lax.all_gather(value_down, 'chip', axis=0, tiled=True)  73.8 us
    all_gather x1, blocking collectives, on_device(): result = lax.all_gather(result, ('chip', 'core'), axis=0, tiled=True)  20.8 us
    dot_general x6, matrix products, mm(): return jnp.dot(a, b, preferred_element_type=F32)  20.1 us
    unnamed x19, local copies, waits for them, and re-layouts  15 us
    all_to_all x1, waiting for transfers between devices, on_device(): lax.all_to_all(sending, ('chip', 'core'), split_axis=0, concat_axis=0, ti...  12.5 us
    dynamic_slice x1, local copies, waits for them, and re-layouts, on_device(): lax.dynamic_index_in_dim(by_core, 1 - core, 2, keepdims=False)  6.33 us
  transfers between devices with their start and end apart: 5, of which 3 were waited for; matrix products, arithmetic and copies ran while one was open for 14% of the time, Pallas kernels for 0%

profile of v1, /device:TPU:0, one launch (start us, length us, event | category | flops | bytes accessed | tf_op | source)
XLA Modules:
  0.0 252.5 jit_solution(18163818413774467890)
XLA Ops:
  6.5 0.0 copy-start
  6.5 0.0 all-gather.5.cloned.1.call-start
  6.5 0.7 all-gather.5.cloned.1.call-update
  7.3 0.0 all-gather.3.cloned.1.call-start
  7.3 0.7 all-gather.3.cloned.1.call-update
  8.0 77.6 %all-gather.5.cloned.1.call-done = bf16[4096,512]{1,0:T(8,128)(2,1)} async-done(((bf16[512,512]{1,0:T(8,128)(2,1)}), bf16[4096,512]{1,0:T(8,128)(2,1)}) %all-gather.5.cloned.1.call-update) | async-done | bytes 4194320 | tf_op jit(solution)/shard_map/all_gather | solution.py:33
  85.6 0.0 collective-permute-start.1
  85.6 73.8 %all-gather.3.cloned.1.call-done = bf16[4096,512]{1,0:T(8,128)(2,1)} async-done(((bf16[512,512]{1,0:T(8,128)(2,1)}), bf16[4096,512]{1,0:T(8,128)(2,1)}) %all-gather.3.cloned.1.call-update) | async-done | bytes 4194320 | tf_op jit(solution)/shard_map/all_gather | solution.py:34
  159.4 0.0 collective-permute-start
  159.4 0.0 copy-start.6
  159.4 0.0 copy-start.4
  159.4 12.0 %copy.54 = bf16[512,8192]{0,1:T(8,128)(2,1)} copy(bf16[512,8192]{1,0:T(8,128)(2,1)} %param.8) | data formatting | bytes 16777216 | tf_op args[0]
  171.5 0.0 copy-done.6
  171.5 0.2 reduce-window.8
  171.6 0.0 copy-done.4
  171.6 0.3 reshape.166
  172.0 0.1 compare_and_fusion
  172.0 0.0 copy-start.2
  172.0 6.3 %constant_dynamic-slice_fusion = (bf16[512,8,1,512]{0,3,2,1:T(8,128)(2,1)}, bf16[512,8,1,512]{0,3,2,1:T(8,128)(2,1)S(1)}) fusion(bf16[512,8,2,512]{0,3,2,1:T(8,128)(2,1)} %bitcast.75, s32[]{:T(128)S(6)} %select_n.27, s32[]{:T(128)S(6)} %select_n.26), kind=kLoop, calls=%fused_computation.53 | loop fusion | bytes 16777224 | tf_op jit(solution)/shard_map/jit(dynamic_index_in_dim)/dynamic_slice | solution.py:39
  178.4 0.0 copy-done.2
  178.4 0.0 copy-start.1
  178.4 2.3 fusion.40
  180.7 0.0 copy-done.1
  180.7 2.3 fusion.39
  183.1 0.0 collective-permute-done.1
  183.1 0.0 copy-done
  183.1 7.3 %fusion.4 = bf16[64,8,8,128]{3,1,2,0:T(8,128)(2,1)} fusion(bf16[512,1024]{1,0:T(8,128)(2,1)S(1)} %copy-done, f32[512,512]{1,0:T(8,128)S(1)} %fusion.40, bf16[512,4096]{0,1:T(8,128)(2,1)} %bitcast.76, bf16[4096,512]{1,0:T(8,128)(2,1)} %collective-permute-done.1), kind=kOutput, calls=%fused_computation.8 | convolution fusion | flops 2685403136 | bytes 11534336 | tf_op jit(solution)/shard_map/dot_general | solution.py:14
  190.4 1.5 copy.82
  191.9 0.0 collective-permute-done
  191.9 7.6 %fusion.3 = bf16[64,8,8,128]{3,1,2,0:T(8,128)(2,1)} fusion(bf16[512,1024]{1,0:T(8,128)(2,1)} %param.12, f32[512,512]{1,0:T(8,128)S(1)} %fusion.39, bf16[512,4096]{0,1:T(8,128)(2,1)} %bitcast.77, bf16[4096,512]{1,0:T(8,128)(2,1)} %collective-permute-done), kind=kOutput, calls=%fused_computation.7 | convolution fusion | flops 2685403136 | bytes 11534336 | tf_op jit(solution)/shard_map/dot_general | solution.py:14
  199.5 1.5 copy.83
  201.0 0.6 fusion
  201.7 0.7 fusion.1
  202.4 0.0 copy-start.5
  202.4 0.7 convolution_bitcast_fusion.1
  203.1 0.0 copy-start.3
  203.2 0.1 stack_reshape.7
  203.3 0.1 stack_reshape.6
  203.4 0.1 reshape.168
  203.5 0.9 select_maximum_fusion
  204.4 3.8 %all-to-all-start = ((f32[16,72,128]{2,1,0:T(8,128)}), f32[16,72,128]{2,1,0:T(8,128)S(1)}, u32[]{:S(2)}, u32[]{:S(2)}) async-start(f32[16,72,128]{2,1,0:T(8,128)} %select_maximum_fusion), calls=%async_computation | async-start | bytes 1179648 | tf_op jit(solution)/shard_map/all_to_all | solution.py:81
  208.1 0.0 copy-done.5
  208.2 0.3 fusion.9
  208.4 1.3 fusion.38
  209.8 0.1 reshape.171
  209.8 0.3 fusion.23
  210.1 0.1 reshape.174
  210.2 0.0 copy-done.3
  210.2 0.3 fusion.10
  210.5 0.3 convolution_bitcast_fusion
  210.9 0.1 copy.67
  210.9 12.5 %all-to-all-done = f32[16,72,128]{2,1,0:T(8,128)S(1)} async-done(((f32[16,72,128]{2,1,0:T(8,128)}), f32[16,72,128]{2,1,0:T(8,128)S(1)}, u32[]{:S(2)}, u32[]{:S(2)}) %all-to-all-start) | async-done | bytes 589856 | tf_op jit(solution)/shard_map/all_to_all | solution.py:81
  223.5 0.1 fusion.37
  223.6 0.1 dynamic-slice_maximum_fusion
  223.7 0.1 multiply_add_fusion
  223.7 0.2 fusion.20
  224.0 0.1 divide_convert_fusion
  224.1 20.8 %all_gather.11 = bf16[1024,128]{1,0:T(8,128)(2,1)S(1)} all-gather(bf16[64,128]{1,0:T(8,128)(2,1)S(1)} %divide_convert_fusion), channel_id=1, replica_groups=mesh['groups'=2,'chip'=8,'core'=2] {'chip','core'}, dimensions={0}, use_global_device_ids=true | all-gather | bytes 278528 | tf_op jit(solution)/shard_map/all_gather | solution.py:90
  244.8 0.8 reshape.175
  (15 shorter events, 0.2 us)
Async XLA Ops:
  6.5 176.5 %copy-start = (bf16[512,1024]{1,0:T(8,128)(2,1)S(1)}, bf16[512,1024]{1,0:T(8,128)(2,1)}, u32[]{:S(2)}) copy-start(bf16[512,1024]{1,0:T(8,128)(2,1)} %param.11) | copy-start | bytes 3145732
  6.5 79.1 %all-gather.5.cloned.1.call-start = ((), (), s32[]{:S(2)}) async-start(), calls=%async_computation.2 | async-start | bytes 4718592 | tf_op jit(solution)/shard_map/all_gather | solution.py:33
  7.3 152.2 %all-gather.3.cloned.1.call-start = ((), (), s32[]{:S(2)}) async-start(), calls=%async_computation.1 | async-start | bytes 4718592 | tf_op jit(solution)/shard_map/all_gather | solution.py:34
  85.6 97.5 %collective-permute-start.1 = (bf16[4096,512]{1,0:T(8,128)(2,1)}, bf16[4096,512]{1,0:T(8,128)(2,1)}, u32[]{:S(2)}, u32[]{:S(2)}) collective-permute-start(bf16[4096,512]{1,0:T(8,128)(2,1)} %all-gather.5.cloned.1.call-done), channel_id=1, source_target_pairs={{0,1},{1,0},{2,3},{3,2},{4,5},{5,4},{6,7},{7,6},{8,9},{9,8},{10,11... | collective-permute-start | bytes 12582920 | tf_op jit(solution)/shard_map/ppermute | solution.py:35
  159.4 32.5 %collective-permute-start = (bf16[4096,512]{1,0:T(8,128)(2,1)}, bf16[4096,512]{1,0:T(8,128)(2,1)}, u32[]{:S(2)}, u32[]{:S(2)}) collective-permute-start(bf16[4096,512]{1,0:T(8,128)(2,1)} %all-gather.3.cloned.1.call-done), channel_id=1, source_target_pairs={{0,1},{1,0},{2,3},{3,2},{4,5},{5,4},{6,7},{7,6},{8,9},{9,8},{10,11... | collective-permute-start | bytes 12582920 | tf_op jit(solution)/shard_map/ppermute | solution.py:36
  159.4 12.0 %copy-start.6 = (s32[4]{0:T(128)S(1)}, s32[4]{0:T(128)}, u32[]{:S(2)}) copy-start(s32[4]{0:T(128)} %param.13) | copy-start | bytes 52
  159.4 12.2 %copy-start.4 = (bf16[4,4,8192]{2,1,0:T(4,128)(2,1)S(1)}, bf16[4,4,8192]{2,1,0:T(4,128)(2,1)}, u32[]{:S(2)}) copy-start(bf16[4,4,8192]{2,1,0:T(4,128)(2,1)} %param.14) | copy-start | bytes 786436
  172.0 6.3 %copy-start.2 = (bf16[4096,512]{1,0:T(8,128)(2,1)S(1)}, bf16[4096,512]{1,0:T(8,128)(2,1)}, u32[]{:S(2)}) copy-start(bf16[4096,512]{1,0:T(8,128)(2,1)} %all-gather.5.cloned.1.call-done) | copy-start | bytes 12582916
  178.4 2.4 copy-start.1
  202.4 5.7 %copy-start.5 = (bf16[4,4,1024]{2,1,0:T(4,128)(2,1)S(1)}, bf16[4,4,1024]{2,1,0:T(4,128)(2,1)}, u32[]{:S(2)}) copy-start(bf16[4,4,1024]{2,1,0:T(4,128)(2,1)} %param.15) | copy-start | bytes 98308
  203.1 7.1 %copy-start.3 = (bf16[512,1024]{1,0:T(8,128)(2,1)S(1)}, bf16[512,1024]{1,0:T(8,128)(2,1)}, u32[]{:S(2)}) copy-start(bf16[512,1024]{1,0:T(8,128)(2,1)} %param.12) | copy-start | bytes 3145732
  204.4 19.1 %all-to-all-start = ((f32[16,72,128]{2,1,0:T(8,128)}), f32[16,72,128]{2,1,0:T(8,128)S(1)}, u32[]{:S(2)}, u32[]{:S(2)}) async-start(f32[16,72,128]{2,1,0:T(8,128)} %select_maximum_fusion), calls=%async_computation | async-start | bytes 1179648 | tf_op jit(solution)/shard_map/all_to_all | solution.py:81
Sparse Core Ops, SparseCore 0:
  9.5 76.0 all-gather.4
  87.7 71.6 all-gather.2

commit v2 on v1

v2 whole, which is shorter than its diff:
```python
import jax
import jax.numpy as jnp
from jax import lax
from jax.sharding import Mesh, PartitionSpec as P

QH = 64
KVH = 8
DH = 128
CORES = 2
BF = jnp.bfloat16
F32 = jnp.float32
SWAP = [(0, 1), (1, 0)]


def mm(a, b):
    return jnp.dot(a, b, preferred_element_type=F32)


def project(tokens, theirs, block):
    chips = lax.axis_size("chip")
    chip = lax.axis_index("chip")
    rows = block.shape[0]
    if chips > 8:
        full = lax.all_gather(block, "chip", axis=0, tiled=True)
        return mm(tokens, full), mm(theirs, full)
    cycle = list(range(0, chips, 2)) + list(range(chips - 1, 0, -2))
    last = chips - 1
    place = jnp.where(chip & 1 == 0, chip >> 1, last - (chip >> 1))
    chains = 2
    piece = rows // (2 * chains)
    right = [(cycle[i], cycle[(i + 1) % chips]) for i in range(chips)]
    left = [(b, a) for a, b in right]

    def block_of(spot):
        spot = jnp.where(spot < 0, spot + chips, jnp.where(spot > last, spot - chips, spot))
        return jnp.where(spot < chips // 2, 2 * spot, 2 * (last - spot) + 1) * rows

    def term(x, start, part):
        return mm(lax.dynamic_slice_in_dim(x, start, part.shape[0], 1, allow_negative_indices=False), part)

    held = [block[k * piece : (k + 1) * piece] for k in range(2 * chains)]
    todo = [(chip * rows, block)]
    mine_sum = theirs_sum = 0.0
    for step in range(1, chips):
        for k in range(2 * chains):
            held[k] = lax.ppermute(held[k], "chip", right if k < chains else left)
        if step == min(3, last):
            held, theirs = lax.optimization_barrier((held, theirs))
        for k in range(2 * chains):
            todo.append((block_of(place - step if k < chains else place + step) + k * piece, held[k]))
        if step >= min(3, last):
            for start, part in todo:
                mine_sum = mine_sum + term(tokens, start, part)
                theirs_sum = theirs_sum + term(theirs, start, part)
            todo = []
    return mine_sum, theirs_sum


def on_device(tokens, key_down, value_down, key_up, value_up, prompt_lens, queries, new_latent):
    chips = lax.axis_size("chip")
    chip = lax.axis_index("chip")
    core = lax.axis_index("core")
    first = core == 0
    tok_rows = tokens.shape[0]
    lat_width = key_down.shape[1]
    group = QH // KVH
    heads = KVH // CORES
    scale = 1.0 / DH**0.5
    steps_count, req_count = (queries.shape[0], queries.shape[1])
    pairs = steps_count * req_count
    rows = pairs * heads * group
    share = rows // chips

    theirs = lax.ppermute(tokens, "core", SWAP)
    own_part = jnp.where(first, key_down, value_down)
    got_part = lax.ppermute(jnp.where(first, value_down, key_down), "core", SWAP)
    block = jnp.concatenate([jnp.where(first, own_part, got_part), jnp.where(first, got_part, own_part)], 0)
    mine_sum, theirs_sum = project(tokens, theirs, block)

    query = lax.dynamic_index_in_dim(
        queries.reshape(steps_count, req_count, CORES, heads * group * DH), core, 2, keepdims=False
    ).reshape(steps_count, req_count, heads, group, DH)
    key_up = lax.dynamic_slice_in_dim(key_up, core * heads * DH, heads * DH, 1)
    value_up = lax.dynamic_slice_in_dim(value_up, core * heads * DH, heads * DH, 1)
    flat_new = new_latent.reshape(pairs, 2 * lat_width)
    new_keys = mm(flat_new[:, :lat_width], key_up).astype(BF).reshape(steps_count, req_count, heads, DH)
    new_values = mm(flat_new[:, lat_width:], value_up).astype(BF).reshape(steps_count, req_count, heads, DH)
    causal = (jnp.arange(steps_count)[:, None] >= jnp.arange(steps_count)[None, :])[:, None, None, None, :]
    fresh = jnp.einsum("srgjd,urgd->srgju", query, new_keys, preferred_element_type=F32) * scale
    fresh = jnp.where(causal, fresh, -1e30)
    fresh_top = jnp.max(fresh, -1)
    fresh_weights = jnp.where(causal, jnp.exp(fresh - fresh_top[..., None]), 0.0)
    fresh_total = jnp.sum(fresh_weights, -1)
    fresh_summed = jnp.einsum("srgju,urgd->srgjd", fresh_weights.astype(BF), new_values, preferred_element_type=F32)

    def my_share(x):
        return lax.dynamic_slice_in_dim(x, chip * share, share, 0)

    fresh_top = my_share(fresh_top.reshape(rows))
    fresh_total = my_share(fresh_total.reshape(rows))
    fresh_summed = my_share(fresh_summed.reshape(rows, DH))

    mine = mine_sum.astype(BF)
    other = theirs_sum.astype(BF)
    have = jnp.concatenate([jnp.where(first, mine, other), jnp.where(first, other, mine)], 0)
    got = lax.ppermute(have, "core", SWAP)
    key_latent = jnp.where(first, have, got)
    value_latent = jnp.where(first, got, have)
    keys = mm(key_latent, key_up).astype(BF)
    values = mm(value_latent, value_up).astype(BF)
    position = chip * CORES * tok_rows + jnp.arange(CORES * tok_rows, dtype=jnp.int32)
    offsets = jnp.cumsum(prompt_lens) - prompt_lens
    member = (position[None, :] >= offsets[:, None]) & (position[None, :] < (offsets + prompt_lens)[:, None])
    key_heads = keys.reshape(-1, heads, DH)
    value_heads = values.reshape(-1, heads, DH)
    scores = jnp.einsum("srgjd,tgd->srgjt", query, key_heads, preferred_element_type=F32) * scale
    visible = member[None, :, None, None, :]
    scores = jnp.where(visible, scores, -1e30)
    top = jnp.max(scores, -1)
    weights = jnp.where(visible, jnp.exp(scores - top[..., None]), 0.0)
    total = jnp.sum(weights, -1)
    summed = jnp.einsum("srgjt,tgd->srgjd", weights.astype(BF), value_heads, preferred_element_type=F32)

    stats = jnp.stack([top.reshape(chips, share), total.reshape(chips, share)], 1).reshape(chips, 1, 2 * share)
    stats = jnp.pad(stats, ((0, 0), (0, 7), (0, DH - 2 * share)))
    sending = jnp.concatenate([summed.reshape(chips, share, DH), stats], 1)
    arrived = lax.all_to_all(sending, "chip", split_axis=0, concat_axis=0, tiled=True)
    tops = arrived[:, share, :share]
    totals = arrived[:, share, share : 2 * share]
    overall = jnp.maximum(jnp.max(tops, 0), fresh_top)
    carried = jnp.exp(tops - overall[None])
    fresh_carried = jnp.exp(fresh_top - overall)
    total = jnp.sum(totals * carried, 0) + fresh_total * fresh_carried
    summed = jnp.sum(arrived[:, :share] * carried[..., None], 0) + fresh_summed * fresh_carried[:, None]
    result = (summed / total[:, None]).astype(BF)

    if chips & (chips - 1) == 0:
        whole = result.reshape(1, share, DH)
        span = 1
        while span < chips:
            away = lax.ppermute(whole, "chip", [(c, c ^ span) for c in range(chips)])
            upper = (chip & span) != 0
            whole = jnp.concatenate([jnp.where(upper, away, whole), jnp.where(upper, whole, away)], 0)
            span *= 2
    else:
        whole = lax.all_gather(result, "chip", axis=0, tiled=True)
    whole = whole.reshape(pairs, 1, rows // pairs * DH)
    away = lax.ppermute(whole, "core", SWAP)
    whole = jnp.concatenate([jnp.where(first, whole, away), jnp.where(first, away, whole)], 1)
    return whole.reshape(steps_count, req_count, QH * DH)


def solution(mesh):
    groups, n_ctx = mesh.shape["groups"], mesh.shape["ctx"]
    split = Mesh(mesh.devices.reshape(groups, n_ctx // CORES, CORES), ("groups", "chip", "core"))
    ctx = ("chip", "core")
    return jax.shard_map(
        on_device,
        mesh=split,
        in_specs=(
            P(("groups",) + ctx, None),
            P(ctx, None),
            P(ctx, None),
            P(),
            P(),
            P("groups"),
            P(None, "groups", None),
            P(None, "groups", None),
        ),
        out_specs=P(None, "groups", None),
        check_vma=False,
    )
```

time: 253 us -> 163 us (0.64)
  waiting for transfers between devices: 165 us -> 47 us
  matrix products: 23.1 us -> 61.9 us
  starting transfers between devices: 3.81 us -> 39.4 us
  blocking collectives: 20.8 us -> 0 us
  local copies, waits for them, and re-layouts: 23.1 us -> 7.2 us
  between operations: 13.6 us -> 0.7 us
  other arithmetic: 2.65 us -> 5.39 us
    all_gather x2 -> x0, waiting for transfers between devices: 151 us -> none  [the longest x1 77.6 us: on_device(): key_mine = lax.all_gather(key_down, 'chip', axis=0, tiled=True)]
    ppermute x2 -> x35, waiting for transfers between devices: 0.01 us -> 38.1 us  [the longest x28 14.7 us: project(): held[k] = lax.ppermute(held[k], 'chip', right if k < chains else left)]
    dot_general x6 -> x62, matrix products: 20.1 us -> 57.7 us  [mm(): return jnp.dot(a, b, preferred_element_type=F32)]
    ppermute x2 -> x35, starting transfers between devices: 0.01 us -> 35.1 us  [the longest x28 30.3 us: project(): held[k] = lax.ppermute(held[k], 'chip', right if k < chains else left)]
    all_gather x1 -> x0, blocking collectives: 20.8 us -> none  [on_device(): result = lax.all_gather(result, ('chip', 'core'), axis=0, tiled=True)]
    unnamed x19 -> x12, local copies, waits for them, and re-layouts: 15 us -> 0.04 us
    dynamic_slice x1, local copies, waits for them, and re-layouts: 6.33 us -> 0.81 us  [on_device(): lax.dynamic_index_in_dim(queries.reshape(steps_count, req_count, CORES, h...]
    all_to_all x1, waiting for transfers between devices: 12.5 us -> 8.93 us  [on_device(): lax.all_to_all(sending, 'chip', split_axis=0, concat_axis=0, tiled=True)]
  transfers between devices with their start and end apart: 5 -> 36, of which waited for: 3 -> 15; matrix products, arithmetic and copies ran while one was open for 14% -> 39% of each run, Pallas kernels for 0% -> 0%
where the time goes in v2:
time: 163 us; the launch traced here: 162 us
  matrix products  61.9 us (38%)
  waiting for transfers between devices  47 us (29%)
  starting transfers between devices  39.4 us (24%)
  local copies, waits for them, and re-layouts  7.2 us (4%)
  other arithmetic  5.39 us (3%)
    dot_general x62, matrix products, mm(): return jnp.dot(a, b, preferred_element_type=F32)  57.7 us
    ppermute x28, starting transfers between devices, project(): held[k] = lax.ppermute(held[k], 'chip', right if k < chains else left)  30.3 us
    ppermute x28, waiting for transfers between devices, project(): held[k] = lax.ppermute(held[k], 'chip', right if k < chains else left)  14.7 us
    ppermute x1, waiting for transfers between devices, on_device(): lax.ppermute(jnp.where(first, value_down, key_down), 'core', SWAP)  12.2 us
    ppermute x3, waiting for transfers between devices, on_device(): away = lax.ppermute(whole, 'chip', [(c, c ^ span) for c in range(chips)])  9.11 us
    all_to_all x1, waiting for transfers between devices, on_device(): lax.all_to_all(sending, 'chip', split_axis=0, concat_axis=0, tiled=True)  8.93 us
    all_to_all x1, starting transfers between devices, on_device(): lax.all_to_all(sending, 'chip', split_axis=0, concat_axis=0, tiled=True)  4.38 us
    ppermute x3, starting transfers between devices, on_device(): away = lax.ppermute(whole, 'chip', [(c, c ^ span) for c in range(chips)])  3.94 us
  transfers between devices with their start and end apart: 36, of which 15 were waited for; matrix products, arithmetic and copies ran while one was open for 39% of the time, Pallas kernels for 0%

profile of v2, /device:TPU:0, one launch (start us, length us, event | category | flops | bytes accessed | tf_op | source)
XLA Modules:
  0.0 161.6 jit_solution(11438623516612690229)
XLA Ops:
  1.8 12.2 %collective-permute-done = bf16[512,512]{1,0:T(8,128)(2,1)S(1)} collective-permute-done((bf16[512,512]{1,0:T(8,128)(2,1)S(1)}, bf16[512,512]{1,0:T(8,128)(2,1)S(1)}, u32[]{:S(2)}, u32[]{:S(2)}) %collective-permute-start) | collective-permute-done | bytes 524320 | tf_op jit(solution)/shard_map/ppermute | solution.py:76
  16.0 2.9 %collective-permute-start.4 = (bf16[256,512]{1,0:T(8,128)(2,1)}, bf16[256,512]{1,0:T(8,128)(2,1)S(1)}, u32[]{:S(2)}, u32[]{:S(2)}) collective-permute-start(bf16[256,512]{1,0:T(8,128)(2,1)} %get-tuple-element.23), channel_id=1, source_target_pairs={{4,0},{8,4},{12,8},{14,12},{10,14},{6,10},{2,6},{0,2},{5,1},{9,5},... | collective-permute-start | bytes 786440 | tf_op jit(solution)/shard_map/ppermute | solution.py:46
  18.9 1.6 collective-permute-start.3
  26.3 2.0 %collective-permute-start.8 = (bf16[256,512]{1,0:T(8,128)(2,1)S(1)}, bf16[256,512]{1,0:T(8,128)(2,1)S(1)}, u32[]{:S(2)}, u32[]{:S(2)}) collective-permute-start(bf16[256,512]{1,0:T(8,128)(2,1)S(1)} %collective-permute-done.4), channel_id=1, source_target_pairs={{4,0},{8,4},{12,8},{14,12},{10,14},{6,10},{2,6},{0,2},{5,1},{9,5},... | collective-permute-start | bytes 786440 | tf_op jit(solution)/shard_map/ppermute | solution.py:46
  28.3 3.5 %collective-permute-done.3 = bf16[256,512]{1,0:T(8,128)(2,1)S(1)} collective-permute-done((bf16[256,512]{1,0:T(8,128)(2,1)}, bf16[256,512]{1,0:T(8,128)(2,1)S(1)}, u32[]{:S(2)}, u32[]{:S(2)}) %collective-permute-start.3) | collective-permute-done | bytes 262176 | tf_op jit(solution)/shard_map/ppermute | solution.py:46
  31.8 2.0 %collective-permute-start.7 = (bf16[256,512]{1,0:T(8,128)(2,1)S(1)}, bf16[256,512]{1,0:T(8,128)(2,1)S(1)}, u32[]{:S(2)}, u32[]{:S(2)}) collective-permute-start(bf16[256,512]{1,0:T(8,128)(2,1)S(1)} %collective-permute-done.3), channel_id=1, source_target_pairs={{4,0},{8,4},{12,8},{14,12},{10,14},{6,10},{2,6},{0,2},{5,1},{9,5},... | collective-permute-start | bytes 786440 | tf_op jit(solution)/shard_map/ppermute | solution.py:46
  35.9 1.2 fusion.170
  37.2 1.2 fusion.164
  38.4 1.3 fusion.166
  39.7 1.2 fusion.168
  41.0 2.1 %fusion.6 = f32[512,512]{1,0:T(8,128)S(1)} fusion(f32[512,512]{1,0:T(8,128)S(1)} %fusion.164, f32[512,512]{1,0:T(8,128)S(1)} %fusion.166, f32[512,512]{1,0:T(8,128)S(1)} %fusion.168, f32[512,512]{1,0:T(8,128)S(1)} %fusion.170, bf16[512,8192]{1,0:T(8,128)(2,1)} %param.8, s32[]{:T(128)S(6)} %mul.224, bf16[512,512]{1,0:T(8,128)(2,1)S(1)} %get-tuple-element.19, ...), kind=kOutput, calls=%fused_computation.12 | convolution fusion | flops 540016640 | bytes 7340036 | tf_op jit(solution)/shard_map/dot_general | solution.py:16
  43.1 1.6 %collective-permute-start.10 = (bf16[256,512]{1,0:T(8,128)(2,1)S(1)}, bf16[256,512]{1,0:T(8,128)(2,1)S(1)}, u32[]{:S(2)}, u32[]{:S(2)}) collective-permute-start(bf16[256,512]{1,0:T(8,128)(2,1)S(1)} %collective-permute-done.6), channel_id=1, source_target_pairs={{0,4},{4,8},{8,12},{12,14},{14,10},{10,6},{6,2},{2,0},{1,5},{5,9},... | collective-permute-start | bytes 786440 | tf_op jit(solution)/shard_map/ppermute | solution.py:46
  45.2 1.5 collective-permute-start.12
  46.7 2.0 %collective-permute-done.5 = bf16[256,512]{1,0:T(8,128)(2,1)S(1)} collective-permute-done((bf16[256,512]{1,0:T(8,128)(2,1)S(1)}, bf16[256,512]{1,0:T(8,128)(2,1)S(1)}, u32[]{:S(2)}, u32[]{:S(2)}) %collective-permute-start.5) | collective-permute-done | bytes 262176 | tf_op jit(solution)/shard_map/ppermute | solution.py:46
  50.0 1.2 fusion.159
  51.9 2.4 %collective-permute-done.10 = bf16[256,512]{1,0:T(8,128)(2,1)S(1)} collective-permute-done((bf16[256,512]{1,0:T(8,128)(2,1)S(1)}, bf16[256,512]{1,0:T(8,128)(2,1)S(1)}, u32[]{:S(2)}, u32[]{:S(2)}) %collective-permute-start.10) | collective-permute-done | bytes 262176 | tf_op jit(solution)/shard_map/ppermute | solution.py:46
  54.3 1.7 %collective-permute-done.12 = bf16[256,512]{1,0:T(8,128)(2,1)S(1)} collective-permute-done((bf16[256,512]{1,0:T(8,128)(2,1)S(1)}, bf16[256,512]{1,0:T(8,128)(2,1)S(1)}, u32[]{:S(2)}, u32[]{:S(2)}) %collective-permute-start.12) | collective-permute-done | bytes 262176 | tf_op jit(solution)/shard_map/ppermute | solution.py:46
  56.0 1.3 collective-permute-done.9
  57.4 1.6 collective-permute-start.16
  60.0 1.2 fusion.101
  61.3 1.3 fusion.103
  62.5 1.6 collective-permute-start.17
  65.8 1.3 fusion.115
  67.1 1.2 fusion.117
  68.3 1.2 fusion.119
  69.6 2.0 %fusion.8 = f32[512,512]{1,0:T(8,128)S(1)} fusion(f32[512,512]{1,0:T(8,128)S(1)} %fusion.113, f32[512,512]{1,0:T(8,128)S(1)} %fusion.115, f32[512,512]{1,0:T(8,128)S(1)} %fusion.117, f32[512,512]{1,0:T(8,128)S(1)} %fusion.119, bf16[512,8192]{1,0:T(8,128)(2,1)} %collective-permute-done.13, s32[]{:T(128)S(6)} %mul.224, ...), kind=kOutput, calls=%fused_computation.14 | convolution fusion | flops 540016640 | bytes 7340036 | tf_op jit(solution)/shard_map/dot_general | solution.py:16
  71.6 1.2 fusion.106
  72.8 1.2 fusion.108
  74.1 1.2 fusion.110
  75.3 1.4 fusion.34
  77.0 1.3 fusion.99
  80.1 1.6 collective-permute-start.21
  81.7 1.6 collective-permute-start.20
  85.4 1.2 fusion.95
  86.7 1.2 fusion.93
  87.9 1.2 fusion.91
  89.2 1.5 fusion.40
  91.9 1.3 fusion.88
  93.2 2.2 %collective-permute-start.24 = (bf16[256,512]{1,0:T(8,128)(2,1)S(1)}, bf16[256,512]{1,0:T(8,128)(2,1)S(1)}, u32[]{:S(2)}, u32[]{:S(2)}) collective-permute-start(bf16[256,512]{1,0:T(8,128)(2,1)S(1)} %collective-permute-done.20), channel_id=1, source_target_pairs={{4,0},{8,4},{12,8},{14,12},{10,14},{6,10},{2,6},{0,2},{5,1},{9,5},... | collective-permute-start | bytes 786440 | tf_op jit(solution)/shard_map/ppermute | solution.py:46
  95.7 1.2 fusion.86
  97.0 1.7 %collective-permute-start.25 = (bf16[256,512]{1,0:T(8,128)(2,1)S(1)}, bf16[256,512]{1,0:T(8,128)(2,1)S(1)}, u32[]{:S(2)}, u32[]{:S(2)}) collective-permute-start(bf16[256,512]{1,0:T(8,128)(2,1)S(1)} %collective-permute-done.21), channel_id=1, source_target_pairs={{4,0},{8,4},{12,8},{14,12},{10,14},{6,10},{2,6},{0,2},{5,1},{9,5},... | collective-permute-start | bytes 786440 | tf_op jit(solution)/shard_map/ppermute | solution.py:46
  99.0 1.2 fusion.84
  101.0 1.4 fusion.42
  102.8 1.3 fusion.81
  104.1 2.0 %collective-permute-start.28 = (bf16[256,512]{1,0:T(8,128)(2,1)S(1)}, bf16[256,512]{1,0:T(8,128)(2,1)S(1)}, u32[]{:S(2)}, u32[]{:S(2)}) collective-permute-start(bf16[256,512]{1,0:T(8,128)(2,1)S(1)} %collective-permute-done.24), channel_id=1, source_target_pairs={{4,0},{8,4},{12,8},{14,12},{10,14},{6,10},{2,6},{0,2},{5,1},{9,5},... | collective-permute-start | bytes 786440 | tf_op jit(solution)/shard_map/ppermute | solution.py:46
  106.4 1.2 fusion.79
  107.6 1.7 %collective-permute-start.29 = (bf16[256,512]{1,0:T(8,128)(2,1)S(1)}, bf16[256,512]{1,0:T(8,128)(2,1)S(1)}, u32[]{:S(2)}, u32[]{:S(2)}) collective-permute-start(bf16[256,512]{1,0:T(8,128)(2,1)S(1)} %collective-permute-done.25), channel_id=1, source_target_pairs={{4,0},{8,4},{12,8},{14,12},{10,14},{6,10},{2,6},{0,2},{5,1},{9,5},... | collective-permute-start | bytes 786440 | tf_op jit(solution)/shard_map/ppermute | solution.py:46
  109.6 1.3 fusion.77
  111.7 1.4 fusion.44
  113.1 1.5 collective-permute-done.29
  114.6 1.2 fusion.70
  117.8 1.2 fusion.74
  119.3 1.4 fusion.47
  121.8 1.7 %fusion.257 = (f32[4,4,4,8]{3,0,2,1:T(4,128)S(1)}, f32[4,4,4,8,4]{3,4,0,2,1:T(4,128)S(1)}) fusion(bf16[4,4,4,8,128]{4,3,2,1,0:T(8,128)(2,1)} %reshape.163, bf16[4,4,4,128,1]{3,2,1,0,4:T(4,128)(2,1)S(1)} %bitcast.111, pred[4,4]{1,0:T(4,128)(4,1)S(1)} %iota_compare_fusion.1), kind=kOutput, calls=%fused_computation.312 | convolution fusion | flops 529920 | bytes 157712 | tf_op jit(solution)/shard_map/srgjd,urgd->srgju/dot_general | solution.py:89
  125.0 1.5 fusion
  127.2 2.0 %convolution_convert_fusion.1 = bf16[1024,512]{0,1:T(8,128)(2,1)S(1)} fusion(bf16[1024,512]{1,0:T(8,128)(2,1)} %collective-permute-done.30, pred[]{:T(512)S(6)} %eq.6, bf16[512,1024]{1,0:T(8,128)(2,1)S(1)} %copy-done.1, s32[]{:T(128)S(6)} %select_n.343, bf16[512,512]{1,0:T(8,128)(2,1)S(1)} %get-tuple-element.22, bf16[512,512]{1,0:T(8,128)(2,1)S(1)} %get-tuple-element.21), kind=kOutput, calls=%fused_computation.4 | convolution fusion | flops 540016640 | bytes 3670021 | tf_op jit(solution)/shard_map/dot_general | solution.py:16
  131.0 4.4 %all-to-all-start = ((f32[8,72,128]{2,1,0:T(8,128)}), f32[8,72,128]{2,1,0:T(8,128)S(1)}, u32[]{:S(2)}, u32[]{:S(2)}) async-start(f32[8,72,128]{2,1,0:T(8,128)} %select_maximum_fusion), calls=%async_computation | async-start | bytes 589824 | tf_op jit(solution)/shard_map/all_to_all | solution.py:127
  136.3 8.9 %all-to-all-done = f32[8,72,128]{2,1,0:T(8,128)S(1)} async-done(((f32[8,72,128]{2,1,0:T(8,128)}), f32[8,72,128]{2,1,0:T(8,128)S(1)}, u32[]{:S(2)}, u32[]{:S(2)}) %all-to-all-start) | async-done | bytes 294944 | tf_op jit(solution)/shard_map/all_to_all | solution.py:127
  145.8 1.5 collective-permute-start.31
  147.3 2.3 %collective-permute-done.31 = bf16[1,64,128]{2,1,0:T(8,128)(2,1)S(1)} collective-permute-done((bf16[1,64,128]{2,1,0:T(8,128)(2,1)S(1)}, bf16[1,64,128]{2,1,0:T(8,128)(2,1)S(1)}, u32[]{:S(2)}, u32[]{:S(2)}) %collective-permute-start.31) | collective-permute-done | bytes 16416 | tf_op jit(solution)/shard_map/ppermute | solution.py:141
  150.7 2.9 %collective-permute-done.32 = bf16[2,64,128]{2,1,0:T(8,128)(2,1)S(1)} collective-permute-done((bf16[2,64,128]{2,1,0:T(8,128)(2,1)S(1)}, bf16[2,64,128]{2,1,0:T(8,128)(2,1)S(1)}, u32[]{:S(2)}, u32[]{:S(2)}) %collective-permute-start.32) | collective-permute-done | bytes 32800 | tf_op jit(solution)/shard_map/ppermute | solution.py:141
  153.6 1.3 collective-permute-start.33
  154.9 4.0 %collective-permute-done.33 = bf16[4,64,128]{2,1,0:T(8,128)(2,1)S(1)} collective-permute-done((bf16[4,64,128]{2,1,0:T(8,128)(2,1)S(1)}, bf16[4,64,128]{2,1,0:T(8,128)(2,1)S(1)}, u32[]{:S(2)}, u32[]{:S(2)}) %collective-permute-start.33) | collective-permute-done | bytes 65568 | tf_op jit(solution)/shard_map/ppermute | solution.py:141
  159.1 1.3 collective-permute-done.34
  (137 shorter events, 36.5 us)
Async XLA Ops:
  0.0 121.4 %copy-start = (bf16[512,1024]{1,0:T(8,128)(2,1)S(1)}, bf16[512,1024]{1,0:T(8,128)(2,1)}, u32[]{:S(2)}) copy-start(bf16[512,1024]{1,0:T(8,128)(2,1)} %param.11) | copy-start | bytes 3145732
  0.0 57.4 %collective-permute-start.13 = (bf16[512,8192]{1,0:T(8,128)(2,1)}, bf16[512,8192]{1,0:T(8,128)(2,1)}, u32[]{:S(2)}, u32[]{:S(2)}) collective-permute-start(bf16[512,8192]{1,0:T(8,128)(2,1)} %param.8), channel_id=1, source_target_pairs={{0,1},{1,0},{2,3},{3,2},{4,5},{5,4},{6,7},{7,6},{8,9},{9,8},{10,11... | collective-permute-start | bytes 25165832 | tf_op jit(solution)/shard_map/ppermute | solution.py:74
  1.6 12.4 %collective-permute-start = (bf16[512,512]{1,0:T(8,128)(2,1)S(1)}, bf16[512,512]{1,0:T(8,128)(2,1)S(1)}, u32[]{:S(2)}, u32[]{:S(2)}) collective-permute-start(bf16[512,512]{1,0:T(8,128)(2,1)S(1)} %broadcast_select_fusion.4), channel_id=1, source_target_pairs={{0,1},{1,0},{2,3},{3,2},{4,5},{5,4},{6,7},{7,6},{8,9},{9,8},{10,11... | collective-permute-start | bytes 1572872 | tf_op jit(solution)/shard_map/ppermute | solution.py:76
  16.0 10.3 %collective-permute-start.4 = (bf16[256,512]{1,0:T(8,128)(2,1)}, bf16[256,512]{1,0:T(8,128)(2,1)S(1)}, u32[]{:S(2)}, u32[]{:S(2)}) collective-permute-start(bf16[256,512]{1,0:T(8,128)(2,1)} %get-tuple-element.23), channel_id=1, source_target_pairs={{4,0},{8,4},{12,8},{14,12},{10,14},{6,10},{2,6},{0,2},{5,1},{9,5},... | collective-permute-start | bytes 786440 | tf_op jit(solution)/shard_map/ppermute | solution.py:46
  18.9 13.0 %collective-permute-start.3 = (bf16[256,512]{1,0:T(8,128)(2,1)}, bf16[256,512]{1,0:T(8,128)(2,1)S(1)}, u32[]{:S(2)}, u32[]{:S(2)}) collective-permute-start(bf16[256,512]{1,0:T(8,128)(2,1)} %get-tuple-element.24), channel_id=1, source_target_pairs={{4,0},{8,4},{12,8},{14,12},{10,14},{6,10},{2,6},{0,2},{5,1},{9,5},... | collective-permute-start | bytes 786440 | tf_op jit(solution)/shard_map/ppermute | solution.py:46
  21.3 12.6 %collective-permute-start.2 = (bf16[256,512]{1,0:T(8,128)(2,1)}, bf16[256,512]{1,0:T(8,128)(2,1)S(1)}, u32[]{:S(2)}, u32[]{:S(2)}) collective-permute-start(bf16[256,512]{1,0:T(8,128)(2,1)} %get-tuple-element.25), channel_id=1, source_target_pairs={{0,4},{4,8},{8,12},{12,14},{14,10},{10,6},{6,2},{2,0},{1,5},{5,9},... | collective-permute-start | bytes 786440 | tf_op jit(solution)/shard_map/ppermute | solution.py:46
  21.7 13.3 %collective-permute-start.1 = (bf16[256,512]{1,0:T(8,128)(2,1)}, bf16[256,512]{1,0:T(8,128)(2,1)S(1)}, u32[]{:S(2)}, u32[]{:S(2)}) collective-permute-start(bf16[256,512]{1,0:T(8,128)(2,1)} %get-tuple-element.26), channel_id=1, source_target_pairs={{0,4},{4,8},{8,12},{12,14},{14,10},{10,6},{6,2},{2,0},{1,5},{5,9},... | collective-permute-start | bytes 786440 | tf_op jit(solution)/shard_map/ppermute | solution.py:46
  26.3 24.9 %slice-start = ((s8[8388608]{0:T(1024)(128)(4,1)}), s8[4194304]{0:T(1024)(128)(4,1)S(1)}, s32[]{:S(2)}) async-start(s8[8388608]{0:T(1024)(128)(4,1)} %bitcast.104), calls=%async_computation.1 | async-start | bytes 8388608
  26.3 18.9 %collective-permute-start.8 = (bf16[256,512]{1,0:T(8,128)(2,1)S(1)}, bf16[256,512]{1,0:T(8,128)(2,1)S(1)}, u32[]{:S(2)}, u32[]{:S(2)}) collective-permute-start(bf16[256,512]{1,0:T(8,128)(2,1)S(1)} %collective-permute-done.4), channel_id=1, source_target_pairs={{4,0},{8,4},{12,8},{14,12},{10,14},{6,10},{2,6},{0,2},{5,1},{9,5},... | collective-permute-start | bytes 786440 | tf_op jit(solution)/shard_map/ppermute | solution.py:46
  31.8 12.9 %collective-permute-start.7 = (bf16[256,512]{1,0:T(8,128)(2,1)S(1)}, bf16[256,512]{1,0:T(8,128)(2,1)S(1)}, u32[]{:S(2)}, u32[]{:S(2)}) collective-permute-start(bf16[256,512]{1,0:T(8,128)(2,1)S(1)} %collective-permute-done.3), channel_id=1, source_target_pairs={{4,0},{8,4},{12,8},{14,12},{10,14},{6,10},{2,6},{0,2},{5,1},{9,5},... | collective-permute-start | bytes 786440 | tf_op jit(solution)/shard_map/ppermute | solution.py:46
  33.8 9.2 %collective-permute-start.6 = (bf16[256,512]{1,0:T(8,128)(2,1)S(1)}, bf16[256,512]{1,0:T(8,128)(2,1)S(1)}, u32[]{:S(2)}, u32[]{:S(2)}) collective-permute-start(bf16[256,512]{1,0:T(8,128)(2,1)S(1)} %collective-permute-done.2), channel_id=1, source_target_pairs={{0,4},{4,8},{8,12},{12,14},{14,10},{10,6},{6,2},{2,0},{1,5},{5,9},... | collective-permute-start | bytes 786440 | tf_op jit(solution)/shard_map/ppermute | solution.py:46
  35.1 13.6 %collective-permute-start.5 = (bf16[256,512]{1,0:T(8,128)(2,1)S(1)}, bf16[256,512]{1,0:T(8,128)(2,1)S(1)}, u32[]{:S(2)}, u32[]{:S(2)}) collective-permute-start(bf16[256,512]{1,0:T(8,128)(2,1)S(1)} %collective-permute-done.1), channel_id=1, source_target_pairs={{0,4},{4,8},{8,12},{12,14},{14,10},{10,6},{6,2},{2,0},{1,5},{5,9},... | collective-permute-start | bytes 786440 | tf_op jit(solution)/shard_map/ppermute | solution.py:46
  40.9 10.3 %slice-start.1 = ((s8[8388608]{0:T(1024)(128)(4,1)}), s8[4194304]{0:T(1024)(128)(4,1)S(1)}, s32[]{:S(2)}) async-start(s8[8388608]{0:T(1024)(128)(4,1)} %bitcast.104), calls=%async_computation.2 | async-start | bytes 8388608
  43.1 11.2 %collective-permute-start.10 = (bf16[256,512]{1,0:T(8,128)(2,1)S(1)}, bf16[256,512]{1,0:T(8,128)(2,1)S(1)}, u32[]{:S(2)}, u32[]{:S(2)}) collective-permute-start(bf16[256,512]{1,0:T(8,128)(2,1)S(1)} %collective-permute-done.6), channel_id=1, source_target_pairs={{0,4},{4,8},{8,12},{12,14},{14,10},{10,6},{6,2},{2,0},{1,5},{5,9},... | collective-permute-start | bytes 786440 | tf_op jit(solution)/shard_map/ppermute | solution.py:46
  44.7 9.6 %collective-permute-start.11 = (bf16[256,512]{1,0:T(8,128)(2,1)S(1)}, bf16[256,512]{1,0:T(8,128)(2,1)S(1)}, u32[]{:S(2)}, u32[]{:S(2)}) collective-permute-start(bf16[256,512]{1,0:T(8,128)(2,1)S(1)} %collective-permute-done.7), channel_id=1, source_target_pairs={{4,0},{8,4},{12,8},{14,12},{10,14},{6,10},{2,6},{0,2},{5,1},{9,5},... | collective-permute-start | bytes 786440 | tf_op jit(solution)/shard_map/ppermute | solution.py:46
  45.2 10.8 %collective-permute-start.12 = (bf16[256,512]{1,0:T(8,128)(2,1)S(1)}, bf16[256,512]{1,0:T(8,128)(2,1)S(1)}, u32[]{:S(2)}, u32[]{:S(2)}) collective-permute-start(bf16[256,512]{1,0:T(8,128)(2,1)S(1)} %collective-permute-done.8), channel_id=1, source_target_pairs={{4,0},{8,4},{12,8},{14,12},{10,14},{6,10},{2,6},{0,2},{5,1},{9,5},... | collective-permute-start | bytes 786440 | tf_op jit(solution)/shard_map/ppermute | solution.py:46
  48.7 8.7 %collective-permute-start.9 = (bf16[256,512]{1,0:T(8,128)(2,1)S(1)}, bf16[256,512]{1,0:T(8,128)(2,1)S(1)}, u32[]{:S(2)}, u32[]{:S(2)}) collective-permute-start(bf16[256,512]{1,0:T(8,128)(2,1)S(1)} %collective-permute-done.5), channel_id=1, source_target_pairs={{0,4},{4,8},{8,12},{12,14},{14,10},{10,6},{6,2},{2,0},{1,5},{5,9},... | collective-permute-start | bytes 786440 | tf_op jit(solution)/shard_map/ppermute | solution.py:46
  57.4 21.5 %collective-permute-start.16 = (bf16[256,512]{1,0:T(8,128)(2,1)S(1)}, bf16[256,512]{1,0:T(8,128)(2,1)S(1)}, u32[]{:S(2)}, u32[]{:S(2)}) collective-permute-start(bf16[256,512]{1,0:T(8,128)(2,1)S(1)} %collective-permute-done.11), channel_id=1, source_target_pairs={{4,0},{8,4},{12,8},{14,12},{10,14},{6,10},{2,6},{0,2},{5,1},{9,5},... | collective-permute-start | bytes 786440 | tf_op jit(solution)/shard_map/ppermute | solution.py:46
  59.0 20.2 %collective-permute-start.15 = (bf16[256,512]{1,0:T(8,128)(2,1)S(1)}, bf16[256,512]{1,0:T(8,128)(2,1)S(1)}, u32[]{:S(2)}, u32[]{:S(2)}) collective-permute-start(bf16[256,512]{1,0:T(8,128)(2,1)S(1)} %collective-permute-done.10), channel_id=1, source_target_pairs={{0,4},{4,8},{8,12},{12,14},{14,10},{10,6},{6,2},{2,0},{1,5},{5,9},... | collective-permute-start | bytes 786440 | tf_op jit(solution)/shard_map/ppermute | solution.py:46
  62.5 16.0 %collective-permute-start.17 = (bf16[256,512]{1,0:T(8,128)(2,1)S(1)}, bf16[256,512]{1,0:T(8,128)(2,1)S(1)}, u32[]{:S(2)}, u32[]{:S(2)}) collective-permute-start(bf16[256,512]{1,0:T(8,128)(2,1)S(1)} %collective-permute-done.12), channel_id=1, source_target_pairs={{4,0},{8,4},{12,8},{14,12},{10,14},{6,10},{2,6},{0,2},{5,1},{9,5},... | collective-permute-start | bytes 786440 | tf_op jit(solution)/shard_map/ppermute | solution.py:46
  64.1 14.1 %collective-permute-start.14 = (bf16[256,512]{1,0:T(8,128)(2,1)S(1)}, bf16[256,512]{1,0:T(8,128)(2,1)S(1)}, u32[]{:S(2)}, u32[]{:S(2)}) collective-permute-start(bf16[256,512]{1,0:T(8,128)(2,1)S(1)} %collective-permute-done.9), channel_id=1, source_target_pairs={{0,4},{4,8},{8,12},{12,14},{14,10},{10,6},{6,2},{2,0},{1,5},{5,9},... | collective-permute-start | bytes 786440 | tf_op jit(solution)/shard_map/ppermute | solution.py:46
  80.1 16.9 %collective-permute-start.21 = (bf16[256,512]{1,0:T(8,128)(2,1)S(1)}, bf16[256,512]{1,0:T(8,128)(2,1)S(1)}, u32[]{:S(2)}, u32[]{:S(2)}) collective-permute-start(bf16[256,512]{1,0:T(8,128)(2,1)S(1)} %collective-permute-done.17), channel_id=1, source_target_pairs={{4,0},{8,4},{12,8},{14,12},{10,14},{6,10},{2,6},{0,2},{5,1},{9,5},... | collective-permute-start | bytes 786440 | tf_op jit(solution)/shard_map/ppermute | solution.py:46
  81.7 11.5 %collective-permute-start.20 = (bf16[256,512]{1,0:T(8,128)(2,1)S(1)}, bf16[256,512]{1,0:T(8,128)(2,1)S(1)}, u32[]{:S(2)}, u32[]{:S(2)}) collective-permute-start(bf16[256,512]{1,0:T(8,128)(2,1)S(1)} %collective-permute-done.16), channel_id=1, source_target_pairs={{4,0},{8,4},{12,8},{14,12},{10,14},{6,10},{2,6},{0,2},{5,1},{9,5},... | collective-permute-start | bytes 786440 | tf_op jit(solution)/shard_map/ppermute | solution.py:46
  83.3 8.4 %collective-permute-start.19 = (bf16[256,512]{1,0:T(8,128)(2,1)S(1)}, bf16[256,512]{1,0:T(8,128)(2,1)S(1)}, u32[]{:S(2)}, u32[]{:S(2)}) collective-permute-start(bf16[256,512]{1,0:T(8,128)(2,1)S(1)} %collective-permute-done.15), channel_id=1, source_target_pairs={{0,4},{4,8},{8,12},{12,14},{14,10},{10,6},{6,2},{2,0},{1,5},{5,9},... | collective-permute-start | bytes 786440 | tf_op jit(solution)/shard_map/ppermute | solution.py:46
  83.7 16.5 %collective-permute-start.18 = (bf16[256,512]{1,0:T(8,128)(2,1)S(1)}, bf16[256,512]{1,0:T(8,128)(2,1)S(1)}, u32[]{:S(2)}, u32[]{:S(2)}) collective-permute-start(bf16[256,512]{1,0:T(8,128)(2,1)S(1)} %collective-permute-done.14), channel_id=1, source_target_pairs={{0,4},{4,8},{8,12},{12,14},{14,10},{10,6},{6,2},{2,0},{1,5},{5,9},... | collective-permute-start | bytes 786440 | tf_op jit(solution)/shard_map/ppermute | solution.py:46
  91.6 10.8 %collective-permute-start.23 = (bf16[256,512]{1,0:T(8,128)(2,1)S(1)}, bf16[256,512]{1,0:T(8,128)(2,1)S(1)}, u32[]{:S(2)}, u32[]{:S(2)}) collective-permute-start(bf16[256,512]{1,0:T(8,128)(2,1)S(1)} %collective-permute-done.19), channel_id=1, source_target_pairs={{0,4},{4,8},{8,12},{12,14},{14,10},{10,6},{6,2},{2,0},{1,5},{5,9},... | collective-permute-start | bytes 786440 | tf_op jit(solution)/shard_map/ppermute | solution.py:46
  93.2 10.9 %collective-permute-start.24 = (bf16[256,512]{1,0:T(8,128)(2,1)S(1)}, bf16[256,512]{1,0:T(8,128)(2,1)S(1)}, u32[]{:S(2)}, u32[]{:S(2)}) collective-permute-start(bf16[256,512]{1,0:T(8,128)(2,1)S(1)} %collective-permute-done.20), channel_id=1, source_target_pairs={{4,0},{8,4},{12,8},{14,12},{10,14},{6,10},{2,6},{0,2},{5,1},{9,5},... | collective-permute-start | bytes 786440 | tf_op jit(solution)/shard_map/ppermute | solution.py:46
  97.0 10.7 %collective-permute-start.25 = (bf16[256,512]{1,0:T(8,128)(2,1)S(1)}, bf16[256,512]{1,0:T(8,128)(2,1)S(1)}, u32[]{:S(2)}, u32[]{:S(2)}) collective-permute-start(bf16[256,512]{1,0:T(8,128)(2,1)S(1)} %collective-permute-done.21), channel_id=1, source_target_pairs={{4,0},{8,4},{12,8},{14,12},{10,14},{6,10},{2,6},{0,2},{5,1},{9,5},... | collective-permute-start | bytes 786440 | tf_op jit(solution)/shard_map/ppermute | solution.py:46
  100.2 10.7 %collective-permute-start.22 = (bf16[256,512]{1,0:T(8,128)(2,1)S(1)}, bf16[256,512]{1,0:T(8,128)(2,1)S(1)}, u32[]{:S(2)}, u32[]{:S(2)}) collective-permute-start(bf16[256,512]{1,0:T(8,128)(2,1)S(1)} %collective-permute-done.18), channel_id=1, source_target_pairs={{0,4},{4,8},{8,12},{12,14},{14,10},{10,6},{6,2},{2,0},{1,5},{5,9},... | collective-permute-start | bytes 786440 | tf_op jit(solution)/shard_map/ppermute | solution.py:46
  102.4 15.3 %collective-permute-start.27 = (bf16[256,512]{1,0:T(8,128)(2,1)S(1)}, bf16[256,512]{1,0:T(8,128)(2,1)S(1)}, u32[]{:S(2)}, u32[]{:S(2)}) collective-permute-start(bf16[256,512]{1,0:T(8,128)(2,1)S(1)} %collective-permute-done.23), channel_id=1, source_target_pairs={{0,4},{4,8},{8,12},{12,14},{14,10},{10,6},{6,2},{2,0},{1,5},{5,9},... | collective-permute-start | bytes 786440 | tf_op jit(solution)/shard_map/ppermute | solution.py:46
  104.1 12.1 %collective-permute-start.28 = (bf16[256,512]{1,0:T(8,128)(2,1)S(1)}, bf16[256,512]{1,0:T(8,128)(2,1)S(1)}, u32[]{:S(2)}, u32[]{:S(2)}) collective-permute-start(bf16[256,512]{1,0:T(8,128)(2,1)S(1)} %collective-permute-done.24), channel_id=1, source_target_pairs={{4,0},{8,4},{12,8},{14,12},{10,14},{6,10},{2,6},{0,2},{5,1},{9,5},... | collective-permute-start | bytes 786440 | tf_op jit(solution)/shard_map/ppermute | solution.py:46
  107.6 7.0 %collective-permute-start.29 = (bf16[256,512]{1,0:T(8,128)(2,1)S(1)}, bf16[256,512]{1,0:T(8,128)(2,1)S(1)}, u32[]{:S(2)}, u32[]{:S(2)}) collective-permute-start(bf16[256,512]{1,0:T(8,128)(2,1)S(1)} %collective-permute-done.25), channel_id=1, source_target_pairs={{4,0},{8,4},{12,8},{14,12},{10,14},{6,10},{2,6},{0,2},{5,1},{9,5},... | collective-permute-start | bytes 786440 | tf_op jit(solution)/shard_map/ppermute | solution.py:46
  110.9 8.4 %collective-permute-start.26 = (bf16[256,512]{1,0:T(8,128)(2,1)S(1)}, bf16[256,512]{1,0:T(8,128)(2,1)S(1)}, u32[]{:S(2)}, u32[]{:S(2)}) collective-permute-start(bf16[256,512]{1,0:T(8,128)(2,1)S(1)} %collective-permute-done.22), channel_id=1, source_target_pairs={{0,4},{4,8},{8,12},{12,14},{14,10},{10,6},{6,2},{2,0},{1,5},{5,9},... | collective-permute-start | bytes 786440 | tf_op jit(solution)/shard_map/ppermute | solution.py:46
  117.7 3.9 %copy-start.3 = (s32[4]{0:T(128)S(1)}, s32[4]{0:T(128)}, u32[]{:S(2)}) copy-start(s32[4]{0:T(128)} %param.13) | copy-start | bytes 52
  121.3 2.9 %collective-permute-start.30 = (bf16[1024,512]{1,0:T(8,128)(2,1)S(1)}, bf16[1024,512]{1,0:T(8,128)(2,1)}, u32[]{:S(2)}, u32[]{:S(2)}) collective-permute-start(bf16[1024,512]{1,0:T(8,128)(2,1)S(1)} %pad_maximum_fusion.1), channel_id=1, source_target_pairs={{0,1},{1,0},{2,3},{3,2},{4,5},{5,4},{6,7},{7,6},{8,9},{9,8},{10,11... | collective-permute-start | bytes 3145736 | tf_op jit(solution)/shard_map/ppermute | solution.py:106
  121.6 5.6 %copy-start.1 = (bf16[512,1024]{1,0:T(8,128)(2,1)S(1)}, bf16[512,1024]{1,0:T(8,128)(2,1)}, u32[]{:S(2)}) copy-start(bf16[512,1024]{1,0:T(8,128)(2,1)} %param.12) | copy-start | bytes 3145732
  126.5 9.3 %copy-start.2 = (bf16[512,1024]{1,0:T(8,128)(2,1)S(1)}, bf16[512,1024]{1,0:T(8,128)(2,1)}, u32[]{:S(2)}) copy-start(bf16[512,1024]{1,0:T(8,128)(2,1)} %param.12) | copy-start | bytes 3145732
  131.0 14.3 %all-to-all-start = ((f32[8,72,128]{2,1,0:T(8,128)}), f32[8,72,128]{2,1,0:T(8,128)S(1)}, u32[]{:S(2)}, u32[]{:S(2)}) async-start(f32[8,72,128]{2,1,0:T(8,128)} %select_maximum_fusion), calls=%async_computation | async-start | bytes 589824 | tf_op jit(solution)/shard_map/all_to_all | solution.py:127
  145.8 3.8 %collective-permute-start.31 = (bf16[1,64,128]{2,1,0:T(8,128)(2,1)S(1)}, bf16[1,64,128]{2,1,0:T(8,128)(2,1)S(1)}, u32[]{:S(2)}, u32[]{:S(2)}) collective-permute-start(bf16[1,64,128]{2,1,0:T(8,128)(2,1)S(1)} %fusion.185), channel_id=1, source_target_pairs={{0,2},{2,0},{4,6},{6,4},{8,10},{10,8},{12,14},{14,12},{1,3},{3,1},... | collective-permute-start | bytes 49160 | tf_op jit(solution)/shard_map/ppermute | solution.py:141
  149.6 4.0 %collective-permute-start.32 = (bf16[2,64,128]{2,1,0:T(8,128)(2,1)S(1)}, bf16[2,64,128]{2,1,0:T(8,128)(2,1)S(1)}, u32[]{:S(2)}, u32[]{:S(2)}) collective-permute-start(bf16[2,64,128]{2,1,0:T(8,128)(2,1)S(1)} %pad_maximum_fusion.7), channel_id=1, source_target_pairs={{0,4},{2,6},{4,0},{6,2},{8,12},{10,14},{12,8},{14,10},{1,5},{3,7},... | collective-permute-start | bytes 98312 | tf_op jit(solution)/shard_map/ppermute | solution.py:141
  153.6 5.2 %collective-permute-start.33 = (bf16[4,64,128]{2,1,0:T(8,128)(2,1)S(1)}, bf16[4,64,128]{2,1,0:T(8,128)(2,1)S(1)}, u32[]{:S(2)}, u32[]{:S(2)}) collective-permute-start(bf16[4,64,128]{2,1,0:T(8,128)(2,1)S(1)} %pad_maximum_fusion.6), channel_id=1, source_target_pairs={{0,8},{2,10},{4,12},{6,14},{8,0},{10,2},{12,4},{14,6},{1,9},{3,11}... | collective-permute-start | bytes 196616 | tf_op jit(solution)/shard_map/ppermute | solution.py:141
  159.0 1.4 collective-permute-start.34

commit v3 on v2

--- a/solution.py
+++ b/solution.py
@@ -1,6 +1,8 @@
 import jax
 import jax.numpy as jnp
 from jax import lax
+from jax.experimental import pallas as pl
+from jax.experimental.pallas import tpu as pltpu
 from jax.sharding import Mesh, PartitionSpec as P
 
 QH = 64
@@ -16,44 +18,111 @@
     return jnp.dot(a, b, preferred_element_type=F32)
 
 
-def project(tokens, theirs, block):
+def add_pieces(tokens, theirs, pieces, total, core=None):
+    tok_rows = tokens.shape[0]
+    depth, width = pieces[0][1].shape
+    count = len(pieces)
+    last = core is not None
+    places = jnp.stack([start for start, _ in pieces] + ([core * tok_rows, (1 - core) * tok_rows] if last else []))
+
+    def kernel(places_ref, mine_ref, theirs_ref, *refs):
+        parts = refs[:count]
+        total_ref, out_ref, mark_ref, columns, sems = refs[count:] if total is not None else (None,) + refs[count:]
+        copies = []
+        for k in range(count):
+            for j, source in enumerate((mine_ref, theirs_ref)):
+                start = pl.multiple_of(places_ref[k], 128)
+                copy = pltpu.make_async_copy(source.at[:, pl.ds(start, depth)], columns.at[j, k], sems.at[j, k])
+                copy.start()
+                copies.append(copy)
+        sums = [None, None]
+        for k in range(count):
+            for j in range(2):
+                copies[2 * k + j].wait()
+                term = mm(columns[j, k], parts[k][...])
+                rows = pl.ds(j * tok_rows, tok_rows)
+                if k == 0:
+                    before = None if total is None else total_ref[rows, :]
+                else:
+                    before = sums[j]
+                sums[j] = term if before is None else before + term
+        for j in range(2):
+            if last:
+                out_ref[pl.ds(pl.multiple_of(places_ref[count + j], tok_rows), tok_rows), :] = sums[j].astype(BF)
+            else:
+                out_ref[pl.ds(j * tok_rows, tok_rows), :] = sums[j]
+        mark_ref[...] = jnp.zeros_like(mark_ref)
+
+    in_vmem = pl.BlockSpec(memory_space=pltpu.VMEM)
+    in_hbm = pl.BlockSpec(memory_space=pltpu.HBM)
+    sums = [] if total is None else [total]
+    return pl.pallas_call(
+        kernel,
+        out_shape=(
+            jax.ShapeDtypeStruct((2 * tok_rows, width), BF if last else F32),
+            jax.ShapeDtypeStruct((8, 128), F32),
+        ),
+        in_specs=[pl.BlockSpec(memory_space=pltpu.SMEM), in_hbm, in_hbm] + [in_vmem] * (count + len(sums)),
+        out_specs=(in_vmem, in_vmem),
+        scratch_shapes=[
+            pltpu.VMEM((2, count, tok_rows, depth), BF),
+            pltpu.SemaphoreType.DMA((2, count)),
+        ],
+        compiler_params=pltpu.CompilerParams(vmem_limit_bytes=48 * 2**20),
+        cost_estimate=pl.CostEstimate(
+            flops=4 * tok_rows * depth * width * count,
+            bytes_accessed=4 * tok_rows * depth * count,
+            transcendentals=0,
+        ),
+    )(places, tokens, theirs, *[part for _, part in pieces], *sums)
+
+
+def project(tokens, key_down, value_down):
     chips = lax.axis_size("chip")
     chip = lax.axis_index("chip")
-    rows = block.shape[0]
+    core = lax.axis_index("core")
+    first = core == 0
+    shard = key_down.shape[0]
+    rows = CORES * shard
+    own = jnp.where(first, key_down, value_down)
+    got = lax.ppermute(jnp.where(first, value_down, key_down), "core", SWAP)
     if chips > 8:
+        theirs = lax.ppermute(tokens, "core", SWAP)
+        block = jnp.concatenate([jnp.where(first, own, got), jnp.where(first, got, own)], 0)
         full = lax.all_gather(block, "chip", axis=0, tiled=True)
-        return mm(tokens, full), mm(theirs, full)
+        mine, other = mm(tokens, full).astype(BF), mm(theirs, full).astype(BF)
+        return jnp.concatenate([jnp.where(first, mine, other), jnp.where(first, other, mine)], 0)
     cycle = list(range(0, chips, 2)) + list(range(chips - 1, 0, -2))
     last = chips - 1
     place = jnp.where(chip & 1 == 0, chip >> 1, last - (chip >> 1))
     chains = 2
-    piece = rows // (2 * chains)
+    piece = shard // chains
     right = [(cycle[i], cycle[(i + 1) % chips]) for i in range(chips)]
     left = [(b, a) for a, b in right]
-
-    def block_of(spot):
+    ways = [right] * chains + [left] * chains
+
+    def start_of(k, step):
+        spot = place - step if k < chains else place + step
         spot = jnp.where(spot < 0, spot + chips, jnp.where(spot > last, spot - chips, spot))
-        return jnp.where(spot < chips // 2, 2 * spot, 2 * (last - spot) + 1) * rows
-
-    def term(x, start, part):
-        return mm(lax.dynamic_slice_in_dim(x, start, part.shape[0], 1, allow_negative_indices=False), part)
-
-    held = [block[k * piece : (k + 1) * piece] for k in range(2 * chains)]
-    todo = [(chip * rows, block)]
-    mine_sum = theirs_sum = 0.0
+        source = jnp.where(spot < chips // 2, 2 * spot, 2 * (last - spot) + 1)
+        return source * rows + (core if k < chains else 1 - core) * shard + k % chains * piece
+
+    held = [own[k * piece : (k + 1) * piece] for k in range(chains)]
+    got, tokens_later = lax.optimization_barrier((got, tokens))
+    held += [got[k * piece : (k + 1) * piece] for k in range(chains)]
+    theirs = lax.ppermute(tokens_later, "core", SWAP)
+    steps = [[(start_of(k, 0), held[k]) for k in range(2 * chains)]]
+    total = None
+    mark = None
     for step in range(1, chips):
         for k in range(2 * chains):
-            held[k] = lax.ppermute(held[k], "chip", right if k < chains else left)
-        if step == min(3, last):
-            held, theirs = lax.optimization_barrier((held, theirs))
-        for k in range(2 * chains):
-            todo.append((block_of(place - step if k < chains else place + step) + k * piece, held[k]))
-        if step >= min(3, last):
-            for start, part in todo:
-                mine_sum = mine_sum + term(tokens, start, part)
-                theirs_sum = theirs_sum + term(theirs, start, part)
-            todo = []
-    return mine_sum, theirs_sum
+            if mark is not None:
+                held[k], _ = lax.optimization_barrier((held[k], mark))
+            held[k] = lax.ppermute(held[k], "chip", ways[k])
+        steps.append([(start_of(k, step), held[k]) for k in range(2 * chains)])
+        while steps and (step >= 3 and len(steps) > 1):
+            total, mark = add_pieces(tokens, theirs, steps.pop(0), total)
+    return add_pieces(tokens, theirs, steps.pop(0), total, core)[0]
 
 
 def on_device(tokens, key_down, value_down, key_up, value_up, prompt_lens, queries, new_latent):
@@ -71,11 +140,7 @@
     rows = pairs * heads * group
     share = rows // chips
 
-    theirs = lax.ppermute(tokens, "core", SWAP)
-    own_part = jnp.where(first, key_down, value_down)
-    got_part = lax.ppermute(jnp.where(first, value_down, key_down), "core", SWAP)
-    block = jnp.concatenate([jnp.where(first, own_part, got_part), jnp.where(first, got_part, own_part)], 0)
-    mine_sum, theirs_sum = project(tokens, theirs, block)
+    have = project(tokens, key_down, value_down)
 
     query = lax.dynamic_index_in_dim(
         queries.reshape(steps_count, req_count, CORES, heads * group * DH), core, 2, keepdims=False
@@ -100,9 +165,6 @@
     fresh_total = my_share(fresh_total.reshape(rows))
     fresh_summed = my_share(fresh_summed.reshape(rows, DH))
 
-    mine = mine_sum.astype(BF)
-    other = theirs_sum.astype(BF)
-    have = jnp.concatenate([jnp.where(first, mine, other), jnp.where(first, other, mine)], 0)
     got = lax.ppermute(have, "core", SWAP)
     key_latent = jnp.where(first, have, got)
     value_latent = jnp.where(first, got, have)

time: 163 us -> 145 us (0.89)
  matrix products: 61.9 us -> 5.45 us
  Pallas kernels: 0 us -> 35.4 us
  local copies, waits for them, and re-layouts: 7.2 us -> 13.8 us
  waiting for transfers between devices: 47 us -> 42.8 us
  starting transfers between devices: 39.4 us -> 41.9 us
    dot_general x62 -> x4, matrix products: 57.7 us -> 3.12 us  [mm(): return jnp.dot(a, b, preferred_element_type=F32)]
    pallas_call x0 -> x8, Pallas kernels: none -> 35.4 us  [add_pieces(): pl.pallas_call(kernel, out_shape=(jax.ShapeDtypeStruct((2 * tok_rows, wid...]
    unnamed x12 -> x16, local copies, waits for them, and re-layouts: 0.04 us -> 6.47 us
    ppermute x30, waiting for transfers between devices: 26.9 us -> 21.7 us  [the longest x28 20.1 us: project(): held[k] = lax.ppermute(held[k], 'chip', ways[k])]
    ppermute x30, starting transfers between devices: 31 us -> 32.8 us  [the longest x28 31.9 us: project(): held[k] = lax.ppermute(held[k], 'chip', ways[k])]
  transfers between devices with their start and end apart: 36 -> 36, of which waited for: 15 -> 15; matrix products, arithmetic and copies ran while one was open for 39% -> 6% of each run, Pallas kernels for 0% -> 21%
where the time goes in v3:
time: 145 us; the launch traced here: 144 us
  waiting for transfers between devices  42.8 us (30%)
  starting transfers between devices  41.9 us (29%)
  Pallas kernels  35.4 us (24%)
  local copies, waits for them, and re-layouts  13.8 us (10%)
  matrix products  5.45 us (4%)
  other arithmetic  4.35 us (3%)
    pallas_call x8, Pallas kernels, add_pieces(): pl.pallas_call(kernel, out_shape=(jax.ShapeDtypeStruct((2 * tok_rows, wid...  35.4 us
    ppermute x28, starting transfers between devices, project(): held[k] = lax.ppermute(held[k], 'chip', ways[k])  31.9 us
    ppermute x28, waiting for transfers between devices, project(): held[k] = lax.ppermute(held[k], 'chip', ways[k])  20.1 us
    ppermute x3, waiting for transfers between devices, on_device(): away = lax.ppermute(whole, 'chip', [(c, c ^ span) for c in range(chips)])  9.12 us
    all_to_all x1, waiting for transfers between devices, on_device(): lax.all_to_all(sending, 'chip', split_axis=0, concat_axis=0, tiled=True)  8.95 us
    unnamed x16, local copies, waits for them, and re-layouts  6.47 us
    all_to_all x1, starting transfers between devices, on_device(): lax.all_to_all(sending, 'chip', split_axis=0, concat_axis=0, tiled=True)  5 us
    ppermute x3, starting transfers between devices, on_device(): away = lax.ppermute(whole, 'chip', [(c, c ^ span) for c in range(chips)])  3.93 us
  transfers between devices with their start and end apart: 36, of which 15 were waited for; matrix products, arithmetic and copies ran while one was open for 6% of the time, Pallas kernels for 21%

profile of v3, /device:TPU:0, one launch (start us, length us, event | category | flops | bytes accessed | tf_op | source)
XLA Modules:
  0.0 144.1 jit_solution(11419728214146379256)
XLA Ops:
  0.0 1.4 broadcast_select_fusion
  1.4 0.5 collective-permute-start
  1.9 1.5 %collective-permute-done = bf16[512,512]{1,0:T(8,128)(2,1)S(1)} collective-permute-done((bf16[512,512]{1,0:T(8,128)(2,1)S(1)}, bf16[512,512]{1,0:T(8,128)(2,1)S(1)}, u32[]{:S(2)}, u32[]{:S(2)}) %collective-permute-start) | collective-permute-done | bytes 524320 | tf_op jit(solution)/shard_map/ppermute | solution.py:88
  3.8 2.8 %collective-permute-start.2 = (bf16[256,512]{1,0:T(8,128)(2,1)S(1)}, bf16[256,512]{1,0:T(8,128)(2,1)S(1)}, u32[]{:S(2)}, u32[]{:S(2)}) collective-permute-start(bf16[256,512]{1,0:T(8,128)(2,1)S(1)} %get-tuple-element.74.refs_0_), channel_id=1, source_target_pairs={{0,4},{4,8},{8,12},{12,14},{14,10},{10,6},{6,2},{2,0},{1,5},{5,9},... | collective-permute-start | bytes 786440 | tf_op jit(solution)/shard_map/ppermute | solution.py:121
  6.6 1.6 %collective-permute-start.5 = (bf16[256,512]{1,0:T(8,128)(2,1)S(1)}, bf16[256,512]{1,0:T(8,128)(2,1)S(1)}, u32[]{:S(2)}, u32[]{:S(2)}) collective-permute-start(bf16[256,512]{1,0:T(8,128)(2,1)S(1)} %get-tuple-element.73.refs_1_), channel_id=1, source_target_pairs={{0,4},{4,8},{8,12},{12,14},{14,10},{10,6},{6,2},{2,0},{1,5},{5,9},... | collective-permute-start | bytes 786440 | tf_op jit(solution)/shard_map/ppermute | solution.py:121
  8.2 0.5 collective-permute-start.9
  8.8 4.9 %collective-permute-done.2.refs_0_ = bf16[256,512]{1,0:T(8,128)(2,1)S(1)} collective-permute-done((bf16[256,512]{1,0:T(8,128)(2,1)S(1)}, bf16[256,512]{1,0:T(8,128)(2,1)S(1)}, u32[]{:S(2)}, u32[]{:S(2)}) %collective-permute-start.2) | collective-permute-done | bytes 262176 | tf_op jit(solution)/shard_map/ppermute | solution.py:121
  13.7 2.0 %collective-permute-start.3 = (bf16[256,512]{1,0:T(8,128)(2,1)S(1)}, bf16[256,512]{1,0:T(8,128)(2,1)S(1)}, u32[]{:S(2)}, u32[]{:S(2)}) collective-permute-start(bf16[256,512]{1,0:T(8,128)(2,1)S(1)} %collective-permute-done.2.refs_0_), channel_id=1, source_target_pairs={{0,4},{4,8},{8,12},{12,14},{14,10},{10,6},{6,2},{2,0},{1,5},{5,9},... | collective-permute-start | bytes 786440 | tf_op jit(solution)/shard_map/ppermute | solution.py:121
  15.7 3.6 %collective-permute-done.5.refs_1_ = bf16[256,512]{1,0:T(8,128)(2,1)S(1)} collective-permute-done((bf16[256,512]{1,0:T(8,128)(2,1)S(1)}, bf16[256,512]{1,0:T(8,128)(2,1)S(1)}, u32[]{:S(2)}, u32[]{:S(2)}) %collective-permute-start.5) | collective-permute-done | bytes 262176 | tf_op jit(solution)/shard_map/ppermute | solution.py:121
  19.3 2.0 %collective-permute-start.6 = (bf16[256,512]{1,0:T(8,128)(2,1)S(1)}, bf16[256,512]{1,0:T(8,128)(2,1)}, u32[]{:S(2)}, u32[]{:S(2)}) collective-permute-start(bf16[256,512]{1,0:T(8,128)(2,1)S(1)} %collective-permute-done.5.refs_1_), channel_id=1, source_target_pairs={{0,4},{4,8},{8,12},{12,14},{14,10},{10,6},{6,2},{2,0},{1,5},{5,9},... | collective-permute-start | bytes 786440 | tf_op jit(solution)/shard_map/ppermute | solution.py:121
  21.4 0.5 collective-permute-done.7.refs_2_
  21.9 1.4 collective-permute-start.8
  23.6 6.8 %collective-permute-done.6.refs_1_ = bf16[256,512]{1,0:T(8,128)(2,1)} collective-permute-done((bf16[256,512]{1,0:T(8,128)(2,1)S(1)}, bf16[256,512]{1,0:T(8,128)(2,1)}, u32[]{:S(2)}, u32[]{:S(2)}) %collective-permute-start.6) | collective-permute-done | bytes 262176 | tf_op jit(solution)/shard_map/ppermute | solution.py:121
  30.3 1.8 %collective-permute-start.12 = (bf16[256,512]{1,0:T(8,128)(2,1)}, bf16[256,512]{1,0:T(8,128)(2,1)}, u32[]{:S(2)}, u32[]{:S(2)}) collective-permute-start(bf16[256,512]{1,0:T(8,128)(2,1)} %collective-permute-done.6.refs_1_), channel_id=1, source_target_pairs={{0,4},{4,8},{8,12},{12,14},{14,10},{10,6},{6,2},{2,0},{1,5},{5,9},... | collective-permute-start | bytes 786440 | tf_op jit(solution)/shard_map/ppermute | solution.py:121
  32.1 1.6 %collective-permute-start.4 = (bf16[256,512]{1,0:T(8,128)(2,1)S(1)}, bf16[256,512]{1,0:T(8,128)(2,1)}, u32[]{:S(2)}, u32[]{:S(2)}) collective-permute-start(bf16[256,512]{1,0:T(8,128)(2,1)S(1)} %collective-permute-done.3.refs_0_), channel_id=1, source_target_pairs={{0,4},{4,8},{8,12},{12,14},{14,10},{10,6},{6,2},{2,0},{1,5},{5,9},... | collective-permute-start | bytes 786440 | tf_op jit(solution)/shard_map/ppermute | solution.py:121
  34.5 1.5 %collective-permute-start.14 = (bf16[256,512]{1,0:T(8,128)(2,1)}, bf16[256,512]{1,0:T(8,128)(2,1)}, u32[]{:S(2)}, u32[]{:S(2)}) collective-permute-start(bf16[256,512]{1,0:T(8,128)(2,1)} %collective-permute-done.10.refs_3_), channel_id=1, source_target_pairs={{4,0},{8,4},{12,8},{14,12},{10,14},{6,10},{2,6},{0,2},{5,1},{9,5},... | collective-permute-start | bytes 786440 | tf_op jit(solution)/shard_map/ppermute | solution.py:121
  36.0 3.9 %shard_map.82 = (f32[1024,512]{1,0:T(8,128)S(1)}, f32[8,128]{1,0:T(8,128)}) custom-call(s32[4]{0:T(128)S(1)} %pad_add_fusion.2.places_ref, bf16[512,8192]{1,0:T(8,128)(2,1)} %mine_ref.15, bf16[512,8192]{1,0:T(8,128)(2,1)} %collective-permute-done.1.theirs_ref, bf16[256,512]{1,0:T(8,128)(2,1)S(1)} %get-tuple-element.74.refs_0_, ...), custom_call_target="tpu_custom_call" | custom-call | flops 1073741824 | bytes 2097152 | tf_op jit(solution)/shard_map/pallas_call | solution.py:59
  39.9 4.0 %shard_map.83 = (f32[1024,512]{1,0:T(8,128)S(1)}, f32[8,128]{1,0:T(8,128)}) custom-call(s32[4]{0:T(128)S(1)} %pad_add_fusion.1.places_ref, bf16[512,8192]{1,0:T(8,128)(2,1)} %mine_ref.15, bf16[512,8192]{1,0:T(8,128)(2,1)} %collective-permute-done.1.theirs_ref, bf16[256,512]{1,0:T(8,128)(2,1)S(1)} %collective-permute-done.2.refs_0_, ...), custom_call_target="tpu_custom_call" | custom-call | flops 1073741824 | bytes 2097152 | tf_op jit(solution)/shard_map/pallas_call | solution.py:59
  43.8 4.5 %shard_map.84 = (f32[1024,512]{1,0:T(8,128)S(1)}, f32[8,128]{1,0:T(8,128)}) custom-call(s32[4]{0:T(128)S(1)} %pad_add_fusion.places_ref, bf16[512,8192]{1,0:T(8,128)(2,1)} %mine_ref.15, bf16[512,8192]{1,0:T(8,128)(2,1)} %collective-permute-done.1.theirs_ref, bf16[256,512]{1,0:T(8,128)(2,1)S(1)} %collective-permute-done.3.refs_0_, ...), custom_call_target="tpu_custom_call" | custom-call | flops 1073741824 | bytes 2097152 | tf_op jit(solution)/shard_map/pallas_call | solution.py:59
  48.4 1.7 %collective-permute-start.18 = (bf16[256,512]{1,0:T(8,128)(2,1)}, bf16[256,512]{1,0:T(8,128)(2,1)}, u32[]{:S(2)}, u32[]{:S(2)}) collective-permute-start(bf16[256,512]{1,0:T(8,128)(2,1)} %collective-permute-done.14.refs_3_), channel_id=1, source_target_pairs={{4,0},{8,4},{12,8},{14,12},{10,14},{6,10},{2,6},{0,2},{5,1},{9,5},... | collective-permute-start | bytes 786440 | tf_op jit(solution)/shard_map/ppermute | solution.py:121
  50.1 1.5 %collective-permute-start.17 = (bf16[256,512]{1,0:T(8,128)(2,1)}, bf16[256,512]{1,0:T(8,128)(2,1)}, u32[]{:S(2)}, u32[]{:S(2)}) collective-permute-start(bf16[256,512]{1,0:T(8,128)(2,1)} %collective-permute-done.13.refs_2_), channel_id=1, source_target_pairs={{4,0},{8,4},{12,8},{14,12},{10,14},{6,10},{2,6},{0,2},{5,1},{9,5},... | collective-permute-start | bytes 786440 | tf_op jit(solution)/shard_map/ppermute | solution.py:121
  52.6 4.6 %shard_map.85 = (f32[1024,512]{1,0:T(8,128)S(1)}, f32[8,128]{1,0:T(8,128)}) custom-call(s32[4]{0:T(128)S(1)} %pad_add_fusion.3.places_ref, bf16[512,8192]{1,0:T(8,128)(2,1)} %mine_ref.15, bf16[512,8192]{1,0:T(8,128)(2,1)} %collective-permute-done.1.theirs_ref, bf16[256,512]{1,0:T(8,128)(2,1)} %collective-permute-done.4.refs_0_, ...), custom_call_target="tpu_custom_call" | custom-call | flops 1073741824 | bytes 2097152 | tf_op jit(solution)/shard_map/pallas_call | solution.py:59
  57.2 1.4 copy-done.1
  58.6 1.7 %collective-permute-start.22 = (bf16[256,512]{1,0:T(8,128)(2,1)}, bf16[256,512]{1,0:T(8,128)(2,1)}, u32[]{:S(2)}, u32[]{:S(2)}) collective-permute-start(bf16[256,512]{1,0:T(8,128)(2,1)} %collective-permute-done.18.refs_3_), channel_id=1, source_target_pairs={{4,0},{8,4},{12,8},{14,12},{10,14},{6,10},{2,6},{0,2},{5,1},{9,5},... | collective-permute-start | bytes 786440 | tf_op jit(solution)/shard_map/ppermute | solution.py:121
  60.3 1.7 %collective-permute-done.17.refs_2_ = bf16[256,512]{1,0:T(8,128)(2,1)} collective-permute-done((bf16[256,512]{1,0:T(8,128)(2,1)}, bf16[256,512]{1,0:T(8,128)(2,1)}, u32[]{:S(2)}, u32[]{:S(2)}) %collective-permute-start.17) | collective-permute-done | bytes 262176 | tf_op jit(solution)/shard_map/ppermute | solution.py:121
  62.0 1.6 %collective-permute-start.21 = (bf16[256,512]{1,0:T(8,128)(2,1)}, bf16[256,512]{1,0:T(8,128)(2,1)}, u32[]{:S(2)}, u32[]{:S(2)}) collective-permute-start(bf16[256,512]{1,0:T(8,128)(2,1)} %collective-permute-done.17.refs_2_), channel_id=1, source_target_pairs={{4,0},{8,4},{12,8},{14,12},{10,14},{6,10},{2,6},{0,2},{5,1},{9,5},... | collective-permute-start | bytes 786440 | tf_op jit(solution)/shard_map/ppermute | solution.py:121
  64.0 0.5 collective-permute-done.11.refs_0_
  64.5 0.9 collective-permute-start.15
  65.5 1.6 %copy-done.2 = f32[1024,512]{1,0:T(8,128)S(1)} copy-done((f32[1024,512]{1,0:T(8,128)S(1)}, f32[1024,512]{1,0:T(8,128)}, u32[]{:S(2)}) %copy-start.2) | copy-done | bytes 2097176
  67.1 4.6 %shard_map.86 = (f32[1024,512]{1,0:T(8,128)S(1)}, f32[8,128]{1,0:T(8,128)}) custom-call(s32[4]{0:T(128)S(1)} %pad_add_fusion.4.places_ref, bf16[512,8192]{1,0:T(8,128)(2,1)} %mine_ref.15, bf16[512,8192]{1,0:T(8,128)(2,1)} %collective-permute-done.1.theirs_ref, bf16[256,512]{1,0:T(8,128)(2,1)} %collective-permute-done.11.refs_0_, ...), custom_call_target="tpu_custom_call" | custom-call | flops 1073741824 | bytes 2097152 | tf_op jit(solution)/shard_map/pallas_call | solution.py:59
  71.8 1.4 copy-done.3
  73.2 1.1 collective-permute-start.28
  74.3 1.5 %collective-permute-start.26 = (bf16[256,512]{1,0:T(8,128)(2,1)}, bf16[256,512]{1,0:T(8,128)(2,1)}, u32[]{:S(2)}, u32[]{:S(2)}) collective-permute-start(bf16[256,512]{1,0:T(8,128)(2,1)} %collective-permute-done.21.refs_2_), channel_id=1, source_target_pairs={{4,0},{8,4},{12,8},{14,12},{10,14},{6,10},{2,6},{0,2},{5,1},{9,5},... | collective-permute-start | bytes 786440 | tf_op jit(solution)/shard_map/ppermute | solution.py:121
  75.8 0.5 collective-permute-start.24
  76.3 0.9 collective-permute-start.19
  77.3 1.6 %copy-done.4 = f32[1024,512]{1,0:T(8,128)S(1)} copy-done((f32[1024,512]{1,0:T(8,128)S(1)}, f32[1024,512]{1,0:T(8,128)}, u32[]{:S(2)}) %copy-start.4) | copy-done | bytes 2097176
  78.9 4.6 %shard_map.87 = (f32[1024,512]{1,0:T(8,128)S(1)}, f32[8,128]{1,0:T(8,128)}) custom-call(s32[4]{0:T(128)S(1)} %pad_add_fusion.5.places_ref, bf16[512,8192]{1,0:T(8,128)(2,1)} %mine_ref.15, bf16[512,8192]{1,0:T(8,128)(2,1)} %collective-permute-done.1.theirs_ref, bf16[256,512]{1,0:T(8,128)(2,1)} %collective-permute-done.15.refs_0_, ...), custom_call_target="tpu_custom_call" | custom-call | flops 1073741824 | bytes 2097152 | tf_op jit(solution)/shard_map/pallas_call | solution.py:59
  83.6 1.1 collective-permute-start.29
  84.7 2.0 %collective-permute-start.27 = (bf16[256,512]{1,0:T(8,128)(2,1)}, bf16[256,512]{1,0:T(8,128)(2,1)}, u32[]{:S(2)}, u32[]{:S(2)}) collective-permute-start(bf16[256,512]{1,0:T(8,128)(2,1)} %collective-permute-done.26.refs_2_), channel_id=1, source_target_pairs={{4,0},{8,4},{12,8},{14,12},{10,14},{6,10},{2,6},{0,2},{5,1},{9,5},... | collective-permute-start | bytes 786440 | tf_op jit(solution)/shard_map/ppermute | solution.py:121
  86.7 1.7 %collective-permute-done.19.refs_0_ = bf16[256,512]{1,0:T(8,128)(2,1)} collective-permute-done((bf16[256,512]{1,0:T(8,128)(2,1)}, bf16[256,512]{1,0:T(8,128)(2,1)}, u32[]{:S(2)}, u32[]{:S(2)}) %collective-permute-start.19) | collective-permute-done | bytes 262176 | tf_op jit(solution)/shard_map/ppermute | solution.py:121
  88.7 1.9 %reshape.162 = bf16[4,4,2,4096]{3,2,1,0:T(2,128)(2,1)} reshape(bf16[4,4,8192]{2,1,0:T(4,128)(2,1)} %param.14) | data formatting | bytes 524288 | tf_op jit(solution)/shard_map/reshape | solution.py:146
  90.6 1.8 %dynamic-slice_reduce_fusion = bf16[4,4,4096]{2,1,0:T(4,128)(2,1)S(1)} fusion(bf16[4,4,2,4096]{3,2,1,0:T(2,128)(2,1)} %reshape.162, s32[]{:T(128)S(6)} %select_n.346), kind=kLoop, calls=%fused_computation.36 | loop fusion | bytes 262148 | tf_op jit(solution)/shard_map/jit(dynamic_index_in_dim)/dynamic_slice | solution.py:145
  92.4 0.8 reshape.163
  93.4 0.8 reshape.166
  94.3 4.5 %shard_map.88 = (f32[1024,512]{1,0:T(8,128)S(1)}, f32[8,128]{1,0:T(8,128)}) custom-call(s32[4]{0:T(128)S(1)} %pad_add_fusion.6.places_ref, bf16[512,8192]{1,0:T(8,128)(2,1)} %mine_ref.15, bf16[512,8192]{1,0:T(8,128)(2,1)} %collective-permute-done.1.theirs_ref, bf16[256,512]{1,0:T(8,128)(2,1)} %collective-permute-done.19.refs_0_, ...), custom_call_target="tpu_custom_call" | custom-call | flops 1073741824 | bytes 2097152 | tf_op jit(solution)/shard_map/pallas_call | solution.py:59
  98.9 4.6 %shard_map.89 = (bf16[1024,512]{1,0:T(8,128)(2,1)S(1)}, f32[8,128]{1,0:T(8,128)}) custom-call(s32[6]{0:T(128)S(1)} %stack.135.places_ref, bf16[512,8192]{1,0:T(8,128)(2,1)} %mine_ref.15, bf16[512,8192]{1,0:T(8,128)(2,1)} %collective-permute-done.1.theirs_ref, bf16[256,512]{1,0:T(8,128)(2,1)} %collective-permute-done.23.refs_0_, ...), custom_call_target="tpu_custom_call" | custom-call | flops 1073741824 | bytes 2097152 | tf_op jit(solution)/shard_map/pallas_call | solution.py:59
  104.0 0.7 fusion.47
  104.7 1.7 %collective-permute-done.30 = bf16[1024,512]{1,0:T(8,128)(2,1)} collective-permute-done((bf16[1024,512]{1,0:T(8,128)(2,1)S(1)}, bf16[1024,512]{1,0:T(8,128)(2,1)}, u32[]{:S(2)}, u32[]{:S(2)}) %collective-permute-start.30) | collective-permute-done | bytes 1048608 | tf_op jit(solution)/shard_map/ppermute | solution.py:168
  106.4 0.8 convolution_convert_fusion
  107.2 0.6 fusion
  107.8 0.7 fusion.1
  109.0 2.0 %convolution_convert_fusion.1 = bf16[1024,512]{0,1:T(8,128)(2,1)S(1)} fusion(bf16[1024,512]{1,0:T(8,128)(2,1)} %collective-permute-done.30, bf16[1024,512]{1,0:T(8,128)(2,1)S(1)} %get-tuple-element.64, pred[]{:T(512)S(6)} %eq.7, bf16[512,1024]{1,0:T(8,128)(2,1)S(1)} %copy-done.5, s32[]{:T(128)S(6)} %select_n.344), kind=kOutput, calls=%fused_computation.4 | convolution fusion | flops 537919488 | bytes 3670021 | tf_op jit(solution)/shard_map/dot_general | solution.py:18
  111.0 0.7 convolution_bitcast_fusion.1
  112.1 0.7 select_maximum_fusion
  112.8 5.0 %all-to-all-start = ((f32[8,72,128]{2,1,0:T(8,128)}), f32[8,72,128]{2,1,0:T(8,128)S(1)}, u32[]{:S(2)}, u32[]{:S(2)}) async-start(f32[8,72,128]{2,1,0:T(8,128)} %select_maximum_fusion), calls=%async_computation | async-start | bytes 589824 | tf_op jit(solution)/shard_map/all_to_all | solution.py:189
  118.8 8.9 %all-to-all-done = f32[8,72,128]{2,1,0:T(8,128)S(1)} async-done(((f32[8,72,128]{2,1,0:T(8,128)}), f32[8,72,128]{2,1,0:T(8,128)S(1)}, u32[]{:S(2)}, u32[]{:S(2)}) %all-to-all-start) | async-done | bytes 294944 | tf_op jit(solution)/shard_map/all_to_all | solution.py:189
  128.2 1.5 %collective-permute-start.31 = (bf16[1,64,128]{2,1,0:T(8,128)(2,1)S(1)}, bf16[1,64,128]{2,1,0:T(8,128)(2,1)S(1)}, u32[]{:S(2)}, u32[]{:S(2)}) collective-permute-start(bf16[1,64,128]{2,1,0:T(8,128)(2,1)S(1)} %fusion.35), channel_id=1, source_target_pairs={{0,2},{2,0},{4,6},{6,4},{8,10},{10,8},{12,14},{14,12},{1,3},{3,1},... | collective-permute-start | bytes 49160 | tf_op jit(solution)/shard_map/ppermute | solution.py:203
  129.8 2.3 %collective-permute-done.31 = bf16[1,64,128]{2,1,0:T(8,128)(2,1)S(1)} collective-permute-done((bf16[1,64,128]{2,1,0:T(8,128)(2,1)S(1)}, bf16[1,64,128]{2,1,0:T(8,128)(2,1)S(1)}, u32[]{:S(2)}, u32[]{:S(2)}) %collective-permute-start.31) | collective-permute-done | bytes 16416 | tf_op jit(solution)/shard_map/ppermute | solution.py:203
  132.0 1.1 collective-permute-start.32
  133.2 2.9 %collective-permute-done.32 = bf16[2,64,128]{2,1,0:T(8,128)(2,1)S(1)} collective-permute-done((bf16[2,64,128]{2,1,0:T(8,128)(2,1)S(1)}, bf16[2,64,128]{2,1,0:T(8,128)(2,1)S(1)}, u32[]{:S(2)}, u32[]{:S(2)}) %collective-permute-start.32) | collective-permute-done | bytes 32800 | tf_op jit(solution)/shard_map/ppermute | solution.py:203
  136.1 1.3 collective-permute-start.33
  137.3 4.0 %collective-permute-done.33 = bf16[4,64,128]{2,1,0:T(8,128)(2,1)S(1)} collective-permute-done((bf16[4,64,128]{2,1,0:T(8,128)(2,1)S(1)}, bf16[4,64,128]{2,1,0:T(8,128)(2,1)S(1)}, u32[]{:S(2)}, u32[]{:S(2)}) %collective-permute-start.33) | collective-permute-done | bytes 65568 | tf_op jit(solution)/shard_map/ppermute | solution.py:203
  141.5 1.3 collective-permute-done.34
  143.2 0.9 reshape.174
  (96 shorter events, 6.8 us)
Async XLA Ops:
  0.0 103.6 %copy-start = (bf16[512,1024]{1,0:T(8,128)(2,1)S(1)}, bf16[512,1024]{1,0:T(8,128)(2,1)}, u32[]{:S(2)}) copy-start(bf16[512,1024]{1,0:T(8,128)(2,1)} %param.11) | copy-start | bytes 3145732
  1.4 2.1 %collective-permute-start = (bf16[512,512]{1,0:T(8,128)(2,1)S(1)}, bf16[512,512]{1,0:T(8,128)(2,1)S(1)}, u32[]{:S(2)}, u32[]{:S(2)}) collective-permute-start(bf16[512,512]{1,0:T(8,128)(2,1)S(1)} %get-tuple-element.70), channel_id=1, source_target_pairs={{0,1},{1,0},{2,3},{3,2},{4,5},{5,4},{6,7},{7,6},{8,9},{9,8},{10,11... | collective-permute-start | bytes 1572872 | tf_op jit(solution)/shard_map/ppermute | solution.py:88
  3.4 32.6 %collective-permute-start.1 = (bf16[512,8192]{1,0:T(8,128)(2,1)}, bf16[512,8192]{1,0:T(8,128)(2,1)}, u32[]{:S(2)}, u32[]{:S(2)}) collective-permute-start(bf16[512,8192]{1,0:T(8,128)(2,1)} %mine_ref.15), channel_id=1, source_target_pairs={{0,1},{1,0},{2,3},{3,2},{4,5},{5,4},{6,7},{7,6},{8,9},{9,8},{10,11... | collective-permute-start | bytes 25165832 | tf_op jit(solution)/shard_map/ppermute | solution.py:113
  3.8 9.9 %collective-permute-start.2 = (bf16[256,512]{1,0:T(8,128)(2,1)S(1)}, bf16[256,512]{1,0:T(8,128)(2,1)S(1)}, u32[]{:S(2)}, u32[]{:S(2)}) collective-permute-start(bf16[256,512]{1,0:T(8,128)(2,1)S(1)} %get-tuple-element.74.refs_0_), channel_id=1, source_target_pairs={{0,4},{4,8},{8,12},{12,14},{14,10},{10,6},{6,2},{2,0},{1,5},{5,9},... | collective-permute-start | bytes 786440 | tf_op jit(solution)/shard_map/ppermute | solution.py:121
  6.6 12.7 %collective-permute-start.5 = (bf16[256,512]{1,0:T(8,128)(2,1)S(1)}, bf16[256,512]{1,0:T(8,128)(2,1)S(1)}, u32[]{:S(2)}, u32[]{:S(2)}) collective-permute-start(bf16[256,512]{1,0:T(8,128)(2,1)S(1)} %get-tuple-element.73.refs_1_), channel_id=1, source_target_pairs={{0,4},{4,8},{8,12},{12,14},{14,10},{10,6},{6,2},{2,0},{1,5},{5,9},... | collective-permute-start | bytes 786440 | tf_op jit(solution)/shard_map/ppermute | solution.py:121
  8.2 13.1 %collective-permute-start.9 = (bf16[256,512]{1,0:T(8,128)(2,1)S(1)}, bf16[256,512]{1,0:T(8,128)(2,1)S(1)}, u32[]{:S(2)}, u32[]{:S(2)}) collective-permute-start(bf16[256,512]{1,0:T(8,128)(2,1)S(1)} %get-tuple-element.71.refs_3_), channel_id=1, source_target_pairs={{4,0},{8,4},{12,8},{14,12},{10,14},{6,10},{2,6},{0,2},{5,1},{9,5},... | collective-permute-start | bytes 786440 | tf_op jit(solution)/shard_map/ppermute | solution.py:121
  8.7 13.2 %collective-permute-start.7 = (bf16[256,512]{1,0:T(8,128)(2,1)S(1)}, bf16[256,512]{1,0:T(8,128)(2,1)S(1)}, u32[]{:S(2)}, u32[]{:S(2)}) collective-permute-start(bf16[256,512]{1,0:T(8,128)(2,1)S(1)} %get-tuple-element.72.refs_2_), channel_id=1, source_target_pairs={{4,0},{8,4},{12,8},{14,12},{10,14},{6,10},{2,6},{0,2},{5,1},{9,5},... | collective-permute-start | bytes 786440 | tf_op jit(solution)/shard_map/ppermute | solution.py:121
  13.7 18.4 %collective-permute-start.3 = (bf16[256,512]{1,0:T(8,128)(2,1)S(1)}, bf16[256,512]{1,0:T(8,128)(2,1)S(1)}, u32[]{:S(2)}, u32[]{:S(2)}) collective-permute-start(bf16[256,512]{1,0:T(8,128)(2,1)S(1)} %collective-permute-done.2.refs_0_), channel_id=1, source_target_pairs={{0,4},{4,8},{8,12},{12,14},{14,10},{10,6},{6,2},{2,0},{1,5},{5,9},... | collective-permute-start | bytes 786440 | tf_op jit(solution)/shard_map/ppermute | solution.py:121
  19.3 11.0 %collective-permute-start.6 = (bf16[256,512]{1,0:T(8,128)(2,1)S(1)}, bf16[256,512]{1,0:T(8,128)(2,1)}, u32[]{:S(2)}, u32[]{:S(2)}) collective-permute-start(bf16[256,512]{1,0:T(8,128)(2,1)S(1)} %collective-permute-done.5.refs_1_), channel_id=1, source_target_pairs={{0,4},{4,8},{8,12},{12,14},{14,10},{10,6},{6,2},{2,0},{1,5},{5,9},... | collective-permute-start | bytes 786440 | tf_op jit(solution)/shard_map/ppermute | solution.py:121
  21.4 13.1 %collective-permute-start.10 = (bf16[256,512]{1,0:T(8,128)(2,1)S(1)}, bf16[256,512]{1,0:T(8,128)(2,1)}, u32[]{:S(2)}, u32[]{:S(2)}) collective-permute-start(bf16[256,512]{1,0:T(8,128)(2,1)S(1)} %collective-permute-done.9.refs_3_), channel_id=1, source_target_pairs={{4,0},{8,4},{12,8},{14,12},{10,14},{6,10},{2,6},{0,2},{5,1},{9,5},... | collective-permute-start | bytes 786440 | tf_op jit(solution)/shard_map/ppermute | solution.py:121
  21.9 12.1 %collective-permute-start.8 = (bf16[256,512]{1,0:T(8,128)(2,1)S(1)}, bf16[256,512]{1,0:T(8,128)(2,1)}, u32[]{:S(2)}, u32[]{:S(2)}) collective-permute-start(bf16[256,512]{1,0:T(8,128)(2,1)S(1)} %collective-permute-done.7.refs_2_), channel_id=1, source_target_pairs={{4,0},{8,4},{12,8},{14,12},{10,14},{6,10},{2,6},{0,2},{5,1},{9,5},... | collective-permute-start | bytes 786440 | tf_op jit(solution)/shard_map/ppermute | solution.py:121
  30.3 21.3 %collective-permute-start.12 = (bf16[256,512]{1,0:T(8,128)(2,1)}, bf16[256,512]{1,0:T(8,128)(2,1)}, u32[]{:S(2)}, u32[]{:S(2)}) collective-permute-start(bf16[256,512]{1,0:T(8,128)(2,1)} %collective-permute-done.6.refs_1_), channel_id=1, source_target_pairs={{0,4},{4,8},{8,12},{12,14},{14,10},{10,6},{6,2},{2,0},{1,5},{5,9},... | collective-permute-start | bytes 786440 | tf_op jit(solution)/shard_map/ppermute | solution.py:121
  32.1 20.0 %collective-permute-start.4 = (bf16[256,512]{1,0:T(8,128)(2,1)S(1)}, bf16[256,512]{1,0:T(8,128)(2,1)}, u32[]{:S(2)}, u32[]{:S(2)}) collective-permute-start(bf16[256,512]{1,0:T(8,128)(2,1)S(1)} %collective-permute-done.3.refs_0_), channel_id=1, source_target_pairs={{0,4},{4,8},{8,12},{12,14},{14,10},{10,6},{6,2},{2,0},{1,5},{5,9},... | collective-permute-start | bytes 786440 | tf_op jit(solution)/shard_map/ppermute | solution.py:121
  34.0 16.1 %collective-permute-start.13 = (bf16[256,512]{1,0:T(8,128)(2,1)}, bf16[256,512]{1,0:T(8,128)(2,1)}, u32[]{:S(2)}, u32[]{:S(2)}) collective-permute-start(bf16[256,512]{1,0:T(8,128)(2,1)} %collective-permute-done.8.refs_2_), channel_id=1, source_target_pairs={{4,0},{8,4},{12,8},{14,12},{10,14},{6,10},{2,6},{0,2},{5,1},{9,5},... | collective-permute-start | bytes 786440 | tf_op jit(solution)/shard_map/ppermute | solution.py:121
  34.5 13.9 %collective-permute-start.14 = (bf16[256,512]{1,0:T(8,128)(2,1)}, bf16[256,512]{1,0:T(8,128)(2,1)}, u32[]{:S(2)}, u32[]{:S(2)}) collective-permute-start(bf16[256,512]{1,0:T(8,128)(2,1)} %collective-permute-done.10.refs_3_), channel_id=1, source_target_pairs={{4,0},{8,4},{12,8},{14,12},{10,14},{6,10},{2,6},{0,2},{5,1},{9,5},... | collective-permute-start | bytes 786440 | tf_op jit(solution)/shard_map/ppermute | solution.py:121
  48.4 10.2 %collective-permute-start.18 = (bf16[256,512]{1,0:T(8,128)(2,1)}, bf16[256,512]{1,0:T(8,128)(2,1)}, u32[]{:S(2)}, u32[]{:S(2)}) collective-permute-start(bf16[256,512]{1,0:T(8,128)(2,1)} %collective-permute-done.14.refs_3_), channel_id=1, source_target_pairs={{4,0},{8,4},{12,8},{14,12},{10,14},{6,10},{2,6},{0,2},{5,1},{9,5},... | collective-permute-start | bytes 786440 | tf_op jit(solution)/shard_map/ppermute | solution.py:121
  50.1 11.9 %collective-permute-start.17 = (bf16[256,512]{1,0:T(8,128)(2,1)}, bf16[256,512]{1,0:T(8,128)(2,1)}, u32[]{:S(2)}, u32[]{:S(2)}) collective-permute-start(bf16[256,512]{1,0:T(8,128)(2,1)} %collective-permute-done.13.refs_2_), channel_id=1, source_target_pairs={{4,0},{8,4},{12,8},{14,12},{10,14},{6,10},{2,6},{0,2},{5,1},{9,5},... | collective-permute-start | bytes 786440 | tf_op jit(solution)/shard_map/ppermute | solution.py:121
  51.7 11.9 %collective-permute-start.16 = (bf16[256,512]{1,0:T(8,128)(2,1)}, bf16[256,512]{1,0:T(8,128)(2,1)}, u32[]{:S(2)}, u32[]{:S(2)}) collective-permute-start(bf16[256,512]{1,0:T(8,128)(2,1)} %collective-permute-done.12.refs_1_), channel_id=1, source_target_pairs={{0,4},{4,8},{8,12},{12,14},{14,10},{10,6},{6,2},{2,0},{1,5},{5,9},... | collective-permute-start | bytes 786440 | tf_op jit(solution)/shard_map/ppermute | solution.py:121
  52.1 12.4 %collective-permute-start.11 = (bf16[256,512]{1,0:T(8,128)(2,1)}, bf16[256,512]{1,0:T(8,128)(2,1)}, u32[]{:S(2)}, u32[]{:S(2)}) collective-permute-start(bf16[256,512]{1,0:T(8,128)(2,1)} %collective-permute-done.4.refs_0_), channel_id=1, source_target_pairs={{0,4},{4,8},{8,12},{12,14},{14,10},{10,6},{6,2},{2,0},{1,5},{5,9},... | collective-permute-start | bytes 786440 | tf_op jit(solution)/shard_map/ppermute | solution.py:121
  57.2 1.4 copy-start.1
  58.6 14.6 %collective-permute-start.22 = (bf16[256,512]{1,0:T(8,128)(2,1)}, bf16[256,512]{1,0:T(8,128)(2,1)}, u32[]{:S(2)}, u32[]{:S(2)}) collective-permute-start(bf16[256,512]{1,0:T(8,128)(2,1)} %collective-permute-done.18.refs_3_), channel_id=1, source_target_pairs={{4,0},{8,4},{12,8},{14,12},{10,14},{6,10},{2,6},{0,2},{5,1},{9,5},... | collective-permute-start | bytes 786440 | tf_op jit(solution)/shard_map/ppermute | solution.py:121
  62.0 12.3 %collective-permute-start.21 = (bf16[256,512]{1,0:T(8,128)(2,1)}, bf16[256,512]{1,0:T(8,128)(2,1)}, u32[]{:S(2)}, u32[]{:S(2)}) collective-permute-start(bf16[256,512]{1,0:T(8,128)(2,1)} %collective-permute-done.17.refs_2_), channel_id=1, source_target_pairs={{4,0},{8,4},{12,8},{14,12},{10,14},{6,10},{2,6},{0,2},{5,1},{9,5},... | collective-permute-start | bytes 786440 | tf_op jit(solution)/shard_map/ppermute | solution.py:121
  63.6 12.2 %collective-permute-start.20 = (bf16[256,512]{1,0:T(8,128)(2,1)}, bf16[256,512]{1,0:T(8,128)(2,1)}, u32[]{:S(2)}, u32[]{:S(2)}) collective-permute-start(bf16[256,512]{1,0:T(8,128)(2,1)} %collective-permute-done.16.refs_1_), channel_id=1, source_target_pairs={{0,4},{4,8},{8,12},{12,14},{14,10},{10,6},{6,2},{2,0},{1,5},{5,9},... | collective-permute-start | bytes 786440 | tf_op jit(solution)/shard_map/ppermute | solution.py:121
  64.5 11.8 %collective-permute-start.15 = (bf16[256,512]{1,0:T(8,128)(2,1)}, bf16[256,512]{1,0:T(8,128)(2,1)}, u32[]{:S(2)}, u32[]{:S(2)}) collective-permute-start(bf16[256,512]{1,0:T(8,128)(2,1)} %collective-permute-done.11.refs_0_), channel_id=1, source_target_pairs={{0,4},{4,8},{8,12},{12,14},{14,10},{10,6},{6,2},{2,0},{1,5},{5,9},... | collective-permute-start | bytes 786440 | tf_op jit(solution)/shard_map/ppermute | solution.py:121
  65.5 1.6 %copy-start.2 = (f32[1024,512]{1,0:T(8,128)S(1)}, f32[1024,512]{1,0:T(8,128)}, u32[]{:S(2)}) copy-start(f32[1024,512]{1,0:T(8,128)} %copy-done.1) | copy-start | bytes 6291460
  71.8 1.4 copy-start.3
  73.2 10.4 %collective-permute-start.28 = (bf16[256,512]{1,0:T(8,128)(2,1)}, bf16[256,512]{1,0:T(8,128)(2,1)S(1)}, u32[]{:S(2)}, u32[]{:S(2)}) collective-permute-start(bf16[256,512]{1,0:T(8,128)(2,1)} %collective-permute-done.22.refs_3_), channel_id=1, source_target_pairs={{4,0},{8,4},{12,8},{14,12},{10,14},{6,10},{2,6},{0,2},{5,1},{9,5},... | collective-permute-start | bytes 786440 | tf_op jit(solution)/shard_map/ppermute | solution.py:121
  74.3 10.4 %collective-permute-start.26 = (bf16[256,512]{1,0:T(8,128)(2,1)}, bf16[256,512]{1,0:T(8,128)(2,1)}, u32[]{:S(2)}, u32[]{:S(2)}) collective-permute-start(bf16[256,512]{1,0:T(8,128)(2,1)} %collective-permute-done.21.refs_2_), channel_id=1, source_target_pairs={{4,0},{8,4},{12,8},{14,12},{10,14},{6,10},{2,6},{0,2},{5,1},{9,5},... | collective-permute-start | bytes 786440 | tf_op jit(solution)/shard_map/ppermute | solution.py:121
  75.8 10.9 %collective-permute-start.24 = (bf16[256,512]{1,0:T(8,128)(2,1)}, bf16[256,512]{1,0:T(8,128)(2,1)}, u32[]{:S(2)}, u32[]{:S(2)}) collective-permute-start(bf16[256,512]{1,0:T(8,128)(2,1)} %collective-permute-done.20.refs_1_), channel_id=1, source_target_pairs={{0,4},{4,8},{8,12},{12,14},{14,10},{10,6},{6,2},{2,0},{1,5},{5,9},... | collective-permute-start | bytes 786440 | tf_op jit(solution)/shard_map/ppermute | solution.py:121
  76.3 12.2 %collective-permute-start.19 = (bf16[256,512]{1,0:T(8,128)(2,1)}, bf16[256,512]{1,0:T(8,128)(2,1)}, u32[]{:S(2)}, u32[]{:S(2)}) collective-permute-start(bf16[256,512]{1,0:T(8,128)(2,1)} %collective-permute-done.15.refs_0_), channel_id=1, source_target_pairs={{0,4},{4,8},{8,12},{12,14},{14,10},{10,6},{6,2},{2,0},{1,5},{5,9},... | collective-permute-start | bytes 786440 | tf_op jit(solution)/shard_map/ppermute | solution.py:121
  77.3 1.6 %copy-start.4 = (f32[1024,512]{1,0:T(8,128)S(1)}, f32[1024,512]{1,0:T(8,128)}, u32[]{:S(2)}) copy-start(f32[1024,512]{1,0:T(8,128)} %copy-done.3) | copy-start | bytes 6291460
  78.9 14.3 %copy-start.7 = (s32[4]{0:T(128)S(1)}, s32[4]{0:T(128)}, u32[]{:S(2)}) copy-start(s32[4]{0:T(128)} %param.13) | copy-start | bytes 52
  83.6 15.3 %collective-permute-start.29 = (bf16[256,512]{1,0:T(8,128)(2,1)S(1)}, bf16[256,512]{1,0:T(8,128)(2,1)}, u32[]{:S(2)}, u32[]{:S(2)}) collective-permute-start(bf16[256,512]{1,0:T(8,128)(2,1)S(1)} %collective-permute-done.28.refs_3_), channel_id=1, source_target_pairs={{4,0},{8,4},{12,8},{14,12},{10,14},{6,10},{2,6},{0,2},{5,1},{9,5},... | collective-permute-start | bytes 786440 | tf_op jit(solution)/shard_map/ppermute | solution.py:121
  84.7 14.2 %collective-permute-start.27 = (bf16[256,512]{1,0:T(8,128)(2,1)}, bf16[256,512]{1,0:T(8,128)(2,1)}, u32[]{:S(2)}, u32[]{:S(2)}) collective-permute-start(bf16[256,512]{1,0:T(8,128)(2,1)} %collective-permute-done.26.refs_2_), channel_id=1, source_target_pairs={{4,0},{8,4},{12,8},{14,12},{10,14},{6,10},{2,6},{0,2},{5,1},{9,5},... | collective-permute-start | bytes 786440 | tf_op jit(solution)/shard_map/ppermute | solution.py:121
  86.7 12.2 %collective-permute-start.25 = (bf16[256,512]{1,0:T(8,128)(2,1)}, bf16[256,512]{1,0:T(8,128)(2,1)}, u32[]{:S(2)}, u32[]{:S(2)}) collective-permute-start(bf16[256,512]{1,0:T(8,128)(2,1)} %collective-permute-done.24.refs_1_), channel_id=1, source_target_pairs={{0,4},{4,8},{8,12},{12,14},{14,10},{10,6},{6,2},{2,0},{1,5},{5,9},... | collective-permute-start | bytes 786440 | tf_op jit(solution)/shard_map/ppermute | solution.py:121
  88.5 10.4 %collective-permute-start.23 = (bf16[256,512]{1,0:T(8,128)(2,1)}, bf16[256,512]{1,0:T(8,128)(2,1)}, u32[]{:S(2)}, u32[]{:S(2)}) collective-permute-start(bf16[256,512]{1,0:T(8,128)(2,1)} %collective-permute-done.19.refs_0_), channel_id=1, source_target_pairs={{0,4},{4,8},{8,12},{12,14},{14,10},{10,6},{6,2},{2,0},{1,5},{5,9},... | collective-permute-start | bytes 786440 | tf_op jit(solution)/shard_map/ppermute | solution.py:121
  98.9 5.1 %copy-start.6 = (bf16[4,4,4,8,128]{4,3,2,1,0:T(8,128)(2,1)S(1)}, bf16[4,4,4,8,128]{4,3,2,1,0:T(8,128)(2,1)}, u32[]{:S(2)}) copy-start(bf16[4,4,4,8,128]{4,3,2,1,0:T(8,128)(2,1)} %reshape.163) | copy-start | bytes 393220
  103.6 2.9 %collective-permute-start.30 = (bf16[1024,512]{1,0:T(8,128)(2,1)S(1)}, bf16[1024,512]{1,0:T(8,128)(2,1)}, u32[]{:S(2)}, u32[]{:S(2)}) collective-permute-start(bf16[1024,512]{1,0:T(8,128)(2,1)S(1)} %get-tuple-element.64), channel_id=1, source_target_pairs={{0,1},{1,0},{2,3},{3,2},{4,5},{5,4},{6,7},{7,6},{8,9},{9,8},{10,11... | collective-permute-start | bytes 3145736 | tf_op jit(solution)/shard_map/ppermute | solution.py:168
  107.8 1.2 copy-start.5
  112.8 14.9 %all-to-all-start = ((f32[8,72,128]{2,1,0:T(8,128)}), f32[8,72,128]{2,1,0:T(8,128)S(1)}, u32[]{:S(2)}, u32[]{:S(2)}) async-start(f32[8,72,128]{2,1,0:T(8,128)} %select_maximum_fusion), calls=%async_computation | async-start | bytes 589824 | tf_op jit(solution)/shard_map/all_to_all | solution.py:189
  128.2 3.8 %collective-permute-start.31 = (bf16[1,64,128]{2,1,0:T(8,128)(2,1)S(1)}, bf16[1,64,128]{2,1,0:T(8,128)(2,1)S(1)}, u32[]{:S(2)}, u32[]{:S(2)}) collective-permute-start(bf16[1,64,128]{2,1,0:T(8,128)(2,1)S(1)} %fusion.35), channel_id=1, source_target_pairs={{0,2},{2,0},{4,6},{6,4},{8,10},{10,8},{12,14},{14,12},{1,3},{3,1},... | collective-permute-start | bytes 49160 | tf_op jit(solution)/shard_map/ppermute | solution.py:203
  132.0 4.0 %collective-permute-start.32 = (bf16[2,64,128]{2,1,0:T(8,128)(2,1)S(1)}, bf16[2,64,128]{2,1,0:T(8,128)(2,1)S(1)}, u32[]{:S(2)}, u32[]{:S(2)}) collective-permute-start(bf16[2,64,128]{2,1,0:T(8,128)(2,1)S(1)} %pad_maximum_fusion.3), channel_id=1, source_target_pairs={{0,4},{2,6},{4,0},{6,2},{8,12},{10,14},{12,8},{14,10},{1,5},{3,7},... | collective-permute-start | bytes 98312 | tf_op jit(solution)/shard_map/ppermute | solution.py:203
  136.1 5.2 %collective-permute-start.33 = (bf16[4,64,128]{2,1,0:T(8,128)(2,1)S(1)}, bf16[4,64,128]{2,1,0:T(8,128)(2,1)S(1)}, u32[]{:S(2)}, u32[]{:S(2)}) collective-permute-start(bf16[4,64,128]{2,1,0:T(8,128)(2,1)S(1)} %pad_maximum_fusion.2), channel_id=1, source_target_pairs={{0,8},{2,10},{4,12},{6,14},{8,0},{10,2},{12,4},{14,6},{1,9},{3,11}... | collective-permute-start | bytes 196616 | tf_op jit(solution)/shard_map/ppermute | solution.py:203
  141.4 1.4 collective-permute-start.34

commit v4 on v3

--- a/solution.py
+++ b/solution.py
@@ -18,43 +18,49 @@
     return jnp.dot(a, b, preferred_element_type=F32)
 
 
-def add_pieces(tokens, theirs, pieces, total, core=None):
+def add_pieces(tokens, theirs, groups, total, core=None):
     tok_rows = tokens.shape[0]
-    depth, width = pieces[0][1].shape
-    count = len(pieces)
+    width = groups[0][1][0].shape[1]
+    depths = [[part.shape[0] for part in parts] for _, parts in groups]
+    span = sum(depths[0])
+    deep = span * len(groups)
+    flat = [part for _, parts in groups for part in parts]
+    count = len(flat)
     last = core is not None
-    places = jnp.stack([start for start, _ in pieces] + ([core * tok_rows, (1 - core) * tok_rows] if last else []))
+    places = jnp.stack([start for start, _ in groups] + ([core * tok_rows, (1 - core) * tok_rows] if last else []))
 
     def kernel(places_ref, mine_ref, theirs_ref, *refs):
         parts = refs[:count]
-        total_ref, out_ref, mark_ref, columns, sems = refs[count:] if total is not None else (None,) + refs[count:]
+        total_ref, out_ref, mark_ref, columns, weights, sems = (
+            refs[count:] if total is not None else (None,) + refs[count:]
+        )
         copies = []
-        for k in range(count):
-            for j, source in enumerate((mine_ref, theirs_ref)):
-                start = pl.multiple_of(places_ref[k], 128)
-                copy = pltpu.make_async_copy(source.at[:, pl.ds(start, depth)], columns.at[j, k], sems.at[j, k])
+        for j, source in enumerate((mine_ref, theirs_ref)):
+            for g in range(len(groups)):
+                start = pl.multiple_of(places_ref[g], 128)
+                copy = pltpu.make_async_copy(
+                    source.at[:, pl.ds(start, span)], columns.at[j, :, pl.ds(g * span, span)], sems.at[j, g]
+                )
                 copy.start()
                 copies.append(copy)
-        sums = [None, None]
-        for k in range(count):
-            for j in range(2):
-                copies[2 * k + j].wait()
-                term = mm(columns[j, k], parts[k][...])
-                rows = pl.ds(j * tok_rows, tok_rows)
-                if k == 0:
-                    before = None if total is None else total_ref[rows, :]
-                else:
-                    before = sums[j]
-                sums[j] = term if before is None else before + term
+        at = 0
+        for part in parts:
+            weights[at : at + part.shape[0], :] = part[...]
+            at += part.shape[0]
+        mark_ref[...] = jnp.zeros_like(mark_ref)
         for j in range(2):
+            for g in range(len(groups)):
+                copies[j * len(groups) + g].wait()
+            rows = pl.ds(j * tok_rows, tok_rows)
+            term = mm(columns[j], weights[...])
+            if total is not None:
+                term = total_ref[rows, :] + term
             if last:
-                out_ref[pl.ds(pl.multiple_of(places_ref[count + j], tok_rows), tok_rows), :] = sums[j].astype(BF)
-            else:
-                out_ref[pl.ds(j * tok_rows, tok_rows), :] = sums[j]
-        mark_ref[...] = jnp.zeros_like(mark_ref)
+                rows = pl.ds(pl.multiple_of(places_ref[len(groups) + j], tok_rows), tok_rows)
+            out_ref[rows, :] = term.astype(out_ref.dtype)
 
     in_vmem = pl.BlockSpec(memory_space=pltpu.VMEM)
-    in_hbm = pl.BlockSpec(memory_space=pltpu.HBM)
+    in_any = pl.BlockSpec(memory_space=pl.ANY)
     sums = [] if total is None else [total]
     return pl.pallas_call(
         kernel,
@@ -62,19 +68,19 @@
             jax.ShapeDtypeStruct((2 * tok_rows, width), BF if last else F32),
             jax.ShapeDtypeStruct((8, 128), F32),
         ),
-        in_specs=[pl.BlockSpec(memory_space=pltpu.SMEM), in_hbm, in_hbm] + [in_vmem] * (count + len(sums)),
+        in_specs=[pl.BlockSpec(memory_space=pltpu.SMEM), in_any, in_any] + [in_vmem] * (count + len(sums)),
         out_specs=(in_vmem, in_vmem),
         scratch_shapes=[
-            pltpu.VMEM((2, count, tok_rows, depth), BF),
-            pltpu.SemaphoreType.DMA((2, count)),
+            pltpu.VMEM((2, tok_rows, deep), BF),
+            pltpu.VMEM((deep, width), BF),
+            pltpu.SemaphoreType.DMA((2, len(groups))),
         ],
+        input_output_aliases={} if total is None or last else {3 + count: 0},
         compiler_params=pltpu.CompilerParams(vmem_limit_bytes=48 * 2**20),
         cost_estimate=pl.CostEstimate(
-            flops=4 * tok_rows * depth * width * count,
-            bytes_accessed=4 * tok_rows * depth * count,
-            transcendentals=0,
+            flops=4 * tok_rows * deep * width, bytes_accessed=4 * tok_rows * deep, transcendentals=0
         ),
-    )(places, tokens, theirs, *[part for _, part in pieces], *sums)
+    )(places, tokens, theirs, *flat, *sums)
 
 
 def project(tokens, key_down, value_down):
@@ -101,28 +107,32 @@
     left = [(b, a) for a, b in right]
     ways = [right] * chains + [left] * chains
 
-    def start_of(k, step):
-        spot = place - step if k < chains else place + step
+    def start_of(way, step):
+        spot = place - step if way == 0 else place + step
         spot = jnp.where(spot < 0, spot + chips, jnp.where(spot > last, spot - chips, spot))
         source = jnp.where(spot < chips // 2, 2 * spot, 2 * (last - spot) + 1)
-        return source * rows + (core if k < chains else 1 - core) * shard + k % chains * piece
+        return source * rows + (core if way == 0 else 1 - core) * shard
 
     held = [own[k * piece : (k + 1) * piece] for k in range(chains)]
     got, tokens_later = lax.optimization_barrier((got, tokens))
     held += [got[k * piece : (k + 1) * piece] for k in range(chains)]
     theirs = lax.ppermute(tokens_later, "core", SWAP)
-    steps = [[(start_of(k, 0), held[k]) for k in range(2 * chains)]]
+    todo = [(start_of(0, 0), [own]), (start_of(1, 0), [got])]
     total = None
     mark = None
     for step in range(1, chips):
+        ready = todo
         for k in range(2 * chains):
             if mark is not None:
                 held[k], _ = lax.optimization_barrier((held[k], mark))
             held[k] = lax.ppermute(held[k], "chip", ways[k])
-        steps.append([(start_of(k, step), held[k]) for k in range(2 * chains)])
-        while steps and (step >= 3 and len(steps) > 1):
-            total, mark = add_pieces(tokens, theirs, steps.pop(0), total)
-    return add_pieces(tokens, theirs, steps.pop(0), total, core)[0]
+        arriving = [(start_of(w, step), held[w * chains : (w + 1) * chains]) for w in range(2)]
+        if step == 1:
+            todo = todo + arriving
+        else:
+            total, mark = add_pieces(tokens, theirs, ready, total)
+            todo = arriving
+    return add_pieces(tokens, theirs, todo, total, core)[0]
 
 
 def on_device(tokens, key_down, value_down, key_up, value_up, prompt_lens, queries, new_latent):

time: 145 us -> 142 us (0.979)
  waiting for transfers between devices: 42.8 us -> 50.5 us
  Pallas kernels: 35.4 us -> 29.3 us
  local copies, waits for them, and re-layouts: 13.8 us -> 10.9 us
  starting transfers between devices: 41.9 us -> 40.1 us
    ppermute x28, waiting for transfers between devices: 20.1 us -> 26.9 us  [project(): held[k] = lax.ppermute(held[k], 'chip', ways[k])]
    pallas_call x8 -> x7, Pallas kernels: 35.4 us -> 29.3 us  [add_pieces(): pl.pallas_call(kernel, out_shape=(jax.ShapeDtypeStruct((2 * tok_rows, wid...]
    unnamed x16 -> x22, local copies, waits for them, and re-layouts: 6.47 us -> 3.7 us
    all_to_all x1, starting transfers between devices: 5 us -> 3.42 us  [on_device(): lax.all_to_all(sending, 'chip', split_axis=0, concat_axis=0, tiled=True)]
  transfers between devices with their start and end apart: 36 -> 36, of which waited for: 15 -> 16; matrix products, arithmetic and copies ran while one was open for 6% -> 6% of each run, Pallas kernels for 21% -> 17%
where the time goes in v4:
time: 142 us; the launch traced here: 141 us
  waiting for transfers between devices  50.5 us (36%)
  starting transfers between devices  40.1 us (28%)
  Pallas kernels  29.3 us (21%)
  local copies, waits for them, and re-layouts  10.9 us (8%)
  matrix products  5.83 us (4%)
  other arithmetic  4.33 us (3%)
    ppermute x28, starting transfers between devices, project(): held[k] = lax.ppermute(held[k], 'chip', ways[k])  31.8 us
    pallas_call x7, Pallas kernels, add_pieces(): pl.pallas_call(kernel, out_shape=(jax.ShapeDtypeStruct((2 * tok_rows, wid...  29.3 us
    ppermute x28, waiting for transfers between devices, project(): held[k] = lax.ppermute(held[k], 'chip', ways[k])  26.9 us
    ppermute x3, waiting for transfers between devices, on_device(): away = lax.ppermute(whole, 'chip', [(c, c ^ span) for c in range(chips)])  9.97 us
    all_to_all x1, waiting for transfers between devices, on_device(): lax.all_to_all(sending, 'chip', split_axis=0, concat_axis=0, tiled=True)  8.94 us
    ppermute x3, starting transfers between devices, on_device(): away = lax.ppermute(whole, 'chip', [(c, c ^ span) for c in range(chips)])  3.85 us
    unnamed x22, local copies, waits for them, and re-layouts  3.7 us
    dot_general x4, matrix products, mm(): return jnp.dot(a, b, preferred_element_type=F32)  3.5 us
  transfers between devices with their start and end apart: 36, of which 16 were waited for; matrix products, arithmetic and copies ran while one was open for 6% of the time, Pallas kernels for 17%

profile of v4, /device:TPU:0, one launch (start us, length us, event | category | flops | bytes accessed | tf_op | source)
XLA Modules:
  0.0 141.4 jit_solution(17625345912990359039)
XLA Ops:
  0.0 1.4 broadcast_select_fusion
  1.4 0.5 collective-permute-start
  1.9 1.5 %collective-permute-done.refs_1_ = bf16[512,512]{1,0:T(8,128)(2,1)S(1)} collective-permute-done((bf16[512,512]{1,0:T(8,128)(2,1)S(1)}, bf16[512,512]{1,0:T(8,128)(2,1)S(1)}, u32[]{:S(2)}, u32[]{:S(2)}) %collective-permute-start) | collective-permute-done | bytes 524320 | tf_op jit(solution)/shard_map/ppermute | solution.py:94
  3.8 0.8 copy-done.1
  4.6 2.7 %collective-permute-start.2 = (bf16[256,512]{1,0:T(8,128)(2,1)S(1)}, bf16[256,512]{1,0:T(8,128)(2,1)S(1)}, u32[]{:S(2)}, u32[]{:S(2)}) collective-permute-start(bf16[256,512]{1,0:T(8,128)(2,1)S(1)} %get-tuple-element.82), channel_id=1, source_target_pairs={{0,4},{4,8},{8,12},{12,14},{14,10},{10,6},{6,2},{2,0},{1,5},{5,9},... | collective-permute-start | bytes 786440 | tf_op jit(solution)/shard_map/ppermute | solution.py:128
  7.4 1.6 %collective-permute-start.4 = (bf16[256,512]{1,0:T(8,128)(2,1)S(1)}, bf16[256,512]{1,0:T(8,128)(2,1)}, u32[]{:S(2)}, u32[]{:S(2)}) collective-permute-start(bf16[256,512]{1,0:T(8,128)(2,1)S(1)} %get-tuple-element.81), channel_id=1, source_target_pairs={{0,4},{4,8},{8,12},{12,14},{14,10},{10,6},{6,2},{2,0},{1,5},{5,9},... | collective-permute-start | bytes 786440 | tf_op jit(solution)/shard_map/ppermute | solution.py:128
  9.0 0.5 collective-permute-start.6
  9.5 4.9 %collective-permute-done.2.refs_2_ = bf16[256,512]{1,0:T(8,128)(2,1)S(1)} collective-permute-done((bf16[256,512]{1,0:T(8,128)(2,1)S(1)}, bf16[256,512]{1,0:T(8,128)(2,1)S(1)}, u32[]{:S(2)}, u32[]{:S(2)}) %collective-permute-start.2) | collective-permute-done | bytes 262176 | tf_op jit(solution)/shard_map/ppermute | solution.py:128
  14.5 2.0 %collective-permute-start.3 = (bf16[256,512]{1,0:T(8,128)(2,1)S(1)}, bf16[256,512]{1,0:T(8,128)(2,1)}, u32[]{:S(2)}, u32[]{:S(2)}) collective-permute-start(bf16[256,512]{1,0:T(8,128)(2,1)S(1)} %collective-permute-done.2.refs_2_), channel_id=1, source_target_pairs={{0,4},{4,8},{8,12},{12,14},{14,10},{10,6},{6,2},{2,0},{1,5},{5,9},... | collective-permute-start | bytes 786440 | tf_op jit(solution)/shard_map/ppermute | solution.py:128
  16.5 3.7 %collective-permute-done.4.refs_3_ = bf16[256,512]{1,0:T(8,128)(2,1)} collective-permute-done((bf16[256,512]{1,0:T(8,128)(2,1)S(1)}, bf16[256,512]{1,0:T(8,128)(2,1)}, u32[]{:S(2)}, u32[]{:S(2)}) %collective-permute-start.4) | collective-permute-done | bytes 262176 | tf_op jit(solution)/shard_map/ppermute | solution.py:128
  20.2 2.0 %collective-permute-start.8 = (bf16[256,512]{1,0:T(8,128)(2,1)}, bf16[256,512]{1,0:T(8,128)(2,1)}, u32[]{:S(2)}, u32[]{:S(2)}) collective-permute-start(bf16[256,512]{1,0:T(8,128)(2,1)} %collective-permute-done.4.refs_3_), channel_id=1, source_target_pairs={{0,4},{4,8},{8,12},{12,14},{14,10},{10,6},{6,2},{2,0},{1,5},{5,9},... | collective-permute-start | bytes 786440 | tf_op jit(solution)/shard_map/ppermute | solution.py:128
  22.2 0.5 collective-permute-done.5.refs_4_
  22.8 1.4 %collective-permute-start.9 = (bf16[256,512]{1,0:T(8,128)(2,1)}, bf16[256,512]{1,0:T(8,128)(2,1)}, u32[]{:S(2)}, u32[]{:S(2)}) collective-permute-start(bf16[256,512]{1,0:T(8,128)(2,1)} %collective-permute-done.5.refs_4_), channel_id=1, source_target_pairs={{4,0},{8,4},{12,8},{14,12},{10,14},{6,10},{2,6},{0,2},{5,1},{9,5},... | collective-permute-start | bytes 786440 | tf_op jit(solution)/shard_map/ppermute | solution.py:128
  24.3 1.0 copy-done.2
  25.3 1.0 copy-done.4
  26.4 5.2 %shard_map.82 = (f32[1024,512]{1,0:T(8,128)S(1)}, f32[8,128]{1,0:T(8,128)}) custom-call(s32[4]{0:T(128)S(1)} %pad_add_fusion.1.places_ref, bf16[512,8192]{1,0:T(8,128)(2,1)} %mine_ref.13, bf16[512,8192]{1,0:T(8,128)(2,1)} %collective-permute-done.1.theirs_ref, bf16[512,512]{1,0:T(8,128)(2,1)S(1)} %copy-done.2, bf16[512,512]{1,0:T(8,128)(2,1)S(1)} %copy-done.4, ...), custom_call_target="tpu_custom_call" | custom-call | flops 2147483648 | bytes 4194304 | tf_op jit(solution)/shard_map/pallas_call | solution.py:65
  31.8 1.4 %collective-permute-start.14 = (bf16[256,512]{1,0:T(8,128)(2,1)}, bf16[256,512]{1,0:T(8,128)(2,1)}, u32[]{:S(2)}, u32[]{:S(2)}) collective-permute-start(bf16[256,512]{1,0:T(8,128)(2,1)} %collective-permute-done.10.refs_3_), channel_id=1, source_target_pairs={{4,0},{8,4},{12,8},{14,12},{10,14},{6,10},{2,6},{0,2},{5,1},{9,5},... | collective-permute-start | bytes 786440 | tf_op jit(solution)/shard_map/ppermute | solution.py:128
  33.2 4.2 %collective-permute-done.9.refs_2_ = bf16[256,512]{1,0:T(8,128)(2,1)} collective-permute-done((bf16[256,512]{1,0:T(8,128)(2,1)}, bf16[256,512]{1,0:T(8,128)(2,1)}, u32[]{:S(2)}, u32[]{:S(2)}) %collective-permute-start.9) | collective-permute-done | bytes 262176 | tf_op jit(solution)/shard_map/ppermute | solution.py:128
  37.4 2.0 %collective-permute-start.12 = (bf16[256,512]{1,0:T(8,128)(2,1)}, bf16[256,512]{1,0:T(8,128)(2,1)}, u32[]{:S(2)}, u32[]{:S(2)}) collective-permute-start(bf16[256,512]{1,0:T(8,128)(2,1)} %collective-permute-done.8.refs_1_), channel_id=1, source_target_pairs={{0,4},{4,8},{8,12},{12,14},{14,10},{10,6},{6,2},{2,0},{1,5},{5,9},... | collective-permute-start | bytes 786440 | tf_op jit(solution)/shard_map/ppermute | solution.py:128
  39.4 1.6 %collective-permute-start.7 = (bf16[256,512]{1,0:T(8,128)(2,1)}, bf16[256,512]{1,0:T(8,128)(2,1)S(1)}, u32[]{:S(2)}, u32[]{:S(2)}) collective-permute-start(bf16[256,512]{1,0:T(8,128)(2,1)} %collective-permute-done.3.refs_0_), channel_id=1, source_target_pairs={{0,4},{4,8},{8,12},{12,14},{14,10},{10,6},{6,2},{2,0},{1,5},{5,9},... | collective-permute-start | bytes 786440 | tf_op jit(solution)/shard_map/ppermute | solution.py:128
  41.1 3.9 %shard_map.83 = (f32[1024,512]{1,0:T(8,128)S(1)}, f32[8,128]{1,0:T(8,128)}) custom-call(s32[2]{0:T(128)S(1)} %pad_add_fusion.2.places_ref, bf16[512,8192]{1,0:T(8,128)(2,1)} %mine_ref.13, bf16[512,8192]{1,0:T(8,128)(2,1)} %collective-permute-done.1.theirs_ref, bf16[256,512]{1,0:T(8,128)(2,1)} %collective-permute-done.3.refs_0_, ...), custom_call_target="tpu_custom_call", output_to_operand_aliasing={{0}: (7, {})} | custom-call | flops 1073741824 | bytes 2097152 | tf_op jit(solution)/shard_map/pallas_call | solution.py:65
  45.0 0.5 collective-permute-start.18
  45.5 3.2 %collective-permute-done.13.refs_2_ = bf16[256,512]{1,0:T(8,128)(2,1)} collective-permute-done((bf16[256,512]{1,0:T(8,128)(2,1)}, bf16[256,512]{1,0:T(8,128)(2,1)}, u32[]{:S(2)}, u32[]{:S(2)}) %collective-permute-start.13) | collective-permute-done | bytes 262176 | tf_op jit(solution)/shard_map/ppermute | solution.py:128
  48.6 2.0 %collective-permute-start.16 = (bf16[256,512]{1,0:T(8,128)(2,1)}, bf16[256,512]{1,0:T(8,128)(2,1)}, u32[]{:S(2)}, u32[]{:S(2)}) collective-permute-start(bf16[256,512]{1,0:T(8,128)(2,1)} %collective-permute-done.12.refs_1_), channel_id=1, source_target_pairs={{0,4},{4,8},{8,12},{12,14},{14,10},{10,6},{6,2},{2,0},{1,5},{5,9},... | collective-permute-start | bytes 786440 | tf_op jit(solution)/shard_map/ppermute | solution.py:128
  50.7 1.6 %collective-permute-start.11 = (bf16[256,512]{1,0:T(8,128)(2,1)S(1)}, bf16[256,512]{1,0:T(8,128)(2,1)}, u32[]{:S(2)}, u32[]{:S(2)}) collective-permute-start(bf16[256,512]{1,0:T(8,128)(2,1)S(1)} %collective-permute-done.7.refs_0_), channel_id=1, source_target_pairs={{0,4},{4,8},{8,12},{12,14},{14,10},{10,6},{6,2},{2,0},{1,5},{5,9},... | collective-permute-start | bytes 786440 | tf_op jit(solution)/shard_map/ppermute | solution.py:128
  52.3 3.8 %shard_map.84 = (f32[1024,512]{1,0:T(8,128)S(1)}, f32[8,128]{1,0:T(8,128)}) custom-call(s32[2]{0:T(128)S(1)} %pad_add_fusion.3.places_ref, bf16[512,8192]{1,0:T(8,128)(2,1)} %mine_ref.13, bf16[512,8192]{1,0:T(8,128)(2,1)} %collective-permute-done.1.theirs_ref, bf16[256,512]{1,0:T(8,128)(2,1)S(1)} %collective-permute-done.7.refs_0_, ...), custom_call_target="tpu_custom_call", output_to_operand_aliasing={{0}: (7, {})} | custom-call | flops 1073741824 | bytes 2097152 | tf_op jit(solution)/shard_map/pallas_call | solution.py:65
  56.1 0.5 collective-permute-start.22
  56.6 3.6 %collective-permute-done.17.refs_2_ = bf16[256,512]{1,0:T(8,128)(2,1)} collective-permute-done((bf16[256,512]{1,0:T(8,128)(2,1)}, bf16[256,512]{1,0:T(8,128)(2,1)}, u32[]{:S(2)}, u32[]{:S(2)}) %collective-permute-start.17) | collective-permute-done | bytes 262176 | tf_op jit(solution)/shard_map/ppermute | solution.py:128
  60.6 1.6 %collective-permute-start.20 = (bf16[256,512]{1,0:T(8,128)(2,1)}, bf16[256,512]{1,0:T(8,128)(2,1)}, u32[]{:S(2)}, u32[]{:S(2)}) collective-permute-start(bf16[256,512]{1,0:T(8,128)(2,1)} %collective-permute-done.16.refs_1_), channel_id=1, source_target_pairs={{0,4},{4,8},{8,12},{12,14},{14,10},{10,6},{6,2},{2,0},{1,5},{5,9},... | collective-permute-start | bytes 786440 | tf_op jit(solution)/shard_map/ppermute | solution.py:128
  62.2 1.6 %collective-permute-start.15 = (bf16[256,512]{1,0:T(8,128)(2,1)}, bf16[256,512]{1,0:T(8,128)(2,1)}, u32[]{:S(2)}, u32[]{:S(2)}) collective-permute-start(bf16[256,512]{1,0:T(8,128)(2,1)} %collective-permute-done.11.refs_0_), channel_id=1, source_target_pairs={{0,4},{4,8},{8,12},{12,14},{14,10},{10,6},{6,2},{2,0},{1,5},{5,9},... | collective-permute-start | bytes 786440 | tf_op jit(solution)/shard_map/ppermute | solution.py:128
  63.9 3.9 %shard_map.85 = (f32[1024,512]{1,0:T(8,128)S(1)}, f32[8,128]{1,0:T(8,128)}) custom-call(s32[2]{0:T(128)S(1)} %pad_add_fusion.4.places_ref, bf16[512,8192]{1,0:T(8,128)(2,1)} %mine_ref.13, bf16[512,8192]{1,0:T(8,128)(2,1)} %collective-permute-done.1.theirs_ref, bf16[256,512]{1,0:T(8,128)(2,1)} %collective-permute-done.11.refs_0_, ...), custom_call_target="tpu_custom_call", output_to_operand_aliasing={{0}: (7, {})} | custom-call | flops 1073741824 | bytes 2097152 | tf_op jit(solution)/shard_map/pallas_call | solution.py:65
  67.8 0.5 collective-permute-start.28
  68.3 3.2 %collective-permute-done.21.refs_2_ = bf16[256,512]{1,0:T(8,128)(2,1)} collective-permute-done((bf16[256,512]{1,0:T(8,128)(2,1)}, bf16[256,512]{1,0:T(8,128)(2,1)}, u32[]{:S(2)}, u32[]{:S(2)}) %collective-permute-start.21) | collective-permute-done | bytes 262176 | tf_op jit(solution)/shard_map/ppermute | solution.py:128
  71.9 1.6 %collective-permute-start.24 = (bf16[256,512]{1,0:T(8,128)(2,1)}, bf16[256,512]{1,0:T(8,128)(2,1)}, u32[]{:S(2)}, u32[]{:S(2)}) collective-permute-start(bf16[256,512]{1,0:T(8,128)(2,1)} %collective-permute-done.20.refs_1_), channel_id=1, source_target_pairs={{0,4},{4,8},{8,12},{12,14},{14,10},{10,6},{6,2},{2,0},{1,5},{5,9},... | collective-permute-start | bytes 786440 | tf_op jit(solution)/shard_map/ppermute | solution.py:128
  73.5 1.6 %collective-permute-start.19 = (bf16[256,512]{1,0:T(8,128)(2,1)}, bf16[256,512]{1,0:T(8,128)(2,1)}, u32[]{:S(2)}, u32[]{:S(2)}) collective-permute-start(bf16[256,512]{1,0:T(8,128)(2,1)} %collective-permute-done.15.refs_0_), channel_id=1, source_target_pairs={{0,4},{4,8},{8,12},{12,14},{14,10},{10,6},{6,2},{2,0},{1,5},{5,9},... | collective-permute-start | bytes 786440 | tf_op jit(solution)/shard_map/ppermute | solution.py:128
  75.1 3.9 %shard_map.86 = (f32[1024,512]{1,0:T(8,128)S(1)}, f32[8,128]{1,0:T(8,128)}) custom-call(s32[2]{0:T(128)S(1)} %pad_add_fusion.5.places_ref, bf16[512,8192]{1,0:T(8,128)(2,1)} %mine_ref.13, bf16[512,8192]{1,0:T(8,128)(2,1)} %collective-permute-done.1.theirs_ref, bf16[256,512]{1,0:T(8,128)(2,1)} %collective-permute-done.15.refs_0_, ...), custom_call_target="tpu_custom_call", output_to_operand_aliasing={{0}: (7, {})} | custom-call | flops 1073741824 | bytes 2097152 | tf_op jit(solution)/shard_map/pallas_call | solution.py:65
  79.0 0.5 collective-permute-start.29
  79.5 3.5 %collective-permute-done.26.refs_2_ = bf16[256,512]{1,0:T(8,128)(2,1)} collective-permute-done((bf16[256,512]{1,0:T(8,128)(2,1)}, bf16[256,512]{1,0:T(8,128)(2,1)}, u32[]{:S(2)}, u32[]{:S(2)}) %collective-permute-start.26) | collective-permute-done | bytes 262176 | tf_op jit(solution)/shard_map/ppermute | solution.py:128
  83.4 1.6 %collective-permute-start.25 = (bf16[256,512]{1,0:T(8,128)(2,1)}, bf16[256,512]{1,0:T(8,128)(2,1)}, u32[]{:S(2)}, u32[]{:S(2)}) collective-permute-start(bf16[256,512]{1,0:T(8,128)(2,1)} %collective-permute-done.24.refs_1_), channel_id=1, source_target_pairs={{0,4},{4,8},{8,12},{12,14},{14,10},{10,6},{6,2},{2,0},{1,5},{5,9},... | collective-permute-start | bytes 786440 | tf_op jit(solution)/shard_map/ppermute | solution.py:128
  85.0 1.5 %collective-permute-start.23 = (bf16[256,512]{1,0:T(8,128)(2,1)}, bf16[256,512]{1,0:T(8,128)(2,1)}, u32[]{:S(2)}, u32[]{:S(2)}) collective-permute-start(bf16[256,512]{1,0:T(8,128)(2,1)} %collective-permute-done.19.refs_0_), channel_id=1, source_target_pairs={{0,4},{4,8},{8,12},{12,14},{14,10},{10,6},{6,2},{2,0},{1,5},{5,9},... | collective-permute-start | bytes 786440 | tf_op jit(solution)/shard_map/ppermute | solution.py:128
  86.6 1.9 %reshape.162 = bf16[4,4,2,4096]{3,2,1,0:T(2,128)(2,1)} reshape(bf16[4,4,8192]{2,1,0:T(4,128)(2,1)} %param.14) | data formatting | bytes 524288 | tf_op jit(solution)/shard_map/reshape | solution.py:156
  88.6 1.8 %dynamic-slice_reduce_fusion = bf16[4,4,4096]{2,1,0:T(4,128)(2,1)S(1)} fusion(bf16[4,4,2,4096]{3,2,1,0:T(2,128)(2,1)} %reshape.162, s32[]{:T(128)S(6)} %select_n.298), kind=kLoop, calls=%fused_computation.36 | loop fusion | bytes 262148 | tf_op jit(solution)/shard_map/jit(dynamic_index_in_dim)/dynamic_slice | solution.py:155
  90.3 0.8 reshape.163
  91.3 0.8 reshape.166
  92.2 3.8 %shard_map.87 = (f32[1024,512]{1,0:T(8,128)S(1)}, f32[8,128]{1,0:T(8,128)}) custom-call(s32[2]{0:T(128)S(1)} %pad_add_fusion.6.places_ref, bf16[512,8192]{1,0:T(8,128)(2,1)} %mine_ref.13, bf16[512,8192]{1,0:T(8,128)(2,1)} %collective-permute-done.1.theirs_ref, bf16[256,512]{1,0:T(8,128)(2,1)} %collective-permute-done.19.refs_0_, ...), custom_call_target="tpu_custom_call", output_to_operand_aliasing={{0}: (7, {})} | custom-call | flops 1073741824 | bytes 2097152 | tf_op jit(solution)/shard_map/pallas_call | solution.py:65
  96.0 4.9 %shard_map.88 = (bf16[1024,512]{1,0:T(8,128)(2,1)}, f32[8,128]{1,0:T(8,128)}) custom-call(s32[4]{0:T(128)S(1)} %pad_add_fusion.places_ref, bf16[512,8192]{1,0:T(8,128)(2,1)} %mine_ref.13, bf16[512,8192]{1,0:T(8,128)(2,1)} %collective-permute-done.1.theirs_ref, bf16[256,512]{1,0:T(8,128)(2,1)} %collective-permute-done.23.refs_0_, ...), custom_call_target="tpu_custom_call" | custom-call | flops 1073741824 | bytes 2097152 | tf_op jit(solution)/shard_map/pallas_call | solution.py:65
  101.4 0.7 fusion.47
  102.1 1.8 %collective-permute-done.30 = bf16[1024,512]{1,0:T(8,128)(2,1)S(1)} collective-permute-done((bf16[1024,512]{1,0:T(8,128)(2,1)}, bf16[1024,512]{1,0:T(8,128)(2,1)S(1)}, u32[]{:S(2)}, u32[]{:S(2)}) %collective-permute-start.30) | collective-permute-done | bytes 1048608 | tf_op jit(solution)/shard_map/ppermute | solution.py:178
  103.9 2.4 %convolution_convert_fusion = bf16[1024,512]{0,1:T(8,128)(2,1)S(1)} fusion(bf16[1024,512]{1,0:T(8,128)(2,1)} %get-tuple-element.72, bf16[1024,512]{1,0:T(8,128)(2,1)S(1)} %collective-permute-done.30, pred[]{:T(512)S(6)} %eq.7, bf16[512,1024]{1,0:T(8,128)(2,1)S(1)} %copy-done, s32[]{:T(128)S(6)} %select_n.296), kind=kOutput, calls=%fused_computation.3 | convolution fusion | flops 537919488 | bytes 3670021 | tf_op jit(solution)/shard_map/dot_general | solution.py:18
  106.2 0.6 fusion
  106.9 0.7 fusion.1
  108.4 0.8 convolution_convert_fusion.1
  109.2 0.7 convolution_bitcast_fusion.1
  110.2 0.7 select_maximum_fusion
  111.0 3.4 %all-to-all-start = ((f32[8,72,128]{2,1,0:T(8,128)}), f32[8,72,128]{2,1,0:T(8,128)S(1)}, u32[]{:S(2)}, u32[]{:S(2)}) async-start(f32[8,72,128]{2,1,0:T(8,128)} %select_maximum_fusion), calls=%async_computation | async-start | bytes 589824 | tf_op jit(solution)/shard_map/all_to_all | solution.py:199
  115.4 8.9 %all-to-all-done = f32[8,72,128]{2,1,0:T(8,128)S(1)} async-done(((f32[8,72,128]{2,1,0:T(8,128)}), f32[8,72,128]{2,1,0:T(8,128)S(1)}, u32[]{:S(2)}, u32[]{:S(2)}) %all-to-all-start) | async-done | bytes 294944 | tf_op jit(solution)/shard_map/all_to_all | solution.py:199
  124.8 1.5 %collective-permute-start.31 = (bf16[1,64,128]{2,1,0:T(8,128)(2,1)S(1)}, bf16[1,64,128]{2,1,0:T(8,128)(2,1)S(1)}, u32[]{:S(2)}, u32[]{:S(2)}) collective-permute-start(bf16[1,64,128]{2,1,0:T(8,128)(2,1)S(1)} %fusion.35), channel_id=1, source_target_pairs={{0,2},{2,0},{4,6},{6,4},{8,10},{10,8},{12,14},{14,12},{1,3},{3,1},... | collective-permute-start | bytes 49160 | tf_op jit(solution)/shard_map/ppermute | solution.py:213
  126.4 2.3 %collective-permute-done.31 = bf16[1,64,128]{2,1,0:T(8,128)(2,1)S(1)} collective-permute-done((bf16[1,64,128]{2,1,0:T(8,128)(2,1)S(1)}, bf16[1,64,128]{2,1,0:T(8,128)(2,1)S(1)}, u32[]{:S(2)}, u32[]{:S(2)}) %collective-permute-start.31) | collective-permute-done | bytes 16416 | tf_op jit(solution)/shard_map/ppermute | solution.py:213
  128.6 1.1 collective-permute-start.32
  129.8 2.9 %collective-permute-done.32 = bf16[2,64,128]{2,1,0:T(8,128)(2,1)S(1)} collective-permute-done((bf16[2,64,128]{2,1,0:T(8,128)(2,1)S(1)}, bf16[2,64,128]{2,1,0:T(8,128)(2,1)S(1)}, u32[]{:S(2)}, u32[]{:S(2)}) %collective-permute-start.32) | collective-permute-done | bytes 32800 | tf_op jit(solution)/shard_map/ppermute | solution.py:213
  132.8 1.2 collective-permute-start.33
  133.9 4.8 %collective-permute-done.33 = bf16[4,64,128]{2,1,0:T(8,128)(2,1)S(1)} collective-permute-done((bf16[4,64,128]{2,1,0:T(8,128)(2,1)S(1)}, bf16[4,64,128]{2,1,0:T(8,128)(2,1)S(1)}, u32[]{:S(2)}, u32[]{:S(2)}) %collective-permute-start.33) | collective-permute-done | bytes 65568 | tf_op jit(solution)/shard_map/ppermute | solution.py:213
  138.9 1.3 collective-permute-done.34
  140.5 0.9 reshape.174
  (100 shorter events, 6.3 us)
Async XLA Ops:
  0.0 101.0 %copy-start = (bf16[512,1024]{1,0:T(8,128)(2,1)S(1)}, bf16[512,1024]{1,0:T(8,128)(2,1)}, u32[]{:S(2)}) copy-start(bf16[512,1024]{1,0:T(8,128)(2,1)} %param.11) | copy-start | bytes 3145732
  1.4 2.1 %collective-permute-start = (bf16[512,512]{1,0:T(8,128)(2,1)S(1)}, bf16[512,512]{1,0:T(8,128)(2,1)S(1)}, u32[]{:S(2)}, u32[]{:S(2)}) collective-permute-start(bf16[512,512]{1,0:T(8,128)(2,1)S(1)} %get-tuple-element.78), channel_id=1, source_target_pairs={{0,1},{1,0},{2,3},{3,2},{4,5},{5,4},{6,7},{7,6},{8,9},{9,8},{10,11... | collective-permute-start | bytes 1572872 | tf_op jit(solution)/shard_map/ppermute | solution.py:94
  3.4 5.5 %copy-start.3 = (bf16[512,512]{1,0:T(8,128)(2,1)}, bf16[512,512]{1,0:T(8,128)(2,1)S(1)}, u32[]{:S(2)}) copy-start(bf16[512,512]{1,0:T(8,128)(2,1)S(1)} %collective-permute-done.refs_1_) | copy-start | bytes 1572868
  3.4 20.9 %collective-permute-start.1 = (bf16[512,8192]{1,0:T(8,128)(2,1)}, bf16[512,8192]{1,0:T(8,128)(2,1)}, u32[]{:S(2)}, u32[]{:S(2)}) collective-permute-start(bf16[512,8192]{1,0:T(8,128)(2,1)} %mine_ref.13), channel_id=1, source_target_pairs={{0,1},{1,0},{2,3},{3,2},{4,5},{5,4},{6,7},{7,6},{8,9},{9,8},{10,11... | collective-permute-start | bytes 25165832 | tf_op jit(solution)/shard_map/ppermute | solution.py:119
  3.8 0.8 copy-start.1
  4.6 9.8 %collective-permute-start.2 = (bf16[256,512]{1,0:T(8,128)(2,1)S(1)}, bf16[256,512]{1,0:T(8,128)(2,1)S(1)}, u32[]{:S(2)}, u32[]{:S(2)}) collective-permute-start(bf16[256,512]{1,0:T(8,128)(2,1)S(1)} %get-tuple-element.82), channel_id=1, source_target_pairs={{0,4},{4,8},{8,12},{12,14},{14,10},{10,6},{6,2},{2,0},{1,5},{5,9},... | collective-permute-start | bytes 786440 | tf_op jit(solution)/shard_map/ppermute | solution.py:128
  7.4 12.8 %collective-permute-start.4 = (bf16[256,512]{1,0:T(8,128)(2,1)S(1)}, bf16[256,512]{1,0:T(8,128)(2,1)}, u32[]{:S(2)}, u32[]{:S(2)}) collective-permute-start(bf16[256,512]{1,0:T(8,128)(2,1)S(1)} %get-tuple-element.81), channel_id=1, source_target_pairs={{0,4},{4,8},{8,12},{12,14},{14,10},{10,6},{6,2},{2,0},{1,5},{5,9},... | collective-permute-start | bytes 786440 | tf_op jit(solution)/shard_map/ppermute | solution.py:128
  9.0 13.2 %collective-permute-start.6 = (bf16[256,512]{1,0:T(8,128)(2,1)S(1)}, bf16[256,512]{1,0:T(8,128)(2,1)}, u32[]{:S(2)}, u32[]{:S(2)}) collective-permute-start(bf16[256,512]{1,0:T(8,128)(2,1)S(1)} %get-tuple-element.79), channel_id=1, source_target_pairs={{4,0},{8,4},{12,8},{14,12},{10,14},{6,10},{2,6},{0,2},{5,1},{9,5},... | collective-permute-start | bytes 786440 | tf_op jit(solution)/shard_map/ppermute | solution.py:128
  9.5 13.3 %collective-permute-start.5 = (bf16[256,512]{1,0:T(8,128)(2,1)S(1)}, bf16[256,512]{1,0:T(8,128)(2,1)}, u32[]{:S(2)}, u32[]{:S(2)}) collective-permute-start(bf16[256,512]{1,0:T(8,128)(2,1)S(1)} %get-tuple-element.80), channel_id=1, source_target_pairs={{4,0},{8,4},{12,8},{14,12},{10,14},{6,10},{2,6},{0,2},{5,1},{9,5},... | collective-permute-start | bytes 786440 | tf_op jit(solution)/shard_map/ppermute | solution.py:128
  14.5 25.0 %collective-permute-start.3 = (bf16[256,512]{1,0:T(8,128)(2,1)S(1)}, bf16[256,512]{1,0:T(8,128)(2,1)}, u32[]{:S(2)}, u32[]{:S(2)}) collective-permute-start(bf16[256,512]{1,0:T(8,128)(2,1)S(1)} %collective-permute-done.2.refs_2_), channel_id=1, source_target_pairs={{0,4},{4,8},{8,12},{12,14},{14,10},{10,6},{6,2},{2,0},{1,5},{5,9},... | collective-permute-start | bytes 786440 | tf_op jit(solution)/shard_map/ppermute | solution.py:128
  20.2 17.2 %collective-permute-start.8 = (bf16[256,512]{1,0:T(8,128)(2,1)}, bf16[256,512]{1,0:T(8,128)(2,1)}, u32[]{:S(2)}, u32[]{:S(2)}) collective-permute-start(bf16[256,512]{1,0:T(8,128)(2,1)} %collective-permute-done.4.refs_3_), channel_id=1, source_target_pairs={{0,4},{4,8},{8,12},{12,14},{14,10},{10,6},{6,2},{2,0},{1,5},{5,9},... | collective-permute-start | bytes 786440 | tf_op jit(solution)/shard_map/ppermute | solution.py:128
  22.2 9.6 %collective-permute-start.10 = (bf16[256,512]{1,0:T(8,128)(2,1)}, bf16[256,512]{1,0:T(8,128)(2,1)}, u32[]{:S(2)}, u32[]{:S(2)}) collective-permute-start(bf16[256,512]{1,0:T(8,128)(2,1)} %collective-permute-done.6.refs_5_), channel_id=1, source_target_pairs={{4,0},{8,4},{12,8},{14,12},{10,14},{6,10},{2,6},{0,2},{5,1},{9,5},... | collective-permute-start | bytes 786440 | tf_op jit(solution)/shard_map/ppermute | solution.py:128
  22.8 14.6 %collective-permute-start.9 = (bf16[256,512]{1,0:T(8,128)(2,1)}, bf16[256,512]{1,0:T(8,128)(2,1)}, u32[]{:S(2)}, u32[]{:S(2)}) collective-permute-start(bf16[256,512]{1,0:T(8,128)(2,1)} %collective-permute-done.5.refs_4_), channel_id=1, source_target_pairs={{4,0},{8,4},{12,8},{14,12},{10,14},{6,10},{2,6},{0,2},{5,1},{9,5},... | collective-permute-start | bytes 786440 | tf_op jit(solution)/shard_map/ppermute | solution.py:128
  24.3 1.0 copy-start.2
  25.3 1.0 copy-start.4
  31.8 13.2 %collective-permute-start.14 = (bf16[256,512]{1,0:T(8,128)(2,1)}, bf16[256,512]{1,0:T(8,128)(2,1)}, u32[]{:S(2)}, u32[]{:S(2)}) collective-permute-start(bf16[256,512]{1,0:T(8,128)(2,1)} %collective-permute-done.10.refs_3_), channel_id=1, source_target_pairs={{4,0},{8,4},{12,8},{14,12},{10,14},{6,10},{2,6},{0,2},{5,1},{9,5},... | collective-permute-start | bytes 786440 | tf_op jit(solution)/shard_map/ppermute | solution.py:128
  37.4 11.2 %collective-permute-start.13 = (bf16[256,512]{1,0:T(8,128)(2,1)}, bf16[256,512]{1,0:T(8,128)(2,1)}, u32[]{:S(2)}, u32[]{:S(2)}) collective-permute-start(bf16[256,512]{1,0:T(8,128)(2,1)} %collective-permute-done.9.refs_2_), channel_id=1, source_target_pairs={{4,0},{8,4},{12,8},{14,12},{10,14},{6,10},{2,6},{0,2},{5,1},{9,5},... | collective-permute-start | bytes 786440 | tf_op jit(solution)/shard_map/ppermute | solution.py:128
  37.4 11.2 %collective-permute-start.12 = (bf16[256,512]{1,0:T(8,128)(2,1)}, bf16[256,512]{1,0:T(8,128)(2,1)}, u32[]{:S(2)}, u32[]{:S(2)}) collective-permute-start(bf16[256,512]{1,0:T(8,128)(2,1)} %collective-permute-done.8.refs_1_), channel_id=1, source_target_pairs={{0,4},{4,8},{8,12},{12,14},{14,10},{10,6},{6,2},{2,0},{1,5},{5,9},... | collective-permute-start | bytes 786440 | tf_op jit(solution)/shard_map/ppermute | solution.py:128
  39.4 11.2 %collective-permute-start.7 = (bf16[256,512]{1,0:T(8,128)(2,1)}, bf16[256,512]{1,0:T(8,128)(2,1)S(1)}, u32[]{:S(2)}, u32[]{:S(2)}) collective-permute-start(bf16[256,512]{1,0:T(8,128)(2,1)} %collective-permute-done.3.refs_0_), channel_id=1, source_target_pairs={{0,4},{4,8},{8,12},{12,14},{14,10},{10,6},{6,2},{2,0},{1,5},{5,9},... | collective-permute-start | bytes 786440 | tf_op jit(solution)/shard_map/ppermute | solution.py:128
  45.0 11.1 %collective-permute-start.18 = (bf16[256,512]{1,0:T(8,128)(2,1)}, bf16[256,512]{1,0:T(8,128)(2,1)}, u32[]{:S(2)}, u32[]{:S(2)}) collective-permute-start(bf16[256,512]{1,0:T(8,128)(2,1)} %collective-permute-done.14.refs_3_), channel_id=1, source_target_pairs={{4,0},{8,4},{12,8},{14,12},{10,14},{6,10},{2,6},{0,2},{5,1},{9,5},... | collective-permute-start | bytes 786440 | tf_op jit(solution)/shard_map/ppermute | solution.py:128
  48.6 11.6 %collective-permute-start.17 = (bf16[256,512]{1,0:T(8,128)(2,1)}, bf16[256,512]{1,0:T(8,128)(2,1)}, u32[]{:S(2)}, u32[]{:S(2)}) collective-permute-start(bf16[256,512]{1,0:T(8,128)(2,1)} %collective-permute-done.13.refs_2_), channel_id=1, source_target_pairs={{4,0},{8,4},{12,8},{14,12},{10,14},{6,10},{2,6},{0,2},{5,1},{9,5},... | collective-permute-start | bytes 786440 | tf_op jit(solution)/shard_map/ppermute | solution.py:128
  48.6 12.0 %collective-permute-start.16 = (bf16[256,512]{1,0:T(8,128)(2,1)}, bf16[256,512]{1,0:T(8,128)(2,1)}, u32[]{:S(2)}, u32[]{:S(2)}) collective-permute-start(bf16[256,512]{1,0:T(8,128)(2,1)} %collective-permute-done.12.refs_1_), channel_id=1, source_target_pairs={{0,4},{4,8},{8,12},{12,14},{14,10},{10,6},{6,2},{2,0},{1,5},{5,9},... | collective-permute-start | bytes 786440 | tf_op jit(solution)/shard_map/ppermute | solution.py:128
  50.7 11.6 %collective-permute-start.11 = (bf16[256,512]{1,0:T(8,128)(2,1)S(1)}, bf16[256,512]{1,0:T(8,128)(2,1)}, u32[]{:S(2)}, u32[]{:S(2)}) collective-permute-start(bf16[256,512]{1,0:T(8,128)(2,1)S(1)} %collective-permute-done.7.refs_0_), channel_id=1, source_target_pairs={{0,4},{4,8},{8,12},{12,14},{14,10},{10,6},{6,2},{2,0},{1,5},{5,9},... | collective-permute-start | bytes 786440 | tf_op jit(solution)/shard_map/ppermute | solution.py:128
  56.1 11.6 %collective-permute-start.22 = (bf16[256,512]{1,0:T(8,128)(2,1)}, bf16[256,512]{1,0:T(8,128)(2,1)}, u32[]{:S(2)}, u32[]{:S(2)}) collective-permute-start(bf16[256,512]{1,0:T(8,128)(2,1)} %collective-permute-done.18.refs_3_), channel_id=1, source_target_pairs={{4,0},{8,4},{12,8},{14,12},{10,14},{6,10},{2,6},{0,2},{5,1},{9,5},... | collective-permute-start | bytes 786440 | tf_op jit(solution)/shard_map/ppermute | solution.py:128
  60.2 11.2 %collective-permute-start.21 = (bf16[256,512]{1,0:T(8,128)(2,1)}, bf16[256,512]{1,0:T(8,128)(2,1)}, u32[]{:S(2)}, u32[]{:S(2)}) collective-permute-start(bf16[256,512]{1,0:T(8,128)(2,1)} %collective-permute-done.17.refs_2_), channel_id=1, source_target_pairs={{4,0},{8,4},{12,8},{14,12},{10,14},{6,10},{2,6},{0,2},{5,1},{9,5},... | collective-permute-start | bytes 786440 | tf_op jit(solution)/shard_map/ppermute | solution.py:128
  60.6 11.2 %collective-permute-start.20 = (bf16[256,512]{1,0:T(8,128)(2,1)}, bf16[256,512]{1,0:T(8,128)(2,1)}, u32[]{:S(2)}, u32[]{:S(2)}) collective-permute-start(bf16[256,512]{1,0:T(8,128)(2,1)} %collective-permute-done.16.refs_1_), channel_id=1, source_target_pairs={{0,4},{4,8},{8,12},{12,14},{14,10},{10,6},{6,2},{2,0},{1,5},{5,9},... | collective-permute-start | bytes 786440 | tf_op jit(solution)/shard_map/ppermute | solution.py:128
  62.2 11.2 %collective-permute-start.15 = (bf16[256,512]{1,0:T(8,128)(2,1)}, bf16[256,512]{1,0:T(8,128)(2,1)}, u32[]{:S(2)}, u32[]{:S(2)}) collective-permute-start(bf16[256,512]{1,0:T(8,128)(2,1)} %collective-permute-done.11.refs_0_), channel_id=1, source_target_pairs={{0,4},{4,8},{8,12},{12,14},{14,10},{10,6},{6,2},{2,0},{1,5},{5,9},... | collective-permute-start | bytes 786440 | tf_op jit(solution)/shard_map/ppermute | solution.py:128
  67.8 11.2 %collective-permute-start.28 = (bf16[256,512]{1,0:T(8,128)(2,1)}, bf16[256,512]{1,0:T(8,128)(2,1)S(1)}, u32[]{:S(2)}, u32[]{:S(2)}) collective-permute-start(bf16[256,512]{1,0:T(8,128)(2,1)} %collective-permute-done.22.refs_3_), channel_id=1, source_target_pairs={{4,0},{8,4},{12,8},{14,12},{10,14},{6,10},{2,6},{0,2},{5,1},{9,5},... | collective-permute-start | bytes 786440 | tf_op jit(solution)/shard_map/ppermute | solution.py:128
  71.4 11.6 %collective-permute-start.26 = (bf16[256,512]{1,0:T(8,128)(2,1)}, bf16[256,512]{1,0:T(8,128)(2,1)}, u32[]{:S(2)}, u32[]{:S(2)}) collective-permute-start(bf16[256,512]{1,0:T(8,128)(2,1)} %collective-permute-done.21.refs_2_), channel_id=1, source_target_pairs={{4,0},{8,4},{12,8},{14,12},{10,14},{6,10},{2,6},{0,2},{5,1},{9,5},... | collective-permute-start | bytes 786440 | tf_op jit(solution)/shard_map/ppermute | solution.py:128
  71.9 11.6 %collective-permute-start.24 = (bf16[256,512]{1,0:T(8,128)(2,1)}, bf16[256,512]{1,0:T(8,128)(2,1)}, u32[]{:S(2)}, u32[]{:S(2)}) collective-permute-start(bf16[256,512]{1,0:T(8,128)(2,1)} %collective-permute-done.20.refs_1_), channel_id=1, source_target_pairs={{0,4},{4,8},{8,12},{12,14},{14,10},{10,6},{6,2},{2,0},{1,5},{5,9},... | collective-permute-start | bytes 786440 | tf_op jit(solution)/shard_map/ppermute | solution.py:128
  73.5 11.6 %collective-permute-start.19 = (bf16[256,512]{1,0:T(8,128)(2,1)}, bf16[256,512]{1,0:T(8,128)(2,1)}, u32[]{:S(2)}, u32[]{:S(2)}) collective-permute-start(bf16[256,512]{1,0:T(8,128)(2,1)} %collective-permute-done.15.refs_0_), channel_id=1, source_target_pairs={{0,4},{4,8},{8,12},{12,14},{14,10},{10,6},{6,2},{2,0},{1,5},{5,9},... | collective-permute-start | bytes 786440 | tf_op jit(solution)/shard_map/ppermute | solution.py:128
  75.1 16.0 %copy-start.10 = (s32[4]{0:T(128)S(1)}, s32[4]{0:T(128)}, u32[]{:S(2)}) copy-start(s32[4]{0:T(128)} %param.13) | copy-start | bytes 52
  79.0 17.0 %collective-permute-start.29 = (bf16[256,512]{1,0:T(8,128)(2,1)S(1)}, bf16[256,512]{1,0:T(8,128)(2,1)}, u32[]{:S(2)}, u32[]{:S(2)}) collective-permute-start(bf16[256,512]{1,0:T(8,128)(2,1)S(1)} %collective-permute-done.28.refs_3_), channel_id=1, source_target_pairs={{4,0},{8,4},{12,8},{14,12},{10,14},{6,10},{2,6},{0,2},{5,1},{9,5},... | collective-permute-start | bytes 786440 | tf_op jit(solution)/shard_map/ppermute | solution.py:128
  83.0 13.0 %collective-permute-start.27 = (bf16[256,512]{1,0:T(8,128)(2,1)}, bf16[256,512]{1,0:T(8,128)(2,1)}, u32[]{:S(2)}, u32[]{:S(2)}) collective-permute-start(bf16[256,512]{1,0:T(8,128)(2,1)} %collective-permute-done.26.refs_2_), channel_id=1, source_target_pairs={{4,0},{8,4},{12,8},{14,12},{10,14},{6,10},{2,6},{0,2},{5,1},{9,5},... | collective-permute-start | bytes 786440 | tf_op jit(solution)/shard_map/ppermute | solution.py:128
  83.4 12.6 %collective-permute-start.25 = (bf16[256,512]{1,0:T(8,128)(2,1)}, bf16[256,512]{1,0:T(8,128)(2,1)}, u32[]{:S(2)}, u32[]{:S(2)}) collective-permute-start(bf16[256,512]{1,0:T(8,128)(2,1)} %collective-permute-done.24.refs_1_), channel_id=1, source_target_pairs={{0,4},{4,8},{8,12},{12,14},{14,10},{10,6},{6,2},{2,0},{1,5},{5,9},... | collective-permute-start | bytes 786440 | tf_op jit(solution)/shard_map/ppermute | solution.py:128
  85.0 11.0 %collective-permute-start.23 = (bf16[256,512]{1,0:T(8,128)(2,1)}, bf16[256,512]{1,0:T(8,128)(2,1)}, u32[]{:S(2)}, u32[]{:S(2)}) collective-permute-start(bf16[256,512]{1,0:T(8,128)(2,1)} %collective-permute-done.19.refs_0_), channel_id=1, source_target_pairs={{0,4},{4,8},{8,12},{12,14},{14,10},{10,6},{6,2},{2,0},{1,5},{5,9},... | collective-permute-start | bytes 786440 | tf_op jit(solution)/shard_map/ppermute | solution.py:128
  96.0 5.3 %copy-start.7 = (bf16[4,4,4,8,128]{4,3,2,1,0:T(8,128)(2,1)S(1)}, bf16[4,4,4,8,128]{4,3,2,1,0:T(8,128)(2,1)}, u32[]{:S(2)}) copy-start(bf16[4,4,4,8,128]{4,3,2,1,0:T(8,128)(2,1)} %reshape.163) | copy-start | bytes 393220
  100.9 2.9 %collective-permute-start.30 = (bf16[1024,512]{1,0:T(8,128)(2,1)}, bf16[1024,512]{1,0:T(8,128)(2,1)S(1)}, u32[]{:S(2)}, u32[]{:S(2)}) collective-permute-start(bf16[1024,512]{1,0:T(8,128)(2,1)} %get-tuple-element.72), channel_id=1, source_target_pairs={{0,1},{1,0},{2,3},{3,2},{4,5},{5,4},{6,7},{7,6},{8,9},{9,8},{10,11... | collective-permute-start | bytes 3145736 | tf_op jit(solution)/shard_map/ppermute | solution.py:178
  103.9 2.4 %copy-start.8 = (bf16[1024,512]{1,0:T(8,128)(2,1)}, bf16[1024,512]{1,0:T(8,128)(2,1)S(1)}, u32[]{:S(2)}) copy-start(bf16[1024,512]{1,0:T(8,128)(2,1)S(1)} %collective-permute-done.30) | copy-start | bytes 3145732
  106.8 1.2 copy-start.5
  106.9 1.5 %copy-start.9 = (bf16[1024,512]{1,0:T(8,128)(2,1)S(1)}, bf16[1024,512]{1,0:T(8,128)(2,1)}, u32[]{:S(2)}) copy-start(bf16[1024,512]{1,0:T(8,128)(2,1)} %copy-done.8) | copy-start | bytes 3145732
  109.9 4.9 %copy-start.6 = (bf16[512,1024]{1,0:T(8,128)(2,1)S(1)}, bf16[512,1024]{1,0:T(8,128)(2,1)}, u32[]{:S(2)}) copy-start(bf16[512,1024]{1,0:T(8,128)(2,1)} %param.12) | copy-start | bytes 3145732
  111.0 13.3 %all-to-all-start = ((f32[8,72,128]{2,1,0:T(8,128)}), f32[8,72,128]{2,1,0:T(8,128)S(1)}, u32[]{:S(2)}, u32[]{:S(2)}) async-start(f32[8,72,128]{2,1,0:T(8,128)} %select_maximum_fusion), calls=%async_computation | async-start | bytes 589824 | tf_op jit(solution)/shard_map/all_to_all | solution.py:199
  124.8 3.8 %collective-permute-start.31 = (bf16[1,64,128]{2,1,0:T(8,128)(2,1)S(1)}, bf16[1,64,128]{2,1,0:T(8,128)(2,1)S(1)}, u32[]{:S(2)}, u32[]{:S(2)}) collective-permute-start(bf16[1,64,128]{2,1,0:T(8,128)(2,1)S(1)} %fusion.35), channel_id=1, source_target_pairs={{0,2},{2,0},{4,6},{6,4},{8,10},{10,8},{12,14},{14,12},{1,3},{3,1},... | collective-permute-start | bytes 49160 | tf_op jit(solution)/shard_map/ppermute | solution.py:213
  128.6 4.1 %collective-permute-start.32 = (bf16[2,64,128]{2,1,0:T(8,128)(2,1)S(1)}, bf16[2,64,128]{2,1,0:T(8,128)(2,1)S(1)}, u32[]{:S(2)}, u32[]{:S(2)}) collective-permute-start(bf16[2,64,128]{2,1,0:T(8,128)(2,1)S(1)} %pad_maximum_fusion.3), channel_id=1, source_target_pairs={{0,4},{2,6},{4,0},{6,2},{8,12},{10,14},{12,8},{14,10},{1,5},{3,7},... | collective-permute-start | bytes 98312 | tf_op jit(solution)/shard_map/ppermute | solution.py:213
  132.8 5.9 %collective-permute-start.33 = (bf16[4,64,128]{2,1,0:T(8,128)(2,1)S(1)}, bf16[4,64,128]{2,1,0:T(8,128)(2,1)S(1)}, u32[]{:S(2)}, u32[]{:S(2)}) collective-permute-start(bf16[4,64,128]{2,1,0:T(8,128)(2,1)S(1)} %pad_maximum_fusion.2), channel_id=1, source_target_pairs={{0,8},{2,10},{4,12},{6,14},{8,0},{10,2},{12,4},{14,6},{1,9},{3,11}... | collective-permute-start | bytes 196616 | tf_op jit(solution)/shard_map/ppermute | solution.py:213
  138.8 1.4 collective-permute-start.34

commit v5 on v4

--- a/solution.py
+++ b/solution.py
@@ -83,7 +83,7 @@
     )(places, tokens, theirs, *flat, *sums)
 
 
-def project(tokens, key_down, value_down):
+def project(tokens, key_down, value_down, early):
     chips = lax.axis_size("chip")
     chip = lax.axis_index("chip")
     core = lax.axis_index("core")
@@ -97,7 +97,7 @@
         block = jnp.concatenate([jnp.where(first, own, got), jnp.where(first, got, own)], 0)
         full = lax.all_gather(block, "chip", axis=0, tiled=True)
         mine, other = mm(tokens, full).astype(BF), mm(theirs, full).astype(BF)
-        return jnp.concatenate([jnp.where(first, mine, other), jnp.where(first, other, mine)], 0)
+        return jnp.concatenate([jnp.where(first, mine, other), jnp.where(first, other, mine)], 0), early
     cycle = list(range(0, chips, 2)) + list(range(chips - 1, 0, -2))
     last = chips - 1
     place = jnp.where(chip & 1 == 0, chip >> 1, last - (chip >> 1))
@@ -122,6 +122,8 @@
     mark = None
     for step in range(1, chips):
         ready = todo
+        if step == 2:
+            held[0], early = lax.optimization_barrier((held[0], early))
         for k in range(2 * chains):
             if mark is not None:
                 held[k], _ = lax.optimization_barrier((held[k], mark))
@@ -132,7 +134,92 @@
         else:
             total, mark = add_pieces(tokens, theirs, ready, total)
             todo = arriving
-    return add_pieces(tokens, theirs, todo, total, core)[0]
+    return add_pieces(tokens, theirs, todo, total, core)[0], early
+
+
+def attend(have, got, core, key_up, value_up, query, bounds, chips):
+    heads, rows = query.shape[:2]
+    tokens = have.shape[0]
+    pairs = rows // 8
+    blocks = pairs * heads // chips
+    scale = 1.0 / DH**0.5
+
+    def kernel(core_ref, have_ref, got_ref, key_up_ref, value_up_ref, query_ref, bounds_ref, out_ref):
+        first = core_ref[0] == 0
+        have, got = have_ref[...], got_ref[...]
+        keys = mm(jnp.where(first, have, got), key_up_ref[...]).astype(BF)
+        values = mm(jnp.where(first, got, have), value_up_ref[...]).astype(BF)
+        position = lax.broadcasted_iota(jnp.int32, (tokens, rows), 0)
+        visible = (position >= bounds_ref[0:1, :]) & (position < bounds_ref[1:2, :])
+        tops, totals = [], []
+        for g in range(heads):
+            lanes = slice(g * DH, (g + 1) * DH)
+            scores = scale * lax.dot_general(
+                keys[:, lanes], query_ref[g], (((1,), (1,)), ((), ())), preferred_element_type=F32
+            )
+            scores = jnp.where(visible, scores, -1e30)
+            top = jnp.max(scores, 0, keepdims=True)
+            weights = jnp.where(visible, jnp.exp(scores - top), 0.0)
+            tops.append(top)
+            totals.append(jnp.sum(weights, 0, keepdims=True))
+            summed = lax.dot_general(
+                weights.astype(BF), values[:, lanes], (((0,), (0,)), ((), ())), preferred_element_type=F32
+            )
+            for pair in range(pairs):
+                block = pair * heads + g
+                out_ref[block // blocks, block % blocks] = summed[pair * 8 : (pair + 1) * 8]
+        stats = jnp.transpose(jnp.concatenate(tops + totals, 0))
+        stride = min(blocks, heads)
+        for chip in range(chips):
+            spots = [divmod(b, heads) for b in range(chip * blocks, (chip + 1) * blocks, stride)]
+            sides = [
+                stats[pair * 8 : (pair + 1) * 8, side + g : side + g + stride] for side in (0, heads) for pair, g in spots
+            ]
+            out_ref[chip, blocks] = jnp.zeros((8, DH), F32)
+            out_ref[chip, blocks, :, : 2 * blocks] = jnp.concatenate(sides, 1)
+
+    in_vmem = pl.BlockSpec(memory_space=pltpu.VMEM)
+    return pl.pallas_call(
+        kernel,
+        out_shape=jax.ShapeDtypeStruct((chips, blocks + 1, 8, DH), F32),
+        in_specs=[pl.BlockSpec(memory_space=pltpu.SMEM)] + [in_vmem] * 6,
+        out_specs=in_vmem,
+        compiler_params=pltpu.CompilerParams(vmem_limit_bytes=40 * 2**20),
+        cost_estimate=pl.CostEstimate(
+            flops=4 * tokens * (have.shape[1] * heads * DH + heads * rows * DH),
+            bytes_accessed=4 * tokens * have.shape[1],
+            transcendentals=tokens * heads * rows,
+        ),
+    )(core.reshape(1), have, got, key_up, value_up, query, bounds)
+
+
+def merge(arrived, fresh_stats, fresh_summed):
+    chips, blocks = arrived.shape[0], arrived.shape[1] - 1
+
+    def kernel(arrived_ref, stats_ref, summed_ref, out_ref):
+        results = []
+        for b in range(blocks):
+            top = arrived_ref[:, blocks, :, b : b + 1]
+            total = arrived_ref[:, blocks, :, blocks + b : blocks + b + 1]
+            fresh_top = stats_ref[:, b : b + 1]
+            overall = jnp.maximum(jnp.max(top, 0), fresh_top)
+            carried = jnp.exp(top - overall[None])
+            fresh_carried = jnp.exp(fresh_top - overall)
+            total = jnp.sum(total * carried, 0) + stats_ref[:, blocks + b : blocks + b + 1] * fresh_carried
+            summed = jnp.sum(arrived_ref[:, b] * carried, 0) + summed_ref[b * 8 : (b + 1) * 8, :] * fresh_carried
+            results.append(summed / total)
+        out_ref[...] = jnp.concatenate(results, 0).astype(BF)
+
+    in_vmem = pl.BlockSpec(memory_space=pltpu.VMEM)
+    return pl.pallas_call(
+        kernel,
+        out_shape=jax.ShapeDtypeStruct((blocks * 8, DH), BF),
+        in_specs=[in_vmem] * 3,
+        out_specs=in_vmem,
+        cost_estimate=pl.CostEstimate(
+            flops=2 * chips * blocks * 8 * DH, bytes_accessed=4 * arrived.size, transcendentals=chips * blocks * 8
+        ),
+    )(arrived, fresh_stats, fresh_summed)
 
 
 def on_device(tokens, key_down, value_down, key_up, value_up, prompt_lens, queries, new_latent):
@@ -149,8 +236,6 @@
     pairs = steps_count * req_count
     rows = pairs * heads * group
     share = rows // chips
-
-    have = project(tokens, key_down, value_down)
 
     query = lax.dynamic_index_in_dim(
         queries.reshape(steps_count, req_count, CORES, heads * group * DH), core, 2, keepdims=False
@@ -171,49 +256,35 @@
     def my_share(x):
         return lax.dynamic_slice_in_dim(x, chip * share, share, 0)
 
-    fresh_top = my_share(fresh_top.reshape(rows))
-    fresh_total = my_share(fresh_total.reshape(rows))
     fresh_summed = my_share(fresh_summed.reshape(rows, DH))
-
+    fresh_stats = [my_share(x.reshape(rows)).reshape(-1, group).T for x in (fresh_top, fresh_total)]
+    fresh_stats = jnp.pad(jnp.concatenate(fresh_stats, 1), ((0, 0), (0, DH - 2 * share // group)))
+
+    offsets = jnp.cumsum(prompt_lens) - prompt_lens
+    bounds = jnp.stack([offsets, offsets + prompt_lens]) - chip * CORES * tok_rows
+    bounds = jnp.broadcast_to(bounds[:, None, :, None], (2, steps_count, req_count, group)).reshape(2, -1)
+    by_head = query.transpose(2, 0, 1, 3, 4).reshape(heads, pairs * group, DH)
+
+    early = (by_head, bounds, key_up, value_up, fresh_stats, fresh_summed)
+    have, early = project(tokens, key_down, value_down, early)
+    by_head, bounds, key_up, value_up, fresh_stats, fresh_summed = early
     got = lax.ppermute(have, "core", SWAP)
-    key_latent = jnp.where(first, have, got)
-    value_latent = jnp.where(first, got, have)
-    keys = mm(key_latent, key_up).astype(BF)
-    values = mm(value_latent, value_up).astype(BF)
-    position = chip * CORES * tok_rows + jnp.arange(CORES * tok_rows, dtype=jnp.int32)
-    offsets = jnp.cumsum(prompt_lens) - prompt_lens
-    member = (position[None, :] >= offsets[:, None]) & (position[None, :] < (offsets + prompt_lens)[:, None])
-    key_heads = keys.reshape(-1, heads, DH)
-    value_heads = values.reshape(-1, heads, DH)
-    scores = jnp.einsum("srgjd,tgd->srgjt", query, key_heads, preferred_element_type=F32) * scale
-    visible = member[None, :, None, None, :]
-    scores = jnp.where(visible, scores, -1e30)
-    top = jnp.max(scores, -1)
-    weights = jnp.where(visible, jnp.exp(scores - top[..., None]), 0.0)
-    total = jnp.sum(weights, -1)
-    summed = jnp.einsum("srgjt,tgd->srgjd", weights.astype(BF), value_heads, preferred_element_type=F32)
-
-    stats = jnp.stack([top.reshape(chips, share), total.reshape(chips, share)], 1).reshape(chips, 1, 2 * share)
-    stats = jnp.pad(stats, ((0, 0), (0, 7), (0, DH - 2 * share)))
-    sending = jnp.concatenate([summed.reshape(chips, share, DH), stats], 1)
+    sending = attend(have, got, core, key_up, value_up, by_head, bounds, chips)
+
     arrived = lax.all_to_all(sending, "chip", split_axis=0, concat_axis=0, tiled=True)
-    tops = arrived[:, share, :share]
-    totals = arrived[:, share, share : 2 * share]
-    overall = jnp.maximum(jnp.max(tops, 0), fresh_top)
-    carried = jnp.exp(tops - overall[None])
-    fresh_carried = jnp.exp(fresh_top - overall)
-    total = jnp.sum(totals * carried, 0) + fresh_total * fresh_carried
-    summed = jnp.sum(arrived[:, :share] * carried[..., None], 0) + fresh_summed * fresh_carried[:, None]
-    result = (summed / total[:, None]).astype(BF)
-
-    if chips & (chips - 1) == 0:
-        whole = result.reshape(1, share, DH)
-        span = 1
-        while span < chips:
-            away = lax.ppermute(whole, "chip", [(c, c ^ span) for c in range(chips)])
-            upper = (chip & span) != 0
-            whole = jnp.concatenate([jnp.where(upper, away, whole), jnp.where(upper, whole, away)], 0)
-            span *= 2
+    result = merge(arrived, fresh_stats, fresh_summed)
+
+    if chips == 8:
+        near = lax.ppermute(result, "chip", [(c, c ^ 1) for c in range(chips)])
+        upper = chip & 1 == 1
+        couple = jnp.concatenate([jnp.where(upper, near, result), jnp.where(upper, result, near)], 0)
+        far = [couple] + [lax.ppermute(couple, "chip", [(c, c ^ (2 * d)) for c in range(chips)]) for d in range(1, 4)]
+        odd, high = chip & 2 != 0, chip & 4 != 0
+
+        def of(z):
+            return jnp.where(high, jnp.where(odd, far[z ^ 3], far[z ^ 2]), jnp.where(odd, far[z ^ 1], far[z]))
+
+        whole = jnp.concatenate([of(z) for z in range(4)], 0)
     else:
         whole = lax.all_gather(result, "chip", axis=0, tiled=True)
     whole = whole.reshape(pairs, 1, rows // pairs * DH)

time: 142 us -> 139 us (0.979)
  blocking collectives: 0 us -> 15.4 us
  waiting for transfers between devices: 50.5 us -> 41.3 us
  starting transfers between devices: 40.1 us -> 34.9 us
  matrix products: 5.83 us -> 1.35 us
  Pallas kernels: 29.3 us -> 32.6 us
  local copies, waits for them, and re-layouts: 10.9 us -> 8.91 us
    all_to_all x0 -> x1, blocking collectives: none -> 15.4 us  [on_device(): lax.all_to_all(sending, 'chip', split_axis=0, concat_axis=0, tiled=True)]
    all_to_all x1 -> x0, waiting for transfers between devices: 8.94 us -> none  [on_device(): lax.all_to_all(sending, 'chip', split_axis=0, concat_axis=0, tiled=True)]
    pallas_call x0 -> x2, Pallas kernels: none -> 4.68 us  [the longest x1 2.74 us: attend(): pl.pallas_call(kernel, out_shape=jax.ShapeDtypeStruct((chips, blocks + 1,...]
    all_to_all x1 -> x0, starting transfers between devices: 3.42 us -> none  [on_device(): lax.all_to_all(sending, 'chip', split_axis=0, concat_axis=0, tiled=True)]
    ppermute x3 -> x4, waiting for transfers between devices: 9.97 us -> 6.6 us  [the longest x3 3.35 us: on_device(): lax.ppermute(couple, 'chip', [(c, c ^ 2 * d) for c in range(chips)])]
    dot_general x4 -> x2, matrix products: 3.5 us -> 0.34 us  [mm(): return jnp.dot(a, b, preferred_element_type=F32)]
    ppermute x28, starting transfers between devices: 31.8 us -> 28.7 us  [project(): held[k] = lax.ppermute(held[k], 'chip', ways[k])]
    ppermute x28, waiting for transfers between devices: 26.9 us -> 29.1 us  [project(): held[k] = lax.ppermute(held[k], 'chip', ways[k])]
  transfers between devices with their start and end apart: 36 -> 36, of which waited for: 16 -> 25; matrix products, arithmetic and copies ran while one was open for 6% -> 5% of each run, Pallas kernels for 17% -> 17%
where the time goes in v5:
time: 139 us; the launch traced here: 138 us
  waiting for transfers between devices  41.3 us (30%)
  starting transfers between devices  34.9 us (25%)
  Pallas kernels  32.6 us (23%)
  blocking collectives  15.4 us (11%)
  local copies, waits for them, and re-layouts  8.91 us (6%)
  other arithmetic  3.71 us (3%)
    ppermute x28, waiting for transfers between devices, project(): held[k] = lax.ppermute(held[k], 'chip', ways[k])  29.1 us
    ppermute x28, starting transfers between devices, project(): held[k] = lax.ppermute(held[k], 'chip', ways[k])  28.7 us
    pallas_call x7, Pallas kernels, add_pieces(): pl.pallas_call(kernel, out_shape=(jax.ShapeDtypeStruct((2 * tok_rows, wid...  27.9 us
    all_to_all x1, blocking collectives, on_device(): lax.all_to_all(sending, 'chip', split_axis=0, concat_axis=0, tiled=True)  15.4 us
    ppermute x3, starting transfers between devices, on_device(): lax.ppermute(couple, 'chip', [(c, c ^ 2 * d) for c in range(chips)])  4.44 us
    unnamed x18, local copies, waits for them, and re-layouts  3.55 us
    ppermute x3, waiting for transfers between devices, on_device(): lax.ppermute(couple, 'chip', [(c, c ^ 2 * d) for c in range(chips)])  3.35 us
    ppermute x1, waiting for transfers between devices, on_device(): near = lax.ppermute(result, 'chip', [(c, c ^ 1) for c in range(chips)])  3.25 us
  transfers between devices with their start and end apart: 36, of which 25 were waited for; matrix products, arithmetic and copies ran while one was open for 5% of the time, Pallas kernels for 17%

profile of v5, /device:TPU:0, one launch (start us, length us, event | category | flops | bytes accessed | tf_op | source)
XLA Modules:
  0.0 138.4 jit_solution(5626818356921462342)
XLA Ops:
  0.0 1.3 broadcast_select_fusion
  1.3 0.5 collective-permute-start
  1.9 1.5 %collective-permute-done.refs_1_ = bf16[512,512]{1,0:T(8,128)(2,1)S(1)} collective-permute-done((bf16[512,512]{1,0:T(8,128)(2,1)S(1)}, bf16[512,512]{1,0:T(8,128)(2,1)S(1)}, u32[]{:S(2)}, u32[]{:S(2)}) %collective-permute-start) | collective-permute-done | bytes 524320 | tf_op jit(solution)/shard_map/ppermute | solution.py:94
  3.8 2.8 %collective-permute-start.4 = (bf16[256,512]{1,0:T(8,128)(2,1)S(1)}, bf16[256,512]{1,0:T(8,128)(2,1)S(1)}, u32[]{:S(2)}, u32[]{:S(2)}) collective-permute-start(bf16[256,512]{1,0:T(8,128)(2,1)S(1)} %get-tuple-element.91), channel_id=1, source_target_pairs={{0,4},{4,8},{8,12},{12,14},{14,10},{10,6},{6,2},{2,0},{1,5},{5,9},... | collective-permute-start | bytes 786440 | tf_op jit(solution)/shard_map/ppermute | solution.py:130
  6.6 1.6 %collective-permute-start.2 = (bf16[256,512]{1,0:T(8,128)(2,1)S(1)}, bf16[256,512]{1,0:T(8,128)(2,1)}, u32[]{:S(2)}, u32[]{:S(2)}) collective-permute-start(bf16[256,512]{1,0:T(8,128)(2,1)S(1)} %get-tuple-element.92), channel_id=1, source_target_pairs={{0,4},{4,8},{8,12},{12,14},{14,10},{10,6},{6,2},{2,0},{1,5},{5,9},... | collective-permute-start | bytes 786440 | tf_op jit(solution)/shard_map/ppermute | solution.py:130
  8.7 0.8 dynamic-slice_reduce_fusion
  9.6 1.3 constant_dynamic-slice_fusion.1
  11.1 0.8 copy-done
  12.1 0.7 fusion.19
  15.0 0.7 select_maximum_fusion.stats_ref
  15.6 0.6 constant_dynamic-slice_fusion.summed_ref
  16.3 2.8 %collective-permute-done.2.refs_2_ = bf16[256,512]{1,0:T(8,128)(2,1)} collective-permute-done((bf16[256,512]{1,0:T(8,128)(2,1)S(1)}, bf16[256,512]{1,0:T(8,128)(2,1)}, u32[]{:S(2)}, u32[]{:S(2)}) %collective-permute-start.2) | collective-permute-done | bytes 262176 | tf_op jit(solution)/shard_map/ppermute | solution.py:130
  19.1 1.8 %collective-permute-start.3 = (bf16[256,512]{1,0:T(8,128)(2,1)}, bf16[256,512]{1,0:T(8,128)(2,1)}, u32[]{:S(2)}, u32[]{:S(2)}) collective-permute-start(bf16[256,512]{1,0:T(8,128)(2,1)} %collective-permute-done.2.refs_2_), channel_id=1, source_target_pairs={{0,4},{4,8},{8,12},{12,14},{14,10},{10,6},{6,2},{2,0},{1,5},{5,9},... | collective-permute-start | bytes 786440 | tf_op jit(solution)/shard_map/ppermute | solution.py:130
  20.9 1.6 %collective-permute-start.8 = (bf16[256,512]{1,0:T(8,128)(2,1)S(1)}, bf16[256,512]{1,0:T(8,128)(2,1)}, u32[]{:S(2)}, u32[]{:S(2)}) collective-permute-start(bf16[256,512]{1,0:T(8,128)(2,1)S(1)} %collective-permute-done.4.refs_3_), channel_id=1, source_target_pairs={{0,4},{4,8},{8,12},{12,14},{14,10},{10,6},{6,2},{2,0},{1,5},{5,9},... | collective-permute-start | bytes 786440 | tf_op jit(solution)/shard_map/ppermute | solution.py:130
  23.2 5.2 %collective-permute-done.5.refs_4_ = bf16[256,512]{1,0:T(8,128)(2,1)} collective-permute-done((bf16[256,512]{1,0:T(8,128)(2,1)S(1)}, bf16[256,512]{1,0:T(8,128)(2,1)}, u32[]{:S(2)}, u32[]{:S(2)}) %collective-permute-start.5) | collective-permute-done | bytes 262176 | tf_op jit(solution)/shard_map/ppermute | solution.py:130
  28.9 1.0 copy-done.3
  30.0 5.2 %shard_map.82 = (f32[1024,512]{1,0:T(8,128)S(1)}, f32[8,128]{1,0:T(8,128)}) custom-call(s32[4]{0:T(128)S(1)} %pad_add_fusion.1.places_ref, bf16[512,8192]{1,0:T(8,128)(2,1)} %mine_ref.13, bf16[512,8192]{1,0:T(8,128)(2,1)} %collective-permute-done.1.theirs_ref, bf16[512,512]{1,0:T(8,128)(2,1)S(1)} %get-tuple-element.87.refs_0_, ...), custom_call_target="tpu_custom_call" | custom-call | flops 2147483648 | bytes 4194304 | tf_op jit(solution)/shard_map/pallas_call | solution.py:65
  35.3 2.0 %collective-permute-start.7 = (bf16[256,512]{1,0:T(8,128)(2,1)}, bf16[256,512]{1,0:T(8,128)(2,1)S(1)}, u32[]{:S(2)}, u32[]{:S(2)}) collective-permute-start(bf16[256,512]{1,0:T(8,128)(2,1)} %collective-permute-done.3.refs_0_), channel_id=1, source_target_pairs={{0,4},{4,8},{8,12},{12,14},{14,10},{10,6},{6,2},{2,0},{1,5},{5,9},... | collective-permute-start | bytes 786440 | tf_op jit(solution)/shard_map/ppermute | solution.py:130
  37.3 1.6 %collective-permute-start.12 = (bf16[256,512]{1,0:T(8,128)(2,1)}, bf16[256,512]{1,0:T(8,128)(2,1)}, u32[]{:S(2)}, u32[]{:S(2)}) collective-permute-start(bf16[256,512]{1,0:T(8,128)(2,1)} %collective-permute-done.8.refs_1_), channel_id=1, source_target_pairs={{0,4},{4,8},{8,12},{12,14},{14,10},{10,6},{6,2},{2,0},{1,5},{5,9},... | collective-permute-start | bytes 786440 | tf_op jit(solution)/shard_map/ppermute | solution.py:130
  38.9 0.8 collective-permute-done.9.refs_2_
  40.1 3.9 %shard_map.83 = (f32[1024,512]{1,0:T(8,128)S(1)}, f32[8,128]{1,0:T(8,128)}) custom-call(s32[2]{0:T(128)S(1)} %pad_add_fusion.2.places_ref, bf16[512,8192]{1,0:T(8,128)(2,1)} %mine_ref.13, bf16[512,8192]{1,0:T(8,128)(2,1)} %collective-permute-done.1.theirs_ref, bf16[256,512]{1,0:T(8,128)(2,1)} %collective-permute-done.3.refs_0_, ...), custom_call_target="tpu_custom_call", output_to_operand_aliasing={{0}: (7, {})} | custom-call | flops 1073741824 | bytes 2097152 | tf_op jit(solution)/shard_map/pallas_call | solution.py:65
  44.0 1.1 collective-permute-done.14.refs_3_
  45.6 1.6 %collective-permute-start.11 = (bf16[256,512]{1,0:T(8,128)(2,1)S(1)}, bf16[256,512]{1,0:T(8,128)(2,1)}, u32[]{:S(2)}, u32[]{:S(2)}) collective-permute-start(bf16[256,512]{1,0:T(8,128)(2,1)S(1)} %collective-permute-done.7.refs_0_), channel_id=1, source_target_pairs={{0,4},{4,8},{8,12},{12,14},{14,10},{10,6},{6,2},{2,0},{1,5},{5,9},... | collective-permute-start | bytes 786440 | tf_op jit(solution)/shard_map/ppermute | solution.py:130
  47.2 1.4 collective-permute-done.12.refs_1_
  48.5 1.3 collective-permute-start.16
  49.8 1.1 collective-permute-done.13.refs_2_
  51.4 3.7 %shard_map.84 = (f32[1024,512]{1,0:T(8,128)S(1)}, f32[8,128]{1,0:T(8,128)}) custom-call(s32[2]{0:T(128)S(1)} %pad_add_fusion.3.places_ref, bf16[512,8192]{1,0:T(8,128)(2,1)} %mine_ref.13, bf16[512,8192]{1,0:T(8,128)(2,1)} %collective-permute-done.1.theirs_ref, bf16[256,512]{1,0:T(8,128)(2,1)S(1)} %collective-permute-done.7.refs_0_, ...), custom_call_target="tpu_custom_call", output_to_operand_aliasing={{0}: (7, {})} | custom-call | flops 1073741824 | bytes 2097152 | tf_op jit(solution)/shard_map/pallas_call | solution.py:65
  55.1 1.4 collective-permute-done.18.refs_3_
  56.9 1.6 %collective-permute-start.15 = (bf16[256,512]{1,0:T(8,128)(2,1)}, bf16[256,512]{1,0:T(8,128)(2,1)S(1)}, u32[]{:S(2)}, u32[]{:S(2)}) collective-permute-start(bf16[256,512]{1,0:T(8,128)(2,1)} %collective-permute-done.11.refs_0_), channel_id=1, source_target_pairs={{0,4},{4,8},{8,12},{12,14},{14,10},{10,6},{6,2},{2,0},{1,5},{5,9},... | collective-permute-start | bytes 786440 | tf_op jit(solution)/shard_map/ppermute | solution.py:130
  58.5 0.9 collective-permute-done.16.refs_1_
  59.4 1.3 collective-permute-start.20
  60.7 1.4 collective-permute-done.17.refs_2_
  62.6 3.9 %shard_map.85 = (f32[1024,512]{1,0:T(8,128)S(1)}, f32[8,128]{1,0:T(8,128)}) custom-call(s32[2]{0:T(128)S(1)} %pad_add_fusion.4.places_ref, bf16[512,8192]{1,0:T(8,128)(2,1)} %mine_ref.13, bf16[512,8192]{1,0:T(8,128)(2,1)} %collective-permute-done.1.theirs_ref, bf16[256,512]{1,0:T(8,128)(2,1)} %collective-permute-done.11.refs_0_, ...), custom_call_target="tpu_custom_call", output_to_operand_aliasing={{0}: (7, {})} | custom-call | flops 1073741824 | bytes 2097152 | tf_op jit(solution)/shard_map/pallas_call | solution.py:65
  66.5 1.1 collective-permute-done.22.refs_3_
  68.1 0.7 copy-done.4
  68.8 0.9 collective-permute-done.20.refs_1_
  69.6 1.4 %collective-permute-start.24 = (bf16[256,512]{1,0:T(8,128)(2,1)}, bf16[256,512]{1,0:T(8,128)(2,1)S(1)}, u32[]{:S(2)}, u32[]{:S(2)}) collective-permute-start(bf16[256,512]{1,0:T(8,128)(2,1)} %collective-permute-done.20.refs_1_), channel_id=1, source_target_pairs={{0,4},{4,8},{8,12},{12,14},{14,10},{10,6},{6,2},{2,0},{1,5},{5,9},... | collective-permute-start | bytes 786440 | tf_op jit(solution)/shard_map/ppermute | solution.py:130
  71.0 1.6 %collective-permute-start.19 = (bf16[256,512]{1,0:T(8,128)(2,1)}, bf16[256,512]{1,0:T(8,128)(2,1)}, u32[]{:S(2)}, u32[]{:S(2)}) collective-permute-start(bf16[256,512]{1,0:T(8,128)(2,1)} %copy-done.4), channel_id=1, source_target_pairs={{0,4},{4,8},{8,12},{12,14},{14,10},{10,6},{6,2},{2,0},{1,5},{5,9},... | collective-permute-start | bytes 786440 | tf_op jit(solution)/shard_map/ppermute | solution.py:130
  72.6 0.7 collective-permute-done.21.refs_2_
  73.9 0.9 copy-done.5
  74.8 3.7 %shard_map.86 = (f32[1024,512]{1,0:T(8,128)S(1)}, f32[8,128]{1,0:T(8,128)}) custom-call(s32[2]{0:T(128)S(1)} %pad_add_fusion.5.places_ref, bf16[512,8192]{1,0:T(8,128)(2,1)} %mine_ref.13, bf16[512,8192]{1,0:T(8,128)(2,1)} %collective-permute-done.1.theirs_ref, bf16[256,512]{1,0:T(8,128)(2,1)S(1)} %copy-done.5, ...), custom_call_target="tpu_custom_call", output_to_operand_aliasing={{0}: (7, {})} | custom-call | flops 1073741824 | bytes 2097152 | tf_op jit(solution)/shard_map/pallas_call | solution.py:65
  78.8 2.6 %collective-permute-done.19.refs_0_ = bf16[256,512]{1,0:T(8,128)(2,1)} collective-permute-done((bf16[256,512]{1,0:T(8,128)(2,1)}, bf16[256,512]{1,0:T(8,128)(2,1)}, u32[]{:S(2)}, u32[]{:S(2)}) %collective-permute-start.19) | collective-permute-done | bytes 262176 | tf_op jit(solution)/shard_map/ppermute | solution.py:130
  81.4 2.0 %collective-permute-done.26.refs_2_ = bf16[256,512]{1,0:T(8,128)(2,1)} collective-permute-done((bf16[256,512]{1,0:T(8,128)(2,1)}, bf16[256,512]{1,0:T(8,128)(2,1)}, u32[]{:S(2)}, u32[]{:S(2)}) %collective-permute-start.26) | collective-permute-done | bytes 262176 | tf_op jit(solution)/shard_map/ppermute | solution.py:130
  83.8 1.6 %collective-permute-start.23 = (bf16[256,512]{1,0:T(8,128)(2,1)}, bf16[256,512]{1,0:T(8,128)(2,1)}, u32[]{:S(2)}, u32[]{:S(2)}) collective-permute-start(bf16[256,512]{1,0:T(8,128)(2,1)} %collective-permute-done.19.refs_0_), channel_id=1, source_target_pairs={{0,4},{4,8},{8,12},{12,14},{14,10},{10,6},{6,2},{2,0},{1,5},{5,9},... | collective-permute-start | bytes 786440 | tf_op jit(solution)/shard_map/ppermute | solution.py:130
  85.4 1.6 %collective-permute-start.25 = (bf16[256,512]{1,0:T(8,128)(2,1)S(1)}, bf16[256,512]{1,0:T(8,128)(2,1)}, u32[]{:S(2)}, u32[]{:S(2)}) collective-permute-start(bf16[256,512]{1,0:T(8,128)(2,1)S(1)} %collective-permute-done.24.refs_1_), channel_id=1, source_target_pairs={{0,4},{4,8},{8,12},{12,14},{14,10},{10,6},{6,2},{2,0},{1,5},{5,9},... | collective-permute-start | bytes 786440 | tf_op jit(solution)/shard_map/ppermute | solution.py:130
  87.6 3.7 %shard_map.87 = (f32[1024,512]{1,0:T(8,128)S(1)}, f32[8,128]{1,0:T(8,128)}) custom-call(s32[2]{0:T(128)S(1)} %pad_add_fusion.6.places_ref, bf16[512,8192]{1,0:T(8,128)(2,1)} %mine_ref.13, bf16[512,8192]{1,0:T(8,128)(2,1)} %collective-permute-done.1.theirs_ref, bf16[256,512]{1,0:T(8,128)(2,1)} %collective-permute-done.19.refs_0_, ...), custom_call_target="tpu_custom_call", output_to_operand_aliasing={{0}: (7, {})} | custom-call | flops 1073741824 | bytes 2097152 | tf_op jit(solution)/shard_map/pallas_call | solution.py:65
  91.3 1.5 %collective-permute-done.27.refs_2_ = bf16[256,512]{1,0:T(8,128)(2,1)S(1)} collective-permute-done((bf16[256,512]{1,0:T(8,128)(2,1)}, bf16[256,512]{1,0:T(8,128)(2,1)S(1)}, u32[]{:S(2)}, u32[]{:S(2)}) %collective-permute-start.27) | collective-permute-done | bytes 262176 | tf_op jit(solution)/shard_map/ppermute | solution.py:130
  92.8 0.6 collective-permute-done.23.refs_0_
  93.4 3.2 %collective-permute-done.25.refs_1_ = bf16[256,512]{1,0:T(8,128)(2,1)} collective-permute-done((bf16[256,512]{1,0:T(8,128)(2,1)S(1)}, bf16[256,512]{1,0:T(8,128)(2,1)}, u32[]{:S(2)}, u32[]{:S(2)}) %collective-permute-start.25) | collective-permute-done | bytes 262176 | tf_op jit(solution)/shard_map/ppermute | solution.py:130
  96.6 3.8 %shard_map.88 = (bf16[1024,512]{1,0:T(8,128)(2,1)S(1)}, f32[8,128]{1,0:T(8,128)}) custom-call(s32[4]{0:T(128)S(1)} %pad_add_fusion.places_ref, bf16[512,8192]{1,0:T(8,128)(2,1)} %mine_ref.13, bf16[512,8192]{1,0:T(8,128)(2,1)} %collective-permute-done.1.theirs_ref, bf16[256,512]{1,0:T(8,128)(2,1)} %collective-permute-done.23.refs_0_, ...), custom_call_target="tpu_custom_call" | custom-call | flops 1073741824 | bytes 2097152 | tf_op jit(solution)/shard_map/pallas_call | solution.py:65
  100.5 2.6 %collective-permute-done.30.got_ref = bf16[1024,512]{1,0:T(8,128)(2,1)S(1)} collective-permute-done((bf16[1024,512]{1,0:T(8,128)(2,1)S(1)}, bf16[1024,512]{1,0:T(8,128)(2,1)S(1)}, u32[]{:S(2)}, u32[]{:S(2)}) %collective-permute-start.30) | collective-permute-done | bytes 1048608 | tf_op jit(solution)/shard_map/ppermute | solution.py:271
  103.2 2.7 %shard_map.89 = f32[8,9,8,128]{3,2,1,0:T(8,128)S(1)} custom-call(s32[1]{0:T(128)} %bitcast.core_ref, bf16[1024,512]{1,0:T(8,128)(2,1)S(1)} %get-tuple-element.80.have_ref, bf16[1024,512]{1,0:T(8,128)(2,1)S(1)} %collective-permute-done.30.got_ref, bf16[512,512]{1,0:T(8,128)(2,1)S(1)} %copy-done.1, bf16[512,512]{1,0:T(8,128)(2,1)S(1)} %get-tuple-element.82.value_up_ref, ...), custom_call_target="tpu_custom_call" | custom-call | flops 1342177280 | bytes 2097152 | tf_op jit(solution)/shard_map/pallas_call | solution.py:182
  105.9 15.4 %all_to_all.5.arrived_ref = f32[8,9,8,128]{3,2,1,0:T(8,128)} all-to-all(f32[8,9,8,128]{3,2,1,0:T(8,128)S(1)} %shard_map.89), channel_id=1, replica_groups=mesh['groups'=2,'chip'=8,'core'=2] {'chip'}, dimensions={0} | all-to-all | bytes 589824 | tf_op jit(solution)/shard_map/all_to_all | solution.py:274
  121.3 1.9 %shard_map.90 = bf16[64,128]{1,0:T(8,128)(2,1)} custom-call(f32[8,9,8,128]{3,2,1,0:T(8,128)} %all_to_all.5.arrived_ref, f32[8,128]{1,0:T(8,128)} %select_maximum_fusion.stats_ref, f32[64,128]{1,0:T(8,128)} %constant_dynamic-slice_fusion.summed_ref), custom_call_target="tpu_custom_call" | custom-call | flops 131072 | bytes 294912 | tf_op jit(solution)/shard_map/pallas_call | solution.py:214
  123.2 0.7 collective-permute-start.31
  123.9 3.3 %collective-permute-done.31 = bf16[64,128]{1,0:T(8,128)(2,1)S(1)} collective-permute-done((bf16[64,128]{1,0:T(8,128)(2,1)}, bf16[64,128]{1,0:T(8,128)(2,1)S(1)}, u32[]{:S(2)}, u32[]{:S(2)}) %collective-permute-start.31) | collective-permute-done | bytes 16416 | tf_op jit(solution)/shard_map/ppermute | solution.py:278
  127.2 0.7 broadcast_select_fusion.13
  127.9 0.7 collective-permute-start.34
  128.6 1.4 collective-permute-start.33
  130.0 2.4 %collective-permute-start.32 = (bf16[128,128]{1,0:T(8,128)(2,1)S(1)}, bf16[128,128]{1,0:T(8,128)(2,1)S(1)}, u32[]{:S(2)}, u32[]{:S(2)}) collective-permute-start(bf16[128,128]{1,0:T(8,128)(2,1)S(1)} %pad_maximum_fusion.2), channel_id=1, source_target_pairs={{0,12},{2,14},{4,8},{6,10},{8,4},{10,6},{12,0},{14,2},{1,13},{3,15... | collective-permute-start | bytes 98312 | tf_op jit(solution)/shard_map/ppermute | solution.py:281
  132.3 1.1 collective-permute-done.33
  133.4 2.3 %collective-permute-done.32 = bf16[128,128]{1,0:T(8,128)(2,1)S(1)} collective-permute-done((bf16[128,128]{1,0:T(8,128)(2,1)S(1)}, bf16[128,128]{1,0:T(8,128)(2,1)S(1)}, u32[]{:S(2)}, u32[]{:S(2)}) %collective-permute-start.32) | collective-permute-done | bytes 32800 | tf_op jit(solution)/shard_map/ppermute | solution.py:281
  135.9 1.3 collective-permute-done.35
  137.6 0.9 reshape.95
  (87 shorter events, 10.2 us)
Async XLA Ops:
  0.0 8.2 %copy-start.8 = (s32[4]{0:T(128)S(1)}, s32[4]{0:T(128)}, u32[]{:S(2)}) copy-start(s32[4]{0:T(128)} %param.13) | copy-start | bytes 52
  0.0 8.3 %copy-start.7 = (bf16[4,4,1024]{2,1,0:T(4,128)(2,1)S(1)}, bf16[4,4,1024]{2,1,0:T(4,128)(2,1)}, u32[]{:S(2)}) copy-start(bf16[4,4,1024]{2,1,0:T(4,128)(2,1)} %param.15) | copy-start | bytes 98308
  0.0 8.4 %copy-start.6 = (bf16[4,4,8192]{2,1,0:T(4,128)(2,1)S(1)}, bf16[4,4,8192]{2,1,0:T(4,128)(2,1)}, u32[]{:S(2)}) copy-start(bf16[4,4,8192]{2,1,0:T(4,128)(2,1)} %param.14) | copy-start | bytes 786436
  1.3 2.1 %collective-permute-start = (bf16[512,512]{1,0:T(8,128)(2,1)S(1)}, bf16[512,512]{1,0:T(8,128)(2,1)S(1)}, u32[]{:S(2)}, u32[]{:S(2)}) collective-permute-start(bf16[512,512]{1,0:T(8,128)(2,1)S(1)} %get-tuple-element.88), channel_id=1, source_target_pairs={{0,1},{1,0},{2,3},{3,2},{4,5},{5,4},{6,7},{7,6},{8,9},{9,8},{10,11... | collective-permute-start | bytes 1572872 | tf_op jit(solution)/shard_map/ppermute | solution.py:94
  3.4 10.0 %copy-start.2 = (bf16[512,512]{1,0:T(8,128)(2,1)}, bf16[512,512]{1,0:T(8,128)(2,1)S(1)}, u32[]{:S(2)}) copy-start(bf16[512,512]{1,0:T(8,128)(2,1)S(1)} %collective-permute-done.refs_1_) | copy-start | bytes 1572868
  3.4 25.5 %collective-permute-start.1 = (bf16[512,8192]{1,0:T(8,128)(2,1)}, bf16[512,8192]{1,0:T(8,128)(2,1)}, u32[]{:S(2)}, u32[]{:S(2)}) collective-permute-start(bf16[512,8192]{1,0:T(8,128)(2,1)} %mine_ref.13), channel_id=1, source_target_pairs={{0,1},{1,0},{2,3},{3,2},{4,5},{5,4},{6,7},{7,6},{8,9},{9,8},{10,11... | collective-permute-start | bytes 25165832 | tf_op jit(solution)/shard_map/ppermute | solution.py:119
  3.8 17.1 %collective-permute-start.4 = (bf16[256,512]{1,0:T(8,128)(2,1)S(1)}, bf16[256,512]{1,0:T(8,128)(2,1)S(1)}, u32[]{:S(2)}, u32[]{:S(2)}) collective-permute-start(bf16[256,512]{1,0:T(8,128)(2,1)S(1)} %get-tuple-element.91), channel_id=1, source_target_pairs={{0,4},{4,8},{8,12},{12,14},{14,10},{10,6},{6,2},{2,0},{1,5},{5,9},... | collective-permute-start | bytes 786440 | tf_op jit(solution)/shard_map/ppermute | solution.py:130
  6.6 12.5 %collective-permute-start.2 = (bf16[256,512]{1,0:T(8,128)(2,1)S(1)}, bf16[256,512]{1,0:T(8,128)(2,1)}, u32[]{:S(2)}, u32[]{:S(2)}) collective-permute-start(bf16[256,512]{1,0:T(8,128)(2,1)S(1)} %get-tuple-element.92), channel_id=1, source_target_pairs={{0,4},{4,8},{8,12},{12,14},{14,10},{10,6},{6,2},{2,0},{1,5},{5,9},... | collective-permute-start | bytes 786440 | tf_op jit(solution)/shard_map/ppermute | solution.py:130
  11.1 0.8 copy-start
  13.4 9.4 %collective-permute-start.6 = (bf16[256,512]{1,0:T(8,128)(2,1)S(1)}, bf16[256,512]{1,0:T(8,128)(2,1)}, u32[]{:S(2)}, u32[]{:S(2)}) collective-permute-start(bf16[256,512]{1,0:T(8,128)(2,1)S(1)} %get-tuple-element.89), channel_id=1, source_target_pairs={{4,0},{8,4},{12,8},{14,12},{10,14},{6,10},{2,6},{0,2},{5,1},{9,5},... | collective-permute-start | bytes 786440 | tf_op jit(solution)/shard_map/ppermute | solution.py:130
  13.9 14.5 %collective-permute-start.5 = (bf16[256,512]{1,0:T(8,128)(2,1)S(1)}, bf16[256,512]{1,0:T(8,128)(2,1)}, u32[]{:S(2)}, u32[]{:S(2)}) collective-permute-start(bf16[256,512]{1,0:T(8,128)(2,1)S(1)} %get-tuple-element.90), channel_id=1, source_target_pairs={{4,0},{8,4},{12,8},{14,12},{10,14},{6,10},{2,6},{0,2},{5,1},{9,5},... | collective-permute-start | bytes 786440 | tf_op jit(solution)/shard_map/ppermute | solution.py:130
  19.1 16.2 %collective-permute-start.3 = (bf16[256,512]{1,0:T(8,128)(2,1)}, bf16[256,512]{1,0:T(8,128)(2,1)}, u32[]{:S(2)}, u32[]{:S(2)}) collective-permute-start(bf16[256,512]{1,0:T(8,128)(2,1)} %collective-permute-done.2.refs_2_), channel_id=1, source_target_pairs={{0,4},{4,8},{8,12},{12,14},{14,10},{10,6},{6,2},{2,0},{1,5},{5,9},... | collective-permute-start | bytes 786440 | tf_op jit(solution)/shard_map/ppermute | solution.py:130
  20.9 16.4 %collective-permute-start.8 = (bf16[256,512]{1,0:T(8,128)(2,1)S(1)}, bf16[256,512]{1,0:T(8,128)(2,1)}, u32[]{:S(2)}, u32[]{:S(2)}) collective-permute-start(bf16[256,512]{1,0:T(8,128)(2,1)S(1)} %collective-permute-done.4.refs_3_), channel_id=1, source_target_pairs={{0,4},{4,8},{8,12},{12,14},{14,10},{10,6},{6,2},{2,0},{1,5},{5,9},... | collective-permute-start | bytes 786440 | tf_op jit(solution)/shard_map/ppermute | solution.py:130
  22.8 12.4 %collective-permute-start.10 = (bf16[256,512]{1,0:T(8,128)(2,1)}, bf16[256,512]{1,0:T(8,128)(2,1)}, u32[]{:S(2)}, u32[]{:S(2)}) collective-permute-start(bf16[256,512]{1,0:T(8,128)(2,1)} %collective-permute-done.6.refs_5_), channel_id=1, source_target_pairs={{4,0},{8,4},{12,8},{14,12},{10,14},{6,10},{2,6},{0,2},{5,1},{9,5},... | collective-permute-start | bytes 786440 | tf_op jit(solution)/shard_map/ppermute | solution.py:130
  28.4 11.2 %collective-permute-start.9 = (bf16[256,512]{1,0:T(8,128)(2,1)}, bf16[256,512]{1,0:T(8,128)(2,1)}, u32[]{:S(2)}, u32[]{:S(2)}) collective-permute-start(bf16[256,512]{1,0:T(8,128)(2,1)} %collective-permute-done.5.refs_4_), channel_id=1, source_target_pairs={{4,0},{8,4},{12,8},{14,12},{10,14},{6,10},{2,6},{0,2},{5,1},{9,5},... | collective-permute-start | bytes 786440 | tf_op jit(solution)/shard_map/ppermute | solution.py:130
  28.9 1.0 copy-start.3
  35.2 9.9 %collective-permute-start.14 = (bf16[256,512]{1,0:T(8,128)(2,1)}, bf16[256,512]{1,0:T(8,128)(2,1)S(1)}, u32[]{:S(2)}, u32[]{:S(2)}) collective-permute-start(bf16[256,512]{1,0:T(8,128)(2,1)} %collective-permute-done.10.refs_3_), channel_id=1, source_target_pairs={{4,0},{8,4},{12,8},{14,12},{10,14},{6,10},{2,6},{0,2},{5,1},{9,5},... | collective-permute-start | bytes 786440 | tf_op jit(solution)/shard_map/ppermute | solution.py:130
  35.3 10.3 %collective-permute-start.7 = (bf16[256,512]{1,0:T(8,128)(2,1)}, bf16[256,512]{1,0:T(8,128)(2,1)S(1)}, u32[]{:S(2)}, u32[]{:S(2)}) collective-permute-start(bf16[256,512]{1,0:T(8,128)(2,1)} %collective-permute-done.3.refs_0_), channel_id=1, source_target_pairs={{0,4},{4,8},{8,12},{12,14},{14,10},{10,6},{6,2},{2,0},{1,5},{5,9},... | collective-permute-start | bytes 786440 | tf_op jit(solution)/shard_map/ppermute | solution.py:130
  37.3 11.3 %collective-permute-start.12 = (bf16[256,512]{1,0:T(8,128)(2,1)}, bf16[256,512]{1,0:T(8,128)(2,1)}, u32[]{:S(2)}, u32[]{:S(2)}) collective-permute-start(bf16[256,512]{1,0:T(8,128)(2,1)} %collective-permute-done.8.refs_1_), channel_id=1, source_target_pairs={{0,4},{4,8},{8,12},{12,14},{14,10},{10,6},{6,2},{2,0},{1,5},{5,9},... | collective-permute-start | bytes 786440 | tf_op jit(solution)/shard_map/ppermute | solution.py:130
  39.6 11.2 %collective-permute-start.13 = (bf16[256,512]{1,0:T(8,128)(2,1)}, bf16[256,512]{1,0:T(8,128)(2,1)}, u32[]{:S(2)}, u32[]{:S(2)}) collective-permute-start(bf16[256,512]{1,0:T(8,128)(2,1)} %collective-permute-done.9.refs_2_), channel_id=1, source_target_pairs={{4,0},{8,4},{12,8},{14,12},{10,14},{6,10},{2,6},{0,2},{5,1},{9,5},... | collective-permute-start | bytes 786440 | tf_op jit(solution)/shard_map/ppermute | solution.py:130
  45.1 11.3 %collective-permute-start.18 = (bf16[256,512]{1,0:T(8,128)(2,1)S(1)}, bf16[256,512]{1,0:T(8,128)(2,1)}, u32[]{:S(2)}, u32[]{:S(2)}) collective-permute-start(bf16[256,512]{1,0:T(8,128)(2,1)S(1)} %collective-permute-done.14.refs_3_), channel_id=1, source_target_pairs={{4,0},{8,4},{12,8},{14,12},{10,14},{6,10},{2,6},{0,2},{5,1},{9,5},... | collective-permute-start | bytes 786440 | tf_op jit(solution)/shard_map/ppermute | solution.py:130
  45.6 11.3 %collective-permute-start.11 = (bf16[256,512]{1,0:T(8,128)(2,1)S(1)}, bf16[256,512]{1,0:T(8,128)(2,1)}, u32[]{:S(2)}, u32[]{:S(2)}) collective-permute-start(bf16[256,512]{1,0:T(8,128)(2,1)S(1)} %collective-permute-done.7.refs_0_), channel_id=1, source_target_pairs={{0,4},{4,8},{8,12},{12,14},{14,10},{10,6},{6,2},{2,0},{1,5},{5,9},... | collective-permute-start | bytes 786440 | tf_op jit(solution)/shard_map/ppermute | solution.py:130
  48.5 10.9 %collective-permute-start.16 = (bf16[256,512]{1,0:T(8,128)(2,1)}, bf16[256,512]{1,0:T(8,128)(2,1)}, u32[]{:S(2)}, u32[]{:S(2)}) collective-permute-start(bf16[256,512]{1,0:T(8,128)(2,1)} %collective-permute-done.12.refs_1_), channel_id=1, source_target_pairs={{0,4},{4,8},{8,12},{12,14},{14,10},{10,6},{6,2},{2,0},{1,5},{5,9},... | collective-permute-start | bytes 786440 | tf_op jit(solution)/shard_map/ppermute | solution.py:130
  50.9 11.2 %collective-permute-start.17 = (bf16[256,512]{1,0:T(8,128)(2,1)}, bf16[256,512]{1,0:T(8,128)(2,1)}, u32[]{:S(2)}, u32[]{:S(2)}) collective-permute-start(bf16[256,512]{1,0:T(8,128)(2,1)} %collective-permute-done.13.refs_2_), channel_id=1, source_target_pairs={{4,0},{8,4},{12,8},{14,12},{10,14},{6,10},{2,6},{0,2},{5,1},{9,5},... | collective-permute-start | bytes 786440 | tf_op jit(solution)/shard_map/ppermute | solution.py:130
  56.5 11.1 %collective-permute-start.22 = (bf16[256,512]{1,0:T(8,128)(2,1)}, bf16[256,512]{1,0:T(8,128)(2,1)S(1)}, u32[]{:S(2)}, u32[]{:S(2)}) collective-permute-start(bf16[256,512]{1,0:T(8,128)(2,1)} %collective-permute-done.18.refs_3_), channel_id=1, source_target_pairs={{4,0},{8,4},{12,8},{14,12},{10,14},{6,10},{2,6},{0,2},{5,1},{9,5},... | collective-permute-start | bytes 786440 | tf_op jit(solution)/shard_map/ppermute | solution.py:130
  56.9 11.1 %collective-permute-start.15 = (bf16[256,512]{1,0:T(8,128)(2,1)}, bf16[256,512]{1,0:T(8,128)(2,1)S(1)}, u32[]{:S(2)}, u32[]{:S(2)}) collective-permute-start(bf16[256,512]{1,0:T(8,128)(2,1)} %collective-permute-done.11.refs_0_), channel_id=1, source_target_pairs={{0,4},{4,8},{8,12},{12,14},{14,10},{10,6},{6,2},{2,0},{1,5},{5,9},... | collective-permute-start | bytes 786440 | tf_op jit(solution)/shard_map/ppermute | solution.py:130
  59.4 10.2 %collective-permute-start.20 = (bf16[256,512]{1,0:T(8,128)(2,1)}, bf16[256,512]{1,0:T(8,128)(2,1)}, u32[]{:S(2)}, u32[]{:S(2)}) collective-permute-start(bf16[256,512]{1,0:T(8,128)(2,1)} %collective-permute-done.16.refs_1_), channel_id=1, source_target_pairs={{0,4},{4,8},{8,12},{12,14},{14,10},{10,6},{6,2},{2,0},{1,5},{5,9},... | collective-permute-start | bytes 786440 | tf_op jit(solution)/shard_map/ppermute | solution.py:130
  62.1 11.2 %collective-permute-start.21 = (bf16[256,512]{1,0:T(8,128)(2,1)}, bf16[256,512]{1,0:T(8,128)(2,1)}, u32[]{:S(2)}, u32[]{:S(2)}) collective-permute-start(bf16[256,512]{1,0:T(8,128)(2,1)} %collective-permute-done.17.refs_2_), channel_id=1, source_target_pairs={{4,0},{8,4},{12,8},{14,12},{10,14},{6,10},{2,6},{0,2},{5,1},{9,5},... | collective-permute-start | bytes 786440 | tf_op jit(solution)/shard_map/ppermute | solution.py:130
  67.6 11.2 %collective-permute-start.28 = (bf16[256,512]{1,0:T(8,128)(2,1)S(1)}, bf16[256,512]{1,0:T(8,128)(2,1)S(1)}, u32[]{:S(2)}, u32[]{:S(2)}) collective-permute-start(bf16[256,512]{1,0:T(8,128)(2,1)S(1)} %collective-permute-done.22.refs_3_), channel_id=1, source_target_pairs={{4,0},{8,4},{12,8},{14,12},{10,14},{6,10},{2,6},{0,2},{5,1},{9,5},... | collective-permute-start | bytes 786440 | tf_op jit(solution)/shard_map/ppermute | solution.py:130
  68.1 0.7 copy-start.4
  69.6 9.2 %collective-permute-start.24 = (bf16[256,512]{1,0:T(8,128)(2,1)}, bf16[256,512]{1,0:T(8,128)(2,1)S(1)}, u32[]{:S(2)}, u32[]{:S(2)}) collective-permute-start(bf16[256,512]{1,0:T(8,128)(2,1)} %collective-permute-done.20.refs_1_), channel_id=1, source_target_pairs={{0,4},{4,8},{8,12},{12,14},{14,10},{10,6},{6,2},{2,0},{1,5},{5,9},... | collective-permute-start | bytes 786440 | tf_op jit(solution)/shard_map/ppermute | solution.py:130
  71.0 10.4 %collective-permute-start.19 = (bf16[256,512]{1,0:T(8,128)(2,1)}, bf16[256,512]{1,0:T(8,128)(2,1)}, u32[]{:S(2)}, u32[]{:S(2)}) collective-permute-start(bf16[256,512]{1,0:T(8,128)(2,1)} %copy-done.4), channel_id=1, source_target_pairs={{0,4},{4,8},{8,12},{12,14},{14,10},{10,6},{6,2},{2,0},{1,5},{5,9},... | collective-permute-start | bytes 786440 | tf_op jit(solution)/shard_map/ppermute | solution.py:130
  73.3 10.0 %collective-permute-start.26 = (bf16[256,512]{1,0:T(8,128)(2,1)}, bf16[256,512]{1,0:T(8,128)(2,1)}, u32[]{:S(2)}, u32[]{:S(2)}) collective-permute-start(bf16[256,512]{1,0:T(8,128)(2,1)} %collective-permute-done.21.refs_2_), channel_id=1, source_target_pairs={{4,0},{8,4},{12,8},{14,12},{10,14},{6,10},{2,6},{0,2},{5,1},{9,5},... | collective-permute-start | bytes 786440 | tf_op jit(solution)/shard_map/ppermute | solution.py:130
  73.8 0.9 copy-start.5
  83.4 9.5 %collective-permute-start.27 = (bf16[256,512]{1,0:T(8,128)(2,1)}, bf16[256,512]{1,0:T(8,128)(2,1)S(1)}, u32[]{:S(2)}, u32[]{:S(2)}) collective-permute-start(bf16[256,512]{1,0:T(8,128)(2,1)} %collective-permute-done.26.refs_2_), channel_id=1, source_target_pairs={{4,0},{8,4},{12,8},{14,12},{10,14},{6,10},{2,6},{0,2},{5,1},{9,5},... | collective-permute-start | bytes 786440 | tf_op jit(solution)/shard_map/ppermute | solution.py:130
  83.8 9.6 %collective-permute-start.23 = (bf16[256,512]{1,0:T(8,128)(2,1)}, bf16[256,512]{1,0:T(8,128)(2,1)}, u32[]{:S(2)}, u32[]{:S(2)}) collective-permute-start(bf16[256,512]{1,0:T(8,128)(2,1)} %collective-permute-done.19.refs_0_), channel_id=1, source_target_pairs={{0,4},{4,8},{8,12},{12,14},{14,10},{10,6},{6,2},{2,0},{1,5},{5,9},... | collective-permute-start | bytes 786440 | tf_op jit(solution)/shard_map/ppermute | solution.py:130
  85.4 11.2 %collective-permute-start.25 = (bf16[256,512]{1,0:T(8,128)(2,1)S(1)}, bf16[256,512]{1,0:T(8,128)(2,1)}, u32[]{:S(2)}, u32[]{:S(2)}) collective-permute-start(bf16[256,512]{1,0:T(8,128)(2,1)S(1)} %collective-permute-done.24.refs_1_), channel_id=1, source_target_pairs={{0,4},{4,8},{8,12},{12,14},{14,10},{10,6},{6,2},{2,0},{1,5},{5,9},... | collective-permute-start | bytes 786440 | tf_op jit(solution)/shard_map/ppermute | solution.py:130
  87.0 9.6 %collective-permute-start.29 = (bf16[256,512]{1,0:T(8,128)(2,1)S(1)}, bf16[256,512]{1,0:T(8,128)(2,1)}, u32[]{:S(2)}, u32[]{:S(2)}) collective-permute-start(bf16[256,512]{1,0:T(8,128)(2,1)S(1)} %collective-permute-done.28.refs_3_), channel_id=1, source_target_pairs={{4,0},{8,4},{12,8},{14,12},{10,14},{6,10},{2,6},{0,2},{5,1},{9,5},... | collective-permute-start | bytes 786440 | tf_op jit(solution)/shard_map/ppermute | solution.py:130
  96.6 6.6 %copy-start.1 = (bf16[512,512]{1,0:T(8,128)(2,1)S(1)}, bf16[512,512]{1,0:T(8,128)(2,1)}, u32[]{:S(2)}) copy-start(bf16[512,512]{1,0:T(8,128)(2,1)} %copy-done) | copy-start | bytes 1572868
  100.4 2.7 %collective-permute-start.30 = (bf16[1024,512]{1,0:T(8,128)(2,1)S(1)}, bf16[1024,512]{1,0:T(8,128)(2,1)S(1)}, u32[]{:S(2)}, u32[]{:S(2)}) collective-permute-start(bf16[1024,512]{1,0:T(8,128)(2,1)S(1)} %get-tuple-element.80.have_ref), channel_id=1, source_target_pairs={{0,1},{1,0},{2,3},{3,2},{4,5},{5,4},{6,7},{7,6},{8,9},{9,8},{10,11... | collective-permute-start | bytes 3145736 | tf_op jit(solution)/shard_map/ppermute | solution.py:271
  123.2 3.9 %collective-permute-start.31 = (bf16[64,128]{1,0:T(8,128)(2,1)}, bf16[64,128]{1,0:T(8,128)(2,1)S(1)}, u32[]{:S(2)}, u32[]{:S(2)}) collective-permute-start(bf16[64,128]{1,0:T(8,128)(2,1)} %shard_map.90), channel_id=1, source_target_pairs={{0,2},{2,0},{4,6},{6,4},{8,10},{10,8},{12,14},{14,12},{1,3},{3,1},... | collective-permute-start | bytes 49160 | tf_op jit(solution)/shard_map/ppermute | solution.py:278
  127.9 4.4 %collective-permute-start.34 = (bf16[128,128]{1,0:T(8,128)(2,1)S(1)}, bf16[128,128]{1,0:T(8,128)(2,1)S(1)}, u32[]{:S(2)}, u32[]{:S(2)}) collective-permute-start(bf16[128,128]{1,0:T(8,128)(2,1)S(1)} %pad_maximum_fusion.2), channel_id=1, source_target_pairs={{0,4},{2,6},{4,0},{6,2},{8,12},{10,14},{12,8},{14,10},{1,5},{3,7},... | collective-permute-start | bytes 98312 | tf_op jit(solution)/shard_map/ppermute | solution.py:281
  128.6 4.8 %collective-permute-start.33 = (bf16[128,128]{1,0:T(8,128)(2,1)S(1)}, bf16[128,128]{1,0:T(8,128)(2,1)S(1)}, u32[]{:S(2)}, u32[]{:S(2)}) collective-permute-start(bf16[128,128]{1,0:T(8,128)(2,1)S(1)} %pad_maximum_fusion.2), channel_id=1, source_target_pairs={{0,8},{2,10},{4,12},{6,14},{8,0},{10,2},{12,4},{14,6},{1,9},{3,11}... | collective-permute-start | bytes 98312 | tf_op jit(solution)/shard_map/ppermute | solution.py:281
  130.0 5.7 %collective-permute-start.32 = (bf16[128,128]{1,0:T(8,128)(2,1)S(1)}, bf16[128,128]{1,0:T(8,128)(2,1)S(1)}, u32[]{:S(2)}, u32[]{:S(2)}) collective-permute-start(bf16[128,128]{1,0:T(8,128)(2,1)S(1)} %pad_maximum_fusion.2), channel_id=1, source_target_pairs={{0,12},{2,14},{4,8},{6,10},{8,4},{10,6},{12,0},{14,2},{1,13},{3,15... | collective-permute-start | bytes 98312 | tf_op jit(solution)/shard_map/ppermute | solution.py:281
  135.8 1.4 %collective-permute-start.35 = (bf16[16,1,4096]{2,0,1:T(8,128)(2,1)S(1)}, bf16[16,1,4096]{2,0,1:T(8,128)(2,1)S(1)}, u32[]{:S(2)}, u32[]{:S(2)}) collective-permute-start(bf16[16,1,4096]{2,0,1:T(8,128)(2,1)S(1)} %reshape.94), channel_id=1, source_target_pairs={{0,1},{1,0},{2,3},{3,2},{4,5},{5,4},{6,7},{7,6},{8,9},{9,8},{10,11... | collective-permute-start | bytes 393224 | tf_op jit(solution)/shard_map/ppermute | solution.py:291

commit v6 on v5

--- a/solution.py
+++ b/solution.py
@@ -18,45 +18,48 @@
     return jnp.dot(a, b, preferred_element_type=F32)
 
 
-def add_pieces(tokens, theirs, groups, total, core=None):
+def add_pieces(tokens, theirs, halves, total, part, core=None):
     tok_rows = tokens.shape[0]
-    width = groups[0][1][0].shape[1]
-    depths = [[part.shape[0] for part in parts] for _, parts in groups]
-    span = sum(depths[0])
-    deep = span * len(groups)
-    flat = [part for _, parts in groups for part in parts]
+    span = sum(x.shape[0] for x in halves[0][1:])
+    width = halves[0][1].shape[1]
+    deep = span * len(halves)
+    flat = [x for half in halves for x in half[1:]]
     count = len(flat)
     last = core is not None
-    places = jnp.stack([start for start, _ in groups] + ([core * tok_rows, (1 - core) * tok_rows] if last else []))
+    places = jnp.stack([half[0] for half in halves] + [part] + ([core, 1 - core] if last else []))
 
     def kernel(places_ref, mine_ref, theirs_ref, *refs):
-        parts = refs[:count]
+        parts = list(refs[:count])
         total_ref, out_ref, mark_ref, columns, weights, sems = (
             refs[count:] if total is not None else (None,) + refs[count:]
         )
         copies = []
         for j, source in enumerate((mine_ref, theirs_ref)):
-            for g in range(len(groups)):
-                start = pl.multiple_of(places_ref[g], 128)
+            for h in range(len(halves)):
+                start = pl.multiple_of(places_ref[h], 128)
                 copy = pltpu.make_async_copy(
-                    source.at[:, pl.ds(start, span)], columns.at[j, :, pl.ds(g * span, span)], sems.at[j, g]
+                    source.at[:, pl.ds(start, span)], columns.at[j, :, pl.ds(h * span, span)], sems.at[j, h]
                 )
                 copy.start()
                 copies.append(copy)
-        at = 0
-        for part in parts:
-            weights[at : at + part.shape[0], :] = part[...]
-            at += part.shape[0]
+        for h, half in enumerate(halves):
+            at = h * span
+            shared = half[1].shape[0]
+            weights[at : at + shared, :] = parts.pop(0)[...]
+            if len(half) > 2:
+                rest = half[2].shape[0]
+                for turn in (places_ref[len(halves)], 1 - places_ref[len(halves)]):
+                    weights[pl.ds(pl.multiple_of(at + shared + turn * rest, rest), rest), :] = parts.pop(0)[...]
         mark_ref[...] = jnp.zeros_like(mark_ref)
         for j in range(2):
-            for g in range(len(groups)):
-                copies[j * len(groups) + g].wait()
+            for h in range(len(halves)):
+                copies[j * len(halves) + h].wait()
             rows = pl.ds(j * tok_rows, tok_rows)
             term = mm(columns[j], weights[...])
             if total is not None:
                 term = total_ref[rows, :] + term
             if last:
-                rows = pl.ds(pl.multiple_of(places_ref[len(groups) + j], tok_rows), tok_rows)
+                rows = pl.ds(pl.multiple_of(places_ref[len(halves) + 1 + j] * tok_rows, tok_rows), tok_rows)
             out_ref[rows, :] = term.astype(out_ref.dtype)
 
     in_vmem = pl.BlockSpec(memory_space=pltpu.VMEM)
@@ -73,7 +76,7 @@
         scratch_shapes=[
             pltpu.VMEM((2, tok_rows, deep), BF),
             pltpu.VMEM((deep, width), BF),
-            pltpu.SemaphoreType.DMA((2, len(groups))),
+            pltpu.SemaphoreType.DMA((2, len(halves))),
         ],
         input_output_aliases={} if total is None or last else {3 + count: 0},
         compiler_params=pltpu.CompilerParams(vmem_limit_bytes=48 * 2**20),
@@ -83,29 +86,27 @@
     )(places, tokens, theirs, *flat, *sums)
 
 
-def project(tokens, key_down, value_down, early):
+def project(tokens, key_down, value_down, prepare, inputs):
     chips = lax.axis_size("chip")
     chip = lax.axis_index("chip")
     core = lax.axis_index("core")
+    part = lax.axis_index("groups")
     first = core == 0
     shard = key_down.shape[0]
     rows = CORES * shard
     own = jnp.where(first, key_down, value_down)
     got = lax.ppermute(jnp.where(first, value_down, key_down), "core", SWAP)
-    if chips > 8:
+    if chips != 8 or lax.axis_size("groups") != 2:
         theirs = lax.ppermute(tokens, "core", SWAP)
         block = jnp.concatenate([jnp.where(first, own, got), jnp.where(first, got, own)], 0)
         full = lax.all_gather(block, "chip", axis=0, tiled=True)
         mine, other = mm(tokens, full).astype(BF), mm(theirs, full).astype(BF)
-        return jnp.concatenate([jnp.where(first, mine, other), jnp.where(first, other, mine)], 0), early
+        return jnp.concatenate([jnp.where(first, mine, other), jnp.where(first, other, mine)], 0), prepare(*inputs)
     cycle = list(range(0, chips, 2)) + list(range(chips - 1, 0, -2))
     last = chips - 1
     place = jnp.where(chip & 1 == 0, chip >> 1, last - (chip >> 1))
-    chains = 2
-    piece = shard // chains
     right = [(cycle[i], cycle[(i + 1) % chips]) for i in range(chips)]
-    left = [(b, a) for a, b in right]
-    ways = [right] * chains + [left] * chains
+    ways = (right, [(b, a) for a, b in right])
 
     def start_of(way, step):
         spot = place - step if way == 0 else place + step
@@ -113,28 +114,45 @@
         source = jnp.where(spot < chips // 2, 2 * spot, 2 * (last - spot) + 1)
         return source * rows + (core if way == 0 else 1 - core) * shard
 
-    held = [own[k * piece : (k + 1) * piece] for k in range(chains)]
+    rest = shard // 4
+    shared = shard - 2 * rest
+
+    def turns(half):
+        return jnp.where(part == 0, half[shared : shared + rest], half[shared + rest :])
+
+    both, single = [own[:shared]], [turns(own)]
     got, tokens_later = lax.optimization_barrier((got, tokens))
-    held += [got[k * piece : (k + 1) * piece] for k in range(chains)]
+    both.append(got[:shared])
+    single.append(turns(got))
     theirs = lax.ppermute(tokens_later, "core", SWAP)
-    todo = [(start_of(0, 0), [own]), (start_of(1, 0), [got])]
-    total = None
-    mark = None
+    todo = [(start_of(0, 0), own), (start_of(1, 0), got)]
+    calls = {3: 4, 5: 4, 7: 4}
+    total = mark = others = None
     for step in range(1, chips):
-        ready = todo
         if step == 2:
-            held[0], early = lax.optimization_barrier((held[0], early))
-        for k in range(2 * chains):
-            if mark is not None:
-                held[k], _ = lax.optimization_barrier((held[k], mark))
-            held[k] = lax.ppermute(held[k], "chip", ways[k])
-        arriving = [(start_of(w, step), held[w * chains : (w + 1) * chains]) for w in range(2)]
-        if step == 1:
-            todo = todo + arriving
-        else:
-            total, mark = add_pieces(tokens, theirs, ready, total)
-            todo = arriving
-    return add_pieces(tokens, theirs, todo, total, core)[0], early
+            both, single, inputs = lax.optimization_barrier((both, single, inputs))
+            early = prepare(*inputs)
+        if step == 4:
+            both[0], early = lax.optimization_barrier((both[0], early))
+        if mark is not None:
+            both = [lax.optimization_barrier((x, mark))[0] for x in both]
+            single = [lax.optimization_barrier((x, mark))[0] for x in single]
+            mark = None
+        passed = single
+        both = [lax.ppermute(x, "chip", way) for x, way in zip(both, ways)]
+        single = [lax.ppermute(x, "chip", way) for x, way in zip(single, ways)]
+        if step > 1:
+            crossed = lax.ppermute(jnp.concatenate(passed, 0), "groups", SWAP)
+            others = [crossed[:rest], crossed[rest:]]
+            todo += [(start_of(w, step - 1), before[w], passed[w], others[w]) for w in range(2)]
+        before = both
+        if step in calls:
+            ready, todo = todo[: calls[step]], todo[calls[step] :]
+            total, mark = add_pieces(tokens, theirs, ready, total, part)
+    others = [lax.ppermute(x, "chip", way) for x, way in zip(others, ways)]
+    total, _ = add_pieces(tokens, theirs, todo, total, part)
+    final = [(start_of(w, last), both[w], single[w], others[w]) for w in range(2)]
+    return add_pieces(tokens, theirs, final, total, part, core)[0], early
 
 
 def attend(have, got, core, key_up, value_up, query, bounds, chips):
@@ -237,36 +255,37 @@
     rows = pairs * heads * group
     share = rows // chips
 
-    query = lax.dynamic_index_in_dim(
-        queries.reshape(steps_count, req_count, CORES, heads * group * DH), core, 2, keepdims=False
-    ).reshape(steps_count, req_count, heads, group, DH)
-    key_up = lax.dynamic_slice_in_dim(key_up, core * heads * DH, heads * DH, 1)
-    value_up = lax.dynamic_slice_in_dim(value_up, core * heads * DH, heads * DH, 1)
-    flat_new = new_latent.reshape(pairs, 2 * lat_width)
-    new_keys = mm(flat_new[:, :lat_width], key_up).astype(BF).reshape(steps_count, req_count, heads, DH)
-    new_values = mm(flat_new[:, lat_width:], value_up).astype(BF).reshape(steps_count, req_count, heads, DH)
-    causal = (jnp.arange(steps_count)[:, None] >= jnp.arange(steps_count)[None, :])[:, None, None, None, :]
-    fresh = jnp.einsum("srgjd,urgd->srgju", query, new_keys, preferred_element_type=F32) * scale
-    fresh = jnp.where(causal, fresh, -1e30)
-    fresh_top = jnp.max(fresh, -1)
-    fresh_weights = jnp.where(causal, jnp.exp(fresh - fresh_top[..., None]), 0.0)
-    fresh_total = jnp.sum(fresh_weights, -1)
-    fresh_summed = jnp.einsum("srgju,urgd->srgjd", fresh_weights.astype(BF), new_values, preferred_element_type=F32)
-
-    def my_share(x):
-        return lax.dynamic_slice_in_dim(x, chip * share, share, 0)
-
-    fresh_summed = my_share(fresh_summed.reshape(rows, DH))
-    fresh_stats = [my_share(x.reshape(rows)).reshape(-1, group).T for x in (fresh_top, fresh_total)]
-    fresh_stats = jnp.pad(jnp.concatenate(fresh_stats, 1), ((0, 0), (0, DH - 2 * share // group)))
-
-    offsets = jnp.cumsum(prompt_lens) - prompt_lens
-    bounds = jnp.stack([offsets, offsets + prompt_lens]) - chip * CORES * tok_rows
-    bounds = jnp.broadcast_to(bounds[:, None, :, None], (2, steps_count, req_count, group)).reshape(2, -1)
-    by_head = query.transpose(2, 0, 1, 3, 4).reshape(heads, pairs * group, DH)
-
-    early = (by_head, bounds, key_up, value_up, fresh_stats, fresh_summed)
-    have, early = project(tokens, key_down, value_down, early)
+    def prepare(queries, new_latent, key_up, value_up):
+        query = lax.dynamic_index_in_dim(
+            queries.reshape(steps_count, req_count, CORES, heads * group * DH), core, 2, keepdims=False
+        ).reshape(steps_count, req_count, heads, group, DH)
+        key_up = lax.dynamic_slice_in_dim(key_up, core * heads * DH, heads * DH, 1)
+        value_up = lax.dynamic_slice_in_dim(value_up, core * heads * DH, heads * DH, 1)
+        flat_new = new_latent.reshape(pairs, 2 * lat_width)
+        new_keys = mm(flat_new[:, :lat_width], key_up).astype(BF).reshape(steps_count, req_count, heads, DH)
+        new_values = mm(flat_new[:, lat_width:], value_up).astype(BF).reshape(steps_count, req_count, heads, DH)
+        causal = (jnp.arange(steps_count)[:, None] >= jnp.arange(steps_count)[None, :])[:, None, None, None, :]
+        fresh = jnp.einsum("srgjd,urgd->srgju", query, new_keys, preferred_element_type=F32) * scale
+        fresh = jnp.where(causal, fresh, -1e30)
+        fresh_top = jnp.max(fresh, -1)
+        fresh_weights = jnp.where(causal, jnp.exp(fresh - fresh_top[..., None]), 0.0)
+        fresh_total = jnp.sum(fresh_weights, -1)
+        fresh_summed = jnp.einsum("srgju,urgd->srgjd", fresh_weights.astype(BF), new_values, preferred_element_type=F32)
+
+        def my_share(x):
+            return lax.dynamic_slice_in_dim(x, chip * share, share, 0)
+
+        fresh_summed = my_share(fresh_summed.reshape(rows, DH))
+        fresh_stats = [my_share(x.reshape(rows)).reshape(-1, group).T for x in (fresh_top, fresh_total)]
+        fresh_stats = jnp.pad(jnp.concatenate(fresh_stats, 1), ((0, 0), (0, DH - 2 * share // group)))
+
+        offsets = jnp.cumsum(prompt_lens) - prompt_lens
+        bounds = jnp.stack([offsets, offsets + prompt_lens]) - chip * CORES * tok_rows
+        bounds = jnp.broadcast_to(bounds[:, None, :, None], (2, steps_count, req_count, group)).reshape(2, -1)
+        by_head = query.transpose(2, 0, 1, 3, 4).reshape(heads, pairs * group, DH)
+        return by_head, bounds, key_up, value_up, fresh_stats, fresh_summed
+
+    have, early = project(tokens, key_down, value_down, prepare, (queries, new_latent, key_up, value_up))
     by_head, bounds, key_up, value_up, fresh_stats, fresh_summed = early
     got = lax.ppermute(have, "core", SWAP)
     sending = attend(have, got, core, key_up, value_up, by_head, bounds, chips)

time: 139 us -> 140 us (level)
  waiting for transfers between devices: 41.3 us -> 32.4 us
  starting transfers between devices: 34.9 us -> 41.9 us
  Pallas kernels: 32.6 us -> 26.2 us
  local copies, waits for them, and re-layouts: 8.91 us -> 14.6 us
  other arithmetic: 3.71 us -> 6.41 us
    ppermute x28 -> x36, waiting for transfers between devices: 29.1 us -> 21.4 us  [the longest x14 13.1 us: project(): both = [lax.ppermute(x, 'chip', way) for x, way in zip(both, ways)]]
    ppermute x28 -> x36, starting transfers between devices: 28.7 us -> 35.7 us  [the longest x14 15.4 us: project(): single = [lax.ppermute(x, 'chip', way) for x, way in zip(single, ways)]]
    pallas_call x7 -> x5, Pallas kernels: 27.9 us -> 21.5 us  [add_pieces(): pl.pallas_call(kernel, out_shape=(jax.ShapeDtypeStruct((2 * tok_rows, wid...]
    reshape x12, local copies, waits for them, and re-layouts: 1.08 us -> 4.1 us  [the longest x1 1.37 us: prepare(): flat_new = new_latent.reshape(pairs, 2 * lat_width)]
    concatenate x1 -> x7, other arithmetic: 0.67 us -> 3.08 us  [the longest x6 2.43 us: project(): crossed = lax.ppermute(jnp.concatenate(passed, 0), 'groups', SWAP)]
    slice x2 -> x8, local copies, waits for them, and re-layouts: 0.07 us -> 2.08 us  [the longest x6 2.04 us: project(): others = [crossed[:rest], crossed[rest:]]]
    unnamed x18 -> x24, local copies, waits for them, and re-layouts: 3.55 us -> 2.83 us
  transfers between devices with their start and end apart: 36 -> 44, of which waited for: 25 -> 16; matrix products, arithmetic and copies ran while one was open for 5% -> 12% of each run, Pallas kernels for 17% -> 13%
where the time goes in v6:
time: 140 us; the launch traced here: 139 us
  starting transfers between devices  41.9 us (30%)
  waiting for transfers between devices  32.4 us (23%)
  Pallas kernels  26.2 us (19%)
  blocking collectives  14.9 us (11%)
  local copies, waits for them, and re-layouts  14.6 us (10%)
  other arithmetic  6.41 us (5%)
  matrix products  2.07 us (1%)
    pallas_call x5, Pallas kernels, add_pieces(): pl.pallas_call(kernel, out_shape=(jax.ShapeDtypeStruct((2 * tok_rows, wid...  21.5 us
    ppermute x14, starting transfers between devices, project(): single = [lax.ppermute(x, 'chip', way) for x, way in zip(single, ways)]  15.4 us
    all_to_all x1, blocking collectives, on_device(): lax.all_to_all(sending, 'chip', split_axis=0, concat_axis=0, tiled=True)  14.9 us
    ppermute x14, starting transfers between devices, project(): both = [lax.ppermute(x, 'chip', way) for x, way in zip(both, ways)]  13.5 us
    ppermute x14, waiting for transfers between devices, project(): both = [lax.ppermute(x, 'chip', way) for x, way in zip(both, ways)]  13.1 us
    ppermute x14, waiting for transfers between devices, project(): single = [lax.ppermute(x, 'chip', way) for x, way in zip(single, ways)]  6.74 us
    ppermute x6, starting transfers between devices, project(): crossed = lax.ppermute(jnp.concatenate(passed, 0), 'groups', SWAP)  4.72 us
    ppermute x3, starting transfers between devices, on_device(): lax.ppermute(couple, 'chip', [(c, c ^ 2 * d) for c in range(chips)])  4.45 us
  transfers between devices with their start and end apart: 44, of which 16 were waited for; matrix products, arithmetic and copies ran while one was open for 12% of the time, Pallas kernels for 13%

profile of v6, /device:TPU:0, one launch (start us, length us, event | category | flops | bytes accessed | tf_op | source)
XLA Modules:
  0.0 139.2 jit_solution(25678725178257259)
XLA Ops:
  0.0 1.4 broadcast_select_fusion
  1.9 1.5 %collective-permute-done.refs_1_ = bf16[512,512]{1,0:T(8,128)(2,1)S(1)} collective-permute-done((bf16[512,512]{1,0:T(8,128)(2,1)S(1)}, bf16[512,512]{1,0:T(8,128)(2,1)S(1)}, u32[]{:S(2)}, u32[]{:S(2)}) %collective-permute-start) | collective-permute-done | bytes 524320 | tf_op jit(solution)/shard_map/ppermute | solution.py:98
  3.8 2.8 %collective-permute-start.4 = (bf16[128,512]{1,0:T(8,128)(2,1)S(1)}, bf16[128,512]{1,0:T(8,128)(2,1)S(1)}, u32[]{:S(2)}, u32[]{:S(2)}) collective-permute-start(bf16[128,512]{1,0:T(8,128)(2,1)S(1)} %slice_select_fusion), channel_id=1, source_target_pairs={{0,4},{4,8},{8,12},{12,14},{14,10},{10,6},{6,2},{2,0},{1,5},{5,9},... | collective-permute-start | bytes 393224 | tf_op jit(solution)/shard_map/ppermute | solution.py:143
  6.6 1.6 %collective-permute-start.2 = (bf16[256,512]{1,0:T(8,128)(2,1)S(1)}, bf16[256,512]{1,0:T(8,128)(2,1)S(1)}, u32[]{:S(2)}, u32[]{:S(2)}) collective-permute-start(bf16[256,512]{1,0:T(8,128)(2,1)S(1)} %slice.80), channel_id=1, source_target_pairs={{0,4},{4,8},{8,12},{12,14},{14,10},{10,6},{6,2},{2,0},{1,5},{5,9},... | collective-permute-start | bytes 786440 | tf_op jit(solution)/shard_map/ppermute | solution.py:142
  9.7 0.7 broadcast_in_dim.30
  10.4 0.8 reshape.85.bounds_ref
  11.5 4.7 %collective-permute-done.2.refs_2_ = bf16[256,512]{1,0:T(8,128)(2,1)S(1)} collective-permute-done((bf16[256,512]{1,0:T(8,128)(2,1)S(1)}, bf16[256,512]{1,0:T(8,128)(2,1)S(1)}, u32[]{:S(2)}, u32[]{:S(2)}) %collective-permute-start.2) | collective-permute-done | bytes 262176 | tf_op jit(solution)/shard_map/ppermute | solution.py:142
  16.2 3.1 %collective-permute-done.5.refs_6_ = bf16[128,512]{1,0:T(8,128)(2,1)S(1)} collective-permute-done((bf16[128,512]{1,0:T(8,128)(2,1)}, bf16[128,512]{1,0:T(8,128)(2,1)S(1)}, u32[]{:S(2)}, u32[]{:S(2)}) %collective-permute-start.5) | collective-permute-done | bytes 131104 | tf_op jit(solution)/shard_map/ppermute | solution.py:143
  19.8 1.6 %collective-permute-start.11 = (bf16[128,512]{1,0:T(8,128)(2,1)S(1)}, bf16[128,512]{1,0:T(8,128)(2,1)}, u32[]{:S(2)}, u32[]{:S(2)}) collective-permute-start(bf16[128,512]{1,0:T(8,128)(2,1)S(1)} %collective-permute-done.4.refs_3_), channel_id=1, source_target_pairs={{0,4},{4,8},{8,12},{12,14},{14,10},{10,6},{6,2},{2,0},{1,5},{5,9},... | collective-permute-start | bytes 393224 | tf_op jit(solution)/shard_map/ppermute | solution.py:143
  21.4 0.7 pad_maximum_fusion
  22.1 1.5 %collective-permute-start.8 = (bf16[256,512]{1,0:T(8,128)(2,1)}, bf16[256,512]{1,0:T(8,128)(2,1)}, u32[]{:S(2)}, u32[]{:S(2)}) collective-permute-start(bf16[256,512]{1,0:T(8,128)(2,1)} %pad_maximum_fusion), channel_id=1, source_target_pairs={{0,16},{16,0},{1,17},{17,1},{2,18},{18,2},{3,19},{19,3},{4,20},{20... | collective-permute-start | bytes 786440 | tf_op jit(solution)/shard_map/ppermute | solution.py:145
  23.6 1.4 reshape.86
  25.0 1.1 constant_dynamic-slice_fusion.1
  26.3 0.8 copy-done
  27.1 1.2 reshape.81
  28.3 0.8 dynamic-slice_reduce_fusion
  29.3 0.9 convolution_convert_fusion
  30.2 0.7 fusion.21
  31.8 1.6 %collective-permute-start.6 = (bf16[256,512]{1,0:T(8,128)(2,1)S(1)}, bf16[256,512]{1,0:T(8,128)(2,1)S(1)}, u32[]{:S(2)}, u32[]{:S(2)}) collective-permute-start(bf16[256,512]{1,0:T(8,128)(2,1)S(1)} %collective-permute-done.2.refs_2_), channel_id=1, source_target_pairs={{0,4},{4,8},{8,12},{12,14},{14,10},{10,6},{6,2},{2,0},{1,5},{5,9},... | collective-permute-start | bytes 786440 | tf_op jit(solution)/shard_map/ppermute | solution.py:142
  34.4 0.7 copy.40
  36.1 0.9 pad_maximum_fusion.1
  38.1 1.0 fusion.20
  39.1 1.6 %collective-permute-start.15 = (bf16[128,512]{1,0:T(8,128)(2,1)}, bf16[128,512]{1,0:T(8,128)(2,1)S(1)}, u32[]{:S(2)}, u32[]{:S(2)}) collective-permute-start(bf16[128,512]{1,0:T(8,128)(2,1)} %collective-permute-done.11.refs_1_), channel_id=1, source_target_pairs={{0,4},{4,8},{8,12},{12,14},{14,10},{10,6},{6,2},{2,0},{1,5},{5,9},... | collective-permute-start | bytes 393224 | tf_op jit(solution)/shard_map/ppermute | solution.py:143
  40.7 2.8 %collective-permute-done.14.refs_3_ = bf16[256,512]{1,0:T(8,128)(2,1)S(1)} collective-permute-done((bf16[256,512]{1,0:T(8,128)(2,1)S(1)}, bf16[256,512]{1,0:T(8,128)(2,1)S(1)}, u32[]{:S(2)}, u32[]{:S(2)}) %collective-permute-start.14) | collective-permute-done | bytes 262176 | tf_op jit(solution)/shard_map/ppermute | solution.py:142
  43.6 2.3 %collective-permute-start.7 = (bf16[256,512]{1,0:T(8,128)(2,1)S(1)}, bf16[256,512]{1,0:T(8,128)(2,1)}, u32[]{:S(2)}, u32[]{:S(2)}) collective-permute-start(bf16[256,512]{1,0:T(8,128)(2,1)S(1)} %collective-permute-done.6.refs_0_), channel_id=1, source_target_pairs={{0,4},{4,8},{8,12},{12,14},{14,10},{10,6},{6,2},{2,0},{1,5},{5,9},... | collective-permute-start | bytes 786440 | tf_op jit(solution)/shard_map/ppermute | solution.py:142
  45.9 1.0 copy-done.3
  46.9 0.9 copy-done.7
  47.9 4.7 %shard_map.82 = (f32[1024,512]{1,0:T(8,128)S(1)}, f32[8,128]{1,0:T(8,128)}) custom-call(s32[5]{0:T(128)S(1)} %stack.95.places_ref, bf16[512,8192]{1,0:T(8,128)(2,1)} %mine_ref.9, bf16[512,8192]{1,0:T(8,128)(2,1)} %collective-permute-done.1.theirs_ref, bf16[512,512]{1,0:T(8,128)(2,1)S(1)} %get-tuple-element.69.refs_0_, bf16[512,512]{1,0:T(8,128)(2,1)S(1)} %copy-done.3, ...), custom_call_target="tpu_custom_call" | custom-call | flops 2147483648 | bytes 4194304 | tf_op jit(solution)/shard_map/pallas_call | solution.py:68
  52.8 2.0 %collective-permute-start.21 = (bf16[128,512]{1,0:T(8,128)(2,1)S(1)}, bf16[128,512]{1,0:T(8,128)(2,1)S(1)}, u32[]{:S(2)}, u32[]{:S(2)}) collective-permute-start(bf16[128,512]{1,0:T(8,128)(2,1)S(1)} %collective-permute-done.15.refs_7_), channel_id=1, source_target_pairs={{0,4},{4,8},{8,12},{12,14},{14,10},{10,6},{6,2},{2,0},{1,5},{5,9},... | collective-permute-start | bytes 393224 | tf_op jit(solution)/shard_map/ppermute | solution.py:143
  55.5 1.7 %collective-permute-start.9 = (bf16[256,512]{1,0:T(8,128)(2,1)}, bf16[256,512]{1,0:T(8,128)(2,1)}, u32[]{:S(2)}, u32[]{:S(2)}) collective-permute-start(bf16[256,512]{1,0:T(8,128)(2,1)} %collective-permute-done.7.refs_6_), channel_id=1, source_target_pairs={{0,4},{4,8},{8,12},{12,14},{14,10},{10,6},{6,2},{2,0},{1,5},{5,9},... | collective-permute-start | bytes 786440 | tf_op jit(solution)/shard_map/ppermute | solution.py:142
  57.1 1.9 %collective-permute-done.25.refs_4_ = bf16[128,512]{1,0:T(8,128)(2,1)S(1)} collective-permute-done((bf16[128,512]{1,0:T(8,128)(2,1)S(1)}, bf16[128,512]{1,0:T(8,128)(2,1)S(1)}, u32[]{:S(2)}, u32[]{:S(2)}) %collective-permute-start.25) | collective-permute-done | bytes 131104 | tf_op jit(solution)/shard_map/ppermute | solution.py:143
  59.1 0.7 pad_maximum_fusion.4
  60.1 1.6 %collective-permute-done.17 = bf16[256,512]{1,0:T(8,128)(2,1)S(1)} collective-permute-done((bf16[256,512]{1,0:T(8,128)(2,1)S(1)}, bf16[256,512]{1,0:T(8,128)(2,1)S(1)}, u32[]{:S(2)}, u32[]{:S(2)}) %collective-permute-start.17) | collective-permute-done | bytes 262176 | tf_op jit(solution)/shard_map/ppermute | solution.py:145
  61.7 1.5 %collective-permute-start.22 = (bf16[128,512]{1,0:T(8,128)(2,1)S(1)}, bf16[128,512]{1,0:T(8,128)(2,1)S(1)}, u32[]{:S(2)}, u32[]{:S(2)}) collective-permute-start(bf16[128,512]{1,0:T(8,128)(2,1)S(1)} %collective-permute-done.21.refs_1_), channel_id=1, source_target_pairs={{0,4},{4,8},{8,12},{12,14},{14,10},{10,6},{6,2},{2,0},{1,5},{5,9},... | collective-permute-start | bytes 393224 | tf_op jit(solution)/shard_map/ppermute | solution.py:143
  63.2 5.2 %shard_map.83 = (f32[1024,512]{1,0:T(8,128)S(1)}, f32[8,128]{1,0:T(8,128)}) custom-call(s32[5]{0:T(128)S(1)} %stack.100.places_ref, bf16[512,8192]{1,0:T(8,128)(2,1)} %mine_ref.9, bf16[512,8192]{1,0:T(8,128)(2,1)} %collective-permute-done.1.theirs_ref, bf16[256,512]{1,0:T(8,128)(2,1)S(1)} %collective-permute-done.6.refs_0_, ...), custom_call_target="tpu_custom_call", output_to_operand_aliasing={{0}: (15, {})} | custom-call | flops 2147483648 | bytes 4194304 | tf_op jit(solution)/shard_map/pallas_call | solution.py:68
  69.0 1.5 %collective-permute-start.23 = (bf16[128,512]{1,0:T(8,128)(2,1)S(1)}, bf16[128,512]{1,0:T(8,128)(2,1)S(1)}, u32[]{:S(2)}, u32[]{:S(2)}) collective-permute-start(bf16[128,512]{1,0:T(8,128)(2,1)S(1)} %collective-permute-done.22.refs_7_), channel_id=1, source_target_pairs={{0,4},{4,8},{8,12},{12,14},{14,10},{10,6},{6,2},{2,0},{1,5},{5,9},... | collective-permute-start | bytes 393224 | tf_op jit(solution)/shard_map/ppermute | solution.py:143
  70.9 0.7 collective-permute-start.37
  71.9 1.6 %collective-permute-done.27.refs_4_ = bf16[128,512]{1,0:T(8,128)(2,1)S(1)} collective-permute-done((bf16[128,512]{1,0:T(8,128)(2,1)S(1)}, bf16[128,512]{1,0:T(8,128)(2,1)S(1)}, u32[]{:S(2)}, u32[]{:S(2)}) %collective-permute-start.27) | collective-permute-done | bytes 131104 | tf_op jit(solution)/shard_map/ppermute | solution.py:143
  74.2 1.7 %collective-permute-start.28 = (bf16[256,512]{1,0:T(8,128)(2,1)S(1)}, bf16[256,512]{1,0:T(8,128)(2,1)S(1)}, u32[]{:S(2)}, u32[]{:S(2)}) collective-permute-start(bf16[256,512]{1,0:T(8,128)(2,1)S(1)} %pad_maximum_fusion.3), channel_id=1, source_target_pairs={{0,16},{16,0},{1,17},{17,1},{2,18},{18,2},{3,19},{19,3},{4,20},{20... | collective-permute-start | bytes 786440 | tf_op jit(solution)/shard_map/ppermute | solution.py:145
  75.9 0.9 collective-permute-start.34
  76.8 1.0 fusion.16
  77.8 3.2 %collective-permute-done.31.refs_9_ = bf16[256,512]{1,0:T(8,128)(2,1)S(1)} collective-permute-done((bf16[256,512]{1,0:T(8,128)(2,1)}, bf16[256,512]{1,0:T(8,128)(2,1)S(1)}, u32[]{:S(2)}, u32[]{:S(2)}) %collective-permute-start.31) | collective-permute-done | bytes 262176 | tf_op jit(solution)/shard_map/ppermute | solution.py:142
  81.0 1.5 %collective-permute-start.24 = (bf16[128,512]{1,0:T(8,128)(2,1)S(1)}, bf16[128,512]{1,0:T(8,128)(2,1)S(1)}, u32[]{:S(2)}, u32[]{:S(2)}) collective-permute-start(bf16[128,512]{1,0:T(8,128)(2,1)S(1)} %collective-permute-done.23.refs_1_), channel_id=1, source_target_pairs={{0,4},{4,8},{8,12},{12,14},{14,10},{10,6},{6,2},{2,0},{1,5},{5,9},... | collective-permute-start | bytes 393224 | tf_op jit(solution)/shard_map/ppermute | solution.py:143
  83.1 1.5 %collective-permute-start.19 = (bf16[256,512]{1,0:T(8,128)(2,1)S(1)}, bf16[256,512]{1,0:T(8,128)(2,1)S(1)}, u32[]{:S(2)}, u32[]{:S(2)}) collective-permute-start(bf16[256,512]{1,0:T(8,128)(2,1)S(1)} %collective-permute-done.10.refs_6_), channel_id=1, source_target_pairs={{0,4},{4,8},{8,12},{12,14},{14,10},{10,6},{6,2},{2,0},{1,5},{5,9},... | collective-permute-start | bytes 786440 | tf_op jit(solution)/shard_map/ppermute | solution.py:142
  84.7 1.0 collective-permute-start.29
  85.7 1.0 collective-permute-start.35
  86.8 2.2 %collective-permute-done.32.refs_3_ = bf16[256,512]{1,0:T(8,128)(2,1)S(1)} collective-permute-done((bf16[256,512]{1,0:T(8,128)(2,1)S(1)}, bf16[256,512]{1,0:T(8,128)(2,1)S(1)}, u32[]{:S(2)}, u32[]{:S(2)}) %collective-permute-start.32) | collective-permute-done | bytes 262176 | tf_op jit(solution)/shard_map/ppermute | solution.py:142
  89.5 1.5 %collective-permute-start.20 = (bf16[256,512]{1,0:T(8,128)(2,1)S(1)}, bf16[256,512]{1,0:T(8,128)(2,1)S(1)}, u32[]{:S(2)}, u32[]{:S(2)}) collective-permute-start(bf16[256,512]{1,0:T(8,128)(2,1)S(1)} %collective-permute-done.19.refs_0_), channel_id=1, source_target_pairs={{0,4},{4,8},{8,12},{12,14},{14,10},{10,6},{6,2},{2,0},{1,5},{5,9},... | collective-permute-start | bytes 786440 | tf_op jit(solution)/shard_map/ppermute | solution.py:142
  91.0 5.2 %shard_map.84 = (f32[1024,512]{1,0:T(8,128)S(1)}, f32[8,128]{1,0:T(8,128)}) custom-call(s32[5]{0:T(128)S(1)} %stack.108.places_ref, bf16[512,8192]{1,0:T(8,128)(2,1)} %mine_ref.9, bf16[512,8192]{1,0:T(8,128)(2,1)} %collective-permute-done.1.theirs_ref, bf16[256,512]{1,0:T(8,128)(2,1)} %collective-permute-done.9.refs_0_, ...), custom_call_target="tpu_custom_call", output_to_operand_aliasing={{0}: (15, {})} | custom-call | flops 2147483648 | bytes 4194304 | tf_op jit(solution)/shard_map/pallas_call | solution.py:68
  96.2 3.2 %shard_map.85 = (f32[1024,512]{1,0:T(8,128)S(1)}, f32[8,128]{1,0:T(8,128)}) custom-call(s32[3]{0:T(128)S(1)} %pad_add_fusion.places_ref, bf16[512,8192]{1,0:T(8,128)(2,1)} %mine_ref.9, bf16[512,8192]{1,0:T(8,128)(2,1)} %collective-permute-done.1.theirs_ref, bf16[256,512]{1,0:T(8,128)(2,1)S(1)} %collective-permute-done.19.refs_0_, ...), custom_call_target="tpu_custom_call", output_to_operand_aliasing={{0}: (9, {})} | custom-call | flops 1073741824 | bytes 2097152 | tf_op jit(solution)/shard_map/pallas_call | solution.py:68
  99.5 3.2 %shard_map.86 = (bf16[1024,512]{1,0:T(8,128)(2,1)S(1)}, f32[8,128]{1,0:T(8,128)}) custom-call(s32[5]{0:T(128)S(1)} %stack.87.places_ref, bf16[512,8192]{1,0:T(8,128)(2,1)} %mine_ref.9, bf16[512,8192]{1,0:T(8,128)(2,1)} %collective-permute-done.1.theirs_ref, bf16[256,512]{1,0:T(8,128)(2,1)S(1)} %collective-permute-done.20.refs_0_, ...), custom_call_target="tpu_custom_call" | custom-call | flops 1073741824 | bytes 2097152 | tf_op jit(solution)/shard_map/pallas_call | solution.py:68
  102.8 2.6 %collective-permute-done.38.got_ref = bf16[1024,512]{1,0:T(8,128)(2,1)S(1)} collective-permute-done((bf16[1024,512]{1,0:T(8,128)(2,1)S(1)}, bf16[1024,512]{1,0:T(8,128)(2,1)S(1)}, u32[]{:S(2)}, u32[]{:S(2)}) %collective-permute-start.38) | collective-permute-done | bytes 1048608 | tf_op jit(solution)/shard_map/ppermute | solution.py:290
  105.5 2.7 %shard_map.87 = f32[8,9,8,128]{3,2,1,0:T(8,128)S(1)} custom-call(s32[1]{0:T(128)} %bitcast.core_ref, bf16[1024,512]{1,0:T(8,128)(2,1)S(1)} %get-tuple-element.62.have_ref, bf16[1024,512]{1,0:T(8,128)(2,1)S(1)} %collective-permute-done.38.got_ref, bf16[512,512]{1,0:T(8,128)(2,1)S(1)} %copy-done.1, bf16[512,512]{1,0:T(8,128)(2,1)S(1)} %get-tuple-element.64.value_up_ref, ...), custom_call_target="tpu_custom_call" | custom-call | flops 1342177280 | bytes 2097152 | tf_op jit(solution)/shard_map/pallas_call | solution.py:200
  108.2 14.9 %all_to_all.5.arrived_ref = f32[8,9,8,128]{3,2,1,0:T(8,128)} all-to-all(f32[8,9,8,128]{3,2,1,0:T(8,128)S(1)} %shard_map.87), channel_id=1, replica_groups=mesh['groups'=2,'chip'=8,'core'=2] {'chip'}, dimensions={0} | all-to-all | bytes 589824 | tf_op jit(solution)/shard_map/all_to_all | solution.py:293
  123.1 1.9 %shard_map.88 = bf16[64,128]{1,0:T(8,128)(2,1)} custom-call(f32[8,9,8,128]{3,2,1,0:T(8,128)} %all_to_all.5.arrived_ref, f32[8,128]{1,0:T(8,128)} %select_maximum_fusion.stats_ref, f32[64,128]{1,0:T(8,128)} %constant_dynamic-slice_fusion.summed_ref), custom_call_target="tpu_custom_call" | custom-call | flops 131072 | bytes 294912 | tf_op jit(solution)/shard_map/pallas_call | solution.py:232
  125.0 0.7 collective-permute-start.39
  125.7 3.3 %collective-permute-done.39 = bf16[64,128]{1,0:T(8,128)(2,1)S(1)} collective-permute-done((bf16[64,128]{1,0:T(8,128)(2,1)}, bf16[64,128]{1,0:T(8,128)(2,1)S(1)}, u32[]{:S(2)}, u32[]{:S(2)}) %collective-permute-start.39) | collective-permute-done | bytes 16416 | tf_op jit(solution)/shard_map/ppermute | solution.py:297
  129.0 0.7 broadcast_select_fusion.13
  129.7 1.5 %collective-permute-start.40 = (bf16[128,128]{1,0:T(8,128)(2,1)S(1)}, bf16[128,128]{1,0:T(8,128)(2,1)S(1)}, u32[]{:S(2)}, u32[]{:S(2)}) collective-permute-start(bf16[128,128]{1,0:T(8,128)(2,1)S(1)} %pad_maximum_fusion.8), channel_id=1, source_target_pairs={{0,12},{2,14},{4,8},{6,10},{8,4},{10,6},{12,0},{14,2},{1,13},{3,15... | collective-permute-start | bytes 98312 | tf_op jit(solution)/shard_map/ppermute | solution.py:300
  131.9 2.3 %collective-permute-start.42 = (bf16[128,128]{1,0:T(8,128)(2,1)S(1)}, bf16[128,128]{1,0:T(8,128)(2,1)S(1)}, u32[]{:S(2)}, u32[]{:S(2)}) collective-permute-start(bf16[128,128]{1,0:T(8,128)(2,1)S(1)} %pad_maximum_fusion.8), channel_id=1, source_target_pairs={{0,4},{2,6},{4,0},{6,2},{8,12},{10,14},{12,8},{14,10},{1,5},{3,7},... | collective-permute-start | bytes 98312 | tf_op jit(solution)/shard_map/ppermute | solution.py:300
  134.2 1.3 collective-permute-done.40
  135.5 0.8 collective-permute-done.41
  136.6 1.3 collective-permute-done.43
  138.3 0.9 reshape.95
  (119 shorter events, 12.7 us)
Async XLA Ops:
  0.0 8.2 %copy-start.11 = (s32[4]{0:T(128)S(1)}, s32[4]{0:T(128)}, u32[]{:S(2)}) copy-start(s32[4]{0:T(128)} %param.13) | copy-start | bytes 52
  0.0 25.0 %copy-start.9 = (bf16[512,1024]{1,0:T(8,128)(2,1)S(1)}, bf16[512,1024]{1,0:T(8,128)(2,1)}, u32[]{:S(2)}) copy-start(bf16[512,1024]{1,0:T(8,128)(2,1)} %param.12) | copy-start | bytes 3145732
  1.4 2.1 %collective-permute-start = (bf16[512,512]{1,0:T(8,128)(2,1)S(1)}, bf16[512,512]{1,0:T(8,128)(2,1)S(1)}, u32[]{:S(2)}, u32[]{:S(2)}) collective-permute-start(bf16[512,512]{1,0:T(8,128)(2,1)S(1)} %get-tuple-element.70), channel_id=1, source_target_pairs={{0,1},{1,0},{2,3},{3,2},{4,5},{5,4},{6,7},{7,6},{8,9},{9,8},{10,11... | collective-permute-start | bytes 1572872 | tf_op jit(solution)/shard_map/ppermute | solution.py:98
  3.4 22.7 %copy-start.2 = (bf16[512,512]{1,0:T(8,128)(2,1)}, bf16[512,512]{1,0:T(8,128)(2,1)S(1)}, u32[]{:S(2)}) copy-start(bf16[512,512]{1,0:T(8,128)(2,1)S(1)} %collective-permute-done.refs_1_) | copy-start | bytes 1572868
  3.4 42.5 %collective-permute-start.1 = (bf16[512,8192]{1,0:T(8,128)(2,1)}, bf16[512,8192]{1,0:T(8,128)(2,1)}, u32[]{:S(2)}, u32[]{:S(2)}) collective-permute-start(bf16[512,8192]{1,0:T(8,128)(2,1)} %mine_ref.9), channel_id=1, source_target_pairs={{0,1},{1,0},{2,3},{3,2},{4,5},{5,4},{6,7},{7,6},{8,9},{9,8},{10,11... | collective-permute-start | bytes 25165832 | tf_op jit(solution)/shard_map/ppermute | solution.py:127
  3.8 7.7 %collective-permute-start.4 = (bf16[128,512]{1,0:T(8,128)(2,1)S(1)}, bf16[128,512]{1,0:T(8,128)(2,1)S(1)}, u32[]{:S(2)}, u32[]{:S(2)}) collective-permute-start(bf16[128,512]{1,0:T(8,128)(2,1)S(1)} %slice_select_fusion), channel_id=1, source_target_pairs={{0,4},{4,8},{8,12},{12,14},{14,10},{10,6},{6,2},{2,0},{1,5},{5,9},... | collective-permute-start | bytes 393224 | tf_op jit(solution)/shard_map/ppermute | solution.py:143
  6.6 9.6 %collective-permute-start.2 = (bf16[256,512]{1,0:T(8,128)(2,1)S(1)}, bf16[256,512]{1,0:T(8,128)(2,1)S(1)}, u32[]{:S(2)}, u32[]{:S(2)}) collective-permute-start(bf16[256,512]{1,0:T(8,128)(2,1)S(1)} %slice.80), channel_id=1, source_target_pairs={{0,4},{4,8},{8,12},{12,14},{14,10},{10,6},{6,2},{2,0},{1,5},{5,9},... | collective-permute-start | bytes 786440 | tf_op jit(solution)/shard_map/ppermute | solution.py:142
  8.5 10.9 %collective-permute-start.3 = (bf16[256,512]{1,0:T(8,128)(2,1)S(1)}, bf16[256,512]{1,0:T(8,128)(2,1)S(1)}, u32[]{:S(2)}, u32[]{:S(2)}) collective-permute-start(bf16[256,512]{1,0:T(8,128)(2,1)S(1)} %slice.61), channel_id=1, source_target_pairs={{4,0},{8,4},{12,8},{14,12},{10,14},{6,10},{2,6},{0,2},{5,1},{9,5},... | collective-permute-start | bytes 786440 | tf_op jit(solution)/shard_map/ppermute | solution.py:142
  9.6 9.7 %collective-permute-start.5 = (bf16[128,512]{1,0:T(8,128)(2,1)}, bf16[128,512]{1,0:T(8,128)(2,1)S(1)}, u32[]{:S(2)}, u32[]{:S(2)}) collective-permute-start(bf16[128,512]{1,0:T(8,128)(2,1)} %slice_select_fusion.1), channel_id=1, source_target_pairs={{4,0},{8,4},{12,8},{14,12},{10,14},{6,10},{2,6},{0,2},{5,1},{9,5},... | collective-permute-start | bytes 393224 | tf_op jit(solution)/shard_map/ppermute | solution.py:143
  16.2 15.7 %copy-start.4 = (bf16[256,512]{1,0:T(8,128)(2,1)}, bf16[256,512]{1,0:T(8,128)(2,1)S(1)}, u32[]{:S(2)}) copy-start(bf16[256,512]{1,0:T(8,128)(2,1)S(1)} %collective-permute-done.2.refs_2_) | copy-start | bytes 786436
  19.3 16.3 %copy-start.6 = (bf16[256,512]{1,0:T(8,128)(2,1)}, bf16[256,512]{1,0:T(8,128)(2,1)S(1)}, u32[]{:S(2)}) copy-start(bf16[256,512]{1,0:T(8,128)(2,1)S(1)} %collective-permute-done.3.refs_5_) | copy-start | bytes 786436
  19.3 16.3 %collective-permute-start.12 = (bf16[128,512]{1,0:T(8,128)(2,1)S(1)}, bf16[128,512]{1,0:T(8,128)(2,1)S(1)}, u32[]{:S(2)}, u32[]{:S(2)}) collective-permute-start(bf16[128,512]{1,0:T(8,128)(2,1)S(1)} %collective-permute-done.5.refs_6_), channel_id=1, source_target_pairs={{4,0},{8,4},{12,8},{14,12},{10,14},{6,10},{2,6},{0,2},{5,1},{9,5},... | collective-permute-start | bytes 393224 | tf_op jit(solution)/shard_map/ppermute | solution.py:143
  19.8 16.3 %collective-permute-start.11 = (bf16[128,512]{1,0:T(8,128)(2,1)S(1)}, bf16[128,512]{1,0:T(8,128)(2,1)}, u32[]{:S(2)}, u32[]{:S(2)}) collective-permute-start(bf16[128,512]{1,0:T(8,128)(2,1)S(1)} %collective-permute-done.4.refs_3_), channel_id=1, source_target_pairs={{0,4},{4,8},{8,12},{12,14},{14,10},{10,6},{6,2},{2,0},{1,5},{5,9},... | collective-permute-start | bytes 393224 | tf_op jit(solution)/shard_map/ppermute | solution.py:143
  22.1 15.6 %collective-permute-start.8 = (bf16[256,512]{1,0:T(8,128)(2,1)}, bf16[256,512]{1,0:T(8,128)(2,1)}, u32[]{:S(2)}, u32[]{:S(2)}) collective-permute-start(bf16[256,512]{1,0:T(8,128)(2,1)} %pad_maximum_fusion), channel_id=1, source_target_pairs={{0,16},{16,0},{1,17},{17,1},{2,18},{18,2},{3,19},{19,3},{4,20},{20... | collective-permute-start | bytes 786440 | tf_op jit(solution)/shard_map/ppermute | solution.py:145
  25.0 1.2 copy-start.10
  26.3 0.8 copy-start
  31.8 7.3 %collective-permute-start.6 = (bf16[256,512]{1,0:T(8,128)(2,1)S(1)}, bf16[256,512]{1,0:T(8,128)(2,1)S(1)}, u32[]{:S(2)}, u32[]{:S(2)}) collective-permute-start(bf16[256,512]{1,0:T(8,128)(2,1)S(1)} %collective-permute-done.2.refs_2_), channel_id=1, source_target_pairs={{0,4},{4,8},{8,12},{12,14},{14,10},{10,6},{6,2},{2,0},{1,5},{5,9},... | collective-permute-start | bytes 786440 | tf_op jit(solution)/shard_map/ppermute | solution.py:142
  33.4 12.5 %copy-start.5 = (bf16[256,512]{1,0:T(8,128)(2,1)S(1)}, bf16[256,512]{1,0:T(8,128)(2,1)}, u32[]{:S(2)}) copy-start(bf16[256,512]{1,0:T(8,128)(2,1)} %copy-done.4) | copy-start | bytes 786436
  35.7 7.9 %collective-permute-start.14 = (bf16[256,512]{1,0:T(8,128)(2,1)S(1)}, bf16[256,512]{1,0:T(8,128)(2,1)S(1)}, u32[]{:S(2)}, u32[]{:S(2)}) collective-permute-start(bf16[256,512]{1,0:T(8,128)(2,1)S(1)} %collective-permute-done.3.refs_5_), channel_id=1, source_target_pairs={{4,0},{8,4},{12,8},{14,12},{10,14},{6,10},{2,6},{0,2},{5,1},{9,5},... | collective-permute-start | bytes 786440 | tf_op jit(solution)/shard_map/ppermute | solution.py:142
  37.1 17.7 %collective-permute-start.13 = (bf16[256,512]{1,0:T(8,128)(2,1)S(1)}, bf16[256,512]{1,0:T(8,128)(2,1)S(1)}, u32[]{:S(2)}, u32[]{:S(2)}) collective-permute-start(bf16[256,512]{1,0:T(8,128)(2,1)S(1)} %pad_maximum_fusion.1), channel_id=1, source_target_pairs={{0,16},{16,0},{1,17},{17,1},{2,18},{18,2},{3,19},{19,3},{4,20},{20... | collective-permute-start | bytes 786440 | tf_op jit(solution)/shard_map/ppermute | solution.py:145
  37.7 14.9 %collective-permute-start.16 = (bf16[128,512]{1,0:T(8,128)(2,1)S(1)}, bf16[128,512]{1,0:T(8,128)(2,1)S(1)}, u32[]{:S(2)}, u32[]{:S(2)}) collective-permute-start(bf16[128,512]{1,0:T(8,128)(2,1)S(1)} %collective-permute-done.12.refs_4_), channel_id=1, source_target_pairs={{4,0},{8,4},{12,8},{14,12},{10,14},{6,10},{2,6},{0,2},{5,1},{9,5},... | collective-permute-start | bytes 393224 | tf_op jit(solution)/shard_map/ppermute | solution.py:143
  39.1 13.5 %collective-permute-start.15 = (bf16[128,512]{1,0:T(8,128)(2,1)}, bf16[128,512]{1,0:T(8,128)(2,1)S(1)}, u32[]{:S(2)}, u32[]{:S(2)}) collective-permute-start(bf16[128,512]{1,0:T(8,128)(2,1)} %collective-permute-done.11.refs_1_), channel_id=1, source_target_pairs={{0,4},{4,8},{8,12},{12,14},{14,10},{10,6},{6,2},{2,0},{1,5},{5,9},... | collective-permute-start | bytes 393224 | tf_op jit(solution)/shard_map/ppermute | solution.py:143
  43.6 11.4 %collective-permute-start.7 = (bf16[256,512]{1,0:T(8,128)(2,1)S(1)}, bf16[256,512]{1,0:T(8,128)(2,1)}, u32[]{:S(2)}, u32[]{:S(2)}) collective-permute-start(bf16[256,512]{1,0:T(8,128)(2,1)S(1)} %collective-permute-done.6.refs_0_), channel_id=1, source_target_pairs={{0,4},{4,8},{8,12},{12,14},{14,10},{10,6},{6,2},{2,0},{1,5},{5,9},... | collective-permute-start | bytes 786440 | tf_op jit(solution)/shard_map/ppermute | solution.py:142
  45.9 9.2 %collective-permute-start.18 = (bf16[256,512]{1,0:T(8,128)(2,1)S(1)}, bf16[256,512]{1,0:T(8,128)(2,1)}, u32[]{:S(2)}, u32[]{:S(2)}) collective-permute-start(bf16[256,512]{1,0:T(8,128)(2,1)S(1)} %collective-permute-done.14.refs_3_), channel_id=1, source_target_pairs={{4,0},{8,4},{12,8},{14,12},{10,14},{6,10},{2,6},{0,2},{5,1},{9,5},... | collective-permute-start | bytes 786440 | tf_op jit(solution)/shard_map/ppermute | solution.py:142
  45.9 1.0 copy-start.3
  46.9 0.9 copy-start.7
  52.6 6.5 %collective-permute-start.25 = (bf16[128,512]{1,0:T(8,128)(2,1)S(1)}, bf16[128,512]{1,0:T(8,128)(2,1)S(1)}, u32[]{:S(2)}, u32[]{:S(2)}) collective-permute-start(bf16[128,512]{1,0:T(8,128)(2,1)S(1)} %collective-permute-done.16.refs_10_), channel_id=1, source_target_pairs={{4,0},{8,4},{12,8},{14,12},{10,14},{6,10},{2,6},{0,2},{5,1},{9,5},... | collective-permute-start | bytes 393224 | tf_op jit(solution)/shard_map/ppermute | solution.py:143
  52.8 6.3 %collective-permute-start.21 = (bf16[128,512]{1,0:T(8,128)(2,1)S(1)}, bf16[128,512]{1,0:T(8,128)(2,1)S(1)}, u32[]{:S(2)}, u32[]{:S(2)}) collective-permute-start(bf16[128,512]{1,0:T(8,128)(2,1)S(1)} %collective-permute-done.15.refs_7_), channel_id=1, source_target_pairs={{0,4},{4,8},{8,12},{12,14},{14,10},{10,6},{6,2},{2,0},{1,5},{5,9},... | collective-permute-start | bytes 393224 | tf_op jit(solution)/shard_map/ppermute | solution.py:143
  54.7 6.9 %collective-permute-start.17 = (bf16[256,512]{1,0:T(8,128)(2,1)S(1)}, bf16[256,512]{1,0:T(8,128)(2,1)S(1)}, u32[]{:S(2)}, u32[]{:S(2)}) collective-permute-start(bf16[256,512]{1,0:T(8,128)(2,1)S(1)} %pad_maximum_fusion.2), channel_id=1, source_target_pairs={{0,16},{16,0},{1,17},{17,1},{2,18},{18,2},{3,19},{19,3},{4,20},{20... | collective-permute-start | bytes 786440 | tf_op jit(solution)/shard_map/ppermute | solution.py:145
  55.1 15.8 %collective-permute-start.30 = (bf16[256,512]{1,0:T(8,128)(2,1)}, bf16[256,512]{1,0:T(8,128)(2,1)}, u32[]{:S(2)}, u32[]{:S(2)}) collective-permute-start(bf16[256,512]{1,0:T(8,128)(2,1)} %collective-permute-done.18.refs_9_), channel_id=1, source_target_pairs={{4,0},{8,4},{12,8},{14,12},{10,14},{6,10},{2,6},{0,2},{5,1},{9,5},... | collective-permute-start | bytes 786440 | tf_op jit(solution)/shard_map/ppermute | solution.py:142
  55.5 16.1 %collective-permute-start.9 = (bf16[256,512]{1,0:T(8,128)(2,1)}, bf16[256,512]{1,0:T(8,128)(2,1)}, u32[]{:S(2)}, u32[]{:S(2)}) collective-permute-start(bf16[256,512]{1,0:T(8,128)(2,1)} %collective-permute-done.7.refs_6_), channel_id=1, source_target_pairs={{0,4},{4,8},{8,12},{12,14},{14,10},{10,6},{6,2},{2,0},{1,5},{5,9},... | collective-permute-start | bytes 786440 | tf_op jit(solution)/shard_map/ppermute | solution.py:142
  59.8 16.1 %collective-permute-start.36 = (bf16[256,512]{1,0:T(8,128)(2,1)}, bf16[256,512]{1,0:T(8,128)(2,1)}, u32[]{:S(2)}, u32[]{:S(2)}) collective-permute-start(bf16[256,512]{1,0:T(8,128)(2,1)} %pad_maximum_fusion.4), channel_id=1, source_target_pairs={{0,16},{16,0},{1,17},{17,1},{2,18},{18,2},{3,19},{19,3},{4,20},{20... | collective-permute-start | bytes 786440 | tf_op jit(solution)/shard_map/ppermute | solution.py:145
  59.8 8.7 %collective-permute-start.26 = (bf16[128,512]{1,0:T(8,128)(2,1)S(1)}, bf16[128,512]{1,0:T(8,128)(2,1)S(1)}, u32[]{:S(2)}, u32[]{:S(2)}) collective-permute-start(bf16[128,512]{1,0:T(8,128)(2,1)S(1)} %collective-permute-done.25.refs_4_), channel_id=1, source_target_pairs={{4,0},{8,4},{12,8},{14,12},{10,14},{6,10},{2,6},{0,2},{5,1},{9,5},... | collective-permute-start | bytes 393224 | tf_op jit(solution)/shard_map/ppermute | solution.py:143
  61.7 6.8 %collective-permute-start.22 = (bf16[128,512]{1,0:T(8,128)(2,1)S(1)}, bf16[128,512]{1,0:T(8,128)(2,1)S(1)}, u32[]{:S(2)}, u32[]{:S(2)}) collective-permute-start(bf16[128,512]{1,0:T(8,128)(2,1)S(1)} %collective-permute-done.21.refs_1_), channel_id=1, source_target_pairs={{0,4},{4,8},{8,12},{12,14},{14,10},{10,6},{6,2},{2,0},{1,5},{5,9},... | collective-permute-start | bytes 393224 | tf_op jit(solution)/shard_map/ppermute | solution.py:143
  68.5 5.0 %collective-permute-start.27 = (bf16[128,512]{1,0:T(8,128)(2,1)S(1)}, bf16[128,512]{1,0:T(8,128)(2,1)S(1)}, u32[]{:S(2)}, u32[]{:S(2)}) collective-permute-start(bf16[128,512]{1,0:T(8,128)(2,1)S(1)} %collective-permute-done.26.refs_10_), channel_id=1, source_target_pairs={{4,0},{8,4},{12,8},{14,12},{10,14},{6,10},{2,6},{0,2},{5,1},{9,5},... | collective-permute-start | bytes 393224 | tf_op jit(solution)/shard_map/ppermute | solution.py:143
  69.0 5.2 %collective-permute-start.23 = (bf16[128,512]{1,0:T(8,128)(2,1)S(1)}, bf16[128,512]{1,0:T(8,128)(2,1)S(1)}, u32[]{:S(2)}, u32[]{:S(2)}) collective-permute-start(bf16[128,512]{1,0:T(8,128)(2,1)S(1)} %collective-permute-done.22.refs_7_), channel_id=1, source_target_pairs={{0,4},{4,8},{8,12},{12,14},{14,10},{10,6},{6,2},{2,0},{1,5},{5,9},... | collective-permute-start | bytes 393224 | tf_op jit(solution)/shard_map/ppermute | solution.py:143
  70.9 12.2 %collective-permute-start.37 = (bf16[256,512]{1,0:T(8,128)(2,1)S(1)}, bf16[256,512]{1,0:T(8,128)(2,1)S(1)}, u32[]{:S(2)}, u32[]{:S(2)}) collective-permute-start(bf16[256,512]{1,0:T(8,128)(2,1)S(1)} %pad_maximum_fusion.5), channel_id=1, source_target_pairs={{0,16},{16,0},{1,17},{17,1},{2,18},{18,2},{3,19},{19,3},{4,20},{20... | collective-permute-start | bytes 786440 | tf_op jit(solution)/shard_map/ppermute | solution.py:145
  71.6 9.5 %collective-permute-start.31 = (bf16[256,512]{1,0:T(8,128)(2,1)}, bf16[256,512]{1,0:T(8,128)(2,1)S(1)}, u32[]{:S(2)}, u32[]{:S(2)}) collective-permute-start(bf16[256,512]{1,0:T(8,128)(2,1)} %collective-permute-done.30.refs_3_), channel_id=1, source_target_pairs={{4,0},{8,4},{12,8},{14,12},{10,14},{6,10},{2,6},{0,2},{5,1},{9,5},... | collective-permute-start | bytes 786440 | tf_op jit(solution)/shard_map/ppermute | solution.py:142
  73.5 9.1 %collective-permute-start.10 = (bf16[256,512]{1,0:T(8,128)(2,1)}, bf16[256,512]{1,0:T(8,128)(2,1)S(1)}, u32[]{:S(2)}, u32[]{:S(2)}) collective-permute-start(bf16[256,512]{1,0:T(8,128)(2,1)} %collective-permute-done.9.refs_0_), channel_id=1, source_target_pairs={{0,4},{4,8},{8,12},{12,14},{14,10},{10,6},{6,2},{2,0},{1,5},{5,9},... | collective-permute-start | bytes 786440 | tf_op jit(solution)/shard_map/ppermute | solution.py:142
  74.2 10.4 %collective-permute-start.28 = (bf16[256,512]{1,0:T(8,128)(2,1)S(1)}, bf16[256,512]{1,0:T(8,128)(2,1)S(1)}, u32[]{:S(2)}, u32[]{:S(2)}) collective-permute-start(bf16[256,512]{1,0:T(8,128)(2,1)S(1)} %pad_maximum_fusion.3), channel_id=1, source_target_pairs={{0,16},{16,0},{1,17},{17,1},{2,18},{18,2},{3,19},{19,3},{4,20},{20... | collective-permute-start | bytes 786440 | tf_op jit(solution)/shard_map/ppermute | solution.py:145
  75.9 9.8 %collective-permute-start.34 = (bf16[128,512]{1,0:T(8,128)(2,1)S(1)}, bf16[128,512]{1,0:T(8,128)(2,1)S(1)}, u32[]{:S(2)}, u32[]{:S(2)}) collective-permute-start(bf16[128,512]{1,0:T(8,128)(2,1)S(1)} %collective-permute-done.27.refs_4_), channel_id=1, source_target_pairs={{4,0},{8,4},{12,8},{14,12},{10,14},{6,10},{2,6},{0,2},{5,1},{9,5},... | collective-permute-start | bytes 393224 | tf_op jit(solution)/shard_map/ppermute | solution.py:143
  81.0 18.4 %collective-permute-start.24 = (bf16[128,512]{1,0:T(8,128)(2,1)S(1)}, bf16[128,512]{1,0:T(8,128)(2,1)S(1)}, u32[]{:S(2)}, u32[]{:S(2)}) collective-permute-start(bf16[128,512]{1,0:T(8,128)(2,1)S(1)} %collective-permute-done.23.refs_1_), channel_id=1, source_target_pairs={{0,4},{4,8},{8,12},{12,14},{14,10},{10,6},{6,2},{2,0},{1,5},{5,9},... | collective-permute-start | bytes 393224 | tf_op jit(solution)/shard_map/ppermute | solution.py:143
  82.6 6.4 %collective-permute-start.32 = (bf16[256,512]{1,0:T(8,128)(2,1)S(1)}, bf16[256,512]{1,0:T(8,128)(2,1)S(1)}, u32[]{:S(2)}, u32[]{:S(2)}) collective-permute-start(bf16[256,512]{1,0:T(8,128)(2,1)S(1)} %collective-permute-done.31.refs_9_), channel_id=1, source_target_pairs={{4,0},{8,4},{12,8},{14,12},{10,14},{6,10},{2,6},{0,2},{5,1},{9,5},... | collective-permute-start | bytes 786440 | tf_op jit(solution)/shard_map/ppermute | solution.py:142
  83.1 6.4 %collective-permute-start.19 = (bf16[256,512]{1,0:T(8,128)(2,1)S(1)}, bf16[256,512]{1,0:T(8,128)(2,1)S(1)}, u32[]{:S(2)}, u32[]{:S(2)}) collective-permute-start(bf16[256,512]{1,0:T(8,128)(2,1)S(1)} %collective-permute-done.10.refs_6_), channel_id=1, source_target_pairs={{0,4},{4,8},{8,12},{12,14},{14,10},{10,6},{6,2},{2,0},{1,5},{5,9},... | collective-permute-start | bytes 786440 | tf_op jit(solution)/shard_map/ppermute | solution.py:142
  84.7 14.8 %collective-permute-start.29 = (bf16[128,512]{1,0:T(8,128)(2,1)S(1)}, bf16[128,512]{1,0:T(8,128)(2,1)S(1)}, u32[]{:S(2)}, u32[]{:S(2)}) collective-permute-start(bf16[128,512]{1,0:T(8,128)(2,1)S(1)} %get-tuple-element.78.refs_2_), channel_id=1, source_target_pairs={{0,4},{4,8},{8,12},{12,14},{14,10},{10,6},{6,2},{2,0},{1,5},{5,9},... | collective-permute-start | bytes 393224 | tf_op jit(solution)/shard_map/ppermute | solution.py:152
  85.7 13.7 %collective-permute-start.35 = (bf16[128,512]{1,0:T(8,128)(2,1)S(1)}, bf16[128,512]{1,0:T(8,128)(2,1)S(1)}, u32[]{:S(2)}, u32[]{:S(2)}) collective-permute-start(bf16[128,512]{1,0:T(8,128)(2,1)S(1)} %get-tuple-element.77.refs_5_), channel_id=1, source_target_pairs={{4,0},{8,4},{12,8},{14,12},{10,14},{6,10},{2,6},{0,2},{5,1},{9,5},... | collective-permute-start | bytes 393224 | tf_op jit(solution)/shard_map/ppermute | solution.py:152
  89.0 10.5 %collective-permute-start.33 = (bf16[256,512]{1,0:T(8,128)(2,1)S(1)}, bf16[256,512]{1,0:T(8,128)(2,1)S(1)}, u32[]{:S(2)}, u32[]{:S(2)}) collective-permute-start(bf16[256,512]{1,0:T(8,128)(2,1)S(1)} %collective-permute-done.32.refs_3_), channel_id=1, source_target_pairs={{4,0},{8,4},{12,8},{14,12},{10,14},{6,10},{2,6},{0,2},{5,1},{9,5},... | collective-permute-start | bytes 786440 | tf_op jit(solution)/shard_map/ppermute | solution.py:142
  89.5 10.0 %collective-permute-start.20 = (bf16[256,512]{1,0:T(8,128)(2,1)S(1)}, bf16[256,512]{1,0:T(8,128)(2,1)S(1)}, u32[]{:S(2)}, u32[]{:S(2)}) collective-permute-start(bf16[256,512]{1,0:T(8,128)(2,1)S(1)} %collective-permute-done.19.refs_0_), channel_id=1, source_target_pairs={{0,4},{4,8},{8,12},{12,14},{14,10},{10,6},{6,2},{2,0},{1,5},{5,9},... | collective-permute-start | bytes 786440 | tf_op jit(solution)/shard_map/ppermute | solution.py:142
  99.5 6.0 %copy-start.1 = (bf16[512,512]{1,0:T(8,128)(2,1)S(1)}, bf16[512,512]{1,0:T(8,128)(2,1)}, u32[]{:S(2)}) copy-start(bf16[512,512]{1,0:T(8,128)(2,1)} %copy-done) | copy-start | bytes 1572868
  99.5 6.0 %copy-start.8 = (bf16[4,4,4,8,128]{4,3,2,1,0:T(8,128)(2,1)S(1)}, bf16[4,4,4,8,128]{4,3,2,1,0:T(8,128)(2,1)}, u32[]{:S(2)}) copy-start(bf16[4,4,4,8,128]{4,3,2,1,0:T(8,128)(2,1)} %copy.40) | copy-start | bytes 393220
  102.7 2.7 %collective-permute-start.38 = (bf16[1024,512]{1,0:T(8,128)(2,1)S(1)}, bf16[1024,512]{1,0:T(8,128)(2,1)S(1)}, u32[]{:S(2)}, u32[]{:S(2)}) collective-permute-start(bf16[1024,512]{1,0:T(8,128)(2,1)S(1)} %get-tuple-element.62.have_ref), channel_id=1, source_target_pairs={{0,1},{1,0},{2,3},{3,2},{4,5},{5,4},{6,7},{7,6},{8,9},{9,8},{10,11... | collective-permute-start | bytes 3145736 | tf_op jit(solution)/shard_map/ppermute | solution.py:290
  125.0 3.9 %collective-permute-start.39 = (bf16[64,128]{1,0:T(8,128)(2,1)}, bf16[64,128]{1,0:T(8,128)(2,1)S(1)}, u32[]{:S(2)}, u32[]{:S(2)}) collective-permute-start(bf16[64,128]{1,0:T(8,128)(2,1)} %shard_map.88), channel_id=1, source_target_pairs={{0,2},{2,0},{4,6},{6,4},{8,10},{10,8},{12,14},{14,12},{1,3},{3,1},... | collective-permute-start | bytes 49160 | tf_op jit(solution)/shard_map/ppermute | solution.py:297
  129.7 5.8 %collective-permute-start.40 = (bf16[128,128]{1,0:T(8,128)(2,1)S(1)}, bf16[128,128]{1,0:T(8,128)(2,1)S(1)}, u32[]{:S(2)}, u32[]{:S(2)}) collective-permute-start(bf16[128,128]{1,0:T(8,128)(2,1)S(1)} %pad_maximum_fusion.8), channel_id=1, source_target_pairs={{0,12},{2,14},{4,8},{6,10},{8,4},{10,6},{12,0},{14,2},{1,13},{3,15... | collective-permute-start | bytes 98312 | tf_op jit(solution)/shard_map/ppermute | solution.py:300
  131.2 5.1 %collective-permute-start.41 = (bf16[128,128]{1,0:T(8,128)(2,1)S(1)}, bf16[128,128]{1,0:T(8,128)(2,1)S(1)}, u32[]{:S(2)}, u32[]{:S(2)}) collective-permute-start(bf16[128,128]{1,0:T(8,128)(2,1)S(1)} %pad_maximum_fusion.8), channel_id=1, source_target_pairs={{0,8},{2,10},{4,12},{6,14},{8,0},{10,2},{12,4},{14,6},{1,9},{3,11}... | collective-permute-start | bytes 98312 | tf_op jit(solution)/shard_map/ppermute | solution.py:300
  131.9 4.5 %collective-permute-start.42 = (bf16[128,128]{1,0:T(8,128)(2,1)S(1)}, bf16[128,128]{1,0:T(8,128)(2,1)S(1)}, u32[]{:S(2)}, u32[]{:S(2)}) collective-permute-start(bf16[128,128]{1,0:T(8,128)(2,1)S(1)} %pad_maximum_fusion.8), channel_id=1, source_target_pairs={{0,4},{2,6},{4,0},{6,2},{8,12},{10,14},{12,8},{14,10},{1,5},{3,7},... | collective-permute-start | bytes 98312 | tf_op jit(solution)/shard_map/ppermute | solution.py:300
  136.5 1.4 %collective-permute-start.43 = (bf16[16,1,4096]{2,0,1:T(8,128)(2,1)S(1)}, bf16[16,1,4096]{2,0,1:T(8,128)(2,1)S(1)}, u32[]{:S(2)}, u32[]{:S(2)}) collective-permute-start(bf16[16,1,4096]{2,0,1:T(8,128)(2,1)S(1)} %reshape.94), channel_id=1, source_target_pairs={{0,1},{1,0},{2,3},{3,2},{4,5},{5,4},{6,7},{7,6},{8,9},{9,8},{10,11... | collective-permute-start | bytes 393224 | tf_op jit(solution)/shard_map/ppermute | solution.py:310

commit v7 on v6

--- a/solution.py
+++ b/solution.py
@@ -20,10 +20,9 @@
 
 def add_pieces(tokens, theirs, halves, total, part, core=None):
     tok_rows = tokens.shape[0]
-    span = sum(x.shape[0] for x in halves[0][1:])
-    width = halves[0][1].shape[1]
+    span, width = tokens.shape[1] // lax.axis_size("chip") // CORES, halves[0][1].shape[1]
     deep = span * len(halves)
-    flat = [x for half in halves for x in half[1:]]
+    flat = [x for half in halves for x in half[1:4]]
     count = len(flat)
     last = core is not None
     places = jnp.stack([half[0] for half in halves] + [part] + ([core, 1 - core] if last else []))
@@ -48,8 +47,10 @@
             weights[at : at + shared, :] = parts.pop(0)[...]
             if len(half) > 2:
                 rest = half[2].shape[0]
-                for turn in (places_ref[len(halves)], 1 - places_ref[len(halves)]):
-                    weights[pl.ds(pl.multiple_of(at + shared + turn * rest, rest), rest), :] = parts.pop(0)[...]
+                turn = places_ref[len(halves)]
+                for turn, skip in ((turn, 0), (1 - turn, half[4] * rest)):
+                    rows = pl.ds(pl.multiple_of(at + shared + turn * rest, rest), rest)
+                    weights[rows, :] = parts.pop(0)[skip : skip + rest, :]
         mark_ref[...] = jnp.zeros_like(mark_ref)
         for j in range(2):
             for h in range(len(halves)):
@@ -127,13 +128,12 @@
     theirs = lax.ppermute(tokens_later, "core", SWAP)
     todo = [(start_of(0, 0), own), (start_of(1, 0), got)]
     calls = {3: 4, 5: 4, 7: 4}
-    total = mark = others = None
+    total = mark = crossed = None
     for step in range(1, chips):
         if step == 2:
-            both, single, inputs = lax.optimization_barrier((both, single, inputs))
-            early = prepare(*inputs)
-        if step == 4:
-            both[0], early = lax.optimization_barrier((both[0], early))
+            both, single = lax.optimization_barrier((both, single))
+        if step == last:
+            _, inputs = lax.optimization_barrier((both[0], inputs))
         if mark is not None:
             both = [lax.optimization_barrier((x, mark))[0] for x in both]
             single = [lax.optimization_barrier((x, mark))[0] for x in single]
@@ -143,16 +143,16 @@
         single = [lax.ppermute(x, "chip", way) for x, way in zip(single, ways)]
         if step > 1:
             crossed = lax.ppermute(jnp.concatenate(passed, 0), "groups", SWAP)
-            others = [crossed[:rest], crossed[rest:]]
-            todo += [(start_of(w, step - 1), before[w], passed[w], others[w]) for w in range(2)]
+            todo += [(start_of(w, step - 1), before[w], passed[w], crossed, w) for w in range(2)]
         before = both
         if step in calls:
             ready, todo = todo[: calls[step]], todo[calls[step] :]
             total, mark = add_pieces(tokens, theirs, ready, total, part)
-    others = [lax.ppermute(x, "chip", way) for x, way in zip(others, ways)]
+    crossed, _ = lax.optimization_barrier((crossed, mark))
+    others = [lax.ppermute(crossed[w * rest : (w + 1) * rest], "chip", ways[w]) for w in range(2)]
     total, _ = add_pieces(tokens, theirs, todo, total, part)
-    final = [(start_of(w, last), both[w], single[w], others[w]) for w in range(2)]
-    return add_pieces(tokens, theirs, final, total, part, core)[0], early
+    final = [(start_of(w, last), both[w], single[w], others[w], 0) for w in range(2)]
+    return add_pieces(tokens, theirs, final, total, part, core)[0], prepare(*inputs)
 
 
 def attend(have, got, core, key_up, value_up, query, bounds, chips):
@@ -165,8 +165,9 @@
     def kernel(core_ref, have_ref, got_ref, key_up_ref, value_up_ref, query_ref, bounds_ref, out_ref):
         first = core_ref[0] == 0
         have, got = have_ref[...], got_ref[...]
-        keys = mm(jnp.where(first, have, got), key_up_ref[...]).astype(BF)
-        values = mm(jnp.where(first, got, have), value_up_ref[...]).astype(BF)
+        lanes = pl.ds(pl.multiple_of(core_ref[0] * heads * DH, heads * DH), heads * DH)
+        keys = mm(jnp.where(first, have, got), key_up_ref[:, lanes]).astype(BF)
+        values = mm(jnp.where(first, got, have), value_up_ref[:, lanes]).astype(BF)
         position = lax.broadcasted_iota(jnp.int32, (tokens, rows), 0)
         visible = (position >= bounds_ref[0:1, :]) & (position < bounds_ref[1:2, :])
         tops, totals = [], []
@@ -255,42 +256,44 @@
     rows = pairs * heads * group
     share = rows // chips
 
-    def prepare(queries, new_latent, key_up, value_up):
-        query = lax.dynamic_index_in_dim(
-            queries.reshape(steps_count, req_count, CORES, heads * group * DH), core, 2, keepdims=False
-        ).reshape(steps_count, req_count, heads, group, DH)
-        key_up = lax.dynamic_slice_in_dim(key_up, core * heads * DH, heads * DH, 1)
-        value_up = lax.dynamic_slice_in_dim(value_up, core * heads * DH, heads * DH, 1)
-        flat_new = new_latent.reshape(pairs, 2 * lat_width)
-        new_keys = mm(flat_new[:, :lat_width], key_up).astype(BF).reshape(steps_count, req_count, heads, DH)
-        new_values = mm(flat_new[:, lat_width:], value_up).astype(BF).reshape(steps_count, req_count, heads, DH)
-        causal = (jnp.arange(steps_count)[:, None] >= jnp.arange(steps_count)[None, :])[:, None, None, None, :]
-        fresh = jnp.einsum("srgjd,urgd->srgju", query, new_keys, preferred_element_type=F32) * scale
-        fresh = jnp.where(causal, fresh, -1e30)
-        fresh_top = jnp.max(fresh, -1)
-        fresh_weights = jnp.where(causal, jnp.exp(fresh - fresh_top[..., None]), 0.0)
-        fresh_total = jnp.sum(fresh_weights, -1)
-        fresh_summed = jnp.einsum("srgju,urgd->srgjd", fresh_weights.astype(BF), new_values, preferred_element_type=F32)
-
-        def my_share(x):
-            return lax.dynamic_slice_in_dim(x, chip * share, share, 0)
-
-        fresh_summed = my_share(fresh_summed.reshape(rows, DH))
-        fresh_stats = [my_share(x.reshape(rows)).reshape(-1, group).T for x in (fresh_top, fresh_total)]
-        fresh_stats = jnp.pad(jnp.concatenate(fresh_stats, 1), ((0, 0), (0, DH - 2 * share // group)))
-
-        offsets = jnp.cumsum(prompt_lens) - prompt_lens
-        bounds = jnp.stack([offsets, offsets + prompt_lens]) - chip * CORES * tok_rows
-        bounds = jnp.broadcast_to(bounds[:, None, :, None], (2, steps_count, req_count, group)).reshape(2, -1)
-        by_head = query.transpose(2, 0, 1, 3, 4).reshape(heads, pairs * group, DH)
-        return by_head, bounds, key_up, value_up, fresh_stats, fresh_summed
-
-    have, early = project(tokens, key_down, value_down, prepare, (queries, new_latent, key_up, value_up))
-    by_head, bounds, key_up, value_up, fresh_stats, fresh_summed = early
+    def by_head(queries):
+        mine = lax.dynamic_slice_in_dim(queries, core * heads * group * DH, heads * group * DH, 2)
+        return mine.reshape(steps_count, req_count, heads, group, DH).transpose(2, 0, 1, 3, 4)
+
+    have, query = project(tokens, key_down, value_down, by_head, (queries,))
     got = lax.ppermute(have, "core", SWAP)
-    sending = attend(have, got, core, key_up, value_up, by_head, bounds, chips)
-
-    arrived = lax.all_to_all(sending, "chip", split_axis=0, concat_axis=0, tiled=True)
+
+    offsets = jnp.cumsum(prompt_lens) - prompt_lens
+    bounds = jnp.stack([offsets, offsets + prompt_lens]) - chip * CORES * tok_rows
+    bounds = jnp.broadcast_to(bounds[:, None, :, None], (2, steps_count, req_count, group)).reshape(2, -1)
+    sending = attend(have, got, core, key_up, value_up, query.reshape(heads, -1, DH), bounds, chips)
+
+    sending, query, new_latent = lax.optimization_barrier((sending, query, new_latent))
+    flat_new = new_latent.reshape(pairs, 2 * lat_width)
+
+    def my_heads(latent, up):
+        full = lax.dynamic_slice_in_dim(mm(latent, up), core * heads * DH, heads * DH, 1)
+        return full.astype(BF).reshape(steps_count, req_count, heads, DH)
+
+    new_keys = my_heads(flat_new[:, :lat_width], key_up)
+    new_values = my_heads(flat_new[:, lat_width:], value_up)
+    causal = (jnp.arange(steps_count)[:, None] >= jnp.arange(steps_count)[None, :])[:, None, None, None, :]
+    fresh = jnp.einsum("gsrjd,urgd->srgju", query, new_keys, preferred_element_type=F32) * scale
+    fresh = jnp.where(causal, fresh, -1e30)
+    fresh_top = jnp.max(fresh, -1)
+    fresh_weights = jnp.where(causal, jnp.exp(fresh - fresh_top[..., None]), 0.0)
+    fresh_total = jnp.sum(fresh_weights, -1)
+    fresh_summed = jnp.einsum("srgju,urgd->srgjd", fresh_weights.astype(BF), new_values, preferred_element_type=F32)
+
+    def my_share(x):
+        return lax.dynamic_slice_in_dim(x, chip * share, share, 0)
+
+    fresh_summed = my_share(fresh_summed.reshape(rows, DH))
+    fresh_stats = [my_share(x.reshape(rows)).reshape(-1, group).T for x in (fresh_top, fresh_total)]
+    fresh_stats = jnp.pad(jnp.concatenate(fresh_stats, 1), ((0, 0), (0, DH - 2 * share // group)))
+
+    flat = sending.reshape(chips, -1, DH)
+    arrived = lax.all_to_all(flat, "chip", split_axis=0, concat_axis=0, tiled=True).reshape(sending.shape)
     result = merge(arrived, fresh_stats, fresh_summed)
 
     if chips == 8:

time: 140 us -> 149 us (1.064)
  blocking collectives: 14.9 us -> 0 us
  waiting for transfers between devices: 32.4 us -> 44.8 us
  starting transfers between devices: 41.9 us -> 47.6 us
  Pallas kernels: 26.2 us -> 30.2 us
  other arithmetic: 6.41 us -> 8.09 us
    all_to_all x1 -> x0, blocking collectives: 14.9 us -> none  [on_device(): lax.all_to_all(sending, 'chip', split_axis=0, concat_axis=0, tiled=True)]
    ppermute x14, waiting for transfers between devices: 6.74 us -> 17.2 us  [project(): single = [lax.ppermute(x, 'chip', way) for x, way in zip(single, ways)]]
    unnamed x24 -> x48, local copies, waits for them, and re-layouts: 2.83 us -> 11.1 us
    ppermute x14, waiting for transfers between devices: 13.1 us -> 5.34 us  [project(): both = [lax.ppermute(x, 'chip', way) for x, way in zip(both, ways)]]
    all_to_all x0 -> x1, waiting for transfers between devices: none -> 7.5 us  [on_device(): lax.all_to_all(flat, 'chip', split_axis=0, concat_axis=0, tiled=True)]
    all_to_all x0 -> x1, starting transfers between devices: none -> 3.55 us  [on_device(): lax.all_to_all(flat, 'chip', split_axis=0, concat_axis=0, tiled=True)]
    ppermute x6, waiting for transfers between devices: 1.6 us -> 4.89 us  [project(): crossed = lax.ppermute(jnp.concatenate(passed, 0), 'groups', SWAP)]
    reshape x12 -> x11, local copies, waits for them, and re-layouts: 4.1 us -> 1.55 us  [the longest x1 0.77 us: on_device(): flat_new = new_latent.reshape(pairs, 2 * lat_width)]
  transfers between devices with their start and end apart: 44 -> 45, of which waited for: 16 -> 21; matrix products, arithmetic and copies ran while one was open for 12% -> 6% of each run, Pallas kernels for 13% -> 13%
where the time goes in v7:
time: 149 us; the launch traced here: 148 us
  starting transfers between devices  47.6 us (32%)
  waiting for transfers between devices  44.8 us (30%)
  Pallas kernels  30.2 us (20%)
  local copies, waits for them, and re-layouts  15.3 us (10%)
  other arithmetic  8.09 us (5%)
  matrix products  1.51 us (1%)
    pallas_call x5, Pallas kernels, add_pieces(): pl.pallas_call(kernel, out_shape=(jax.ShapeDtypeStruct((2 * tok_rows, wid...  23.6 us
    ppermute x14, waiting for transfers between devices, project(): single = [lax.ppermute(x, 'chip', way) for x, way in zip(single, ways)]  17.2 us
    ppermute x14, starting transfers between devices, project(): single = [lax.ppermute(x, 'chip', way) for x, way in zip(single, ways)]  15 us
    ppermute x14, starting transfers between devices, project(): both = [lax.ppermute(x, 'chip', way) for x, way in zip(both, ways)]  14.3 us
    unnamed x48, local copies, waits for them, and re-layouts  11.1 us
    all_to_all x1, waiting for transfers between devices, on_device(): lax.all_to_all(flat, 'chip', split_axis=0, concat_axis=0, tiled=True)  7.5 us
    ppermute x6, starting transfers between devices, project(): crossed = lax.ppermute(jnp.concatenate(passed, 0), 'groups', SWAP)  6.21 us
    ppermute x14, waiting for transfers between devices, project(): both = [lax.ppermute(x, 'chip', way) for x, way in zip(both, ways)]  5.34 us
  transfers between devices with their start and end apart: 45, of which 21 were waited for; matrix products, arithmetic and copies ran while one was open for 6% of the time, Pallas kernels for 13%

profile of v7, /device:TPU:0, one launch (start us, length us, event | category | flops | bytes accessed | tf_op | source)
XLA Modules:
  0.0 147.9 jit_solution(7309488079388842855)
XLA Ops:
  0.0 1.3 broadcast_select_fusion
  1.8 1.5 %collective-permute-done.refs_1_ = bf16[512,512]{1,0:T(8,128)(2,1)S(1)} collective-permute-done((bf16[512,512]{1,0:T(8,128)(2,1)S(1)}, bf16[512,512]{1,0:T(8,128)(2,1)S(1)}, u32[]{:S(2)}, u32[]{:S(2)}) %collective-permute-start) | collective-permute-done | bytes 524320 | tf_op jit(solution)/shard_map/ppermute | solution.py:99
  3.8 2.8 %collective-permute-start.4 = (bf16[128,512]{1,0:T(8,128)(2,1)S(1)}, bf16[128,512]{1,0:T(8,128)(2,1)S(1)}, u32[]{:S(2)}, u32[]{:S(2)}) collective-permute-start(bf16[128,512]{1,0:T(8,128)(2,1)S(1)} %slice_select_fusion), channel_id=1, source_target_pairs={{0,4},{4,8},{8,12},{12,14},{14,10},{10,6},{6,2},{2,0},{1,5},{5,9},... | collective-permute-start | bytes 393224 | tf_op jit(solution)/shard_map/ppermute | solution.py:143
  6.6 1.6 %collective-permute-start.2 = (bf16[256,512]{1,0:T(8,128)(2,1)S(1)}, bf16[256,512]{1,0:T(8,128)(2,1)S(1)}, u32[]{:S(2)}, u32[]{:S(2)}) collective-permute-start(bf16[256,512]{1,0:T(8,128)(2,1)S(1)} %slice.40), channel_id=1, source_target_pairs={{0,4},{4,8},{8,12},{12,14},{14,10},{10,6},{6,2},{2,0},{1,5},{5,9},... | collective-permute-start | bytes 786440 | tf_op jit(solution)/shard_map/ppermute | solution.py:142
  8.8 2.0 %collective-permute-done.4.refs_3_ = bf16[128,512]{1,0:T(8,128)(2,1)S(1)} collective-permute-done((bf16[128,512]{1,0:T(8,128)(2,1)S(1)}, bf16[128,512]{1,0:T(8,128)(2,1)S(1)}, u32[]{:S(2)}, u32[]{:S(2)}) %collective-permute-start.4) | collective-permute-done | bytes 131104 | tf_op jit(solution)/shard_map/ppermute | solution.py:143
  10.8 5.3 %collective-permute-done.2.refs_2_ = bf16[256,512]{1,0:T(8,128)(2,1)S(1)} collective-permute-done((bf16[256,512]{1,0:T(8,128)(2,1)S(1)}, bf16[256,512]{1,0:T(8,128)(2,1)S(1)}, u32[]{:S(2)}, u32[]{:S(2)}) %collective-permute-start.2) | collective-permute-done | bytes 262176 | tf_op jit(solution)/shard_map/ppermute | solution.py:142
  16.1 3.0 %collective-permute-done.5.refs_6_ = bf16[128,512]{1,0:T(8,128)(2,1)S(1)} collective-permute-done((bf16[128,512]{1,0:T(8,128)(2,1)S(1)}, bf16[128,512]{1,0:T(8,128)(2,1)S(1)}, u32[]{:S(2)}, u32[]{:S(2)}) %collective-permute-start.5) | collective-permute-done | bytes 131104 | tf_op jit(solution)/shard_map/ppermute | solution.py:143
  19.6 1.6 %collective-permute-start.8 = (bf16[256,512]{1,0:T(8,128)(2,1)S(1)}, bf16[256,512]{1,0:T(8,128)(2,1)S(1)}, u32[]{:S(2)}, u32[]{:S(2)}) collective-permute-start(bf16[256,512]{1,0:T(8,128)(2,1)S(1)} %pad_maximum_fusion), channel_id=1, source_target_pairs={{0,16},{16,0},{1,17},{17,1},{2,18},{18,2},{3,19},{19,3},{4,20},{20... | collective-permute-start | bytes 786440 | tf_op jit(solution)/shard_map/ppermute | solution.py:145
  21.6 1.6 %collective-permute-start.6 = (bf16[256,512]{1,0:T(8,128)(2,1)S(1)}, bf16[256,512]{1,0:T(8,128)(2,1)}, u32[]{:S(2)}, u32[]{:S(2)}) collective-permute-start(bf16[256,512]{1,0:T(8,128)(2,1)S(1)} %collective-permute-done.2.refs_2_), channel_id=1, source_target_pairs={{0,4},{4,8},{8,12},{12,14},{14,10},{10,6},{6,2},{2,0},{1,5},{5,9},... | collective-permute-start | bytes 786440 | tf_op jit(solution)/shard_map/ppermute | solution.py:142
  23.2 2.3 %collective-permute-done.12.refs_4_ = bf16[128,512]{1,0:T(8,128)(2,1)S(1)} collective-permute-done((bf16[128,512]{1,0:T(8,128)(2,1)S(1)}, bf16[128,512]{1,0:T(8,128)(2,1)S(1)}, u32[]{:S(2)}, u32[]{:S(2)}) %collective-permute-start.12) | collective-permute-done | bytes 131104 | tf_op jit(solution)/shard_map/ppermute | solution.py:143
  25.5 1.6 %collective-permute-start.11 = (bf16[128,512]{1,0:T(8,128)(2,1)S(1)}, bf16[128,512]{1,0:T(8,128)(2,1)}, u32[]{:S(2)}, u32[]{:S(2)}) collective-permute-start(bf16[128,512]{1,0:T(8,128)(2,1)S(1)} %collective-permute-done.4.refs_3_), channel_id=1, source_target_pairs={{0,4},{4,8},{8,12},{12,14},{14,10},{10,6},{6,2},{2,0},{1,5},{5,9},... | collective-permute-start | bytes 393224 | tf_op jit(solution)/shard_map/ppermute | solution.py:143
  27.1 3.8 %collective-permute-done.11.refs_1_ = bf16[128,512]{1,0:T(8,128)(2,1)} collective-permute-done((bf16[128,512]{1,0:T(8,128)(2,1)S(1)}, bf16[128,512]{1,0:T(8,128)(2,1)}, u32[]{:S(2)}, u32[]{:S(2)}) %collective-permute-start.11) | collective-permute-done | bytes 131104 | tf_op jit(solution)/shard_map/ppermute | solution.py:143
  30.9 1.6 %pad_maximum_fusion.1 = bf16[256,512]{1,0:T(8,128)(2,1)} fusion(bf16[128,512]{1,0:T(8,128)(2,1)S(1)} %collective-permute-done.12.refs_4_, bf16[128,512]{1,0:T(8,128)(2,1)} %collective-permute-done.11.refs_1_), kind=kLoop, calls=%fused_computation.7 | loop fusion | flops 524288 | bytes 524288 | tf_op jit(solution)/shard_map/concatenate | solution.py:145
  32.6 1.2 collective-permute-start.13
  34.5 0.9 collective-permute-start.16
  35.4 1.1 collective-permute-start.15
  36.5 0.9 collective-permute-start.18
  37.4 1.2 collective-permute-start.7
  38.6 0.9 copy-done.2
  39.6 0.9 copy-done.13
  40.5 0.9 copy-done.15
  41.4 0.9 copy-done.17
  42.3 0.9 copy-done.19
  43.3 4.7 %shard_map.82 = (f32[1024,512]{1,0:T(8,128)S(1)}, f32[8,128]{1,0:T(8,128)}) custom-call(s32[5]{0:T(128)S(1)} %stack.92.places_ref, bf16[512,8192]{1,0:T(8,128)(2,1)} %mine_ref.9, bf16[512,8192]{1,0:T(8,128)(2,1)} %collective-permute-done.1.theirs_ref, bf16[512,512]{1,0:T(8,128)(2,1)S(1)} %get-tuple-element.55.refs_0_, ...), custom_call_target="tpu_custom_call" | custom-call | flops 2147483648 | bytes 4194304 | tf_op jit(solution)/shard_map/pallas_call | solution.py:69
  48.0 1.0 pad_maximum_fusion.2
  48.9 0.9 collective-permute-start.17
  49.8 1.6 %collective-permute-start.25 = (bf16[128,512]{1,0:T(8,128)(2,1)}, bf16[128,512]{1,0:T(8,128)(2,1)S(1)}, u32[]{:S(2)}, u32[]{:S(2)}) collective-permute-start(bf16[128,512]{1,0:T(8,128)(2,1)} %collective-permute-done.16.refs_10_), channel_id=1, source_target_pairs={{4,0},{8,4},{12,8},{14,12},{10,14},{6,10},{2,6},{0,2},{5,1},{9,5},... | collective-permute-start | bytes 393224 | tf_op jit(solution)/shard_map/ppermute | solution.py:143
  52.0 1.6 %collective-permute-start.30 = (bf16[256,512]{1,0:T(8,128)(2,1)}, bf16[256,512]{1,0:T(8,128)(2,1)}, u32[]{:S(2)}, u32[]{:S(2)}) collective-permute-start(bf16[256,512]{1,0:T(8,128)(2,1)} %collective-permute-done.18.refs_9_), channel_id=1, source_target_pairs={{4,0},{8,4},{12,8},{14,12},{10,14},{6,10},{2,6},{0,2},{5,1},{9,5},... | collective-permute-start | bytes 786440 | tf_op jit(solution)/shard_map/ppermute | solution.py:142
  54.0 1.4 collective-permute-done.25.refs_4_
  55.4 1.6 %collective-permute-start.26 = (bf16[128,512]{1,0:T(8,128)(2,1)S(1)}, bf16[128,512]{1,0:T(8,128)(2,1)S(1)}, u32[]{:S(2)}, u32[]{:S(2)}) collective-permute-start(bf16[128,512]{1,0:T(8,128)(2,1)S(1)} %collective-permute-done.25.refs_4_), channel_id=1, source_target_pairs={{4,0},{8,4},{12,8},{14,12},{10,14},{6,10},{2,6},{0,2},{5,1},{9,5},... | collective-permute-start | bytes 393224 | tf_op jit(solution)/shard_map/ppermute | solution.py:143
  57.4 5.6 %shard_map.83 = (f32[1024,512]{1,0:T(8,128)S(1)}, f32[8,128]{1,0:T(8,128)}) custom-call(s32[5]{0:T(128)S(1)} %stack.97.places_ref, bf16[512,8192]{1,0:T(8,128)(2,1)} %mine_ref.9, bf16[512,8192]{1,0:T(8,128)(2,1)} %collective-permute-done.1.theirs_ref, bf16[256,512]{1,0:T(8,128)(2,1)} %collective-permute-done.6.refs_0_, ...), custom_call_target="tpu_custom_call", output_to_operand_aliasing={{0}: (15, {})} | custom-call | flops 2147483648 | bytes 4194304 | tf_op jit(solution)/shard_map/pallas_call | solution.py:69
  63.4 1.6 %collective-permute-start.27 = (bf16[128,512]{1,0:T(8,128)(2,1)S(1)}, bf16[128,512]{1,0:T(8,128)(2,1)S(1)}, u32[]{:S(2)}, u32[]{:S(2)}) collective-permute-start(bf16[128,512]{1,0:T(8,128)(2,1)S(1)} %collective-permute-done.26.refs_10_), channel_id=1, source_target_pairs={{4,0},{8,4},{12,8},{14,12},{10,14},{6,10},{2,6},{0,2},{5,1},{9,5},... | collective-permute-start | bytes 393224 | tf_op jit(solution)/shard_map/ppermute | solution.py:143
  65.4 1.6 %collective-permute-start.31 = (bf16[256,512]{1,0:T(8,128)(2,1)}, bf16[256,512]{1,0:T(8,128)(2,1)}, u32[]{:S(2)}, u32[]{:S(2)}) collective-permute-start(bf16[256,512]{1,0:T(8,128)(2,1)} %collective-permute-done.30.refs_3_), channel_id=1, source_target_pairs={{4,0},{8,4},{12,8},{14,12},{10,14},{6,10},{2,6},{0,2},{5,1},{9,5},... | collective-permute-start | bytes 786440 | tf_op jit(solution)/shard_map/ppermute | solution.py:142
  67.5 0.9 collective-permute-done.27.refs_4_
  68.4 1.6 %collective-permute-done.23.refs_1_ = bf16[128,512]{1,0:T(8,128)(2,1)S(1)} collective-permute-done((bf16[128,512]{1,0:T(8,128)(2,1)S(1)}, bf16[128,512]{1,0:T(8,128)(2,1)S(1)}, u32[]{:S(2)}, u32[]{:S(2)}) %collective-permute-start.23) | collective-permute-done | bytes 131104 | tf_op jit(solution)/shard_map/ppermute | solution.py:143
  72.6 1.5 %collective-permute-start.36 = (bf16[256,512]{1,0:T(8,128)(2,1)}, bf16[256,512]{1,0:T(8,128)(2,1)S(1)}, u32[]{:S(2)}, u32[]{:S(2)}) collective-permute-start(bf16[256,512]{1,0:T(8,128)(2,1)} %pad_maximum_fusion.4), channel_id=1, source_target_pairs={{0,16},{16,0},{1,17},{17,1},{2,18},{18,2},{3,19},{19,3},{4,20},{20... | collective-permute-start | bytes 786440 | tf_op jit(solution)/shard_map/ppermute | solution.py:145
  75.3 1.4 collective-permute-start.32
  77.6 1.3 collective-permute-done.28.refs_2_.refs_5_
  78.9 1.6 %collective-permute-start.34 = (bf16[128,512]{1,0:T(8,128)(2,1)}, bf16[128,512]{1,0:T(8,128)(2,1)S(1)}, u32[]{:S(2)}, u32[]{:S(2)}) collective-permute-start(bf16[128,512]{1,0:T(8,128)(2,1)} %copy-done.10), channel_id=1, source_target_pairs={{4,0},{8,4},{12,8},{14,12},{10,14},{6,10},{2,6},{0,2},{5,1},{9,5},... | collective-permute-start | bytes 393224 | tf_op jit(solution)/shard_map/ppermute | solution.py:143
  80.5 1.2 collective-permute-done.36.refs_2_.refs_5_
  82.1 2.4 %collective-permute-done.37.refs_8_.refs_11_ = bf16[256,512]{1,0:T(8,128)(2,1)S(1)} collective-permute-done((bf16[256,512]{1,0:T(8,128)(2,1)}, bf16[256,512]{1,0:T(8,128)(2,1)S(1)}, u32[]{:S(2)}, u32[]{:S(2)}) %collective-permute-start.37) | collective-permute-done | bytes 262176 | tf_op jit(solution)/shard_map/ppermute | solution.py:145
  84.9 1.9 %collective-permute-done.34.refs_4_ = bf16[128,512]{1,0:T(8,128)(2,1)S(1)} collective-permute-done((bf16[128,512]{1,0:T(8,128)(2,1)}, bf16[128,512]{1,0:T(8,128)(2,1)S(1)}, u32[]{:S(2)}, u32[]{:S(2)}) %collective-permute-start.34) | collective-permute-done | bytes 131104 | tf_op jit(solution)/shard_map/ppermute | solution.py:143
  86.8 1.1 collective-permute-start.35
  87.9 1.1 collective-permute-start.33
  89.0 0.9 collective-permute-start.20
  89.9 0.9 copy-done.7
  90.8 5.4 %shard_map.84 = (f32[1024,512]{1,0:T(8,128)S(1)}, f32[8,128]{1,0:T(8,128)}) custom-call(s32[5]{0:T(128)S(1)} %stack.105.places_ref, bf16[512,8192]{1,0:T(8,128)(2,1)} %mine_ref.9, bf16[512,8192]{1,0:T(8,128)(2,1)} %collective-permute-done.1.theirs_ref, bf16[256,512]{1,0:T(8,128)(2,1)} %collective-permute-done.9.refs_0_, ...), custom_call_target="tpu_custom_call", output_to_operand_aliasing={{0}: (15, {})} | custom-call | flops 2147483648 | bytes 4194304 | tf_op jit(solution)/shard_map/pallas_call | solution.py:69
  96.2 3.7 %shard_map.85 = (f32[1024,512]{1,0:T(8,128)S(1)}, f32[8,128]{1,0:T(8,128)}) custom-call(s32[3]{0:T(128)S(1)} %pad_add_fusion.places_ref, bf16[512,8192]{1,0:T(8,128)(2,1)} %mine_ref.9, bf16[512,8192]{1,0:T(8,128)(2,1)} %collective-permute-done.1.theirs_ref, bf16[256,512]{1,0:T(8,128)(2,1)} %collective-permute-done.19.refs_0_, ...), custom_call_target="tpu_custom_call", output_to_operand_aliasing={{0}: (9, {})} | custom-call | flops 1073741824 | bytes 2097152 | tf_op jit(solution)/shard_map/pallas_call | solution.py:69
  100.0 4.2 %shard_map.86 = (bf16[1024,512]{1,0:T(8,128)(2,1)}, f32[8,128]{1,0:T(8,128)}) custom-call(s32[5]{0:T(128)S(1)} %stack.87.places_ref, bf16[512,8192]{1,0:T(8,128)(2,1)} %mine_ref.9, bf16[512,8192]{1,0:T(8,128)(2,1)} %collective-permute-done.1.theirs_ref, bf16[256,512]{1,0:T(8,128)(2,1)S(1)} %collective-permute-done.20.refs_0_, ...), custom_call_target="tpu_custom_call" | custom-call | flops 1073741824 | bytes 2097152 | tf_op jit(solution)/shard_map/pallas_call | solution.py:69
  105.0 2.2 %collective-permute-done.38.got_ref = bf16[1024,512]{1,0:T(8,128)(2,1)S(1)} collective-permute-done((bf16[1024,512]{1,0:T(8,128)(2,1)}, bf16[1024,512]{1,0:T(8,128)(2,1)S(1)}, u32[]{:S(2)}, u32[]{:S(2)}) %collective-permute-start.38) | collective-permute-done | bytes 1048608 | tf_op jit(solution)/shard_map/ppermute | solution.py:264
  107.2 1.0 copy-done.20
  108.2 1.2 copy-done.4
  109.4 1.2 copy-done.21
  110.6 4.8 %shard_map.87 = f32[8,9,8,128]{3,2,1,0:T(8,128)} custom-call(s32[1]{0:T(128)} %bitcast.core_ref, bf16[1024,512]{1,0:T(8,128)(2,1)} %get-tuple-element.50.have_ref, bf16[1024,512]{1,0:T(8,128)(2,1)S(1)} %copy-done.21, bf16[512,1024]{1,0:T(8,128)(2,1)S(1)} %copy-done.3, bf16[512,1024]{1,0:T(8,128)(2,1)S(1)} %copy-done.4, bf16[4,128,128]{2,1,0:T(8,128)(2,1)S(1)} %bitcast.44, ...), custom_call_target="tpu_custom_call" | custom-call | flops 1342177280 | bytes 2097152 | tf_op jit(solution)/shard_map/pallas_call | solution.py:201
  117.4 3.6 %all-to-all-start = ((f32[8,72,128]{2,1,0:T(8,128)}), f32[8,72,128]{2,1,0:T(8,128)S(1)}, u32[]{:S(2)}, u32[]{:S(2)}) async-start(f32[8,72,128]{2,1,0:T(8,128)} %bitcast.25), calls=%async_computation | async-start | bytes 589824 | tf_op jit(solution)/shard_map/all_to_all | solution.py:296
  123.5 7.5 %all-to-all-done = f32[8,72,128]{2,1,0:T(8,128)S(1)} async-done(((f32[8,72,128]{2,1,0:T(8,128)}), f32[8,72,128]{2,1,0:T(8,128)S(1)}, u32[]{:S(2)}, u32[]{:S(2)}) %all-to-all-start) | async-done | bytes 294944 | tf_op jit(solution)/shard_map/all_to_all | solution.py:296
  131.7 1.9 %shard_map.88 = bf16[64,128]{1,0:T(8,128)(2,1)} custom-call(f32[8,9,8,128]{3,2,1,0:T(8,128)} %bitcast.45, f32[8,128]{1,0:T(8,128)} %select_maximum_fusion.stats_ref, f32[64,128]{1,0:T(8,128)} %constant_dynamic-slice_fusion.summed_ref), custom_call_target="tpu_custom_call" | custom-call | flops 131072 | bytes 294912 | tf_op jit(solution)/shard_map/pallas_call | solution.py:233
  133.6 1.5 collective-permute-start.39
  135.1 2.5 %collective-permute-done.39 = bf16[64,128]{1,0:T(8,128)(2,1)S(1)} collective-permute-done((bf16[64,128]{1,0:T(8,128)(2,1)}, bf16[64,128]{1,0:T(8,128)(2,1)S(1)}, u32[]{:S(2)}, u32[]{:S(2)}) %collective-permute-start.39) | collective-permute-done | bytes 16416 | tf_op jit(solution)/shard_map/ppermute | solution.py:300
  138.3 1.3 collective-permute-start.40
  139.6 1.3 collective-permute-start.41
  140.9 1.9 %collective-permute-start.42 = (bf16[128,128]{1,0:T(8,128)(2,1)S(1)}, bf16[128,128]{1,0:T(8,128)(2,1)S(1)}, u32[]{:S(2)}, u32[]{:S(2)}) collective-permute-start(bf16[128,128]{1,0:T(8,128)(2,1)S(1)} %pad_maximum_fusion.8), channel_id=1, source_target_pairs={{0,4},{2,6},{4,0},{6,2},{8,12},{10,14},{12,8},{14,10},{1,5},{3,7},... | collective-permute-start | bytes 98312 | tf_op jit(solution)/shard_map/ppermute | solution.py:303
  142.8 1.3 collective-permute-done.40
  145.3 1.3 collective-permute-done.43
  (138 shorter events, 20.6 us)
Async XLA Ops:
  0.0 104.7 %copy-start = (bf16[4,4,8192]{2,1,0:T(4,128)(2,1)S(1)}, bf16[4,4,8192]{2,1,0:T(4,128)(2,1)}, u32[]{:S(2)}) copy-start(bf16[4,4,8192]{2,1,0:T(4,128)(2,1)} %param.14) | copy-start | bytes 786436
  1.3 2.1 %collective-permute-start = (bf16[512,512]{1,0:T(8,128)(2,1)S(1)}, bf16[512,512]{1,0:T(8,128)(2,1)S(1)}, u32[]{:S(2)}, u32[]{:S(2)}) collective-permute-start(bf16[512,512]{1,0:T(8,128)(2,1)S(1)} %get-tuple-element.56), channel_id=1, source_target_pairs={{0,1},{1,0},{2,3},{3,2},{4,5},{5,4},{6,7},{7,6},{8,9},{9,8},{10,11... | collective-permute-start | bytes 1572872 | tf_op jit(solution)/shard_map/ppermute | solution.py:99
  3.4 34.0 %collective-permute-start.1 = (bf16[512,8192]{1,0:T(8,128)(2,1)}, bf16[512,8192]{1,0:T(8,128)(2,1)}, u32[]{:S(2)}, u32[]{:S(2)}) collective-permute-start(bf16[512,8192]{1,0:T(8,128)(2,1)} %mine_ref.9), channel_id=1, source_target_pairs={{0,1},{1,0},{2,3},{3,2},{4,5},{5,4},{6,7},{7,6},{8,9},{9,8},{10,11... | collective-permute-start | bytes 25165832 | tf_op jit(solution)/shard_map/ppermute | solution.py:128
  3.8 7.1 %collective-permute-start.4 = (bf16[128,512]{1,0:T(8,128)(2,1)S(1)}, bf16[128,512]{1,0:T(8,128)(2,1)S(1)}, u32[]{:S(2)}, u32[]{:S(2)}) collective-permute-start(bf16[128,512]{1,0:T(8,128)(2,1)S(1)} %slice_select_fusion), channel_id=1, source_target_pairs={{0,4},{4,8},{8,12},{12,14},{14,10},{10,6},{6,2},{2,0},{1,5},{5,9},... | collective-permute-start | bytes 393224 | tf_op jit(solution)/shard_map/ppermute | solution.py:143
  6.6 9.6 %collective-permute-start.2 = (bf16[256,512]{1,0:T(8,128)(2,1)S(1)}, bf16[256,512]{1,0:T(8,128)(2,1)S(1)}, u32[]{:S(2)}, u32[]{:S(2)}) collective-permute-start(bf16[256,512]{1,0:T(8,128)(2,1)S(1)} %slice.40), channel_id=1, source_target_pairs={{0,4},{4,8},{8,12},{12,14},{14,10},{10,6},{6,2},{2,0},{1,5},{5,9},... | collective-permute-start | bytes 786440 | tf_op jit(solution)/shard_map/ppermute | solution.py:142
  8.2 10.9 %collective-permute-start.3 = (bf16[256,512]{1,0:T(8,128)(2,1)S(1)}, bf16[256,512]{1,0:T(8,128)(2,1)S(1)}, u32[]{:S(2)}, u32[]{:S(2)}) collective-permute-start(bf16[256,512]{1,0:T(8,128)(2,1)S(1)} %slice.31), channel_id=1, source_target_pairs={{4,0},{8,4},{12,8},{14,12},{10,14},{6,10},{2,6},{0,2},{5,1},{9,5},... | collective-permute-start | bytes 786440 | tf_op jit(solution)/shard_map/ppermute | solution.py:142
  8.7 10.4 %collective-permute-start.5 = (bf16[128,512]{1,0:T(8,128)(2,1)S(1)}, bf16[128,512]{1,0:T(8,128)(2,1)S(1)}, u32[]{:S(2)}, u32[]{:S(2)}) collective-permute-start(bf16[128,512]{1,0:T(8,128)(2,1)S(1)} %slice_select_fusion.1), channel_id=1, source_target_pairs={{4,0},{8,4},{12,8},{14,12},{10,14},{6,10},{2,6},{0,2},{5,1},{9,5},... | collective-permute-start | bytes 393224 | tf_op jit(solution)/shard_map/ppermute | solution.py:143
  10.8 26.6 %copy-start.12 = (bf16[128,512]{1,0:T(8,128)(2,1)}, bf16[128,512]{1,0:T(8,128)(2,1)S(1)}, u32[]{:S(2)}) copy-start(bf16[128,512]{1,0:T(8,128)(2,1)S(1)} %collective-permute-done.4.refs_3_) | copy-start | bytes 393220
  16.1 21.3 %copy-start.16 = (bf16[256,512]{1,0:T(8,128)(2,1)}, bf16[256,512]{1,0:T(8,128)(2,1)S(1)}, u32[]{:S(2)}) copy-start(bf16[256,512]{1,0:T(8,128)(2,1)S(1)} %collective-permute-done.2.refs_2_) | copy-start | bytes 786436
  19.1 18.3 %copy-start.14 = (bf16[128,512]{1,0:T(8,128)(2,1)}, bf16[128,512]{1,0:T(8,128)(2,1)S(1)}, u32[]{:S(2)}) copy-start(bf16[128,512]{1,0:T(8,128)(2,1)S(1)} %collective-permute-done.5.refs_6_) | copy-start | bytes 393220
  19.1 18.3 %copy-start.18 = (bf16[256,512]{1,0:T(8,128)(2,1)}, bf16[256,512]{1,0:T(8,128)(2,1)S(1)}, u32[]{:S(2)}) copy-start(bf16[256,512]{1,0:T(8,128)(2,1)S(1)} %collective-permute-done.3.refs_5_) | copy-start | bytes 786436
  19.1 6.4 %collective-permute-start.12 = (bf16[128,512]{1,0:T(8,128)(2,1)S(1)}, bf16[128,512]{1,0:T(8,128)(2,1)S(1)}, u32[]{:S(2)}, u32[]{:S(2)}) collective-permute-start(bf16[128,512]{1,0:T(8,128)(2,1)S(1)} %collective-permute-done.5.refs_6_), channel_id=1, source_target_pairs={{4,0},{8,4},{12,8},{14,12},{10,14},{6,10},{2,6},{0,2},{5,1},{9,5},... | collective-permute-start | bytes 393224 | tf_op jit(solution)/shard_map/ppermute | solution.py:143
  19.6 14.2 %collective-permute-start.8 = (bf16[256,512]{1,0:T(8,128)(2,1)S(1)}, bf16[256,512]{1,0:T(8,128)(2,1)S(1)}, u32[]{:S(2)}, u32[]{:S(2)}) collective-permute-start(bf16[256,512]{1,0:T(8,128)(2,1)S(1)} %pad_maximum_fusion), channel_id=1, source_target_pairs={{0,16},{16,0},{1,17},{17,1},{2,18},{18,2},{3,19},{19,3},{4,20},{20... | collective-permute-start | bytes 786440 | tf_op jit(solution)/shard_map/ppermute | solution.py:145
  21.2 14.2 %collective-permute-start.14 = (bf16[256,512]{1,0:T(8,128)(2,1)S(1)}, bf16[256,512]{1,0:T(8,128)(2,1)}, u32[]{:S(2)}, u32[]{:S(2)}) collective-permute-start(bf16[256,512]{1,0:T(8,128)(2,1)S(1)} %collective-permute-done.3.refs_5_), channel_id=1, source_target_pairs={{4,0},{8,4},{12,8},{14,12},{10,14},{6,10},{2,6},{0,2},{5,1},{9,5},... | collective-permute-start | bytes 786440 | tf_op jit(solution)/shard_map/ppermute | solution.py:142
  21.6 14.9 %collective-permute-start.6 = (bf16[256,512]{1,0:T(8,128)(2,1)S(1)}, bf16[256,512]{1,0:T(8,128)(2,1)}, u32[]{:S(2)}, u32[]{:S(2)}) collective-permute-start(bf16[256,512]{1,0:T(8,128)(2,1)S(1)} %collective-permute-done.2.refs_2_), channel_id=1, source_target_pairs={{0,4},{4,8},{8,12},{12,14},{14,10},{10,6},{6,2},{2,0},{1,5},{5,9},... | collective-permute-start | bytes 786440 | tf_op jit(solution)/shard_map/ppermute | solution.py:142
  25.5 5.5 %collective-permute-start.11 = (bf16[128,512]{1,0:T(8,128)(2,1)S(1)}, bf16[128,512]{1,0:T(8,128)(2,1)}, u32[]{:S(2)}, u32[]{:S(2)}) collective-permute-start(bf16[128,512]{1,0:T(8,128)(2,1)S(1)} %collective-permute-done.4.refs_3_), channel_id=1, source_target_pairs={{0,4},{4,8},{8,12},{12,14},{14,10},{10,6},{6,2},{2,0},{1,5},{5,9},... | collective-permute-start | bytes 393224 | tf_op jit(solution)/shard_map/ppermute | solution.py:143
  32.6 21.0 %collective-permute-start.13 = (bf16[256,512]{1,0:T(8,128)(2,1)}, bf16[256,512]{1,0:T(8,128)(2,1)}, u32[]{:S(2)}, u32[]{:S(2)}) collective-permute-start(bf16[256,512]{1,0:T(8,128)(2,1)} %pad_maximum_fusion.1), channel_id=1, source_target_pairs={{0,16},{16,0},{1,17},{17,1},{2,18},{18,2},{3,19},{19,3},{4,20},{20... | collective-permute-start | bytes 786440 | tf_op jit(solution)/shard_map/ppermute | solution.py:145
  34.5 13.5 %collective-permute-start.16 = (bf16[128,512]{1,0:T(8,128)(2,1)S(1)}, bf16[128,512]{1,0:T(8,128)(2,1)}, u32[]{:S(2)}, u32[]{:S(2)}) collective-permute-start(bf16[128,512]{1,0:T(8,128)(2,1)S(1)} %collective-permute-done.12.refs_4_), channel_id=1, source_target_pairs={{4,0},{8,4},{12,8},{14,12},{10,14},{6,10},{2,6},{0,2},{5,1},{9,5},... | collective-permute-start | bytes 393224 | tf_op jit(solution)/shard_map/ppermute | solution.py:143
  35.4 12.6 %collective-permute-start.15 = (bf16[128,512]{1,0:T(8,128)(2,1)}, bf16[128,512]{1,0:T(8,128)(2,1)}, u32[]{:S(2)}, u32[]{:S(2)}) collective-permute-start(bf16[128,512]{1,0:T(8,128)(2,1)} %collective-permute-done.11.refs_1_), channel_id=1, source_target_pairs={{0,4},{4,8},{8,12},{12,14},{14,10},{10,6},{6,2},{2,0},{1,5},{5,9},... | collective-permute-start | bytes 393224 | tf_op jit(solution)/shard_map/ppermute | solution.py:143
  36.5 14.9 %collective-permute-start.18 = (bf16[256,512]{1,0:T(8,128)(2,1)}, bf16[256,512]{1,0:T(8,128)(2,1)}, u32[]{:S(2)}, u32[]{:S(2)}) collective-permute-start(bf16[256,512]{1,0:T(8,128)(2,1)} %collective-permute-done.14.refs_3_), channel_id=1, source_target_pairs={{4,0},{8,4},{12,8},{14,12},{10,14},{6,10},{2,6},{0,2},{5,1},{9,5},... | collective-permute-start | bytes 786440 | tf_op jit(solution)/shard_map/ppermute | solution.py:142
  37.4 14.5 %collective-permute-start.7 = (bf16[256,512]{1,0:T(8,128)(2,1)}, bf16[256,512]{1,0:T(8,128)(2,1)}, u32[]{:S(2)}, u32[]{:S(2)}) collective-permute-start(bf16[256,512]{1,0:T(8,128)(2,1)} %collective-permute-done.6.refs_0_), channel_id=1, source_target_pairs={{0,4},{4,8},{8,12},{12,14},{14,10},{10,6},{6,2},{2,0},{1,5},{5,9},... | collective-permute-start | bytes 786440 | tf_op jit(solution)/shard_map/ppermute | solution.py:142
  38.6 0.9 copy-start.2
  39.6 0.9 copy-start.13
  41.4 0.9 copy-start.17
  42.3 0.9 copy-start.19
  48.9 8.5 %collective-permute-start.17 = (bf16[256,512]{1,0:T(8,128)(2,1)S(1)}, bf16[256,512]{1,0:T(8,128)(2,1)S(1)}, u32[]{:S(2)}, u32[]{:S(2)}) collective-permute-start(bf16[256,512]{1,0:T(8,128)(2,1)S(1)} %pad_maximum_fusion.2), channel_id=1, source_target_pairs={{0,16},{16,0},{1,17},{17,1},{2,18},{18,2},{3,19},{19,3},{4,20},{20... | collective-permute-start | bytes 786440 | tf_op jit(solution)/shard_map/ppermute | solution.py:145
  49.8 5.6 %collective-permute-start.25 = (bf16[128,512]{1,0:T(8,128)(2,1)}, bf16[128,512]{1,0:T(8,128)(2,1)S(1)}, u32[]{:S(2)}, u32[]{:S(2)}) collective-permute-start(bf16[128,512]{1,0:T(8,128)(2,1)} %collective-permute-done.16.refs_10_), channel_id=1, source_target_pairs={{4,0},{8,4},{12,8},{14,12},{10,14},{6,10},{2,6},{0,2},{5,1},{9,5},... | collective-permute-start | bytes 393224 | tf_op jit(solution)/shard_map/ppermute | solution.py:143
  51.4 5.6 %collective-permute-start.21 = (bf16[128,512]{1,0:T(8,128)(2,1)}, bf16[128,512]{1,0:T(8,128)(2,1)S(1)}, u32[]{:S(2)}, u32[]{:S(2)}) collective-permute-start(bf16[128,512]{1,0:T(8,128)(2,1)} %collective-permute-done.15.refs_7_), channel_id=1, source_target_pairs={{0,4},{4,8},{8,12},{12,14},{14,10},{10,6},{6,2},{2,0},{1,5},{5,9},... | collective-permute-start | bytes 393224 | tf_op jit(solution)/shard_map/ppermute | solution.py:143
  52.0 13.5 %collective-permute-start.30 = (bf16[256,512]{1,0:T(8,128)(2,1)}, bf16[256,512]{1,0:T(8,128)(2,1)}, u32[]{:S(2)}, u32[]{:S(2)}) collective-permute-start(bf16[256,512]{1,0:T(8,128)(2,1)} %collective-permute-done.18.refs_9_), channel_id=1, source_target_pairs={{4,0},{8,4},{12,8},{14,12},{10,14},{6,10},{2,6},{0,2},{5,1},{9,5},... | collective-permute-start | bytes 786440 | tf_op jit(solution)/shard_map/ppermute | solution.py:142
  53.5 13.5 %collective-permute-start.9 = (bf16[256,512]{1,0:T(8,128)(2,1)}, bf16[256,512]{1,0:T(8,128)(2,1)}, u32[]{:S(2)}, u32[]{:S(2)}) collective-permute-start(bf16[256,512]{1,0:T(8,128)(2,1)} %collective-permute-done.7.refs_6_), channel_id=1, source_target_pairs={{0,4},{4,8},{8,12},{12,14},{14,10},{10,6},{6,2},{2,0},{1,5},{5,9},... | collective-permute-start | bytes 786440 | tf_op jit(solution)/shard_map/ppermute | solution.py:142
  55.4 7.7 %collective-permute-start.26 = (bf16[128,512]{1,0:T(8,128)(2,1)S(1)}, bf16[128,512]{1,0:T(8,128)(2,1)S(1)}, u32[]{:S(2)}, u32[]{:S(2)}) collective-permute-start(bf16[128,512]{1,0:T(8,128)(2,1)S(1)} %collective-permute-done.25.refs_4_), channel_id=1, source_target_pairs={{4,0},{8,4},{12,8},{14,12},{10,14},{6,10},{2,6},{0,2},{5,1},{9,5},... | collective-permute-start | bytes 393224 | tf_op jit(solution)/shard_map/ppermute | solution.py:143
  57.0 6.4 %collective-permute-start.22 = (bf16[128,512]{1,0:T(8,128)(2,1)S(1)}, bf16[128,512]{1,0:T(8,128)(2,1)S(1)}, u32[]{:S(2)}, u32[]{:S(2)}) collective-permute-start(bf16[128,512]{1,0:T(8,128)(2,1)S(1)} %collective-permute-done.21.refs_1_), channel_id=1, source_target_pairs={{0,4},{4,8},{8,12},{12,14},{14,10},{10,6},{6,2},{2,0},{1,5},{5,9},... | collective-permute-start | bytes 393224 | tf_op jit(solution)/shard_map/ppermute | solution.py:143
  63.4 10.7 %copy-start.6 = (bf16[128,512]{1,0:T(8,128)(2,1)}, bf16[128,512]{1,0:T(8,128)(2,1)S(1)}, u32[]{:S(2)}) copy-start(bf16[128,512]{1,0:T(8,128)(2,1)S(1)} %collective-permute-done.22.refs_7_) | copy-start | bytes 393220
  63.4 5.0 %collective-permute-start.27 = (bf16[128,512]{1,0:T(8,128)(2,1)S(1)}, bf16[128,512]{1,0:T(8,128)(2,1)S(1)}, u32[]{:S(2)}, u32[]{:S(2)}) collective-permute-start(bf16[128,512]{1,0:T(8,128)(2,1)S(1)} %collective-permute-done.26.refs_10_), channel_id=1, source_target_pairs={{4,0},{8,4},{12,8},{14,12},{10,14},{6,10},{2,6},{0,2},{5,1},{9,5},... | collective-permute-start | bytes 393224 | tf_op jit(solution)/shard_map/ppermute | solution.py:143
  65.0 5.0 %collective-permute-start.23 = (bf16[128,512]{1,0:T(8,128)(2,1)S(1)}, bf16[128,512]{1,0:T(8,128)(2,1)S(1)}, u32[]{:S(2)}, u32[]{:S(2)}) collective-permute-start(bf16[128,512]{1,0:T(8,128)(2,1)S(1)} %collective-permute-done.22.refs_7_), channel_id=1, source_target_pairs={{0,4},{4,8},{8,12},{12,14},{14,10},{10,6},{6,2},{2,0},{1,5},{5,9},... | collective-permute-start | bytes 393224 | tf_op jit(solution)/shard_map/ppermute | solution.py:143
  65.4 9.9 %collective-permute-start.31 = (bf16[256,512]{1,0:T(8,128)(2,1)}, bf16[256,512]{1,0:T(8,128)(2,1)}, u32[]{:S(2)}, u32[]{:S(2)}) collective-permute-start(bf16[256,512]{1,0:T(8,128)(2,1)} %collective-permute-done.30.refs_3_), channel_id=1, source_target_pairs={{4,0},{8,4},{12,8},{14,12},{10,14},{6,10},{2,6},{0,2},{5,1},{9,5},... | collective-permute-start | bytes 786440 | tf_op jit(solution)/shard_map/ppermute | solution.py:142
  67.0 9.7 %collective-permute-start.10 = (bf16[256,512]{1,0:T(8,128)(2,1)}, bf16[256,512]{1,0:T(8,128)(2,1)}, u32[]{:S(2)}, u32[]{:S(2)}) collective-permute-start(bf16[256,512]{1,0:T(8,128)(2,1)} %collective-permute-done.9.refs_0_), channel_id=1, source_target_pairs={{0,4},{4,8},{8,12},{12,14},{14,10},{10,6},{6,2},{2,0},{1,5},{5,9},... | collective-permute-start | bytes 786440 | tf_op jit(solution)/shard_map/ppermute | solution.py:142
  68.4 1.6 %copy-start.10 = (bf16[128,512]{1,0:T(8,128)(2,1)}, bf16[128,512]{1,0:T(8,128)(2,1)S(1)}, u32[]{:S(2)}) copy-start(bf16[128,512]{1,0:T(8,128)(2,1)S(1)} %collective-permute-done.27.refs_4_) | copy-start | bytes 393220
  71.3 7.6 %collective-permute-start.28 = (bf16[256,512]{1,0:T(8,128)(2,1)}, bf16[256,512]{1,0:T(8,128)(2,1)S(1)}, u32[]{:S(2)}, u32[]{:S(2)}) collective-permute-start(bf16[256,512]{1,0:T(8,128)(2,1)} %pad_maximum_fusion.3), channel_id=1, source_target_pairs={{0,16},{16,0},{1,17},{17,1},{2,18},{18,2},{3,19},{19,3},{4,20},{20... | collective-permute-start | bytes 786440 | tf_op jit(solution)/shard_map/ppermute | solution.py:145
  72.6 9.1 %collective-permute-start.36 = (bf16[256,512]{1,0:T(8,128)(2,1)}, bf16[256,512]{1,0:T(8,128)(2,1)S(1)}, u32[]{:S(2)}, u32[]{:S(2)}) collective-permute-start(bf16[256,512]{1,0:T(8,128)(2,1)} %pad_maximum_fusion.4), channel_id=1, source_target_pairs={{0,16},{16,0},{1,17},{17,1},{2,18},{18,2},{3,19},{19,3},{4,20},{20... | collective-permute-start | bytes 786440 | tf_op jit(solution)/shard_map/ppermute | solution.py:145
  74.8 9.7 %collective-permute-start.37 = (bf16[256,512]{1,0:T(8,128)(2,1)}, bf16[256,512]{1,0:T(8,128)(2,1)S(1)}, u32[]{:S(2)}, u32[]{:S(2)}) collective-permute-start(bf16[256,512]{1,0:T(8,128)(2,1)} %pad_maximum_fusion.5), channel_id=1, source_target_pairs={{0,16},{16,0},{1,17},{17,1},{2,18},{18,2},{3,19},{19,3},{4,20},{20... | collective-permute-start | bytes 786440 | tf_op jit(solution)/shard_map/ppermute | solution.py:145
  75.3 12.5 %collective-permute-start.32 = (bf16[256,512]{1,0:T(8,128)(2,1)}, bf16[256,512]{1,0:T(8,128)(2,1)}, u32[]{:S(2)}, u32[]{:S(2)}) collective-permute-start(bf16[256,512]{1,0:T(8,128)(2,1)} %collective-permute-done.31.refs_9_), channel_id=1, source_target_pairs={{4,0},{8,4},{12,8},{14,12},{10,14},{6,10},{2,6},{0,2},{5,1},{9,5},... | collective-permute-start | bytes 786440 | tf_op jit(solution)/shard_map/ppermute | solution.py:142
  76.7 12.3 %collective-permute-start.19 = (bf16[256,512]{1,0:T(8,128)(2,1)}, bf16[256,512]{1,0:T(8,128)(2,1)}, u32[]{:S(2)}, u32[]{:S(2)}) collective-permute-start(bf16[256,512]{1,0:T(8,128)(2,1)} %collective-permute-done.10.refs_6_), channel_id=1, source_target_pairs={{0,4},{4,8},{8,12},{12,14},{14,10},{10,6},{6,2},{2,0},{1,5},{5,9},... | collective-permute-start | bytes 786440 | tf_op jit(solution)/shard_map/ppermute | solution.py:142
  78.9 7.9 %collective-permute-start.34 = (bf16[128,512]{1,0:T(8,128)(2,1)}, bf16[128,512]{1,0:T(8,128)(2,1)S(1)}, u32[]{:S(2)}, u32[]{:S(2)}) collective-permute-start(bf16[128,512]{1,0:T(8,128)(2,1)} %copy-done.10), channel_id=1, source_target_pairs={{4,0},{8,4},{12,8},{14,12},{10,14},{6,10},{2,6},{0,2},{5,1},{9,5},... | collective-permute-start | bytes 393224 | tf_op jit(solution)/shard_map/ppermute | solution.py:143
  81.7 18.2 %collective-permute-start.24 = (bf16[128,512]{1,0:T(8,128)(2,1)}, bf16[128,512]{1,0:T(8,128)(2,1)S(1)}, u32[]{:S(2)}, u32[]{:S(2)}) collective-permute-start(bf16[128,512]{1,0:T(8,128)(2,1)} %copy-done.8), channel_id=1, source_target_pairs={{0,4},{4,8},{8,12},{12,14},{14,10},{10,6},{6,2},{2,0},{1,5},{5,9},... | collective-permute-start | bytes 393224 | tf_op jit(solution)/shard_map/ppermute | solution.py:143
  84.5 15.4 %collective-permute-start.29 = (bf16[128,512]{1,0:T(8,128)(2,1)S(1)}, bf16[128,512]{1,0:T(8,128)(2,1)S(1)}, u32[]{:S(2)}, u32[]{:S(2)}) collective-permute-start(bf16[128,512]{1,0:T(8,128)(2,1)S(1)} %get-tuple-element.60), channel_id=1, source_target_pairs={{0,4},{4,8},{8,12},{12,14},{14,10},{10,6},{6,2},{2,0},{1,5},{5,9},... | collective-permute-start | bytes 393224 | tf_op jit(solution)/shard_map/ppermute | solution.py:152
  86.8 13.2 %collective-permute-start.35 = (bf16[128,512]{1,0:T(8,128)(2,1)S(1)}, bf16[128,512]{1,0:T(8,128)(2,1)S(1)}, u32[]{:S(2)}, u32[]{:S(2)}) collective-permute-start(bf16[128,512]{1,0:T(8,128)(2,1)S(1)} %get-tuple-element.59), channel_id=1, source_target_pairs={{4,0},{8,4},{12,8},{14,12},{10,14},{6,10},{2,6},{0,2},{5,1},{9,5},... | collective-permute-start | bytes 393224 | tf_op jit(solution)/shard_map/ppermute | solution.py:152
  87.9 12.1 %collective-permute-start.33 = (bf16[256,512]{1,0:T(8,128)(2,1)}, bf16[256,512]{1,0:T(8,128)(2,1)S(1)}, u32[]{:S(2)}, u32[]{:S(2)}) collective-permute-start(bf16[256,512]{1,0:T(8,128)(2,1)} %collective-permute-done.32.refs_3_), channel_id=1, source_target_pairs={{4,0},{8,4},{12,8},{14,12},{10,14},{6,10},{2,6},{0,2},{5,1},{9,5},... | collective-permute-start | bytes 786440 | tf_op jit(solution)/shard_map/ppermute | solution.py:142
  89.0 11.0 %collective-permute-start.20 = (bf16[256,512]{1,0:T(8,128)(2,1)}, bf16[256,512]{1,0:T(8,128)(2,1)S(1)}, u32[]{:S(2)}, u32[]{:S(2)}) collective-permute-start(bf16[256,512]{1,0:T(8,128)(2,1)} %collective-permute-done.19.refs_0_), channel_id=1, source_target_pairs={{0,4},{4,8},{8,12},{12,14},{14,10},{10,6},{6,2},{2,0},{1,5},{5,9},... | collective-permute-start | bytes 786440 | tf_op jit(solution)/shard_map/ppermute | solution.py:142
  90.8 5.4 %copy-start.9 = (bf16[128,512]{1,0:T(8,128)(2,1)S(1)}, bf16[128,512]{1,0:T(8,128)(2,1)}, u32[]{:S(2)}) copy-start(bf16[128,512]{1,0:T(8,128)(2,1)} %copy-done.8) | copy-start | bytes 393220
  90.8 5.4 %copy-start.11 = (bf16[128,512]{1,0:T(8,128)(2,1)S(1)}, bf16[128,512]{1,0:T(8,128)(2,1)}, u32[]{:S(2)}) copy-start(bf16[128,512]{1,0:T(8,128)(2,1)} %copy-done.10) | copy-start | bytes 393220
  100.0 4.3 %copy-start.23 = (s32[4]{0:T(128)S(1)}, s32[4]{0:T(128)}, u32[]{:S(2)}) copy-start(s32[4]{0:T(128)} %param.13) | copy-start | bytes 52
  100.0 8.2 %copy-start.3 = (bf16[512,1024]{1,0:T(8,128)(2,1)S(1)}, bf16[512,1024]{1,0:T(8,128)(2,1)}, u32[]{:S(2)}) copy-start(bf16[512,1024]{1,0:T(8,128)(2,1)} %key_up_ref.1) | copy-start | bytes 3145732
  104.2 2.9 %collective-permute-start.38 = (bf16[1024,512]{1,0:T(8,128)(2,1)}, bf16[1024,512]{1,0:T(8,128)(2,1)S(1)}, u32[]{:S(2)}, u32[]{:S(2)}) collective-permute-start(bf16[1024,512]{1,0:T(8,128)(2,1)} %get-tuple-element.50.have_ref), channel_id=1, source_target_pairs={{0,1},{1,0},{2,3},{3,2},{4,5},{5,4},{6,7},{7,6},{8,9},{9,8},{10,11... | collective-permute-start | bytes 3145736 | tf_op jit(solution)/shard_map/ppermute | solution.py:264
  107.2 1.0 copy-start.20
  108.2 1.2 copy-start.4
  109.4 1.2 copy-start.21
  110.6 5.8 %copy-start.5 = (bf16[512,1024]{1,0:T(8,128)(2,1)S(1)}, bf16[512,1024]{1,0:T(8,128)(2,1)}, u32[]{:S(2)}) copy-start(bf16[512,1024]{1,0:T(8,128)(2,1)} %value_up_ref.1) | copy-start | bytes 3145732
  117.4 13.5 %all-to-all-start = ((f32[8,72,128]{2,1,0:T(8,128)}), f32[8,72,128]{2,1,0:T(8,128)S(1)}, u32[]{:S(2)}, u32[]{:S(2)}) async-start(f32[8,72,128]{2,1,0:T(8,128)} %bitcast.25), calls=%async_computation | async-start | bytes 589824 | tf_op jit(solution)/shard_map/all_to_all | solution.py:296
  133.6 3.9 %collective-permute-start.39 = (bf16[64,128]{1,0:T(8,128)(2,1)}, bf16[64,128]{1,0:T(8,128)(2,1)S(1)}, u32[]{:S(2)}, u32[]{:S(2)}) collective-permute-start(bf16[64,128]{1,0:T(8,128)(2,1)} %shard_map.88), channel_id=1, source_target_pairs={{0,2},{2,0},{4,6},{6,4},{8,10},{10,8},{12,14},{14,12},{1,3},{3,1},... | collective-permute-start | bytes 49160 | tf_op jit(solution)/shard_map/ppermute | solution.py:300
  138.3 5.8 %collective-permute-start.40 = (bf16[128,128]{1,0:T(8,128)(2,1)S(1)}, bf16[128,128]{1,0:T(8,128)(2,1)S(1)}, u32[]{:S(2)}, u32[]{:S(2)}) collective-permute-start(bf16[128,128]{1,0:T(8,128)(2,1)S(1)} %pad_maximum_fusion.8), channel_id=1, source_target_pairs={{0,12},{2,14},{4,8},{6,10},{8,4},{10,6},{12,0},{14,2},{1,13},{3,15... | collective-permute-start | bytes 98312 | tf_op jit(solution)/shard_map/ppermute | solution.py:303
  139.6 5.3 %collective-permute-start.41 = (bf16[128,128]{1,0:T(8,128)(2,1)S(1)}, bf16[128,128]{1,0:T(8,128)(2,1)S(1)}, u32[]{:S(2)}, u32[]{:S(2)}) collective-permute-start(bf16[128,128]{1,0:T(8,128)(2,1)S(1)} %pad_maximum_fusion.8), channel_id=1, source_target_pairs={{0,8},{2,10},{4,12},{6,14},{8,0},{10,2},{12,4},{14,6},{1,9},{3,11}... | collective-permute-start | bytes 98312 | tf_op jit(solution)/shard_map/ppermute | solution.py:303
  140.9 4.2 %collective-permute-start.42 = (bf16[128,128]{1,0:T(8,128)(2,1)S(1)}, bf16[128,128]{1,0:T(8,128)(2,1)S(1)}, u32[]{:S(2)}, u32[]{:S(2)}) collective-permute-start(bf16[128,128]{1,0:T(8,128)(2,1)S(1)} %pad_maximum_fusion.8), channel_id=1, source_target_pairs={{0,4},{2,6},{4,0},{6,2},{8,12},{10,14},{12,8},{14,10},{1,5},{3,7},... | collective-permute-start | bytes 98312 | tf_op jit(solution)/shard_map/ppermute | solution.py:303
  145.3 1.4 collective-permute-start.43
  (5 other events, 3.9 us)

commit v8 on v5

--- a/solution.py
+++ b/solution.py
@@ -59,6 +59,7 @@
                 rows = pl.ds(pl.multiple_of(places_ref[len(groups) + j], tok_rows), tok_rows)
             out_ref[rows, :] = term.astype(out_ref.dtype)
 
+    tokens = pltpu.with_memory_space_constraint(tokens, pltpu.HBM)
     in_vmem = pl.BlockSpec(memory_space=pltpu.VMEM)
     in_any = pl.BlockSpec(memory_space=pl.ANY)
     sums = [] if total is None else [total]
@@ -76,14 +77,14 @@
             pltpu.SemaphoreType.DMA((2, len(groups))),
         ],
         input_output_aliases={} if total is None or last else {3 + count: 0},
-        compiler_params=pltpu.CompilerParams(vmem_limit_bytes=48 * 2**20),
+        compiler_params=pltpu.CompilerParams(vmem_limit_bytes=30 * 2**20),
         cost_estimate=pl.CostEstimate(
             flops=4 * tok_rows * deep * width, bytes_accessed=4 * tok_rows * deep, transcendentals=0
         ),
     )(places, tokens, theirs, *flat, *sums)
 
 
-def project(tokens, key_down, value_down, early):
+def project(tokens, key_down, value_down, prepare, inputs):
     chips = lax.axis_size("chip")
     chip = lax.axis_index("chip")
     core = lax.axis_index("core")
@@ -97,7 +98,7 @@
         block = jnp.concatenate([jnp.where(first, own, got), jnp.where(first, got, own)], 0)
         full = lax.all_gather(block, "chip", axis=0, tiled=True)
         mine, other = mm(tokens, full).astype(BF), mm(theirs, full).astype(BF)
-        return jnp.concatenate([jnp.where(first, mine, other), jnp.where(first, other, mine)], 0), early
+        return jnp.concatenate([jnp.where(first, mine, other), jnp.where(first, other, mine)], 0), prepare(*inputs)
     cycle = list(range(0, chips, 2)) + list(range(chips - 1, 0, -2))
     last = chips - 1
     place = jnp.where(chip & 1 == 0, chip >> 1, last - (chip >> 1))
@@ -123,7 +124,9 @@
     for step in range(1, chips):
         ready = todo
         if step == 2:
-            held[0], early = lax.optimization_barrier((held[0], early))
+            held = lax.optimization_barrier(held)
+        if step == last:
+            _, inputs = lax.optimization_barrier((held[0], inputs))
         for k in range(2 * chains):
             if mark is not None:
                 held[k], _ = lax.optimization_barrier((held[k], mark))
@@ -134,7 +137,7 @@
         else:
             total, mark = add_pieces(tokens, theirs, ready, total)
             todo = arriving
-    return add_pieces(tokens, theirs, todo, total, core)[0], early
+    return add_pieces(tokens, theirs, todo, total, core)[0], prepare(*inputs)
 
 
 def attend(have, got, core, key_up, value_up, query, bounds, chips):
@@ -147,8 +150,9 @@
     def kernel(core_ref, have_ref, got_ref, key_up_ref, value_up_ref, query_ref, bounds_ref, out_ref):
         first = core_ref[0] == 0
         have, got = have_ref[...], got_ref[...]
-        keys = mm(jnp.where(first, have, got), key_up_ref[...]).astype(BF)
-        values = mm(jnp.where(first, got, have), value_up_ref[...]).astype(BF)
+        lanes = pl.ds(pl.multiple_of(core_ref[0] * heads * DH, heads * DH), heads * DH)
+        keys = mm(jnp.where(first, have, got), key_up_ref[:, lanes]).astype(BF)
+        values = mm(jnp.where(first, got, have), value_up_ref[:, lanes]).astype(BF)
         position = lax.broadcasted_iota(jnp.int32, (tokens, rows), 0)
         visible = (position >= bounds_ref[0:1, :]) & (position < bounds_ref[1:2, :])
         tops, totals = [], []
@@ -184,7 +188,7 @@
         out_shape=jax.ShapeDtypeStruct((chips, blocks + 1, 8, DH), F32),
         in_specs=[pl.BlockSpec(memory_space=pltpu.SMEM)] + [in_vmem] * 6,
         out_specs=in_vmem,
-        compiler_params=pltpu.CompilerParams(vmem_limit_bytes=40 * 2**20),
+        compiler_params=pltpu.CompilerParams(vmem_limit_bytes=24 * 2**20),
         cost_estimate=pl.CostEstimate(
             flops=4 * tokens * (have.shape[1] * heads * DH + heads * rows * DH),
             bytes_accessed=4 * tokens * have.shape[1],
@@ -237,16 +241,29 @@
     rows = pairs * heads * group
     share = rows // chips
 
-    query = lax.dynamic_index_in_dim(
-        queries.reshape(steps_count, req_count, CORES, heads * group * DH), core, 2, keepdims=False
-    ).reshape(steps_count, req_count, heads, group, DH)
-    key_up = lax.dynamic_slice_in_dim(key_up, core * heads * DH, heads * DH, 1)
-    value_up = lax.dynamic_slice_in_dim(value_up, core * heads * DH, heads * DH, 1)
+    def by_head(queries):
+        mine = lax.dynamic_slice_in_dim(queries, core * heads * group * DH, heads * group * DH, 2)
+        return mine.reshape(steps_count, req_count, heads, group, DH).transpose(2, 0, 1, 3, 4)
+
+    have, query = project(tokens, key_down, value_down, by_head, (queries,))
+    got = lax.ppermute(have, "core", SWAP)
+
+    offsets = jnp.cumsum(prompt_lens) - prompt_lens
+    bounds = jnp.stack([offsets, offsets + prompt_lens]) - chip * CORES * tok_rows
+    bounds = jnp.broadcast_to(bounds[:, None, :, None], (2, steps_count, req_count, group)).reshape(2, -1)
+    sending = attend(have, got, core, key_up, value_up, query.reshape(heads, -1, DH), bounds, chips)
+
+    sending, query, new_latent = lax.optimization_barrier((sending, query, new_latent))
     flat_new = new_latent.reshape(pairs, 2 * lat_width)
-    new_keys = mm(flat_new[:, :lat_width], key_up).astype(BF).reshape(steps_count, req_count, heads, DH)
-    new_values = mm(flat_new[:, lat_width:], value_up).astype(BF).reshape(steps_count, req_count, heads, DH)
+
+    def my_heads(latent, up):
+        full = lax.dynamic_slice_in_dim(mm(latent, up), core * heads * DH, heads * DH, 1)
+        return full.astype(BF).reshape(steps_count, req_count, heads, DH)
+
+    new_keys = my_heads(flat_new[:, :lat_width], key_up)
+    new_values = my_heads(flat_new[:, lat_width:], value_up)
     causal = (jnp.arange(steps_count)[:, None] >= jnp.arange(steps_count)[None, :])[:, None, None, None, :]
-    fresh = jnp.einsum("srgjd,urgd->srgju", query, new_keys, preferred_element_type=F32) * scale
+    fresh = jnp.einsum("gsrjd,urgd->srgju", query, new_keys, preferred_element_type=F32) * scale
     fresh = jnp.where(causal, fresh, -1e30)
     fresh_top = jnp.max(fresh, -1)
     fresh_weights = jnp.where(causal, jnp.exp(fresh - fresh_top[..., None]), 0.0)
@@ -260,18 +277,8 @@
     fresh_stats = [my_share(x.reshape(rows)).reshape(-1, group).T for x in (fresh_top, fresh_total)]
     fresh_stats = jnp.pad(jnp.concatenate(fresh_stats, 1), ((0, 0), (0, DH - 2 * share // group)))
 
-    offsets = jnp.cumsum(prompt_lens) - prompt_lens
-    bounds = jnp.stack([offsets, offsets + prompt_lens]) - chip * CORES * tok_rows
-    bounds = jnp.broadcast_to(bounds[:, None, :, None], (2, steps_count, req_count, group)).reshape(2, -1)
-    by_head = query.transpose(2, 0, 1, 3, 4).reshape(heads, pairs * group, DH)
-
-    early = (by_head, bounds, key_up, value_up, fresh_stats, fresh_summed)
-    have, early = project(tokens, key_down, value_down, early)
-    by_head, bounds, key_up, value_up, fresh_stats, fresh_summed = early
-    got = lax.ppermute(have, "core", SWAP)
-    sending = attend(have, got, core, key_up, value_up, by_head, bounds, chips)
-
-    arrived = lax.all_to_all(sending, "chip", split_axis=0, concat_axis=0, tiled=True)
+    flat = sending.reshape(chips, -1, DH)
+    arrived = lax.all_to_all(flat, "chip", split_axis=0, concat_axis=0, tiled=True).reshape(sending.shape)
     result = merge(arrived, fresh_stats, fresh_summed)
 
     if chips == 8:

time: 139 us -> 144 us (1.036)
  blocking collectives: 15.4 us -> 0 us
  waiting for transfers between devices: 41.3 us -> 50.2 us
  starting transfers between devices: 34.9 us -> 41.1 us
  Pallas kernels: 32.6 us -> 35.6 us
  local copies, waits for them, and re-layouts: 8.91 us -> 10.5 us
    all_to_all x1 -> x0, blocking collectives: 15.4 us -> none  [on_device(): lax.all_to_all(sending, 'chip', split_axis=0, concat_axis=0, tiled=True)]
    all_to_all x0 -> x1, waiting for transfers between devices: none -> 7.41 us  [on_device(): lax.all_to_all(flat, 'chip', split_axis=0, concat_axis=0, tiled=True)]
    all_to_all x0 -> x1, starting transfers between devices: none -> 4.83 us  [on_device(): lax.all_to_all(flat, 'chip', split_axis=0, concat_axis=0, tiled=True)]
    unnamed x18 -> x26, local copies, waits for them, and re-layouts: 3.55 us -> 7.49 us
    ppermute x28, waiting for transfers between devices: 29.1 us -> 32.9 us  [project(): held[k] = lax.ppermute(held[k], 'chip', ways[k])]
    dynamic_slice x2 -> x1, local copies, waits for them, and re-layouts: 2.09 us -> 0.06 us  [by_head(): lax.dynamic_slice_in_dim(queries, core * heads * group * DH, heads * grou...]
    pallas_call x1, Pallas kernels: 2.74 us -> 4.73 us  [attend(): pl.pallas_call(kernel, out_shape=jax.ShapeDtypeStruct((chips, blocks + 1,...]
  transfers between devices with their start and end apart: 36 -> 37, of which waited for: 25 -> 19; matrix products, arithmetic and copies ran while one was open for 5% -> 3% of each run, Pallas kernels for 17% -> 17%
where the time goes in v8:
time: 144 us; the launch traced here: 143 us
  waiting for transfers between devices  50.2 us (35%)
  starting transfers between devices  41.1 us (29%)
  Pallas kernels  35.6 us (25%)
  local copies, waits for them, and re-layouts  10.5 us (7%)
  other arithmetic  3.72 us (3%)
  matrix products  1.51 us (1%)
    ppermute x28, waiting for transfers between devices, project(): held[k] = lax.ppermute(held[k], 'chip', ways[k])  32.9 us
    ppermute x28, starting transfers between devices, project(): held[k] = lax.ppermute(held[k], 'chip', ways[k])  29.3 us
    pallas_call x7, Pallas kernels, add_pieces(): pl.pallas_call(kernel, out_shape=(jax.ShapeDtypeStruct((2 * tok_rows, wid...  28.9 us
    unnamed x26, local copies, waits for them, and re-layouts  7.49 us
    all_to_all x1, waiting for transfers between devices, on_device(): lax.all_to_all(flat, 'chip', split_axis=0, concat_axis=0, tiled=True)  7.41 us
    all_to_all x1, starting transfers between devices, on_device(): lax.all_to_all(flat, 'chip', split_axis=0, concat_axis=0, tiled=True)  4.83 us
    pallas_call x1, Pallas kernels, attend(): pl.pallas_call(kernel, out_shape=jax.ShapeDtypeStruct((chips, blocks + 1,...  4.73 us
    ppermute x3, starting transfers between devices, on_device(): lax.ppermute(couple, 'chip', [(c, c ^ 2 * d) for c in range(chips)])  4.45 us
  transfers between devices with their start and end apart: 37, of which 19 were waited for; matrix products, arithmetic and copies ran while one was open for 3% of the time, Pallas kernels for 17%

profile of v8, /device:TPU:0, one launch (start us, length us, event | category | flops | bytes accessed | tf_op | source)
XLA Modules:
  0.0 143.0 jit_solution(13907367951333950424)
XLA Ops:
  0.0 1.3 broadcast_select_fusion
  1.3 0.5 collective-permute-start
  1.8 1.5 %collective-permute-done.refs_1_ = bf16[512,512]{1,0:T(8,128)(2,1)S(1)} collective-permute-done((bf16[512,512]{1,0:T(8,128)(2,1)S(1)}, bf16[512,512]{1,0:T(8,128)(2,1)S(1)}, u32[]{:S(2)}, u32[]{:S(2)}) %collective-permute-start) | collective-permute-done | bytes 524320 | tf_op jit(solution)/shard_map/ppermute | solution.py:95
  3.8 2.8 %collective-permute-start.2 = (bf16[256,512]{1,0:T(8,128)(2,1)S(1)}, bf16[256,512]{1,0:T(8,128)(2,1)}, u32[]{:S(2)}, u32[]{:S(2)}) collective-permute-start(bf16[256,512]{1,0:T(8,128)(2,1)S(1)} %get-tuple-element.94), channel_id=1, source_target_pairs={{0,4},{4,8},{8,12},{12,14},{14,10},{10,6},{6,2},{2,0},{1,5},{5,9},... | collective-permute-start | bytes 786440 | tf_op jit(solution)/shard_map/ppermute | solution.py:133
  6.6 1.6 %collective-permute-start.3 = (bf16[256,512]{1,0:T(8,128)(2,1)S(1)}, bf16[256,512]{1,0:T(8,128)(2,1)}, u32[]{:S(2)}, u32[]{:S(2)}) collective-permute-start(bf16[256,512]{1,0:T(8,128)(2,1)S(1)} %get-tuple-element.93), channel_id=1, source_target_pairs={{0,4},{4,8},{8,12},{12,14},{14,10},{10,6},{6,2},{2,0},{1,5},{5,9},... | collective-permute-start | bytes 786440 | tf_op jit(solution)/shard_map/ppermute | solution.py:133
  8.7 5.0 %collective-permute-done.2.refs_2_ = bf16[256,512]{1,0:T(8,128)(2,1)} collective-permute-done((bf16[256,512]{1,0:T(8,128)(2,1)S(1)}, bf16[256,512]{1,0:T(8,128)(2,1)}, u32[]{:S(2)}, u32[]{:S(2)}) %collective-permute-start.2) | collective-permute-done | bytes 262176 | tf_op jit(solution)/shard_map/ppermute | solution.py:133
  13.8 5.3 %collective-permute-done.3.refs_3_ = bf16[256,512]{1,0:T(8,128)(2,1)} collective-permute-done((bf16[256,512]{1,0:T(8,128)(2,1)S(1)}, bf16[256,512]{1,0:T(8,128)(2,1)}, u32[]{:S(2)}, u32[]{:S(2)}) %collective-permute-start.3) | collective-permute-done | bytes 262176 | tf_op jit(solution)/shard_map/ppermute | solution.py:133
  19.1 2.9 %collective-permute-done.5.refs_5_ = bf16[256,512]{1,0:T(8,128)(2,1)} collective-permute-done((bf16[256,512]{1,0:T(8,128)(2,1)S(1)}, bf16[256,512]{1,0:T(8,128)(2,1)}, u32[]{:S(2)}, u32[]{:S(2)}) %collective-permute-start.5) | collective-permute-done | bytes 262176 | tf_op jit(solution)/shard_map/ppermute | solution.py:133
  22.4 1.6 %collective-permute-start.6 = (bf16[256,512]{1,0:T(8,128)(2,1)}, bf16[256,512]{1,0:T(8,128)(2,1)}, u32[]{:S(2)}, u32[]{:S(2)}) collective-permute-start(bf16[256,512]{1,0:T(8,128)(2,1)} %collective-permute-done.2.refs_2_), channel_id=1, source_target_pairs={{0,4},{4,8},{8,12},{12,14},{14,10},{10,6},{6,2},{2,0},{1,5},{5,9},... | collective-permute-start | bytes 786440 | tf_op jit(solution)/shard_map/ppermute | solution.py:133
  24.0 1.6 %collective-permute-start.8 = (bf16[256,512]{1,0:T(8,128)(2,1)}, bf16[256,512]{1,0:T(8,128)(2,1)}, u32[]{:S(2)}, u32[]{:S(2)}) collective-permute-start(bf16[256,512]{1,0:T(8,128)(2,1)} %collective-permute-done.3.refs_3_), channel_id=1, source_target_pairs={{0,4},{4,8},{8,12},{12,14},{14,10},{10,6},{6,2},{2,0},{1,5},{5,9},... | collective-permute-start | bytes 786440 | tf_op jit(solution)/shard_map/ppermute | solution.py:133
  26.1 5.3 %shard_map.82 = (f32[1024,512]{1,0:T(8,128)S(1)}, f32[8,128]{1,0:T(8,128)}) custom-call(s32[4]{0:T(128)S(1)} %pad_add_fusion.1.places_ref, bf16[512,8192]{1,0:T(8,128)(2,1)} %mine_ref.13, bf16[512,8192]{1,0:T(8,128)(2,1)} %collective-permute-done.1.theirs_ref, bf16[512,512]{1,0:T(8,128)(2,1)S(1)} %get-tuple-element.89.refs_0_, ...), custom_call_target="tpu_custom_call" | custom-call | flops 2147483648 | bytes 4194304 | tf_op jit(solution)/shard_map/pallas_call | solution.py:66
  32.0 5.2 %collective-permute-done.9.refs_2_ = bf16[256,512]{1,0:T(8,128)(2,1)} collective-permute-done((bf16[256,512]{1,0:T(8,128)(2,1)}, bf16[256,512]{1,0:T(8,128)(2,1)}, u32[]{:S(2)}, u32[]{:S(2)}) %collective-permute-start.9) | collective-permute-done | bytes 262176 | tf_op jit(solution)/shard_map/ppermute | solution.py:133
  37.6 1.6 %collective-permute-start.12 = (bf16[256,512]{1,0:T(8,128)(2,1)}, bf16[256,512]{1,0:T(8,128)(2,1)}, u32[]{:S(2)}, u32[]{:S(2)}) collective-permute-start(bf16[256,512]{1,0:T(8,128)(2,1)} %collective-permute-done.8.refs_1_), channel_id=1, source_target_pairs={{0,4},{4,8},{8,12},{12,14},{14,10},{10,6},{6,2},{2,0},{1,5},{5,9},... | collective-permute-start | bytes 786440 | tf_op jit(solution)/shard_map/ppermute | solution.py:133
  39.2 1.6 %collective-permute-start.7 = (bf16[256,512]{1,0:T(8,128)(2,1)}, bf16[256,512]{1,0:T(8,128)(2,1)}, u32[]{:S(2)}, u32[]{:S(2)}) collective-permute-start(bf16[256,512]{1,0:T(8,128)(2,1)} %collective-permute-done.6.refs_0_), channel_id=1, source_target_pairs={{0,4},{4,8},{8,12},{12,14},{14,10},{10,6},{6,2},{2,0},{1,5},{5,9},... | collective-permute-start | bytes 786440 | tf_op jit(solution)/shard_map/ppermute | solution.py:133
  40.8 3.9 %shard_map.83 = (f32[1024,512]{1,0:T(8,128)S(1)}, f32[8,128]{1,0:T(8,128)}) custom-call(s32[2]{0:T(128)S(1)} %pad_add_fusion.2.places_ref, bf16[512,8192]{1,0:T(8,128)(2,1)} %mine_ref.13, bf16[512,8192]{1,0:T(8,128)(2,1)} %collective-permute-done.1.theirs_ref, bf16[256,512]{1,0:T(8,128)(2,1)} %collective-permute-done.6.refs_0_, ...), custom_call_target="tpu_custom_call", output_to_operand_aliasing={{0}: (7, {})} | custom-call | flops 1073741824 | bytes 2097152 | tf_op jit(solution)/shard_map/pallas_call | solution.py:66
  44.7 0.5 collective-permute-start.18
  45.2 3.1 %collective-permute-done.13.refs_2_ = bf16[256,512]{1,0:T(8,128)(2,1)S(1)} collective-permute-done((bf16[256,512]{1,0:T(8,128)(2,1)}, bf16[256,512]{1,0:T(8,128)(2,1)S(1)}, u32[]{:S(2)}, u32[]{:S(2)}) %collective-permute-start.13) | collective-permute-done | bytes 262176 | tf_op jit(solution)/shard_map/ppermute | solution.py:133
  48.7 1.6 %collective-permute-start.16 = (bf16[256,512]{1,0:T(8,128)(2,1)}, bf16[256,512]{1,0:T(8,128)(2,1)}, u32[]{:S(2)}, u32[]{:S(2)}) collective-permute-start(bf16[256,512]{1,0:T(8,128)(2,1)} %collective-permute-done.12.refs_1_), channel_id=1, source_target_pairs={{0,4},{4,8},{8,12},{12,14},{14,10},{10,6},{6,2},{2,0},{1,5},{5,9},... | collective-permute-start | bytes 786440 | tf_op jit(solution)/shard_map/ppermute | solution.py:133
  50.3 1.6 %collective-permute-start.11 = (bf16[256,512]{1,0:T(8,128)(2,1)}, bf16[256,512]{1,0:T(8,128)(2,1)}, u32[]{:S(2)}, u32[]{:S(2)}) collective-permute-start(bf16[256,512]{1,0:T(8,128)(2,1)} %collective-permute-done.7.refs_0_), channel_id=1, source_target_pairs={{0,4},{4,8},{8,12},{12,14},{14,10},{10,6},{6,2},{2,0},{1,5},{5,9},... | collective-permute-start | bytes 786440 | tf_op jit(solution)/shard_map/ppermute | solution.py:133
  52.0 3.7 %shard_map.84 = (f32[1024,512]{1,0:T(8,128)S(1)}, f32[8,128]{1,0:T(8,128)}) custom-call(s32[2]{0:T(128)S(1)} %pad_add_fusion.3.places_ref, bf16[512,8192]{1,0:T(8,128)(2,1)} %mine_ref.13, bf16[512,8192]{1,0:T(8,128)(2,1)} %collective-permute-done.1.theirs_ref, bf16[256,512]{1,0:T(8,128)(2,1)} %collective-permute-done.7.refs_0_, ...), custom_call_target="tpu_custom_call", output_to_operand_aliasing={{0}: (7, {})} | custom-call | flops 1073741824 | bytes 2097152 | tf_op jit(solution)/shard_map/pallas_call | solution.py:66
  55.7 0.5 collective-permute-start.22
  56.2 3.5 %collective-permute-done.17.refs_2_ = bf16[256,512]{1,0:T(8,128)(2,1)} collective-permute-done((bf16[256,512]{1,0:T(8,128)(2,1)S(1)}, bf16[256,512]{1,0:T(8,128)(2,1)}, u32[]{:S(2)}, u32[]{:S(2)}) %collective-permute-start.17) | collective-permute-done | bytes 262176 | tf_op jit(solution)/shard_map/ppermute | solution.py:133
  60.2 1.6 %collective-permute-start.20 = (bf16[256,512]{1,0:T(8,128)(2,1)}, bf16[256,512]{1,0:T(8,128)(2,1)}, u32[]{:S(2)}, u32[]{:S(2)}) collective-permute-start(bf16[256,512]{1,0:T(8,128)(2,1)} %collective-permute-done.16.refs_1_), channel_id=1, source_target_pairs={{0,4},{4,8},{8,12},{12,14},{14,10},{10,6},{6,2},{2,0},{1,5},{5,9},... | collective-permute-start | bytes 786440 | tf_op jit(solution)/shard_map/ppermute | solution.py:133
  61.8 1.5 %collective-permute-start.15 = (bf16[256,512]{1,0:T(8,128)(2,1)}, bf16[256,512]{1,0:T(8,128)(2,1)}, u32[]{:S(2)}, u32[]{:S(2)}) collective-permute-start(bf16[256,512]{1,0:T(8,128)(2,1)} %collective-permute-done.11.refs_0_), channel_id=1, source_target_pairs={{0,4},{4,8},{8,12},{12,14},{14,10},{10,6},{6,2},{2,0},{1,5},{5,9},... | collective-permute-start | bytes 786440 | tf_op jit(solution)/shard_map/ppermute | solution.py:133
  63.4 3.9 %shard_map.85 = (f32[1024,512]{1,0:T(8,128)S(1)}, f32[8,128]{1,0:T(8,128)}) custom-call(s32[2]{0:T(128)S(1)} %pad_add_fusion.4.places_ref, bf16[512,8192]{1,0:T(8,128)(2,1)} %mine_ref.13, bf16[512,8192]{1,0:T(8,128)(2,1)} %collective-permute-done.1.theirs_ref, bf16[256,512]{1,0:T(8,128)(2,1)} %collective-permute-done.11.refs_0_, ...), custom_call_target="tpu_custom_call", output_to_operand_aliasing={{0}: (7, {})} | custom-call | flops 1073741824 | bytes 2097152 | tf_op jit(solution)/shard_map/pallas_call | solution.py:66
  67.2 0.6 collective-permute-start.28
  67.8 3.1 %collective-permute-done.21.refs_2_ = bf16[256,512]{1,0:T(8,128)(2,1)S(1)} collective-permute-done((bf16[256,512]{1,0:T(8,128)(2,1)}, bf16[256,512]{1,0:T(8,128)(2,1)S(1)}, u32[]{:S(2)}, u32[]{:S(2)}) %collective-permute-start.21) | collective-permute-done | bytes 262176 | tf_op jit(solution)/shard_map/ppermute | solution.py:133
  71.3 1.6 %collective-permute-start.24 = (bf16[256,512]{1,0:T(8,128)(2,1)}, bf16[256,512]{1,0:T(8,128)(2,1)}, u32[]{:S(2)}, u32[]{:S(2)}) collective-permute-start(bf16[256,512]{1,0:T(8,128)(2,1)} %collective-permute-done.20.refs_1_), channel_id=1, source_target_pairs={{0,4},{4,8},{8,12},{12,14},{14,10},{10,6},{6,2},{2,0},{1,5},{5,9},... | collective-permute-start | bytes 786440 | tf_op jit(solution)/shard_map/ppermute | solution.py:133
  72.9 1.5 %collective-permute-start.19 = (bf16[256,512]{1,0:T(8,128)(2,1)}, bf16[256,512]{1,0:T(8,128)(2,1)}, u32[]{:S(2)}, u32[]{:S(2)}) collective-permute-start(bf16[256,512]{1,0:T(8,128)(2,1)} %collective-permute-done.15.refs_0_), channel_id=1, source_target_pairs={{0,4},{4,8},{8,12},{12,14},{14,10},{10,6},{6,2},{2,0},{1,5},{5,9},... | collective-permute-start | bytes 786440 | tf_op jit(solution)/shard_map/ppermute | solution.py:133
  74.5 3.7 %shard_map.86 = (f32[1024,512]{1,0:T(8,128)S(1)}, f32[8,128]{1,0:T(8,128)}) custom-call(s32[2]{0:T(128)S(1)} %pad_add_fusion.5.places_ref, bf16[512,8192]{1,0:T(8,128)(2,1)} %mine_ref.13, bf16[512,8192]{1,0:T(8,128)(2,1)} %collective-permute-done.1.theirs_ref, bf16[256,512]{1,0:T(8,128)(2,1)} %collective-permute-done.15.refs_0_, ...), custom_call_target="tpu_custom_call", output_to_operand_aliasing={{0}: (7, {})} | custom-call | flops 1073741824 | bytes 2097152 | tf_op jit(solution)/shard_map/pallas_call | solution.py:66
  78.2 0.6 collective-permute-start.29
  78.8 3.4 %collective-permute-done.26.refs_2_ = bf16[256,512]{1,0:T(8,128)(2,1)S(1)} collective-permute-done((bf16[256,512]{1,0:T(8,128)(2,1)S(1)}, bf16[256,512]{1,0:T(8,128)(2,1)S(1)}, u32[]{:S(2)}, u32[]{:S(2)}) %collective-permute-start.26) | collective-permute-done | bytes 262176 | tf_op jit(solution)/shard_map/ppermute | solution.py:133
  82.2 0.5 collective-permute-start.27
  82.7 1.5 %collective-permute-start.25 = (bf16[256,512]{1,0:T(8,128)(2,1)}, bf16[256,512]{1,0:T(8,128)(2,1)}, u32[]{:S(2)}, u32[]{:S(2)}) collective-permute-start(bf16[256,512]{1,0:T(8,128)(2,1)} %collective-permute-done.24.refs_1_), channel_id=1, source_target_pairs={{0,4},{4,8},{8,12},{12,14},{14,10},{10,6},{6,2},{2,0},{1,5},{5,9},... | collective-permute-start | bytes 786440 | tf_op jit(solution)/shard_map/ppermute | solution.py:133
  84.2 1.5 %collective-permute-start.23 = (bf16[256,512]{1,0:T(8,128)(2,1)}, bf16[256,512]{1,0:T(8,128)(2,1)}, u32[]{:S(2)}, u32[]{:S(2)}) collective-permute-start(bf16[256,512]{1,0:T(8,128)(2,1)} %collective-permute-done.19.refs_0_), channel_id=1, source_target_pairs={{0,4},{4,8},{8,12},{12,14},{14,10},{10,6},{6,2},{2,0},{1,5},{5,9},... | collective-permute-start | bytes 786440 | tf_op jit(solution)/shard_map/ppermute | solution.py:133
  85.8 3.7 %shard_map.87 = (f32[1024,512]{1,0:T(8,128)S(1)}, f32[8,128]{1,0:T(8,128)}) custom-call(s32[2]{0:T(128)S(1)} %pad_add_fusion.6.places_ref, bf16[512,8192]{1,0:T(8,128)(2,1)} %mine_ref.13, bf16[512,8192]{1,0:T(8,128)(2,1)} %collective-permute-done.1.theirs_ref, bf16[256,512]{1,0:T(8,128)(2,1)} %collective-permute-done.19.refs_0_, ...), custom_call_target="tpu_custom_call", output_to_operand_aliasing={{0}: (7, {})} | custom-call | flops 1073741824 | bytes 2097152 | tf_op jit(solution)/shard_map/pallas_call | solution.py:66
  89.5 0.7 copy-done.4
  90.2 0.9 collective-permute-done.27.refs_2_
  91.1 0.7 copy-done.6
  92.3 0.9 copy-done.5
  93.2 0.9 copy-done.7
  94.2 4.7 %shard_map.88 = (bf16[1024,512]{1,0:T(8,128)(2,1)}, f32[8,128]{1,0:T(8,128)}) custom-call(s32[4]{0:T(128)S(1)} %pad_add_fusion.places_ref, bf16[512,8192]{1,0:T(8,128)(2,1)} %mine_ref.13, bf16[512,8192]{1,0:T(8,128)(2,1)} %collective-permute-done.1.theirs_ref, bf16[256,512]{1,0:T(8,128)(2,1)} %collective-permute-done.23.refs_0_, ...), custom_call_target="tpu_custom_call" | custom-call | flops 1073741824 | bytes 2097152 | tf_op jit(solution)/shard_map/pallas_call | solution.py:66
  99.7 2.2 %collective-permute-done.30.got_ref = bf16[1024,512]{1,0:T(8,128)(2,1)S(1)} collective-permute-done((bf16[1024,512]{1,0:T(8,128)(2,1)}, bf16[1024,512]{1,0:T(8,128)(2,1)S(1)}, u32[]{:S(2)}, u32[]{:S(2)}) %collective-permute-start.30) | collective-permute-done | bytes 1048608 | tf_op jit(solution)/shard_map/ppermute | solution.py:249
  101.9 1.0 copy-done.8
  102.9 1.2 copy-done.2
  104.1 1.2 copy-done.9
  105.4 4.7 %shard_map.89 = f32[8,9,8,128]{3,2,1,0:T(8,128)} custom-call(s32[1]{0:T(128)} %bitcast.core_ref, bf16[1024,512]{1,0:T(8,128)(2,1)} %get-tuple-element.84.have_ref, bf16[1024,512]{1,0:T(8,128)(2,1)S(1)} %copy-done.9, bf16[512,1024]{1,0:T(8,128)(2,1)S(1)} %copy-done.1, bf16[512,1024]{1,0:T(8,128)(2,1)S(1)} %copy-done.2, bf16[4,128,128]{2,1,0:T(8,128)(2,1)S(1)} %bitcast.44, ...), custom_call_target="tpu_custom_call" | custom-call | flops 1342177280 | bytes 2097152 | tf_op jit(solution)/shard_map/pallas_call | solution.py:186
  110.6 0.7 fusion.19
  111.4 4.8 %all-to-all-start = ((f32[8,72,128]{2,1,0:T(8,128)}), f32[8,72,128]{2,1,0:T(8,128)S(1)}, u32[]{:S(2)}, u32[]{:S(2)}) async-start(f32[8,72,128]{2,1,0:T(8,128)} %bitcast.25), calls=%async_computation | async-start | bytes 589824 | tf_op jit(solution)/shard_map/all_to_all | solution.py:281
  117.4 0.7 select_maximum_fusion.stats_ref
  118.1 0.6 constant_dynamic-slice_fusion.summed_ref
  118.7 7.4 %all-to-all-done = f32[8,72,128]{2,1,0:T(8,128)S(1)} async-done(((f32[8,72,128]{2,1,0:T(8,128)}), f32[8,72,128]{2,1,0:T(8,128)S(1)}, u32[]{:S(2)}, u32[]{:S(2)}) %all-to-all-start) | async-done | bytes 294944 | tf_op jit(solution)/shard_map/all_to_all | solution.py:281
  126.1 0.7 copy-done.10
  126.8 1.9 %shard_map.90 = bf16[64,128]{1,0:T(8,128)(2,1)} custom-call(f32[8,9,8,128]{3,2,1,0:T(8,128)} %bitcast.45, f32[8,128]{1,0:T(8,128)} %select_maximum_fusion.stats_ref, f32[64,128]{1,0:T(8,128)} %constant_dynamic-slice_fusion.summed_ref), custom_call_target="tpu_custom_call" | custom-call | flops 131072 | bytes 294912 | tf_op jit(solution)/shard_map/pallas_call | solution.py:218
  128.7 1.5 %collective-permute-start.31 = (bf16[64,128]{1,0:T(8,128)(2,1)}, bf16[64,128]{1,0:T(8,128)(2,1)S(1)}, u32[]{:S(2)}, u32[]{:S(2)}) collective-permute-start(bf16[64,128]{1,0:T(8,128)(2,1)} %shard_map.90), channel_id=1, source_target_pairs={{0,2},{2,0},{4,6},{6,4},{8,10},{10,8},{12,14},{14,12},{1,3},{3,1},... | collective-permute-start | bytes 49160 | tf_op jit(solution)/shard_map/ppermute | solution.py:285
  130.2 2.5 %collective-permute-done.31 = bf16[64,128]{1,0:T(8,128)(2,1)S(1)} collective-permute-done((bf16[64,128]{1,0:T(8,128)(2,1)}, bf16[64,128]{1,0:T(8,128)(2,1)S(1)}, u32[]{:S(2)}, u32[]{:S(2)}) %collective-permute-start.31) | collective-permute-done | bytes 16416 | tf_op jit(solution)/shard_map/ppermute | solution.py:285
  132.7 0.7 broadcast_select_fusion.13
  133.4 1.2 collective-permute-start.32
  134.7 1.3 collective-permute-start.33
  136.0 1.9 %collective-permute-start.34 = (bf16[128,128]{1,0:T(8,128)(2,1)S(1)}, bf16[128,128]{1,0:T(8,128)(2,1)S(1)}, u32[]{:S(2)}, u32[]{:S(2)}) collective-permute-start(bf16[128,128]{1,0:T(8,128)(2,1)S(1)} %pad_maximum_fusion.2), channel_id=1, source_target_pairs={{0,4},{2,6},{4,0},{6,2},{8,12},{10,14},{12,8},{14,10},{1,5},{3,7},... | collective-permute-start | bytes 98312 | tf_op jit(solution)/shard_map/ppermute | solution.py:288
  137.9 1.3 collective-permute-done.32
  139.2 0.8 collective-permute-done.33
  140.5 1.3 collective-permute-done.35
  142.1 0.9 reshape.98
  (95 shorter events, 8.5 us)
Async XLA Ops:
  0.0 99.4 %copy-start = (bf16[4,4,8192]{2,1,0:T(4,128)(2,1)S(1)}, bf16[4,4,8192]{2,1,0:T(4,128)(2,1)}, u32[]{:S(2)}) copy-start(bf16[4,4,8192]{2,1,0:T(4,128)(2,1)} %param.14) | copy-start | bytes 786436
  1.3 2.1 %collective-permute-start = (bf16[512,512]{1,0:T(8,128)(2,1)S(1)}, bf16[512,512]{1,0:T(8,128)(2,1)S(1)}, u32[]{:S(2)}, u32[]{:S(2)}) collective-permute-start(bf16[512,512]{1,0:T(8,128)(2,1)S(1)} %get-tuple-element.90), channel_id=1, source_target_pairs={{0,1},{1,0},{2,3},{3,2},{4,5},{5,4},{6,7},{7,6},{8,9},{9,8},{10,11... | collective-permute-start | bytes 1572872 | tf_op jit(solution)/shard_map/ppermute | solution.py:95
  3.4 22.7 %collective-permute-start.1 = (bf16[512,8192]{1,0:T(8,128)(2,1)}, bf16[512,8192]{1,0:T(8,128)(2,1)}, u32[]{:S(2)}, u32[]{:S(2)}) collective-permute-start(bf16[512,8192]{1,0:T(8,128)(2,1)} %mine_ref.13), channel_id=1, source_target_pairs={{0,1},{1,0},{2,3},{3,2},{4,5},{5,4},{6,7},{7,6},{8,9},{9,8},{10,11... | collective-permute-start | bytes 25165832 | tf_op jit(solution)/shard_map/ppermute | solution.py:120
  3.8 10.0 %collective-permute-start.2 = (bf16[256,512]{1,0:T(8,128)(2,1)S(1)}, bf16[256,512]{1,0:T(8,128)(2,1)}, u32[]{:S(2)}, u32[]{:S(2)}) collective-permute-start(bf16[256,512]{1,0:T(8,128)(2,1)S(1)} %get-tuple-element.94), channel_id=1, source_target_pairs={{0,4},{4,8},{8,12},{12,14},{14,10},{10,6},{6,2},{2,0},{1,5},{5,9},... | collective-permute-start | bytes 786440 | tf_op jit(solution)/shard_map/ppermute | solution.py:133
  6.6 12.5 %collective-permute-start.3 = (bf16[256,512]{1,0:T(8,128)(2,1)S(1)}, bf16[256,512]{1,0:T(8,128)(2,1)}, u32[]{:S(2)}, u32[]{:S(2)}) collective-permute-start(bf16[256,512]{1,0:T(8,128)(2,1)S(1)} %get-tuple-element.93), channel_id=1, source_target_pairs={{0,4},{4,8},{8,12},{12,14},{14,10},{10,6},{6,2},{2,0},{1,5},{5,9},... | collective-permute-start | bytes 786440 | tf_op jit(solution)/shard_map/ppermute | solution.py:133
  8.2 10.9 %collective-permute-start.4 = (bf16[256,512]{1,0:T(8,128)(2,1)S(1)}, bf16[256,512]{1,0:T(8,128)(2,1)}, u32[]{:S(2)}, u32[]{:S(2)}) collective-permute-start(bf16[256,512]{1,0:T(8,128)(2,1)S(1)} %get-tuple-element.92), channel_id=1, source_target_pairs={{4,0},{8,4},{12,8},{14,12},{10,14},{6,10},{2,6},{0,2},{5,1},{9,5},... | collective-permute-start | bytes 786440 | tf_op jit(solution)/shard_map/ppermute | solution.py:133
  8.7 13.3 %collective-permute-start.5 = (bf16[256,512]{1,0:T(8,128)(2,1)S(1)}, bf16[256,512]{1,0:T(8,128)(2,1)}, u32[]{:S(2)}, u32[]{:S(2)}) collective-permute-start(bf16[256,512]{1,0:T(8,128)(2,1)S(1)} %get-tuple-element.91), channel_id=1, source_target_pairs={{4,0},{8,4},{12,8},{14,12},{10,14},{6,10},{2,6},{0,2},{5,1},{9,5},... | collective-permute-start | bytes 786440 | tf_op jit(solution)/shard_map/ppermute | solution.py:133
  22.0 9.6 %collective-permute-start.10 = (bf16[256,512]{1,0:T(8,128)(2,1)}, bf16[256,512]{1,0:T(8,128)(2,1)}, u32[]{:S(2)}, u32[]{:S(2)}) collective-permute-start(bf16[256,512]{1,0:T(8,128)(2,1)} %collective-permute-done.5.refs_5_), channel_id=1, source_target_pairs={{4,0},{8,4},{12,8},{14,12},{10,14},{6,10},{2,6},{0,2},{5,1},{9,5},... | collective-permute-start | bytes 786440 | tf_op jit(solution)/shard_map/ppermute | solution.py:133
  22.4 16.8 %collective-permute-start.6 = (bf16[256,512]{1,0:T(8,128)(2,1)}, bf16[256,512]{1,0:T(8,128)(2,1)}, u32[]{:S(2)}, u32[]{:S(2)}) collective-permute-start(bf16[256,512]{1,0:T(8,128)(2,1)} %collective-permute-done.2.refs_2_), channel_id=1, source_target_pairs={{0,4},{4,8},{8,12},{12,14},{14,10},{10,6},{6,2},{2,0},{1,5},{5,9},... | collective-permute-start | bytes 786440 | tf_op jit(solution)/shard_map/ppermute | solution.py:133
  24.0 13.6 %collective-permute-start.8 = (bf16[256,512]{1,0:T(8,128)(2,1)}, bf16[256,512]{1,0:T(8,128)(2,1)}, u32[]{:S(2)}, u32[]{:S(2)}) collective-permute-start(bf16[256,512]{1,0:T(8,128)(2,1)} %collective-permute-done.3.refs_3_), channel_id=1, source_target_pairs={{0,4},{4,8},{8,12},{12,14},{14,10},{10,6},{6,2},{2,0},{1,5},{5,9},... | collective-permute-start | bytes 786440 | tf_op jit(solution)/shard_map/ppermute | solution.py:133
  25.6 11.6 %collective-permute-start.9 = (bf16[256,512]{1,0:T(8,128)(2,1)}, bf16[256,512]{1,0:T(8,128)(2,1)}, u32[]{:S(2)}, u32[]{:S(2)}) collective-permute-start(bf16[256,512]{1,0:T(8,128)(2,1)} %collective-permute-done.4.refs_4_), channel_id=1, source_target_pairs={{4,0},{8,4},{12,8},{14,12},{10,14},{6,10},{2,6},{0,2},{5,1},{9,5},... | collective-permute-start | bytes 786440 | tf_op jit(solution)/shard_map/ppermute | solution.py:133
  31.5 13.2 %collective-permute-start.14 = (bf16[256,512]{1,0:T(8,128)(2,1)}, bf16[256,512]{1,0:T(8,128)(2,1)S(1)}, u32[]{:S(2)}, u32[]{:S(2)}) collective-permute-start(bf16[256,512]{1,0:T(8,128)(2,1)} %collective-permute-done.10.refs_3_), channel_id=1, source_target_pairs={{4,0},{8,4},{12,8},{14,12},{10,14},{6,10},{2,6},{0,2},{5,1},{9,5},... | collective-permute-start | bytes 786440 | tf_op jit(solution)/shard_map/ppermute | solution.py:133
  37.1 11.1 %collective-permute-start.13 = (bf16[256,512]{1,0:T(8,128)(2,1)}, bf16[256,512]{1,0:T(8,128)(2,1)S(1)}, u32[]{:S(2)}, u32[]{:S(2)}) collective-permute-start(bf16[256,512]{1,0:T(8,128)(2,1)} %collective-permute-done.9.refs_2_), channel_id=1, source_target_pairs={{4,0},{8,4},{12,8},{14,12},{10,14},{6,10},{2,6},{0,2},{5,1},{9,5},... | collective-permute-start | bytes 786440 | tf_op jit(solution)/shard_map/ppermute | solution.py:133
  37.6 11.1 %collective-permute-start.12 = (bf16[256,512]{1,0:T(8,128)(2,1)}, bf16[256,512]{1,0:T(8,128)(2,1)}, u32[]{:S(2)}, u32[]{:S(2)}) collective-permute-start(bf16[256,512]{1,0:T(8,128)(2,1)} %collective-permute-done.8.refs_1_), channel_id=1, source_target_pairs={{0,4},{4,8},{8,12},{12,14},{14,10},{10,6},{6,2},{2,0},{1,5},{5,9},... | collective-permute-start | bytes 786440 | tf_op jit(solution)/shard_map/ppermute | solution.py:133
  39.2 11.1 %collective-permute-start.7 = (bf16[256,512]{1,0:T(8,128)(2,1)}, bf16[256,512]{1,0:T(8,128)(2,1)}, u32[]{:S(2)}, u32[]{:S(2)}) collective-permute-start(bf16[256,512]{1,0:T(8,128)(2,1)} %collective-permute-done.6.refs_0_), channel_id=1, source_target_pairs={{0,4},{4,8},{8,12},{12,14},{14,10},{10,6},{6,2},{2,0},{1,5},{5,9},... | collective-permute-start | bytes 786440 | tf_op jit(solution)/shard_map/ppermute | solution.py:133
  44.7 11.0 %collective-permute-start.18 = (bf16[256,512]{1,0:T(8,128)(2,1)S(1)}, bf16[256,512]{1,0:T(8,128)(2,1)}, u32[]{:S(2)}, u32[]{:S(2)}) collective-permute-start(bf16[256,512]{1,0:T(8,128)(2,1)S(1)} %collective-permute-done.14.refs_3_), channel_id=1, source_target_pairs={{4,0},{8,4},{12,8},{14,12},{10,14},{6,10},{2,6},{0,2},{5,1},{9,5},... | collective-permute-start | bytes 786440 | tf_op jit(solution)/shard_map/ppermute | solution.py:133
  48.3 11.5 %collective-permute-start.17 = (bf16[256,512]{1,0:T(8,128)(2,1)S(1)}, bf16[256,512]{1,0:T(8,128)(2,1)}, u32[]{:S(2)}, u32[]{:S(2)}) collective-permute-start(bf16[256,512]{1,0:T(8,128)(2,1)S(1)} %collective-permute-done.13.refs_2_), channel_id=1, source_target_pairs={{4,0},{8,4},{12,8},{14,12},{10,14},{6,10},{2,6},{0,2},{5,1},{9,5},... | collective-permute-start | bytes 786440 | tf_op jit(solution)/shard_map/ppermute | solution.py:133
  48.7 11.5 %collective-permute-start.16 = (bf16[256,512]{1,0:T(8,128)(2,1)}, bf16[256,512]{1,0:T(8,128)(2,1)}, u32[]{:S(2)}, u32[]{:S(2)}) collective-permute-start(bf16[256,512]{1,0:T(8,128)(2,1)} %collective-permute-done.12.refs_1_), channel_id=1, source_target_pairs={{0,4},{4,8},{8,12},{12,14},{14,10},{10,6},{6,2},{2,0},{1,5},{5,9},... | collective-permute-start | bytes 786440 | tf_op jit(solution)/shard_map/ppermute | solution.py:133
  50.3 11.5 %collective-permute-start.11 = (bf16[256,512]{1,0:T(8,128)(2,1)}, bf16[256,512]{1,0:T(8,128)(2,1)}, u32[]{:S(2)}, u32[]{:S(2)}) collective-permute-start(bf16[256,512]{1,0:T(8,128)(2,1)} %collective-permute-done.7.refs_0_), channel_id=1, source_target_pairs={{0,4},{4,8},{8,12},{12,14},{14,10},{10,6},{6,2},{2,0},{1,5},{5,9},... | collective-permute-start | bytes 786440 | tf_op jit(solution)/shard_map/ppermute | solution.py:133
  55.7 11.6 %collective-permute-start.22 = (bf16[256,512]{1,0:T(8,128)(2,1)}, bf16[256,512]{1,0:T(8,128)(2,1)S(1)}, u32[]{:S(2)}, u32[]{:S(2)}) collective-permute-start(bf16[256,512]{1,0:T(8,128)(2,1)} %collective-permute-done.18.refs_3_), channel_id=1, source_target_pairs={{4,0},{8,4},{12,8},{14,12},{10,14},{6,10},{2,6},{0,2},{5,1},{9,5},... | collective-permute-start | bytes 786440 | tf_op jit(solution)/shard_map/ppermute | solution.py:133
  59.7 11.1 %collective-permute-start.21 = (bf16[256,512]{1,0:T(8,128)(2,1)}, bf16[256,512]{1,0:T(8,128)(2,1)S(1)}, u32[]{:S(2)}, u32[]{:S(2)}) collective-permute-start(bf16[256,512]{1,0:T(8,128)(2,1)} %collective-permute-done.17.refs_2_), channel_id=1, source_target_pairs={{4,0},{8,4},{12,8},{14,12},{10,14},{6,10},{2,6},{0,2},{5,1},{9,5},... | collective-permute-start | bytes 786440 | tf_op jit(solution)/shard_map/ppermute | solution.py:133
  60.2 11.1 %collective-permute-start.20 = (bf16[256,512]{1,0:T(8,128)(2,1)}, bf16[256,512]{1,0:T(8,128)(2,1)}, u32[]{:S(2)}, u32[]{:S(2)}) collective-permute-start(bf16[256,512]{1,0:T(8,128)(2,1)} %collective-permute-done.16.refs_1_), channel_id=1, source_target_pairs={{0,4},{4,8},{8,12},{12,14},{14,10},{10,6},{6,2},{2,0},{1,5},{5,9},... | collective-permute-start | bytes 786440 | tf_op jit(solution)/shard_map/ppermute | solution.py:133
  61.8 11.1 %collective-permute-start.15 = (bf16[256,512]{1,0:T(8,128)(2,1)}, bf16[256,512]{1,0:T(8,128)(2,1)}, u32[]{:S(2)}, u32[]{:S(2)}) collective-permute-start(bf16[256,512]{1,0:T(8,128)(2,1)} %collective-permute-done.11.refs_0_), channel_id=1, source_target_pairs={{0,4},{4,8},{8,12},{12,14},{14,10},{10,6},{6,2},{2,0},{1,5},{5,9},... | collective-permute-start | bytes 786440 | tf_op jit(solution)/shard_map/ppermute | solution.py:133
  67.2 11.0 %collective-permute-start.28 = (bf16[256,512]{1,0:T(8,128)(2,1)S(1)}, bf16[256,512]{1,0:T(8,128)(2,1)S(1)}, u32[]{:S(2)}, u32[]{:S(2)}) collective-permute-start(bf16[256,512]{1,0:T(8,128)(2,1)S(1)} %collective-permute-done.22.refs_3_), channel_id=1, source_target_pairs={{4,0},{8,4},{12,8},{14,12},{10,14},{6,10},{2,6},{0,2},{5,1},{9,5},... | collective-permute-start | bytes 786440 | tf_op jit(solution)/shard_map/ppermute | solution.py:133
  70.9 11.3 %collective-permute-start.26 = (bf16[256,512]{1,0:T(8,128)(2,1)S(1)}, bf16[256,512]{1,0:T(8,128)(2,1)S(1)}, u32[]{:S(2)}, u32[]{:S(2)}) collective-permute-start(bf16[256,512]{1,0:T(8,128)(2,1)S(1)} %collective-permute-done.21.refs_2_), channel_id=1, source_target_pairs={{4,0},{8,4},{12,8},{14,12},{10,14},{6,10},{2,6},{0,2},{5,1},{9,5},... | collective-permute-start | bytes 786440 | tf_op jit(solution)/shard_map/ppermute | solution.py:133
  71.3 11.4 %collective-permute-start.24 = (bf16[256,512]{1,0:T(8,128)(2,1)}, bf16[256,512]{1,0:T(8,128)(2,1)}, u32[]{:S(2)}, u32[]{:S(2)}) collective-permute-start(bf16[256,512]{1,0:T(8,128)(2,1)} %collective-permute-done.20.refs_1_), channel_id=1, source_target_pairs={{0,4},{4,8},{8,12},{12,14},{14,10},{10,6},{6,2},{2,0},{1,5},{5,9},... | collective-permute-start | bytes 786440 | tf_op jit(solution)/shard_map/ppermute | solution.py:133
  72.9 11.3 %collective-permute-start.19 = (bf16[256,512]{1,0:T(8,128)(2,1)}, bf16[256,512]{1,0:T(8,128)(2,1)}, u32[]{:S(2)}, u32[]{:S(2)}) collective-permute-start(bf16[256,512]{1,0:T(8,128)(2,1)} %collective-permute-done.15.refs_0_), channel_id=1, source_target_pairs={{0,4},{4,8},{8,12},{12,14},{14,10},{10,6},{6,2},{2,0},{1,5},{5,9},... | collective-permute-start | bytes 786440 | tf_op jit(solution)/shard_map/ppermute | solution.py:133
  78.2 11.3 %collective-permute-start.29 = (bf16[256,512]{1,0:T(8,128)(2,1)S(1)}, bf16[256,512]{1,0:T(8,128)(2,1)S(1)}, u32[]{:S(2)}, u32[]{:S(2)}) collective-permute-start(bf16[256,512]{1,0:T(8,128)(2,1)S(1)} %collective-permute-done.28.refs_3_), channel_id=1, source_target_pairs={{4,0},{8,4},{12,8},{14,12},{10,14},{6,10},{2,6},{0,2},{5,1},{9,5},... | collective-permute-start | bytes 786440 | tf_op jit(solution)/shard_map/ppermute | solution.py:133
  82.2 8.9 %collective-permute-start.27 = (bf16[256,512]{1,0:T(8,128)(2,1)S(1)}, bf16[256,512]{1,0:T(8,128)(2,1)S(1)}, u32[]{:S(2)}, u32[]{:S(2)}) collective-permute-start(bf16[256,512]{1,0:T(8,128)(2,1)S(1)} %collective-permute-done.26.refs_2_), channel_id=1, source_target_pairs={{4,0},{8,4},{12,8},{14,12},{10,14},{6,10},{2,6},{0,2},{5,1},{9,5},... | collective-permute-start | bytes 786440 | tf_op jit(solution)/shard_map/ppermute | solution.py:133
  82.7 9.1 %collective-permute-start.25 = (bf16[256,512]{1,0:T(8,128)(2,1)}, bf16[256,512]{1,0:T(8,128)(2,1)}, u32[]{:S(2)}, u32[]{:S(2)}) collective-permute-start(bf16[256,512]{1,0:T(8,128)(2,1)} %collective-permute-done.24.refs_1_), channel_id=1, source_target_pairs={{0,4},{4,8},{8,12},{12,14},{14,10},{10,6},{6,2},{2,0},{1,5},{5,9},... | collective-permute-start | bytes 786440 | tf_op jit(solution)/shard_map/ppermute | solution.py:133
  84.2 8.1 %collective-permute-start.23 = (bf16[256,512]{1,0:T(8,128)(2,1)}, bf16[256,512]{1,0:T(8,128)(2,1)}, u32[]{:S(2)}, u32[]{:S(2)}) collective-permute-start(bf16[256,512]{1,0:T(8,128)(2,1)} %collective-permute-done.19.refs_0_), channel_id=1, source_target_pairs={{0,4},{4,8},{8,12},{12,14},{14,10},{10,6},{6,2},{2,0},{1,5},{5,9},... | collective-permute-start | bytes 786440 | tf_op jit(solution)/shard_map/ppermute | solution.py:133
  89.5 0.7 copy-start.4
  91.1 0.7 copy-start.6
  92.3 1.0 copy-start.5
  93.2 0.9 copy-start.7
  94.2 4.8 %copy-start.12 = (s32[4]{0:T(128)S(1)}, s32[4]{0:T(128)}, u32[]{:S(2)}) copy-start(s32[4]{0:T(128)} %param.13) | copy-start | bytes 52
  94.2 8.7 %copy-start.1 = (bf16[512,1024]{1,0:T(8,128)(2,1)S(1)}, bf16[512,1024]{1,0:T(8,128)(2,1)}, u32[]{:S(2)}) copy-start(bf16[512,1024]{1,0:T(8,128)(2,1)} %key_up_ref.1) | copy-start | bytes 3145732
  98.9 2.9 %collective-permute-start.30 = (bf16[1024,512]{1,0:T(8,128)(2,1)}, bf16[1024,512]{1,0:T(8,128)(2,1)S(1)}, u32[]{:S(2)}, u32[]{:S(2)}) collective-permute-start(bf16[1024,512]{1,0:T(8,128)(2,1)} %get-tuple-element.84.have_ref), channel_id=1, source_target_pairs={{0,1},{1,0},{2,3},{3,2},{4,5},{5,4},{6,7},{7,6},{8,9},{9,8},{10,11... | collective-permute-start | bytes 3145736 | tf_op jit(solution)/shard_map/ppermute | solution.py:249
  101.9 1.0 copy-start.8
  102.9 1.2 copy-start.2
  104.1 1.2 copy-start.9
  105.3 4.7 %copy-start.11 = (bf16[4,4,1024]{2,1,0:T(4,128)(2,1)S(1)}, bf16[4,4,1024]{2,1,0:T(4,128)(2,1)}, u32[]{:S(2)}) copy-start(bf16[4,4,1024]{2,1,0:T(4,128)(2,1)} %param.15) | copy-start | bytes 98308
  105.4 5.0 %copy-start.3 = (bf16[512,1024]{1,0:T(8,128)(2,1)S(1)}, bf16[512,1024]{1,0:T(8,128)(2,1)}, u32[]{:S(2)}) copy-start(bf16[512,1024]{1,0:T(8,128)(2,1)} %value_up_ref.1) | copy-start | bytes 3145732
  111.4 14.7 %all-to-all-start = ((f32[8,72,128]{2,1,0:T(8,128)}), f32[8,72,128]{2,1,0:T(8,128)S(1)}, u32[]{:S(2)}, u32[]{:S(2)}) async-start(f32[8,72,128]{2,1,0:T(8,128)} %bitcast.25), calls=%async_computation | async-start | bytes 589824 | tf_op jit(solution)/shard_map/all_to_all | solution.py:281
  126.1 0.7 copy-start.10
  128.7 3.9 %collective-permute-start.31 = (bf16[64,128]{1,0:T(8,128)(2,1)}, bf16[64,128]{1,0:T(8,128)(2,1)S(1)}, u32[]{:S(2)}, u32[]{:S(2)}) collective-permute-start(bf16[64,128]{1,0:T(8,128)(2,1)} %shard_map.90), channel_id=1, source_target_pairs={{0,2},{2,0},{4,6},{6,4},{8,10},{10,8},{12,14},{14,12},{1,3},{3,1},... | collective-permute-start | bytes 49160 | tf_op jit(solution)/shard_map/ppermute | solution.py:285
  133.4 5.8 %collective-permute-start.32 = (bf16[128,128]{1,0:T(8,128)(2,1)S(1)}, bf16[128,128]{1,0:T(8,128)(2,1)S(1)}, u32[]{:S(2)}, u32[]{:S(2)}) collective-permute-start(bf16[128,128]{1,0:T(8,128)(2,1)S(1)} %pad_maximum_fusion.2), channel_id=1, source_target_pairs={{0,12},{2,14},{4,8},{6,10},{8,4},{10,6},{12,0},{14,2},{1,13},{3,15... | collective-permute-start | bytes 98312 | tf_op jit(solution)/shard_map/ppermute | solution.py:288
  134.7 5.3 %collective-permute-start.33 = (bf16[128,128]{1,0:T(8,128)(2,1)S(1)}, bf16[128,128]{1,0:T(8,128)(2,1)S(1)}, u32[]{:S(2)}, u32[]{:S(2)}) collective-permute-start(bf16[128,128]{1,0:T(8,128)(2,1)S(1)} %pad_maximum_fusion.2), channel_id=1, source_target_pairs={{0,8},{2,10},{4,12},{6,14},{8,0},{10,2},{12,4},{14,6},{1,9},{3,11}... | collective-permute-start | bytes 98312 | tf_op jit(solution)/shard_map/ppermute | solution.py:288
  136.0 4.2 %collective-permute-start.34 = (bf16[128,128]{1,0:T(8,128)(2,1)S(1)}, bf16[128,128]{1,0:T(8,128)(2,1)S(1)}, u32[]{:S(2)}, u32[]{:S(2)}) collective-permute-start(bf16[128,128]{1,0:T(8,128)(2,1)S(1)} %pad_maximum_fusion.2), channel_id=1, source_target_pairs={{0,4},{2,6},{4,0},{6,2},{8,12},{10,14},{12,8},{14,10},{1,5},{3,7},... | collective-permute-start | bytes 98312 | tf_op jit(solution)/shard_map/ppermute | solution.py:288
  140.4 1.4 collective-permute-start.35

commit v9 on v8

--- a/solution.py
+++ b/solution.py
@@ -31,7 +31,7 @@
 
     def kernel(places_ref, mine_ref, theirs_ref, *refs):
         parts = refs[:count]
-        total_ref, out_ref, mark_ref, columns, weights, sems = (
+        total_ref, out_ref, mark_ref, columns, weights, sems, loaded = (
             refs[count:] if total is not None else (None,) + refs[count:]
         )
         copies = []
@@ -44,10 +44,15 @@
                 copy.start()
                 copies.append(copy)
         at = 0
-        for part in parts:
-            weights[at : at + part.shape[0], :] = part[...]
+        loads = []
+        for k, part in enumerate(parts):
+            load = pltpu.make_async_copy(part, weights.at[pl.ds(at, part.shape[0])], loaded.at[k])
+            load.start()
+            loads.append(load)
             at += part.shape[0]
         mark_ref[...] = jnp.zeros_like(mark_ref)
+        for load in loads:
+            load.wait()
         for j in range(2):
             for g in range(len(groups)):
                 copies[j * len(groups) + g].wait()
@@ -69,12 +74,13 @@
             jax.ShapeDtypeStruct((2 * tok_rows, width), BF if last else F32),
             jax.ShapeDtypeStruct((8, 128), F32),
         ),
-        in_specs=[pl.BlockSpec(memory_space=pltpu.SMEM), in_any, in_any] + [in_vmem] * (count + len(sums)),
+        in_specs=[pl.BlockSpec(memory_space=pltpu.SMEM)] + [in_any] * (2 + count) + [in_vmem] * len(sums),
         out_specs=(in_vmem, in_vmem),
         scratch_shapes=[
             pltpu.VMEM((2, tok_rows, deep), BF),
             pltpu.VMEM((deep, width), BF),
             pltpu.SemaphoreType.DMA((2, len(groups))),
+            pltpu.SemaphoreType.DMA((count,)),
         ],
         input_output_aliases={} if total is None or last else {3 + count: 0},
         compiler_params=pltpu.CompilerParams(vmem_limit_bytes=30 * 2**20),
@@ -147,12 +153,24 @@
     blocks = pairs * heads // chips
     scale = 1.0 / DH**0.5
 
-    def kernel(core_ref, have_ref, got_ref, key_up_ref, value_up_ref, query_ref, bounds_ref, out_ref):
-        first = core_ref[0] == 0
-        have, got = have_ref[...], got_ref[...]
-        lanes = pl.ds(pl.multiple_of(core_ref[0] * heads * DH, heads * DH), heads * DH)
-        keys = mm(jnp.where(first, have, got), key_up_ref[:, lanes]).astype(BF)
-        values = mm(jnp.where(first, got, have), value_up_ref[:, lanes]).astype(BF)
+    def kernel(core_ref, have_any, got_any, key_any, value_any, query_any, bounds_ref, out_ref, *scratch):
+        latents, ups, query_ref, sems = scratch
+        core = core_ref[0]
+        lanes = pl.ds(pl.multiple_of(core * heads * DH, heads * DH), heads * DH)
+        pairs_of = [
+            (have_any, latents.at[core]),
+            (got_any, latents.at[1 - core]),
+            (key_any.at[:, lanes], ups.at[0]),
+            (value_any.at[:, lanes], ups.at[1]),
+            (query_any, query_ref),
+        ]
+        copies = [pltpu.make_async_copy(source, target, sems.at[k]) for k, (source, target) in enumerate(pairs_of)]
+        for copy in copies:
+            copy.start()
+        for copy in copies:
+            copy.wait()
+        keys = mm(latents[0], ups[0]).astype(BF)
+        values = mm(latents[1], ups[1]).astype(BF)
         position = lax.broadcasted_iota(jnp.int32, (tokens, rows), 0)
         visible = (position >= bounds_ref[0:1, :]) & (position < bounds_ref[1:2, :])
         tops, totals = [], []
@@ -186,8 +204,14 @@
     return pl.pallas_call(
         kernel,
         out_shape=jax.ShapeDtypeStruct((chips, blocks + 1, 8, DH), F32),
-        in_specs=[pl.BlockSpec(memory_space=pltpu.SMEM)] + [in_vmem] * 6,
+        in_specs=[pl.BlockSpec(memory_space=pltpu.SMEM)] + [pl.BlockSpec(memory_space=pl.ANY)] * 5 + [in_vmem],
         out_specs=in_vmem,
+        scratch_shapes=[
+            pltpu.VMEM((2,) + have.shape, BF),
+            pltpu.VMEM((2, have.shape[1], heads * DH), BF),
+            pltpu.VMEM(query.shape, BF),
+            pltpu.SemaphoreType.DMA((5,)),
+        ],
         compiler_params=pltpu.CompilerParams(vmem_limit_bytes=24 * 2**20),
         cost_estimate=pl.CostEstimate(
             flops=4 * tokens * (have.shape[1] * heads * DH + heads * rows * DH),
@@ -220,6 +244,7 @@
         out_shape=jax.ShapeDtypeStruct((blocks * 8, DH), BF),
         in_specs=[in_vmem] * 3,
         out_specs=in_vmem,
+        compiler_params=pltpu.CompilerParams(vmem_limit_bytes=8 * 2**20),
         cost_estimate=pl.CostEstimate(
             flops=2 * chips * blocks * 8 * DH, bytes_accessed=4 * arrived.size, transcendentals=chips * blocks * 8
         ),

time: 144 us -> 140 us (0.972)
    pallas_call x1, Pallas kernels: 1.93 us -> 0.36 us  [merge(): pl.pallas_call(kernel, out_shape=jax.ShapeDtypeStruct((blocks * 8, DH), B...]
    unnamed x26 -> x24, local copies, waits for them, and re-layouts: 7.49 us -> 6.77 us
  transfers between devices with their start and end apart: 37 -> 37, of which waited for: 19 -> 18; matrix products, arithmetic and copies ran while one was open for 3% -> 2% of each run, Pallas kernels for 17% -> 18%
where the time goes in v9:
time: 140 us
  waiting for transfers between devices  50.7 us (36%)
  starting transfers between devices  41.2 us (29%)
  Pallas kernels  34.5 us (25%)
  local copies, waits for them, and re-layouts  9.2 us (7%)
  other arithmetic  2.42 us (2%)
  matrix products  1.51 us (1%)
    ppermute x28, waiting for transfers between devices, project(): held[k] = lax.ppermute(held[k], 'chip', ways[k])  32.4 us
    ppermute x28, starting transfers between devices, project(): held[k] = lax.ppermute(held[k], 'chip', ways[k])  29.3 us
    pallas_call x7, Pallas kernels, add_pieces(): pl.pallas_call(kernel, out_shape=(jax.ShapeDtypeStruct((2 * tok_rows, wid...  29.3 us
    all_to_all x1, waiting for transfers between devices, on_device(): lax.all_to_all(flat, 'chip', split_axis=0, concat_axis=0, tiled=True)  8.6 us
    unnamed x24, local copies, waits for them, and re-layouts  6.77 us
    all_to_all x1, starting transfers between devices, on_device(): lax.all_to_all(flat, 'chip', split_axis=0, concat_axis=0, tiled=True)  4.83 us
    pallas_call x1, Pallas kernels, attend(): pl.pallas_call(kernel, out_shape=jax.ShapeDtypeStruct((chips, blocks + 1,...  4.79 us
    ppermute x3, starting transfers between devices, on_device(): lax.ppermute(couple, 'chip', [(c, c ^ 2 * d) for c in range(chips)])  4.45 us
  transfers between devices with their start and end apart: 37, of which 18 were waited for; matrix products, arithmetic and copies ran while one was open for 2% of the time, Pallas kernels for 18%

profile of v9, /device:TPU:0, one launch (start us, length us, event | category | flops | bytes accessed | tf_op | source)
XLA Modules:
  0.0 139.9 jit_solution(5472014170329952369)
XLA Ops:
  0.0 1.3 broadcast_select_fusion
  1.3 0.5 collective-permute-start
  1.8 1.5 %collective-permute-done.refs_1_ = bf16[512,512]{1,0:T(8,128)(2,1)S(1)} collective-permute-done((bf16[512,512]{1,0:T(8,128)(2,1)S(1)}, bf16[512,512]{1,0:T(8,128)(2,1)S(1)}, u32[]{:S(2)}, u32[]{:S(2)}) %collective-permute-start) | collective-permute-done | bytes 524320 | tf_op jit(solution)/shard_map/ppermute | solution.py:101
  3.8 2.8 %collective-permute-start.2 = (bf16[256,512]{1,0:T(8,128)(2,1)S(1)}, bf16[256,512]{1,0:T(8,128)(2,1)}, u32[]{:S(2)}, u32[]{:S(2)}) collective-permute-start(bf16[256,512]{1,0:T(8,128)(2,1)S(1)} %get-tuple-element.94), channel_id=1, source_target_pairs={{0,4},{4,8},{8,12},{12,14},{14,10},{10,6},{6,2},{2,0},{1,5},{5,9},... | collective-permute-start | bytes 786440 | tf_op jit(solution)/shard_map/ppermute | solution.py:139
  6.6 1.6 %collective-permute-start.3 = (bf16[256,512]{1,0:T(8,128)(2,1)S(1)}, bf16[256,512]{1,0:T(8,128)(2,1)}, u32[]{:S(2)}, u32[]{:S(2)}) collective-permute-start(bf16[256,512]{1,0:T(8,128)(2,1)S(1)} %get-tuple-element.93), channel_id=1, source_target_pairs={{0,4},{4,8},{8,12},{12,14},{14,10},{10,6},{6,2},{2,0},{1,5},{5,9},... | collective-permute-start | bytes 786440 | tf_op jit(solution)/shard_map/ppermute | solution.py:139
  8.2 0.5 collective-permute-start.4
  8.7 5.0 %collective-permute-done.2.refs_2_ = bf16[256,512]{1,0:T(8,128)(2,1)} collective-permute-done((bf16[256,512]{1,0:T(8,128)(2,1)S(1)}, bf16[256,512]{1,0:T(8,128)(2,1)}, u32[]{:S(2)}, u32[]{:S(2)}) %collective-permute-start.2) | collective-permute-done | bytes 262176 | tf_op jit(solution)/shard_map/ppermute | solution.py:139
  13.8 5.3 %collective-permute-done.3.refs_3_ = bf16[256,512]{1,0:T(8,128)(2,1)} collective-permute-done((bf16[256,512]{1,0:T(8,128)(2,1)S(1)}, bf16[256,512]{1,0:T(8,128)(2,1)}, u32[]{:S(2)}, u32[]{:S(2)}) %collective-permute-start.3) | collective-permute-done | bytes 262176 | tf_op jit(solution)/shard_map/ppermute | solution.py:139
  19.1 2.9 %collective-permute-done.5.refs_5_ = bf16[256,512]{1,0:T(8,128)(2,1)} collective-permute-done((bf16[256,512]{1,0:T(8,128)(2,1)S(1)}, bf16[256,512]{1,0:T(8,128)(2,1)}, u32[]{:S(2)}, u32[]{:S(2)}) %collective-permute-start.5) | collective-permute-done | bytes 262176 | tf_op jit(solution)/shard_map/ppermute | solution.py:139
  22.4 1.6 %collective-permute-start.6 = (bf16[256,512]{1,0:T(8,128)(2,1)}, bf16[256,512]{1,0:T(8,128)(2,1)}, u32[]{:S(2)}, u32[]{:S(2)}) collective-permute-start(bf16[256,512]{1,0:T(8,128)(2,1)} %collective-permute-done.2.refs_2_), channel_id=1, source_target_pairs={{0,4},{4,8},{8,12},{12,14},{14,10},{10,6},{6,2},{2,0},{1,5},{5,9},... | collective-permute-start | bytes 786440 | tf_op jit(solution)/shard_map/ppermute | solution.py:139
  24.0 1.6 %collective-permute-start.8 = (bf16[256,512]{1,0:T(8,128)(2,1)}, bf16[256,512]{1,0:T(8,128)(2,1)}, u32[]{:S(2)}, u32[]{:S(2)}) collective-permute-start(bf16[256,512]{1,0:T(8,128)(2,1)} %collective-permute-done.3.refs_3_), channel_id=1, source_target_pairs={{0,4},{4,8},{8,12},{12,14},{14,10},{10,6},{6,2},{2,0},{1,5},{5,9},... | collective-permute-start | bytes 786440 | tf_op jit(solution)/shard_map/ppermute | solution.py:139
  25.6 0.4 collective-permute-start.9
  26.1 5.7 %shard_map.82 = (f32[1024,512]{1,0:T(8,128)S(1)}, f32[8,128]{1,0:T(8,128)}) custom-call(s32[4]{0:T(128)S(1)} %pad_add_fusion.1.places_ref, bf16[512,8192]{1,0:T(8,128)(2,1)} %mine_ref.13, bf16[512,8192]{1,0:T(8,128)(2,1)} %collective-permute-done.1.theirs_ref, bf16[512,512]{1,0:T(8,128)(2,1)S(1)} %get-tuple-element.89.refs_0_, ...), custom_call_target="tpu_custom_call" | custom-call | flops 2147483648 | bytes 4194304 | tf_op jit(solution)/shard_map/pallas_call | solution.py:71
  31.8 0.5 collective-permute-start.14
  32.3 4.8 %collective-permute-done.9.refs_2_ = bf16[256,512]{1,0:T(8,128)(2,1)} collective-permute-done((bf16[256,512]{1,0:T(8,128)(2,1)}, bf16[256,512]{1,0:T(8,128)(2,1)}, u32[]{:S(2)}, u32[]{:S(2)}) %collective-permute-start.9) | collective-permute-done | bytes 262176 | tf_op jit(solution)/shard_map/ppermute | solution.py:139
  37.6 1.6 %collective-permute-start.12 = (bf16[256,512]{1,0:T(8,128)(2,1)}, bf16[256,512]{1,0:T(8,128)(2,1)}, u32[]{:S(2)}, u32[]{:S(2)}) collective-permute-start(bf16[256,512]{1,0:T(8,128)(2,1)} %collective-permute-done.8.refs_1_), channel_id=1, source_target_pairs={{0,4},{4,8},{8,12},{12,14},{14,10},{10,6},{6,2},{2,0},{1,5},{5,9},... | collective-permute-start | bytes 786440 | tf_op jit(solution)/shard_map/ppermute | solution.py:139
  39.2 1.6 %collective-permute-start.7 = (bf16[256,512]{1,0:T(8,128)(2,1)}, bf16[256,512]{1,0:T(8,128)(2,1)}, u32[]{:S(2)}, u32[]{:S(2)}) collective-permute-start(bf16[256,512]{1,0:T(8,128)(2,1)} %collective-permute-done.6.refs_0_), channel_id=1, source_target_pairs={{0,4},{4,8},{8,12},{12,14},{14,10},{10,6},{6,2},{2,0},{1,5},{5,9},... | collective-permute-start | bytes 786440 | tf_op jit(solution)/shard_map/ppermute | solution.py:139
  40.8 3.9 %shard_map.83 = (f32[1024,512]{1,0:T(8,128)S(1)}, f32[8,128]{1,0:T(8,128)}) custom-call(s32[2]{0:T(128)S(1)} %pad_add_fusion.2.places_ref, bf16[512,8192]{1,0:T(8,128)(2,1)} %mine_ref.13, bf16[512,8192]{1,0:T(8,128)(2,1)} %collective-permute-done.1.theirs_ref, bf16[256,512]{1,0:T(8,128)(2,1)} %collective-permute-done.6.refs_0_, ...), custom_call_target="tpu_custom_call", output_to_operand_aliasing={{0}: (7, {})} | custom-call | flops 1073741824 | bytes 2097152 | tf_op jit(solution)/shard_map/pallas_call | solution.py:71
  44.7 0.5 collective-permute-start.18
  45.2 3.0 %collective-permute-done.13.refs_2_ = bf16[256,512]{1,0:T(8,128)(2,1)S(1)} collective-permute-done((bf16[256,512]{1,0:T(8,128)(2,1)}, bf16[256,512]{1,0:T(8,128)(2,1)S(1)}, u32[]{:S(2)}, u32[]{:S(2)}) %collective-permute-start.13) | collective-permute-done | bytes 262176 | tf_op jit(solution)/shard_map/ppermute | solution.py:139
  48.7 1.6 %collective-permute-start.16 = (bf16[256,512]{1,0:T(8,128)(2,1)}, bf16[256,512]{1,0:T(8,128)(2,1)}, u32[]{:S(2)}, u32[]{:S(2)}) collective-permute-start(bf16[256,512]{1,0:T(8,128)(2,1)} %collective-permute-done.12.refs_1_), channel_id=1, source_target_pairs={{0,4},{4,8},{8,12},{12,14},{14,10},{10,6},{6,2},{2,0},{1,5},{5,9},... | collective-permute-start | bytes 786440 | tf_op jit(solution)/shard_map/ppermute | solution.py:139
  50.3 1.6 %collective-permute-start.11 = (bf16[256,512]{1,0:T(8,128)(2,1)}, bf16[256,512]{1,0:T(8,128)(2,1)}, u32[]{:S(2)}, u32[]{:S(2)}) collective-permute-start(bf16[256,512]{1,0:T(8,128)(2,1)} %collective-permute-done.7.refs_0_), channel_id=1, source_target_pairs={{0,4},{4,8},{8,12},{12,14},{14,10},{10,6},{6,2},{2,0},{1,5},{5,9},... | collective-permute-start | bytes 786440 | tf_op jit(solution)/shard_map/ppermute | solution.py:139
  52.0 3.7 %shard_map.84 = (f32[1024,512]{1,0:T(8,128)S(1)}, f32[8,128]{1,0:T(8,128)}) custom-call(s32[2]{0:T(128)S(1)} %pad_add_fusion.3.places_ref, bf16[512,8192]{1,0:T(8,128)(2,1)} %mine_ref.13, bf16[512,8192]{1,0:T(8,128)(2,1)} %collective-permute-done.1.theirs_ref, bf16[256,512]{1,0:T(8,128)(2,1)} %collective-permute-done.7.refs_0_, ...), custom_call_target="tpu_custom_call", output_to_operand_aliasing={{0}: (7, {})} | custom-call | flops 1073741824 | bytes 2097152 | tf_op jit(solution)/shard_map/pallas_call | solution.py:71
  55.7 0.5 collective-permute-start.22
  56.2 3.5 %collective-permute-done.17.refs_2_ = bf16[256,512]{1,0:T(8,128)(2,1)} collective-permute-done((bf16[256,512]{1,0:T(8,128)(2,1)S(1)}, bf16[256,512]{1,0:T(8,128)(2,1)}, u32[]{:S(2)}, u32[]{:S(2)}) %collective-permute-start.17) | collective-permute-done | bytes 262176 | tf_op jit(solution)/shard_map/ppermute | solution.py:139
  59.8 0.4 collective-permute-start.21
  60.2 1.6 %collective-permute-start.20 = (bf16[256,512]{1,0:T(8,128)(2,1)}, bf16[256,512]{1,0:T(8,128)(2,1)}, u32[]{:S(2)}, u32[]{:S(2)}) collective-permute-start(bf16[256,512]{1,0:T(8,128)(2,1)} %collective-permute-done.16.refs_1_), channel_id=1, source_target_pairs={{0,4},{4,8},{8,12},{12,14},{14,10},{10,6},{6,2},{2,0},{1,5},{5,9},... | collective-permute-start | bytes 786440 | tf_op jit(solution)/shard_map/ppermute | solution.py:139
  61.8 1.5 %collective-permute-start.15 = (bf16[256,512]{1,0:T(8,128)(2,1)}, bf16[256,512]{1,0:T(8,128)(2,1)}, u32[]{:S(2)}, u32[]{:S(2)}) collective-permute-start(bf16[256,512]{1,0:T(8,128)(2,1)} %collective-permute-done.11.refs_0_), channel_id=1, source_target_pairs={{0,4},{4,8},{8,12},{12,14},{14,10},{10,6},{6,2},{2,0},{1,5},{5,9},... | collective-permute-start | bytes 786440 | tf_op jit(solution)/shard_map/ppermute | solution.py:139
  63.4 3.9 %shard_map.85 = (f32[1024,512]{1,0:T(8,128)S(1)}, f32[8,128]{1,0:T(8,128)}) custom-call(s32[2]{0:T(128)S(1)} %pad_add_fusion.4.places_ref, bf16[512,8192]{1,0:T(8,128)(2,1)} %mine_ref.13, bf16[512,8192]{1,0:T(8,128)(2,1)} %collective-permute-done.1.theirs_ref, bf16[256,512]{1,0:T(8,128)(2,1)} %collective-permute-done.11.refs_0_, ...), custom_call_target="tpu_custom_call", output_to_operand_aliasing={{0}: (7, {})} | custom-call | flops 1073741824 | bytes 2097152 | tf_op jit(solution)/shard_map/pallas_call | solution.py:71
  67.3 0.6 collective-permute-start.28
  67.8 3.0 %collective-permute-done.21.refs_2_ = bf16[256,512]{1,0:T(8,128)(2,1)S(1)} collective-permute-done((bf16[256,512]{1,0:T(8,128)(2,1)}, bf16[256,512]{1,0:T(8,128)(2,1)S(1)}, u32[]{:S(2)}, u32[]{:S(2)}) %collective-permute-start.21) | collective-permute-done | bytes 262176 | tf_op jit(solution)/shard_map/ppermute | solution.py:139
  71.3 1.6 %collective-permute-start.24 = (bf16[256,512]{1,0:T(8,128)(2,1)}, bf16[256,512]{1,0:T(8,128)(2,1)}, u32[]{:S(2)}, u32[]{:S(2)}) collective-permute-start(bf16[256,512]{1,0:T(8,128)(2,1)} %collective-permute-done.20.refs_1_), channel_id=1, source_target_pairs={{0,4},{4,8},{8,12},{12,14},{14,10},{10,6},{6,2},{2,0},{1,5},{5,9},... | collective-permute-start | bytes 786440 | tf_op jit(solution)/shard_map/ppermute | solution.py:139
  72.9 1.5 %collective-permute-start.19 = (bf16[256,512]{1,0:T(8,128)(2,1)}, bf16[256,512]{1,0:T(8,128)(2,1)}, u32[]{:S(2)}, u32[]{:S(2)}) collective-permute-start(bf16[256,512]{1,0:T(8,128)(2,1)} %collective-permute-done.15.refs_0_), channel_id=1, source_target_pairs={{0,4},{4,8},{8,12},{12,14},{14,10},{10,6},{6,2},{2,0},{1,5},{5,9},... | collective-permute-start | bytes 786440 | tf_op jit(solution)/shard_map/ppermute | solution.py:139
  74.5 3.7 %shard_map.86 = (f32[1024,512]{1,0:T(8,128)S(1)}, f32[8,128]{1,0:T(8,128)}) custom-call(s32[2]{0:T(128)S(1)} %pad_add_fusion.5.places_ref, bf16[512,8192]{1,0:T(8,128)(2,1)} %mine_ref.13, bf16[512,8192]{1,0:T(8,128)(2,1)} %collective-permute-done.1.theirs_ref, bf16[256,512]{1,0:T(8,128)(2,1)} %collective-permute-done.15.refs_0_, ...), custom_call_target="tpu_custom_call", output_to_operand_aliasing={{0}: (7, {})} | custom-call | flops 1073741824 | bytes 2097152 | tf_op jit(solution)/shard_map/pallas_call | solution.py:71
  78.3 0.6 collective-permute-start.29
  78.8 3.4 %collective-permute-done.26.refs_2_ = bf16[256,512]{1,0:T(8,128)(2,1)S(1)} collective-permute-done((bf16[256,512]{1,0:T(8,128)(2,1)S(1)}, bf16[256,512]{1,0:T(8,128)(2,1)S(1)}, u32[]{:S(2)}, u32[]{:S(2)}) %collective-permute-start.26) | collective-permute-done | bytes 262176 | tf_op jit(solution)/shard_map/ppermute | solution.py:139
  82.2 0.5 collective-permute-start.27
  82.7 1.5 %collective-permute-start.25 = (bf16[256,512]{1,0:T(8,128)(2,1)}, bf16[256,512]{1,0:T(8,128)(2,1)}, u32[]{:S(2)}, u32[]{:S(2)}) collective-permute-start(bf16[256,512]{1,0:T(8,128)(2,1)} %collective-permute-done.24.refs_1_), channel_id=1, source_target_pairs={{0,4},{4,8},{8,12},{12,14},{14,10},{10,6},{6,2},{2,0},{1,5},{5,9},... | collective-permute-start | bytes 786440 | tf_op jit(solution)/shard_map/ppermute | solution.py:139
  84.2 1.4 %collective-permute-start.23 = (bf16[256,512]{1,0:T(8,128)(2,1)}, bf16[256,512]{1,0:T(8,128)(2,1)}, u32[]{:S(2)}, u32[]{:S(2)}) collective-permute-start(bf16[256,512]{1,0:T(8,128)(2,1)} %collective-permute-done.19.refs_0_), channel_id=1, source_target_pairs={{0,4},{4,8},{8,12},{12,14},{14,10},{10,6},{6,2},{2,0},{1,5},{5,9},... | collective-permute-start | bytes 786440 | tf_op jit(solution)/shard_map/ppermute | solution.py:139
  85.8 3.7 %shard_map.87 = (f32[1024,512]{1,0:T(8,128)S(1)}, f32[8,128]{1,0:T(8,128)}) custom-call(s32[2]{0:T(128)S(1)} %pad_add_fusion.6.places_ref, bf16[512,8192]{1,0:T(8,128)(2,1)} %mine_ref.13, bf16[512,8192]{1,0:T(8,128)(2,1)} %collective-permute-done.1.theirs_ref, bf16[256,512]{1,0:T(8,128)(2,1)} %collective-permute-done.19.refs_0_, ...), custom_call_target="tpu_custom_call", output_to_operand_aliasing={{0}: (7, {})} | custom-call | flops 1073741824 | bytes 2097152 | tf_op jit(solution)/shard_map/pallas_call | solution.py:71
  89.6 0.7 copy-done.4
  90.3 0.8 collective-permute-done.27.refs_2_
  91.1 0.7 copy-done.6
  91.8 0.5 collective-permute-done.23.refs_0_
  92.3 0.9 copy-done.5
  93.2 0.9 copy-done.7
  94.2 4.7 %shard_map.88 = (bf16[1024,512]{1,0:T(8,128)(2,1)}, f32[8,128]{1,0:T(8,128)}) custom-call(s32[4]{0:T(128)S(1)} %pad_add_fusion.places_ref, bf16[512,8192]{1,0:T(8,128)(2,1)} %mine_ref.13, bf16[512,8192]{1,0:T(8,128)(2,1)} %collective-permute-done.1.theirs_ref, bf16[256,512]{1,0:T(8,128)(2,1)} %collective-permute-done.23.refs_0_, ...), custom_call_target="tpu_custom_call" | custom-call | flops 1073741824 | bytes 2097152 | tf_op jit(solution)/shard_map/pallas_call | solution.py:71
  99.6 2.2 %collective-permute-done.30.got_any = bf16[1024,512]{1,0:T(8,128)(2,1)S(1)} collective-permute-done((bf16[1024,512]{1,0:T(8,128)(2,1)}, bf16[1024,512]{1,0:T(8,128)(2,1)S(1)}, u32[]{:S(2)}, u32[]{:S(2)}) %collective-permute-start.30) | collective-permute-done | bytes 1048608 | tf_op jit(solution)/shard_map/ppermute | solution.py:274
  101.8 1.0 copy-done.8
  102.8 1.2 copy-done.2
  104.0 1.2 copy-done.9
  105.3 4.8 %shard_map.89 = f32[8,9,8,128]{3,2,1,0:T(8,128)} custom-call(s32[1]{0:T(128)} %bitcast.core_ref, bf16[1024,512]{1,0:T(8,128)(2,1)} %get-tuple-element.84.have_any, bf16[1024,512]{1,0:T(8,128)(2,1)S(1)} %copy-done.9, bf16[512,1024]{1,0:T(8,128)(2,1)S(1)} %copy-done.1, bf16[512,1024]{1,0:T(8,128)(2,1)S(1)} %copy-done.2, bf16[4,128,128]{2,1,0:T(8,128)(2,1)S(1)} %bitcast.45, ...), custom_call_target="tpu_custom_call" | custom-call | flops 1342177280 | bytes 2097152 | tf_op jit(solution)/shard_map/pallas_call | solution.py:204
  110.6 0.7 fusion.19
  111.4 4.8 %all-to-all-start = ((f32[8,72,128]{2,1,0:T(8,128)}), f32[8,72,128]{2,1,0:T(8,128)S(1)}, u32[]{:S(2)}, u32[]{:S(2)}) async-start(f32[8,72,128]{2,1,0:T(8,128)} %bitcast.25), calls=%async_computation | async-start | bytes 589824 | tf_op jit(solution)/shard_map/all_to_all | solution.py:306
  117.5 8.6 %all-to-all-done = f32[8,72,128]{2,1,0:T(8,128)S(1)} async-done(((f32[8,72,128]{2,1,0:T(8,128)}), f32[8,72,128]{2,1,0:T(8,128)S(1)}, u32[]{:S(2)}, u32[]{:S(2)}) %all-to-all-start) | async-done | bytes 294944 | tf_op jit(solution)/shard_map/all_to_all | solution.py:306
  126.5 1.5 %collective-permute-start.31 = (bf16[64,128]{1,0:T(8,128)(2,1)S(1)}, bf16[64,128]{1,0:T(8,128)(2,1)S(1)}, u32[]{:S(2)}, u32[]{:S(2)}) collective-permute-start(bf16[64,128]{1,0:T(8,128)(2,1)S(1)} %shard_map.90), channel_id=1, source_target_pairs={{0,2},{2,0},{4,6},{6,4},{8,10},{10,8},{12,14},{14,12},{1,3},{3,1},... | collective-permute-start | bytes 49160 | tf_op jit(solution)/shard_map/ppermute | solution.py:310
  128.0 2.3 %collective-permute-done.31 = bf16[64,128]{1,0:T(8,128)(2,1)S(1)} collective-permute-done((bf16[64,128]{1,0:T(8,128)(2,1)S(1)}, bf16[64,128]{1,0:T(8,128)(2,1)S(1)}, u32[]{:S(2)}, u32[]{:S(2)}) %collective-permute-start.31) | collective-permute-done | bytes 16416 | tf_op jit(solution)/shard_map/ppermute | solution.py:310
  130.3 1.2 collective-permute-start.32
  131.5 1.3 collective-permute-start.33
  132.9 1.9 %collective-permute-start.34 = (bf16[128,128]{1,0:T(8,128)(2,1)S(1)}, bf16[128,128]{1,0:T(8,128)(2,1)S(1)}, u32[]{:S(2)}, u32[]{:S(2)}) collective-permute-start(bf16[128,128]{1,0:T(8,128)(2,1)S(1)} %pad_maximum_fusion.2), channel_id=1, source_target_pairs={{0,4},{2,6},{4,0},{6,2},{8,12},{10,14},{12,8},{14,10},{1,5},{3,7},... | collective-permute-start | bytes 98312 | tf_op jit(solution)/shard_map/ppermute | solution.py:313
  134.7 1.3 collective-permute-done.32
  136.1 0.8 collective-permute-done.33
  137.3 1.3 collective-permute-done.35
  139.0 0.9 reshape.98
  (93 shorter events, 6.5 us)
Async XLA Ops:
  0.0 99.4 %copy-start = (bf16[4,4,8192]{2,1,0:T(4,128)(2,1)S(1)}, bf16[4,4,8192]{2,1,0:T(4,128)(2,1)}, u32[]{:S(2)}) copy-start(bf16[4,4,8192]{2,1,0:T(4,128)(2,1)} %param.14) | copy-start | bytes 786436
  1.3 2.1 %collective-permute-start = (bf16[512,512]{1,0:T(8,128)(2,1)S(1)}, bf16[512,512]{1,0:T(8,128)(2,1)S(1)}, u32[]{:S(2)}, u32[]{:S(2)}) collective-permute-start(bf16[512,512]{1,0:T(8,128)(2,1)S(1)} %get-tuple-element.90), channel_id=1, source_target_pairs={{0,1},{1,0},{2,3},{3,2},{4,5},{5,4},{6,7},{7,6},{8,9},{9,8},{10,11... | collective-permute-start | bytes 1572872 | tf_op jit(solution)/shard_map/ppermute | solution.py:101
  3.4 22.7 %collective-permute-start.1 = (bf16[512,8192]{1,0:T(8,128)(2,1)}, bf16[512,8192]{1,0:T(8,128)(2,1)}, u32[]{:S(2)}, u32[]{:S(2)}) collective-permute-start(bf16[512,8192]{1,0:T(8,128)(2,1)} %mine_ref.13), channel_id=1, source_target_pairs={{0,1},{1,0},{2,3},{3,2},{4,5},{5,4},{6,7},{7,6},{8,9},{9,8},{10,11... | collective-permute-start | bytes 25165832 | tf_op jit(solution)/shard_map/ppermute | solution.py:126
  3.8 10.0 %collective-permute-start.2 = (bf16[256,512]{1,0:T(8,128)(2,1)S(1)}, bf16[256,512]{1,0:T(8,128)(2,1)}, u32[]{:S(2)}, u32[]{:S(2)}) collective-permute-start(bf16[256,512]{1,0:T(8,128)(2,1)S(1)} %get-tuple-element.94), channel_id=1, source_target_pairs={{0,4},{4,8},{8,12},{12,14},{14,10},{10,6},{6,2},{2,0},{1,5},{5,9},... | collective-permute-start | bytes 786440 | tf_op jit(solution)/shard_map/ppermute | solution.py:139
  6.6 12.5 %collective-permute-start.3 = (bf16[256,512]{1,0:T(8,128)(2,1)S(1)}, bf16[256,512]{1,0:T(8,128)(2,1)}, u32[]{:S(2)}, u32[]{:S(2)}) collective-permute-start(bf16[256,512]{1,0:T(8,128)(2,1)S(1)} %get-tuple-element.93), channel_id=1, source_target_pairs={{0,4},{4,8},{8,12},{12,14},{14,10},{10,6},{6,2},{2,0},{1,5},{5,9},... | collective-permute-start | bytes 786440 | tf_op jit(solution)/shard_map/ppermute | solution.py:139
  8.2 10.9 %collective-permute-start.4 = (bf16[256,512]{1,0:T(8,128)(2,1)S(1)}, bf16[256,512]{1,0:T(8,128)(2,1)}, u32[]{:S(2)}, u32[]{:S(2)}) collective-permute-start(bf16[256,512]{1,0:T(8,128)(2,1)S(1)} %get-tuple-element.92), channel_id=1, source_target_pairs={{4,0},{8,4},{12,8},{14,12},{10,14},{6,10},{2,6},{0,2},{5,1},{9,5},... | collective-permute-start | bytes 786440 | tf_op jit(solution)/shard_map/ppermute | solution.py:139
  8.7 13.3 %collective-permute-start.5 = (bf16[256,512]{1,0:T(8,128)(2,1)S(1)}, bf16[256,512]{1,0:T(8,128)(2,1)}, u32[]{:S(2)}, u32[]{:S(2)}) collective-permute-start(bf16[256,512]{1,0:T(8,128)(2,1)S(1)} %get-tuple-element.91), channel_id=1, source_target_pairs={{4,0},{8,4},{12,8},{14,12},{10,14},{6,10},{2,6},{0,2},{5,1},{9,5},... | collective-permute-start | bytes 786440 | tf_op jit(solution)/shard_map/ppermute | solution.py:139
  22.0 9.8 %collective-permute-start.10 = (bf16[256,512]{1,0:T(8,128)(2,1)}, bf16[256,512]{1,0:T(8,128)(2,1)}, u32[]{:S(2)}, u32[]{:S(2)}) collective-permute-start(bf16[256,512]{1,0:T(8,128)(2,1)} %collective-permute-done.5.refs_5_), channel_id=1, source_target_pairs={{4,0},{8,4},{12,8},{14,12},{10,14},{6,10},{2,6},{0,2},{5,1},{9,5},... | collective-permute-start | bytes 786440 | tf_op jit(solution)/shard_map/ppermute | solution.py:139
  22.4 16.8 %collective-permute-start.6 = (bf16[256,512]{1,0:T(8,128)(2,1)}, bf16[256,512]{1,0:T(8,128)(2,1)}, u32[]{:S(2)}, u32[]{:S(2)}) collective-permute-start(bf16[256,512]{1,0:T(8,128)(2,1)} %collective-permute-done.2.refs_2_), channel_id=1, source_target_pairs={{0,4},{4,8},{8,12},{12,14},{14,10},{10,6},{6,2},{2,0},{1,5},{5,9},... | collective-permute-start | bytes 786440 | tf_op jit(solution)/shard_map/ppermute | solution.py:139
  24.0 13.6 %collective-permute-start.8 = (bf16[256,512]{1,0:T(8,128)(2,1)}, bf16[256,512]{1,0:T(8,128)(2,1)}, u32[]{:S(2)}, u32[]{:S(2)}) collective-permute-start(bf16[256,512]{1,0:T(8,128)(2,1)} %collective-permute-done.3.refs_3_), channel_id=1, source_target_pairs={{0,4},{4,8},{8,12},{12,14},{14,10},{10,6},{6,2},{2,0},{1,5},{5,9},... | collective-permute-start | bytes 786440 | tf_op jit(solution)/shard_map/ppermute | solution.py:139
  25.6 11.6 %collective-permute-start.9 = (bf16[256,512]{1,0:T(8,128)(2,1)}, bf16[256,512]{1,0:T(8,128)(2,1)}, u32[]{:S(2)}, u32[]{:S(2)}) collective-permute-start(bf16[256,512]{1,0:T(8,128)(2,1)} %collective-permute-done.4.refs_4_), channel_id=1, source_target_pairs={{4,0},{8,4},{12,8},{14,12},{10,14},{6,10},{2,6},{0,2},{5,1},{9,5},... | collective-permute-start | bytes 786440 | tf_op jit(solution)/shard_map/ppermute | solution.py:139
  31.8 12.9 %collective-permute-start.14 = (bf16[256,512]{1,0:T(8,128)(2,1)}, bf16[256,512]{1,0:T(8,128)(2,1)S(1)}, u32[]{:S(2)}, u32[]{:S(2)}) collective-permute-start(bf16[256,512]{1,0:T(8,128)(2,1)} %collective-permute-done.10.refs_3_), channel_id=1, source_target_pairs={{4,0},{8,4},{12,8},{14,12},{10,14},{6,10},{2,6},{0,2},{5,1},{9,5},... | collective-permute-start | bytes 786440 | tf_op jit(solution)/shard_map/ppermute | solution.py:139
  37.1 11.1 %collective-permute-start.13 = (bf16[256,512]{1,0:T(8,128)(2,1)}, bf16[256,512]{1,0:T(8,128)(2,1)S(1)}, u32[]{:S(2)}, u32[]{:S(2)}) collective-permute-start(bf16[256,512]{1,0:T(8,128)(2,1)} %collective-permute-done.9.refs_2_), channel_id=1, source_target_pairs={{4,0},{8,4},{12,8},{14,12},{10,14},{6,10},{2,6},{0,2},{5,1},{9,5},... | collective-permute-start | bytes 786440 | tf_op jit(solution)/shard_map/ppermute | solution.py:139
  37.6 11.1 %collective-permute-start.12 = (bf16[256,512]{1,0:T(8,128)(2,1)}, bf16[256,512]{1,0:T(8,128)(2,1)}, u32[]{:S(2)}, u32[]{:S(2)}) collective-permute-start(bf16[256,512]{1,0:T(8,128)(2,1)} %collective-permute-done.8.refs_1_), channel_id=1, source_target_pairs={{0,4},{4,8},{8,12},{12,14},{14,10},{10,6},{6,2},{2,0},{1,5},{5,9},... | collective-permute-start | bytes 786440 | tf_op jit(solution)/shard_map/ppermute | solution.py:139
  39.2 11.1 %collective-permute-start.7 = (bf16[256,512]{1,0:T(8,128)(2,1)}, bf16[256,512]{1,0:T(8,128)(2,1)}, u32[]{:S(2)}, u32[]{:S(2)}) collective-permute-start(bf16[256,512]{1,0:T(8,128)(2,1)} %collective-permute-done.6.refs_0_), channel_id=1, source_target_pairs={{0,4},{4,8},{8,12},{12,14},{14,10},{10,6},{6,2},{2,0},{1,5},{5,9},... | collective-permute-start | bytes 786440 | tf_op jit(solution)/shard_map/ppermute | solution.py:139
  44.7 11.0 %collective-permute-start.18 = (bf16[256,512]{1,0:T(8,128)(2,1)S(1)}, bf16[256,512]{1,0:T(8,128)(2,1)}, u32[]{:S(2)}, u32[]{:S(2)}) collective-permute-start(bf16[256,512]{1,0:T(8,128)(2,1)S(1)} %collective-permute-done.14.refs_3_), channel_id=1, source_target_pairs={{4,0},{8,4},{12,8},{14,12},{10,14},{6,10},{2,6},{0,2},{5,1},{9,5},... | collective-permute-start | bytes 786440 | tf_op jit(solution)/shard_map/ppermute | solution.py:139
  48.3 11.5 %collective-permute-start.17 = (bf16[256,512]{1,0:T(8,128)(2,1)S(1)}, bf16[256,512]{1,0:T(8,128)(2,1)}, u32[]{:S(2)}, u32[]{:S(2)}) collective-permute-start(bf16[256,512]{1,0:T(8,128)(2,1)S(1)} %collective-permute-done.13.refs_2_), channel_id=1, source_target_pairs={{4,0},{8,4},{12,8},{14,12},{10,14},{6,10},{2,6},{0,2},{5,1},{9,5},... | collective-permute-start | bytes 786440 | tf_op jit(solution)/shard_map/ppermute | solution.py:139
  48.7 11.5 %collective-permute-start.16 = (bf16[256,512]{1,0:T(8,128)(2,1)}, bf16[256,512]{1,0:T(8,128)(2,1)}, u32[]{:S(2)}, u32[]{:S(2)}) collective-permute-start(bf16[256,512]{1,0:T(8,128)(2,1)} %collective-permute-done.12.refs_1_), channel_id=1, source_target_pairs={{0,4},{4,8},{8,12},{12,14},{14,10},{10,6},{6,2},{2,0},{1,5},{5,9},... | collective-permute-start | bytes 786440 | tf_op jit(solution)/shard_map/ppermute | solution.py:139
  50.3 11.5 %collective-permute-start.11 = (bf16[256,512]{1,0:T(8,128)(2,1)}, bf16[256,512]{1,0:T(8,128)(2,1)}, u32[]{:S(2)}, u32[]{:S(2)}) collective-permute-start(bf16[256,512]{1,0:T(8,128)(2,1)} %collective-permute-done.7.refs_0_), channel_id=1, source_target_pairs={{0,4},{4,8},{8,12},{12,14},{14,10},{10,6},{6,2},{2,0},{1,5},{5,9},... | collective-permute-start | bytes 786440 | tf_op jit(solution)/shard_map/ppermute | solution.py:139
  55.7 11.6 %collective-permute-start.22 = (bf16[256,512]{1,0:T(8,128)(2,1)}, bf16[256,512]{1,0:T(8,128)(2,1)S(1)}, u32[]{:S(2)}, u32[]{:S(2)}) collective-permute-start(bf16[256,512]{1,0:T(8,128)(2,1)} %collective-permute-done.18.refs_3_), channel_id=1, source_target_pairs={{4,0},{8,4},{12,8},{14,12},{10,14},{6,10},{2,6},{0,2},{5,1},{9,5},... | collective-permute-start | bytes 786440 | tf_op jit(solution)/shard_map/ppermute | solution.py:139
  59.8 11.1 %collective-permute-start.21 = (bf16[256,512]{1,0:T(8,128)(2,1)}, bf16[256,512]{1,0:T(8,128)(2,1)S(1)}, u32[]{:S(2)}, u32[]{:S(2)}) collective-permute-start(bf16[256,512]{1,0:T(8,128)(2,1)} %collective-permute-done.17.refs_2_), channel_id=1, source_target_pairs={{4,0},{8,4},{12,8},{14,12},{10,14},{6,10},{2,6},{0,2},{5,1},{9,5},... | collective-permute-start | bytes 786440 | tf_op jit(solution)/shard_map/ppermute | solution.py:139
  60.2 11.1 %collective-permute-start.20 = (bf16[256,512]{1,0:T(8,128)(2,1)}, bf16[256,512]{1,0:T(8,128)(2,1)}, u32[]{:S(2)}, u32[]{:S(2)}) collective-permute-start(bf16[256,512]{1,0:T(8,128)(2,1)} %collective-permute-done.16.refs_1_), channel_id=1, source_target_pairs={{0,4},{4,8},{8,12},{12,14},{14,10},{10,6},{6,2},{2,0},{1,5},{5,9},... | collective-permute-start | bytes 786440 | tf_op jit(solution)/shard_map/ppermute | solution.py:139
  61.8 11.1 %collective-permute-start.15 = (bf16[256,512]{1,0:T(8,128)(2,1)}, bf16[256,512]{1,0:T(8,128)(2,1)}, u32[]{:S(2)}, u32[]{:S(2)}) collective-permute-start(bf16[256,512]{1,0:T(8,128)(2,1)} %collective-permute-done.11.refs_0_), channel_id=1, source_target_pairs={{0,4},{4,8},{8,12},{12,14},{14,10},{10,6},{6,2},{2,0},{1,5},{5,9},... | collective-permute-start | bytes 786440 | tf_op jit(solution)/shard_map/ppermute | solution.py:139
  67.3 11.0 %collective-permute-start.28 = (bf16[256,512]{1,0:T(8,128)(2,1)S(1)}, bf16[256,512]{1,0:T(8,128)(2,1)S(1)}, u32[]{:S(2)}, u32[]{:S(2)}) collective-permute-start(bf16[256,512]{1,0:T(8,128)(2,1)S(1)} %collective-permute-done.22.refs_3_), channel_id=1, source_target_pairs={{4,0},{8,4},{12,8},{14,12},{10,14},{6,10},{2,6},{0,2},{5,1},{9,5},... | collective-permute-start | bytes 786440 | tf_op jit(solution)/shard_map/ppermute | solution.py:139
  70.9 11.3 %collective-permute-start.26 = (bf16[256,512]{1,0:T(8,128)(2,1)S(1)}, bf16[256,512]{1,0:T(8,128)(2,1)S(1)}, u32[]{:S(2)}, u32[]{:S(2)}) collective-permute-start(bf16[256,512]{1,0:T(8,128)(2,1)S(1)} %collective-permute-done.21.refs_2_), channel_id=1, source_target_pairs={{4,0},{8,4},{12,8},{14,12},{10,14},{6,10},{2,6},{0,2},{5,1},{9,5},... | collective-permute-start | bytes 786440 | tf_op jit(solution)/shard_map/ppermute | solution.py:139
  71.3 11.4 %collective-permute-start.24 = (bf16[256,512]{1,0:T(8,128)(2,1)}, bf16[256,512]{1,0:T(8,128)(2,1)}, u32[]{:S(2)}, u32[]{:S(2)}) collective-permute-start(bf16[256,512]{1,0:T(8,128)(2,1)} %collective-permute-done.20.refs_1_), channel_id=1, source_target_pairs={{0,4},{4,8},{8,12},{12,14},{14,10},{10,6},{6,2},{2,0},{1,5},{5,9},... | collective-permute-start | bytes 786440 | tf_op jit(solution)/shard_map/ppermute | solution.py:139
  72.9 11.3 %collective-permute-start.19 = (bf16[256,512]{1,0:T(8,128)(2,1)}, bf16[256,512]{1,0:T(8,128)(2,1)}, u32[]{:S(2)}, u32[]{:S(2)}) collective-permute-start(bf16[256,512]{1,0:T(8,128)(2,1)} %collective-permute-done.15.refs_0_), channel_id=1, source_target_pairs={{0,4},{4,8},{8,12},{12,14},{14,10},{10,6},{6,2},{2,0},{1,5},{5,9},... | collective-permute-start | bytes 786440 | tf_op jit(solution)/shard_map/ppermute | solution.py:139
  78.3 11.3 %collective-permute-start.29 = (bf16[256,512]{1,0:T(8,128)(2,1)S(1)}, bf16[256,512]{1,0:T(8,128)(2,1)S(1)}, u32[]{:S(2)}, u32[]{:S(2)}) collective-permute-start(bf16[256,512]{1,0:T(8,128)(2,1)S(1)} %collective-permute-done.28.refs_3_), channel_id=1, source_target_pairs={{4,0},{8,4},{12,8},{14,12},{10,14},{6,10},{2,6},{0,2},{5,1},{9,5},... | collective-permute-start | bytes 786440 | tf_op jit(solution)/shard_map/ppermute | solution.py:139
  82.2 8.9 %collective-permute-start.27 = (bf16[256,512]{1,0:T(8,128)(2,1)S(1)}, bf16[256,512]{1,0:T(8,128)(2,1)S(1)}, u32[]{:S(2)}, u32[]{:S(2)}) collective-permute-start(bf16[256,512]{1,0:T(8,128)(2,1)S(1)} %collective-permute-done.26.refs_2_), channel_id=1, source_target_pairs={{4,0},{8,4},{12,8},{14,12},{10,14},{6,10},{2,6},{0,2},{5,1},{9,5},... | collective-permute-start | bytes 786440 | tf_op jit(solution)/shard_map/ppermute | solution.py:139
  82.7 9.1 %collective-permute-start.25 = (bf16[256,512]{1,0:T(8,128)(2,1)}, bf16[256,512]{1,0:T(8,128)(2,1)}, u32[]{:S(2)}, u32[]{:S(2)}) collective-permute-start(bf16[256,512]{1,0:T(8,128)(2,1)} %collective-permute-done.24.refs_1_), channel_id=1, source_target_pairs={{0,4},{4,8},{8,12},{12,14},{14,10},{10,6},{6,2},{2,0},{1,5},{5,9},... | collective-permute-start | bytes 786440 | tf_op jit(solution)/shard_map/ppermute | solution.py:139
  84.2 8.1 %collective-permute-start.23 = (bf16[256,512]{1,0:T(8,128)(2,1)}, bf16[256,512]{1,0:T(8,128)(2,1)}, u32[]{:S(2)}, u32[]{:S(2)}) collective-permute-start(bf16[256,512]{1,0:T(8,128)(2,1)} %collective-permute-done.19.refs_0_), channel_id=1, source_target_pairs={{0,4},{4,8},{8,12},{12,14},{14,10},{10,6},{6,2},{2,0},{1,5},{5,9},... | collective-permute-start | bytes 786440 | tf_op jit(solution)/shard_map/ppermute | solution.py:139
  89.6 0.7 copy-start.4
  91.1 0.7 copy-start.6
  92.3 1.0 copy-start.5
  93.2 0.9 copy-start.7
  94.2 4.8 %copy-start.11 = (s32[4]{0:T(128)S(1)}, s32[4]{0:T(128)}, u32[]{:S(2)}) copy-start(s32[4]{0:T(128)} %param.13) | copy-start | bytes 52
  94.2 8.6 %copy-start.1 = (bf16[512,1024]{1,0:T(8,128)(2,1)S(1)}, bf16[512,1024]{1,0:T(8,128)(2,1)}, u32[]{:S(2)}) copy-start(bf16[512,1024]{1,0:T(8,128)(2,1)} %key_any.1) | copy-start | bytes 3145732
  98.9 2.9 %collective-permute-start.30 = (bf16[1024,512]{1,0:T(8,128)(2,1)}, bf16[1024,512]{1,0:T(8,128)(2,1)S(1)}, u32[]{:S(2)}, u32[]{:S(2)}) collective-permute-start(bf16[1024,512]{1,0:T(8,128)(2,1)} %get-tuple-element.84.have_any), channel_id=1, source_target_pairs={{0,1},{1,0},{2,3},{3,2},{4,5},{5,4},{6,7},{7,6},{8,9},{9,8},{10,11... | collective-permute-start | bytes 3145736 | tf_op jit(solution)/shard_map/ppermute | solution.py:274
  101.8 1.0 copy-start.8
  102.8 1.2 copy-start.2
  104.0 1.2 copy-start.9
  105.3 4.8 %copy-start.10 = (bf16[4,4,1024]{2,1,0:T(4,128)(2,1)S(1)}, bf16[4,4,1024]{2,1,0:T(4,128)(2,1)}, u32[]{:S(2)}) copy-start(bf16[4,4,1024]{2,1,0:T(4,128)(2,1)} %param.15) | copy-start | bytes 98308
  105.3 5.1 %copy-start.3 = (bf16[512,1024]{1,0:T(8,128)(2,1)S(1)}, bf16[512,1024]{1,0:T(8,128)(2,1)}, u32[]{:S(2)}) copy-start(bf16[512,1024]{1,0:T(8,128)(2,1)} %value_any.1) | copy-start | bytes 3145732
  111.4 14.7 %all-to-all-start = ((f32[8,72,128]{2,1,0:T(8,128)}), f32[8,72,128]{2,1,0:T(8,128)S(1)}, u32[]{:S(2)}, u32[]{:S(2)}) async-start(f32[8,72,128]{2,1,0:T(8,128)} %bitcast.25), calls=%async_computation | async-start | bytes 589824 | tf_op jit(solution)/shard_map/all_to_all | solution.py:306
  126.5 3.8 %collective-permute-start.31 = (bf16[64,128]{1,0:T(8,128)(2,1)S(1)}, bf16[64,128]{1,0:T(8,128)(2,1)S(1)}, u32[]{:S(2)}, u32[]{:S(2)}) collective-permute-start(bf16[64,128]{1,0:T(8,128)(2,1)S(1)} %shard_map.90), channel_id=1, source_target_pairs={{0,2},{2,0},{4,6},{6,4},{8,10},{10,8},{12,14},{14,12},{1,3},{3,1},... | collective-permute-start | bytes 49160 | tf_op jit(solution)/shard_map/ppermute | solution.py:310
  130.3 5.8 %collective-permute-start.32 = (bf16[128,128]{1,0:T(8,128)(2,1)S(1)}, bf16[128,128]{1,0:T(8,128)(2,1)S(1)}, u32[]{:S(2)}, u32[]{:S(2)}) collective-permute-start(bf16[128,128]{1,0:T(8,128)(2,1)S(1)} %pad_maximum_fusion.2), channel_id=1, source_target_pairs={{0,12},{2,14},{4,8},{6,10},{8,4},{10,6},{12,0},{14,2},{1,13},{3,15... | collective-permute-start | bytes 98312 | tf_op jit(solution)/shard_map/ppermute | solution.py:313
  131.5 5.3 %collective-permute-start.33 = (bf16[128,128]{1,0:T(8,128)(2,1)S(1)}, bf16[128,128]{1,0:T(8,128)(2,1)S(1)}, u32[]{:S(2)}, u32[]{:S(2)}) collective-permute-start(bf16[128,128]{1,0:T(8,128)(2,1)S(1)} %pad_maximum_fusion.2), channel_id=1, source_target_pairs={{0,8},{2,10},{4,12},{6,14},{8,0},{10,2},{12,4},{14,6},{1,9},{3,11}... | collective-permute-start | bytes 98312 | tf_op jit(solution)/shard_map/ppermute | solution.py:313
  132.9 4.2 %collective-permute-start.34 = (bf16[128,128]{1,0:T(8,128)(2,1)S(1)}, bf16[128,128]{1,0:T(8,128)(2,1)S(1)}, u32[]{:S(2)}, u32[]{:S(2)}) collective-permute-start(bf16[128,128]{1,0:T(8,128)(2,1)S(1)} %pad_maximum_fusion.2), channel_id=1, source_target_pairs={{0,4},{2,6},{4,0},{6,2},{8,12},{10,14},{12,8},{14,10},{1,5},{3,7},... | collective-permute-start | bytes 98312 | tf_op jit(solution)/shard_map/ppermute | solution.py:313
  137.2 1.4 %collective-permute-start.35 = (bf16[16,1,4096]{2,0,1:T(8,128)(2,1)S(1)}, bf16[16,1,4096]{2,0,1:T(8,128)(2,1)S(1)}, u32[]{:S(2)}, u32[]{:S(2)}) collective-permute-start(bf16[16,1,4096]{2,0,1:T(8,128)(2,1)S(1)} %reshape.97), channel_id=1, source_target_pairs={{0,1},{1,0},{2,3},{3,2},{4,5},{5,4},{6,7},{7,6},{8,9},{9,8},{10,11... | collective-permute-start | bytes 393224 | tf_op jit(solution)/shard_map/ppermute | solution.py:323

commit v10 on v9

--- a/solution.py
+++ b/solution.py
@@ -83,7 +83,7 @@
             pltpu.SemaphoreType.DMA((count,)),
         ],
         input_output_aliases={} if total is None or last else {3 + count: 0},
-        compiler_params=pltpu.CompilerParams(vmem_limit_bytes=30 * 2**20),
+        compiler_params=pltpu.CompilerParams(vmem_limit_bytes=20 * 2**20),
         cost_estimate=pl.CostEstimate(
             flops=4 * tok_rows * deep * width, bytes_accessed=4 * tok_rows * deep, transcendentals=0
         ),
@@ -167,9 +167,11 @@
         copies = [pltpu.make_async_copy(source, target, sems.at[k]) for k, (source, target) in enumerate(pairs_of)]
         for copy in copies:
             copy.start()
-        for copy in copies:
+        for copy in copies[:3]:
             copy.wait()
         keys = mm(latents[0], ups[0]).astype(BF)
+        for copy in copies[3:]:
+            copy.wait()
         values = mm(latents[1], ups[1]).astype(BF)
         position = lax.broadcasted_iota(jnp.int32, (tokens, rows), 0)
         visible = (position >= bounds_ref[0:1, :]) & (position < bounds_ref[1:2, :])
@@ -200,6 +202,7 @@
             out_ref[chip, blocks] = jnp.zeros((8, DH), F32)
             out_ref[chip, blocks, :, : 2 * blocks] = jnp.concatenate(sides, 1)
 
+    ups = [pltpu.with_memory_space_constraint(x, pltpu.HBM) for x in (key_up, value_up)]
     in_vmem = pl.BlockSpec(memory_space=pltpu.VMEM)
     return pl.pallas_call(
         kernel,
@@ -212,13 +215,13 @@
             pltpu.VMEM(query.shape, BF),
             pltpu.SemaphoreType.DMA((5,)),
         ],
-        compiler_params=pltpu.CompilerParams(vmem_limit_bytes=24 * 2**20),
+        compiler_params=pltpu.CompilerParams(vmem_limit_bytes=16 * 2**20),
         cost_estimate=pl.CostEstimate(
             flops=4 * tokens * (have.shape[1] * heads * DH + heads * rows * DH),
             bytes_accessed=4 * tokens * have.shape[1],
             transcendentals=tokens * heads * rows,
         ),
-    )(core.reshape(1), have, got, key_up, value_up, query, bounds)
+    )(core.reshape(1), have, got, *ups, query, bounds)
 
 
 def merge(arrived, fresh_stats, fresh_summed):

time: 140 us -> 136 us (0.971)
  local copies, waits for them, and re-layouts: 9.2 us -> 3.2 us
    unnamed x24 -> x8, local copies, waits for them, and re-layouts: 6.77 us -> 0.02 us
    ppermute x28, waiting for transfers between devices: 32.4 us -> 33.8 us  [project(): held[k] = lax.ppermute(held[k], 'chip', ways[k])]
where the time goes in v10:
time: 136 us
  waiting for transfers between devices  52.1 us (38%)
  starting transfers between devices  41.2 us (30%)
  Pallas kernels  34.8 us (26%)
  local copies, waits for them, and re-layouts  3.2 us (2%)
  other arithmetic  2.42 us (2%)
  matrix products  1.51 us (1%)
    ppermute x28, waiting for transfers between devices, project(): held[k] = lax.ppermute(held[k], 'chip', ways[k])  33.8 us
    ppermute x28, starting transfers between devices, project(): held[k] = lax.ppermute(held[k], 'chip', ways[k])  29.3 us
    pallas_call x7, Pallas kernels, add_pieces(): pl.pallas_call(kernel, out_shape=(jax.ShapeDtypeStruct((2 * tok_rows, wid...  29.3 us
    all_to_all x1, waiting for transfers between devices, on_device(): lax.all_to_all(flat, 'chip', split_axis=0, concat_axis=0, tiled=True)  8.61 us
    pallas_call x1, Pallas kernels, attend(): pl.pallas_call(kernel, out_shape=jax.ShapeDtypeStruct((chips, blocks + 1,...  5.14 us
    all_to_all x1, starting transfers between devices, on_device(): lax.all_to_all(flat, 'chip', split_axis=0, concat_axis=0, tiled=True)  4.83 us
    ppermute x3, starting transfers between devices, on_device(): lax.ppermute(couple, 'chip', [(c, c ^ 2 * d) for c in range(chips)])  4.45 us
  transfers between devices with their start and end apart: 37, of which 18 were waited for; matrix products, arithmetic and copies ran while one was open for 2% of the time, Pallas kernels for 18%

profile of v10, /device:TPU:0, one launch (start us, length us, event | category | flops | bytes accessed | tf_op | source)
XLA Modules:
  0.0 135.6 jit_solution(11299367146652342587)
XLA Ops:
  0.0 1.3 broadcast_select_fusion
  1.3 0.5 collective-permute-start
  1.8 1.5 %collective-permute-done.refs_1_ = bf16[512,512]{1,0:T(8,128)(2,1)S(1)} collective-permute-done((bf16[512,512]{1,0:T(8,128)(2,1)S(1)}, bf16[512,512]{1,0:T(8,128)(2,1)S(1)}, u32[]{:S(2)}, u32[]{:S(2)}) %collective-permute-start) | collective-permute-done | bytes 524320 | tf_op jit(solution)/shard_map/ppermute | solution.py:101
  3.4 0.4 collective-permute-start.1
  3.8 2.8 %collective-permute-start.2 = (bf16[256,512]{1,0:T(8,128)(2,1)S(1)}, bf16[256,512]{1,0:T(8,128)(2,1)}, u32[]{:S(2)}, u32[]{:S(2)}) collective-permute-start(bf16[256,512]{1,0:T(8,128)(2,1)S(1)} %get-tuple-element.94), channel_id=1, source_target_pairs={{0,4},{4,8},{8,12},{12,14},{14,10},{10,6},{6,2},{2,0},{1,5},{5,9},... | collective-permute-start | bytes 786440 | tf_op jit(solution)/shard_map/ppermute | solution.py:139
  6.6 1.6 %collective-permute-start.3 = (bf16[256,512]{1,0:T(8,128)(2,1)S(1)}, bf16[256,512]{1,0:T(8,128)(2,1)}, u32[]{:S(2)}, u32[]{:S(2)}) collective-permute-start(bf16[256,512]{1,0:T(8,128)(2,1)S(1)} %get-tuple-element.93), channel_id=1, source_target_pairs={{0,4},{4,8},{8,12},{12,14},{14,10},{10,6},{6,2},{2,0},{1,5},{5,9},... | collective-permute-start | bytes 786440 | tf_op jit(solution)/shard_map/ppermute | solution.py:139
  8.2 0.5 collective-permute-start.4
  8.7 5.0 %collective-permute-done.2.refs_2_ = bf16[256,512]{1,0:T(8,128)(2,1)} collective-permute-done((bf16[256,512]{1,0:T(8,128)(2,1)S(1)}, bf16[256,512]{1,0:T(8,128)(2,1)}, u32[]{:S(2)}, u32[]{:S(2)}) %collective-permute-start.2) | collective-permute-done | bytes 262176 | tf_op jit(solution)/shard_map/ppermute | solution.py:139
  13.8 5.3 %collective-permute-done.3.refs_3_ = bf16[256,512]{1,0:T(8,128)(2,1)} collective-permute-done((bf16[256,512]{1,0:T(8,128)(2,1)S(1)}, bf16[256,512]{1,0:T(8,128)(2,1)}, u32[]{:S(2)}, u32[]{:S(2)}) %collective-permute-start.3) | collective-permute-done | bytes 262176 | tf_op jit(solution)/shard_map/ppermute | solution.py:139
  19.1 2.9 %collective-permute-done.5.refs_5_ = bf16[256,512]{1,0:T(8,128)(2,1)} collective-permute-done((bf16[256,512]{1,0:T(8,128)(2,1)S(1)}, bf16[256,512]{1,0:T(8,128)(2,1)}, u32[]{:S(2)}, u32[]{:S(2)}) %collective-permute-start.5) | collective-permute-done | bytes 262176 | tf_op jit(solution)/shard_map/ppermute | solution.py:139
  22.0 0.4 collective-permute-start.10
  22.4 1.6 %collective-permute-start.6 = (bf16[256,512]{1,0:T(8,128)(2,1)}, bf16[256,512]{1,0:T(8,128)(2,1)}, u32[]{:S(2)}, u32[]{:S(2)}) collective-permute-start(bf16[256,512]{1,0:T(8,128)(2,1)} %collective-permute-done.2.refs_2_), channel_id=1, source_target_pairs={{0,4},{4,8},{8,12},{12,14},{14,10},{10,6},{6,2},{2,0},{1,5},{5,9},... | collective-permute-start | bytes 786440 | tf_op jit(solution)/shard_map/ppermute | solution.py:139
  24.0 1.6 %collective-permute-start.8 = (bf16[256,512]{1,0:T(8,128)(2,1)}, bf16[256,512]{1,0:T(8,128)(2,1)}, u32[]{:S(2)}, u32[]{:S(2)}) collective-permute-start(bf16[256,512]{1,0:T(8,128)(2,1)} %collective-permute-done.3.refs_3_), channel_id=1, source_target_pairs={{0,4},{4,8},{8,12},{12,14},{14,10},{10,6},{6,2},{2,0},{1,5},{5,9},... | collective-permute-start | bytes 786440 | tf_op jit(solution)/shard_map/ppermute | solution.py:139
  25.6 0.4 collective-permute-start.9
  26.1 5.7 %shard_map.82 = (f32[1024,512]{1,0:T(8,128)S(1)}, f32[8,128]{1,0:T(8,128)}) custom-call(s32[4]{0:T(128)S(1)} %pad_add_fusion.1.places_ref, bf16[512,8192]{1,0:T(8,128)(2,1)} %mine_ref.13, bf16[512,8192]{1,0:T(8,128)(2,1)} %collective-permute-done.1.theirs_ref, bf16[512,512]{1,0:T(8,128)(2,1)S(1)} %get-tuple-element.89.refs_0_, ...), custom_call_target="tpu_custom_call" | custom-call | flops 2147483648 | bytes 4194304 | tf_op jit(solution)/shard_map/pallas_call | solution.py:71
  31.8 0.5 collective-permute-start.14
  32.3 4.8 %collective-permute-done.9.refs_2_ = bf16[256,512]{1,0:T(8,128)(2,1)} collective-permute-done((bf16[256,512]{1,0:T(8,128)(2,1)}, bf16[256,512]{1,0:T(8,128)(2,1)}, u32[]{:S(2)}, u32[]{:S(2)}) %collective-permute-start.9) | collective-permute-done | bytes 262176 | tf_op jit(solution)/shard_map/ppermute | solution.py:139
  37.1 0.4 collective-permute-start.13
  37.6 1.6 %collective-permute-start.12 = (bf16[256,512]{1,0:T(8,128)(2,1)}, bf16[256,512]{1,0:T(8,128)(2,1)}, u32[]{:S(2)}, u32[]{:S(2)}) collective-permute-start(bf16[256,512]{1,0:T(8,128)(2,1)} %collective-permute-done.8.refs_1_), channel_id=1, source_target_pairs={{0,4},{4,8},{8,12},{12,14},{14,10},{10,6},{6,2},{2,0},{1,5},{5,9},... | collective-permute-start | bytes 786440 | tf_op jit(solution)/shard_map/ppermute | solution.py:139
  39.2 1.6 %collective-permute-start.7 = (bf16[256,512]{1,0:T(8,128)(2,1)}, bf16[256,512]{1,0:T(8,128)(2,1)}, u32[]{:S(2)}, u32[]{:S(2)}) collective-permute-start(bf16[256,512]{1,0:T(8,128)(2,1)} %collective-permute-done.6.refs_0_), channel_id=1, source_target_pairs={{0,4},{4,8},{8,12},{12,14},{14,10},{10,6},{6,2},{2,0},{1,5},{5,9},... | collective-permute-start | bytes 786440 | tf_op jit(solution)/shard_map/ppermute | solution.py:139
  40.8 3.9 %shard_map.83 = (f32[1024,512]{1,0:T(8,128)S(1)}, f32[8,128]{1,0:T(8,128)}) custom-call(s32[2]{0:T(128)S(1)} %pad_add_fusion.2.places_ref, bf16[512,8192]{1,0:T(8,128)(2,1)} %mine_ref.13, bf16[512,8192]{1,0:T(8,128)(2,1)} %collective-permute-done.1.theirs_ref, bf16[256,512]{1,0:T(8,128)(2,1)} %collective-permute-done.6.refs_0_, ...), custom_call_target="tpu_custom_call", output_to_operand_aliasing={{0}: (7, {})} | custom-call | flops 1073741824 | bytes 2097152 | tf_op jit(solution)/shard_map/pallas_call | solution.py:71
  44.7 0.5 collective-permute-start.18
  45.2 3.0 %collective-permute-done.13.refs_2_ = bf16[256,512]{1,0:T(8,128)(2,1)S(1)} collective-permute-done((bf16[256,512]{1,0:T(8,128)(2,1)}, bf16[256,512]{1,0:T(8,128)(2,1)S(1)}, u32[]{:S(2)}, u32[]{:S(2)}) %collective-permute-start.13) | collective-permute-done | bytes 262176 | tf_op jit(solution)/shard_map/ppermute | solution.py:139
  48.3 0.4 collective-permute-start.17
  48.7 1.6 %collective-permute-start.16 = (bf16[256,512]{1,0:T(8,128)(2,1)}, bf16[256,512]{1,0:T(8,128)(2,1)}, u32[]{:S(2)}, u32[]{:S(2)}) collective-permute-start(bf16[256,512]{1,0:T(8,128)(2,1)} %collective-permute-done.12.refs_1_), channel_id=1, source_target_pairs={{0,4},{4,8},{8,12},{12,14},{14,10},{10,6},{6,2},{2,0},{1,5},{5,9},... | collective-permute-start | bytes 786440 | tf_op jit(solution)/shard_map/ppermute | solution.py:139
  50.3 1.6 %collective-permute-start.11 = (bf16[256,512]{1,0:T(8,128)(2,1)}, bf16[256,512]{1,0:T(8,128)(2,1)}, u32[]{:S(2)}, u32[]{:S(2)}) collective-permute-start(bf16[256,512]{1,0:T(8,128)(2,1)} %collective-permute-done.7.refs_0_), channel_id=1, source_target_pairs={{0,4},{4,8},{8,12},{12,14},{14,10},{10,6},{6,2},{2,0},{1,5},{5,9},... | collective-permute-start | bytes 786440 | tf_op jit(solution)/shard_map/ppermute | solution.py:139
  52.0 3.7 %shard_map.84 = (f32[1024,512]{1,0:T(8,128)S(1)}, f32[8,128]{1,0:T(8,128)}) custom-call(s32[2]{0:T(128)S(1)} %pad_add_fusion.3.places_ref, bf16[512,8192]{1,0:T(8,128)(2,1)} %mine_ref.13, bf16[512,8192]{1,0:T(8,128)(2,1)} %collective-permute-done.1.theirs_ref, bf16[256,512]{1,0:T(8,128)(2,1)} %collective-permute-done.7.refs_0_, ...), custom_call_target="tpu_custom_call", output_to_operand_aliasing={{0}: (7, {})} | custom-call | flops 1073741824 | bytes 2097152 | tf_op jit(solution)/shard_map/pallas_call | solution.py:71
  55.7 0.5 collective-permute-start.22
  56.2 3.5 %collective-permute-done.17.refs_2_ = bf16[256,512]{1,0:T(8,128)(2,1)} collective-permute-done((bf16[256,512]{1,0:T(8,128)(2,1)S(1)}, bf16[256,512]{1,0:T(8,128)(2,1)}, u32[]{:S(2)}, u32[]{:S(2)}) %collective-permute-start.17) | collective-permute-done | bytes 262176 | tf_op jit(solution)/shard_map/ppermute | solution.py:139
  59.8 0.4 collective-permute-start.21
  60.2 1.6 %collective-permute-start.20 = (bf16[256,512]{1,0:T(8,128)(2,1)}, bf16[256,512]{1,0:T(8,128)(2,1)}, u32[]{:S(2)}, u32[]{:S(2)}) collective-permute-start(bf16[256,512]{1,0:T(8,128)(2,1)} %collective-permute-done.16.refs_1_), channel_id=1, source_target_pairs={{0,4},{4,8},{8,12},{12,14},{14,10},{10,6},{6,2},{2,0},{1,5},{5,9},... | collective-permute-start | bytes 786440 | tf_op jit(solution)/shard_map/ppermute | solution.py:139
  61.8 1.5 %collective-permute-start.15 = (bf16[256,512]{1,0:T(8,128)(2,1)}, bf16[256,512]{1,0:T(8,128)(2,1)}, u32[]{:S(2)}, u32[]{:S(2)}) collective-permute-start(bf16[256,512]{1,0:T(8,128)(2,1)} %collective-permute-done.11.refs_0_), channel_id=1, source_target_pairs={{0,4},{4,8},{8,12},{12,14},{14,10},{10,6},{6,2},{2,0},{1,5},{5,9},... | collective-permute-start | bytes 786440 | tf_op jit(solution)/shard_map/ppermute | solution.py:139
  63.4 3.9 %shard_map.85 = (f32[1024,512]{1,0:T(8,128)S(1)}, f32[8,128]{1,0:T(8,128)}) custom-call(s32[2]{0:T(128)S(1)} %pad_add_fusion.4.places_ref, bf16[512,8192]{1,0:T(8,128)(2,1)} %mine_ref.13, bf16[512,8192]{1,0:T(8,128)(2,1)} %collective-permute-done.1.theirs_ref, bf16[256,512]{1,0:T(8,128)(2,1)} %collective-permute-done.11.refs_0_, ...), custom_call_target="tpu_custom_call", output_to_operand_aliasing={{0}: (7, {})} | custom-call | flops 1073741824 | bytes 2097152 | tf_op jit(solution)/shard_map/pallas_call | solution.py:71
  67.3 0.6 collective-permute-start.28
  67.8 3.0 %collective-permute-done.21.refs_2_ = bf16[256,512]{1,0:T(8,128)(2,1)S(1)} collective-permute-done((bf16[256,512]{1,0:T(8,128)(2,1)}, bf16[256,512]{1,0:T(8,128)(2,1)S(1)}, u32[]{:S(2)}, u32[]{:S(2)}) %collective-permute-start.21) | collective-permute-done | bytes 262176 | tf_op jit(solution)/shard_map/ppermute | solution.py:139
  70.9 0.4 collective-permute-start.26
  71.3 1.6 %collective-permute-start.24 = (bf16[256,512]{1,0:T(8,128)(2,1)}, bf16[256,512]{1,0:T(8,128)(2,1)}, u32[]{:S(2)}, u32[]{:S(2)}) collective-permute-start(bf16[256,512]{1,0:T(8,128)(2,1)} %collective-permute-done.20.refs_1_), channel_id=1, source_target_pairs={{0,4},{4,8},{8,12},{12,14},{14,10},{10,6},{6,2},{2,0},{1,5},{5,9},... | collective-permute-start | bytes 786440 | tf_op jit(solution)/shard_map/ppermute | solution.py:139
  72.9 1.5 %collective-permute-start.19 = (bf16[256,512]{1,0:T(8,128)(2,1)}, bf16[256,512]{1,0:T(8,128)(2,1)}, u32[]{:S(2)}, u32[]{:S(2)}) collective-permute-start(bf16[256,512]{1,0:T(8,128)(2,1)} %collective-permute-done.15.refs_0_), channel_id=1, source_target_pairs={{0,4},{4,8},{8,12},{12,14},{14,10},{10,6},{6,2},{2,0},{1,5},{5,9},... | collective-permute-start | bytes 786440 | tf_op jit(solution)/shard_map/ppermute | solution.py:139
  74.5 3.7 %shard_map.86 = (f32[1024,512]{1,0:T(8,128)S(1)}, f32[8,128]{1,0:T(8,128)}) custom-call(s32[2]{0:T(128)S(1)} %pad_add_fusion.5.places_ref, bf16[512,8192]{1,0:T(8,128)(2,1)} %mine_ref.13, bf16[512,8192]{1,0:T(8,128)(2,1)} %collective-permute-done.1.theirs_ref, bf16[256,512]{1,0:T(8,128)(2,1)} %collective-permute-done.15.refs_0_, ...), custom_call_target="tpu_custom_call", output_to_operand_aliasing={{0}: (7, {})} | custom-call | flops 1073741824 | bytes 2097152 | tf_op jit(solution)/shard_map/pallas_call | solution.py:71
  78.3 0.6 collective-permute-start.29
  78.8 3.4 %collective-permute-done.26.refs_2_ = bf16[256,512]{1,0:T(8,128)(2,1)S(1)} collective-permute-done((bf16[256,512]{1,0:T(8,128)(2,1)S(1)}, bf16[256,512]{1,0:T(8,128)(2,1)S(1)}, u32[]{:S(2)}, u32[]{:S(2)}) %collective-permute-start.26) | collective-permute-done | bytes 262176 | tf_op jit(solution)/shard_map/ppermute | solution.py:139
  82.2 0.5 collective-permute-start.27
  82.7 1.5 %collective-permute-start.25 = (bf16[256,512]{1,0:T(8,128)(2,1)}, bf16[256,512]{1,0:T(8,128)(2,1)}, u32[]{:S(2)}, u32[]{:S(2)}) collective-permute-start(bf16[256,512]{1,0:T(8,128)(2,1)} %collective-permute-done.24.refs_1_), channel_id=1, source_target_pairs={{0,4},{4,8},{8,12},{12,14},{14,10},{10,6},{6,2},{2,0},{1,5},{5,9},... | collective-permute-start | bytes 786440 | tf_op jit(solution)/shard_map/ppermute | solution.py:139
  84.2 1.4 %collective-permute-start.23 = (bf16[256,512]{1,0:T(8,128)(2,1)}, bf16[256,512]{1,0:T(8,128)(2,1)}, u32[]{:S(2)}, u32[]{:S(2)}) collective-permute-start(bf16[256,512]{1,0:T(8,128)(2,1)} %collective-permute-done.19.refs_0_), channel_id=1, source_target_pairs={{0,4},{4,8},{8,12},{12,14},{14,10},{10,6},{6,2},{2,0},{1,5},{5,9},... | collective-permute-start | bytes 786440 | tf_op jit(solution)/shard_map/ppermute | solution.py:139
  85.8 3.7 %shard_map.87 = (f32[1024,512]{1,0:T(8,128)S(1)}, f32[8,128]{1,0:T(8,128)}) custom-call(s32[2]{0:T(128)S(1)} %pad_add_fusion.6.places_ref, bf16[512,8192]{1,0:T(8,128)(2,1)} %mine_ref.13, bf16[512,8192]{1,0:T(8,128)(2,1)} %collective-permute-done.1.theirs_ref, bf16[256,512]{1,0:T(8,128)(2,1)} %collective-permute-done.19.refs_0_, ...), custom_call_target="tpu_custom_call", output_to_operand_aliasing={{0}: (7, {})} | custom-call | flops 1073741824 | bytes 2097152 | tf_op jit(solution)/shard_map/pallas_call | solution.py:71
  89.6 1.5 %collective-permute-done.27.refs_2_ = bf16[256,512]{1,0:T(8,128)(2,1)S(1)} collective-permute-done((bf16[256,512]{1,0:T(8,128)(2,1)S(1)}, bf16[256,512]{1,0:T(8,128)(2,1)S(1)}, u32[]{:S(2)}, u32[]{:S(2)}) %collective-permute-start.27) | collective-permute-done | bytes 262176 | tf_op jit(solution)/shard_map/ppermute | solution.py:139
  91.1 1.2 collective-permute-done.23.refs_0_
  92.3 4.7 %shard_map.88 = (bf16[1024,512]{1,0:T(8,128)(2,1)}, f32[8,128]{1,0:T(8,128)}) custom-call(s32[4]{0:T(128)S(1)} %pad_add_fusion.places_ref, bf16[512,8192]{1,0:T(8,128)(2,1)} %mine_ref.13, bf16[512,8192]{1,0:T(8,128)(2,1)} %collective-permute-done.1.theirs_ref, bf16[256,512]{1,0:T(8,128)(2,1)} %collective-permute-done.23.refs_0_, ...), custom_call_target="tpu_custom_call" | custom-call | flops 1073741824 | bytes 2097152 | tf_op jit(solution)/shard_map/pallas_call | solution.py:71
  97.7 2.2 %collective-permute-done.30.got_any = bf16[1024,512]{1,0:T(8,128)(2,1)S(1)} collective-permute-done((bf16[1024,512]{1,0:T(8,128)(2,1)}, bf16[1024,512]{1,0:T(8,128)(2,1)S(1)}, u32[]{:S(2)}, u32[]{:S(2)}) %collective-permute-start.30) | collective-permute-done | bytes 1048608 | tf_op jit(solution)/shard_map/ppermute | solution.py:277
  99.9 5.1 %shard_map.89 = f32[8,9,8,128]{3,2,1,0:T(8,128)} custom-call(s32[1]{0:T(128)} %bitcast.core_ref, bf16[1024,512]{1,0:T(8,128)(2,1)} %get-tuple-element.84.have_any, bf16[1024,512]{1,0:T(8,128)(2,1)S(1)} %collective-permute-done.30.got_any, bf16[512,1024]{1,0:T(8,128)(2,1)} %key_any.1, bf16[512,1024]{1,0:T(8,128)(2,1)} %value_any.1, ...), custom_call_target="tpu_custom_call" | custom-call | flops 1342177280 | bytes 2097152 | tf_op jit(solution)/shard_map/pallas_call | solution.py:207
  105.1 0.8 reshape.89
  106.4 0.7 fusion.19
  107.1 4.8 %all-to-all-start = ((f32[8,72,128]{2,1,0:T(8,128)}), f32[8,72,128]{2,1,0:T(8,128)S(1)}, u32[]{:S(2)}, u32[]{:S(2)}) async-start(f32[8,72,128]{2,1,0:T(8,128)} %bitcast.25), calls=%async_computation | async-start | bytes 589824 | tf_op jit(solution)/shard_map/all_to_all | solution.py:309
  113.3 8.6 %all-to-all-done = f32[8,72,128]{2,1,0:T(8,128)S(1)} async-done(((f32[8,72,128]{2,1,0:T(8,128)}), f32[8,72,128]{2,1,0:T(8,128)S(1)}, u32[]{:S(2)}, u32[]{:S(2)}) %all-to-all-start) | async-done | bytes 294944 | tf_op jit(solution)/shard_map/all_to_all | solution.py:309
  121.9 0.4 shard_map.90
  122.2 1.5 %collective-permute-start.31 = (bf16[64,128]{1,0:T(8,128)(2,1)S(1)}, bf16[64,128]{1,0:T(8,128)(2,1)S(1)}, u32[]{:S(2)}, u32[]{:S(2)}) collective-permute-start(bf16[64,128]{1,0:T(8,128)(2,1)S(1)} %shard_map.90), channel_id=1, source_target_pairs={{0,2},{2,0},{4,6},{6,4},{8,10},{10,8},{12,14},{14,12},{1,3},{3,1},... | collective-permute-start | bytes 49160 | tf_op jit(solution)/shard_map/ppermute | solution.py:313
  123.8 2.3 %collective-permute-done.31 = bf16[64,128]{1,0:T(8,128)(2,1)S(1)} collective-permute-done((bf16[64,128]{1,0:T(8,128)(2,1)S(1)}, bf16[64,128]{1,0:T(8,128)(2,1)S(1)}, u32[]{:S(2)}, u32[]{:S(2)}) %collective-permute-start.31) | collective-permute-done | bytes 16416 | tf_op jit(solution)/shard_map/ppermute | solution.py:313
  126.1 1.2 collective-permute-start.32
  127.3 1.3 collective-permute-start.33
  128.6 1.9 %collective-permute-start.34 = (bf16[128,128]{1,0:T(8,128)(2,1)S(1)}, bf16[128,128]{1,0:T(8,128)(2,1)S(1)}, u32[]{:S(2)}, u32[]{:S(2)}) collective-permute-start(bf16[128,128]{1,0:T(8,128)(2,1)S(1)} %pad_maximum_fusion.2), channel_id=1, source_target_pairs={{0,4},{2,6},{4,0},{6,2},{8,12},{10,14},{12,8},{14,10},{1,5},{3,7},... | collective-permute-start | bytes 98312 | tf_op jit(solution)/shard_map/ppermute | solution.py:316
  130.5 1.3 collective-permute-done.32
  131.8 0.8 collective-permute-done.33
  133.1 1.3 collective-permute-done.35
  134.8 0.9 reshape.98
  (77 shorter events, 4.0 us)
Async XLA Ops:
  0.0 97.5 %copy-start = (bf16[4,4,8192]{2,1,0:T(4,128)(2,1)S(1)}, bf16[4,4,8192]{2,1,0:T(4,128)(2,1)}, u32[]{:S(2)}) copy-start(bf16[4,4,8192]{2,1,0:T(4,128)(2,1)} %param.14) | copy-start | bytes 786436
  1.3 2.1 %collective-permute-start = (bf16[512,512]{1,0:T(8,128)(2,1)S(1)}, bf16[512,512]{1,0:T(8,128)(2,1)S(1)}, u32[]{:S(2)}, u32[]{:S(2)}) collective-permute-start(bf16[512,512]{1,0:T(8,128)(2,1)S(1)} %get-tuple-element.90), channel_id=1, source_target_pairs={{0,1},{1,0},{2,3},{3,2},{4,5},{5,4},{6,7},{7,6},{8,9},{9,8},{10,11... | collective-permute-start | bytes 1572872 | tf_op jit(solution)/shard_map/ppermute | solution.py:101
  3.4 22.7 %collective-permute-start.1 = (bf16[512,8192]{1,0:T(8,128)(2,1)}, bf16[512,8192]{1,0:T(8,128)(2,1)}, u32[]{:S(2)}, u32[]{:S(2)}) collective-permute-start(bf16[512,8192]{1,0:T(8,128)(2,1)} %mine_ref.13), channel_id=1, source_target_pairs={{0,1},{1,0},{2,3},{3,2},{4,5},{5,4},{6,7},{7,6},{8,9},{9,8},{10,11... | collective-permute-start | bytes 25165832 | tf_op jit(solution)/shard_map/ppermute | solution.py:126
  3.8 10.0 %collective-permute-start.2 = (bf16[256,512]{1,0:T(8,128)(2,1)S(1)}, bf16[256,512]{1,0:T(8,128)(2,1)}, u32[]{:S(2)}, u32[]{:S(2)}) collective-permute-start(bf16[256,512]{1,0:T(8,128)(2,1)S(1)} %get-tuple-element.94), channel_id=1, source_target_pairs={{0,4},{4,8},{8,12},{12,14},{14,10},{10,6},{6,2},{2,0},{1,5},{5,9},... | collective-permute-start | bytes 786440 | tf_op jit(solution)/shard_map/ppermute | solution.py:139
  6.6 12.5 %collective-permute-start.3 = (bf16[256,512]{1,0:T(8,128)(2,1)S(1)}, bf16[256,512]{1,0:T(8,128)(2,1)}, u32[]{:S(2)}, u32[]{:S(2)}) collective-permute-start(bf16[256,512]{1,0:T(8,128)(2,1)S(1)} %get-tuple-element.93), channel_id=1, source_target_pairs={{0,4},{4,8},{8,12},{12,14},{14,10},{10,6},{6,2},{2,0},{1,5},{5,9},... | collective-permute-start | bytes 786440 | tf_op jit(solution)/shard_map/ppermute | solution.py:139
  8.2 10.9 %collective-permute-start.4 = (bf16[256,512]{1,0:T(8,128)(2,1)S(1)}, bf16[256,512]{1,0:T(8,128)(2,1)}, u32[]{:S(2)}, u32[]{:S(2)}) collective-permute-start(bf16[256,512]{1,0:T(8,128)(2,1)S(1)} %get-tuple-element.92), channel_id=1, source_target_pairs={{4,0},{8,4},{12,8},{14,12},{10,14},{6,10},{2,6},{0,2},{5,1},{9,5},... | collective-permute-start | bytes 786440 | tf_op jit(solution)/shard_map/ppermute | solution.py:139
  8.7 13.3 %collective-permute-start.5 = (bf16[256,512]{1,0:T(8,128)(2,1)S(1)}, bf16[256,512]{1,0:T(8,128)(2,1)}, u32[]{:S(2)}, u32[]{:S(2)}) collective-permute-start(bf16[256,512]{1,0:T(8,128)(2,1)S(1)} %get-tuple-element.91), channel_id=1, source_target_pairs={{4,0},{8,4},{12,8},{14,12},{10,14},{6,10},{2,6},{0,2},{5,1},{9,5},... | collective-permute-start | bytes 786440 | tf_op jit(solution)/shard_map/ppermute | solution.py:139
  22.0 9.8 %collective-permute-start.10 = (bf16[256,512]{1,0:T(8,128)(2,1)}, bf16[256,512]{1,0:T(8,128)(2,1)}, u32[]{:S(2)}, u32[]{:S(2)}) collective-permute-start(bf16[256,512]{1,0:T(8,128)(2,1)} %collective-permute-done.5.refs_5_), channel_id=1, source_target_pairs={{4,0},{8,4},{12,8},{14,12},{10,14},{6,10},{2,6},{0,2},{5,1},{9,5},... | collective-permute-start | bytes 786440 | tf_op jit(solution)/shard_map/ppermute | solution.py:139
  22.4 16.8 %collective-permute-start.6 = (bf16[256,512]{1,0:T(8,128)(2,1)}, bf16[256,512]{1,0:T(8,128)(2,1)}, u32[]{:S(2)}, u32[]{:S(2)}) collective-permute-start(bf16[256,512]{1,0:T(8,128)(2,1)} %collective-permute-done.2.refs_2_), channel_id=1, source_target_pairs={{0,4},{4,8},{8,12},{12,14},{14,10},{10,6},{6,2},{2,0},{1,5},{5,9},... | collective-permute-start | bytes 786440 | tf_op jit(solution)/shard_map/ppermute | solution.py:139
  24.0 13.6 %collective-permute-start.8 = (bf16[256,512]{1,0:T(8,128)(2,1)}, bf16[256,512]{1,0:T(8,128)(2,1)}, u32[]{:S(2)}, u32[]{:S(2)}) collective-permute-start(bf16[256,512]{1,0:T(8,128)(2,1)} %collective-permute-done.3.refs_3_), channel_id=1, source_target_pairs={{0,4},{4,8},{8,12},{12,14},{14,10},{10,6},{6,2},{2,0},{1,5},{5,9},... | collective-permute-start | bytes 786440 | tf_op jit(solution)/shard_map/ppermute | solution.py:139
  25.6 11.6 %collective-permute-start.9 = (bf16[256,512]{1,0:T(8,128)(2,1)}, bf16[256,512]{1,0:T(8,128)(2,1)}, u32[]{:S(2)}, u32[]{:S(2)}) collective-permute-start(bf16[256,512]{1,0:T(8,128)(2,1)} %collective-permute-done.4.refs_4_), channel_id=1, source_target_pairs={{4,0},{8,4},{12,8},{14,12},{10,14},{6,10},{2,6},{0,2},{5,1},{9,5},... | collective-permute-start | bytes 786440 | tf_op jit(solution)/shard_map/ppermute | solution.py:139
  31.8 12.9 %collective-permute-start.14 = (bf16[256,512]{1,0:T(8,128)(2,1)}, bf16[256,512]{1,0:T(8,128)(2,1)S(1)}, u32[]{:S(2)}, u32[]{:S(2)}) collective-permute-start(bf16[256,512]{1,0:T(8,128)(2,1)} %collective-permute-done.10.refs_3_), channel_id=1, source_target_pairs={{4,0},{8,4},{12,8},{14,12},{10,14},{6,10},{2,6},{0,2},{5,1},{9,5},... | collective-permute-start | bytes 786440 | tf_op jit(solution)/shard_map/ppermute | solution.py:139
  37.1 11.1 %collective-permute-start.13 = (bf16[256,512]{1,0:T(8,128)(2,1)}, bf16[256,512]{1,0:T(8,128)(2,1)S(1)}, u32[]{:S(2)}, u32[]{:S(2)}) collective-permute-start(bf16[256,512]{1,0:T(8,128)(2,1)} %collective-permute-done.9.refs_2_), channel_id=1, source_target_pairs={{4,0},{8,4},{12,8},{14,12},{10,14},{6,10},{2,6},{0,2},{5,1},{9,5},... | collective-permute-start | bytes 786440 | tf_op jit(solution)/shard_map/ppermute | solution.py:139
  37.6 11.1 %collective-permute-start.12 = (bf16[256,512]{1,0:T(8,128)(2,1)}, bf16[256,512]{1,0:T(8,128)(2,1)}, u32[]{:S(2)}, u32[]{:S(2)}) collective-permute-start(bf16[256,512]{1,0:T(8,128)(2,1)} %collective-permute-done.8.refs_1_), channel_id=1, source_target_pairs={{0,4},{4,8},{8,12},{12,14},{14,10},{10,6},{6,2},{2,0},{1,5},{5,9},... | collective-permute-start | bytes 786440 | tf_op jit(solution)/shard_map/ppermute | solution.py:139
  39.2 11.1 %collective-permute-start.7 = (bf16[256,512]{1,0:T(8,128)(2,1)}, bf16[256,512]{1,0:T(8,128)(2,1)}, u32[]{:S(2)}, u32[]{:S(2)}) collective-permute-start(bf16[256,512]{1,0:T(8,128)(2,1)} %collective-permute-done.6.refs_0_), channel_id=1, source_target_pairs={{0,4},{4,8},{8,12},{12,14},{14,10},{10,6},{6,2},{2,0},{1,5},{5,9},... | collective-permute-start | bytes 786440 | tf_op jit(solution)/shard_map/ppermute | solution.py:139
  44.7 11.0 %collective-permute-start.18 = (bf16[256,512]{1,0:T(8,128)(2,1)S(1)}, bf16[256,512]{1,0:T(8,128)(2,1)}, u32[]{:S(2)}, u32[]{:S(2)}) collective-permute-start(bf16[256,512]{1,0:T(8,128)(2,1)S(1)} %collective-permute-done.14.refs_3_), channel_id=1, source_target_pairs={{4,0},{8,4},{12,8},{14,12},{10,14},{6,10},{2,6},{0,2},{5,1},{9,5},... | collective-permute-start | bytes 786440 | tf_op jit(solution)/shard_map/ppermute | solution.py:139
  48.3 11.5 %collective-permute-start.17 = (bf16[256,512]{1,0:T(8,128)(2,1)S(1)}, bf16[256,512]{1,0:T(8,128)(2,1)}, u32[]{:S(2)}, u32[]{:S(2)}) collective-permute-start(bf16[256,512]{1,0:T(8,128)(2,1)S(1)} %collective-permute-done.13.refs_2_), channel_id=1, source_target_pairs={{4,0},{8,4},{12,8},{14,12},{10,14},{6,10},{2,6},{0,2},{5,1},{9,5},... | collective-permute-start | bytes 786440 | tf_op jit(solution)/shard_map/ppermute | solution.py:139
  48.7 11.5 %collective-permute-start.16 = (bf16[256,512]{1,0:T(8,128)(2,1)}, bf16[256,512]{1,0:T(8,128)(2,1)}, u32[]{:S(2)}, u32[]{:S(2)}) collective-permute-start(bf16[256,512]{1,0:T(8,128)(2,1)} %collective-permute-done.12.refs_1_), channel_id=1, source_target_pairs={{0,4},{4,8},{8,12},{12,14},{14,10},{10,6},{6,2},{2,0},{1,5},{5,9},... | collective-permute-start | bytes 786440 | tf_op jit(solution)/shard_map/ppermute | solution.py:139
  50.3 11.5 %collective-permute-start.11 = (bf16[256,512]{1,0:T(8,128)(2,1)}, bf16[256,512]{1,0:T(8,128)(2,1)}, u32[]{:S(2)}, u32[]{:S(2)}) collective-permute-start(bf16[256,512]{1,0:T(8,128)(2,1)} %collective-permute-done.7.refs_0_), channel_id=1, source_target_pairs={{0,4},{4,8},{8,12},{12,14},{14,10},{10,6},{6,2},{2,0},{1,5},{5,9},... | collective-permute-start | bytes 786440 | tf_op jit(solution)/shard_map/ppermute | solution.py:139
  55.7 11.6 %collective-permute-start.22 = (bf16[256,512]{1,0:T(8,128)(2,1)}, bf16[256,512]{1,0:T(8,128)(2,1)S(1)}, u32[]{:S(2)}, u32[]{:S(2)}) collective-permute-start(bf16[256,512]{1,0:T(8,128)(2,1)} %collective-permute-done.18.refs_3_), channel_id=1, source_target_pairs={{4,0},{8,4},{12,8},{14,12},{10,14},{6,10},{2,6},{0,2},{5,1},{9,5},... | collective-permute-start | bytes 786440 | tf_op jit(solution)/shard_map/ppermute | solution.py:139
  59.8 11.1 %collective-permute-start.21 = (bf16[256,512]{1,0:T(8,128)(2,1)}, bf16[256,512]{1,0:T(8,128)(2,1)S(1)}, u32[]{:S(2)}, u32[]{:S(2)}) collective-permute-start(bf16[256,512]{1,0:T(8,128)(2,1)} %collective-permute-done.17.refs_2_), channel_id=1, source_target_pairs={{4,0},{8,4},{12,8},{14,12},{10,14},{6,10},{2,6},{0,2},{5,1},{9,5},... | collective-permute-start | bytes 786440 | tf_op jit(solution)/shard_map/ppermute | solution.py:139
  60.2 11.1 %collective-permute-start.20 = (bf16[256,512]{1,0:T(8,128)(2,1)}, bf16[256,512]{1,0:T(8,128)(2,1)}, u32[]{:S(2)}, u32[]{:S(2)}) collective-permute-start(bf16[256,512]{1,0:T(8,128)(2,1)} %collective-permute-done.16.refs_1_), channel_id=1, source_target_pairs={{0,4},{4,8},{8,12},{12,14},{14,10},{10,6},{6,2},{2,0},{1,5},{5,9},... | collective-permute-start | bytes 786440 | tf_op jit(solution)/shard_map/ppermute | solution.py:139
  61.8 11.1 %collective-permute-start.15 = (bf16[256,512]{1,0:T(8,128)(2,1)}, bf16[256,512]{1,0:T(8,128)(2,1)}, u32[]{:S(2)}, u32[]{:S(2)}) collective-permute-start(bf16[256,512]{1,0:T(8,128)(2,1)} %collective-permute-done.11.refs_0_), channel_id=1, source_target_pairs={{0,4},{4,8},{8,12},{12,14},{14,10},{10,6},{6,2},{2,0},{1,5},{5,9},... | collective-permute-start | bytes 786440 | tf_op jit(solution)/shard_map/ppermute | solution.py:139
  67.3 11.0 %collective-permute-start.28 = (bf16[256,512]{1,0:T(8,128)(2,1)S(1)}, bf16[256,512]{1,0:T(8,128)(2,1)S(1)}, u32[]{:S(2)}, u32[]{:S(2)}) collective-permute-start(bf16[256,512]{1,0:T(8,128)(2,1)S(1)} %collective-permute-done.22.refs_3_), channel_id=1, source_target_pairs={{4,0},{8,4},{12,8},{14,12},{10,14},{6,10},{2,6},{0,2},{5,1},{9,5},... | collective-permute-start | bytes 786440 | tf_op jit(solution)/shard_map/ppermute | solution.py:139
  70.9 11.3 %collective-permute-start.26 = (bf16[256,512]{1,0:T(8,128)(2,1)S(1)}, bf16[256,512]{1,0:T(8,128)(2,1)S(1)}, u32[]{:S(2)}, u32[]{:S(2)}) collective-permute-start(bf16[256,512]{1,0:T(8,128)(2,1)S(1)} %collective-permute-done.21.refs_2_), channel_id=1, source_target_pairs={{4,0},{8,4},{12,8},{14,12},{10,14},{6,10},{2,6},{0,2},{5,1},{9,5},... | collective-permute-start | bytes 786440 | tf_op jit(solution)/shard_map/ppermute | solution.py:139
  71.3 11.4 %collective-permute-start.24 = (bf16[256,512]{1,0:T(8,128)(2,1)}, bf16[256,512]{1,0:T(8,128)(2,1)}, u32[]{:S(2)}, u32[]{:S(2)}) collective-permute-start(bf16[256,512]{1,0:T(8,128)(2,1)} %collective-permute-done.20.refs_1_), channel_id=1, source_target_pairs={{0,4},{4,8},{8,12},{12,14},{14,10},{10,6},{6,2},{2,0},{1,5},{5,9},... | collective-permute-start | bytes 786440 | tf_op jit(solution)/shard_map/ppermute | solution.py:139
  72.9 11.3 %collective-permute-start.19 = (bf16[256,512]{1,0:T(8,128)(2,1)}, bf16[256,512]{1,0:T(8,128)(2,1)}, u32[]{:S(2)}, u32[]{:S(2)}) collective-permute-start(bf16[256,512]{1,0:T(8,128)(2,1)} %collective-permute-done.15.refs_0_), channel_id=1, source_target_pairs={{0,4},{4,8},{8,12},{12,14},{14,10},{10,6},{6,2},{2,0},{1,5},{5,9},... | collective-permute-start | bytes 786440 | tf_op jit(solution)/shard_map/ppermute | solution.py:139
  78.3 11.3 %collective-permute-start.29 = (bf16[256,512]{1,0:T(8,128)(2,1)S(1)}, bf16[256,512]{1,0:T(8,128)(2,1)S(1)}, u32[]{:S(2)}, u32[]{:S(2)}) collective-permute-start(bf16[256,512]{1,0:T(8,128)(2,1)S(1)} %collective-permute-done.28.refs_3_), channel_id=1, source_target_pairs={{4,0},{8,4},{12,8},{14,12},{10,14},{6,10},{2,6},{0,2},{5,1},{9,5},... | collective-permute-start | bytes 786440 | tf_op jit(solution)/shard_map/ppermute | solution.py:139
  82.2 8.9 %collective-permute-start.27 = (bf16[256,512]{1,0:T(8,128)(2,1)S(1)}, bf16[256,512]{1,0:T(8,128)(2,1)S(1)}, u32[]{:S(2)}, u32[]{:S(2)}) collective-permute-start(bf16[256,512]{1,0:T(8,128)(2,1)S(1)} %collective-permute-done.26.refs_2_), channel_id=1, source_target_pairs={{4,0},{8,4},{12,8},{14,12},{10,14},{6,10},{2,6},{0,2},{5,1},{9,5},... | collective-permute-start | bytes 786440 | tf_op jit(solution)/shard_map/ppermute | solution.py:139
  82.7 8.4 %collective-permute-start.25 = (bf16[256,512]{1,0:T(8,128)(2,1)}, bf16[256,512]{1,0:T(8,128)(2,1)}, u32[]{:S(2)}, u32[]{:S(2)}) collective-permute-start(bf16[256,512]{1,0:T(8,128)(2,1)} %collective-permute-done.24.refs_1_), channel_id=1, source_target_pairs={{0,4},{4,8},{8,12},{12,14},{14,10},{10,6},{6,2},{2,0},{1,5},{5,9},... | collective-permute-start | bytes 786440 | tf_op jit(solution)/shard_map/ppermute | solution.py:139
  84.2 8.1 %collective-permute-start.23 = (bf16[256,512]{1,0:T(8,128)(2,1)}, bf16[256,512]{1,0:T(8,128)(2,1)}, u32[]{:S(2)}, u32[]{:S(2)}) collective-permute-start(bf16[256,512]{1,0:T(8,128)(2,1)} %collective-permute-done.19.refs_0_), channel_id=1, source_target_pairs={{0,4},{4,8},{8,12},{12,14},{14,10},{10,6},{6,2},{2,0},{1,5},{5,9},... | collective-permute-start | bytes 786440 | tf_op jit(solution)/shard_map/ppermute | solution.py:139
  92.3 4.8 %copy-start.3 = (s32[4]{0:T(128)S(1)}, s32[4]{0:T(128)}, u32[]{:S(2)}) copy-start(s32[4]{0:T(128)} %param.13) | copy-start | bytes 52
  97.0 2.9 %collective-permute-start.30 = (bf16[1024,512]{1,0:T(8,128)(2,1)}, bf16[1024,512]{1,0:T(8,128)(2,1)S(1)}, u32[]{:S(2)}, u32[]{:S(2)}) collective-permute-start(bf16[1024,512]{1,0:T(8,128)(2,1)} %get-tuple-element.84.have_any), channel_id=1, source_target_pairs={{0,1},{1,0},{2,3},{3,2},{4,5},{5,4},{6,7},{7,6},{8,9},{9,8},{10,11... | collective-permute-start | bytes 3145736 | tf_op jit(solution)/shard_map/ppermute | solution.py:277
  99.9 5.9 %copy-start.1 = (bf16[512,1024]{1,0:T(8,128)(2,1)S(1)}, bf16[512,1024]{1,0:T(8,128)(2,1)}, u32[]{:S(2)}) copy-start(bf16[512,1024]{1,0:T(8,128)(2,1)} %key_any.1) | copy-start | bytes 3145732
  99.9 6.2 %copy-start.2 = (bf16[512,1024]{1,0:T(8,128)(2,1)S(1)}, bf16[512,1024]{1,0:T(8,128)(2,1)}, u32[]{:S(2)}) copy-start(bf16[512,1024]{1,0:T(8,128)(2,1)} %value_any.1) | copy-start | bytes 3145732
  107.1 14.7 %all-to-all-start = ((f32[8,72,128]{2,1,0:T(8,128)}), f32[8,72,128]{2,1,0:T(8,128)S(1)}, u32[]{:S(2)}, u32[]{:S(2)}) async-start(f32[8,72,128]{2,1,0:T(8,128)} %bitcast.25), calls=%async_computation | async-start | bytes 589824 | tf_op jit(solution)/shard_map/all_to_all | solution.py:309
  122.2 3.8 %collective-permute-start.31 = (bf16[64,128]{1,0:T(8,128)(2,1)S(1)}, bf16[64,128]{1,0:T(8,128)(2,1)S(1)}, u32[]{:S(2)}, u32[]{:S(2)}) collective-permute-start(bf16[64,128]{1,0:T(8,128)(2,1)S(1)} %shard_map.90), channel_id=1, source_target_pairs={{0,2},{2,0},{4,6},{6,4},{8,10},{10,8},{12,14},{14,12},{1,3},{3,1},... | collective-permute-start | bytes 49160 | tf_op jit(solution)/shard_map/ppermute | solution.py:313
  126.1 5.8 %collective-permute-start.32 = (bf16[128,128]{1,0:T(8,128)(2,1)S(1)}, bf16[128,128]{1,0:T(8,128)(2,1)S(1)}, u32[]{:S(2)}, u32[]{:S(2)}) collective-permute-start(bf16[128,128]{1,0:T(8,128)(2,1)S(1)} %pad_maximum_fusion.2), channel_id=1, source_target_pairs={{0,12},{2,14},{4,8},{6,10},{8,4},{10,6},{12,0},{14,2},{1,13},{3,15... | collective-permute-start | bytes 98312 | tf_op jit(solution)/shard_map/ppermute | solution.py:316
  127.3 5.3 %collective-permute-start.33 = (bf16[128,128]{1,0:T(8,128)(2,1)S(1)}, bf16[128,128]{1,0:T(8,128)(2,1)S(1)}, u32[]{:S(2)}, u32[]{:S(2)}) collective-permute-start(bf16[128,128]{1,0:T(8,128)(2,1)S(1)} %pad_maximum_fusion.2), channel_id=1, source_target_pairs={{0,8},{2,10},{4,12},{6,14},{8,0},{10,2},{12,4},{14,6},{1,9},{3,11}... | collective-permute-start | bytes 98312 | tf_op jit(solution)/shard_map/ppermute | solution.py:316
  128.6 4.2 %collective-permute-start.34 = (bf16[128,128]{1,0:T(8,128)(2,1)S(1)}, bf16[128,128]{1,0:T(8,128)(2,1)S(1)}, u32[]{:S(2)}, u32[]{:S(2)}) collective-permute-start(bf16[128,128]{1,0:T(8,128)(2,1)S(1)} %pad_maximum_fusion.2), channel_id=1, source_target_pairs={{0,4},{2,6},{4,0},{6,2},{8,12},{10,14},{12,8},{14,10},{1,5},{3,7},... | collective-permute-start | bytes 98312 | tf_op jit(solution)/shard_map/ppermute | solution.py:316
  133.0 1.4 %collective-permute-start.35 = (bf16[16,1,4096]{2,0,1:T(8,128)(2,1)S(1)}, bf16[16,1,4096]{2,0,1:T(8,128)(2,1)S(1)}, u32[]{:S(2)}, u32[]{:S(2)}) collective-permute-start(bf16[16,1,4096]{2,0,1:T(8,128)(2,1)S(1)} %reshape.97), channel_id=1, source_target_pairs={{0,1},{1,0},{2,3},{3,2},{4,5},{5,4},{6,7},{7,6},{8,9},{9,8},{10,11... | collective-permute-start | bytes 393224 | tf_op jit(solution)/shard_map/ppermute | solution.py:326

commit v11 on v7

--- a/solution.py
+++ b/solution.py
@@ -29,7 +29,7 @@
 
     def kernel(places_ref, mine_ref, theirs_ref, *refs):
         parts = list(refs[:count])
-        total_ref, out_ref, mark_ref, columns, weights, sems = (
+        total_ref, out_ref, mark_ref, columns, weights, sems, loaded = (
             refs[count:] if total is not None else (None,) + refs[count:]
         )
         copies = []
@@ -41,17 +41,25 @@
                 )
                 copy.start()
                 copies.append(copy)
+        loads = []
+
+        def load(source, place):
+            copy = pltpu.make_async_copy(source, weights.at[pl.ds(place, source.shape[0])], loaded.at[len(loads)])
+            copy.start()
+            loads.append(copy)
+
+        turn = places_ref[len(halves)]
         for h, half in enumerate(halves):
-            at = h * span
             shared = half[1].shape[0]
-            weights[at : at + shared, :] = parts.pop(0)[...]
+            load(parts.pop(0), h * span)
             if len(half) > 2:
                 rest = half[2].shape[0]
-                turn = places_ref[len(halves)]
-                for turn, skip in ((turn, 0), (1 - turn, half[4] * rest)):
-                    rows = pl.ds(pl.multiple_of(at + shared + turn * rest, rest), rest)
-                    weights[rows, :] = parts.pop(0)[skip : skip + rest, :]
+                first = h * span + shared
+                load(parts.pop(0), pl.multiple_of(first + turn * rest, rest))
+                load(parts.pop(0).at[pl.ds(half[4] * rest, rest)], pl.multiple_of(first + (1 - turn) * rest, rest))
         mark_ref[...] = jnp.zeros_like(mark_ref)
+        for copy in loads:
+            copy.wait()
         for j in range(2):
             for h in range(len(halves)):
                 copies[j * len(halves) + h].wait()
@@ -63,6 +71,7 @@
                 rows = pl.ds(pl.multiple_of(places_ref[len(halves) + 1 + j] * tok_rows, tok_rows), tok_rows)
             out_ref[rows, :] = term.astype(out_ref.dtype)
 
+    tokens = pltpu.with_memory_space_constraint(tokens, pltpu.HBM)
     in_vmem = pl.BlockSpec(memory_space=pltpu.VMEM)
     in_any = pl.BlockSpec(memory_space=pl.ANY)
     sums = [] if total is None else [total]
@@ -72,15 +81,16 @@
             jax.ShapeDtypeStruct((2 * tok_rows, width), BF if last else F32),
             jax.ShapeDtypeStruct((8, 128), F32),
         ),
-        in_specs=[pl.BlockSpec(memory_space=pltpu.SMEM), in_any, in_any] + [in_vmem] * (count + len(sums)),
+        in_specs=[pl.BlockSpec(memory_space=pltpu.SMEM)] + [in_any] * (2 + count) + [in_vmem] * len(sums),
         out_specs=(in_vmem, in_vmem),
         scratch_shapes=[
             pltpu.VMEM((2, tok_rows, deep), BF),
             pltpu.VMEM((deep, width), BF),
             pltpu.SemaphoreType.DMA((2, len(halves))),
+            pltpu.SemaphoreType.DMA((count,)),
         ],
         input_output_aliases={} if total is None or last else {3 + count: 0},
-        compiler_params=pltpu.CompilerParams(vmem_limit_bytes=48 * 2**20),
+        compiler_params=pltpu.CompilerParams(vmem_limit_bytes=20 * 2**20),
         cost_estimate=pl.CostEstimate(
             flops=4 * tok_rows * deep * width, bytes_accessed=4 * tok_rows * deep, transcendentals=0
         ),
@@ -127,7 +137,7 @@
     single.append(turns(got))
     theirs = lax.ppermute(tokens_later, "core", SWAP)
     todo = [(start_of(0, 0), own), (start_of(1, 0), got)]
-    calls = {3: 4, 5: 4, 7: 4}
+    calls = {3: 4, 4: 2, 5: 2, 6: 2, 7: 2}
     total = mark = crossed = None
     for step in range(1, chips):
         if step == 2:
@@ -162,12 +172,26 @@
     blocks = pairs * heads // chips
     scale = 1.0 / DH**0.5
 
-    def kernel(core_ref, have_ref, got_ref, key_up_ref, value_up_ref, query_ref, bounds_ref, out_ref):
-        first = core_ref[0] == 0
-        have, got = have_ref[...], got_ref[...]
-        lanes = pl.ds(pl.multiple_of(core_ref[0] * heads * DH, heads * DH), heads * DH)
-        keys = mm(jnp.where(first, have, got), key_up_ref[:, lanes]).astype(BF)
-        values = mm(jnp.where(first, got, have), value_up_ref[:, lanes]).astype(BF)
+    def kernel(core_ref, have_any, got_any, key_any, value_any, query_any, bounds_ref, out_ref, *scratch):
+        latents, ups, query_ref, sems = scratch
+        core = core_ref[0]
+        lanes = pl.ds(pl.multiple_of(core * heads * DH, heads * DH), heads * DH)
+        pairs_of = [
+            (have_any, latents.at[core]),
+            (got_any, latents.at[1 - core]),
+            (key_any.at[:, lanes], ups.at[0]),
+            (value_any.at[:, lanes], ups.at[1]),
+            (query_any, query_ref),
+        ]
+        copies = [pltpu.make_async_copy(source, target, sems.at[k]) for k, (source, target) in enumerate(pairs_of)]
+        for copy in copies:
+            copy.start()
+        for copy in copies[:3]:
+            copy.wait()
+        keys = mm(latents[0], ups[0]).astype(BF)
+        for copy in copies[3:]:
+            copy.wait()
+        values = mm(latents[1], ups[1]).astype(BF)
         position = lax.broadcasted_iota(jnp.int32, (tokens, rows), 0)
         visible = (position >= bounds_ref[0:1, :]) & (position < bounds_ref[1:2, :])
         tops, totals = [], []
@@ -197,19 +221,26 @@
             out_ref[chip, blocks] = jnp.zeros((8, DH), F32)
             out_ref[chip, blocks, :, : 2 * blocks] = jnp.concatenate(sides, 1)
 
+    ups = [pltpu.with_memory_space_constraint(x, pltpu.HBM) for x in (key_up, value_up)]
     in_vmem = pl.BlockSpec(memory_space=pltpu.VMEM)
     return pl.pallas_call(
         kernel,
         out_shape=jax.ShapeDtypeStruct((chips, blocks + 1, 8, DH), F32),
-        in_specs=[pl.BlockSpec(memory_space=pltpu.SMEM)] + [in_vmem] * 6,
+        in_specs=[pl.BlockSpec(memory_space=pltpu.SMEM)] + [pl.BlockSpec(memory_space=pl.ANY)] * 5 + [in_vmem],
         out_specs=in_vmem,
-        compiler_params=pltpu.CompilerParams(vmem_limit_bytes=40 * 2**20),
+        scratch_shapes=[
+            pltpu.VMEM((2,) + have.shape, BF),
+            pltpu.VMEM((2, have.shape[1], heads * DH), BF),
+            pltpu.VMEM(query.shape, BF),
+            pltpu.SemaphoreType.DMA((5,)),
+        ],
+        compiler_params=pltpu.CompilerParams(vmem_limit_bytes=16 * 2**20),
         cost_estimate=pl.CostEstimate(
             flops=4 * tokens * (have.shape[1] * heads * DH + heads * rows * DH),
             bytes_accessed=4 * tokens * have.shape[1],
             transcendentals=tokens * heads * rows,
         ),
-    )(core.reshape(1), have, got, key_up, value_up, query, bounds)
+    )(core.reshape(1), have, got, *ups, query, bounds)
 
 
 def merge(arrived, fresh_stats, fresh_summed):
@@ -235,6 +266,7 @@
         out_shape=jax.ShapeDtypeStruct((blocks * 8, DH), BF),
         in_specs=[in_vmem] * 3,
         out_specs=in_vmem,
+        compiler_params=pltpu.CompilerParams(vmem_limit_bytes=8 * 2**20),
         cost_estimate=pl.CostEstimate(
             flops=2 * chips * blocks * 8 * DH, bytes_accessed=4 * arrived.size, transcendentals=chips * blocks * 8
         ),

time: 149 us -> 143 us (0.960)
  waiting for transfers between devices: 44.8 us -> 38 us
  local copies, waits for them, and re-layouts: 15.3 us -> 9.79 us
  starting transfers between devices: 47.6 us -> 50.3 us
  matrix products: 1.51 us -> 3.96 us
  Pallas kernels: 30.2 us -> 32.4 us
    ppermute x14, waiting for transfers between devices: 17.2 us -> 12.5 us  [project(): single = [lax.ppermute(x, 'chip', way) for x, way in zip(single, ways)]]
    ppermute x6, waiting for transfers between devices: 4.89 us -> 0.31 us  [project(): crossed = lax.ppermute(jnp.concatenate(passed, 0), 'groups', SWAP)]
    unnamed x48 -> x34, local copies, waits for them, and re-layouts: 11.1 us -> 7.21 us
    pallas_call x5 -> x7, Pallas kernels: 23.6 us -> 27.2 us  [add_pieces(): pl.pallas_call(kernel, out_shape=(jax.ShapeDtypeStruct((2 * tok_rows, wid...]
    dot_general x2, matrix products: 0.5 us -> 2.95 us  [mm(): return jnp.dot(a, b, preferred_element_type=F32)]
    ppermute x14, waiting for transfers between devices: 5.34 us -> 7.05 us  [project(): both = [lax.ppermute(x, 'chip', way) for x, way in zip(both, ways)]]
    pallas_call x1, Pallas kernels: 1.93 us -> 0.36 us  [merge(): pl.pallas_call(kernel, out_shape=jax.ShapeDtypeStruct((blocks * 8, DH), B...]
  transfers between devices with their start and end apart: 45 -> 45, of which waited for: 21 -> 16; matrix products, arithmetic and copies ran while one was open for 6% -> 5% of each run, Pallas kernels for 13% -> 17%
where the time goes in v11:
time: 143 us; the launch traced here: 142 us
  starting transfers between devices  50.3 us (35%)
  waiting for transfers between devices  38 us (27%)
  Pallas kernels  32.4 us (23%)
  local copies, waits for them, and re-layouts  9.79 us (7%)
  other arithmetic  7.1 us (5%)
  matrix products  3.96 us (3%)
    pallas_call x7, Pallas kernels, add_pieces(): pl.pallas_call(kernel, out_shape=(jax.ShapeDtypeStruct((2 * tok_rows, wid...  27.2 us
    ppermute x14, starting transfers between devices, project(): single = [lax.ppermute(x, 'chip', way) for x, way in zip(single, ways)]  15 us
    ppermute x14, starting transfers between devices, project(): both = [lax.ppermute(x, 'chip', way) for x, way in zip(both, ways)]  14.4 us
    ppermute x14, waiting for transfers between devices, project(): single = [lax.ppermute(x, 'chip', way) for x, way in zip(single, ways)]  12.5 us
    all_to_all x1, waiting for transfers between devices, on_device(): lax.all_to_all(flat, 'chip', split_axis=0, concat_axis=0, tiled=True)  8.59 us
    unnamed x34, local copies, waits for them, and re-layouts  7.21 us
    ppermute x14, waiting for transfers between devices, project(): both = [lax.ppermute(x, 'chip', way) for x, way in zip(both, ways)]  7.05 us
    ppermute x6, starting transfers between devices, project(): crossed = lax.ppermute(jnp.concatenate(passed, 0), 'groups', SWAP)  6.87 us
  transfers between devices with their start and end apart: 45, of which 16 were waited for; matrix products, arithmetic and copies ran while one was open for 5% of the time, Pallas kernels for 17%

profile of v11, /device:TPU:0, one launch (start us, length us, event | category | flops | bytes accessed | tf_op | source)
XLA Modules:
  0.0 142.0 jit_solution(11799246621518008716)
XLA Ops:
  0.0 1.3 broadcast_select_fusion
  1.8 1.5 %collective-permute-done.refs_1_ = bf16[512,512]{1,0:T(8,128)(2,1)S(1)} collective-permute-done((bf16[512,512]{1,0:T(8,128)(2,1)S(1)}, bf16[512,512]{1,0:T(8,128)(2,1)S(1)}, u32[]{:S(2)}, u32[]{:S(2)}) %collective-permute-start) | collective-permute-done | bytes 524320 | tf_op jit(solution)/shard_map/ppermute | solution.py:109
  3.8 2.8 %collective-permute-start.4 = (bf16[128,512]{1,0:T(8,128)(2,1)S(1)}, bf16[128,512]{1,0:T(8,128)(2,1)S(1)}, u32[]{:S(2)}, u32[]{:S(2)}) collective-permute-start(bf16[128,512]{1,0:T(8,128)(2,1)S(1)} %slice_select_fusion), channel_id=1, source_target_pairs={{0,4},{4,8},{8,12},{12,14},{14,10},{10,6},{6,2},{2,0},{1,5},{5,9},... | collective-permute-start | bytes 393224 | tf_op jit(solution)/shard_map/ppermute | solution.py:153
  6.6 1.6 %collective-permute-start.2 = (bf16[256,512]{1,0:T(8,128)(2,1)S(1)}, bf16[256,512]{1,0:T(8,128)(2,1)S(1)}, u32[]{:S(2)}, u32[]{:S(2)}) collective-permute-start(bf16[256,512]{1,0:T(8,128)(2,1)S(1)} %slice.40), channel_id=1, source_target_pairs={{0,4},{4,8},{8,12},{12,14},{14,10},{10,6},{6,2},{2,0},{1,5},{5,9},... | collective-permute-start | bytes 786440 | tf_op jit(solution)/shard_map/ppermute | solution.py:152
  8.8 2.0 %collective-permute-done.4.refs_3_ = bf16[128,512]{1,0:T(8,128)(2,1)S(1)} collective-permute-done((bf16[128,512]{1,0:T(8,128)(2,1)S(1)}, bf16[128,512]{1,0:T(8,128)(2,1)S(1)}, u32[]{:S(2)}, u32[]{:S(2)}) %collective-permute-start.4) | collective-permute-done | bytes 131104 | tf_op jit(solution)/shard_map/ppermute | solution.py:153
  10.8 5.3 %collective-permute-done.2.refs_2_ = bf16[256,512]{1,0:T(8,128)(2,1)S(1)} collective-permute-done((bf16[256,512]{1,0:T(8,128)(2,1)S(1)}, bf16[256,512]{1,0:T(8,128)(2,1)S(1)}, u32[]{:S(2)}, u32[]{:S(2)}) %collective-permute-start.2) | collective-permute-done | bytes 262176 | tf_op jit(solution)/shard_map/ppermute | solution.py:152
  16.1 3.0 %collective-permute-done.5.refs_6_ = bf16[128,512]{1,0:T(8,128)(2,1)S(1)} collective-permute-done((bf16[128,512]{1,0:T(8,128)(2,1)S(1)}, bf16[128,512]{1,0:T(8,128)(2,1)S(1)}, u32[]{:S(2)}, u32[]{:S(2)}) %collective-permute-start.5) | collective-permute-done | bytes 131104 | tf_op jit(solution)/shard_map/ppermute | solution.py:153
  19.6 1.6 %collective-permute-start.8 = (bf16[256,512]{1,0:T(8,128)(2,1)S(1)}, bf16[256,512]{1,0:T(8,128)(2,1)S(1)}, u32[]{:S(2)}, u32[]{:S(2)}) collective-permute-start(bf16[256,512]{1,0:T(8,128)(2,1)S(1)} %pad_maximum_fusion), channel_id=1, source_target_pairs={{0,16},{16,0},{1,17},{17,1},{2,18},{18,2},{3,19},{19,3},{4,20},{20... | collective-permute-start | bytes 786440 | tf_op jit(solution)/shard_map/ppermute | solution.py:155
  21.6 1.6 %collective-permute-start.6 = (bf16[256,512]{1,0:T(8,128)(2,1)S(1)}, bf16[256,512]{1,0:T(8,128)(2,1)}, u32[]{:S(2)}, u32[]{:S(2)}) collective-permute-start(bf16[256,512]{1,0:T(8,128)(2,1)S(1)} %collective-permute-done.2.refs_2_), channel_id=1, source_target_pairs={{0,4},{4,8},{8,12},{12,14},{14,10},{10,6},{6,2},{2,0},{1,5},{5,9},... | collective-permute-start | bytes 786440 | tf_op jit(solution)/shard_map/ppermute | solution.py:152
  23.2 2.3 %collective-permute-done.11.refs_4_ = bf16[128,512]{1,0:T(8,128)(2,1)S(1)} collective-permute-done((bf16[128,512]{1,0:T(8,128)(2,1)S(1)}, bf16[128,512]{1,0:T(8,128)(2,1)S(1)}, u32[]{:S(2)}, u32[]{:S(2)}) %collective-permute-start.11) | collective-permute-done | bytes 131104 | tf_op jit(solution)/shard_map/ppermute | solution.py:153
  25.5 1.6 %collective-permute-start.10 = (bf16[128,512]{1,0:T(8,128)(2,1)S(1)}, bf16[128,512]{1,0:T(8,128)(2,1)}, u32[]{:S(2)}, u32[]{:S(2)}) collective-permute-start(bf16[128,512]{1,0:T(8,128)(2,1)S(1)} %collective-permute-done.4.refs_3_), channel_id=1, source_target_pairs={{0,4},{4,8},{8,12},{12,14},{14,10},{10,6},{6,2},{2,0},{1,5},{5,9},... | collective-permute-start | bytes 393224 | tf_op jit(solution)/shard_map/ppermute | solution.py:153
  27.1 3.8 %collective-permute-done.10.refs_1_ = bf16[128,512]{1,0:T(8,128)(2,1)} collective-permute-done((bf16[128,512]{1,0:T(8,128)(2,1)S(1)}, bf16[128,512]{1,0:T(8,128)(2,1)}, u32[]{:S(2)}, u32[]{:S(2)}) %collective-permute-start.10) | collective-permute-done | bytes 131104 | tf_op jit(solution)/shard_map/ppermute | solution.py:153
  30.9 1.6 %pad_maximum_fusion.1 = bf16[256,512]{1,0:T(8,128)(2,1)} fusion(bf16[128,512]{1,0:T(8,128)(2,1)S(1)} %collective-permute-done.11.refs_4_, bf16[128,512]{1,0:T(8,128)(2,1)} %collective-permute-done.10.refs_1_), kind=kLoop, calls=%fused_computation.7 | loop fusion | flops 524288 | bytes 524288 | tf_op jit(solution)/shard_map/concatenate | solution.py:155
  32.6 1.2 collective-permute-start.12
  34.5 0.9 collective-permute-start.16
  35.4 1.1 collective-permute-start.15
  36.5 0.9 collective-permute-start.18
  37.5 1.2 collective-permute-start.7
  38.6 0.9 copy-done.2
  39.6 0.9 copy-done.8
  40.5 0.9 copy-done.10
  41.4 0.9 copy-done.12
  42.3 0.9 copy-done.14
  43.3 4.7 %shard_map.82 = (f32[1024,512]{1,0:T(8,128)S(1)}, f32[8,128]{1,0:T(8,128)}) custom-call(s32[5]{0:T(128)S(1)} %stack.100.places_ref, bf16[512,8192]{1,0:T(8,128)(2,1)} %mine_ref.13, bf16[512,8192]{1,0:T(8,128)(2,1)} %collective-permute-done.1.theirs_ref, bf16[512,512]{1,0:T(8,128)(2,1)S(1)} %get-tuple-element.79.refs_0_, ...), custom_call_target="tpu_custom_call" | custom-call | flops 2147483648 | bytes 4194304 | tf_op jit(solution)/shard_map/pallas_call | solution.py:78
  48.0 1.0 collective-permute-start.21
  49.0 1.1 collective-permute-start.20
  50.1 1.0 pad_maximum_fusion.2
  51.1 0.9 collective-permute-start.17
  52.1 1.6 %collective-permute-start.23 = (bf16[256,512]{1,0:T(8,128)(2,1)}, bf16[256,512]{1,0:T(8,128)(2,1)}, u32[]{:S(2)}, u32[]{:S(2)}) collective-permute-start(bf16[256,512]{1,0:T(8,128)(2,1)} %collective-permute-done.18.refs_3_), channel_id=1, source_target_pairs={{4,0},{8,4},{12,8},{14,12},{10,14},{6,10},{2,6},{0,2},{5,1},{9,5},... | collective-permute-start | bytes 786440 | tf_op jit(solution)/shard_map/ppermute | solution.py:152
  54.1 3.9 %shard_map.83 = (f32[1024,512]{1,0:T(8,128)S(1)}, f32[8,128]{1,0:T(8,128)}) custom-call(s32[3]{0:T(128)S(1)} %add_add_fusion.places_ref, bf16[512,8192]{1,0:T(8,128)(2,1)} %mine_ref.13, bf16[512,8192]{1,0:T(8,128)(2,1)} %collective-permute-done.1.theirs_ref, bf16[256,512]{1,0:T(8,128)(2,1)} %collective-permute-done.6.refs_0_, ...), custom_call_target="tpu_custom_call", output_to_operand_aliasing={{0}: (9, {})} | custom-call | flops 1073741824 | bytes 2097152 | tf_op jit(solution)/shard_map/pallas_call | solution.py:78
  58.1 1.6 %collective-permute-start.28 = (bf16[128,512]{1,0:T(8,128)(2,1)S(1)}, bf16[128,512]{1,0:T(8,128)(2,1)S(1)}, u32[]{:S(2)}, u32[]{:S(2)}) collective-permute-start(bf16[128,512]{1,0:T(8,128)(2,1)S(1)} %collective-permute-done.21.refs_4_), channel_id=1, source_target_pairs={{4,0},{8,4},{12,8},{14,12},{10,14},{6,10},{2,6},{0,2},{5,1},{9,5},... | collective-permute-start | bytes 393224 | tf_op jit(solution)/shard_map/ppermute | solution.py:153
  60.9 1.2 collective-permute-start.22
  62.1 3.9 %shard_map.84 = (f32[1024,512]{1,0:T(8,128)S(1)}, f32[8,128]{1,0:T(8,128)}) custom-call(s32[3]{0:T(128)S(1)} %add_add_fusion.1.places_ref, bf16[512,8192]{1,0:T(8,128)(2,1)} %mine_ref.13, bf16[512,8192]{1,0:T(8,128)(2,1)} %collective-permute-done.1.theirs_ref, bf16[256,512]{1,0:T(8,128)(2,1)} %collective-permute-done.7.refs_0_, ...), custom_call_target="tpu_custom_call", output_to_operand_aliasing={{0}: (9, {})} | custom-call | flops 1073741824 | bytes 2097152 | tf_op jit(solution)/shard_map/pallas_call | solution.py:78
  66.1 1.6 %collective-permute-start.32 = (bf16[256,512]{1,0:T(8,128)(2,1)}, bf16[256,512]{1,0:T(8,128)(2,1)}, u32[]{:S(2)}, u32[]{:S(2)}) collective-permute-start(bf16[256,512]{1,0:T(8,128)(2,1)} %collective-permute-done.23.refs_3_), channel_id=1, source_target_pairs={{4,0},{8,4},{12,8},{14,12},{10,14},{6,10},{2,6},{0,2},{5,1},{9,5},... | collective-permute-start | bytes 786440 | tf_op jit(solution)/shard_map/ppermute | solution.py:152
  68.2 1.5 %collective-permute-start.29 = (bf16[128,512]{1,0:T(8,128)(2,1)S(1)}, bf16[128,512]{1,0:T(8,128)(2,1)S(1)}, u32[]{:S(2)}, u32[]{:S(2)}) collective-permute-start(bf16[128,512]{1,0:T(8,128)(2,1)S(1)} %collective-permute-done.28.refs_4_), channel_id=1, source_target_pairs={{4,0},{8,4},{12,8},{14,12},{10,14},{6,10},{2,6},{0,2},{5,1},{9,5},... | collective-permute-start | bytes 393224 | tf_op jit(solution)/shard_map/ppermute | solution.py:153
  70.3 0.9 copy-done.4
  71.2 0.9 copy-done.6
  72.1 3.8 %shard_map.85 = (f32[1024,512]{1,0:T(8,128)S(1)}, f32[8,128]{1,0:T(8,128)}) custom-call(s32[3]{0:T(128)S(1)} %add_add_fusion.2.places_ref, bf16[512,8192]{1,0:T(8,128)(2,1)} %mine_ref.13, bf16[512,8192]{1,0:T(8,128)(2,1)} %collective-permute-done.1.theirs_ref, bf16[256,512]{1,0:T(8,128)(2,1)} %collective-permute-done.9.refs_0_, ...), custom_call_target="tpu_custom_call", output_to_operand_aliasing={{0}: (9, {})} | custom-call | flops 1073741824 | bytes 2097152 | tf_op jit(solution)/shard_map/pallas_call | solution.py:78
  75.9 1.4 collective-permute-done.26.refs_1_
  77.3 0.7 pad_maximum_fusion.4
  78.4 1.9 %collective-permute-start.33 = (bf16[256,512]{1,0:T(8,128)(2,1)}, bf16[256,512]{1,0:T(8,128)(2,1)}, u32[]{:S(2)}, u32[]{:S(2)}) collective-permute-start(bf16[256,512]{1,0:T(8,128)(2,1)} %collective-permute-done.32.refs_3_), channel_id=1, source_target_pairs={{4,0},{8,4},{12,8},{14,12},{10,14},{6,10},{2,6},{0,2},{5,1},{9,5},... | collective-permute-start | bytes 786440 | tf_op jit(solution)/shard_map/ppermute | solution.py:152
  81.3 1.7 %collective-permute-start.37 = (bf16[256,512]{1,0:T(8,128)(2,1)}, bf16[256,512]{1,0:T(8,128)(2,1)S(1)}, u32[]{:S(2)}, u32[]{:S(2)}) collective-permute-start(bf16[256,512]{1,0:T(8,128)(2,1)} %pad_maximum_fusion.5), channel_id=1, source_target_pairs={{0,16},{16,0},{1,17},{17,1},{2,18},{18,2},{3,19},{19,3},{4,20},{20... | collective-permute-start | bytes 786440 | tf_op jit(solution)/shard_map/ppermute | solution.py:155
  83.1 1.3 collective-permute-start.35
  85.2 1.7 %collective-permute-done.33.refs_3_ = bf16[256,512]{1,0:T(8,128)(2,1)} collective-permute-done((bf16[256,512]{1,0:T(8,128)(2,1)}, bf16[256,512]{1,0:T(8,128)(2,1)}, u32[]{:S(2)}, u32[]{:S(2)}) %collective-permute-start.33) | collective-permute-done | bytes 262176 | tf_op jit(solution)/shard_map/ppermute | solution.py:152
  87.0 1.5 %collective-permute-start.34 = (bf16[256,512]{1,0:T(8,128)(2,1)}, bf16[256,512]{1,0:T(8,128)(2,1)S(1)}, u32[]{:S(2)}, u32[]{:S(2)}) collective-permute-start(bf16[256,512]{1,0:T(8,128)(2,1)} %collective-permute-done.33.refs_3_), channel_id=1, source_target_pairs={{4,0},{8,4},{12,8},{14,12},{10,14},{6,10},{2,6},{0,2},{5,1},{9,5},... | collective-permute-start | bytes 786440 | tf_op jit(solution)/shard_map/ppermute | solution.py:152
  89.0 1.4 %collective-permute-start.31 = (bf16[128,512]{1,0:T(8,128)(2,1)S(1)}, bf16[128,512]{1,0:T(8,128)(2,1)S(1)}, u32[]{:S(2)}, u32[]{:S(2)}) collective-permute-start(bf16[128,512]{1,0:T(8,128)(2,1)S(1)} %get-tuple-element.84), channel_id=1, source_target_pairs={{0,4},{4,8},{8,12},{12,14},{14,10},{10,6},{6,2},{2,0},{1,5},{5,9},... | collective-permute-start | bytes 393224 | tf_op jit(solution)/shard_map/ppermute | solution.py:162
  91.1 3.8 %shard_map.86 = (f32[1024,512]{1,0:T(8,128)S(1)}, f32[8,128]{1,0:T(8,128)}) custom-call(s32[3]{0:T(128)S(1)} %add_add_fusion.4.places_ref, bf16[512,8192]{1,0:T(8,128)(2,1)} %mine_ref.13, bf16[512,8192]{1,0:T(8,128)(2,1)} %collective-permute-done.1.theirs_ref, bf16[256,512]{1,0:T(8,128)(2,1)} %collective-permute-done.14.refs_0_, ...), custom_call_target="tpu_custom_call", output_to_operand_aliasing={{0}: (9, {})} | custom-call | flops 1073741824 | bytes 2097152 | tf_op jit(solution)/shard_map/pallas_call | solution.py:78
  95.0 3.8 %shard_map.87 = (f32[1024,512]{1,0:T(8,128)S(1)}, f32[8,128]{1,0:T(8,128)}) custom-call(s32[3]{0:T(128)S(1)} %add_add_fusion.3.places_ref, bf16[512,8192]{1,0:T(8,128)(2,1)} %mine_ref.13, bf16[512,8192]{1,0:T(8,128)(2,1)} %collective-permute-done.1.theirs_ref, bf16[256,512]{1,0:T(8,128)(2,1)} %collective-permute-done.19.refs_0_, ...), custom_call_target="tpu_custom_call", output_to_operand_aliasing={{0}: (9, {})} | custom-call | flops 1073741824 | bytes 2097152 | tf_op jit(solution)/shard_map/pallas_call | solution.py:78
  98.9 3.3 %shard_map.88 = (bf16[1024,512]{1,0:T(8,128)(2,1)S(1)}, f32[8,128]{1,0:T(8,128)}) custom-call(s32[5]{0:T(128)S(1)} %stack.95.places_ref, bf16[512,8192]{1,0:T(8,128)(2,1)} %mine_ref.13, bf16[512,8192]{1,0:T(8,128)(2,1)} %collective-permute-done.1.theirs_ref, bf16[256,512]{1,0:T(8,128)(2,1)S(1)} %collective-permute-done.24.refs_0_, ...), custom_call_target="tpu_custom_call" | custom-call | flops 1073741824 | bytes 2097152 | tf_op jit(solution)/shard_map/pallas_call | solution.py:78
  102.9 2.0 %collective-permute-done.38.got_any = bf16[1024,512]{1,0:T(8,128)(2,1)S(1)} collective-permute-done((bf16[1024,512]{1,0:T(8,128)(2,1)S(1)}, bf16[1024,512]{1,0:T(8,128)(2,1)S(1)}, u32[]{:S(2)}, u32[]{:S(2)}) %collective-permute-start.38) | collective-permute-done | bytes 1048608 | tf_op jit(solution)/shard_map/ppermute | solution.py:296
  104.9 4.8 %shard_map.89 = f32[8,9,8,128]{3,2,1,0:T(8,128)} custom-call(s32[1]{0:T(128)} %bitcast.core_ref, bf16[1024,512]{1,0:T(8,128)(2,1)S(1)} %get-tuple-element.74.have_any, bf16[1024,512]{1,0:T(8,128)(2,1)S(1)} %collective-permute-done.38.got_any, bf16[512,1024]{1,0:T(8,128)(2,1)} %key_any.1, bf16[512,1024]{1,0:T(8,128)(2,1)} %value_any.1, ...), custom_call_target="tpu_custom_call" | custom-call | flops 1342177280 | bytes 2097152 | tf_op jit(solution)/shard_map/pallas_call | solution.py:226
  109.7 1.5 %fusion.11 = bf16[16,1024]{1,0:T(8,128)(2,1)S(1)} fusion(bf16[512,1024]{1,0:T(8,128)(2,1)} %key_any.1, bf16[16,1024]{1,0:T(8,128)(2,1)S(1)} %reshape.89), kind=kOutput, calls=%fused_computation.38 | convolution fusion | flops 16777216 | bytes 1097728 | tf_op jit(solution)/shard_map/dot_general | solution.py:18
  111.2 1.5 %fusion.9 = bf16[16,1024]{1,0:T(8,128)(2,1)S(1)} fusion(bf16[512,1024]{1,0:T(8,128)(2,1)} %value_any.1, bf16[16,1024]{1,0:T(8,128)(2,1)S(1)} %reshape.89), kind=kOutput, calls=%fused_computation.36 | convolution fusion | flops 16777216 | bytes 1097728 | tf_op jit(solution)/shard_map/dot_general | solution.py:18
  113.5 4.9 %all-to-all-start = ((f32[8,72,128]{2,1,0:T(8,128)}), f32[8,72,128]{2,1,0:T(8,128)S(1)}, u32[]{:S(2)}, u32[]{:S(2)}) async-start(f32[8,72,128]{2,1,0:T(8,128)} %bitcast.25), calls=%async_computation | async-start | bytes 589824 | tf_op jit(solution)/shard_map/all_to_all | solution.py:328
  119.6 8.6 %all-to-all-done = f32[8,72,128]{2,1,0:T(8,128)S(1)} async-done(((f32[8,72,128]{2,1,0:T(8,128)}), f32[8,72,128]{2,1,0:T(8,128)S(1)}, u32[]{:S(2)}, u32[]{:S(2)}) %all-to-all-start) | async-done | bytes 294944 | tf_op jit(solution)/shard_map/all_to_all | solution.py:328
  128.6 1.5 %collective-permute-start.39 = (bf16[64,128]{1,0:T(8,128)(2,1)S(1)}, bf16[64,128]{1,0:T(8,128)(2,1)S(1)}, u32[]{:S(2)}, u32[]{:S(2)}) collective-permute-start(bf16[64,128]{1,0:T(8,128)(2,1)S(1)} %shard_map.90), channel_id=1, source_target_pairs={{0,2},{2,0},{4,6},{6,4},{8,10},{10,8},{12,14},{14,12},{1,3},{3,1},... | collective-permute-start | bytes 49160 | tf_op jit(solution)/shard_map/ppermute | solution.py:332
  130.1 2.3 %collective-permute-done.39 = bf16[64,128]{1,0:T(8,128)(2,1)S(1)} collective-permute-done((bf16[64,128]{1,0:T(8,128)(2,1)S(1)}, bf16[64,128]{1,0:T(8,128)(2,1)S(1)}, u32[]{:S(2)}, u32[]{:S(2)}) %collective-permute-start.39) | collective-permute-done | bytes 16416 | tf_op jit(solution)/shard_map/ppermute | solution.py:332
  132.4 1.2 collective-permute-start.40
  133.7 1.3 collective-permute-start.41
  135.0 1.9 %collective-permute-start.42 = (bf16[128,128]{1,0:T(8,128)(2,1)S(1)}, bf16[128,128]{1,0:T(8,128)(2,1)S(1)}, u32[]{:S(2)}, u32[]{:S(2)}) collective-permute-start(bf16[128,128]{1,0:T(8,128)(2,1)S(1)} %pad_maximum_fusion.8), channel_id=1, source_target_pairs={{0,4},{2,6},{4,0},{6,2},{8,12},{10,14},{12,8},{14,10},{1,5},{3,7},... | collective-permute-start | bytes 98312 | tf_op jit(solution)/shard_map/ppermute | solution.py:335
  136.9 1.3 collective-permute-done.40
  138.2 0.8 collective-permute-done.41
  139.4 1.3 collective-permute-done.43
  141.1 0.9 reshape.98
  (128 shorter events, 13.6 us)
Async XLA Ops:
  0.0 102.6 %copy-start = (bf16[4,4,8192]{2,1,0:T(4,128)(2,1)S(1)}, bf16[4,4,8192]{2,1,0:T(4,128)(2,1)}, u32[]{:S(2)}) copy-start(bf16[4,4,8192]{2,1,0:T(4,128)(2,1)} %param.14) | copy-start | bytes 786436
  1.3 2.1 %collective-permute-start = (bf16[512,512]{1,0:T(8,128)(2,1)S(1)}, bf16[512,512]{1,0:T(8,128)(2,1)S(1)}, u32[]{:S(2)}, u32[]{:S(2)}) collective-permute-start(bf16[512,512]{1,0:T(8,128)(2,1)S(1)} %get-tuple-element.80), channel_id=1, source_target_pairs={{0,1},{1,0},{2,3},{3,2},{4,5},{5,4},{6,7},{7,6},{8,9},{9,8},{10,11... | collective-permute-start | bytes 1572872 | tf_op jit(solution)/shard_map/ppermute | solution.py:109
  3.4 34.0 %collective-permute-start.1 = (bf16[512,8192]{1,0:T(8,128)(2,1)}, bf16[512,8192]{1,0:T(8,128)(2,1)}, u32[]{:S(2)}, u32[]{:S(2)}) collective-permute-start(bf16[512,8192]{1,0:T(8,128)(2,1)} %mine_ref.13), channel_id=1, source_target_pairs={{0,1},{1,0},{2,3},{3,2},{4,5},{5,4},{6,7},{7,6},{8,9},{9,8},{10,11... | collective-permute-start | bytes 25165832 | tf_op jit(solution)/shard_map/ppermute | solution.py:138
  3.8 7.1 %collective-permute-start.4 = (bf16[128,512]{1,0:T(8,128)(2,1)S(1)}, bf16[128,512]{1,0:T(8,128)(2,1)S(1)}, u32[]{:S(2)}, u32[]{:S(2)}) collective-permute-start(bf16[128,512]{1,0:T(8,128)(2,1)S(1)} %slice_select_fusion), channel_id=1, source_target_pairs={{0,4},{4,8},{8,12},{12,14},{14,10},{10,6},{6,2},{2,0},{1,5},{5,9},... | collective-permute-start | bytes 393224 | tf_op jit(solution)/shard_map/ppermute | solution.py:153
  6.6 9.6 %collective-permute-start.2 = (bf16[256,512]{1,0:T(8,128)(2,1)S(1)}, bf16[256,512]{1,0:T(8,128)(2,1)S(1)}, u32[]{:S(2)}, u32[]{:S(2)}) collective-permute-start(bf16[256,512]{1,0:T(8,128)(2,1)S(1)} %slice.40), channel_id=1, source_target_pairs={{0,4},{4,8},{8,12},{12,14},{14,10},{10,6},{6,2},{2,0},{1,5},{5,9},... | collective-permute-start | bytes 786440 | tf_op jit(solution)/shard_map/ppermute | solution.py:152
  8.2 10.9 %collective-permute-start.3 = (bf16[256,512]{1,0:T(8,128)(2,1)S(1)}, bf16[256,512]{1,0:T(8,128)(2,1)S(1)}, u32[]{:S(2)}, u32[]{:S(2)}) collective-permute-start(bf16[256,512]{1,0:T(8,128)(2,1)S(1)} %slice.31), channel_id=1, source_target_pairs={{4,0},{8,4},{12,8},{14,12},{10,14},{6,10},{2,6},{0,2},{5,1},{9,5},... | collective-permute-start | bytes 786440 | tf_op jit(solution)/shard_map/ppermute | solution.py:152
  8.7 10.4 %collective-permute-start.5 = (bf16[128,512]{1,0:T(8,128)(2,1)S(1)}, bf16[128,512]{1,0:T(8,128)(2,1)S(1)}, u32[]{:S(2)}, u32[]{:S(2)}) collective-permute-start(bf16[128,512]{1,0:T(8,128)(2,1)S(1)} %slice_select_fusion.1), channel_id=1, source_target_pairs={{4,0},{8,4},{12,8},{14,12},{10,14},{6,10},{2,6},{0,2},{5,1},{9,5},... | collective-permute-start | bytes 393224 | tf_op jit(solution)/shard_map/ppermute | solution.py:153
  10.8 26.6 %copy-start.7 = (bf16[128,512]{1,0:T(8,128)(2,1)}, bf16[128,512]{1,0:T(8,128)(2,1)S(1)}, u32[]{:S(2)}) copy-start(bf16[128,512]{1,0:T(8,128)(2,1)S(1)} %collective-permute-done.4.refs_3_) | copy-start | bytes 393220
  16.1 21.3 %copy-start.11 = (bf16[256,512]{1,0:T(8,128)(2,1)}, bf16[256,512]{1,0:T(8,128)(2,1)S(1)}, u32[]{:S(2)}) copy-start(bf16[256,512]{1,0:T(8,128)(2,1)S(1)} %collective-permute-done.2.refs_2_) | copy-start | bytes 786436
  19.1 18.3 %copy-start.9 = (bf16[128,512]{1,0:T(8,128)(2,1)}, bf16[128,512]{1,0:T(8,128)(2,1)S(1)}, u32[]{:S(2)}) copy-start(bf16[128,512]{1,0:T(8,128)(2,1)S(1)} %collective-permute-done.5.refs_6_) | copy-start | bytes 393220
  19.1 18.4 %copy-start.13 = (bf16[256,512]{1,0:T(8,128)(2,1)}, bf16[256,512]{1,0:T(8,128)(2,1)S(1)}, u32[]{:S(2)}) copy-start(bf16[256,512]{1,0:T(8,128)(2,1)S(1)} %collective-permute-done.3.refs_5_) | copy-start | bytes 786436
  19.1 6.4 %collective-permute-start.11 = (bf16[128,512]{1,0:T(8,128)(2,1)S(1)}, bf16[128,512]{1,0:T(8,128)(2,1)S(1)}, u32[]{:S(2)}, u32[]{:S(2)}) collective-permute-start(bf16[128,512]{1,0:T(8,128)(2,1)S(1)} %collective-permute-done.5.refs_6_), channel_id=1, source_target_pairs={{4,0},{8,4},{12,8},{14,12},{10,14},{6,10},{2,6},{0,2},{5,1},{9,5},... | collective-permute-start | bytes 393224 | tf_op jit(solution)/shard_map/ppermute | solution.py:153
  19.6 14.2 %collective-permute-start.8 = (bf16[256,512]{1,0:T(8,128)(2,1)S(1)}, bf16[256,512]{1,0:T(8,128)(2,1)S(1)}, u32[]{:S(2)}, u32[]{:S(2)}) collective-permute-start(bf16[256,512]{1,0:T(8,128)(2,1)S(1)} %pad_maximum_fusion), channel_id=1, source_target_pairs={{0,16},{16,0},{1,17},{17,1},{2,18},{18,2},{3,19},{19,3},{4,20},{20... | collective-permute-start | bytes 786440 | tf_op jit(solution)/shard_map/ppermute | solution.py:155
  21.2 14.2 %collective-permute-start.13 = (bf16[256,512]{1,0:T(8,128)(2,1)S(1)}, bf16[256,512]{1,0:T(8,128)(2,1)}, u32[]{:S(2)}, u32[]{:S(2)}) collective-permute-start(bf16[256,512]{1,0:T(8,128)(2,1)S(1)} %collective-permute-done.3.refs_5_), channel_id=1, source_target_pairs={{4,0},{8,4},{12,8},{14,12},{10,14},{6,10},{2,6},{0,2},{5,1},{9,5},... | collective-permute-start | bytes 786440 | tf_op jit(solution)/shard_map/ppermute | solution.py:152
  21.6 14.9 %collective-permute-start.6 = (bf16[256,512]{1,0:T(8,128)(2,1)S(1)}, bf16[256,512]{1,0:T(8,128)(2,1)}, u32[]{:S(2)}, u32[]{:S(2)}) collective-permute-start(bf16[256,512]{1,0:T(8,128)(2,1)S(1)} %collective-permute-done.2.refs_2_), channel_id=1, source_target_pairs={{0,4},{4,8},{8,12},{12,14},{14,10},{10,6},{6,2},{2,0},{1,5},{5,9},... | collective-permute-start | bytes 786440 | tf_op jit(solution)/shard_map/ppermute | solution.py:152
  25.5 5.5 %collective-permute-start.10 = (bf16[128,512]{1,0:T(8,128)(2,1)S(1)}, bf16[128,512]{1,0:T(8,128)(2,1)}, u32[]{:S(2)}, u32[]{:S(2)}) collective-permute-start(bf16[128,512]{1,0:T(8,128)(2,1)S(1)} %collective-permute-done.4.refs_3_), channel_id=1, source_target_pairs={{0,4},{4,8},{8,12},{12,14},{14,10},{10,6},{6,2},{2,0},{1,5},{5,9},... | collective-permute-start | bytes 393224 | tf_op jit(solution)/shard_map/ppermute | solution.py:153
  32.6 21.1 %collective-permute-start.12 = (bf16[256,512]{1,0:T(8,128)(2,1)}, bf16[256,512]{1,0:T(8,128)(2,1)}, u32[]{:S(2)}, u32[]{:S(2)}) collective-permute-start(bf16[256,512]{1,0:T(8,128)(2,1)} %pad_maximum_fusion.1), channel_id=1, source_target_pairs={{0,16},{16,0},{1,17},{17,1},{2,18},{18,2},{3,19},{19,3},{4,20},{20... | collective-permute-start | bytes 786440 | tf_op jit(solution)/shard_map/ppermute | solution.py:155
  33.8 0.7 copy-start.1
  34.5 13.5 %collective-permute-start.16 = (bf16[128,512]{1,0:T(8,128)(2,1)S(1)}, bf16[128,512]{1,0:T(8,128)(2,1)}, u32[]{:S(2)}, u32[]{:S(2)}) collective-permute-start(bf16[128,512]{1,0:T(8,128)(2,1)S(1)} %collective-permute-done.11.refs_4_), channel_id=1, source_target_pairs={{4,0},{8,4},{12,8},{14,12},{10,14},{6,10},{2,6},{0,2},{5,1},{9,5},... | collective-permute-start | bytes 393224 | tf_op jit(solution)/shard_map/ppermute | solution.py:153
  35.4 13.6 %collective-permute-start.15 = (bf16[128,512]{1,0:T(8,128)(2,1)}, bf16[128,512]{1,0:T(8,128)(2,1)}, u32[]{:S(2)}, u32[]{:S(2)}) collective-permute-start(bf16[128,512]{1,0:T(8,128)(2,1)} %collective-permute-done.10.refs_1_), channel_id=1, source_target_pairs={{0,4},{4,8},{8,12},{12,14},{14,10},{10,6},{6,2},{2,0},{1,5},{5,9},... | collective-permute-start | bytes 393224 | tf_op jit(solution)/shard_map/ppermute | solution.py:153
  36.5 14.6 %collective-permute-start.18 = (bf16[256,512]{1,0:T(8,128)(2,1)}, bf16[256,512]{1,0:T(8,128)(2,1)}, u32[]{:S(2)}, u32[]{:S(2)}) collective-permute-start(bf16[256,512]{1,0:T(8,128)(2,1)} %collective-permute-done.13.refs_3_), channel_id=1, source_target_pairs={{4,0},{8,4},{12,8},{14,12},{10,14},{6,10},{2,6},{0,2},{5,1},{9,5},... | collective-permute-start | bytes 786440 | tf_op jit(solution)/shard_map/ppermute | solution.py:152
  37.5 14.6 %collective-permute-start.7 = (bf16[256,512]{1,0:T(8,128)(2,1)}, bf16[256,512]{1,0:T(8,128)(2,1)}, u32[]{:S(2)}, u32[]{:S(2)}) collective-permute-start(bf16[256,512]{1,0:T(8,128)(2,1)} %collective-permute-done.6.refs_0_), channel_id=1, source_target_pairs={{0,4},{4,8},{8,12},{12,14},{14,10},{10,6},{6,2},{2,0},{1,5},{5,9},... | collective-permute-start | bytes 786440 | tf_op jit(solution)/shard_map/ppermute | solution.py:152
  38.6 0.9 copy-start.2
  39.6 0.9 copy-start.8
  40.5 0.9 copy-start.10
  41.4 0.9 copy-start.12
  42.3 0.9 copy-start.14
  48.0 10.0 %collective-permute-start.21 = (bf16[128,512]{1,0:T(8,128)(2,1)}, bf16[128,512]{1,0:T(8,128)(2,1)S(1)}, u32[]{:S(2)}, u32[]{:S(2)}) collective-permute-start(bf16[128,512]{1,0:T(8,128)(2,1)} %collective-permute-done.16.refs_4_), channel_id=1, source_target_pairs={{4,0},{8,4},{12,8},{14,12},{10,14},{6,10},{2,6},{0,2},{5,1},{9,5},... | collective-permute-start | bytes 393224 | tf_op jit(solution)/shard_map/ppermute | solution.py:153
  49.0 10.7 %collective-permute-start.20 = (bf16[128,512]{1,0:T(8,128)(2,1)}, bf16[128,512]{1,0:T(8,128)(2,1)S(1)}, u32[]{:S(2)}, u32[]{:S(2)}) collective-permute-start(bf16[128,512]{1,0:T(8,128)(2,1)} %collective-permute-done.15.refs_1_), channel_id=1, source_target_pairs={{0,4},{4,8},{8,12},{12,14},{14,10},{10,6},{6,2},{2,0},{1,5},{5,9},... | collective-permute-start | bytes 393224 | tf_op jit(solution)/shard_map/ppermute | solution.py:153
  51.1 9.8 %collective-permute-start.17 = (bf16[256,512]{1,0:T(8,128)(2,1)S(1)}, bf16[256,512]{1,0:T(8,128)(2,1)S(1)}, u32[]{:S(2)}, u32[]{:S(2)}) collective-permute-start(bf16[256,512]{1,0:T(8,128)(2,1)S(1)} %pad_maximum_fusion.2), channel_id=1, source_target_pairs={{0,16},{16,0},{1,17},{17,1},{2,18},{18,2},{3,19},{19,3},{4,20},{20... | collective-permute-start | bytes 786440 | tf_op jit(solution)/shard_map/ppermute | solution.py:155
  52.1 14.0 %collective-permute-start.23 = (bf16[256,512]{1,0:T(8,128)(2,1)}, bf16[256,512]{1,0:T(8,128)(2,1)}, u32[]{:S(2)}, u32[]{:S(2)}) collective-permute-start(bf16[256,512]{1,0:T(8,128)(2,1)} %collective-permute-done.18.refs_3_), channel_id=1, source_target_pairs={{4,0},{8,4},{12,8},{14,12},{10,14},{6,10},{2,6},{0,2},{5,1},{9,5},... | collective-permute-start | bytes 786440 | tf_op jit(solution)/shard_map/ppermute | solution.py:152
  53.7 14.0 %collective-permute-start.9 = (bf16[256,512]{1,0:T(8,128)(2,1)}, bf16[256,512]{1,0:T(8,128)(2,1)}, u32[]{:S(2)}, u32[]{:S(2)}) collective-permute-start(bf16[256,512]{1,0:T(8,128)(2,1)} %collective-permute-done.7.refs_0_), channel_id=1, source_target_pairs={{0,4},{4,8},{8,12},{12,14},{14,10},{10,6},{6,2},{2,0},{1,5},{5,9},... | collective-permute-start | bytes 786440 | tf_op jit(solution)/shard_map/ppermute | solution.py:152
  58.1 8.0 %copy-start.3 = (bf16[128,512]{1,0:T(8,128)(2,1)}, bf16[128,512]{1,0:T(8,128)(2,1)S(1)}, u32[]{:S(2)}) copy-start(bf16[128,512]{1,0:T(8,128)(2,1)S(1)} %collective-permute-done.21.refs_4_) | copy-start | bytes 393220
  58.1 8.0 %collective-permute-start.28 = (bf16[128,512]{1,0:T(8,128)(2,1)S(1)}, bf16[128,512]{1,0:T(8,128)(2,1)S(1)}, u32[]{:S(2)}, u32[]{:S(2)}) collective-permute-start(bf16[128,512]{1,0:T(8,128)(2,1)S(1)} %collective-permute-done.21.refs_4_), channel_id=1, source_target_pairs={{4,0},{8,4},{12,8},{14,12},{10,14},{6,10},{2,6},{0,2},{5,1},{9,5},... | collective-permute-start | bytes 393224 | tf_op jit(solution)/shard_map/ppermute | solution.py:153
  59.7 6.3 %copy-start.5 = (bf16[128,512]{1,0:T(8,128)(2,1)}, bf16[128,512]{1,0:T(8,128)(2,1)S(1)}, u32[]{:S(2)}) copy-start(bf16[128,512]{1,0:T(8,128)(2,1)S(1)} %collective-permute-done.20.refs_1_) | copy-start | bytes 393220
  59.7 6.4 %collective-permute-start.25 = (bf16[128,512]{1,0:T(8,128)(2,1)S(1)}, bf16[128,512]{1,0:T(8,128)(2,1)S(1)}, u32[]{:S(2)}, u32[]{:S(2)}) collective-permute-start(bf16[128,512]{1,0:T(8,128)(2,1)S(1)} %collective-permute-done.20.refs_1_), channel_id=1, source_target_pairs={{0,4},{4,8},{8,12},{12,14},{14,10},{10,6},{6,2},{2,0},{1,5},{5,9},... | collective-permute-start | bytes 393224 | tf_op jit(solution)/shard_map/ppermute | solution.py:153
  60.9 9.4 %collective-permute-start.22 = (bf16[256,512]{1,0:T(8,128)(2,1)}, bf16[256,512]{1,0:T(8,128)(2,1)S(1)}, u32[]{:S(2)}, u32[]{:S(2)}) collective-permute-start(bf16[256,512]{1,0:T(8,128)(2,1)} %pad_maximum_fusion.3), channel_id=1, source_target_pairs={{0,16},{16,0},{1,17},{17,1},{2,18},{18,2},{3,19},{19,3},{4,20},{20... | collective-permute-start | bytes 786440 | tf_op jit(solution)/shard_map/ppermute | solution.py:155
  66.1 12.4 %collective-permute-start.32 = (bf16[256,512]{1,0:T(8,128)(2,1)}, bf16[256,512]{1,0:T(8,128)(2,1)}, u32[]{:S(2)}, u32[]{:S(2)}) collective-permute-start(bf16[256,512]{1,0:T(8,128)(2,1)} %collective-permute-done.23.refs_3_), channel_id=1, source_target_pairs={{4,0},{8,4},{12,8},{14,12},{10,14},{6,10},{2,6},{0,2},{5,1},{9,5},... | collective-permute-start | bytes 786440 | tf_op jit(solution)/shard_map/ppermute | solution.py:152
  67.7 12.6 %collective-permute-start.14 = (bf16[256,512]{1,0:T(8,128)(2,1)}, bf16[256,512]{1,0:T(8,128)(2,1)}, u32[]{:S(2)}, u32[]{:S(2)}) collective-permute-start(bf16[256,512]{1,0:T(8,128)(2,1)} %collective-permute-done.9.refs_0_), channel_id=1, source_target_pairs={{0,4},{4,8},{8,12},{12,14},{14,10},{10,6},{6,2},{2,0},{1,5},{5,9},... | collective-permute-start | bytes 786440 | tf_op jit(solution)/shard_map/ppermute | solution.py:152
  68.2 7.8 %collective-permute-start.29 = (bf16[128,512]{1,0:T(8,128)(2,1)S(1)}, bf16[128,512]{1,0:T(8,128)(2,1)S(1)}, u32[]{:S(2)}, u32[]{:S(2)}) collective-permute-start(bf16[128,512]{1,0:T(8,128)(2,1)S(1)} %collective-permute-done.28.refs_4_), channel_id=1, source_target_pairs={{4,0},{8,4},{12,8},{14,12},{10,14},{6,10},{2,6},{0,2},{5,1},{9,5},... | collective-permute-start | bytes 393224 | tf_op jit(solution)/shard_map/ppermute | solution.py:153
  69.7 7.7 %collective-permute-start.26 = (bf16[128,512]{1,0:T(8,128)(2,1)S(1)}, bf16[128,512]{1,0:T(8,128)(2,1)S(1)}, u32[]{:S(2)}, u32[]{:S(2)}) collective-permute-start(bf16[128,512]{1,0:T(8,128)(2,1)S(1)} %collective-permute-done.25.refs_1_), channel_id=1, source_target_pairs={{0,4},{4,8},{8,12},{12,14},{14,10},{10,6},{6,2},{2,0},{1,5},{5,9},... | collective-permute-start | bytes 393224 | tf_op jit(solution)/shard_map/ppermute | solution.py:153
  70.3 0.9 copy-start.4
  71.2 0.9 copy-start.6
  78.1 6.6 %collective-permute-start.30 = (bf16[256,512]{1,0:T(8,128)(2,1)}, bf16[256,512]{1,0:T(8,128)(2,1)S(1)}, u32[]{:S(2)}, u32[]{:S(2)}) collective-permute-start(bf16[256,512]{1,0:T(8,128)(2,1)} %pad_maximum_fusion.4), channel_id=1, source_target_pairs={{0,16},{16,0},{1,17},{17,1},{2,18},{18,2},{3,19},{19,3},{4,20},{20... | collective-permute-start | bytes 786440 | tf_op jit(solution)/shard_map/ppermute | solution.py:155
  78.4 8.5 %collective-permute-start.33 = (bf16[256,512]{1,0:T(8,128)(2,1)}, bf16[256,512]{1,0:T(8,128)(2,1)}, u32[]{:S(2)}, u32[]{:S(2)}) collective-permute-start(bf16[256,512]{1,0:T(8,128)(2,1)} %collective-permute-done.32.refs_3_), channel_id=1, source_target_pairs={{4,0},{8,4},{12,8},{14,12},{10,14},{6,10},{2,6},{0,2},{5,1},{9,5},... | collective-permute-start | bytes 786440 | tf_op jit(solution)/shard_map/ppermute | solution.py:152
  80.3 8.2 %collective-permute-start.19 = (bf16[256,512]{1,0:T(8,128)(2,1)}, bf16[256,512]{1,0:T(8,128)(2,1)}, u32[]{:S(2)}, u32[]{:S(2)}) collective-permute-start(bf16[256,512]{1,0:T(8,128)(2,1)} %collective-permute-done.14.refs_0_), channel_id=1, source_target_pairs={{0,4},{4,8},{8,12},{12,14},{14,10},{10,6},{6,2},{2,0},{1,5},{5,9},... | collective-permute-start | bytes 786440 | tf_op jit(solution)/shard_map/ppermute | solution.py:152
  81.3 7.8 %collective-permute-start.37 = (bf16[256,512]{1,0:T(8,128)(2,1)}, bf16[256,512]{1,0:T(8,128)(2,1)S(1)}, u32[]{:S(2)}, u32[]{:S(2)}) collective-permute-start(bf16[256,512]{1,0:T(8,128)(2,1)} %pad_maximum_fusion.5), channel_id=1, source_target_pairs={{0,16},{16,0},{1,17},{17,1},{2,18},{18,2},{3,19},{19,3},{4,20},{20... | collective-permute-start | bytes 786440 | tf_op jit(solution)/shard_map/ppermute | solution.py:155
  83.1 7.4 %collective-permute-start.35 = (bf16[128,512]{1,0:T(8,128)(2,1)S(1)}, bf16[128,512]{1,0:T(8,128)(2,1)S(1)}, u32[]{:S(2)}, u32[]{:S(2)}) collective-permute-start(bf16[128,512]{1,0:T(8,128)(2,1)S(1)} %collective-permute-done.29.refs_4_), channel_id=1, source_target_pairs={{4,0},{8,4},{12,8},{14,12},{10,14},{6,10},{2,6},{0,2},{5,1},{9,5},... | collective-permute-start | bytes 393224 | tf_op jit(solution)/shard_map/ppermute | solution.py:153
  84.6 14.2 %collective-permute-start.27 = (bf16[128,512]{1,0:T(8,128)(2,1)S(1)}, bf16[128,512]{1,0:T(8,128)(2,1)S(1)}, u32[]{:S(2)}, u32[]{:S(2)}) collective-permute-start(bf16[128,512]{1,0:T(8,128)(2,1)S(1)} %collective-permute-done.26.refs_1_), channel_id=1, source_target_pairs={{0,4},{4,8},{8,12},{12,14},{14,10},{10,6},{6,2},{2,0},{1,5},{5,9},... | collective-permute-start | bytes 393224 | tf_op jit(solution)/shard_map/ppermute | solution.py:153
  87.0 11.9 %collective-permute-start.34 = (bf16[256,512]{1,0:T(8,128)(2,1)}, bf16[256,512]{1,0:T(8,128)(2,1)S(1)}, u32[]{:S(2)}, u32[]{:S(2)}) collective-permute-start(bf16[256,512]{1,0:T(8,128)(2,1)} %collective-permute-done.33.refs_3_), channel_id=1, source_target_pairs={{4,0},{8,4},{12,8},{14,12},{10,14},{6,10},{2,6},{0,2},{5,1},{9,5},... | collective-permute-start | bytes 786440 | tf_op jit(solution)/shard_map/ppermute | solution.py:152
  88.5 10.3 %collective-permute-start.24 = (bf16[256,512]{1,0:T(8,128)(2,1)}, bf16[256,512]{1,0:T(8,128)(2,1)S(1)}, u32[]{:S(2)}, u32[]{:S(2)}) collective-permute-start(bf16[256,512]{1,0:T(8,128)(2,1)} %collective-permute-done.19.refs_0_), channel_id=1, source_target_pairs={{0,4},{4,8},{8,12},{12,14},{14,10},{10,6},{6,2},{2,0},{1,5},{5,9},... | collective-permute-start | bytes 786440 | tf_op jit(solution)/shard_map/ppermute | solution.py:152
  89.0 9.8 %collective-permute-start.31 = (bf16[128,512]{1,0:T(8,128)(2,1)S(1)}, bf16[128,512]{1,0:T(8,128)(2,1)S(1)}, u32[]{:S(2)}, u32[]{:S(2)}) collective-permute-start(bf16[128,512]{1,0:T(8,128)(2,1)S(1)} %get-tuple-element.84), channel_id=1, source_target_pairs={{0,4},{4,8},{8,12},{12,14},{14,10},{10,6},{6,2},{2,0},{1,5},{5,9},... | collective-permute-start | bytes 393224 | tf_op jit(solution)/shard_map/ppermute | solution.py:162
  90.5 8.3 %collective-permute-start.36 = (bf16[128,512]{1,0:T(8,128)(2,1)S(1)}, bf16[128,512]{1,0:T(8,128)(2,1)S(1)}, u32[]{:S(2)}, u32[]{:S(2)}) collective-permute-start(bf16[128,512]{1,0:T(8,128)(2,1)S(1)} %get-tuple-element.83), channel_id=1, source_target_pairs={{4,0},{8,4},{12,8},{14,12},{10,14},{6,10},{2,6},{0,2},{5,1},{9,5},... | collective-permute-start | bytes 393224 | tf_op jit(solution)/shard_map/ppermute | solution.py:162
  98.8 3.4 %copy-start.16 = (s32[4]{0:T(128)S(1)}, s32[4]{0:T(128)}, u32[]{:S(2)}) copy-start(s32[4]{0:T(128)} %param.13) | copy-start | bytes 52
  102.1 2.7 %collective-permute-start.38 = (bf16[1024,512]{1,0:T(8,128)(2,1)S(1)}, bf16[1024,512]{1,0:T(8,128)(2,1)S(1)}, u32[]{:S(2)}, u32[]{:S(2)}) collective-permute-start(bf16[1024,512]{1,0:T(8,128)(2,1)S(1)} %get-tuple-element.74.have_any), channel_id=1, source_target_pairs={{0,1},{1,0},{2,3},{3,2},{4,5},{5,4},{6,7},{7,6},{8,9},{9,8},{10,11... | collective-permute-start | bytes 3145736 | tf_op jit(solution)/shard_map/ppermute | solution.py:296
  104.9 4.8 %copy-start.15 = (bf16[4,4,1024]{2,1,0:T(4,128)(2,1)S(1)}, bf16[4,4,1024]{2,1,0:T(4,128)(2,1)}, u32[]{:S(2)}) copy-start(bf16[4,4,1024]{2,1,0:T(4,128)(2,1)} %param.15) | copy-start | bytes 98308
  113.5 14.8 %all-to-all-start = ((f32[8,72,128]{2,1,0:T(8,128)}), f32[8,72,128]{2,1,0:T(8,128)S(1)}, u32[]{:S(2)}, u32[]{:S(2)}) async-start(f32[8,72,128]{2,1,0:T(8,128)} %bitcast.25), calls=%async_computation | async-start | bytes 589824 | tf_op jit(solution)/shard_map/all_to_all | solution.py:328
  128.6 3.8 %collective-permute-start.39 = (bf16[64,128]{1,0:T(8,128)(2,1)S(1)}, bf16[64,128]{1,0:T(8,128)(2,1)S(1)}, u32[]{:S(2)}, u32[]{:S(2)}) collective-permute-start(bf16[64,128]{1,0:T(8,128)(2,1)S(1)} %shard_map.90), channel_id=1, source_target_pairs={{0,2},{2,0},{4,6},{6,4},{8,10},{10,8},{12,14},{14,12},{1,3},{3,1},... | collective-permute-start | bytes 49160 | tf_op jit(solution)/shard_map/ppermute | solution.py:332
  132.4 5.8 %collective-permute-start.40 = (bf16[128,128]{1,0:T(8,128)(2,1)S(1)}, bf16[128,128]{1,0:T(8,128)(2,1)S(1)}, u32[]{:S(2)}, u32[]{:S(2)}) collective-permute-start(bf16[128,128]{1,0:T(8,128)(2,1)S(1)} %pad_maximum_fusion.8), channel_id=1, source_target_pairs={{0,12},{2,14},{4,8},{6,10},{8,4},{10,6},{12,0},{14,2},{1,13},{3,15... | collective-permute-start | bytes 98312 | tf_op jit(solution)/shard_map/ppermute | solution.py:335
  133.7 5.3 %collective-permute-start.41 = (bf16[128,128]{1,0:T(8,128)(2,1)S(1)}, bf16[128,128]{1,0:T(8,128)(2,1)S(1)}, u32[]{:S(2)}, u32[]{:S(2)}) collective-permute-start(bf16[128,128]{1,0:T(8,128)(2,1)S(1)} %pad_maximum_fusion.8), channel_id=1, source_target_pairs={{0,8},{2,10},{4,12},{6,14},{8,0},{10,2},{12,4},{14,6},{1,9},{3,11}... | collective-permute-start | bytes 98312 | tf_op jit(solution)/shard_map/ppermute | solution.py:335
  135.0 4.2 %collective-permute-start.42 = (bf16[128,128]{1,0:T(8,128)(2,1)S(1)}, bf16[128,128]{1,0:T(8,128)(2,1)S(1)}, u32[]{:S(2)}, u32[]{:S(2)}) collective-permute-start(bf16[128,128]{1,0:T(8,128)(2,1)S(1)} %pad_maximum_fusion.8), channel_id=1, source_target_pairs={{0,4},{2,6},{4,0},{6,2},{8,12},{10,14},{12,8},{14,10},{1,5},{3,7},... | collective-permute-start | bytes 98312 | tf_op jit(solution)/shard_map/ppermute | solution.py:335
  139.4 1.4 collective-permute-start.43

commit v12 on v10

--- a/solution.py
+++ b/solution.py
@@ -153,9 +153,27 @@
     blocks = pairs * heads // chips
     scale = 1.0 / DH**0.5
 
-    def kernel(core_ref, have_any, got_any, key_any, value_any, query_any, bounds_ref, out_ref, *scratch):
-        latents, ups, query_ref, sems = scratch
+    split = chips == 8
+
+    def kernel(core_ref, have_any, got_any, key_any, value_any, query_any, bounds_ref, *refs):
+        outs = refs[:-4]
+        latents, ups, query_ref, sems = refs[-4:]
         core = core_ref[0]
+
+        def put(chip, block, value):
+            if not split:
+                outs[0][chip, block, :, : value.shape[1]] = value
+                return
+            same = core_ref[1] == chip % 2
+
+            @pl.when(same)
+            def _():
+                outs[0][chip // 2, block, :, : value.shape[1]] = value
+
+            @pl.when(jnp.logical_not(same))
+            def _():
+                outs[1][chip // 2, block, :, : value.shape[1]] = value
+
         lanes = pl.ds(pl.multiple_of(core * heads * DH, heads * DH), heads * DH)
         pairs_of = [
             (have_any, latents.at[core]),
@@ -191,7 +209,7 @@
             )
             for pair in range(pairs):
                 block = pair * heads + g
-                out_ref[block // blocks, block % blocks] = summed[pair * 8 : (pair + 1) * 8]
+                put(block // blocks, block % blocks, summed[pair * 8 : (pair + 1) * 8])
         stats = jnp.transpose(jnp.concatenate(tops + totals, 0))
         stride = min(blocks, heads)
         for chip in range(chips):
@@ -199,16 +217,15 @@
             sides = [
                 stats[pair * 8 : (pair + 1) * 8, side + g : side + g + stride] for side in (0, heads) for pair, g in spots
             ]
-            out_ref[chip, blocks] = jnp.zeros((8, DH), F32)
-            out_ref[chip, blocks, :, : 2 * blocks] = jnp.concatenate(sides, 1)
+            put(chip, blocks, jnp.concatenate(sides + [jnp.zeros((8, DH - 2 * blocks), F32)], 1))
 
     ups = [pltpu.with_memory_space_constraint(x, pltpu.HBM) for x in (key_up, value_up)]
     in_vmem = pl.BlockSpec(memory_space=pltpu.VMEM)
     return pl.pallas_call(
         kernel,
-        out_shape=jax.ShapeDtypeStruct((chips, blocks + 1, 8, DH), F32),
+        out_shape=[jax.ShapeDtypeStruct((chips // (1 + split), blocks + 1, 8, DH), F32)] * (1 + split),
         in_specs=[pl.BlockSpec(memory_space=pltpu.SMEM)] + [pl.BlockSpec(memory_space=pl.ANY)] * 5 + [in_vmem],
-        out_specs=in_vmem,
+        out_specs=[in_vmem] * (1 + split),
         scratch_shapes=[
             pltpu.VMEM((2,) + have.shape, BF),
             pltpu.VMEM((2, have.shape[1], heads * DH), BF),
@@ -221,23 +238,33 @@
             bytes_accessed=4 * tokens * have.shape[1],
             transcendentals=tokens * heads * rows,
         ),
-    )(core.reshape(1), have, got, *ups, query, bounds)
-
-
-def merge(arrived, fresh_stats, fresh_summed):
-    chips, blocks = arrived.shape[0], arrived.shape[1] - 1
-
-    def kernel(arrived_ref, stats_ref, summed_ref, out_ref):
+    )(jnp.stack([core, lax.axis_index("chip") & 1]), have, got, *ups, query, bounds)
+
+
+def merge(sources, fresh_stats, fresh_summed):
+    count = len(sources)
+    blocks = sources[0].shape[-3] - 1
+
+    def kernel(*refs):
+        stats_ref, summed_ref, out_ref = refs[count:]
+        parts = refs[:count]
+        if len(parts[0].shape) == 4:
+            parts = [parts[0].at[i] for i in range(parts[0].shape[0])]
         results = []
         for b in range(blocks):
-            top = arrived_ref[:, blocks, :, b : b + 1]
-            total = arrived_ref[:, blocks, :, blocks + b : blocks + b + 1]
+            tops = [part[blocks, :, b : b + 1] for part in parts]
+            totals = [part[blocks, :, blocks + b : blocks + b + 1] for part in parts]
             fresh_top = stats_ref[:, b : b + 1]
-            overall = jnp.maximum(jnp.max(top, 0), fresh_top)
-            carried = jnp.exp(top - overall[None])
-            fresh_carried = jnp.exp(fresh_top - overall)
-            total = jnp.sum(total * carried, 0) + stats_ref[:, blocks + b : blocks + b + 1] * fresh_carried
-            summed = jnp.sum(arrived_ref[:, b] * carried, 0) + summed_ref[b * 8 : (b + 1) * 8, :] * fresh_carried
+            overall = fresh_top
+            for top in tops:
+                overall = jnp.maximum(overall, top)
+            carried = jnp.exp(fresh_top - overall)
+            total = stats_ref[:, blocks + b : blocks + b + 1] * carried
+            summed = summed_ref[b * 8 : (b + 1) * 8, :] * carried
+            for part, top, more in zip(parts, tops, totals):
+                carried = jnp.exp(top - overall)
+                total = total + more * carried
+                summed = summed + part[b] * carried
             results.append(summed / total)
         out_ref[...] = jnp.concatenate(results, 0).astype(BF)
 
@@ -245,13 +272,37 @@
     return pl.pallas_call(
         kernel,
         out_shape=jax.ShapeDtypeStruct((blocks * 8, DH), BF),
-        in_specs=[in_vmem] * 3,
+        in_specs=[in_vmem] * (count + 2),
         out_specs=in_vmem,
         compiler_params=pltpu.CompilerParams(vmem_limit_bytes=8 * 2**20),
-        cost_estimate=pl.CostEstimate(
-            flops=2 * chips * blocks * 8 * DH, bytes_accessed=4 * arrived.size, transcendentals=chips * blocks * 8
-        ),
-    )(arrived, fresh_stats, fresh_summed)
+    )(*sources, fresh_stats, fresh_summed)
+
+
+def pair_up(mine, other, place):
+    count, blocks = mine.shape[0], mine.shape[1] - 1
+
+    def kernel(place_ref, mine_ref, other_ref, *outs):
+        for d in range(count):
+            at = place_ref[0] ^ d
+            stats, more = mine_ref[at, blocks], other_ref[at, blocks]
+            tops, totals = [], []
+            for b in range(blocks):
+                one, two = stats[:, b : b + 1], more[:, b : b + 1]
+                top = jnp.maximum(one, two)
+                one, two = jnp.exp(one - top), jnp.exp(two - top)
+                tops.append(top)
+                totals.append(stats[:, blocks + b : blocks + b + 1] * one + more[:, blocks + b : blocks + b + 1] * two)
+                outs[d][b] = mine_ref[at, b] * one + other_ref[at, b] * two
+            outs[d][blocks] = jnp.concatenate(tops + totals + [jnp.zeros((8, DH - 2 * blocks), F32)], 1)
+
+    in_vmem = pl.BlockSpec(memory_space=pltpu.VMEM)
+    return pl.pallas_call(
+        kernel,
+        out_shape=[jax.ShapeDtypeStruct(mine.shape[1:], F32)] * count,
+        in_specs=[pl.BlockSpec(memory_space=pltpu.SMEM), in_vmem, in_vmem],
+        out_specs=[in_vmem] * count,
+        compiler_params=pltpu.CompilerParams(vmem_limit_bytes=8 * 2**20),
+    )(place.reshape(1), mine, other)
 
 
 def on_device(tokens, key_down, value_down, key_up, value_up, prompt_lens, queries, new_latent):
@@ -281,7 +332,7 @@
     bounds = jnp.broadcast_to(bounds[:, None, :, None], (2, steps_count, req_count, group)).reshape(2, -1)
     sending = attend(have, got, core, key_up, value_up, query.reshape(heads, -1, DH), bounds, chips)
 
-    sending, query, new_latent = lax.optimization_barrier((sending, query, new_latent))
+    _, new_latent = lax.optimization_barrier((have, new_latent))
     flat_new = new_latent.reshape(pairs, 2 * lat_width)
 
     def my_heads(latent, up):
@@ -305,9 +356,15 @@
     fresh_stats = [my_share(x.reshape(rows)).reshape(-1, group).T for x in (fresh_top, fresh_total)]
     fresh_stats = jnp.pad(jnp.concatenate(fresh_stats, 1), ((0, 0), (0, DH - 2 * share // group)))
 
-    flat = sending.reshape(chips, -1, DH)
-    arrived = lax.all_to_all(flat, "chip", split_axis=0, concat_axis=0, tiled=True).reshape(sending.shape)
-    result = merge(arrived, fresh_stats, fresh_summed)
+    if chips == 8:
+        near = [(c, c ^ 1) for c in range(chips)]
+        joined = pair_up(sending[0], lax.ppermute(sending[1], "chip", near), chip >> 1)
+        far = [lax.ppermute(joined[d], "chip", [(c, c ^ (2 * d)) for c in range(chips)]) for d in range(1, 4)]
+        result = merge([joined[0]] + far, fresh_stats, fresh_summed)
+    else:
+        flat = sending[0].reshape(chips, -1, DH)
+        arrived = lax.all_to_all(flat, "chip", split_axis=0, concat_axis=0, tiled=True).reshape(sending[0].shape)
+        result = merge([arrived], fresh_stats, fresh_summed)
 
     if chips == 8:
         near = lax.ppermute(result, "chip", [(c, c ^ 1) for c in range(chips)])

time: 136 us -> 138 us (1.015)
  matrix products: 1.51 us -> 3.96 us
  waiting for transfers between devices: 52.1 us -> 49.7 us
  local copies, waits for them, and re-layouts: 3.2 us -> 4.74 us
    ppermute x0 -> x4, waiting for transfers between devices: none -> 9.83 us  [the longest x3 5.29 us: on_device(): lax.ppermute(joined[d], 'chip', [(c, c ^ 2 * d) for c in range(chips)])]
    all_to_all x1 -> x0, waiting for transfers between devices: 8.61 us -> none  [on_device(): lax.all_to_all(flat, 'chip', split_axis=0, concat_axis=0, tiled=True)]
    ppermute x0 -> x4, starting transfers between devices: none -> 5.32 us  [the longest x3 4.45 us: on_device(): lax.ppermute(joined[d], 'chip', [(c, c ^ 2 * d) for c in range(chips)])]
    all_to_all x1 -> x0, starting transfers between devices: 4.83 us -> none  [on_device(): lax.all_to_all(flat, 'chip', split_axis=0, concat_axis=0, tiled=True)]
    dot_general x2, matrix products: 0.5 us -> 2.95 us  [mm(): return jnp.dot(a, b, preferred_element_type=F32)]
    pallas_call x1 -> x2, Pallas kernels: 5.14 us -> 7.38 us  [the longest x1 7.19 us: attend(): pl.pallas_call(kernel, out_shape=[jax.ShapeDtypeStruct((chips // (1 + spl...]
    ppermute x1, waiting for transfers between devices: 2.19 us -> 0.01 us  [on_device(): got = lax.ppermute(have, 'core', SWAP)]
    ppermute x28, waiting for transfers between devices: 33.8 us -> 31.8 us  [project(): held[k] = lax.ppermute(held[k], 'chip', ways[k])]
  transfers between devices with their start and end apart: 37 -> 40, of which waited for: 18 -> 17; matrix products, arithmetic and copies ran while one was open for 2% -> 7% of each run, Pallas kernels for 18% -> 17%
where the time goes in v12:
time: 138 us
  waiting for transfers between devices  49.7 us (36%)
  starting transfers between devices  40.7 us (29%)
  Pallas kernels  35.6 us (26%)
  local copies, waits for them, and re-layouts  4.74 us (3%)
  matrix products  3.96 us (3%)
  other arithmetic  3.07 us (2%)
    ppermute x28, waiting for transfers between devices, project(): held[k] = lax.ppermute(held[k], 'chip', ways[k])  31.8 us
    ppermute x28, starting transfers between devices, project(): held[k] = lax.ppermute(held[k], 'chip', ways[k])  29.3 us
    pallas_call x7, Pallas kernels, add_pieces(): pl.pallas_call(kernel, out_shape=(jax.ShapeDtypeStruct((2 * tok_rows, wid...  28 us
    pallas_call x1, Pallas kernels, attend(): pl.pallas_call(kernel, out_shape=[jax.ShapeDtypeStruct((chips // (1 + spl...  7.19 us
    ppermute x3, waiting for transfers between devices, on_device(): lax.ppermute(joined[d], 'chip', [(c, c ^ 2 * d) for c in range(chips)])  5.29 us
    ppermute x1, waiting for transfers between devices, on_device(): lax.ppermute(sending[1], 'chip', near)  4.54 us
    ppermute x3, starting transfers between devices, on_device(): lax.ppermute(joined[d], 'chip', [(c, c ^ 2 * d) for c in range(chips)])  4.45 us
    ppermute x3, starting transfers between devices, on_device(): lax.ppermute(couple, 'chip', [(c, c ^ 2 * d) for c in range(chips)])  4.45 us
  transfers between devices with their start and end apart: 40, of which 17 were waited for; matrix products, arithmetic and copies ran while one was open for 7% of the time, Pallas kernels for 17%

profile of v12, /device:TPU:0, one launch (start us, length us, event | category | flops | bytes accessed | tf_op | source)
XLA Modules:
  0.0 138.1 jit_solution(15657135640954873940)
XLA Ops:
  0.0 1.3 broadcast_select_fusion
  1.3 0.5 collective-permute-start
  1.9 1.5 %collective-permute-done.refs_1_ = bf16[512,512]{1,0:T(8,128)(2,1)S(1)} collective-permute-done((bf16[512,512]{1,0:T(8,128)(2,1)S(1)}, bf16[512,512]{1,0:T(8,128)(2,1)S(1)}, u32[]{:S(2)}, u32[]{:S(2)}) %collective-permute-start) | collective-permute-done | bytes 524320 | tf_op jit(solution)/shard_map/ppermute | solution.py:101
  3.8 2.8 %collective-permute-start.2 = (bf16[256,512]{1,0:T(8,128)(2,1)S(1)}, bf16[256,512]{1,0:T(8,128)(2,1)}, u32[]{:S(2)}, u32[]{:S(2)}) collective-permute-start(bf16[256,512]{1,0:T(8,128)(2,1)S(1)} %get-tuple-element.102), channel_id=1, source_target_pairs={{0,4},{4,8},{8,12},{12,14},{14,10},{10,6},{6,2},{2,0},{1,5},{5,9},... | collective-permute-start | bytes 786440 | tf_op jit(solution)/shard_map/ppermute | solution.py:139
  6.6 1.6 %collective-permute-start.3 = (bf16[256,512]{1,0:T(8,128)(2,1)S(1)}, bf16[256,512]{1,0:T(8,128)(2,1)}, u32[]{:S(2)}, u32[]{:S(2)}) collective-permute-start(bf16[256,512]{1,0:T(8,128)(2,1)S(1)} %get-tuple-element.101), channel_id=1, source_target_pairs={{0,4},{4,8},{8,12},{12,14},{14,10},{10,6},{6,2},{2,0},{1,5},{5,9},... | collective-permute-start | bytes 786440 | tf_op jit(solution)/shard_map/ppermute | solution.py:139
  8.2 0.5 collective-permute-start.4
  8.8 0.6 iota_compare_fusion.1
  9.5 4.2 %collective-permute-done.2.refs_2_ = bf16[256,512]{1,0:T(8,128)(2,1)} collective-permute-done((bf16[256,512]{1,0:T(8,128)(2,1)S(1)}, bf16[256,512]{1,0:T(8,128)(2,1)}, u32[]{:S(2)}, u32[]{:S(2)}) %collective-permute-start.2) | collective-permute-done | bytes 262176 | tf_op jit(solution)/shard_map/ppermute | solution.py:139
  13.8 5.3 %collective-permute-done.3.refs_3_ = bf16[256,512]{1,0:T(8,128)(2,1)} collective-permute-done((bf16[256,512]{1,0:T(8,128)(2,1)S(1)}, bf16[256,512]{1,0:T(8,128)(2,1)}, u32[]{:S(2)}, u32[]{:S(2)}) %collective-permute-start.3) | collective-permute-done | bytes 262176 | tf_op jit(solution)/shard_map/ppermute | solution.py:139
  19.1 2.9 %collective-permute-done.5.refs_5_ = bf16[256,512]{1,0:T(8,128)(2,1)} collective-permute-done((bf16[256,512]{1,0:T(8,128)(2,1)S(1)}, bf16[256,512]{1,0:T(8,128)(2,1)}, u32[]{:S(2)}, u32[]{:S(2)}) %collective-permute-start.5) | collective-permute-done | bytes 262176 | tf_op jit(solution)/shard_map/ppermute | solution.py:139
  22.4 1.6 %collective-permute-start.6 = (bf16[256,512]{1,0:T(8,128)(2,1)}, bf16[256,512]{1,0:T(8,128)(2,1)}, u32[]{:S(2)}, u32[]{:S(2)}) collective-permute-start(bf16[256,512]{1,0:T(8,128)(2,1)} %collective-permute-done.2.refs_2_), channel_id=1, source_target_pairs={{0,4},{4,8},{8,12},{12,14},{14,10},{10,6},{6,2},{2,0},{1,5},{5,9},... | collective-permute-start | bytes 786440 | tf_op jit(solution)/shard_map/ppermute | solution.py:139
  24.0 1.6 %collective-permute-start.8 = (bf16[256,512]{1,0:T(8,128)(2,1)}, bf16[256,512]{1,0:T(8,128)(2,1)}, u32[]{:S(2)}, u32[]{:S(2)}) collective-permute-start(bf16[256,512]{1,0:T(8,128)(2,1)} %collective-permute-done.3.refs_3_), channel_id=1, source_target_pairs={{0,4},{4,8},{8,12},{12,14},{14,10},{10,6},{6,2},{2,0},{1,5},{5,9},... | collective-permute-start | bytes 786440 | tf_op jit(solution)/shard_map/ppermute | solution.py:139
  25.6 0.4 collective-permute-start.9
  26.1 5.7 %shard_map.82 = (f32[1024,512]{1,0:T(8,128)S(1)}, f32[8,128]{1,0:T(8,128)}) custom-call(s32[4]{0:T(128)S(1)} %pad_add_fusion.2.places_ref, bf16[512,8192]{1,0:T(8,128)(2,1)} %mine_ref.13, bf16[512,8192]{1,0:T(8,128)(2,1)} %collective-permute-done.1.theirs_ref, bf16[512,512]{1,0:T(8,128)(2,1)S(1)} %get-tuple-element.97.refs_0_, ...), custom_call_target="tpu_custom_call" | custom-call | flops 2147483648 | bytes 4194304 | tf_op jit(solution)/shard_map/pallas_call | solution.py:71
  31.8 0.5 collective-permute-start.14
  32.3 4.8 %collective-permute-done.9.refs_2_ = bf16[256,512]{1,0:T(8,128)(2,1)} collective-permute-done((bf16[256,512]{1,0:T(8,128)(2,1)}, bf16[256,512]{1,0:T(8,128)(2,1)}, u32[]{:S(2)}, u32[]{:S(2)}) %collective-permute-start.9) | collective-permute-done | bytes 262176 | tf_op jit(solution)/shard_map/ppermute | solution.py:139
  37.2 0.4 collective-permute-start.13
  37.6 1.6 %collective-permute-start.12 = (bf16[256,512]{1,0:T(8,128)(2,1)}, bf16[256,512]{1,0:T(8,128)(2,1)S(1)}, u32[]{:S(2)}, u32[]{:S(2)}) collective-permute-start(bf16[256,512]{1,0:T(8,128)(2,1)} %collective-permute-done.8.refs_1_), channel_id=1, source_target_pairs={{0,4},{4,8},{8,12},{12,14},{14,10},{10,6},{6,2},{2,0},{1,5},{5,9},... | collective-permute-start | bytes 786440 | tf_op jit(solution)/shard_map/ppermute | solution.py:139
  39.2 1.6 %collective-permute-start.7 = (bf16[256,512]{1,0:T(8,128)(2,1)}, bf16[256,512]{1,0:T(8,128)(2,1)S(1)}, u32[]{:S(2)}, u32[]{:S(2)}) collective-permute-start(bf16[256,512]{1,0:T(8,128)(2,1)} %collective-permute-done.6.refs_0_), channel_id=1, source_target_pairs={{0,4},{4,8},{8,12},{12,14},{14,10},{10,6},{6,2},{2,0},{1,5},{5,9},... | collective-permute-start | bytes 786440 | tf_op jit(solution)/shard_map/ppermute | solution.py:139
  40.9 3.9 %shard_map.83 = (f32[1024,512]{1,0:T(8,128)S(1)}, f32[8,128]{1,0:T(8,128)}) custom-call(s32[2]{0:T(128)S(1)} %pad_add_fusion.3.places_ref, bf16[512,8192]{1,0:T(8,128)(2,1)} %mine_ref.13, bf16[512,8192]{1,0:T(8,128)(2,1)} %collective-permute-done.1.theirs_ref, bf16[256,512]{1,0:T(8,128)(2,1)} %collective-permute-done.6.refs_0_, ...), custom_call_target="tpu_custom_call", output_to_operand_aliasing={{0}: (7, {})} | custom-call | flops 1073741824 | bytes 2097152 | tf_op jit(solution)/shard_map/pallas_call | solution.py:71
  44.8 0.5 collective-permute-start.18
  45.3 3.0 %collective-permute-done.13.refs_2_ = bf16[256,512]{1,0:T(8,128)(2,1)S(1)} collective-permute-done((bf16[256,512]{1,0:T(8,128)(2,1)}, bf16[256,512]{1,0:T(8,128)(2,1)S(1)}, u32[]{:S(2)}, u32[]{:S(2)}) %collective-permute-start.13) | collective-permute-done | bytes 262176 | tf_op jit(solution)/shard_map/ppermute | solution.py:139
  48.7 1.6 %collective-permute-start.16 = (bf16[256,512]{1,0:T(8,128)(2,1)S(1)}, bf16[256,512]{1,0:T(8,128)(2,1)}, u32[]{:S(2)}, u32[]{:S(2)}) collective-permute-start(bf16[256,512]{1,0:T(8,128)(2,1)S(1)} %collective-permute-done.12.refs_1_), channel_id=1, source_target_pairs={{0,4},{4,8},{8,12},{12,14},{14,10},{10,6},{6,2},{2,0},{1,5},{5,9},... | collective-permute-start | bytes 786440 | tf_op jit(solution)/shard_map/ppermute | solution.py:139
  50.3 1.6 %collective-permute-start.11 = (bf16[256,512]{1,0:T(8,128)(2,1)S(1)}, bf16[256,512]{1,0:T(8,128)(2,1)}, u32[]{:S(2)}, u32[]{:S(2)}) collective-permute-start(bf16[256,512]{1,0:T(8,128)(2,1)S(1)} %collective-permute-done.7.refs_0_), channel_id=1, source_target_pairs={{0,4},{4,8},{8,12},{12,14},{14,10},{10,6},{6,2},{2,0},{1,5},{5,9},... | collective-permute-start | bytes 786440 | tf_op jit(solution)/shard_map/ppermute | solution.py:139
  52.0 3.3 %shard_map.84 = (f32[1024,512]{1,0:T(8,128)S(1)}, f32[8,128]{1,0:T(8,128)}) custom-call(s32[2]{0:T(128)S(1)} %pad_add_fusion.4.places_ref, bf16[512,8192]{1,0:T(8,128)(2,1)} %mine_ref.13, bf16[512,8192]{1,0:T(8,128)(2,1)} %collective-permute-done.1.theirs_ref, bf16[256,512]{1,0:T(8,128)(2,1)S(1)} %collective-permute-done.7.refs_0_, ...), custom_call_target="tpu_custom_call", output_to_operand_aliasing={{0}: (7, {})} | custom-call | flops 1073741824 | bytes 2097152 | tf_op jit(solution)/shard_map/pallas_call | solution.py:71
  55.3 0.5 collective-permute-start.22
  55.8 4.0 %collective-permute-done.17.refs_2_ = bf16[256,512]{1,0:T(8,128)(2,1)} collective-permute-done((bf16[256,512]{1,0:T(8,128)(2,1)S(1)}, bf16[256,512]{1,0:T(8,128)(2,1)}, u32[]{:S(2)}, u32[]{:S(2)}) %collective-permute-start.17) | collective-permute-done | bytes 262176 | tf_op jit(solution)/shard_map/ppermute | solution.py:139
  60.3 1.6 %collective-permute-start.20 = (bf16[256,512]{1,0:T(8,128)(2,1)}, bf16[256,512]{1,0:T(8,128)(2,1)S(1)}, u32[]{:S(2)}, u32[]{:S(2)}) collective-permute-start(bf16[256,512]{1,0:T(8,128)(2,1)} %collective-permute-done.16.refs_1_), channel_id=1, source_target_pairs={{0,4},{4,8},{8,12},{12,14},{14,10},{10,6},{6,2},{2,0},{1,5},{5,9},... | collective-permute-start | bytes 786440 | tf_op jit(solution)/shard_map/ppermute | solution.py:139
  61.9 1.5 %collective-permute-start.15 = (bf16[256,512]{1,0:T(8,128)(2,1)}, bf16[256,512]{1,0:T(8,128)(2,1)S(1)}, u32[]{:S(2)}, u32[]{:S(2)}) collective-permute-start(bf16[256,512]{1,0:T(8,128)(2,1)} %collective-permute-done.11.refs_0_), channel_id=1, source_target_pairs={{0,4},{4,8},{8,12},{12,14},{14,10},{10,6},{6,2},{2,0},{1,5},{5,9},... | collective-permute-start | bytes 786440 | tf_op jit(solution)/shard_map/ppermute | solution.py:139
  63.5 3.9 %shard_map.85 = (f32[1024,512]{1,0:T(8,128)S(1)}, f32[8,128]{1,0:T(8,128)}) custom-call(s32[2]{0:T(128)S(1)} %pad_add_fusion.5.places_ref, bf16[512,8192]{1,0:T(8,128)(2,1)} %mine_ref.13, bf16[512,8192]{1,0:T(8,128)(2,1)} %collective-permute-done.1.theirs_ref, bf16[256,512]{1,0:T(8,128)(2,1)} %collective-permute-done.11.refs_0_, ...), custom_call_target="tpu_custom_call", output_to_operand_aliasing={{0}: (7, {})} | custom-call | flops 1073741824 | bytes 2097152 | tf_op jit(solution)/shard_map/pallas_call | solution.py:71
  67.4 0.6 collective-permute-start.28
  67.9 3.0 %collective-permute-done.21.refs_2_ = bf16[256,512]{1,0:T(8,128)(2,1)S(1)} collective-permute-done((bf16[256,512]{1,0:T(8,128)(2,1)}, bf16[256,512]{1,0:T(8,128)(2,1)S(1)}, u32[]{:S(2)}, u32[]{:S(2)}) %collective-permute-start.21) | collective-permute-done | bytes 262176 | tf_op jit(solution)/shard_map/ppermute | solution.py:139
  71.4 1.6 %collective-permute-start.24 = (bf16[256,512]{1,0:T(8,128)(2,1)S(1)}, bf16[256,512]{1,0:T(8,128)(2,1)}, u32[]{:S(2)}, u32[]{:S(2)}) collective-permute-start(bf16[256,512]{1,0:T(8,128)(2,1)S(1)} %collective-permute-done.20.refs_1_), channel_id=1, source_target_pairs={{0,4},{4,8},{8,12},{12,14},{14,10},{10,6},{6,2},{2,0},{1,5},{5,9},... | collective-permute-start | bytes 786440 | tf_op jit(solution)/shard_map/ppermute | solution.py:139
  73.0 1.5 %collective-permute-start.19 = (bf16[256,512]{1,0:T(8,128)(2,1)S(1)}, bf16[256,512]{1,0:T(8,128)(2,1)}, u32[]{:S(2)}, u32[]{:S(2)}) collective-permute-start(bf16[256,512]{1,0:T(8,128)(2,1)S(1)} %collective-permute-done.15.refs_0_), channel_id=1, source_target_pairs={{0,4},{4,8},{8,12},{12,14},{14,10},{10,6},{6,2},{2,0},{1,5},{5,9},... | collective-permute-start | bytes 786440 | tf_op jit(solution)/shard_map/ppermute | solution.py:139
  74.8 3.3 %shard_map.86 = (f32[1024,512]{1,0:T(8,128)S(1)}, f32[8,128]{1,0:T(8,128)}) custom-call(s32[2]{0:T(128)S(1)} %pad_add_fusion.6.places_ref, bf16[512,8192]{1,0:T(8,128)(2,1)} %mine_ref.13, bf16[512,8192]{1,0:T(8,128)(2,1)} %collective-permute-done.1.theirs_ref, bf16[256,512]{1,0:T(8,128)(2,1)S(1)} %collective-permute-done.15.refs_0_, ...), custom_call_target="tpu_custom_call", output_to_operand_aliasing={{0}: (7, {})} | custom-call | flops 1073741824 | bytes 2097152 | tf_op jit(solution)/shard_map/pallas_call | solution.py:71
  78.1 0.6 collective-permute-start.29
  78.7 3.7 %collective-permute-done.26.refs_2_ = bf16[256,512]{1,0:T(8,128)(2,1)} collective-permute-done((bf16[256,512]{1,0:T(8,128)(2,1)S(1)}, bf16[256,512]{1,0:T(8,128)(2,1)}, u32[]{:S(2)}, u32[]{:S(2)}) %collective-permute-start.26) | collective-permute-done | bytes 262176 | tf_op jit(solution)/shard_map/ppermute | solution.py:139
  82.4 0.5 collective-permute-start.27
  82.9 1.5 %collective-permute-start.25 = (bf16[256,512]{1,0:T(8,128)(2,1)}, bf16[256,512]{1,0:T(8,128)(2,1)S(1)}, u32[]{:S(2)}, u32[]{:S(2)}) collective-permute-start(bf16[256,512]{1,0:T(8,128)(2,1)} %collective-permute-done.24.refs_1_), channel_id=1, source_target_pairs={{0,4},{4,8},{8,12},{12,14},{14,10},{10,6},{6,2},{2,0},{1,5},{5,9},... | collective-permute-start | bytes 786440 | tf_op jit(solution)/shard_map/ppermute | solution.py:139
  84.4 1.4 %collective-permute-start.23 = (bf16[256,512]{1,0:T(8,128)(2,1)}, bf16[256,512]{1,0:T(8,128)(2,1)S(1)}, u32[]{:S(2)}, u32[]{:S(2)}) collective-permute-start(bf16[256,512]{1,0:T(8,128)(2,1)} %collective-permute-done.19.refs_0_), channel_id=1, source_target_pairs={{0,4},{4,8},{8,12},{12,14},{14,10},{10,6},{6,2},{2,0},{1,5},{5,9},... | collective-permute-start | bytes 786440 | tf_op jit(solution)/shard_map/ppermute | solution.py:139
  85.9 0.8 reshape.77
  86.7 0.9 copy.40
  87.7 3.9 %shard_map.87 = (f32[1024,512]{1,0:T(8,128)S(1)}, f32[8,128]{1,0:T(8,128)}) custom-call(s32[2]{0:T(128)S(1)} %pad_add_fusion.7.places_ref, bf16[512,8192]{1,0:T(8,128)(2,1)} %mine_ref.13, bf16[512,8192]{1,0:T(8,128)(2,1)} %collective-permute-done.1.theirs_ref, bf16[256,512]{1,0:T(8,128)(2,1)} %collective-permute-done.19.refs_0_, ...), custom_call_target="tpu_custom_call", output_to_operand_aliasing={{0}: (7, {})} | custom-call | flops 1073741824 | bytes 2097152 | tf_op jit(solution)/shard_map/pallas_call | solution.py:71
  91.6 0.7 collective-permute-done.23.refs_0_
  92.3 4.2 %shard_map.88 = (bf16[1024,512]{1,0:T(8,128)(2,1)}, f32[8,128]{1,0:T(8,128)}) custom-call(s32[4]{0:T(128)S(1)} %pad_add_fusion.1.places_ref, bf16[512,8192]{1,0:T(8,128)(2,1)} %mine_ref.13, bf16[512,8192]{1,0:T(8,128)(2,1)} %collective-permute-done.1.theirs_ref, bf16[256,512]{1,0:T(8,128)(2,1)S(1)} %collective-permute-done.23.refs_0_, ...), custom_call_target="tpu_custom_call" | custom-call | flops 1073741824 | bytes 2097152 | tf_op jit(solution)/shard_map/pallas_call | solution.py:71
  96.6 0.8 reshape.81
  97.4 1.5 %fusion.10 = bf16[16,1024]{1,0:T(8,128)(2,1)S(1)} fusion(bf16[512,1024]{1,0:T(8,128)(2,1)} %value_any.1, bf16[16,1024]{1,0:T(8,128)(2,1)S(1)} %reshape.81), kind=kOutput, calls=%fused_computation.29 | convolution fusion | flops 16777216 | bytes 1097728 | tf_op jit(solution)/shard_map/dot_general | solution.py:18
  98.9 1.5 %fusion.12 = bf16[16,1024]{1,0:T(8,128)(2,1)S(1)} fusion(bf16[512,1024]{1,0:T(8,128)(2,1)} %key_any.1, bf16[16,1024]{1,0:T(8,128)(2,1)S(1)} %reshape.81), kind=kOutput, calls=%fused_computation.31 | convolution fusion | flops 16777216 | bytes 1097728 | tf_op jit(solution)/shard_map/dot_general | solution.py:18
  100.4 0.7 fusion.20
  101.4 7.2 %shard_map.89 = (f32[4,9,8,128]{3,2,1,0:T(8,128)S(1)}, f32[4,9,8,128]{3,2,1,0:T(8,128)S(1)}) custom-call(s32[2]{0:T(128)S(1)} %pad_add_fusion.core_ref, bf16[1024,512]{1,0:T(8,128)(2,1)} %get-tuple-element.88.have_any, bf16[1024,512]{1,0:T(8,128)(2,1)S(1)} %collective-permute-done.30.got_any, bf16[512,1024]{1,0:T(8,128)(2,1)} %key_any.1, ...), custom_call_target="tpu_custom_call" | custom-call | flops 1342177280 | bytes 2097152 | tf_op jit(solution)/shard_map/pallas_call | solution.py:224
  108.6 0.9 collective-permute-start.31
  110.4 4.5 %collective-permute-done.31.other_ref = f32[4,9,8,128]{3,2,1,0:T(8,128)S(1)} collective-permute-done((f32[4,9,8,128]{3,2,1,0:T(8,128)S(1)}, f32[4,9,8,128]{3,2,1,0:T(8,128)S(1)}, u32[]{:S(2)}, u32[]{:S(2)}) %collective-permute-start.31) | collective-permute-done | bytes 147488 | tf_op jit(solution)/shard_map/ppermute | solution.py:361
  115.1 1.6 %collective-permute-start.32 = (f32[9,8,128]{2,1,0:T(8,128)S(1)}, f32[9,8,128]{2,1,0:T(8,128)S(1)}, u32[]{:S(2)}, u32[]{:S(2)}) collective-permute-start(f32[9,8,128]{2,1,0:T(8,128)S(1)} %get-tuple-element.93), channel_id=1, source_target_pairs={{0,4},{2,6},{4,0},{6,2},{8,12},{10,14},{12,8},{14,10},{1,5},{3,7},... | collective-permute-start | bytes 110600 | tf_op jit(solution)/shard_map/ppermute | solution.py:362
  116.7 2.5 %collective-permute-start.33 = (f32[9,8,128]{2,1,0:T(8,128)S(1)}, f32[9,8,128]{2,1,0:T(8,128)S(1)}, u32[]{:S(2)}, u32[]{:S(2)}) collective-permute-start(f32[9,8,128]{2,1,0:T(8,128)S(1)} %get-tuple-element.94), channel_id=1, source_target_pairs={{0,8},{2,10},{4,12},{6,14},{8,0},{10,2},{12,4},{14,6},{1,9},{3,11}... | collective-permute-start | bytes 110600 | tf_op jit(solution)/shard_map/ppermute | solution.py:362
  119.7 2.4 %collective-permute-done.33.refs_2_ = f32[9,8,128]{2,1,0:T(8,128)S(1)} collective-permute-done((f32[9,8,128]{2,1,0:T(8,128)S(1)}, f32[9,8,128]{2,1,0:T(8,128)S(1)}, u32[]{:S(2)}, u32[]{:S(2)}) %collective-permute-start.33) | collective-permute-done | bytes 36896 | tf_op jit(solution)/shard_map/ppermute | solution.py:362
  122.1 2.9 %collective-permute-done.34.refs_3_ = f32[9,8,128]{2,1,0:T(8,128)S(1)} collective-permute-done((f32[9,8,128]{2,1,0:T(8,128)S(1)}, f32[9,8,128]{2,1,0:T(8,128)S(1)}, u32[]{:S(2)}, u32[]{:S(2)}) %collective-permute-start.34) | collective-permute-done | bytes 36896 | tf_op jit(solution)/shard_map/ppermute | solution.py:362
  125.1 0.5 collective-permute-start.35
  125.6 3.3 %collective-permute-done.35 = bf16[64,128]{1,0:T(8,128)(2,1)S(1)} collective-permute-done((bf16[64,128]{1,0:T(8,128)(2,1)S(1)}, bf16[64,128]{1,0:T(8,128)(2,1)S(1)}, u32[]{:S(2)}, u32[]{:S(2)}) %collective-permute-start.35) | collective-permute-done | bytes 16416 | tf_op jit(solution)/shard_map/ppermute | solution.py:370
  128.9 0.5 collective-permute-start.36
  129.6 3.8 %collective-permute-start.38 = (bf16[128,128]{1,0:T(8,128)(2,1)S(1)}, bf16[128,128]{1,0:T(8,128)(2,1)S(1)}, u32[]{:S(2)}, u32[]{:S(2)}) collective-permute-start(bf16[128,128]{1,0:T(8,128)(2,1)S(1)} %pad_maximum_fusion.2), channel_id=1, source_target_pairs={{0,4},{2,6},{4,0},{6,2},{8,12},{10,14},{12,8},{14,10},{1,5},{3,7},... | collective-permute-start | bytes 98312 | tf_op jit(solution)/shard_map/ppermute | solution.py:373
  133.4 1.3 collective-permute-done.36
  134.7 0.6 collective-permute-done.38
  135.5 1.3 collective-permute-done.39
  137.2 0.9 reshape.90
  (85 shorter events, 6.2 us)
Async XLA Ops:
  0.0 85.9 %copy-start = (bf16[4,4,8192]{2,1,0:T(4,128)(2,1)S(1)}, bf16[4,4,8192]{2,1,0:T(4,128)(2,1)}, u32[]{:S(2)}) copy-start(bf16[4,4,8192]{2,1,0:T(4,128)(2,1)} %param.14) | copy-start | bytes 786436
  0.0 9.3 %copy-start.3 = (s32[4]{0:T(128)S(1)}, s32[4]{0:T(128)}, u32[]{:S(2)}) copy-start(s32[4]{0:T(128)} %param.13) | copy-start | bytes 52
  1.3 2.1 %collective-permute-start = (bf16[512,512]{1,0:T(8,128)(2,1)S(1)}, bf16[512,512]{1,0:T(8,128)(2,1)S(1)}, u32[]{:S(2)}, u32[]{:S(2)}) collective-permute-start(bf16[512,512]{1,0:T(8,128)(2,1)S(1)} %get-tuple-element.98), channel_id=1, source_target_pairs={{0,1},{1,0},{2,3},{3,2},{4,5},{5,4},{6,7},{7,6},{8,9},{9,8},{10,11... | collective-permute-start | bytes 1572872 | tf_op jit(solution)/shard_map/ppermute | solution.py:101
  3.4 22.7 %collective-permute-start.1 = (bf16[512,8192]{1,0:T(8,128)(2,1)}, bf16[512,8192]{1,0:T(8,128)(2,1)}, u32[]{:S(2)}, u32[]{:S(2)}) collective-permute-start(bf16[512,8192]{1,0:T(8,128)(2,1)} %mine_ref.13), channel_id=1, source_target_pairs={{0,1},{1,0},{2,3},{3,2},{4,5},{5,4},{6,7},{7,6},{8,9},{9,8},{10,11... | collective-permute-start | bytes 25165832 | tf_op jit(solution)/shard_map/ppermute | solution.py:126
  3.8 10.0 %collective-permute-start.2 = (bf16[256,512]{1,0:T(8,128)(2,1)S(1)}, bf16[256,512]{1,0:T(8,128)(2,1)}, u32[]{:S(2)}, u32[]{:S(2)}) collective-permute-start(bf16[256,512]{1,0:T(8,128)(2,1)S(1)} %get-tuple-element.102), channel_id=1, source_target_pairs={{0,4},{4,8},{8,12},{12,14},{14,10},{10,6},{6,2},{2,0},{1,5},{5,9},... | collective-permute-start | bytes 786440 | tf_op jit(solution)/shard_map/ppermute | solution.py:139
  6.6 12.5 %collective-permute-start.3 = (bf16[256,512]{1,0:T(8,128)(2,1)S(1)}, bf16[256,512]{1,0:T(8,128)(2,1)}, u32[]{:S(2)}, u32[]{:S(2)}) collective-permute-start(bf16[256,512]{1,0:T(8,128)(2,1)S(1)} %get-tuple-element.101), channel_id=1, source_target_pairs={{0,4},{4,8},{8,12},{12,14},{14,10},{10,6},{6,2},{2,0},{1,5},{5,9},... | collective-permute-start | bytes 786440 | tf_op jit(solution)/shard_map/ppermute | solution.py:139
  8.2 10.9 %collective-permute-start.4 = (bf16[256,512]{1,0:T(8,128)(2,1)S(1)}, bf16[256,512]{1,0:T(8,128)(2,1)}, u32[]{:S(2)}, u32[]{:S(2)}) collective-permute-start(bf16[256,512]{1,0:T(8,128)(2,1)S(1)} %get-tuple-element.100), channel_id=1, source_target_pairs={{4,0},{8,4},{12,8},{14,12},{10,14},{6,10},{2,6},{0,2},{5,1},{9,5},... | collective-permute-start | bytes 786440 | tf_op jit(solution)/shard_map/ppermute | solution.py:139
  8.7 13.3 %collective-permute-start.5 = (bf16[256,512]{1,0:T(8,128)(2,1)S(1)}, bf16[256,512]{1,0:T(8,128)(2,1)}, u32[]{:S(2)}, u32[]{:S(2)}) collective-permute-start(bf16[256,512]{1,0:T(8,128)(2,1)S(1)} %get-tuple-element.99), channel_id=1, source_target_pairs={{4,0},{8,4},{12,8},{14,12},{10,14},{6,10},{2,6},{0,2},{5,1},{9,5},... | collective-permute-start | bytes 786440 | tf_op jit(solution)/shard_map/ppermute | solution.py:139
  22.0 9.8 %collective-permute-start.10 = (bf16[256,512]{1,0:T(8,128)(2,1)}, bf16[256,512]{1,0:T(8,128)(2,1)}, u32[]{:S(2)}, u32[]{:S(2)}) collective-permute-start(bf16[256,512]{1,0:T(8,128)(2,1)} %collective-permute-done.5.refs_5_), channel_id=1, source_target_pairs={{4,0},{8,4},{12,8},{14,12},{10,14},{6,10},{2,6},{0,2},{5,1},{9,5},... | collective-permute-start | bytes 786440 | tf_op jit(solution)/shard_map/ppermute | solution.py:139
  22.4 16.8 %collective-permute-start.6 = (bf16[256,512]{1,0:T(8,128)(2,1)}, bf16[256,512]{1,0:T(8,128)(2,1)}, u32[]{:S(2)}, u32[]{:S(2)}) collective-permute-start(bf16[256,512]{1,0:T(8,128)(2,1)} %collective-permute-done.2.refs_2_), channel_id=1, source_target_pairs={{0,4},{4,8},{8,12},{12,14},{14,10},{10,6},{6,2},{2,0},{1,5},{5,9},... | collective-permute-start | bytes 786440 | tf_op jit(solution)/shard_map/ppermute | solution.py:139
  24.0 13.6 %collective-permute-start.8 = (bf16[256,512]{1,0:T(8,128)(2,1)}, bf16[256,512]{1,0:T(8,128)(2,1)}, u32[]{:S(2)}, u32[]{:S(2)}) collective-permute-start(bf16[256,512]{1,0:T(8,128)(2,1)} %collective-permute-done.3.refs_3_), channel_id=1, source_target_pairs={{0,4},{4,8},{8,12},{12,14},{14,10},{10,6},{6,2},{2,0},{1,5},{5,9},... | collective-permute-start | bytes 786440 | tf_op jit(solution)/shard_map/ppermute | solution.py:139
  25.6 11.6 %collective-permute-start.9 = (bf16[256,512]{1,0:T(8,128)(2,1)}, bf16[256,512]{1,0:T(8,128)(2,1)}, u32[]{:S(2)}, u32[]{:S(2)}) collective-permute-start(bf16[256,512]{1,0:T(8,128)(2,1)} %collective-permute-done.4.refs_4_), channel_id=1, source_target_pairs={{4,0},{8,4},{12,8},{14,12},{10,14},{6,10},{2,6},{0,2},{5,1},{9,5},... | collective-permute-start | bytes 786440 | tf_op jit(solution)/shard_map/ppermute | solution.py:139
  31.8 13.0 %collective-permute-start.14 = (bf16[256,512]{1,0:T(8,128)(2,1)}, bf16[256,512]{1,0:T(8,128)(2,1)S(1)}, u32[]{:S(2)}, u32[]{:S(2)}) collective-permute-start(bf16[256,512]{1,0:T(8,128)(2,1)} %collective-permute-done.10.refs_3_), channel_id=1, source_target_pairs={{4,0},{8,4},{12,8},{14,12},{10,14},{6,10},{2,6},{0,2},{5,1},{9,5},... | collective-permute-start | bytes 786440 | tf_op jit(solution)/shard_map/ppermute | solution.py:139
  37.2 11.1 %collective-permute-start.13 = (bf16[256,512]{1,0:T(8,128)(2,1)}, bf16[256,512]{1,0:T(8,128)(2,1)S(1)}, u32[]{:S(2)}, u32[]{:S(2)}) collective-permute-start(bf16[256,512]{1,0:T(8,128)(2,1)} %collective-permute-done.9.refs_2_), channel_id=1, source_target_pairs={{4,0},{8,4},{12,8},{14,12},{10,14},{6,10},{2,6},{0,2},{5,1},{9,5},... | collective-permute-start | bytes 786440 | tf_op jit(solution)/shard_map/ppermute | solution.py:139
  37.6 11.1 %collective-permute-start.12 = (bf16[256,512]{1,0:T(8,128)(2,1)}, bf16[256,512]{1,0:T(8,128)(2,1)S(1)}, u32[]{:S(2)}, u32[]{:S(2)}) collective-permute-start(bf16[256,512]{1,0:T(8,128)(2,1)} %collective-permute-done.8.refs_1_), channel_id=1, source_target_pairs={{0,4},{4,8},{8,12},{12,14},{14,10},{10,6},{6,2},{2,0},{1,5},{5,9},... | collective-permute-start | bytes 786440 | tf_op jit(solution)/shard_map/ppermute | solution.py:139
  39.2 11.1 %collective-permute-start.7 = (bf16[256,512]{1,0:T(8,128)(2,1)}, bf16[256,512]{1,0:T(8,128)(2,1)S(1)}, u32[]{:S(2)}, u32[]{:S(2)}) collective-permute-start(bf16[256,512]{1,0:T(8,128)(2,1)} %collective-permute-done.6.refs_0_), channel_id=1, source_target_pairs={{0,4},{4,8},{8,12},{12,14},{14,10},{10,6},{6,2},{2,0},{1,5},{5,9},... | collective-permute-start | bytes 786440 | tf_op jit(solution)/shard_map/ppermute | solution.py:139
  44.8 10.5 %collective-permute-start.18 = (bf16[256,512]{1,0:T(8,128)(2,1)S(1)}, bf16[256,512]{1,0:T(8,128)(2,1)}, u32[]{:S(2)}, u32[]{:S(2)}) collective-permute-start(bf16[256,512]{1,0:T(8,128)(2,1)S(1)} %collective-permute-done.14.refs_3_), channel_id=1, source_target_pairs={{4,0},{8,4},{12,8},{14,12},{10,14},{6,10},{2,6},{0,2},{5,1},{9,5},... | collective-permute-start | bytes 786440 | tf_op jit(solution)/shard_map/ppermute | solution.py:139
  48.3 11.6 %collective-permute-start.17 = (bf16[256,512]{1,0:T(8,128)(2,1)S(1)}, bf16[256,512]{1,0:T(8,128)(2,1)}, u32[]{:S(2)}, u32[]{:S(2)}) collective-permute-start(bf16[256,512]{1,0:T(8,128)(2,1)S(1)} %collective-permute-done.13.refs_2_), channel_id=1, source_target_pairs={{4,0},{8,4},{12,8},{14,12},{10,14},{6,10},{2,6},{0,2},{5,1},{9,5},... | collective-permute-start | bytes 786440 | tf_op jit(solution)/shard_map/ppermute | solution.py:139
  48.7 11.6 %collective-permute-start.16 = (bf16[256,512]{1,0:T(8,128)(2,1)S(1)}, bf16[256,512]{1,0:T(8,128)(2,1)}, u32[]{:S(2)}, u32[]{:S(2)}) collective-permute-start(bf16[256,512]{1,0:T(8,128)(2,1)S(1)} %collective-permute-done.12.refs_1_), channel_id=1, source_target_pairs={{0,4},{4,8},{8,12},{12,14},{14,10},{10,6},{6,2},{2,0},{1,5},{5,9},... | collective-permute-start | bytes 786440 | tf_op jit(solution)/shard_map/ppermute | solution.py:139
  50.3 11.6 %collective-permute-start.11 = (bf16[256,512]{1,0:T(8,128)(2,1)S(1)}, bf16[256,512]{1,0:T(8,128)(2,1)}, u32[]{:S(2)}, u32[]{:S(2)}) collective-permute-start(bf16[256,512]{1,0:T(8,128)(2,1)S(1)} %collective-permute-done.7.refs_0_), channel_id=1, source_target_pairs={{0,4},{4,8},{8,12},{12,14},{14,10},{10,6},{6,2},{2,0},{1,5},{5,9},... | collective-permute-start | bytes 786440 | tf_op jit(solution)/shard_map/ppermute | solution.py:139
  55.3 12.1 %collective-permute-start.22 = (bf16[256,512]{1,0:T(8,128)(2,1)}, bf16[256,512]{1,0:T(8,128)(2,1)S(1)}, u32[]{:S(2)}, u32[]{:S(2)}) collective-permute-start(bf16[256,512]{1,0:T(8,128)(2,1)} %collective-permute-done.18.refs_3_), channel_id=1, source_target_pairs={{4,0},{8,4},{12,8},{14,12},{10,14},{6,10},{2,6},{0,2},{5,1},{9,5},... | collective-permute-start | bytes 786440 | tf_op jit(solution)/shard_map/ppermute | solution.py:139
  59.8 11.1 %collective-permute-start.21 = (bf16[256,512]{1,0:T(8,128)(2,1)}, bf16[256,512]{1,0:T(8,128)(2,1)S(1)}, u32[]{:S(2)}, u32[]{:S(2)}) collective-permute-start(bf16[256,512]{1,0:T(8,128)(2,1)} %collective-permute-done.17.refs_2_), channel_id=1, source_target_pairs={{4,0},{8,4},{12,8},{14,12},{10,14},{6,10},{2,6},{0,2},{5,1},{9,5},... | collective-permute-start | bytes 786440 | tf_op jit(solution)/shard_map/ppermute | solution.py:139
  60.3 11.1 %collective-permute-start.20 = (bf16[256,512]{1,0:T(8,128)(2,1)}, bf16[256,512]{1,0:T(8,128)(2,1)S(1)}, u32[]{:S(2)}, u32[]{:S(2)}) collective-permute-start(bf16[256,512]{1,0:T(8,128)(2,1)} %collective-permute-done.16.refs_1_), channel_id=1, source_target_pairs={{0,4},{4,8},{8,12},{12,14},{14,10},{10,6},{6,2},{2,0},{1,5},{5,9},... | collective-permute-start | bytes 786440 | tf_op jit(solution)/shard_map/ppermute | solution.py:139
  61.9 11.1 %collective-permute-start.15 = (bf16[256,512]{1,0:T(8,128)(2,1)}, bf16[256,512]{1,0:T(8,128)(2,1)S(1)}, u32[]{:S(2)}, u32[]{:S(2)}) collective-permute-start(bf16[256,512]{1,0:T(8,128)(2,1)} %collective-permute-done.11.refs_0_), channel_id=1, source_target_pairs={{0,4},{4,8},{8,12},{12,14},{14,10},{10,6},{6,2},{2,0},{1,5},{5,9},... | collective-permute-start | bytes 786440 | tf_op jit(solution)/shard_map/ppermute | solution.py:139
  67.4 10.7 %collective-permute-start.28 = (bf16[256,512]{1,0:T(8,128)(2,1)S(1)}, bf16[256,512]{1,0:T(8,128)(2,1)}, u32[]{:S(2)}, u32[]{:S(2)}) collective-permute-start(bf16[256,512]{1,0:T(8,128)(2,1)S(1)} %collective-permute-done.22.refs_3_), channel_id=1, source_target_pairs={{4,0},{8,4},{12,8},{14,12},{10,14},{6,10},{2,6},{0,2},{5,1},{9,5},... | collective-permute-start | bytes 786440 | tf_op jit(solution)/shard_map/ppermute | solution.py:139
  71.0 11.4 %collective-permute-start.26 = (bf16[256,512]{1,0:T(8,128)(2,1)S(1)}, bf16[256,512]{1,0:T(8,128)(2,1)}, u32[]{:S(2)}, u32[]{:S(2)}) collective-permute-start(bf16[256,512]{1,0:T(8,128)(2,1)S(1)} %collective-permute-done.21.refs_2_), channel_id=1, source_target_pairs={{4,0},{8,4},{12,8},{14,12},{10,14},{6,10},{2,6},{0,2},{5,1},{9,5},... | collective-permute-start | bytes 786440 | tf_op jit(solution)/shard_map/ppermute | solution.py:139
  71.4 11.5 %collective-permute-start.24 = (bf16[256,512]{1,0:T(8,128)(2,1)S(1)}, bf16[256,512]{1,0:T(8,128)(2,1)}, u32[]{:S(2)}, u32[]{:S(2)}) collective-permute-start(bf16[256,512]{1,0:T(8,128)(2,1)S(1)} %collective-permute-done.20.refs_1_), channel_id=1, source_target_pairs={{0,4},{4,8},{8,12},{12,14},{14,10},{10,6},{6,2},{2,0},{1,5},{5,9},... | collective-permute-start | bytes 786440 | tf_op jit(solution)/shard_map/ppermute | solution.py:139
  73.0 11.4 %collective-permute-start.19 = (bf16[256,512]{1,0:T(8,128)(2,1)S(1)}, bf16[256,512]{1,0:T(8,128)(2,1)}, u32[]{:S(2)}, u32[]{:S(2)}) collective-permute-start(bf16[256,512]{1,0:T(8,128)(2,1)S(1)} %collective-permute-done.15.refs_0_), channel_id=1, source_target_pairs={{0,4},{4,8},{8,12},{12,14},{14,10},{10,6},{6,2},{2,0},{1,5},{5,9},... | collective-permute-start | bytes 786440 | tf_op jit(solution)/shard_map/ppermute | solution.py:139
  78.1 13.4 %collective-permute-start.29 = (bf16[256,512]{1,0:T(8,128)(2,1)}, bf16[256,512]{1,0:T(8,128)(2,1)S(1)}, u32[]{:S(2)}, u32[]{:S(2)}) collective-permute-start(bf16[256,512]{1,0:T(8,128)(2,1)} %collective-permute-done.28.refs_3_), channel_id=1, source_target_pairs={{4,0},{8,4},{12,8},{14,12},{10,14},{6,10},{2,6},{0,2},{5,1},{9,5},... | collective-permute-start | bytes 786440 | tf_op jit(solution)/shard_map/ppermute | solution.py:139
  82.4 9.2 %collective-permute-start.27 = (bf16[256,512]{1,0:T(8,128)(2,1)}, bf16[256,512]{1,0:T(8,128)(2,1)S(1)}, u32[]{:S(2)}, u32[]{:S(2)}) collective-permute-start(bf16[256,512]{1,0:T(8,128)(2,1)} %collective-permute-done.26.refs_2_), channel_id=1, source_target_pairs={{4,0},{8,4},{12,8},{14,12},{10,14},{6,10},{2,6},{0,2},{5,1},{9,5},... | collective-permute-start | bytes 786440 | tf_op jit(solution)/shard_map/ppermute | solution.py:139
  82.9 8.7 %collective-permute-start.25 = (bf16[256,512]{1,0:T(8,128)(2,1)}, bf16[256,512]{1,0:T(8,128)(2,1)S(1)}, u32[]{:S(2)}, u32[]{:S(2)}) collective-permute-start(bf16[256,512]{1,0:T(8,128)(2,1)} %collective-permute-done.24.refs_1_), channel_id=1, source_target_pairs={{0,4},{4,8},{8,12},{12,14},{14,10},{10,6},{6,2},{2,0},{1,5},{5,9},... | collective-permute-start | bytes 786440 | tf_op jit(solution)/shard_map/ppermute | solution.py:139
  84.4 7.9 %collective-permute-start.23 = (bf16[256,512]{1,0:T(8,128)(2,1)}, bf16[256,512]{1,0:T(8,128)(2,1)S(1)}, u32[]{:S(2)}, u32[]{:S(2)}) collective-permute-start(bf16[256,512]{1,0:T(8,128)(2,1)} %collective-permute-done.19.refs_0_), channel_id=1, source_target_pairs={{0,4},{4,8},{8,12},{12,14},{14,10},{10,6},{6,2},{2,0},{1,5},{5,9},... | collective-permute-start | bytes 786440 | tf_op jit(solution)/shard_map/ppermute | solution.py:139
  96.5 3.9 %copy-start.1 = (bf16[4,4,4,8,128]{4,3,2,1,0:T(8,128)(2,1)S(1)}, bf16[4,4,4,8,128]{4,3,2,1,0:T(8,128)(2,1)}, u32[]{:S(2)}) copy-start(bf16[4,4,4,8,128]{4,3,2,1,0:T(8,128)(2,1)} %reshape.77) | copy-start | bytes 393220
  96.5 3.9 %copy-start.2 = (pred[4,4]{1,0:T(4,128)(4,1)S(1)}, pred[4,4]{1,0:T(4,128)(4,1)}, u32[]{:S(2)}) copy-start(pred[4,4]{1,0:T(4,128)(4,1)} %iota_compare_fusion.1) | copy-start | bytes 52
  96.5 4.9 %collective-permute-start.30 = (bf16[1024,512]{1,0:T(8,128)(2,1)}, bf16[1024,512]{1,0:T(8,128)(2,1)S(1)}, u32[]{:S(2)}, u32[]{:S(2)}) collective-permute-start(bf16[1024,512]{1,0:T(8,128)(2,1)} %get-tuple-element.88.have_any), channel_id=1, source_target_pairs={{0,1},{1,0},{2,3},{3,2},{4,5},{5,4},{6,7},{7,6},{8,9},{9,8},{10,11... | collective-permute-start | bytes 3145736 | tf_op jit(solution)/shard_map/ppermute | solution.py:328
  108.6 6.3 %collective-permute-start.31 = (f32[4,9,8,128]{3,2,1,0:T(8,128)S(1)}, f32[4,9,8,128]{3,2,1,0:T(8,128)S(1)}, u32[]{:S(2)}, u32[]{:S(2)}) collective-permute-start(f32[4,9,8,128]{3,2,1,0:T(8,128)S(1)} %get-tuple-element.91), channel_id=1, source_target_pairs={{0,2},{2,0},{4,6},{6,4},{8,10},{10,8},{12,14},{14,12},{1,3},{3,1},... | collective-permute-start | bytes 442376 | tf_op jit(solution)/shard_map/ppermute | solution.py:361
  115.1 4.5 %collective-permute-start.32 = (f32[9,8,128]{2,1,0:T(8,128)S(1)}, f32[9,8,128]{2,1,0:T(8,128)S(1)}, u32[]{:S(2)}, u32[]{:S(2)}) collective-permute-start(f32[9,8,128]{2,1,0:T(8,128)S(1)} %get-tuple-element.93), channel_id=1, source_target_pairs={{0,4},{2,6},{4,0},{6,2},{8,12},{10,14},{12,8},{14,10},{1,5},{3,7},... | collective-permute-start | bytes 110600 | tf_op jit(solution)/shard_map/ppermute | solution.py:362
  116.7 5.4 %collective-permute-start.33 = (f32[9,8,128]{2,1,0:T(8,128)S(1)}, f32[9,8,128]{2,1,0:T(8,128)S(1)}, u32[]{:S(2)}, u32[]{:S(2)}) collective-permute-start(f32[9,8,128]{2,1,0:T(8,128)S(1)} %get-tuple-element.94), channel_id=1, source_target_pairs={{0,8},{2,10},{4,12},{6,14},{8,0},{10,2},{12,4},{14,6},{1,9},{3,11}... | collective-permute-start | bytes 110600 | tf_op jit(solution)/shard_map/ppermute | solution.py:362
  119.2 5.8 %collective-permute-start.34 = (f32[9,8,128]{2,1,0:T(8,128)S(1)}, f32[9,8,128]{2,1,0:T(8,128)S(1)}, u32[]{:S(2)}, u32[]{:S(2)}) collective-permute-start(f32[9,8,128]{2,1,0:T(8,128)S(1)} %get-tuple-element.95), channel_id=1, source_target_pairs={{0,12},{2,14},{4,8},{6,10},{8,4},{10,6},{12,0},{14,2},{1,13},{3,15... | collective-permute-start | bytes 110600 | tf_op jit(solution)/shard_map/ppermute | solution.py:362
  125.1 3.8 %collective-permute-start.35 = (bf16[64,128]{1,0:T(8,128)(2,1)S(1)}, bf16[64,128]{1,0:T(8,128)(2,1)S(1)}, u32[]{:S(2)}, u32[]{:S(2)}) collective-permute-start(bf16[64,128]{1,0:T(8,128)(2,1)S(1)} %shard_map.91), channel_id=1, source_target_pairs={{0,2},{2,0},{4,6},{6,4},{8,10},{10,8},{12,14},{14,12},{1,3},{3,1},... | collective-permute-start | bytes 49160 | tf_op jit(solution)/shard_map/ppermute | solution.py:370
  128.9 5.8 %collective-permute-start.36 = (bf16[128,128]{1,0:T(8,128)(2,1)S(1)}, bf16[128,128]{1,0:T(8,128)(2,1)S(1)}, u32[]{:S(2)}, u32[]{:S(2)}) collective-permute-start(bf16[128,128]{1,0:T(8,128)(2,1)S(1)} %pad_maximum_fusion.2), channel_id=1, source_target_pairs={{0,12},{2,14},{4,8},{6,10},{8,4},{10,6},{12,0},{14,2},{1,13},{3,15... | collective-permute-start | bytes 98312 | tf_op jit(solution)/shard_map/ppermute | solution.py:373
  129.5 5.3 %collective-permute-start.37 = (bf16[128,128]{1,0:T(8,128)(2,1)S(1)}, bf16[128,128]{1,0:T(8,128)(2,1)S(1)}, u32[]{:S(2)}, u32[]{:S(2)}) collective-permute-start(bf16[128,128]{1,0:T(8,128)(2,1)S(1)} %pad_maximum_fusion.2), channel_id=1, source_target_pairs={{0,8},{2,10},{4,12},{6,14},{8,0},{10,2},{12,4},{14,6},{1,9},{3,11}... | collective-permute-start | bytes 98312 | tf_op jit(solution)/shard_map/ppermute | solution.py:373
  129.6 5.7 %collective-permute-start.38 = (bf16[128,128]{1,0:T(8,128)(2,1)S(1)}, bf16[128,128]{1,0:T(8,128)(2,1)S(1)}, u32[]{:S(2)}, u32[]{:S(2)}) collective-permute-start(bf16[128,128]{1,0:T(8,128)(2,1)S(1)} %pad_maximum_fusion.2), channel_id=1, source_target_pairs={{0,4},{2,6},{4,0},{6,2},{8,12},{10,14},{12,8},{14,10},{1,5},{3,7},... | collective-permute-start | bytes 98312 | tf_op jit(solution)/shard_map/ppermute | solution.py:373
  135.4 1.4 %collective-permute-start.39 = (bf16[16,1,4096]{2,0,1:T(8,128)(2,1)S(1)}, bf16[16,1,4096]{2,0,1:T(8,128)(2,1)S(1)}, u32[]{:S(2)}, u32[]{:S(2)}) collective-permute-start(bf16[16,1,4096]{2,0,1:T(8,128)(2,1)S(1)} %reshape.89), channel_id=1, source_target_pairs={{0,1},{1,0},{2,3},{3,2},{4,5},{5,4},{6,7},{7,6},{8,9},{9,8},{10,11... | collective-permute-start | bytes 393224 | tf_op jit(solution)/shard_map/ppermute | solution.py:383

commit v13 on v8

--- a/solution.py
+++ b/solution.py
@@ -31,7 +31,7 @@
 
     def kernel(places_ref, mine_ref, theirs_ref, *refs):
         parts = refs[:count]
-        total_ref, out_ref, mark_ref, columns, weights, sems = (
+        total_ref, out_ref, mark_ref, columns, weights, sems, loaded = (
             refs[count:] if total is not None else (None,) + refs[count:]
         )
         copies = []
@@ -44,10 +44,15 @@
                 copy.start()
                 copies.append(copy)
         at = 0
-        for part in parts:
-            weights[at : at + part.shape[0], :] = part[...]
+        loads = []
+        for k, part in enumerate(parts):
+            load = pltpu.make_async_copy(part, weights.at[pl.ds(at, part.shape[0])], loaded.at[k])
+            load.start()
+            loads.append(load)
             at += part.shape[0]
         mark_ref[...] = jnp.zeros_like(mark_ref)
+        for load in loads:
+            load.wait()
         for j in range(2):
             for g in range(len(groups)):
                 copies[j * len(groups) + g].wait()
@@ -69,15 +74,16 @@
             jax.ShapeDtypeStruct((2 * tok_rows, width), BF if last else F32),
             jax.ShapeDtypeStruct((8, 128), F32),
         ),
-        in_specs=[pl.BlockSpec(memory_space=pltpu.SMEM), in_any, in_any] + [in_vmem] * (count + len(sums)),
+        in_specs=[pl.BlockSpec(memory_space=pltpu.SMEM)] + [in_any] * (2 + count) + [in_vmem] * len(sums),
         out_specs=(in_vmem, in_vmem),
         scratch_shapes=[
             pltpu.VMEM((2, tok_rows, deep), BF),
             pltpu.VMEM((deep, width), BF),
             pltpu.SemaphoreType.DMA((2, len(groups))),
+            pltpu.SemaphoreType.DMA((count,)),
         ],
         input_output_aliases={} if total is None or last else {3 + count: 0},
-        compiler_params=pltpu.CompilerParams(vmem_limit_bytes=30 * 2**20),
+        compiler_params=pltpu.CompilerParams(vmem_limit_bytes=20 * 2**20),
         cost_estimate=pl.CostEstimate(
             flops=4 * tok_rows * deep * width, bytes_accessed=4 * tok_rows * deep, transcendentals=0
         ),
@@ -125,8 +131,11 @@
         ready = todo
         if step == 2:
             held = lax.optimization_barrier(held)
-        if step == last:
+        if step == 3:
             _, inputs = lax.optimization_barrier((held[0], inputs))
+            early = prepare(*inputs)
+        if step == 5:
+            held[0], early = lax.optimization_barrier((held[0], early))
         for k in range(2 * chains):
             if mark is not None:
                 held[k], _ = lax.optimization_barrier((held[k], mark))
@@ -137,7 +146,7 @@
         else:
             total, mark = add_pieces(tokens, theirs, ready, total)
             todo = arriving
-    return add_pieces(tokens, theirs, todo, total, core)[0], prepare(*inputs)
+    return add_pieces(tokens, theirs, todo, total, core)[0], early
 
 
 def attend(have, got, core, key_up, value_up, query, bounds, chips):
@@ -150,9 +159,8 @@
     def kernel(core_ref, have_ref, got_ref, key_up_ref, value_up_ref, query_ref, bounds_ref, out_ref):
         first = core_ref[0] == 0
         have, got = have_ref[...], got_ref[...]
-        lanes = pl.ds(pl.multiple_of(core_ref[0] * heads * DH, heads * DH), heads * DH)
-        keys = mm(jnp.where(first, have, got), key_up_ref[:, lanes]).astype(BF)
-        values = mm(jnp.where(first, got, have), value_up_ref[:, lanes]).astype(BF)
+        keys = mm(jnp.where(first, have, got), key_up_ref[...]).astype(BF)
+        values = mm(jnp.where(first, got, have), value_up_ref[...]).astype(BF)
         position = lax.broadcasted_iota(jnp.int32, (tokens, rows), 0)
         visible = (position >= bounds_ref[0:1, :]) & (position < bounds_ref[1:2, :])
         tops, totals = [], []
@@ -188,7 +196,7 @@
         out_shape=jax.ShapeDtypeStruct((chips, blocks + 1, 8, DH), F32),
         in_specs=[pl.BlockSpec(memory_space=pltpu.SMEM)] + [in_vmem] * 6,
         out_specs=in_vmem,
-        compiler_params=pltpu.CompilerParams(vmem_limit_bytes=24 * 2**20),
+        compiler_params=pltpu.CompilerParams(vmem_limit_bytes=16 * 2**20),
         cost_estimate=pl.CostEstimate(
             flops=4 * tokens * (have.shape[1] * heads * DH + heads * rows * DH),
             bytes_accessed=4 * tokens * have.shape[1],
@@ -220,6 +228,7 @@
         out_shape=jax.ShapeDtypeStruct((blocks * 8, DH), BF),
         in_specs=[in_vmem] * 3,
         out_specs=in_vmem,
+        compiler_params=pltpu.CompilerParams(vmem_limit_bytes=8 * 2**20),
         cost_estimate=pl.CostEstimate(
             flops=2 * chips * blocks * 8 * DH, bytes_accessed=4 * arrived.size, transcendentals=chips * blocks * 8
         ),
@@ -241,11 +250,14 @@
     rows = pairs * heads * group
     share = rows // chips
 
-    def by_head(queries):
+    def my_heads(queries, key_up, value_up):
         mine = lax.dynamic_slice_in_dim(queries, core * heads * group * DH, heads * group * DH, 2)
-        return mine.reshape(steps_count, req_count, heads, group, DH).transpose(2, 0, 1, 3, 4)
-
-    have, query = project(tokens, key_down, value_down, by_head, (queries,))
+        mine = mine.reshape(steps_count, req_count, heads, group, DH).transpose(2, 0, 1, 3, 4)
+        ups = [lax.dynamic_slice_in_dim(x, core * heads * DH, heads * DH, 1) for x in (key_up, value_up)]
+        return mine, *ups
+
+    have, early = project(tokens, key_down, value_down, my_heads, (queries, key_up, value_up))
+    query, key_up, value_up = early
     got = lax.ppermute(have, "core", SWAP)
 
     offsets = jnp.cumsum(prompt_lens) - prompt_lens
@@ -253,15 +265,10 @@
     bounds = jnp.broadcast_to(bounds[:, None, :, None], (2, steps_count, req_count, group)).reshape(2, -1)
     sending = attend(have, got, core, key_up, value_up, query.reshape(heads, -1, DH), bounds, chips)
 
-    sending, query, new_latent = lax.optimization_barrier((sending, query, new_latent))
+    _, new_latent = lax.optimization_barrier((have, new_latent))
     flat_new = new_latent.reshape(pairs, 2 * lat_width)
-
-    def my_heads(latent, up):
-        full = lax.dynamic_slice_in_dim(mm(latent, up), core * heads * DH, heads * DH, 1)
-        return full.astype(BF).reshape(steps_count, req_count, heads, DH)
-
-    new_keys = my_heads(flat_new[:, :lat_width], key_up)
-    new_values = my_heads(flat_new[:, lat_width:], value_up)
+    new_keys = mm(flat_new[:, :lat_width], key_up).astype(BF).reshape(steps_count, req_count, heads, DH)
+    new_values = mm(flat_new[:, lat_width:], value_up).astype(BF).reshape(steps_count, req_count, heads, DH)
     causal = (jnp.arange(steps_count)[:, None] >= jnp.arange(steps_count)[None, :])[:, None, None, None, :]
     fresh = jnp.einsum("gsrjd,urgd->srgju", query, new_keys, preferred_element_type=F32) * scale
     fresh = jnp.where(causal, fresh, -1e30)

time: 144 us -> 134 us (0.931)
  local copies, waits for them, and re-layouts: 10.5 us -> 4.47 us
    unnamed x26 -> x4, local copies, waits for them, and re-layouts: 7.49 us -> 0.01 us
    pallas_call x1, Pallas kernels: 1.93 us -> 0.36 us  [merge(): pl.pallas_call(kernel, out_shape=jax.ShapeDtypeStruct((blocks * 8, DH), B...]
    ppermute x1, waiting for transfers between devices: 2.19 us -> 0.7 us  [on_device(): got = lax.ppermute(have, 'core', SWAP)]
  transfers between devices with their start and end apart: 37 -> 37, of which waited for: 19 -> 18; matrix products, arithmetic and copies ran while one was open for 3% -> 4% of each run, Pallas kernels for 17% -> 19%
where the time goes in v13:
time: 134 us
  waiting for transfers between devices  50.1 us (37%)
  starting transfers between devices  40 us (30%)
  Pallas kernels  35 us (26%)
  local copies, waits for them, and re-layouts  4.47 us (3%)
  other arithmetic  2.42 us (2%)
  matrix products  1.35 us (1%)
    ppermute x28, waiting for transfers between devices, project(): held[k] = lax.ppermute(held[k], 'chip', ways[k])  33.3 us
    pallas_call x7, Pallas kernels, add_pieces(): pl.pallas_call(kernel, out_shape=(jax.ShapeDtypeStruct((2 * tok_rows, wid...  30 us
    ppermute x28, starting transfers between devices, project(): held[k] = lax.ppermute(held[k], 'chip', ways[k])  29.3 us
    all_to_all x1, waiting for transfers between devices, on_device(): lax.all_to_all(flat, 'chip', split_axis=0, concat_axis=0, tiled=True)  8.6 us
    pallas_call x1, Pallas kernels, attend(): pl.pallas_call(kernel, out_shape=jax.ShapeDtypeStruct((chips, blocks + 1,...  4.67 us
    ppermute x3, starting transfers between devices, on_device(): lax.ppermute(couple, 'chip', [(c, c ^ 2 * d) for c in range(chips)])  4.45 us
    all_to_all x1, starting transfers between devices, on_device(): lax.all_to_all(flat, 'chip', split_axis=0, concat_axis=0, tiled=True)  3.7 us
  transfers between devices with their start and end apart: 37, of which 18 were waited for; matrix products, arithmetic and copies ran while one was open for 4% of the time, Pallas kernels for 19%

profile of v13, /device:TPU:0, one launch (start us, length us, event | category | flops | bytes accessed | tf_op | source)
XLA Modules:
  0.0 133.6 jit_solution(12795318855141622912)
XLA Ops:
  0.0 1.3 broadcast_select_fusion
  1.3 0.5 collective-permute-start
  1.8 1.5 %collective-permute-done.refs_1_ = bf16[512,512]{1,0:T(8,128)(2,1)S(1)} collective-permute-done((bf16[512,512]{1,0:T(8,128)(2,1)S(1)}, bf16[512,512]{1,0:T(8,128)(2,1)S(1)}, u32[]{:S(2)}, u32[]{:S(2)}) %collective-permute-start) | collective-permute-done | bytes 524320 | tf_op jit(solution)/shard_map/ppermute | solution.py:101
  3.4 0.4 collective-permute-start.1
  3.8 2.8 %collective-permute-start.2 = (bf16[256,512]{1,0:T(8,128)(2,1)S(1)}, bf16[256,512]{1,0:T(8,128)(2,1)}, u32[]{:S(2)}, u32[]{:S(2)}) collective-permute-start(bf16[256,512]{1,0:T(8,128)(2,1)S(1)} %get-tuple-element.102), channel_id=1, source_target_pairs={{0,4},{4,8},{8,12},{12,14},{14,10},{10,6},{6,2},{2,0},{1,5},{5,9},... | collective-permute-start | bytes 786440 | tf_op jit(solution)/shard_map/ppermute | solution.py:142
  6.6 1.6 %collective-permute-start.3 = (bf16[256,512]{1,0:T(8,128)(2,1)S(1)}, bf16[256,512]{1,0:T(8,128)(2,1)}, u32[]{:S(2)}, u32[]{:S(2)}) collective-permute-start(bf16[256,512]{1,0:T(8,128)(2,1)S(1)} %get-tuple-element.101), channel_id=1, source_target_pairs={{0,4},{4,8},{8,12},{12,14},{14,10},{10,6},{6,2},{2,0},{1,5},{5,9},... | collective-permute-start | bytes 786440 | tf_op jit(solution)/shard_map/ppermute | solution.py:142
  8.2 0.5 collective-permute-start.4
  8.7 5.0 %collective-permute-done.2.refs_2_ = bf16[256,512]{1,0:T(8,128)(2,1)} collective-permute-done((bf16[256,512]{1,0:T(8,128)(2,1)S(1)}, bf16[256,512]{1,0:T(8,128)(2,1)}, u32[]{:S(2)}, u32[]{:S(2)}) %collective-permute-start.2) | collective-permute-done | bytes 262176 | tf_op jit(solution)/shard_map/ppermute | solution.py:142
  13.8 5.3 %collective-permute-done.3.refs_3_ = bf16[256,512]{1,0:T(8,128)(2,1)} collective-permute-done((bf16[256,512]{1,0:T(8,128)(2,1)S(1)}, bf16[256,512]{1,0:T(8,128)(2,1)}, u32[]{:S(2)}, u32[]{:S(2)}) %collective-permute-start.3) | collective-permute-done | bytes 262176 | tf_op jit(solution)/shard_map/ppermute | solution.py:142
  19.1 2.9 %collective-permute-done.5.refs_5_ = bf16[256,512]{1,0:T(8,128)(2,1)} collective-permute-done((bf16[256,512]{1,0:T(8,128)(2,1)S(1)}, bf16[256,512]{1,0:T(8,128)(2,1)}, u32[]{:S(2)}, u32[]{:S(2)}) %collective-permute-start.5) | collective-permute-done | bytes 262176 | tf_op jit(solution)/shard_map/ppermute | solution.py:142
  22.0 0.4 collective-permute-start.10
  22.4 1.6 %collective-permute-start.6 = (bf16[256,512]{1,0:T(8,128)(2,1)}, bf16[256,512]{1,0:T(8,128)(2,1)}, u32[]{:S(2)}, u32[]{:S(2)}) collective-permute-start(bf16[256,512]{1,0:T(8,128)(2,1)} %collective-permute-done.2.refs_2_), channel_id=1, source_target_pairs={{0,4},{4,8},{8,12},{12,14},{14,10},{10,6},{6,2},{2,0},{1,5},{5,9},... | collective-permute-start | bytes 786440 | tf_op jit(solution)/shard_map/ppermute | solution.py:142
  24.0 1.6 %collective-permute-start.8 = (bf16[256,512]{1,0:T(8,128)(2,1)}, bf16[256,512]{1,0:T(8,128)(2,1)}, u32[]{:S(2)}, u32[]{:S(2)}) collective-permute-start(bf16[256,512]{1,0:T(8,128)(2,1)} %collective-permute-done.3.refs_3_), channel_id=1, source_target_pairs={{0,4},{4,8},{8,12},{12,14},{14,10},{10,6},{6,2},{2,0},{1,5},{5,9},... | collective-permute-start | bytes 786440 | tf_op jit(solution)/shard_map/ppermute | solution.py:142
  25.6 0.4 collective-permute-start.9
  26.1 5.7 %shard_map.82 = (f32[1024,512]{1,0:T(8,128)S(1)}, f32[8,128]{1,0:T(8,128)}) custom-call(s32[4]{0:T(128)S(1)} %pad_add_fusion.1.places_ref, bf16[512,8192]{1,0:T(8,128)(2,1)} %mine_ref.13, bf16[512,8192]{1,0:T(8,128)(2,1)} %collective-permute-done.1.theirs_ref, bf16[512,512]{1,0:T(8,128)(2,1)S(1)} %get-tuple-element.97.refs_0_, ...), custom_call_target="tpu_custom_call" | custom-call | flops 2147483648 | bytes 4194304 | tf_op jit(solution)/shard_map/pallas_call | solution.py:71
  31.8 0.5 collective-permute-start.14
  32.3 4.8 %collective-permute-done.9.refs_2_ = bf16[256,512]{1,0:T(8,128)(2,1)} collective-permute-done((bf16[256,512]{1,0:T(8,128)(2,1)}, bf16[256,512]{1,0:T(8,128)(2,1)}, u32[]{:S(2)}, u32[]{:S(2)}) %collective-permute-start.9) | collective-permute-done | bytes 262176 | tf_op jit(solution)/shard_map/ppermute | solution.py:142
  37.1 0.4 collective-permute-start.13
  37.6 1.6 %collective-permute-start.12 = (bf16[256,512]{1,0:T(8,128)(2,1)}, bf16[256,512]{1,0:T(8,128)(2,1)}, u32[]{:S(2)}, u32[]{:S(2)}) collective-permute-start(bf16[256,512]{1,0:T(8,128)(2,1)} %collective-permute-done.8.refs_1_), channel_id=1, source_target_pairs={{0,4},{4,8},{8,12},{12,14},{14,10},{10,6},{6,2},{2,0},{1,5},{5,9},... | collective-permute-start | bytes 786440 | tf_op jit(solution)/shard_map/ppermute | solution.py:142
  39.2 1.6 %collective-permute-start.7 = (bf16[256,512]{1,0:T(8,128)(2,1)}, bf16[256,512]{1,0:T(8,128)(2,1)}, u32[]{:S(2)}, u32[]{:S(2)}) collective-permute-start(bf16[256,512]{1,0:T(8,128)(2,1)} %collective-permute-done.6.refs_0_), channel_id=1, source_target_pairs={{0,4},{4,8},{8,12},{12,14},{14,10},{10,6},{6,2},{2,0},{1,5},{5,9},... | collective-permute-start | bytes 786440 | tf_op jit(solution)/shard_map/ppermute | solution.py:142
  40.9 3.9 %shard_map.83 = (f32[1024,512]{1,0:T(8,128)S(1)}, f32[8,128]{1,0:T(8,128)}) custom-call(s32[2]{0:T(128)S(1)} %pad_add_fusion.2.places_ref, bf16[512,8192]{1,0:T(8,128)(2,1)} %mine_ref.13, bf16[512,8192]{1,0:T(8,128)(2,1)} %collective-permute-done.1.theirs_ref, bf16[256,512]{1,0:T(8,128)(2,1)} %collective-permute-done.6.refs_0_, ...), custom_call_target="tpu_custom_call", output_to_operand_aliasing={{0}: (7, {})} | custom-call | flops 1073741824 | bytes 2097152 | tf_op jit(solution)/shard_map/pallas_call | solution.py:71
  44.8 0.5 collective-permute-start.18
  45.3 3.1 %collective-permute-done.13.refs_2_ = bf16[256,512]{1,0:T(8,128)(2,1)} collective-permute-done((bf16[256,512]{1,0:T(8,128)(2,1)}, bf16[256,512]{1,0:T(8,128)(2,1)}, u32[]{:S(2)}, u32[]{:S(2)}) %collective-permute-start.13) | collective-permute-done | bytes 262176 | tf_op jit(solution)/shard_map/ppermute | solution.py:142
  48.4 0.4 collective-permute-start.17
  48.8 1.6 %collective-permute-start.16 = (bf16[256,512]{1,0:T(8,128)(2,1)}, bf16[256,512]{1,0:T(8,128)(2,1)}, u32[]{:S(2)}, u32[]{:S(2)}) collective-permute-start(bf16[256,512]{1,0:T(8,128)(2,1)} %collective-permute-done.12.refs_1_), channel_id=1, source_target_pairs={{0,4},{4,8},{8,12},{12,14},{14,10},{10,6},{6,2},{2,0},{1,5},{5,9},... | collective-permute-start | bytes 786440 | tf_op jit(solution)/shard_map/ppermute | solution.py:142
  50.4 1.6 %collective-permute-start.11 = (bf16[256,512]{1,0:T(8,128)(2,1)}, bf16[256,512]{1,0:T(8,128)(2,1)}, u32[]{:S(2)}, u32[]{:S(2)}) collective-permute-start(bf16[256,512]{1,0:T(8,128)(2,1)} %collective-permute-done.7.refs_0_), channel_id=1, source_target_pairs={{0,4},{4,8},{8,12},{12,14},{14,10},{10,6},{6,2},{2,0},{1,5},{5,9},... | collective-permute-start | bytes 786440 | tf_op jit(solution)/shard_map/ppermute | solution.py:142
  52.2 1.3 constant_dynamic-slice_fusion.1
  53.5 3.9 %shard_map.84 = (f32[1024,512]{1,0:T(8,128)S(1)}, f32[8,128]{1,0:T(8,128)}) custom-call(s32[2]{0:T(128)S(1)} %pad_add_fusion.3.places_ref, bf16[512,8192]{1,0:T(8,128)(2,1)} %mine_ref.13, bf16[512,8192]{1,0:T(8,128)(2,1)} %collective-permute-done.1.theirs_ref, bf16[256,512]{1,0:T(8,128)(2,1)} %collective-permute-done.7.refs_0_, ...), custom_call_target="tpu_custom_call", output_to_operand_aliasing={{0}: (7, {})} | custom-call | flops 1073741824 | bytes 2097152 | tf_op jit(solution)/shard_map/pallas_call | solution.py:71
  57.4 0.5 collective-permute-start.22
  57.9 1.6 %collective-permute-done.17.refs_2_ = bf16[256,512]{1,0:T(8,128)(2,1)} collective-permute-done((bf16[256,512]{1,0:T(8,128)(2,1)}, bf16[256,512]{1,0:T(8,128)(2,1)}, u32[]{:S(2)}, u32[]{:S(2)}) %collective-permute-start.17) | collective-permute-done | bytes 262176 | tf_op jit(solution)/shard_map/ppermute | solution.py:142
  59.5 0.4 collective-permute-start.21
  60.0 1.6 %collective-permute-start.20 = (bf16[256,512]{1,0:T(8,128)(2,1)}, bf16[256,512]{1,0:T(8,128)(2,1)}, u32[]{:S(2)}, u32[]{:S(2)}) collective-permute-start(bf16[256,512]{1,0:T(8,128)(2,1)} %collective-permute-done.16.refs_1_), channel_id=1, source_target_pairs={{0,4},{4,8},{8,12},{12,14},{14,10},{10,6},{6,2},{2,0},{1,5},{5,9},... | collective-permute-start | bytes 786440 | tf_op jit(solution)/shard_map/ppermute | solution.py:142
  61.6 1.6 %collective-permute-start.15 = (bf16[256,512]{1,0:T(8,128)(2,1)}, bf16[256,512]{1,0:T(8,128)(2,1)}, u32[]{:S(2)}, u32[]{:S(2)}) collective-permute-start(bf16[256,512]{1,0:T(8,128)(2,1)} %collective-permute-done.11.refs_0_), channel_id=1, source_target_pairs={{0,4},{4,8},{8,12},{12,14},{14,10},{10,6},{6,2},{2,0},{1,5},{5,9},... | collective-permute-start | bytes 786440 | tf_op jit(solution)/shard_map/ppermute | solution.py:142
  63.3 3.9 %shard_map.85 = (f32[1024,512]{1,0:T(8,128)S(1)}, f32[8,128]{1,0:T(8,128)}) custom-call(s32[2]{0:T(128)S(1)} %pad_add_fusion.4.places_ref, bf16[512,8192]{1,0:T(8,128)(2,1)} %mine_ref.13, bf16[512,8192]{1,0:T(8,128)(2,1)} %collective-permute-done.1.theirs_ref, bf16[256,512]{1,0:T(8,128)(2,1)} %collective-permute-done.11.refs_0_, ...), custom_call_target="tpu_custom_call", output_to_operand_aliasing={{0}: (7, {})} | custom-call | flops 1073741824 | bytes 2097152 | tf_op jit(solution)/shard_map/pallas_call | solution.py:71
  67.2 0.4 collective-permute-start.28
  67.6 4.8 %collective-permute-done.21.refs_2_ = bf16[256,512]{1,0:T(8,128)(2,1)} collective-permute-done((bf16[256,512]{1,0:T(8,128)(2,1)}, bf16[256,512]{1,0:T(8,128)(2,1)}, u32[]{:S(2)}, u32[]{:S(2)}) %collective-permute-start.21) | collective-permute-done | bytes 262176 | tf_op jit(solution)/shard_map/ppermute | solution.py:142
  72.4 0.7 collective-permute-start.26
  73.1 1.4 %collective-permute-start.24 = (bf16[256,512]{1,0:T(8,128)(2,1)}, bf16[256,512]{1,0:T(8,128)(2,1)}, u32[]{:S(2)}, u32[]{:S(2)}) collective-permute-start(bf16[256,512]{1,0:T(8,128)(2,1)} %collective-permute-done.20.refs_1_), channel_id=1, source_target_pairs={{0,4},{4,8},{8,12},{12,14},{14,10},{10,6},{6,2},{2,0},{1,5},{5,9},... | collective-permute-start | bytes 786440 | tf_op jit(solution)/shard_map/ppermute | solution.py:142
  74.4 1.4 %collective-permute-start.19 = (bf16[256,512]{1,0:T(8,128)(2,1)}, bf16[256,512]{1,0:T(8,128)(2,1)}, u32[]{:S(2)}, u32[]{:S(2)}) collective-permute-start(bf16[256,512]{1,0:T(8,128)(2,1)} %collective-permute-done.15.refs_0_), channel_id=1, source_target_pairs={{0,4},{4,8},{8,12},{12,14},{14,10},{10,6},{6,2},{2,0},{1,5},{5,9},... | collective-permute-start | bytes 786440 | tf_op jit(solution)/shard_map/ppermute | solution.py:142
  75.9 3.9 %shard_map.86 = (f32[1024,512]{1,0:T(8,128)S(1)}, f32[8,128]{1,0:T(8,128)}) custom-call(s32[2]{0:T(128)S(1)} %pad_add_fusion.5.places_ref, bf16[512,8192]{1,0:T(8,128)(2,1)} %mine_ref.13, bf16[512,8192]{1,0:T(8,128)(2,1)} %collective-permute-done.1.theirs_ref, bf16[256,512]{1,0:T(8,128)(2,1)} %collective-permute-done.15.refs_0_, ...), custom_call_target="tpu_custom_call", output_to_operand_aliasing={{0}: (7, {})} | custom-call | flops 1073741824 | bytes 2097152 | tf_op jit(solution)/shard_map/pallas_call | solution.py:71
  79.8 0.7 collective-permute-start.29
  80.5 3.1 %collective-permute-done.26.refs_2_ = bf16[256,512]{1,0:T(8,128)(2,1)} collective-permute-done((bf16[256,512]{1,0:T(8,128)(2,1)}, bf16[256,512]{1,0:T(8,128)(2,1)}, u32[]{:S(2)}, u32[]{:S(2)}) %collective-permute-start.26) | collective-permute-done | bytes 262176 | tf_op jit(solution)/shard_map/ppermute | solution.py:142
  83.6 0.7 collective-permute-start.27
  84.3 1.4 %collective-permute-start.25 = (bf16[256,512]{1,0:T(8,128)(2,1)}, bf16[256,512]{1,0:T(8,128)(2,1)}, u32[]{:S(2)}, u32[]{:S(2)}) collective-permute-start(bf16[256,512]{1,0:T(8,128)(2,1)} %collective-permute-done.24.refs_1_), channel_id=1, source_target_pairs={{0,4},{4,8},{8,12},{12,14},{14,10},{10,6},{6,2},{2,0},{1,5},{5,9},... | collective-permute-start | bytes 786440 | tf_op jit(solution)/shard_map/ppermute | solution.py:142
  85.8 1.3 collective-permute-start.23
  87.4 3.9 %shard_map.87 = (f32[1024,512]{1,0:T(8,128)S(1)}, f32[8,128]{1,0:T(8,128)}) custom-call(s32[2]{0:T(128)S(1)} %pad_add_fusion.6.places_ref, bf16[512,8192]{1,0:T(8,128)(2,1)} %mine_ref.13, bf16[512,8192]{1,0:T(8,128)(2,1)} %collective-permute-done.1.theirs_ref, bf16[256,512]{1,0:T(8,128)(2,1)} %collective-permute-done.19.refs_0_, ...), custom_call_target="tpu_custom_call", output_to_operand_aliasing={{0}: (7, {})} | custom-call | flops 1073741824 | bytes 2097152 | tf_op jit(solution)/shard_map/pallas_call | solution.py:71
  91.4 2.5 %collective-permute-done.23.refs_0_ = bf16[256,512]{1,0:T(8,128)(2,1)} collective-permute-done((bf16[256,512]{1,0:T(8,128)(2,1)}, bf16[256,512]{1,0:T(8,128)(2,1)}, u32[]{:S(2)}, u32[]{:S(2)}) %collective-permute-start.23) | collective-permute-done | bytes 262176 | tf_op jit(solution)/shard_map/ppermute | solution.py:142
  93.8 4.8 %shard_map.88 = (bf16[1024,512]{1,0:T(8,128)(2,1)}, f32[8,128]{1,0:T(8,128)}) custom-call(s32[4]{0:T(128)S(1)} %pad_add_fusion.places_ref, bf16[512,8192]{1,0:T(8,128)(2,1)} %mine_ref.13, bf16[512,8192]{1,0:T(8,128)(2,1)} %collective-permute-done.1.theirs_ref, bf16[256,512]{1,0:T(8,128)(2,1)} %collective-permute-done.23.refs_0_, ...), custom_call_target="tpu_custom_call" | custom-call | flops 1073741824 | bytes 2097152 | tf_op jit(solution)/shard_map/pallas_call | solution.py:71
  99.0 0.8 reshape.89
  100.2 0.7 fusion.17
  100.9 0.7 collective-permute-done.30.got_ref
  101.6 4.7 %shard_map.89 = f32[8,9,8,128]{3,2,1,0:T(8,128)} custom-call(s32[1]{0:T(128)} %bitcast.core_ref, bf16[1024,512]{1,0:T(8,128)(2,1)} %get-tuple-element.92.have_ref, bf16[1024,512]{1,0:T(8,128)(2,1)S(1)} %collective-permute-done.30.got_ref, bf16[512,512]{1,0:T(8,128)(2,1)S(1)} %get-tuple-element.93.key_up_ref, ...), custom_call_target="tpu_custom_call" | custom-call | flops 1342177280 | bytes 2097152 | tf_op jit(solution)/shard_map/pallas_call | solution.py:194
  106.3 3.7 %all-to-all-start = ((f32[8,72,128]{2,1,0:T(8,128)}), f32[8,72,128]{2,1,0:T(8,128)S(1)}, u32[]{:S(2)}, u32[]{:S(2)}) async-start(f32[8,72,128]{2,1,0:T(8,128)} %bitcast.25), calls=%async_computation | async-start | bytes 589824 | tf_op jit(solution)/shard_map/all_to_all | solution.py:288
  111.2 8.6 %all-to-all-done = f32[8,72,128]{2,1,0:T(8,128)S(1)} async-done(((f32[8,72,128]{2,1,0:T(8,128)}), f32[8,72,128]{2,1,0:T(8,128)S(1)}, u32[]{:S(2)}, u32[]{:S(2)}) %all-to-all-start) | async-done | bytes 294944 | tf_op jit(solution)/shard_map/all_to_all | solution.py:288
  119.8 0.4 shard_map.90
  120.2 1.5 %collective-permute-start.31 = (bf16[64,128]{1,0:T(8,128)(2,1)S(1)}, bf16[64,128]{1,0:T(8,128)(2,1)S(1)}, u32[]{:S(2)}, u32[]{:S(2)}) collective-permute-start(bf16[64,128]{1,0:T(8,128)(2,1)S(1)} %shard_map.90), channel_id=1, source_target_pairs={{0,2},{2,0},{4,6},{6,4},{8,10},{10,8},{12,14},{14,12},{1,3},{3,1},... | collective-permute-start | bytes 49160 | tf_op jit(solution)/shard_map/ppermute | solution.py:292
  121.7 2.3 %collective-permute-done.31 = bf16[64,128]{1,0:T(8,128)(2,1)S(1)} collective-permute-done((bf16[64,128]{1,0:T(8,128)(2,1)S(1)}, bf16[64,128]{1,0:T(8,128)(2,1)S(1)}, u32[]{:S(2)}, u32[]{:S(2)}) %collective-permute-start.31) | collective-permute-done | bytes 16416 | tf_op jit(solution)/shard_map/ppermute | solution.py:292
  124.0 1.2 collective-permute-start.32
  125.3 1.3 %collective-permute-start.33 = (bf16[128,128]{1,0:T(8,128)(2,1)S(1)}, bf16[128,128]{1,0:T(8,128)(2,1)S(1)}, u32[]{:S(2)}, u32[]{:S(2)}) collective-permute-start(bf16[128,128]{1,0:T(8,128)(2,1)S(1)} %pad_maximum_fusion.2), channel_id=1, source_target_pairs={{0,8},{2,10},{4,12},{6,14},{8,0},{10,2},{12,4},{14,6},{1,9},{3,11}... | collective-permute-start | bytes 98312 | tf_op jit(solution)/shard_map/ppermute | solution.py:295
  126.6 1.9 %collective-permute-start.34 = (bf16[128,128]{1,0:T(8,128)(2,1)S(1)}, bf16[128,128]{1,0:T(8,128)(2,1)S(1)}, u32[]{:S(2)}, u32[]{:S(2)}) collective-permute-start(bf16[128,128]{1,0:T(8,128)(2,1)S(1)} %pad_maximum_fusion.2), channel_id=1, source_target_pairs={{0,4},{2,6},{4,0},{6,2},{8,12},{10,14},{12,8},{14,10},{1,5},{3,7},... | collective-permute-start | bytes 98312 | tf_op jit(solution)/shard_map/ppermute | solution.py:295
  128.5 1.3 collective-permute-done.32
  129.8 0.8 collective-permute-done.33
  131.1 1.3 collective-permute-done.35
  132.7 0.9 reshape.98
  (73 shorter events, 3.9 us)
Async XLA Ops:
  0.0 52.0 %copy-start = (bf16[4,4,8192]{2,1,0:T(4,128)(2,1)S(1)}, bf16[4,4,8192]{2,1,0:T(4,128)(2,1)}, u32[]{:S(2)}) copy-start(bf16[4,4,8192]{2,1,0:T(4,128)(2,1)} %param.14) | copy-start | bytes 786436
  1.3 2.1 %collective-permute-start = (bf16[512,512]{1,0:T(8,128)(2,1)S(1)}, bf16[512,512]{1,0:T(8,128)(2,1)S(1)}, u32[]{:S(2)}, u32[]{:S(2)}) collective-permute-start(bf16[512,512]{1,0:T(8,128)(2,1)S(1)} %get-tuple-element.98), channel_id=1, source_target_pairs={{0,1},{1,0},{2,3},{3,2},{4,5},{5,4},{6,7},{7,6},{8,9},{9,8},{10,11... | collective-permute-start | bytes 1572872 | tf_op jit(solution)/shard_map/ppermute | solution.py:101
  3.4 22.7 %collective-permute-start.1 = (bf16[512,8192]{1,0:T(8,128)(2,1)}, bf16[512,8192]{1,0:T(8,128)(2,1)}, u32[]{:S(2)}, u32[]{:S(2)}) collective-permute-start(bf16[512,8192]{1,0:T(8,128)(2,1)} %mine_ref.13), channel_id=1, source_target_pairs={{0,1},{1,0},{2,3},{3,2},{4,5},{5,4},{6,7},{7,6},{8,9},{9,8},{10,11... | collective-permute-start | bytes 25165832 | tf_op jit(solution)/shard_map/ppermute | solution.py:126
  3.8 10.0 %collective-permute-start.2 = (bf16[256,512]{1,0:T(8,128)(2,1)S(1)}, bf16[256,512]{1,0:T(8,128)(2,1)}, u32[]{:S(2)}, u32[]{:S(2)}) collective-permute-start(bf16[256,512]{1,0:T(8,128)(2,1)S(1)} %get-tuple-element.102), channel_id=1, source_target_pairs={{0,4},{4,8},{8,12},{12,14},{14,10},{10,6},{6,2},{2,0},{1,5},{5,9},... | collective-permute-start | bytes 786440 | tf_op jit(solution)/shard_map/ppermute | solution.py:142
  6.6 12.5 %collective-permute-start.3 = (bf16[256,512]{1,0:T(8,128)(2,1)S(1)}, bf16[256,512]{1,0:T(8,128)(2,1)}, u32[]{:S(2)}, u32[]{:S(2)}) collective-permute-start(bf16[256,512]{1,0:T(8,128)(2,1)S(1)} %get-tuple-element.101), channel_id=1, source_target_pairs={{0,4},{4,8},{8,12},{12,14},{14,10},{10,6},{6,2},{2,0},{1,5},{5,9},... | collective-permute-start | bytes 786440 | tf_op jit(solution)/shard_map/ppermute | solution.py:142
  8.2 10.9 %collective-permute-start.4 = (bf16[256,512]{1,0:T(8,128)(2,1)S(1)}, bf16[256,512]{1,0:T(8,128)(2,1)}, u32[]{:S(2)}, u32[]{:S(2)}) collective-permute-start(bf16[256,512]{1,0:T(8,128)(2,1)S(1)} %get-tuple-element.100), channel_id=1, source_target_pairs={{4,0},{8,4},{12,8},{14,12},{10,14},{6,10},{2,6},{0,2},{5,1},{9,5},... | collective-permute-start | bytes 786440 | tf_op jit(solution)/shard_map/ppermute | solution.py:142
  8.7 13.3 %collective-permute-start.5 = (bf16[256,512]{1,0:T(8,128)(2,1)S(1)}, bf16[256,512]{1,0:T(8,128)(2,1)}, u32[]{:S(2)}, u32[]{:S(2)}) collective-permute-start(bf16[256,512]{1,0:T(8,128)(2,1)S(1)} %get-tuple-element.99), channel_id=1, source_target_pairs={{4,0},{8,4},{12,8},{14,12},{10,14},{6,10},{2,6},{0,2},{5,1},{9,5},... | collective-permute-start | bytes 786440 | tf_op jit(solution)/shard_map/ppermute | solution.py:142
  22.0 9.8 %collective-permute-start.10 = (bf16[256,512]{1,0:T(8,128)(2,1)}, bf16[256,512]{1,0:T(8,128)(2,1)}, u32[]{:S(2)}, u32[]{:S(2)}) collective-permute-start(bf16[256,512]{1,0:T(8,128)(2,1)} %collective-permute-done.5.refs_5_), channel_id=1, source_target_pairs={{4,0},{8,4},{12,8},{14,12},{10,14},{6,10},{2,6},{0,2},{5,1},{9,5},... | collective-permute-start | bytes 786440 | tf_op jit(solution)/shard_map/ppermute | solution.py:142
  22.4 16.8 %collective-permute-start.6 = (bf16[256,512]{1,0:T(8,128)(2,1)}, bf16[256,512]{1,0:T(8,128)(2,1)}, u32[]{:S(2)}, u32[]{:S(2)}) collective-permute-start(bf16[256,512]{1,0:T(8,128)(2,1)} %collective-permute-done.2.refs_2_), channel_id=1, source_target_pairs={{0,4},{4,8},{8,12},{12,14},{14,10},{10,6},{6,2},{2,0},{1,5},{5,9},... | collective-permute-start | bytes 786440 | tf_op jit(solution)/shard_map/ppermute | solution.py:142
  24.0 13.6 %collective-permute-start.8 = (bf16[256,512]{1,0:T(8,128)(2,1)}, bf16[256,512]{1,0:T(8,128)(2,1)}, u32[]{:S(2)}, u32[]{:S(2)}) collective-permute-start(bf16[256,512]{1,0:T(8,128)(2,1)} %collective-permute-done.3.refs_3_), channel_id=1, source_target_pairs={{0,4},{4,8},{8,12},{12,14},{14,10},{10,6},{6,2},{2,0},{1,5},{5,9},... | collective-permute-start | bytes 786440 | tf_op jit(solution)/shard_map/ppermute | solution.py:142
  25.6 11.6 %collective-permute-start.9 = (bf16[256,512]{1,0:T(8,128)(2,1)}, bf16[256,512]{1,0:T(8,128)(2,1)}, u32[]{:S(2)}, u32[]{:S(2)}) collective-permute-start(bf16[256,512]{1,0:T(8,128)(2,1)} %collective-permute-done.4.refs_4_), channel_id=1, source_target_pairs={{4,0},{8,4},{12,8},{14,12},{10,14},{6,10},{2,6},{0,2},{5,1},{9,5},... | collective-permute-start | bytes 786440 | tf_op jit(solution)/shard_map/ppermute | solution.py:142
  31.8 13.0 %collective-permute-start.14 = (bf16[256,512]{1,0:T(8,128)(2,1)}, bf16[256,512]{1,0:T(8,128)(2,1)}, u32[]{:S(2)}, u32[]{:S(2)}) collective-permute-start(bf16[256,512]{1,0:T(8,128)(2,1)} %collective-permute-done.10.refs_3_), channel_id=1, source_target_pairs={{4,0},{8,4},{12,8},{14,12},{10,14},{6,10},{2,6},{0,2},{5,1},{9,5},... | collective-permute-start | bytes 786440 | tf_op jit(solution)/shard_map/ppermute | solution.py:142
  37.1 11.2 %collective-permute-start.13 = (bf16[256,512]{1,0:T(8,128)(2,1)}, bf16[256,512]{1,0:T(8,128)(2,1)}, u32[]{:S(2)}, u32[]{:S(2)}) collective-permute-start(bf16[256,512]{1,0:T(8,128)(2,1)} %collective-permute-done.9.refs_2_), channel_id=1, source_target_pairs={{4,0},{8,4},{12,8},{14,12},{10,14},{6,10},{2,6},{0,2},{5,1},{9,5},... | collective-permute-start | bytes 786440 | tf_op jit(solution)/shard_map/ppermute | solution.py:142
  37.6 11.2 %collective-permute-start.12 = (bf16[256,512]{1,0:T(8,128)(2,1)}, bf16[256,512]{1,0:T(8,128)(2,1)}, u32[]{:S(2)}, u32[]{:S(2)}) collective-permute-start(bf16[256,512]{1,0:T(8,128)(2,1)} %collective-permute-done.8.refs_1_), channel_id=1, source_target_pairs={{0,4},{4,8},{8,12},{12,14},{14,10},{10,6},{6,2},{2,0},{1,5},{5,9},... | collective-permute-start | bytes 786440 | tf_op jit(solution)/shard_map/ppermute | solution.py:142
  39.2 11.2 %collective-permute-start.7 = (bf16[256,512]{1,0:T(8,128)(2,1)}, bf16[256,512]{1,0:T(8,128)(2,1)}, u32[]{:S(2)}, u32[]{:S(2)}) collective-permute-start(bf16[256,512]{1,0:T(8,128)(2,1)} %collective-permute-done.6.refs_0_), channel_id=1, source_target_pairs={{0,4},{4,8},{8,12},{12,14},{14,10},{10,6},{6,2},{2,0},{1,5},{5,9},... | collective-permute-start | bytes 786440 | tf_op jit(solution)/shard_map/ppermute | solution.py:142
  44.8 12.6 %collective-permute-start.18 = (bf16[256,512]{1,0:T(8,128)(2,1)}, bf16[256,512]{1,0:T(8,128)(2,1)}, u32[]{:S(2)}, u32[]{:S(2)}) collective-permute-start(bf16[256,512]{1,0:T(8,128)(2,1)} %collective-permute-done.14.refs_3_), channel_id=1, source_target_pairs={{4,0},{8,4},{12,8},{14,12},{10,14},{6,10},{2,6},{0,2},{5,1},{9,5},... | collective-permute-start | bytes 786440 | tf_op jit(solution)/shard_map/ppermute | solution.py:142
  48.4 11.2 %collective-permute-start.17 = (bf16[256,512]{1,0:T(8,128)(2,1)}, bf16[256,512]{1,0:T(8,128)(2,1)}, u32[]{:S(2)}, u32[]{:S(2)}) collective-permute-start(bf16[256,512]{1,0:T(8,128)(2,1)} %collective-permute-done.13.refs_2_), channel_id=1, source_target_pairs={{4,0},{8,4},{12,8},{14,12},{10,14},{6,10},{2,6},{0,2},{5,1},{9,5},... | collective-permute-start | bytes 786440 | tf_op jit(solution)/shard_map/ppermute | solution.py:142
  48.8 11.2 %collective-permute-start.16 = (bf16[256,512]{1,0:T(8,128)(2,1)}, bf16[256,512]{1,0:T(8,128)(2,1)}, u32[]{:S(2)}, u32[]{:S(2)}) collective-permute-start(bf16[256,512]{1,0:T(8,128)(2,1)} %collective-permute-done.12.refs_1_), channel_id=1, source_target_pairs={{0,4},{4,8},{8,12},{12,14},{14,10},{10,6},{6,2},{2,0},{1,5},{5,9},... | collective-permute-start | bytes 786440 | tf_op jit(solution)/shard_map/ppermute | solution.py:142
  50.4 11.2 %collective-permute-start.11 = (bf16[256,512]{1,0:T(8,128)(2,1)}, bf16[256,512]{1,0:T(8,128)(2,1)}, u32[]{:S(2)}, u32[]{:S(2)}) collective-permute-start(bf16[256,512]{1,0:T(8,128)(2,1)} %collective-permute-done.7.refs_0_), channel_id=1, source_target_pairs={{0,4},{4,8},{8,12},{12,14},{14,10},{10,6},{6,2},{2,0},{1,5},{5,9},... | collective-permute-start | bytes 786440 | tf_op jit(solution)/shard_map/ppermute | solution.py:142
  57.4 9.8 %collective-permute-start.22 = (bf16[256,512]{1,0:T(8,128)(2,1)}, bf16[256,512]{1,0:T(8,128)(2,1)}, u32[]{:S(2)}, u32[]{:S(2)}) collective-permute-start(bf16[256,512]{1,0:T(8,128)(2,1)} %collective-permute-done.18.refs_3_), channel_id=1, source_target_pairs={{4,0},{8,4},{12,8},{14,12},{10,14},{6,10},{2,6},{0,2},{5,1},{9,5},... | collective-permute-start | bytes 786440 | tf_op jit(solution)/shard_map/ppermute | solution.py:142
  59.5 12.9 %collective-permute-start.21 = (bf16[256,512]{1,0:T(8,128)(2,1)}, bf16[256,512]{1,0:T(8,128)(2,1)}, u32[]{:S(2)}, u32[]{:S(2)}) collective-permute-start(bf16[256,512]{1,0:T(8,128)(2,1)} %collective-permute-done.17.refs_2_), channel_id=1, source_target_pairs={{4,0},{8,4},{12,8},{14,12},{10,14},{6,10},{2,6},{0,2},{5,1},{9,5},... | collective-permute-start | bytes 786440 | tf_op jit(solution)/shard_map/ppermute | solution.py:142
  60.0 13.1 %collective-permute-start.20 = (bf16[256,512]{1,0:T(8,128)(2,1)}, bf16[256,512]{1,0:T(8,128)(2,1)}, u32[]{:S(2)}, u32[]{:S(2)}) collective-permute-start(bf16[256,512]{1,0:T(8,128)(2,1)} %collective-permute-done.16.refs_1_), channel_id=1, source_target_pairs={{0,4},{4,8},{8,12},{12,14},{14,10},{10,6},{6,2},{2,0},{1,5},{5,9},... | collective-permute-start | bytes 786440 | tf_op jit(solution)/shard_map/ppermute | solution.py:142
  61.6 12.9 %collective-permute-start.15 = (bf16[256,512]{1,0:T(8,128)(2,1)}, bf16[256,512]{1,0:T(8,128)(2,1)}, u32[]{:S(2)}, u32[]{:S(2)}) collective-permute-start(bf16[256,512]{1,0:T(8,128)(2,1)} %collective-permute-done.11.refs_0_), channel_id=1, source_target_pairs={{0,4},{4,8},{8,12},{12,14},{14,10},{10,6},{6,2},{2,0},{1,5},{5,9},... | collective-permute-start | bytes 786440 | tf_op jit(solution)/shard_map/ppermute | solution.py:142
  67.2 12.7 %collective-permute-start.28 = (bf16[256,512]{1,0:T(8,128)(2,1)}, bf16[256,512]{1,0:T(8,128)(2,1)}, u32[]{:S(2)}, u32[]{:S(2)}) collective-permute-start(bf16[256,512]{1,0:T(8,128)(2,1)} %collective-permute-done.22.refs_3_), channel_id=1, source_target_pairs={{4,0},{8,4},{12,8},{14,12},{10,14},{6,10},{2,6},{0,2},{5,1},{9,5},... | collective-permute-start | bytes 786440 | tf_op jit(solution)/shard_map/ppermute | solution.py:142
  72.4 11.2 %collective-permute-start.26 = (bf16[256,512]{1,0:T(8,128)(2,1)}, bf16[256,512]{1,0:T(8,128)(2,1)}, u32[]{:S(2)}, u32[]{:S(2)}) collective-permute-start(bf16[256,512]{1,0:T(8,128)(2,1)} %collective-permute-done.21.refs_2_), channel_id=1, source_target_pairs={{4,0},{8,4},{12,8},{14,12},{10,14},{6,10},{2,6},{0,2},{5,1},{9,5},... | collective-permute-start | bytes 786440 | tf_op jit(solution)/shard_map/ppermute | solution.py:142
  73.1 11.2 %collective-permute-start.24 = (bf16[256,512]{1,0:T(8,128)(2,1)}, bf16[256,512]{1,0:T(8,128)(2,1)}, u32[]{:S(2)}, u32[]{:S(2)}) collective-permute-start(bf16[256,512]{1,0:T(8,128)(2,1)} %collective-permute-done.20.refs_1_), channel_id=1, source_target_pairs={{0,4},{4,8},{8,12},{12,14},{14,10},{10,6},{6,2},{2,0},{1,5},{5,9},... | collective-permute-start | bytes 786440 | tf_op jit(solution)/shard_map/ppermute | solution.py:142
  74.4 11.3 %collective-permute-start.19 = (bf16[256,512]{1,0:T(8,128)(2,1)}, bf16[256,512]{1,0:T(8,128)(2,1)}, u32[]{:S(2)}, u32[]{:S(2)}) collective-permute-start(bf16[256,512]{1,0:T(8,128)(2,1)} %collective-permute-done.15.refs_0_), channel_id=1, source_target_pairs={{0,4},{4,8},{8,12},{12,14},{14,10},{10,6},{6,2},{2,0},{1,5},{5,9},... | collective-permute-start | bytes 786440 | tf_op jit(solution)/shard_map/ppermute | solution.py:142
  75.9 11.2 %copy-start.1 = (s32[4]{0:T(128)S(1)}, s32[4]{0:T(128)}, u32[]{:S(2)}) copy-start(s32[4]{0:T(128)} %param.13) | copy-start | bytes 52
  79.8 11.5 %collective-permute-start.29 = (bf16[256,512]{1,0:T(8,128)(2,1)}, bf16[256,512]{1,0:T(8,128)(2,1)}, u32[]{:S(2)}, u32[]{:S(2)}) collective-permute-start(bf16[256,512]{1,0:T(8,128)(2,1)} %collective-permute-done.28.refs_3_), channel_id=1, source_target_pairs={{4,0},{8,4},{12,8},{14,12},{10,14},{6,10},{2,6},{0,2},{5,1},{9,5},... | collective-permute-start | bytes 786440 | tf_op jit(solution)/shard_map/ppermute | solution.py:142
  83.6 7.7 %collective-permute-start.27 = (bf16[256,512]{1,0:T(8,128)(2,1)}, bf16[256,512]{1,0:T(8,128)(2,1)}, u32[]{:S(2)}, u32[]{:S(2)}) collective-permute-start(bf16[256,512]{1,0:T(8,128)(2,1)} %collective-permute-done.26.refs_2_), channel_id=1, source_target_pairs={{4,0},{8,4},{12,8},{14,12},{10,14},{6,10},{2,6},{0,2},{5,1},{9,5},... | collective-permute-start | bytes 786440 | tf_op jit(solution)/shard_map/ppermute | solution.py:142
  84.3 7.0 %collective-permute-start.25 = (bf16[256,512]{1,0:T(8,128)(2,1)}, bf16[256,512]{1,0:T(8,128)(2,1)}, u32[]{:S(2)}, u32[]{:S(2)}) collective-permute-start(bf16[256,512]{1,0:T(8,128)(2,1)} %collective-permute-done.24.refs_1_), channel_id=1, source_target_pairs={{0,4},{4,8},{8,12},{12,14},{14,10},{10,6},{6,2},{2,0},{1,5},{5,9},... | collective-permute-start | bytes 786440 | tf_op jit(solution)/shard_map/ppermute | solution.py:142
  85.8 8.1 %collective-permute-start.23 = (bf16[256,512]{1,0:T(8,128)(2,1)}, bf16[256,512]{1,0:T(8,128)(2,1)}, u32[]{:S(2)}, u32[]{:S(2)}) collective-permute-start(bf16[256,512]{1,0:T(8,128)(2,1)} %collective-permute-done.19.refs_0_), channel_id=1, source_target_pairs={{0,4},{4,8},{8,12},{12,14},{14,10},{10,6},{6,2},{2,0},{1,5},{5,9},... | collective-permute-start | bytes 786440 | tf_op jit(solution)/shard_map/ppermute | solution.py:142
  98.7 2.9 %collective-permute-start.30 = (bf16[1024,512]{1,0:T(8,128)(2,1)}, bf16[1024,512]{1,0:T(8,128)(2,1)S(1)}, u32[]{:S(2)}, u32[]{:S(2)}) collective-permute-start(bf16[1024,512]{1,0:T(8,128)(2,1)} %get-tuple-element.92.have_ref), channel_id=1, source_target_pairs={{0,1},{1,0},{2,3},{3,2},{4,5},{5,4},{6,7},{7,6},{8,9},{9,8},{10,11... | collective-permute-start | bytes 3145736 | tf_op jit(solution)/shard_map/ppermute | solution.py:261
  106.3 13.6 %all-to-all-start = ((f32[8,72,128]{2,1,0:T(8,128)}), f32[8,72,128]{2,1,0:T(8,128)S(1)}, u32[]{:S(2)}, u32[]{:S(2)}) async-start(f32[8,72,128]{2,1,0:T(8,128)} %bitcast.25), calls=%async_computation | async-start | bytes 589824 | tf_op jit(solution)/shard_map/all_to_all | solution.py:288
  120.2 3.8 %collective-permute-start.31 = (bf16[64,128]{1,0:T(8,128)(2,1)S(1)}, bf16[64,128]{1,0:T(8,128)(2,1)S(1)}, u32[]{:S(2)}, u32[]{:S(2)}) collective-permute-start(bf16[64,128]{1,0:T(8,128)(2,1)S(1)} %shard_map.90), channel_id=1, source_target_pairs={{0,2},{2,0},{4,6},{6,4},{8,10},{10,8},{12,14},{14,12},{1,3},{3,1},... | collective-permute-start | bytes 49160 | tf_op jit(solution)/shard_map/ppermute | solution.py:292
  124.0 5.8 %collective-permute-start.32 = (bf16[128,128]{1,0:T(8,128)(2,1)S(1)}, bf16[128,128]{1,0:T(8,128)(2,1)S(1)}, u32[]{:S(2)}, u32[]{:S(2)}) collective-permute-start(bf16[128,128]{1,0:T(8,128)(2,1)S(1)} %pad_maximum_fusion.2), channel_id=1, source_target_pairs={{0,12},{2,14},{4,8},{6,10},{8,4},{10,6},{12,0},{14,2},{1,13},{3,15... | collective-permute-start | bytes 98312 | tf_op jit(solution)/shard_map/ppermute | solution.py:295
  125.3 5.3 %collective-permute-start.33 = (bf16[128,128]{1,0:T(8,128)(2,1)S(1)}, bf16[128,128]{1,0:T(8,128)(2,1)S(1)}, u32[]{:S(2)}, u32[]{:S(2)}) collective-permute-start(bf16[128,128]{1,0:T(8,128)(2,1)S(1)} %pad_maximum_fusion.2), channel_id=1, source_target_pairs={{0,8},{2,10},{4,12},{6,14},{8,0},{10,2},{12,4},{14,6},{1,9},{3,11}... | collective-permute-start | bytes 98312 | tf_op jit(solution)/shard_map/ppermute | solution.py:295
  126.6 4.2 %collective-permute-start.34 = (bf16[128,128]{1,0:T(8,128)(2,1)S(1)}, bf16[128,128]{1,0:T(8,128)(2,1)S(1)}, u32[]{:S(2)}, u32[]{:S(2)}) collective-permute-start(bf16[128,128]{1,0:T(8,128)(2,1)S(1)} %pad_maximum_fusion.2), channel_id=1, source_target_pairs={{0,4},{2,6},{4,0},{6,2},{8,12},{10,14},{12,8},{14,10},{1,5},{3,7},... | collective-permute-start | bytes 98312 | tf_op jit(solution)/shard_map/ppermute | solution.py:295
  131.0 1.4 %collective-permute-start.35 = (bf16[16,1,4096]{2,0,1:T(8,128)(2,1)S(1)}, bf16[16,1,4096]{2,0,1:T(8,128)(2,1)S(1)}, u32[]{:S(2)}, u32[]{:S(2)}) collective-permute-start(bf16[16,1,4096]{2,0,1:T(8,128)(2,1)S(1)} %reshape.97), channel_id=1, source_target_pairs={{0,1},{1,0},{2,3},{3,2},{4,5},{5,4},{6,7},{7,6},{8,9},{9,8},{10,11... | collective-permute-start | bytes 393224 | tf_op jit(solution)/shard_map/ppermute | solution.py:305

commit v14 on v13

--- a/solution.py
+++ b/solution.py
@@ -121,16 +121,14 @@
         return source * rows + (core if way == 0 else 1 - core) * shard
 
     held = [own[k * piece : (k + 1) * piece] for k in range(chains)]
-    got, tokens_later = lax.optimization_barrier((got, tokens))
     held += [got[k * piece : (k + 1) * piece] for k in range(chains)]
-    theirs = lax.ppermute(tokens_later, "core", SWAP)
     todo = [(start_of(0, 0), [own]), (start_of(1, 0), [got])]
     total = None
     mark = None
     for step in range(1, chips):
-        ready = todo
         if step == 2:
-            held = lax.optimization_barrier(held)
+            held, tokens_later = lax.optimization_barrier((held, tokens))
+            theirs = lax.ppermute(tokens_later, "core", SWAP)
         if step == 3:
             _, inputs = lax.optimization_barrier((held[0], inputs))
             early = prepare(*inputs)
@@ -141,12 +139,12 @@
                 held[k], _ = lax.optimization_barrier((held[k], mark))
             held[k] = lax.ppermute(held[k], "chip", ways[k])
         arriving = [(start_of(w, step), held[w * chains : (w + 1) * chains]) for w in range(2)]
-        if step == 1:
-            todo = todo + arriving
-        else:
+        todo += arriving
+        if step >= 3:
+            ready, todo = (todo[:4], todo[4:]) if total is None else (todo[:2], todo[2:])
             total, mark = add_pieces(tokens, theirs, ready, total)
-            todo = arriving
-    return add_pieces(tokens, theirs, todo, total, core)[0], early
+    total, _ = add_pieces(tokens, theirs, todo[:2], total)
+    return add_pieces(tokens, theirs, todo[2:], total, core)[0], early
 
 
 def attend(have, got, core, key_up, value_up, query, bounds, chips):

time: 134 us -> 136 us (1.015)
  local copies, waits for them, and re-layouts: 4.47 us -> 11.1 us
  waiting for transfers between devices: 50.1 us -> 46.4 us
  Pallas kernels: 35 us -> 33.4 us
    unnamed x4 -> x20, local copies, waits for them, and re-layouts: 0.01 us -> 6.61 us
    ppermute x28, waiting for transfers between devices: 33.3 us -> 31.1 us  [project(): held[k] = lax.ppermute(held[k], 'chip', ways[k])]
    pallas_call x7, Pallas kernels: 30 us -> 28.3 us  [add_pieces(): pl.pallas_call(kernel, out_shape=(jax.ShapeDtypeStruct((2 * tok_rows, wid...]
    ppermute x1, waiting for transfers between devices: 1.54 us -> 0.01 us  [project(): got = lax.ppermute(jnp.where(first, value_down, key_down), 'core', SWAP)]
  transfers between devices with their start and end apart: 37 -> 37, of which waited for: 18 -> 17; matrix products, arithmetic and copies ran while one was open for 4% -> 4% of each run, Pallas kernels for 19% -> 18%
where the time goes in v14:
time: 136 us
  waiting for transfers between devices  46.4 us (34%)
  starting transfers between devices  40.8 us (30%)
  Pallas kernels  33.4 us (25%)
  local copies, waits for them, and re-layouts  11.1 us (8%)
  other arithmetic  2.42 us (2%)
  matrix products  1.36 us (1%)
    ppermute x28, waiting for transfers between devices, project(): held[k] = lax.ppermute(held[k], 'chip', ways[k])  31.1 us
    ppermute x28, starting transfers between devices, project(): held[k] = lax.ppermute(held[k], 'chip', ways[k])  30.1 us
    pallas_call x7, Pallas kernels, add_pieces(): pl.pallas_call(kernel, out_shape=(jax.ShapeDtypeStruct((2 * tok_rows, wid...  28.3 us
    all_to_all x1, waiting for transfers between devices, on_device(): lax.all_to_all(flat, 'chip', split_axis=0, concat_axis=0, tiled=True)  8.6 us
    unnamed x20, local copies, waits for them, and re-layouts  6.61 us
    pallas_call x1, Pallas kernels, attend(): pl.pallas_call(kernel, out_shape=jax.ShapeDtypeStruct((chips, blocks + 1,...  4.66 us
    ppermute x3, starting transfers between devices, on_device(): lax.ppermute(couple, 'chip', [(c, c ^ 2 * d) for c in range(chips)])  4.45 us
    all_to_all x1, starting transfers between devices, on_device(): lax.all_to_all(flat, 'chip', split_axis=0, concat_axis=0, tiled=True)  4.07 us
  transfers between devices with their start and end apart: 37, of which 17 were waited for; matrix products, arithmetic and copies ran while one was open for 4% of the time, Pallas kernels for 18%

profile of v14, /device:TPU:0, one launch (start us, length us, event | category | flops | bytes accessed | tf_op | source)
XLA Modules:
  0.0 135.7 jit_solution(5669805149866301414)
XLA Ops:
  0.0 1.3 broadcast_select_fusion
  1.3 0.5 collective-permute-start.2
  1.9 2.6 %collective-permute-start = (bf16[256,512]{1,0:T(8,128)(2,1)S(1)}, bf16[256,512]{1,0:T(8,128)(2,1)S(1)}, u32[]{:S(2)}, u32[]{:S(2)}) collective-permute-start(bf16[256,512]{1,0:T(8,128)(2,1)S(1)} %get-tuple-element.90), channel_id=1, source_target_pairs={{0,4},{4,8},{8,12},{12,14},{14,10},{10,6},{6,2},{2,0},{1,5},{5,9},... | collective-permute-start | bytes 786440 | tf_op jit(solution)/shard_map/ppermute | solution.py:140
  4.5 1.6 %collective-permute-start.1 = (bf16[256,512]{1,0:T(8,128)(2,1)S(1)}, bf16[256,512]{1,0:T(8,128)(2,1)S(1)}, u32[]{:S(2)}, u32[]{:S(2)}) collective-permute-start(bf16[256,512]{1,0:T(8,128)(2,1)S(1)} %get-tuple-element.89), channel_id=1, source_target_pairs={{0,4},{4,8},{8,12},{12,14},{14,10},{10,6},{6,2},{2,0},{1,5},{5,9},... | collective-permute-start | bytes 786440 | tf_op jit(solution)/shard_map/ppermute | solution.py:140
  6.6 1.3 collective-permute-start.4
  7.9 3.7 %collective-permute-done.refs_2_ = bf16[256,512]{1,0:T(8,128)(2,1)S(1)} collective-permute-done((bf16[256,512]{1,0:T(8,128)(2,1)S(1)}, bf16[256,512]{1,0:T(8,128)(2,1)S(1)}, u32[]{:S(2)}, u32[]{:S(2)}) %collective-permute-start) | collective-permute-done | bytes 262176 | tf_op jit(solution)/shard_map/ppermute | solution.py:140
  11.6 5.4 %collective-permute-done.1.refs_3_ = bf16[256,512]{1,0:T(8,128)(2,1)S(1)} collective-permute-done((bf16[256,512]{1,0:T(8,128)(2,1)S(1)}, bf16[256,512]{1,0:T(8,128)(2,1)S(1)}, u32[]{:S(2)}, u32[]{:S(2)}) %collective-permute-start.1) | collective-permute-done | bytes 262176 | tf_op jit(solution)/shard_map/ppermute | solution.py:140
  17.0 2.9 %collective-permute-done.4.refs_5_ = bf16[256,512]{1,0:T(8,128)(2,1)S(1)} collective-permute-done((bf16[256,512]{1,0:T(8,128)(2,1)S(1)}, bf16[256,512]{1,0:T(8,128)(2,1)S(1)}, u32[]{:S(2)}, u32[]{:S(2)}) %collective-permute-start.4) | collective-permute-done | bytes 262176 | tf_op jit(solution)/shard_map/ppermute | solution.py:140
  20.4 0.7 copy-done.7
  21.1 1.5 %collective-permute-start.10 = (bf16[256,512]{1,0:T(8,128)(2,1)S(1)}, bf16[256,512]{1,0:T(8,128)(2,1)}, u32[]{:S(2)}, u32[]{:S(2)}) collective-permute-start(bf16[256,512]{1,0:T(8,128)(2,1)S(1)} %collective-permute-done.3.refs_4_), channel_id=1, source_target_pairs={{4,0},{8,4},{12,8},{14,12},{10,14},{6,10},{2,6},{0,2},{5,1},{9,5},... | collective-permute-start | bytes 786440 | tf_op jit(solution)/shard_map/ppermute | solution.py:140
  22.6 0.7 copy-done.5
  23.3 0.5 collective-permute-start.9
  23.8 0.7 copy-done.3
  24.5 1.6 %collective-permute-start.6 = (bf16[256,512]{1,0:T(8,128)(2,1)S(1)}, bf16[256,512]{1,0:T(8,128)(2,1)}, u32[]{:S(2)}, u32[]{:S(2)}) collective-permute-start(bf16[256,512]{1,0:T(8,128)(2,1)S(1)} %collective-permute-done.refs_2_), channel_id=1, source_target_pairs={{0,4},{4,8},{8,12},{12,14},{14,10},{10,6},{6,2},{2,0},{1,5},{5,9},... | collective-permute-start | bytes 786440 | tf_op jit(solution)/shard_map/ppermute | solution.py:140
  26.1 0.7 copy-done.1
  26.9 2.3 %collective-permute-done.11.refs_3_ = bf16[256,512]{1,0:T(8,128)(2,1)} collective-permute-done((bf16[256,512]{1,0:T(8,128)(2,1)S(1)}, bf16[256,512]{1,0:T(8,128)(2,1)}, u32[]{:S(2)}, u32[]{:S(2)}) %collective-permute-start.11) | collective-permute-done | bytes 262176 | tf_op jit(solution)/shard_map/ppermute | solution.py:140
  29.6 5.2 %collective-permute-done.10.refs_2_ = bf16[256,512]{1,0:T(8,128)(2,1)} collective-permute-done((bf16[256,512]{1,0:T(8,128)(2,1)S(1)}, bf16[256,512]{1,0:T(8,128)(2,1)}, u32[]{:S(2)}, u32[]{:S(2)}) %collective-permute-start.10) | collective-permute-done | bytes 262176 | tf_op jit(solution)/shard_map/ppermute | solution.py:140
  35.2 1.6 %collective-permute-start.13 = (bf16[256,512]{1,0:T(8,128)(2,1)}, bf16[256,512]{1,0:T(8,128)(2,1)}, u32[]{:S(2)}, u32[]{:S(2)}) collective-permute-start(bf16[256,512]{1,0:T(8,128)(2,1)} %collective-permute-done.9.refs_1_), channel_id=1, source_target_pairs={{0,4},{4,8},{8,12},{12,14},{14,10},{10,6},{6,2},{2,0},{1,5},{5,9},... | collective-permute-start | bytes 786440 | tf_op jit(solution)/shard_map/ppermute | solution.py:140
  37.2 1.2 collective-permute-start.7
  38.5 1.0 copy-done.2
  39.4 0.9 copy-done.4
  40.4 0.9 copy-done.6
  41.3 0.9 copy-done.8
  42.3 4.7 %shard_map.82 = (f32[1024,512]{1,0:T(8,128)S(1)}, f32[8,128]{1,0:T(8,128)}) custom-call(s32[4]{0:T(128)S(1)} %pad_add_fusion.1.places_ref, bf16[512,8192]{1,0:T(8,128)(2,1)} %mine_ref.13, bf16[512,8192]{1,0:T(8,128)(2,1)} %collective-permute-done.5.theirs_ref, bf16[512,512]{1,0:T(8,128)(2,1)S(1)} %get-tuple-element.86.refs_0_, ...), custom_call_target="tpu_custom_call" | custom-call | flops 2147483648 | bytes 4194304 | tf_op jit(solution)/shard_map/pallas_call | solution.py:71
  47.0 0.9 collective-permute-start.19
  47.9 1.6 %collective-permute-start.18 = (bf16[256,512]{1,0:T(8,128)(2,1)}, bf16[256,512]{1,0:T(8,128)(2,1)}, u32[]{:S(2)}, u32[]{:S(2)}) collective-permute-start(bf16[256,512]{1,0:T(8,128)(2,1)} %collective-permute-done.14.refs_2_), channel_id=1, source_target_pairs={{4,0},{8,4},{12,8},{14,12},{10,14},{6,10},{2,6},{0,2},{5,1},{9,5},... | collective-permute-start | bytes 786440 | tf_op jit(solution)/shard_map/ppermute | solution.py:140
  49.9 1.2 collective-permute-start.8
  51.3 1.3 constant_dynamic-slice_fusion.1
  52.6 3.9 %shard_map.83 = (f32[1024,512]{1,0:T(8,128)S(1)}, f32[8,128]{1,0:T(8,128)}) custom-call(s32[2]{0:T(128)S(1)} %pad_add_fusion.2.places_ref, bf16[512,8192]{1,0:T(8,128)(2,1)} %mine_ref.13, bf16[512,8192]{1,0:T(8,128)(2,1)} %collective-permute-done.5.theirs_ref, bf16[256,512]{1,0:T(8,128)(2,1)} %collective-permute-done.6.refs_0_, ...), custom_call_target="tpu_custom_call", output_to_operand_aliasing={{0}: (7, {})} | custom-call | flops 1073741824 | bytes 2097152 | tf_op jit(solution)/shard_map/pallas_call | solution.py:71
  56.6 0.8 collective-permute-start.27
  57.4 4.8 %collective-permute-done.18.refs_2_ = bf16[256,512]{1,0:T(8,128)(2,1)} collective-permute-done((bf16[256,512]{1,0:T(8,128)(2,1)}, bf16[256,512]{1,0:T(8,128)(2,1)}, u32[]{:S(2)}, u32[]{:S(2)}) %collective-permute-start.18) | collective-permute-done | bytes 262176 | tf_op jit(solution)/shard_map/ppermute | solution.py:140
  62.2 0.8 collective-permute-start.24
  63.0 1.2 collective-permute-start.21
  64.3 1.5 %collective-permute-start.12 = (bf16[256,512]{1,0:T(8,128)(2,1)}, bf16[256,512]{1,0:T(8,128)(2,1)}, u32[]{:S(2)}, u32[]{:S(2)}) collective-permute-start(bf16[256,512]{1,0:T(8,128)(2,1)} %collective-permute-done.8.refs_0_), channel_id=1, source_target_pairs={{0,4},{4,8},{8,12},{12,14},{14,10},{10,6},{6,2},{2,0},{1,5},{5,9},... | collective-permute-start | bytes 786440 | tf_op jit(solution)/shard_map/ppermute | solution.py:140
  65.9 3.9 %shard_map.84 = (f32[1024,512]{1,0:T(8,128)S(1)}, f32[8,128]{1,0:T(8,128)}) custom-call(s32[2]{0:T(128)S(1)} %pad_add_fusion.3.places_ref, bf16[512,8192]{1,0:T(8,128)(2,1)} %mine_ref.13, bf16[512,8192]{1,0:T(8,128)(2,1)} %collective-permute-done.5.theirs_ref, bf16[256,512]{1,0:T(8,128)(2,1)} %collective-permute-done.7.refs_0_, ...), custom_call_target="tpu_custom_call", output_to_operand_aliasing={{0}: (7, {})} | custom-call | flops 1073741824 | bytes 2097152 | tf_op jit(solution)/shard_map/pallas_call | solution.py:71
  69.8 0.6 collective-permute-start.28
  70.4 3.1 %collective-permute-done.24.refs_2_ = bf16[256,512]{1,0:T(8,128)(2,1)} collective-permute-done((bf16[256,512]{1,0:T(8,128)(2,1)}, bf16[256,512]{1,0:T(8,128)(2,1)}, u32[]{:S(2)}, u32[]{:S(2)}) %collective-permute-start.24) | collective-permute-done | bytes 262176 | tf_op jit(solution)/shard_map/ppermute | solution.py:140
  73.5 0.8 collective-permute-start.25
  74.3 1.2 collective-permute-start.22
  75.5 1.5 %collective-permute-start.16 = (bf16[256,512]{1,0:T(8,128)(2,1)}, bf16[256,512]{1,0:T(8,128)(2,1)}, u32[]{:S(2)}, u32[]{:S(2)}) collective-permute-start(bf16[256,512]{1,0:T(8,128)(2,1)} %collective-permute-done.12.refs_0_), channel_id=1, source_target_pairs={{0,4},{4,8},{8,12},{12,14},{14,10},{10,6},{6,2},{2,0},{1,5},{5,9},... | collective-permute-start | bytes 786440 | tf_op jit(solution)/shard_map/ppermute | solution.py:140
  77.3 3.9 %shard_map.85 = (f32[1024,512]{1,0:T(8,128)S(1)}, f32[8,128]{1,0:T(8,128)}) custom-call(s32[2]{0:T(128)S(1)} %pad_add_fusion.4.places_ref, bf16[512,8192]{1,0:T(8,128)(2,1)} %mine_ref.13, bf16[512,8192]{1,0:T(8,128)(2,1)} %collective-permute-done.5.theirs_ref, bf16[256,512]{1,0:T(8,128)(2,1)} %collective-permute-done.8.refs_0_, ...), custom_call_target="tpu_custom_call", output_to_operand_aliasing={{0}: (7, {})} | custom-call | flops 1073741824 | bytes 2097152 | tf_op jit(solution)/shard_map/pallas_call | solution.py:71
  81.2 0.6 collective-permute-start.29
  81.8 3.3 %collective-permute-done.25.refs_2_ = bf16[256,512]{1,0:T(8,128)(2,1)} collective-permute-done((bf16[256,512]{1,0:T(8,128)(2,1)}, bf16[256,512]{1,0:T(8,128)(2,1)}, u32[]{:S(2)}, u32[]{:S(2)}) %collective-permute-start.25) | collective-permute-done | bytes 262176 | tf_op jit(solution)/shard_map/ppermute | solution.py:140
  85.1 0.5 collective-permute-start.26
  85.6 1.5 %collective-permute-start.23 = (bf16[256,512]{1,0:T(8,128)(2,1)}, bf16[256,512]{1,0:T(8,128)(2,1)S(1)}, u32[]{:S(2)}, u32[]{:S(2)}) collective-permute-start(bf16[256,512]{1,0:T(8,128)(2,1)} %collective-permute-done.22.refs_1_), channel_id=1, source_target_pairs={{0,4},{4,8},{8,12},{12,14},{14,10},{10,6},{6,2},{2,0},{1,5},{5,9},... | collective-permute-start | bytes 786440 | tf_op jit(solution)/shard_map/ppermute | solution.py:140
  87.1 1.1 collective-permute-start.20
  88.3 3.9 %shard_map.86 = (f32[1024,512]{1,0:T(8,128)S(1)}, f32[8,128]{1,0:T(8,128)}) custom-call(s32[2]{0:T(128)S(1)} %pad_add_fusion.6.places_ref, bf16[512,8192]{1,0:T(8,128)(2,1)} %mine_ref.13, bf16[512,8192]{1,0:T(8,128)(2,1)} %collective-permute-done.5.theirs_ref, bf16[256,512]{1,0:T(8,128)(2,1)} %collective-permute-done.12.refs_0_, ...), custom_call_target="tpu_custom_call", output_to_operand_aliasing={{0}: (7, {})} | custom-call | flops 1073741824 | bytes 2097152 | tf_op jit(solution)/shard_map/pallas_call | solution.py:71
  92.2 3.9 %shard_map.87 = (f32[1024,512]{1,0:T(8,128)S(1)}, f32[8,128]{1,0:T(8,128)}) custom-call(s32[2]{0:T(128)S(1)} %pad_add_fusion.5.places_ref, bf16[512,8192]{1,0:T(8,128)(2,1)} %mine_ref.13, bf16[512,8192]{1,0:T(8,128)(2,1)} %collective-permute-done.5.theirs_ref, bf16[256,512]{1,0:T(8,128)(2,1)} %collective-permute-done.16.refs_0_, ...), custom_call_target="tpu_custom_call", output_to_operand_aliasing={{0}: (7, {})} | custom-call | flops 1073741824 | bytes 2097152 | tf_op jit(solution)/shard_map/pallas_call | solution.py:71
  96.2 4.2 %shard_map.88 = (bf16[1024,512]{1,0:T(8,128)(2,1)}, f32[8,128]{1,0:T(8,128)}) custom-call(s32[4]{0:T(128)S(1)} %pad_add_fusion.places_ref, bf16[512,8192]{1,0:T(8,128)(2,1)} %mine_ref.13, bf16[512,8192]{1,0:T(8,128)(2,1)} %collective-permute-done.5.theirs_ref, bf16[256,512]{1,0:T(8,128)(2,1)S(1)} %collective-permute-done.20.refs_0_, ...), custom_call_target="tpu_custom_call" | custom-call | flops 1073741824 | bytes 2097152 | tf_op jit(solution)/shard_map/pallas_call | solution.py:71
  100.7 0.8 reshape.89
  101.9 0.7 fusion.17
  102.6 0.7 collective-permute-done.30.got_ref
  103.3 4.7 %shard_map.89 = f32[8,9,8,128]{3,2,1,0:T(8,128)} custom-call(s32[1]{0:T(128)} %bitcast.core_ref, bf16[1024,512]{1,0:T(8,128)(2,1)} %get-tuple-element.80.have_ref, bf16[1024,512]{1,0:T(8,128)(2,1)S(1)} %collective-permute-done.30.got_ref, bf16[512,512]{1,0:T(8,128)(2,1)S(1)} %get-tuple-element.81.key_up_ref, ...), custom_call_target="tpu_custom_call" | custom-call | flops 1342177280 | bytes 2097152 | tf_op jit(solution)/shard_map/pallas_call | solution.py:192
  108.0 4.1 %all-to-all-start = ((f32[8,72,128]{2,1,0:T(8,128)}), f32[8,72,128]{2,1,0:T(8,128)S(1)}, u32[]{:S(2)}, u32[]{:S(2)}) async-start(f32[8,72,128]{2,1,0:T(8,128)} %bitcast.25), calls=%async_computation | async-start | bytes 589824 | tf_op jit(solution)/shard_map/all_to_all | solution.py:286
  113.3 8.6 %all-to-all-done = f32[8,72,128]{2,1,0:T(8,128)S(1)} async-done(((f32[8,72,128]{2,1,0:T(8,128)}), f32[8,72,128]{2,1,0:T(8,128)S(1)}, u32[]{:S(2)}, u32[]{:S(2)}) %all-to-all-start) | async-done | bytes 294944 | tf_op jit(solution)/shard_map/all_to_all | solution.py:286
  122.3 1.5 %collective-permute-start.31 = (bf16[64,128]{1,0:T(8,128)(2,1)S(1)}, bf16[64,128]{1,0:T(8,128)(2,1)S(1)}, u32[]{:S(2)}, u32[]{:S(2)}) collective-permute-start(bf16[64,128]{1,0:T(8,128)(2,1)S(1)} %shard_map.90), channel_id=1, source_target_pairs={{0,2},{2,0},{4,6},{6,4},{8,10},{10,8},{12,14},{14,12},{1,3},{3,1},... | collective-permute-start | bytes 49160 | tf_op jit(solution)/shard_map/ppermute | solution.py:290
  123.8 2.3 %collective-permute-done.31 = bf16[64,128]{1,0:T(8,128)(2,1)S(1)} collective-permute-done((bf16[64,128]{1,0:T(8,128)(2,1)S(1)}, bf16[64,128]{1,0:T(8,128)(2,1)S(1)}, u32[]{:S(2)}, u32[]{:S(2)}) %collective-permute-start.31) | collective-permute-done | bytes 16416 | tf_op jit(solution)/shard_map/ppermute | solution.py:290
  126.1 1.2 collective-permute-start.32
  127.3 1.3 collective-permute-start.33
  128.7 1.9 %collective-permute-start.34 = (bf16[128,128]{1,0:T(8,128)(2,1)S(1)}, bf16[128,128]{1,0:T(8,128)(2,1)S(1)}, u32[]{:S(2)}, u32[]{:S(2)}) collective-permute-start(bf16[128,128]{1,0:T(8,128)(2,1)S(1)} %pad_maximum_fusion.2), channel_id=1, source_target_pairs={{0,4},{2,6},{4,0},{6,2},{8,12},{10,14},{12,8},{14,10},{1,5},{3,7},... | collective-permute-start | bytes 98312 | tf_op jit(solution)/shard_map/ppermute | solution.py:293
  130.6 1.3 collective-permute-done.32
  131.9 0.8 collective-permute-done.33
  133.1 1.3 collective-permute-done.35
  134.8 0.9 reshape.98
  (89 shorter events, 6.8 us)
Async XLA Ops:
  0.0 51.1 %copy-start = (bf16[4,4,8192]{2,1,0:T(4,128)(2,1)S(1)}, bf16[4,4,8192]{2,1,0:T(4,128)(2,1)}, u32[]{:S(2)}) copy-start(bf16[4,4,8192]{2,1,0:T(4,128)(2,1)} %param.14) | copy-start | bytes 786436
  1.3 4.8 %collective-permute-start.2 = (bf16[512,512]{1,0:T(8,128)(2,1)S(1)}, bf16[512,512]{1,0:T(8,128)(2,1)S(1)}, u32[]{:S(2)}, u32[]{:S(2)}) collective-permute-start(bf16[512,512]{1,0:T(8,128)(2,1)S(1)} %get-tuple-element.85), channel_id=1, source_target_pairs={{0,1},{1,0},{2,3},{3,2},{4,5},{5,4},{6,7},{7,6},{8,9},{9,8},{10,11... | collective-permute-start | bytes 1572872 | tf_op jit(solution)/shard_map/ppermute | solution.py:101
  1.9 9.7 %collective-permute-start = (bf16[256,512]{1,0:T(8,128)(2,1)S(1)}, bf16[256,512]{1,0:T(8,128)(2,1)S(1)}, u32[]{:S(2)}, u32[]{:S(2)}) collective-permute-start(bf16[256,512]{1,0:T(8,128)(2,1)S(1)} %get-tuple-element.90), channel_id=1, source_target_pairs={{0,4},{4,8},{8,12},{12,14},{14,10},{10,6},{6,2},{2,0},{1,5},{5,9},... | collective-permute-start | bytes 786440 | tf_op jit(solution)/shard_map/ppermute | solution.py:140
  4.5 12.5 %collective-permute-start.1 = (bf16[256,512]{1,0:T(8,128)(2,1)S(1)}, bf16[256,512]{1,0:T(8,128)(2,1)S(1)}, u32[]{:S(2)}, u32[]{:S(2)}) collective-permute-start(bf16[256,512]{1,0:T(8,128)(2,1)S(1)} %get-tuple-element.89), channel_id=1, source_target_pairs={{0,4},{4,8},{8,12},{12,14},{14,10},{10,6},{6,2},{2,0},{1,5},{5,9},... | collective-permute-start | bytes 786440 | tf_op jit(solution)/shard_map/ppermute | solution.py:140
  6.1 10.9 %collective-permute-start.3 = (bf16[256,512]{1,0:T(8,128)(2,1)S(1)}, bf16[256,512]{1,0:T(8,128)(2,1)S(1)}, u32[]{:S(2)}, u32[]{:S(2)}) collective-permute-start(bf16[256,512]{1,0:T(8,128)(2,1)S(1)} %get-tuple-element.88), channel_id=1, source_target_pairs={{4,0},{8,4},{12,8},{14,12},{10,14},{6,10},{2,6},{0,2},{5,1},{9,5},... | collective-permute-start | bytes 786440 | tf_op jit(solution)/shard_map/ppermute | solution.py:140
  6.6 13.3 %collective-permute-start.4 = (bf16[256,512]{1,0:T(8,128)(2,1)S(1)}, bf16[256,512]{1,0:T(8,128)(2,1)S(1)}, u32[]{:S(2)}, u32[]{:S(2)}) collective-permute-start(bf16[256,512]{1,0:T(8,128)(2,1)S(1)} %get-tuple-element.87), channel_id=1, source_target_pairs={{4,0},{8,4},{12,8},{14,12},{10,14},{6,10},{2,6},{0,2},{5,1},{9,5},... | collective-permute-start | bytes 786440 | tf_op jit(solution)/shard_map/ppermute | solution.py:140
  20.0 18.5 %collective-permute-start.5 = (bf16[512,8192]{1,0:T(8,128)(2,1)}, bf16[512,8192]{1,0:T(8,128)(2,1)}, u32[]{:S(2)}, u32[]{:S(2)}) collective-permute-start(bf16[512,8192]{1,0:T(8,128)(2,1)} %mine_ref.13), channel_id=1, source_target_pairs={{0,1},{1,0},{2,3},{3,2},{4,5},{5,4},{6,7},{7,6},{8,9},{9,8},{10,11... | collective-permute-start | bytes 25165832 | tf_op jit(solution)/shard_map/ppermute | solution.py:131
  20.0 9.2 %collective-permute-start.11 = (bf16[256,512]{1,0:T(8,128)(2,1)S(1)}, bf16[256,512]{1,0:T(8,128)(2,1)}, u32[]{:S(2)}, u32[]{:S(2)}) collective-permute-start(bf16[256,512]{1,0:T(8,128)(2,1)S(1)} %collective-permute-done.4.refs_5_), channel_id=1, source_target_pairs={{4,0},{8,4},{12,8},{14,12},{10,14},{6,10},{2,6},{0,2},{5,1},{9,5},... | collective-permute-start | bytes 786440 | tf_op jit(solution)/shard_map/ppermute | solution.py:140
  20.4 0.7 copy-start.7
  21.1 13.7 %collective-permute-start.10 = (bf16[256,512]{1,0:T(8,128)(2,1)S(1)}, bf16[256,512]{1,0:T(8,128)(2,1)}, u32[]{:S(2)}, u32[]{:S(2)}) collective-permute-start(bf16[256,512]{1,0:T(8,128)(2,1)S(1)} %collective-permute-done.3.refs_4_), channel_id=1, source_target_pairs={{4,0},{8,4},{12,8},{14,12},{10,14},{6,10},{2,6},{0,2},{5,1},{9,5},... | collective-permute-start | bytes 786440 | tf_op jit(solution)/shard_map/ppermute | solution.py:140
  22.6 0.7 copy-start.5
  23.3 11.9 %collective-permute-start.9 = (bf16[256,512]{1,0:T(8,128)(2,1)S(1)}, bf16[256,512]{1,0:T(8,128)(2,1)}, u32[]{:S(2)}, u32[]{:S(2)}) collective-permute-start(bf16[256,512]{1,0:T(8,128)(2,1)S(1)} %collective-permute-done.1.refs_3_), channel_id=1, source_target_pairs={{0,4},{4,8},{8,12},{12,14},{14,10},{10,6},{6,2},{2,0},{1,5},{5,9},... | collective-permute-start | bytes 786440 | tf_op jit(solution)/shard_map/ppermute | solution.py:140
  23.8 0.7 copy-start.3
  24.5 12.6 %collective-permute-start.6 = (bf16[256,512]{1,0:T(8,128)(2,1)S(1)}, bf16[256,512]{1,0:T(8,128)(2,1)}, u32[]{:S(2)}, u32[]{:S(2)}) collective-permute-start(bf16[256,512]{1,0:T(8,128)(2,1)S(1)} %collective-permute-done.refs_2_), channel_id=1, source_target_pairs={{0,4},{4,8},{8,12},{12,14},{14,10},{10,6},{6,2},{2,0},{1,5},{5,9},... | collective-permute-start | bytes 786440 | tf_op jit(solution)/shard_map/ppermute | solution.py:140
  26.1 0.7 copy-start.1
  29.2 17.8 %collective-permute-start.15 = (bf16[256,512]{1,0:T(8,128)(2,1)}, bf16[256,512]{1,0:T(8,128)(2,1)}, u32[]{:S(2)}, u32[]{:S(2)}) collective-permute-start(bf16[256,512]{1,0:T(8,128)(2,1)} %collective-permute-done.11.refs_3_), channel_id=1, source_target_pairs={{4,0},{8,4},{12,8},{14,12},{10,14},{6,10},{2,6},{0,2},{5,1},{9,5},... | collective-permute-start | bytes 786440 | tf_op jit(solution)/shard_map/ppermute | solution.py:140
  34.8 13.1 %collective-permute-start.14 = (bf16[256,512]{1,0:T(8,128)(2,1)}, bf16[256,512]{1,0:T(8,128)(2,1)}, u32[]{:S(2)}, u32[]{:S(2)}) collective-permute-start(bf16[256,512]{1,0:T(8,128)(2,1)} %collective-permute-done.10.refs_2_), channel_id=1, source_target_pairs={{4,0},{8,4},{12,8},{14,12},{10,14},{6,10},{2,6},{0,2},{5,1},{9,5},... | collective-permute-start | bytes 786440 | tf_op jit(solution)/shard_map/ppermute | solution.py:140
  35.2 14.2 %collective-permute-start.13 = (bf16[256,512]{1,0:T(8,128)(2,1)}, bf16[256,512]{1,0:T(8,128)(2,1)}, u32[]{:S(2)}, u32[]{:S(2)}) collective-permute-start(bf16[256,512]{1,0:T(8,128)(2,1)} %collective-permute-done.9.refs_1_), channel_id=1, source_target_pairs={{0,4},{4,8},{8,12},{12,14},{14,10},{10,6},{6,2},{2,0},{1,5},{5,9},... | collective-permute-start | bytes 786440 | tf_op jit(solution)/shard_map/ppermute | solution.py:140
  37.2 12.7 %collective-permute-start.7 = (bf16[256,512]{1,0:T(8,128)(2,1)}, bf16[256,512]{1,0:T(8,128)(2,1)}, u32[]{:S(2)}, u32[]{:S(2)}) collective-permute-start(bf16[256,512]{1,0:T(8,128)(2,1)} %collective-permute-done.6.refs_0_), channel_id=1, source_target_pairs={{0,4},{4,8},{8,12},{12,14},{14,10},{10,6},{6,2},{2,0},{1,5},{5,9},... | collective-permute-start | bytes 786440 | tf_op jit(solution)/shard_map/ppermute | solution.py:140
  38.5 1.0 copy-start.2
  39.4 0.9 copy-start.4
  40.4 0.9 copy-start.6
  41.3 0.9 copy-start.8
  47.0 9.6 %collective-permute-start.19 = (bf16[256,512]{1,0:T(8,128)(2,1)}, bf16[256,512]{1,0:T(8,128)(2,1)}, u32[]{:S(2)}, u32[]{:S(2)}) collective-permute-start(bf16[256,512]{1,0:T(8,128)(2,1)} %collective-permute-done.15.refs_3_), channel_id=1, source_target_pairs={{4,0},{8,4},{12,8},{14,12},{10,14},{6,10},{2,6},{0,2},{5,1},{9,5},... | collective-permute-start | bytes 786440 | tf_op jit(solution)/shard_map/ppermute | solution.py:140
  47.9 14.4 %collective-permute-start.18 = (bf16[256,512]{1,0:T(8,128)(2,1)}, bf16[256,512]{1,0:T(8,128)(2,1)}, u32[]{:S(2)}, u32[]{:S(2)}) collective-permute-start(bf16[256,512]{1,0:T(8,128)(2,1)} %collective-permute-done.14.refs_2_), channel_id=1, source_target_pairs={{4,0},{8,4},{12,8},{14,12},{10,14},{6,10},{2,6},{0,2},{5,1},{9,5},... | collective-permute-start | bytes 786440 | tf_op jit(solution)/shard_map/ppermute | solution.py:140
  49.4 13.6 %collective-permute-start.17 = (bf16[256,512]{1,0:T(8,128)(2,1)}, bf16[256,512]{1,0:T(8,128)(2,1)}, u32[]{:S(2)}, u32[]{:S(2)}) collective-permute-start(bf16[256,512]{1,0:T(8,128)(2,1)} %collective-permute-done.13.refs_1_), channel_id=1, source_target_pairs={{0,4},{4,8},{8,12},{12,14},{14,10},{10,6},{6,2},{2,0},{1,5},{5,9},... | collective-permute-start | bytes 786440 | tf_op jit(solution)/shard_map/ppermute | solution.py:140
  49.9 14.4 %collective-permute-start.8 = (bf16[256,512]{1,0:T(8,128)(2,1)}, bf16[256,512]{1,0:T(8,128)(2,1)}, u32[]{:S(2)}, u32[]{:S(2)}) collective-permute-start(bf16[256,512]{1,0:T(8,128)(2,1)} %collective-permute-done.7.refs_0_), channel_id=1, source_target_pairs={{0,4},{4,8},{8,12},{12,14},{14,10},{10,6},{6,2},{2,0},{1,5},{5,9},... | collective-permute-start | bytes 786440 | tf_op jit(solution)/shard_map/ppermute | solution.py:140
  56.6 13.2 %collective-permute-start.27 = (bf16[256,512]{1,0:T(8,128)(2,1)}, bf16[256,512]{1,0:T(8,128)(2,1)}, u32[]{:S(2)}, u32[]{:S(2)}) collective-permute-start(bf16[256,512]{1,0:T(8,128)(2,1)} %collective-permute-done.19.refs_3_), channel_id=1, source_target_pairs={{4,0},{8,4},{12,8},{14,12},{10,14},{6,10},{2,6},{0,2},{5,1},{9,5},... | collective-permute-start | bytes 786440 | tf_op jit(solution)/shard_map/ppermute | solution.py:140
  62.2 11.2 %collective-permute-start.24 = (bf16[256,512]{1,0:T(8,128)(2,1)}, bf16[256,512]{1,0:T(8,128)(2,1)}, u32[]{:S(2)}, u32[]{:S(2)}) collective-permute-start(bf16[256,512]{1,0:T(8,128)(2,1)} %collective-permute-done.18.refs_2_), channel_id=1, source_target_pairs={{4,0},{8,4},{12,8},{14,12},{10,14},{6,10},{2,6},{0,2},{5,1},{9,5},... | collective-permute-start | bytes 786440 | tf_op jit(solution)/shard_map/ppermute | solution.py:140
  63.0 11.2 %collective-permute-start.21 = (bf16[256,512]{1,0:T(8,128)(2,1)}, bf16[256,512]{1,0:T(8,128)(2,1)}, u32[]{:S(2)}, u32[]{:S(2)}) collective-permute-start(bf16[256,512]{1,0:T(8,128)(2,1)} %collective-permute-done.17.refs_1_), channel_id=1, source_target_pairs={{0,4},{4,8},{8,12},{12,14},{14,10},{10,6},{6,2},{2,0},{1,5},{5,9},... | collective-permute-start | bytes 786440 | tf_op jit(solution)/shard_map/ppermute | solution.py:140
  64.3 11.2 %collective-permute-start.12 = (bf16[256,512]{1,0:T(8,128)(2,1)}, bf16[256,512]{1,0:T(8,128)(2,1)}, u32[]{:S(2)}, u32[]{:S(2)}) collective-permute-start(bf16[256,512]{1,0:T(8,128)(2,1)} %collective-permute-done.8.refs_0_), channel_id=1, source_target_pairs={{0,4},{4,8},{8,12},{12,14},{14,10},{10,6},{6,2},{2,0},{1,5},{5,9},... | collective-permute-start | bytes 786440 | tf_op jit(solution)/shard_map/ppermute | solution.py:140
  65.9 11.2 %copy-start.9 = (s32[4]{0:T(128)S(1)}, s32[4]{0:T(128)}, u32[]{:S(2)}) copy-start(s32[4]{0:T(128)} %param.13) | copy-start | bytes 52
  69.8 11.4 %collective-permute-start.28 = (bf16[256,512]{1,0:T(8,128)(2,1)}, bf16[256,512]{1,0:T(8,128)(2,1)}, u32[]{:S(2)}, u32[]{:S(2)}) collective-permute-start(bf16[256,512]{1,0:T(8,128)(2,1)} %collective-permute-done.27.refs_3_), channel_id=1, source_target_pairs={{4,0},{8,4},{12,8},{14,12},{10,14},{6,10},{2,6},{0,2},{5,1},{9,5},... | collective-permute-start | bytes 786440 | tf_op jit(solution)/shard_map/ppermute | solution.py:140
  73.5 11.6 %collective-permute-start.25 = (bf16[256,512]{1,0:T(8,128)(2,1)}, bf16[256,512]{1,0:T(8,128)(2,1)}, u32[]{:S(2)}, u32[]{:S(2)}) collective-permute-start(bf16[256,512]{1,0:T(8,128)(2,1)} %collective-permute-done.24.refs_2_), channel_id=1, source_target_pairs={{4,0},{8,4},{12,8},{14,12},{10,14},{6,10},{2,6},{0,2},{5,1},{9,5},... | collective-permute-start | bytes 786440 | tf_op jit(solution)/shard_map/ppermute | solution.py:140
  74.3 11.3 %collective-permute-start.22 = (bf16[256,512]{1,0:T(8,128)(2,1)}, bf16[256,512]{1,0:T(8,128)(2,1)}, u32[]{:S(2)}, u32[]{:S(2)}) collective-permute-start(bf16[256,512]{1,0:T(8,128)(2,1)} %collective-permute-done.21.refs_1_), channel_id=1, source_target_pairs={{0,4},{4,8},{8,12},{12,14},{14,10},{10,6},{6,2},{2,0},{1,5},{5,9},... | collective-permute-start | bytes 786440 | tf_op jit(solution)/shard_map/ppermute | solution.py:140
  75.5 11.6 %collective-permute-start.16 = (bf16[256,512]{1,0:T(8,128)(2,1)}, bf16[256,512]{1,0:T(8,128)(2,1)}, u32[]{:S(2)}, u32[]{:S(2)}) collective-permute-start(bf16[256,512]{1,0:T(8,128)(2,1)} %collective-permute-done.12.refs_0_), channel_id=1, source_target_pairs={{0,4},{4,8},{8,12},{12,14},{14,10},{10,6},{6,2},{2,0},{1,5},{5,9},... | collective-permute-start | bytes 786440 | tf_op jit(solution)/shard_map/ppermute | solution.py:140
  81.2 14.9 %collective-permute-start.29 = (bf16[256,512]{1,0:T(8,128)(2,1)}, bf16[256,512]{1,0:T(8,128)(2,1)S(1)}, u32[]{:S(2)}, u32[]{:S(2)}) collective-permute-start(bf16[256,512]{1,0:T(8,128)(2,1)} %collective-permute-done.28.refs_3_), channel_id=1, source_target_pairs={{4,0},{8,4},{12,8},{14,12},{10,14},{6,10},{2,6},{0,2},{5,1},{9,5},... | collective-permute-start | bytes 786440 | tf_op jit(solution)/shard_map/ppermute | solution.py:140
  85.1 11.1 %collective-permute-start.26 = (bf16[256,512]{1,0:T(8,128)(2,1)}, bf16[256,512]{1,0:T(8,128)(2,1)S(1)}, u32[]{:S(2)}, u32[]{:S(2)}) collective-permute-start(bf16[256,512]{1,0:T(8,128)(2,1)} %collective-permute-done.25.refs_2_), channel_id=1, source_target_pairs={{4,0},{8,4},{12,8},{14,12},{10,14},{6,10},{2,6},{0,2},{5,1},{9,5},... | collective-permute-start | bytes 786440 | tf_op jit(solution)/shard_map/ppermute | solution.py:140
  85.6 10.6 %collective-permute-start.23 = (bf16[256,512]{1,0:T(8,128)(2,1)}, bf16[256,512]{1,0:T(8,128)(2,1)S(1)}, u32[]{:S(2)}, u32[]{:S(2)}) collective-permute-start(bf16[256,512]{1,0:T(8,128)(2,1)} %collective-permute-done.22.refs_1_), channel_id=1, source_target_pairs={{0,4},{4,8},{8,12},{12,14},{14,10},{10,6},{6,2},{2,0},{1,5},{5,9},... | collective-permute-start | bytes 786440 | tf_op jit(solution)/shard_map/ppermute | solution.py:140
  87.1 9.1 %collective-permute-start.20 = (bf16[256,512]{1,0:T(8,128)(2,1)}, bf16[256,512]{1,0:T(8,128)(2,1)S(1)}, u32[]{:S(2)}, u32[]{:S(2)}) collective-permute-start(bf16[256,512]{1,0:T(8,128)(2,1)} %collective-permute-done.16.refs_0_), channel_id=1, source_target_pairs={{0,4},{4,8},{8,12},{12,14},{14,10},{10,6},{6,2},{2,0},{1,5},{5,9},... | collective-permute-start | bytes 786440 | tf_op jit(solution)/shard_map/ppermute | solution.py:140
  100.4 2.9 %collective-permute-start.30 = (bf16[1024,512]{1,0:T(8,128)(2,1)}, bf16[1024,512]{1,0:T(8,128)(2,1)S(1)}, u32[]{:S(2)}, u32[]{:S(2)}) collective-permute-start(bf16[1024,512]{1,0:T(8,128)(2,1)} %get-tuple-element.80.have_ref), channel_id=1, source_target_pairs={{0,1},{1,0},{2,3},{3,2},{4,5},{5,4},{6,7},{7,6},{8,9},{9,8},{10,11... | collective-permute-start | bytes 3145736 | tf_op jit(solution)/shard_map/ppermute | solution.py:259
  108.0 13.9 %all-to-all-start = ((f32[8,72,128]{2,1,0:T(8,128)}), f32[8,72,128]{2,1,0:T(8,128)S(1)}, u32[]{:S(2)}, u32[]{:S(2)}) async-start(f32[8,72,128]{2,1,0:T(8,128)} %bitcast.25), calls=%async_computation | async-start | bytes 589824 | tf_op jit(solution)/shard_map/all_to_all | solution.py:286
  122.3 3.8 %collective-permute-start.31 = (bf16[64,128]{1,0:T(8,128)(2,1)S(1)}, bf16[64,128]{1,0:T(8,128)(2,1)S(1)}, u32[]{:S(2)}, u32[]{:S(2)}) collective-permute-start(bf16[64,128]{1,0:T(8,128)(2,1)S(1)} %shard_map.90), channel_id=1, source_target_pairs={{0,2},{2,0},{4,6},{6,4},{8,10},{10,8},{12,14},{14,12},{1,3},{3,1},... | collective-permute-start | bytes 49160 | tf_op jit(solution)/shard_map/ppermute | solution.py:290
  126.1 5.8 %collective-permute-start.32 = (bf16[128,128]{1,0:T(8,128)(2,1)S(1)}, bf16[128,128]{1,0:T(8,128)(2,1)S(1)}, u32[]{:S(2)}, u32[]{:S(2)}) collective-permute-start(bf16[128,128]{1,0:T(8,128)(2,1)S(1)} %pad_maximum_fusion.2), channel_id=1, source_target_pairs={{0,12},{2,14},{4,8},{6,10},{8,4},{10,6},{12,0},{14,2},{1,13},{3,15... | collective-permute-start | bytes 98312 | tf_op jit(solution)/shard_map/ppermute | solution.py:293
  127.3 5.3 %collective-permute-start.33 = (bf16[128,128]{1,0:T(8,128)(2,1)S(1)}, bf16[128,128]{1,0:T(8,128)(2,1)S(1)}, u32[]{:S(2)}, u32[]{:S(2)}) collective-permute-start(bf16[128,128]{1,0:T(8,128)(2,1)S(1)} %pad_maximum_fusion.2), channel_id=1, source_target_pairs={{0,8},{2,10},{4,12},{6,14},{8,0},{10,2},{12,4},{14,6},{1,9},{3,11}... | collective-permute-start | bytes 98312 | tf_op jit(solution)/shard_map/ppermute | solution.py:293
  128.7 4.2 %collective-permute-start.34 = (bf16[128,128]{1,0:T(8,128)(2,1)S(1)}, bf16[128,128]{1,0:T(8,128)(2,1)S(1)}, u32[]{:S(2)}, u32[]{:S(2)}) collective-permute-start(bf16[128,128]{1,0:T(8,128)(2,1)S(1)} %pad_maximum_fusion.2), channel_id=1, source_target_pairs={{0,4},{2,6},{4,0},{6,2},{8,12},{10,14},{12,8},{14,10},{1,5},{3,7},... | collective-permute-start | bytes 98312 | tf_op jit(solution)/shard_map/ppermute | solution.py:293
  133.0 1.4 %collective-permute-start.35 = (bf16[16,1,4096]{2,0,1:T(8,128)(2,1)S(1)}, bf16[16,1,4096]{2,0,1:T(8,128)(2,1)S(1)}, u32[]{:S(2)}, u32[]{:S(2)}) collective-permute-start(bf16[16,1,4096]{2,0,1:T(8,128)(2,1)S(1)} %reshape.97), channel_id=1, source_target_pairs={{0,1},{1,0},{2,3},{3,2},{4,5},{5,4},{6,7},{7,6},{8,9},{9,8},{10,11... | collective-permute-start | bytes 393224 | tf_op jit(solution)/shard_map/ppermute | solution.py:303

commit v15 on v14

--- a/solution.py
+++ b/solution.py
@@ -65,6 +65,8 @@
             out_ref[rows, :] = term.astype(out_ref.dtype)
 
     tokens = pltpu.with_memory_space_constraint(tokens, pltpu.HBM)
+    if total is None:
+        flat = flat[:2] + [pltpu.with_memory_space_constraint(x, pltpu.HBM) for x in flat[2:]]
     in_vmem = pl.BlockSpec(memory_space=pltpu.VMEM)
     in_any = pl.BlockSpec(memory_space=pl.ANY)
     sums = [] if total is None else [total]

time: 136 us -> 134 us (0.985)
  local copies, waits for them, and re-layouts: 11.1 us -> 4.49 us
  waiting for transfers between devices: 46.4 us -> 49 us
    unnamed x20 -> x12, local copies, waits for them, and re-layouts: 6.61 us -> 0.02 us
    ppermute x28, waiting for transfers between devices: 31.1 us -> 33.7 us  [project(): held[k] = lax.ppermute(held[k], 'chip', ways[k])]
  transfers between devices with their start and end apart: 37 -> 37, of which waited for: 17 -> 20; matrix products, arithmetic and copies ran while one was open for 4% -> 4% of each run, Pallas kernels for 18% -> 19%
where the time goes in v15:
time: 134 us
  waiting for transfers between devices  49 us (37%)
  starting transfers between devices  41.6 us (31%)
  Pallas kernels  34.4 us (26%)
  local copies, waits for them, and re-layouts  4.49 us (3%)
  other arithmetic  2.42 us (2%)
  matrix products  1.36 us (1%)
    ppermute x28, waiting for transfers between devices, project(): held[k] = lax.ppermute(held[k], 'chip', ways[k])  33.7 us
    ppermute x28, starting transfers between devices, project(): held[k] = lax.ppermute(held[k], 'chip', ways[k])  30.7 us
    pallas_call x7, Pallas kernels, add_pieces(): pl.pallas_call(kernel, out_shape=(jax.ShapeDtypeStruct((2 * tok_rows, wid...  29.3 us
    all_to_all x1, waiting for transfers between devices, on_device(): lax.all_to_all(flat, 'chip', split_axis=0, concat_axis=0, tiled=True)  8.6 us
    pallas_call x1, Pallas kernels, attend(): pl.pallas_call(kernel, out_shape=jax.ShapeDtypeStruct((chips, blocks + 1,...  4.67 us
    ppermute x3, starting transfers between devices, on_device(): lax.ppermute(couple, 'chip', [(c, c ^ 2 * d) for c in range(chips)])  4.45 us
    all_to_all x1, starting transfers between devices, on_device(): lax.all_to_all(flat, 'chip', split_axis=0, concat_axis=0, tiled=True)  4.31 us
  transfers between devices with their start and end apart: 37, of which 20 were waited for; matrix products, arithmetic and copies ran while one was open for 4% of the time, Pallas kernels for 19%

profile of v15, /device:TPU:0, one launch (start us, length us, event | category | flops | bytes accessed | tf_op | source)
XLA Modules:
  0.0 133.6 jit_solution(948308597741320827)
XLA Ops:
  0.0 1.3 broadcast_select_fusion
  1.3 0.5 collective-permute-start.2
  1.9 2.6 %collective-permute-start = (bf16[256,512]{1,0:T(8,128)(2,1)S(1)}, bf16[256,512]{1,0:T(8,128)(2,1)S(1)}, u32[]{:S(2)}, u32[]{:S(2)}) collective-permute-start(bf16[256,512]{1,0:T(8,128)(2,1)S(1)} %get-tuple-element.90), channel_id=1, source_target_pairs={{0,4},{4,8},{8,12},{12,14},{14,10},{10,6},{6,2},{2,0},{1,5},{5,9},... | collective-permute-start | bytes 786440 | tf_op jit(solution)/shard_map/ppermute | solution.py:142
  4.5 1.6 %collective-permute-start.1 = (bf16[256,512]{1,0:T(8,128)(2,1)S(1)}, bf16[256,512]{1,0:T(8,128)(2,1)S(1)}, u32[]{:S(2)}, u32[]{:S(2)}) collective-permute-start(bf16[256,512]{1,0:T(8,128)(2,1)S(1)} %get-tuple-element.89), channel_id=1, source_target_pairs={{0,4},{4,8},{8,12},{12,14},{14,10},{10,6},{6,2},{2,0},{1,5},{5,9},... | collective-permute-start | bytes 786440 | tf_op jit(solution)/shard_map/ppermute | solution.py:142
  6.1 0.5 collective-permute-start.3
  6.6 1.3 collective-permute-start.4
  7.9 3.7 %collective-permute-done.refs_2_ = bf16[256,512]{1,0:T(8,128)(2,1)S(1)} collective-permute-done((bf16[256,512]{1,0:T(8,128)(2,1)S(1)}, bf16[256,512]{1,0:T(8,128)(2,1)S(1)}, u32[]{:S(2)}, u32[]{:S(2)}) %collective-permute-start) | collective-permute-done | bytes 262176 | tf_op jit(solution)/shard_map/ppermute | solution.py:142
  11.6 5.4 %collective-permute-done.1.refs_3_ = bf16[256,512]{1,0:T(8,128)(2,1)S(1)} collective-permute-done((bf16[256,512]{1,0:T(8,128)(2,1)S(1)}, bf16[256,512]{1,0:T(8,128)(2,1)S(1)}, u32[]{:S(2)}, u32[]{:S(2)}) %collective-permute-start.1) | collective-permute-done | bytes 262176 | tf_op jit(solution)/shard_map/ppermute | solution.py:142
  17.1 2.9 %collective-permute-done.4.refs_5_ = bf16[256,512]{1,0:T(8,128)(2,1)S(1)} collective-permute-done((bf16[256,512]{1,0:T(8,128)(2,1)S(1)}, bf16[256,512]{1,0:T(8,128)(2,1)S(1)}, u32[]{:S(2)}, u32[]{:S(2)}) %collective-permute-start.4) | collective-permute-done | bytes 262176 | tf_op jit(solution)/shard_map/ppermute | solution.py:142
  20.0 0.4 collective-permute-start.11
  20.4 1.5 %collective-permute-start.10 = (bf16[256,512]{1,0:T(8,128)(2,1)S(1)}, bf16[256,512]{1,0:T(8,128)(2,1)}, u32[]{:S(2)}, u32[]{:S(2)}) collective-permute-start(bf16[256,512]{1,0:T(8,128)(2,1)S(1)} %collective-permute-done.3.refs_4_), channel_id=1, source_target_pairs={{4,0},{8,4},{12,8},{14,12},{10,14},{6,10},{2,6},{0,2},{5,1},{9,5},... | collective-permute-start | bytes 786440 | tf_op jit(solution)/shard_map/ppermute | solution.py:142
  21.9 0.5 collective-permute-start.9
  22.4 1.6 %collective-permute-start.6 = (bf16[256,512]{1,0:T(8,128)(2,1)S(1)}, bf16[256,512]{1,0:T(8,128)(2,1)}, u32[]{:S(2)}, u32[]{:S(2)}) collective-permute-start(bf16[256,512]{1,0:T(8,128)(2,1)S(1)} %collective-permute-done.refs_2_), channel_id=1, source_target_pairs={{0,4},{4,8},{8,12},{12,14},{14,10},{10,6},{6,2},{2,0},{1,5},{5,9},... | collective-permute-start | bytes 786440 | tf_op jit(solution)/shard_map/ppermute | solution.py:142
  24.1 5.1 %collective-permute-done.11.refs_3_ = bf16[256,512]{1,0:T(8,128)(2,1)} collective-permute-done((bf16[256,512]{1,0:T(8,128)(2,1)S(1)}, bf16[256,512]{1,0:T(8,128)(2,1)}, u32[]{:S(2)}, u32[]{:S(2)}) %collective-permute-start.11) | collective-permute-done | bytes 262176 | tf_op jit(solution)/shard_map/ppermute | solution.py:142
  29.2 0.4 collective-permute-start.15
  29.6 5.2 %collective-permute-done.10.refs_2_ = bf16[256,512]{1,0:T(8,128)(2,1)} collective-permute-done((bf16[256,512]{1,0:T(8,128)(2,1)S(1)}, bf16[256,512]{1,0:T(8,128)(2,1)}, u32[]{:S(2)}, u32[]{:S(2)}) %collective-permute-start.10) | collective-permute-done | bytes 262176 | tf_op jit(solution)/shard_map/ppermute | solution.py:142
  34.8 0.4 collective-permute-start.14
  35.2 1.6 %collective-permute-start.13 = (bf16[256,512]{1,0:T(8,128)(2,1)}, bf16[256,512]{1,0:T(8,128)(2,1)}, u32[]{:S(2)}, u32[]{:S(2)}) collective-permute-start(bf16[256,512]{1,0:T(8,128)(2,1)} %collective-permute-done.9.refs_1_), channel_id=1, source_target_pairs={{0,4},{4,8},{8,12},{12,14},{14,10},{10,6},{6,2},{2,0},{1,5},{5,9},... | collective-permute-start | bytes 786440 | tf_op jit(solution)/shard_map/ppermute | solution.py:142
  36.8 1.6 %collective-permute-start.7 = (bf16[256,512]{1,0:T(8,128)(2,1)}, bf16[256,512]{1,0:T(8,128)(2,1)}, u32[]{:S(2)}, u32[]{:S(2)}) collective-permute-start(bf16[256,512]{1,0:T(8,128)(2,1)} %collective-permute-done.6.refs_0_), channel_id=1, source_target_pairs={{0,4},{4,8},{8,12},{12,14},{14,10},{10,6},{6,2},{2,0},{1,5},{5,9},... | collective-permute-start | bytes 786440 | tf_op jit(solution)/shard_map/ppermute | solution.py:142
  38.5 5.7 %shard_map.82 = (f32[1024,512]{1,0:T(8,128)S(1)}, f32[8,128]{1,0:T(8,128)}) custom-call(s32[4]{0:T(128)S(1)} %pad_add_fusion.1.places_ref, bf16[512,8192]{1,0:T(8,128)(2,1)} %mine_ref.13, bf16[512,8192]{1,0:T(8,128)(2,1)} %collective-permute-done.5.theirs_ref, bf16[512,512]{1,0:T(8,128)(2,1)S(1)} %get-tuple-element.86.refs_0_, ...), custom_call_target="tpu_custom_call" | custom-call | flops 2147483648 | bytes 4194304 | tf_op jit(solution)/shard_map/pallas_call | solution.py:73
  44.2 0.5 collective-permute-start.19
  44.7 0.9 collective-permute-done.14.refs_2_
  45.6 0.4 collective-permute-start.18
  46.1 1.6 %collective-permute-start.17 = (bf16[256,512]{1,0:T(8,128)(2,1)}, bf16[256,512]{1,0:T(8,128)(2,1)}, u32[]{:S(2)}, u32[]{:S(2)}) collective-permute-start(bf16[256,512]{1,0:T(8,128)(2,1)} %collective-permute-done.13.refs_1_), channel_id=1, source_target_pairs={{0,4},{4,8},{8,12},{12,14},{14,10},{10,6},{6,2},{2,0},{1,5},{5,9},... | collective-permute-start | bytes 786440 | tf_op jit(solution)/shard_map/ppermute | solution.py:142
  47.7 0.8 collective-permute-done.7.refs_0_
  48.4 1.6 %collective-permute-start.8 = (bf16[256,512]{1,0:T(8,128)(2,1)}, bf16[256,512]{1,0:T(8,128)(2,1)}, u32[]{:S(2)}, u32[]{:S(2)}) collective-permute-start(bf16[256,512]{1,0:T(8,128)(2,1)} %collective-permute-done.7.refs_0_), channel_id=1, source_target_pairs={{0,4},{4,8},{8,12},{12,14},{14,10},{10,6},{6,2},{2,0},{1,5},{5,9},... | collective-permute-start | bytes 786440 | tf_op jit(solution)/shard_map/ppermute | solution.py:142
  50.2 1.3 constant_dynamic-slice_fusion.1
  51.5 3.9 %shard_map.83 = (f32[1024,512]{1,0:T(8,128)S(1)}, f32[8,128]{1,0:T(8,128)}) custom-call(s32[2]{0:T(128)S(1)} %pad_add_fusion.2.places_ref, bf16[512,8192]{1,0:T(8,128)(2,1)} %mine_ref.13, bf16[512,8192]{1,0:T(8,128)(2,1)} %collective-permute-done.5.theirs_ref, bf16[256,512]{1,0:T(8,128)(2,1)} %collective-permute-done.6.refs_0_, ...), custom_call_target="tpu_custom_call", output_to_operand_aliasing={{0}: (7, {})} | custom-call | flops 1073741824 | bytes 2097152 | tf_op jit(solution)/shard_map/pallas_call | solution.py:73
  55.4 0.6 collective-permute-start.27
  56.0 1.2 collective-permute-done.18.refs_2_
  57.2 0.4 collective-permute-start.24
  57.6 1.6 %collective-permute-start.21 = (bf16[256,512]{1,0:T(8,128)(2,1)}, bf16[256,512]{1,0:T(8,128)(2,1)}, u32[]{:S(2)}, u32[]{:S(2)}) collective-permute-start(bf16[256,512]{1,0:T(8,128)(2,1)} %collective-permute-done.17.refs_1_), channel_id=1, source_target_pairs={{0,4},{4,8},{8,12},{12,14},{14,10},{10,6},{6,2},{2,0},{1,5},{5,9},... | collective-permute-start | bytes 786440 | tf_op jit(solution)/shard_map/ppermute | solution.py:142
  59.3 1.8 %collective-permute-done.8.refs_0_ = bf16[256,512]{1,0:T(8,128)(2,1)} collective-permute-done((bf16[256,512]{1,0:T(8,128)(2,1)}, bf16[256,512]{1,0:T(8,128)(2,1)}, u32[]{:S(2)}, u32[]{:S(2)}) %collective-permute-start.8) | collective-permute-done | bytes 262176 | tf_op jit(solution)/shard_map/ppermute | solution.py:142
  61.1 1.8 %collective-permute-start.12 = (bf16[256,512]{1,0:T(8,128)(2,1)}, bf16[256,512]{1,0:T(8,128)(2,1)}, u32[]{:S(2)}, u32[]{:S(2)}) collective-permute-start(bf16[256,512]{1,0:T(8,128)(2,1)} %collective-permute-done.8.refs_0_), channel_id=1, source_target_pairs={{0,4},{4,8},{8,12},{12,14},{14,10},{10,6},{6,2},{2,0},{1,5},{5,9},... | collective-permute-start | bytes 786440 | tf_op jit(solution)/shard_map/ppermute | solution.py:142
  63.0 3.9 %shard_map.84 = (f32[1024,512]{1,0:T(8,128)S(1)}, f32[8,128]{1,0:T(8,128)}) custom-call(s32[2]{0:T(128)S(1)} %pad_add_fusion.3.places_ref, bf16[512,8192]{1,0:T(8,128)(2,1)} %mine_ref.13, bf16[512,8192]{1,0:T(8,128)(2,1)} %collective-permute-done.5.theirs_ref, bf16[256,512]{1,0:T(8,128)(2,1)} %collective-permute-done.7.refs_0_, ...), custom_call_target="tpu_custom_call", output_to_operand_aliasing={{0}: (7, {})} | custom-call | flops 1073741824 | bytes 2097152 | tf_op jit(solution)/shard_map/pallas_call | solution.py:73
  67.2 2.5 %collective-permute-done.24.refs_2_ = bf16[256,512]{1,0:T(8,128)(2,1)} collective-permute-done((bf16[256,512]{1,0:T(8,128)(2,1)}, bf16[256,512]{1,0:T(8,128)(2,1)}, u32[]{:S(2)}, u32[]{:S(2)}) %collective-permute-start.24) | collective-permute-done | bytes 262176 | tf_op jit(solution)/shard_map/ppermute | solution.py:142
  69.7 0.4 collective-permute-start.25
  70.1 1.6 %collective-permute-start.22 = (bf16[256,512]{1,0:T(8,128)(2,1)}, bf16[256,512]{1,0:T(8,128)(2,1)}, u32[]{:S(2)}, u32[]{:S(2)}) collective-permute-start(bf16[256,512]{1,0:T(8,128)(2,1)} %collective-permute-done.21.refs_1_), channel_id=1, source_target_pairs={{0,4},{4,8},{8,12},{12,14},{14,10},{10,6},{6,2},{2,0},{1,5},{5,9},... | collective-permute-start | bytes 786440 | tf_op jit(solution)/shard_map/ppermute | solution.py:142
  71.7 1.1 collective-permute-done.12.refs_0_
  72.8 1.6 %collective-permute-start.16 = (bf16[256,512]{1,0:T(8,128)(2,1)}, bf16[256,512]{1,0:T(8,128)(2,1)}, u32[]{:S(2)}, u32[]{:S(2)}) collective-permute-start(bf16[256,512]{1,0:T(8,128)(2,1)} %collective-permute-done.12.refs_0_), channel_id=1, source_target_pairs={{0,4},{4,8},{8,12},{12,14},{14,10},{10,6},{6,2},{2,0},{1,5},{5,9},... | collective-permute-start | bytes 786440 | tf_op jit(solution)/shard_map/ppermute | solution.py:142
  74.8 3.9 %shard_map.85 = (f32[1024,512]{1,0:T(8,128)S(1)}, f32[8,128]{1,0:T(8,128)}) custom-call(s32[2]{0:T(128)S(1)} %pad_add_fusion.4.places_ref, bf16[512,8192]{1,0:T(8,128)(2,1)} %mine_ref.13, bf16[512,8192]{1,0:T(8,128)(2,1)} %collective-permute-done.5.theirs_ref, bf16[256,512]{1,0:T(8,128)(2,1)} %collective-permute-done.8.refs_0_, ...), custom_call_target="tpu_custom_call", output_to_operand_aliasing={{0}: (7, {})} | custom-call | flops 1073741824 | bytes 2097152 | tf_op jit(solution)/shard_map/pallas_call | solution.py:73
  78.7 0.4 collective-permute-start.29
  79.1 2.0 %collective-permute-done.25.refs_2_ = bf16[256,512]{1,0:T(8,128)(2,1)} collective-permute-done((bf16[256,512]{1,0:T(8,128)(2,1)}, bf16[256,512]{1,0:T(8,128)(2,1)}, u32[]{:S(2)}, u32[]{:S(2)}) %collective-permute-start.25) | collective-permute-done | bytes 262176 | tf_op jit(solution)/shard_map/ppermute | solution.py:142
  81.5 1.6 %collective-permute-start.23 = (bf16[256,512]{1,0:T(8,128)(2,1)}, bf16[256,512]{1,0:T(8,128)(2,1)S(1)}, u32[]{:S(2)}, u32[]{:S(2)}) collective-permute-start(bf16[256,512]{1,0:T(8,128)(2,1)} %collective-permute-done.22.refs_1_), channel_id=1, source_target_pairs={{0,4},{4,8},{8,12},{12,14},{14,10},{10,6},{6,2},{2,0},{1,5},{5,9},... | collective-permute-start | bytes 786440 | tf_op jit(solution)/shard_map/ppermute | solution.py:142
  83.1 1.1 collective-permute-done.16.refs_0_
  84.2 1.6 %collective-permute-start.20 = (bf16[256,512]{1,0:T(8,128)(2,1)}, bf16[256,512]{1,0:T(8,128)(2,1)S(1)}, u32[]{:S(2)}, u32[]{:S(2)}) collective-permute-start(bf16[256,512]{1,0:T(8,128)(2,1)} %collective-permute-done.16.refs_0_), channel_id=1, source_target_pairs={{0,4},{4,8},{8,12},{12,14},{14,10},{10,6},{6,2},{2,0},{1,5},{5,9},... | collective-permute-start | bytes 786440 | tf_op jit(solution)/shard_map/ppermute | solution.py:142
  86.0 3.9 %shard_map.86 = (f32[1024,512]{1,0:T(8,128)S(1)}, f32[8,128]{1,0:T(8,128)}) custom-call(s32[2]{0:T(128)S(1)} %pad_add_fusion.6.places_ref, bf16[512,8192]{1,0:T(8,128)(2,1)} %mine_ref.13, bf16[512,8192]{1,0:T(8,128)(2,1)} %collective-permute-done.5.theirs_ref, bf16[256,512]{1,0:T(8,128)(2,1)} %collective-permute-done.12.refs_0_, ...), custom_call_target="tpu_custom_call", output_to_operand_aliasing={{0}: (7, {})} | custom-call | flops 1073741824 | bytes 2097152 | tf_op jit(solution)/shard_map/pallas_call | solution.py:73
  89.8 3.9 %shard_map.87 = (f32[1024,512]{1,0:T(8,128)S(1)}, f32[8,128]{1,0:T(8,128)}) custom-call(s32[2]{0:T(128)S(1)} %pad_add_fusion.5.places_ref, bf16[512,8192]{1,0:T(8,128)(2,1)} %mine_ref.13, bf16[512,8192]{1,0:T(8,128)(2,1)} %collective-permute-done.5.theirs_ref, bf16[256,512]{1,0:T(8,128)(2,1)} %collective-permute-done.16.refs_0_, ...), custom_call_target="tpu_custom_call", output_to_operand_aliasing={{0}: (7, {})} | custom-call | flops 1073741824 | bytes 2097152 | tf_op jit(solution)/shard_map/pallas_call | solution.py:73
  93.8 4.2 %shard_map.88 = (bf16[1024,512]{1,0:T(8,128)(2,1)}, f32[8,128]{1,0:T(8,128)}) custom-call(s32[4]{0:T(128)S(1)} %pad_add_fusion.places_ref, bf16[512,8192]{1,0:T(8,128)(2,1)} %mine_ref.13, bf16[512,8192]{1,0:T(8,128)(2,1)} %collective-permute-done.5.theirs_ref, bf16[256,512]{1,0:T(8,128)(2,1)S(1)} %collective-permute-done.20.refs_0_, ...), custom_call_target="tpu_custom_call" | custom-call | flops 1073741824 | bytes 2097152 | tf_op jit(solution)/shard_map/pallas_call | solution.py:73
  98.3 0.8 reshape.89
  99.5 0.7 fusion.17
  100.2 0.7 collective-permute-done.30.got_ref
  100.9 4.7 %shard_map.89 = f32[8,9,8,128]{3,2,1,0:T(8,128)} custom-call(s32[1]{0:T(128)} %bitcast.core_ref, bf16[1024,512]{1,0:T(8,128)(2,1)} %get-tuple-element.80.have_ref, bf16[1024,512]{1,0:T(8,128)(2,1)S(1)} %collective-permute-done.30.got_ref, bf16[512,512]{1,0:T(8,128)(2,1)S(1)} %get-tuple-element.81.key_up_ref, ...), custom_call_target="tpu_custom_call" | custom-call | flops 1342177280 | bytes 2097152 | tf_op jit(solution)/shard_map/pallas_call | solution.py:194
  105.6 4.3 %all-to-all-start = ((f32[8,72,128]{2,1,0:T(8,128)}), f32[8,72,128]{2,1,0:T(8,128)S(1)}, u32[]{:S(2)}, u32[]{:S(2)}) async-start(f32[8,72,128]{2,1,0:T(8,128)} %bitcast.25), calls=%async_computation | async-start | bytes 589824 | tf_op jit(solution)/shard_map/all_to_all | solution.py:288
  111.2 8.6 %all-to-all-done = f32[8,72,128]{2,1,0:T(8,128)S(1)} async-done(((f32[8,72,128]{2,1,0:T(8,128)}), f32[8,72,128]{2,1,0:T(8,128)S(1)}, u32[]{:S(2)}, u32[]{:S(2)}) %all-to-all-start) | async-done | bytes 294944 | tf_op jit(solution)/shard_map/all_to_all | solution.py:288
  120.2 1.5 %collective-permute-start.31 = (bf16[64,128]{1,0:T(8,128)(2,1)S(1)}, bf16[64,128]{1,0:T(8,128)(2,1)S(1)}, u32[]{:S(2)}, u32[]{:S(2)}) collective-permute-start(bf16[64,128]{1,0:T(8,128)(2,1)S(1)} %shard_map.90), channel_id=1, source_target_pairs={{0,2},{2,0},{4,6},{6,4},{8,10},{10,8},{12,14},{14,12},{1,3},{3,1},... | collective-permute-start | bytes 49160 | tf_op jit(solution)/shard_map/ppermute | solution.py:292
  121.7 2.3 %collective-permute-done.31 = bf16[64,128]{1,0:T(8,128)(2,1)S(1)} collective-permute-done((bf16[64,128]{1,0:T(8,128)(2,1)S(1)}, bf16[64,128]{1,0:T(8,128)(2,1)S(1)}, u32[]{:S(2)}, u32[]{:S(2)}) %collective-permute-start.31) | collective-permute-done | bytes 16416 | tf_op jit(solution)/shard_map/ppermute | solution.py:292
  124.0 1.2 collective-permute-start.32
  125.2 1.3 %collective-permute-start.33 = (bf16[128,128]{1,0:T(8,128)(2,1)S(1)}, bf16[128,128]{1,0:T(8,128)(2,1)S(1)}, u32[]{:S(2)}, u32[]{:S(2)}) collective-permute-start(bf16[128,128]{1,0:T(8,128)(2,1)S(1)} %pad_maximum_fusion.2), channel_id=1, source_target_pairs={{0,8},{2,10},{4,12},{6,14},{8,0},{10,2},{12,4},{14,6},{1,9},{3,11}... | collective-permute-start | bytes 98312 | tf_op jit(solution)/shard_map/ppermute | solution.py:295
  126.6 1.9 %collective-permute-start.34 = (bf16[128,128]{1,0:T(8,128)(2,1)S(1)}, bf16[128,128]{1,0:T(8,128)(2,1)S(1)}, u32[]{:S(2)}, u32[]{:S(2)}) collective-permute-start(bf16[128,128]{1,0:T(8,128)(2,1)S(1)} %pad_maximum_fusion.2), channel_id=1, source_target_pairs={{0,4},{2,6},{4,0},{6,2},{8,12},{10,14},{12,8},{14,10},{1,5},{3,7},... | collective-permute-start | bytes 98312 | tf_op jit(solution)/shard_map/ppermute | solution.py:295
  128.4 1.3 collective-permute-done.32
  129.8 0.8 collective-permute-done.33
  131.0 1.3 collective-permute-done.35
  132.7 0.9 reshape.98
  (81 shorter events, 4.8 us)
Async XLA Ops:
  0.0 50.0 %copy-start = (bf16[4,4,8192]{2,1,0:T(4,128)(2,1)S(1)}, bf16[4,4,8192]{2,1,0:T(4,128)(2,1)}, u32[]{:S(2)}) copy-start(bf16[4,4,8192]{2,1,0:T(4,128)(2,1)} %param.14) | copy-start | bytes 786436
  1.3 4.8 %collective-permute-start.2 = (bf16[512,512]{1,0:T(8,128)(2,1)S(1)}, bf16[512,512]{1,0:T(8,128)(2,1)S(1)}, u32[]{:S(2)}, u32[]{:S(2)}) collective-permute-start(bf16[512,512]{1,0:T(8,128)(2,1)S(1)} %get-tuple-element.85), channel_id=1, source_target_pairs={{0,1},{1,0},{2,3},{3,2},{4,5},{5,4},{6,7},{7,6},{8,9},{9,8},{10,11... | collective-permute-start | bytes 1572872 | tf_op jit(solution)/shard_map/ppermute | solution.py:103
  1.9 9.7 %collective-permute-start = (bf16[256,512]{1,0:T(8,128)(2,1)S(1)}, bf16[256,512]{1,0:T(8,128)(2,1)S(1)}, u32[]{:S(2)}, u32[]{:S(2)}) collective-permute-start(bf16[256,512]{1,0:T(8,128)(2,1)S(1)} %get-tuple-element.90), channel_id=1, source_target_pairs={{0,4},{4,8},{8,12},{12,14},{14,10},{10,6},{6,2},{2,0},{1,5},{5,9},... | collective-permute-start | bytes 786440 | tf_op jit(solution)/shard_map/ppermute | solution.py:142
  4.5 12.5 %collective-permute-start.1 = (bf16[256,512]{1,0:T(8,128)(2,1)S(1)}, bf16[256,512]{1,0:T(8,128)(2,1)S(1)}, u32[]{:S(2)}, u32[]{:S(2)}) collective-permute-start(bf16[256,512]{1,0:T(8,128)(2,1)S(1)} %get-tuple-element.89), channel_id=1, source_target_pairs={{0,4},{4,8},{8,12},{12,14},{14,10},{10,6},{6,2},{2,0},{1,5},{5,9},... | collective-permute-start | bytes 786440 | tf_op jit(solution)/shard_map/ppermute | solution.py:142
  6.1 10.9 %collective-permute-start.3 = (bf16[256,512]{1,0:T(8,128)(2,1)S(1)}, bf16[256,512]{1,0:T(8,128)(2,1)S(1)}, u32[]{:S(2)}, u32[]{:S(2)}) collective-permute-start(bf16[256,512]{1,0:T(8,128)(2,1)S(1)} %get-tuple-element.88), channel_id=1, source_target_pairs={{4,0},{8,4},{12,8},{14,12},{10,14},{6,10},{2,6},{0,2},{5,1},{9,5},... | collective-permute-start | bytes 786440 | tf_op jit(solution)/shard_map/ppermute | solution.py:142
  6.6 13.3 %collective-permute-start.4 = (bf16[256,512]{1,0:T(8,128)(2,1)S(1)}, bf16[256,512]{1,0:T(8,128)(2,1)S(1)}, u32[]{:S(2)}, u32[]{:S(2)}) collective-permute-start(bf16[256,512]{1,0:T(8,128)(2,1)S(1)} %get-tuple-element.87), channel_id=1, source_target_pairs={{4,0},{8,4},{12,8},{14,12},{10,14},{6,10},{2,6},{0,2},{5,1},{9,5},... | collective-permute-start | bytes 786440 | tf_op jit(solution)/shard_map/ppermute | solution.py:142
  11.6 26.9 %copy-start.1 = (bf16[256,512]{1,0:T(8,128)(2,1)}, bf16[256,512]{1,0:T(8,128)(2,1)S(1)}, u32[]{:S(2)}) copy-start(bf16[256,512]{1,0:T(8,128)(2,1)S(1)} %collective-permute-done.refs_2_) | copy-start | bytes 786436
  17.0 21.4 %copy-start.2 = (bf16[256,512]{1,0:T(8,128)(2,1)}, bf16[256,512]{1,0:T(8,128)(2,1)S(1)}, u32[]{:S(2)}) copy-start(bf16[256,512]{1,0:T(8,128)(2,1)S(1)} %collective-permute-done.1.refs_3_) | copy-start | bytes 786436
  17.0 21.4 %copy-start.3 = (bf16[256,512]{1,0:T(8,128)(2,1)}, bf16[256,512]{1,0:T(8,128)(2,1)S(1)}, u32[]{:S(2)}) copy-start(bf16[256,512]{1,0:T(8,128)(2,1)S(1)} %collective-permute-done.3.refs_4_) | copy-start | bytes 786436
  20.0 18.5 %copy-start.4 = (bf16[256,512]{1,0:T(8,128)(2,1)}, bf16[256,512]{1,0:T(8,128)(2,1)S(1)}, u32[]{:S(2)}) copy-start(bf16[256,512]{1,0:T(8,128)(2,1)S(1)} %collective-permute-done.4.refs_5_) | copy-start | bytes 786436
  20.0 18.5 %collective-permute-start.5 = (bf16[512,8192]{1,0:T(8,128)(2,1)}, bf16[512,8192]{1,0:T(8,128)(2,1)}, u32[]{:S(2)}, u32[]{:S(2)}) collective-permute-start(bf16[512,8192]{1,0:T(8,128)(2,1)} %mine_ref.13), channel_id=1, source_target_pairs={{0,1},{1,0},{2,3},{3,2},{4,5},{5,4},{6,7},{7,6},{8,9},{9,8},{10,11... | collective-permute-start | bytes 25165832 | tf_op jit(solution)/shard_map/ppermute | solution.py:133
  20.0 9.2 %collective-permute-start.11 = (bf16[256,512]{1,0:T(8,128)(2,1)S(1)}, bf16[256,512]{1,0:T(8,128)(2,1)}, u32[]{:S(2)}, u32[]{:S(2)}) collective-permute-start(bf16[256,512]{1,0:T(8,128)(2,1)S(1)} %collective-permute-done.4.refs_5_), channel_id=1, source_target_pairs={{4,0},{8,4},{12,8},{14,12},{10,14},{6,10},{2,6},{0,2},{5,1},{9,5},... | collective-permute-start | bytes 786440 | tf_op jit(solution)/shard_map/ppermute | solution.py:142
  20.4 14.4 %collective-permute-start.10 = (bf16[256,512]{1,0:T(8,128)(2,1)S(1)}, bf16[256,512]{1,0:T(8,128)(2,1)}, u32[]{:S(2)}, u32[]{:S(2)}) collective-permute-start(bf16[256,512]{1,0:T(8,128)(2,1)S(1)} %collective-permute-done.3.refs_4_), channel_id=1, source_target_pairs={{4,0},{8,4},{12,8},{14,12},{10,14},{6,10},{2,6},{0,2},{5,1},{9,5},... | collective-permute-start | bytes 786440 | tf_op jit(solution)/shard_map/ppermute | solution.py:142
  21.9 13.3 %collective-permute-start.9 = (bf16[256,512]{1,0:T(8,128)(2,1)S(1)}, bf16[256,512]{1,0:T(8,128)(2,1)}, u32[]{:S(2)}, u32[]{:S(2)}) collective-permute-start(bf16[256,512]{1,0:T(8,128)(2,1)S(1)} %collective-permute-done.1.refs_3_), channel_id=1, source_target_pairs={{0,4},{4,8},{8,12},{12,14},{14,10},{10,6},{6,2},{2,0},{1,5},{5,9},... | collective-permute-start | bytes 786440 | tf_op jit(solution)/shard_map/ppermute | solution.py:142
  22.4 14.4 %collective-permute-start.6 = (bf16[256,512]{1,0:T(8,128)(2,1)S(1)}, bf16[256,512]{1,0:T(8,128)(2,1)}, u32[]{:S(2)}, u32[]{:S(2)}) collective-permute-start(bf16[256,512]{1,0:T(8,128)(2,1)S(1)} %collective-permute-done.refs_2_), channel_id=1, source_target_pairs={{0,4},{4,8},{8,12},{12,14},{14,10},{10,6},{6,2},{2,0},{1,5},{5,9},... | collective-permute-start | bytes 786440 | tf_op jit(solution)/shard_map/ppermute | solution.py:142
  29.2 15.0 %collective-permute-start.15 = (bf16[256,512]{1,0:T(8,128)(2,1)}, bf16[256,512]{1,0:T(8,128)(2,1)}, u32[]{:S(2)}, u32[]{:S(2)}) collective-permute-start(bf16[256,512]{1,0:T(8,128)(2,1)} %collective-permute-done.11.refs_3_), channel_id=1, source_target_pairs={{4,0},{8,4},{12,8},{14,12},{10,14},{6,10},{2,6},{0,2},{5,1},{9,5},... | collective-permute-start | bytes 786440 | tf_op jit(solution)/shard_map/ppermute | solution.py:142
  34.8 10.9 %collective-permute-start.14 = (bf16[256,512]{1,0:T(8,128)(2,1)}, bf16[256,512]{1,0:T(8,128)(2,1)}, u32[]{:S(2)}, u32[]{:S(2)}) collective-permute-start(bf16[256,512]{1,0:T(8,128)(2,1)} %collective-permute-done.10.refs_2_), channel_id=1, source_target_pairs={{4,0},{8,4},{12,8},{14,12},{10,14},{6,10},{2,6},{0,2},{5,1},{9,5},... | collective-permute-start | bytes 786440 | tf_op jit(solution)/shard_map/ppermute | solution.py:142
  35.2 10.9 %collective-permute-start.13 = (bf16[256,512]{1,0:T(8,128)(2,1)}, bf16[256,512]{1,0:T(8,128)(2,1)}, u32[]{:S(2)}, u32[]{:S(2)}) collective-permute-start(bf16[256,512]{1,0:T(8,128)(2,1)} %collective-permute-done.9.refs_1_), channel_id=1, source_target_pairs={{0,4},{4,8},{8,12},{12,14},{14,10},{10,6},{6,2},{2,0},{1,5},{5,9},... | collective-permute-start | bytes 786440 | tf_op jit(solution)/shard_map/ppermute | solution.py:142
  36.8 11.6 %collective-permute-start.7 = (bf16[256,512]{1,0:T(8,128)(2,1)}, bf16[256,512]{1,0:T(8,128)(2,1)}, u32[]{:S(2)}, u32[]{:S(2)}) collective-permute-start(bf16[256,512]{1,0:T(8,128)(2,1)} %collective-permute-done.6.refs_0_), channel_id=1, source_target_pairs={{0,4},{4,8},{8,12},{12,14},{14,10},{10,6},{6,2},{2,0},{1,5},{5,9},... | collective-permute-start | bytes 786440 | tf_op jit(solution)/shard_map/ppermute | solution.py:142
  44.2 11.2 %collective-permute-start.19 = (bf16[256,512]{1,0:T(8,128)(2,1)}, bf16[256,512]{1,0:T(8,128)(2,1)}, u32[]{:S(2)}, u32[]{:S(2)}) collective-permute-start(bf16[256,512]{1,0:T(8,128)(2,1)} %collective-permute-done.15.refs_3_), channel_id=1, source_target_pairs={{4,0},{8,4},{12,8},{14,12},{10,14},{6,10},{2,6},{0,2},{5,1},{9,5},... | collective-permute-start | bytes 786440 | tf_op jit(solution)/shard_map/ppermute | solution.py:142
  45.6 11.6 %collective-permute-start.18 = (bf16[256,512]{1,0:T(8,128)(2,1)}, bf16[256,512]{1,0:T(8,128)(2,1)}, u32[]{:S(2)}, u32[]{:S(2)}) collective-permute-start(bf16[256,512]{1,0:T(8,128)(2,1)} %collective-permute-done.14.refs_2_), channel_id=1, source_target_pairs={{4,0},{8,4},{12,8},{14,12},{10,14},{6,10},{2,6},{0,2},{5,1},{9,5},... | collective-permute-start | bytes 786440 | tf_op jit(solution)/shard_map/ppermute | solution.py:142
  46.1 11.5 %collective-permute-start.17 = (bf16[256,512]{1,0:T(8,128)(2,1)}, bf16[256,512]{1,0:T(8,128)(2,1)}, u32[]{:S(2)}, u32[]{:S(2)}) collective-permute-start(bf16[256,512]{1,0:T(8,128)(2,1)} %collective-permute-done.13.refs_1_), channel_id=1, source_target_pairs={{0,4},{4,8},{8,12},{12,14},{14,10},{10,6},{6,2},{2,0},{1,5},{5,9},... | collective-permute-start | bytes 786440 | tf_op jit(solution)/shard_map/ppermute | solution.py:142
  48.4 12.6 %collective-permute-start.8 = (bf16[256,512]{1,0:T(8,128)(2,1)}, bf16[256,512]{1,0:T(8,128)(2,1)}, u32[]{:S(2)}, u32[]{:S(2)}) collective-permute-start(bf16[256,512]{1,0:T(8,128)(2,1)} %collective-permute-done.7.refs_0_), channel_id=1, source_target_pairs={{0,4},{4,8},{8,12},{12,14},{14,10},{10,6},{6,2},{2,0},{1,5},{5,9},... | collective-permute-start | bytes 786440 | tf_op jit(solution)/shard_map/ppermute | solution.py:142
  55.4 11.5 %collective-permute-start.27 = (bf16[256,512]{1,0:T(8,128)(2,1)}, bf16[256,512]{1,0:T(8,128)(2,1)}, u32[]{:S(2)}, u32[]{:S(2)}) collective-permute-start(bf16[256,512]{1,0:T(8,128)(2,1)} %collective-permute-done.19.refs_3_), channel_id=1, source_target_pairs={{4,0},{8,4},{12,8},{14,12},{10,14},{6,10},{2,6},{0,2},{5,1},{9,5},... | collective-permute-start | bytes 786440 | tf_op jit(solution)/shard_map/ppermute | solution.py:142
  57.2 12.4 %collective-permute-start.24 = (bf16[256,512]{1,0:T(8,128)(2,1)}, bf16[256,512]{1,0:T(8,128)(2,1)}, u32[]{:S(2)}, u32[]{:S(2)}) collective-permute-start(bf16[256,512]{1,0:T(8,128)(2,1)} %collective-permute-done.18.refs_2_), channel_id=1, source_target_pairs={{4,0},{8,4},{12,8},{14,12},{10,14},{6,10},{2,6},{0,2},{5,1},{9,5},... | collective-permute-start | bytes 786440 | tf_op jit(solution)/shard_map/ppermute | solution.py:142
  57.6 12.5 %collective-permute-start.21 = (bf16[256,512]{1,0:T(8,128)(2,1)}, bf16[256,512]{1,0:T(8,128)(2,1)}, u32[]{:S(2)}, u32[]{:S(2)}) collective-permute-start(bf16[256,512]{1,0:T(8,128)(2,1)} %collective-permute-done.17.refs_1_), channel_id=1, source_target_pairs={{0,4},{4,8},{8,12},{12,14},{14,10},{10,6},{6,2},{2,0},{1,5},{5,9},... | collective-permute-start | bytes 786440 | tf_op jit(solution)/shard_map/ppermute | solution.py:142
  61.1 11.7 %collective-permute-start.12 = (bf16[256,512]{1,0:T(8,128)(2,1)}, bf16[256,512]{1,0:T(8,128)(2,1)}, u32[]{:S(2)}, u32[]{:S(2)}) collective-permute-start(bf16[256,512]{1,0:T(8,128)(2,1)} %collective-permute-done.8.refs_0_), channel_id=1, source_target_pairs={{0,4},{4,8},{8,12},{12,14},{14,10},{10,6},{6,2},{2,0},{1,5},{5,9},... | collective-permute-start | bytes 786440 | tf_op jit(solution)/shard_map/ppermute | solution.py:142
  63.0 11.5 %copy-start.5 = (s32[4]{0:T(128)S(1)}, s32[4]{0:T(128)}, u32[]{:S(2)}) copy-start(s32[4]{0:T(128)} %param.13) | copy-start | bytes 52
  66.9 11.8 %collective-permute-start.28 = (bf16[256,512]{1,0:T(8,128)(2,1)}, bf16[256,512]{1,0:T(8,128)(2,1)}, u32[]{:S(2)}, u32[]{:S(2)}) collective-permute-start(bf16[256,512]{1,0:T(8,128)(2,1)} %collective-permute-done.27.refs_3_), channel_id=1, source_target_pairs={{4,0},{8,4},{12,8},{14,12},{10,14},{6,10},{2,6},{0,2},{5,1},{9,5},... | collective-permute-start | bytes 786440 | tf_op jit(solution)/shard_map/ppermute | solution.py:142
  69.7 11.4 %collective-permute-start.25 = (bf16[256,512]{1,0:T(8,128)(2,1)}, bf16[256,512]{1,0:T(8,128)(2,1)}, u32[]{:S(2)}, u32[]{:S(2)}) collective-permute-start(bf16[256,512]{1,0:T(8,128)(2,1)} %collective-permute-done.24.refs_2_), channel_id=1, source_target_pairs={{4,0},{8,4},{12,8},{14,12},{10,14},{6,10},{2,6},{0,2},{5,1},{9,5},... | collective-permute-start | bytes 786440 | tf_op jit(solution)/shard_map/ppermute | solution.py:142
  70.1 11.4 %collective-permute-start.22 = (bf16[256,512]{1,0:T(8,128)(2,1)}, bf16[256,512]{1,0:T(8,128)(2,1)}, u32[]{:S(2)}, u32[]{:S(2)}) collective-permute-start(bf16[256,512]{1,0:T(8,128)(2,1)} %collective-permute-done.21.refs_1_), channel_id=1, source_target_pairs={{0,4},{4,8},{8,12},{12,14},{14,10},{10,6},{6,2},{2,0},{1,5},{5,9},... | collective-permute-start | bytes 786440 | tf_op jit(solution)/shard_map/ppermute | solution.py:142
  72.8 11.4 %collective-permute-start.16 = (bf16[256,512]{1,0:T(8,128)(2,1)}, bf16[256,512]{1,0:T(8,128)(2,1)}, u32[]{:S(2)}, u32[]{:S(2)}) collective-permute-start(bf16[256,512]{1,0:T(8,128)(2,1)} %collective-permute-done.12.refs_0_), channel_id=1, source_target_pairs={{0,4},{4,8},{8,12},{12,14},{14,10},{10,6},{6,2},{2,0},{1,5},{5,9},... | collective-permute-start | bytes 786440 | tf_op jit(solution)/shard_map/ppermute | solution.py:142
  78.7 15.1 %collective-permute-start.29 = (bf16[256,512]{1,0:T(8,128)(2,1)}, bf16[256,512]{1,0:T(8,128)(2,1)S(1)}, u32[]{:S(2)}, u32[]{:S(2)}) collective-permute-start(bf16[256,512]{1,0:T(8,128)(2,1)} %collective-permute-done.28.refs_3_), channel_id=1, source_target_pairs={{4,0},{8,4},{12,8},{14,12},{10,14},{6,10},{2,6},{0,2},{5,1},{9,5},... | collective-permute-start | bytes 786440 | tf_op jit(solution)/shard_map/ppermute | solution.py:142
  81.1 12.7 %collective-permute-start.26 = (bf16[256,512]{1,0:T(8,128)(2,1)}, bf16[256,512]{1,0:T(8,128)(2,1)S(1)}, u32[]{:S(2)}, u32[]{:S(2)}) collective-permute-start(bf16[256,512]{1,0:T(8,128)(2,1)} %collective-permute-done.25.refs_2_), channel_id=1, source_target_pairs={{4,0},{8,4},{12,8},{14,12},{10,14},{6,10},{2,6},{0,2},{5,1},{9,5},... | collective-permute-start | bytes 786440 | tf_op jit(solution)/shard_map/ppermute | solution.py:142
  81.5 12.3 %collective-permute-start.23 = (bf16[256,512]{1,0:T(8,128)(2,1)}, bf16[256,512]{1,0:T(8,128)(2,1)S(1)}, u32[]{:S(2)}, u32[]{:S(2)}) collective-permute-start(bf16[256,512]{1,0:T(8,128)(2,1)} %collective-permute-done.22.refs_1_), channel_id=1, source_target_pairs={{0,4},{4,8},{8,12},{12,14},{14,10},{10,6},{6,2},{2,0},{1,5},{5,9},... | collective-permute-start | bytes 786440 | tf_op jit(solution)/shard_map/ppermute | solution.py:142
  84.2 9.5 %collective-permute-start.20 = (bf16[256,512]{1,0:T(8,128)(2,1)}, bf16[256,512]{1,0:T(8,128)(2,1)S(1)}, u32[]{:S(2)}, u32[]{:S(2)}) collective-permute-start(bf16[256,512]{1,0:T(8,128)(2,1)} %collective-permute-done.16.refs_0_), channel_id=1, source_target_pairs={{0,4},{4,8},{8,12},{12,14},{14,10},{10,6},{6,2},{2,0},{1,5},{5,9},... | collective-permute-start | bytes 786440 | tf_op jit(solution)/shard_map/ppermute | solution.py:142
  98.0 2.9 %collective-permute-start.30 = (bf16[1024,512]{1,0:T(8,128)(2,1)}, bf16[1024,512]{1,0:T(8,128)(2,1)S(1)}, u32[]{:S(2)}, u32[]{:S(2)}) collective-permute-start(bf16[1024,512]{1,0:T(8,128)(2,1)} %get-tuple-element.80.have_ref), channel_id=1, source_target_pairs={{0,1},{1,0},{2,3},{3,2},{4,5},{5,4},{6,7},{7,6},{8,9},{9,8},{10,11... | collective-permute-start | bytes 3145736 | tf_op jit(solution)/shard_map/ppermute | solution.py:261
  105.6 14.2 %all-to-all-start = ((f32[8,72,128]{2,1,0:T(8,128)}), f32[8,72,128]{2,1,0:T(8,128)S(1)}, u32[]{:S(2)}, u32[]{:S(2)}) async-start(f32[8,72,128]{2,1,0:T(8,128)} %bitcast.25), calls=%async_computation | async-start | bytes 589824 | tf_op jit(solution)/shard_map/all_to_all | solution.py:288
  120.2 3.8 %collective-permute-start.31 = (bf16[64,128]{1,0:T(8,128)(2,1)S(1)}, bf16[64,128]{1,0:T(8,128)(2,1)S(1)}, u32[]{:S(2)}, u32[]{:S(2)}) collective-permute-start(bf16[64,128]{1,0:T(8,128)(2,1)S(1)} %shard_map.90), channel_id=1, source_target_pairs={{0,2},{2,0},{4,6},{6,4},{8,10},{10,8},{12,14},{14,12},{1,3},{3,1},... | collective-permute-start | bytes 49160 | tf_op jit(solution)/shard_map/ppermute | solution.py:292
  124.0 5.8 %collective-permute-start.32 = (bf16[128,128]{1,0:T(8,128)(2,1)S(1)}, bf16[128,128]{1,0:T(8,128)(2,1)S(1)}, u32[]{:S(2)}, u32[]{:S(2)}) collective-permute-start(bf16[128,128]{1,0:T(8,128)(2,1)S(1)} %pad_maximum_fusion.2), channel_id=1, source_target_pairs={{0,12},{2,14},{4,8},{6,10},{8,4},{10,6},{12,0},{14,2},{1,13},{3,15... | collective-permute-start | bytes 98312 | tf_op jit(solution)/shard_map/ppermute | solution.py:295
  125.2 5.3 %collective-permute-start.33 = (bf16[128,128]{1,0:T(8,128)(2,1)S(1)}, bf16[128,128]{1,0:T(8,128)(2,1)S(1)}, u32[]{:S(2)}, u32[]{:S(2)}) collective-permute-start(bf16[128,128]{1,0:T(8,128)(2,1)S(1)} %pad_maximum_fusion.2), channel_id=1, source_target_pairs={{0,8},{2,10},{4,12},{6,14},{8,0},{10,2},{12,4},{14,6},{1,9},{3,11}... | collective-permute-start | bytes 98312 | tf_op jit(solution)/shard_map/ppermute | solution.py:295
  126.6 4.2 %collective-permute-start.34 = (bf16[128,128]{1,0:T(8,128)(2,1)S(1)}, bf16[128,128]{1,0:T(8,128)(2,1)S(1)}, u32[]{:S(2)}, u32[]{:S(2)}) collective-permute-start(bf16[128,128]{1,0:T(8,128)(2,1)S(1)} %pad_maximum_fusion.2), channel_id=1, source_target_pairs={{0,4},{2,6},{4,0},{6,2},{8,12},{10,14},{12,8},{14,10},{1,5},{3,7},... | collective-permute-start | bytes 98312 | tf_op jit(solution)/shard_map/ppermute | solution.py:295
  130.9 1.4 %collective-permute-start.35 = (bf16[16,1,4096]{2,0,1:T(8,128)(2,1)S(1)}, bf16[16,1,4096]{2,0,1:T(8,128)(2,1)S(1)}, u32[]{:S(2)}, u32[]{:S(2)}) collective-permute-start(bf16[16,1,4096]{2,0,1:T(8,128)(2,1)S(1)} %reshape.97), channel_id=1, source_target_pairs={{0,1},{1,0},{2,3},{3,2},{4,5},{5,4},{6,7},{7,6},{8,9},{9,8},{10,11... | collective-permute-start | bytes 393224 | tf_op jit(solution)/shard_map/ppermute | solution.py:305

commit v16 on v15

--- a/solution.py
+++ b/solution.py
@@ -143,10 +143,10 @@
         arriving = [(start_of(w, step), held[w * chains : (w + 1) * chains]) for w in range(2)]
         todo += arriving
         if step >= 3:
-            ready, todo = (todo[:4], todo[4:]) if total is None else (todo[:2], todo[2:])
+            taken = 4 if step in (3, 4) else 2
+            ready, todo = todo[:taken], todo[taken:]
             total, mark = add_pieces(tokens, theirs, ready, total)
-    total, _ = add_pieces(tokens, theirs, todo[:2], total)
-    return add_pieces(tokens, theirs, todo[2:], total, core)[0], early
+    return add_pieces(tokens, theirs, todo, total, core)[0], early
 
 
 def attend(have, got, core, key_up, value_up, query, bounds, chips):

time: 134 us -> 138 us (1.030)
  waiting for transfers between devices: 49 us -> 54.1 us
    ppermute x28, waiting for transfers between devices: 33.7 us -> 38.8 us  [project(): held[k] = lax.ppermute(held[k], 'chip', ways[k])]
    pallas_call x7 -> x6, Pallas kernels: 29.3 us -> 28.2 us  [add_pieces(): pl.pallas_call(kernel, out_shape=(jax.ShapeDtypeStruct((2 * tok_rows, wid...]
  transfers between devices with their start and end apart: 37 -> 37, of which waited for: 20 -> 20; matrix products, arithmetic and copies ran while one was open for 4% -> 4% of each run, Pallas kernels for 19% -> 17%
where the time goes in v16:
time: 138 us
  waiting for transfers between devices  54.1 us (39%)
  starting transfers between devices  41.8 us (30%)
  Pallas kernels  33.3 us (24%)
  local copies, waits for them, and re-layouts  4.87 us (4%)
  other arithmetic  2.34 us (2%)
    ppermute x28, waiting for transfers between devices, project(): held[k] = lax.ppermute(held[k], 'chip', ways[k])  38.8 us
    ppermute x28, starting transfers between devices, project(): held[k] = lax.ppermute(held[k], 'chip', ways[k])  30.4 us
    pallas_call x6, Pallas kernels, add_pieces(): pl.pallas_call(kernel, out_shape=(jax.ShapeDtypeStruct((2 * tok_rows, wid...  28.2 us
    all_to_all x1, waiting for transfers between devices, on_device(): lax.all_to_all(flat, 'chip', split_axis=0, concat_axis=0, tiled=True)  8.6 us
    all_to_all x1, starting transfers between devices, on_device(): lax.all_to_all(flat, 'chip', split_axis=0, concat_axis=0, tiled=True)  4.68 us
    pallas_call x1, Pallas kernels, attend(): pl.pallas_call(kernel, out_shape=jax.ShapeDtypeStruct((chips, blocks + 1,...  4.67 us
    ppermute x3, starting transfers between devices, on_device(): lax.ppermute(couple, 'chip', [(c, c ^ 2 * d) for c in range(chips)])  4.45 us
  transfers between devices with their start and end apart: 37, of which 20 were waited for; matrix products, arithmetic and copies ran while one was open for 4% of the time, Pallas kernels for 17%

profile of v16, /device:TPU:0, one launch (start us, length us, event | category | flops | bytes accessed | tf_op | source)
XLA Modules:
  0.0 138.0 jit_solution(7877393697891872785)
XLA Ops:
  0.0 1.3 broadcast_select_fusion
  1.3 0.5 collective-permute-start.2
  1.9 2.6 %collective-permute-start = (bf16[256,512]{1,0:T(8,128)(2,1)S(1)}, bf16[256,512]{1,0:T(8,128)(2,1)S(1)}, u32[]{:S(2)}, u32[]{:S(2)}) collective-permute-start(bf16[256,512]{1,0:T(8,128)(2,1)S(1)} %get-tuple-element.88), channel_id=1, source_target_pairs={{0,4},{4,8},{8,12},{12,14},{14,10},{10,6},{6,2},{2,0},{1,5},{5,9},... | collective-permute-start | bytes 786440 | tf_op jit(solution)/shard_map/ppermute | solution.py:142
  4.5 1.6 %collective-permute-start.1 = (bf16[256,512]{1,0:T(8,128)(2,1)S(1)}, bf16[256,512]{1,0:T(8,128)(2,1)S(1)}, u32[]{:S(2)}, u32[]{:S(2)}) collective-permute-start(bf16[256,512]{1,0:T(8,128)(2,1)S(1)} %get-tuple-element.87), channel_id=1, source_target_pairs={{0,4},{4,8},{8,12},{12,14},{14,10},{10,6},{6,2},{2,0},{1,5},{5,9},... | collective-permute-start | bytes 786440 | tf_op jit(solution)/shard_map/ppermute | solution.py:142
  6.1 0.5 collective-permute-start.3
  6.6 1.3 collective-permute-start.4
  7.9 3.7 %collective-permute-done.refs_2_ = bf16[256,512]{1,0:T(8,128)(2,1)S(1)} collective-permute-done((bf16[256,512]{1,0:T(8,128)(2,1)S(1)}, bf16[256,512]{1,0:T(8,128)(2,1)S(1)}, u32[]{:S(2)}, u32[]{:S(2)}) %collective-permute-start) | collective-permute-done | bytes 262176 | tf_op jit(solution)/shard_map/ppermute | solution.py:142
  11.6 5.4 %collective-permute-done.1.refs_3_ = bf16[256,512]{1,0:T(8,128)(2,1)S(1)} collective-permute-done((bf16[256,512]{1,0:T(8,128)(2,1)S(1)}, bf16[256,512]{1,0:T(8,128)(2,1)S(1)}, u32[]{:S(2)}, u32[]{:S(2)}) %collective-permute-start.1) | collective-permute-done | bytes 262176 | tf_op jit(solution)/shard_map/ppermute | solution.py:142
  17.1 2.9 %collective-permute-done.4.refs_5_ = bf16[256,512]{1,0:T(8,128)(2,1)S(1)} collective-permute-done((bf16[256,512]{1,0:T(8,128)(2,1)S(1)}, bf16[256,512]{1,0:T(8,128)(2,1)S(1)}, u32[]{:S(2)}, u32[]{:S(2)}) %collective-permute-start.4) | collective-permute-done | bytes 262176 | tf_op jit(solution)/shard_map/ppermute | solution.py:142
  20.0 1.6 %collective-permute-start.6 = (bf16[256,512]{1,0:T(8,128)(2,1)S(1)}, bf16[256,512]{1,0:T(8,128)(2,1)}, u32[]{:S(2)}, u32[]{:S(2)}) collective-permute-start(bf16[256,512]{1,0:T(8,128)(2,1)S(1)} %collective-permute-done.refs_2_), channel_id=1, source_target_pairs={{0,4},{4,8},{8,12},{12,14},{14,10},{10,6},{6,2},{2,0},{1,5},{5,9},... | collective-permute-start | bytes 786440 | tf_op jit(solution)/shard_map/ppermute | solution.py:142
  21.5 1.5 %collective-permute-start.9 = (bf16[256,512]{1,0:T(8,128)(2,1)S(1)}, bf16[256,512]{1,0:T(8,128)(2,1)}, u32[]{:S(2)}, u32[]{:S(2)}) collective-permute-start(bf16[256,512]{1,0:T(8,128)(2,1)S(1)} %collective-permute-done.1.refs_3_), channel_id=1, source_target_pairs={{0,4},{4,8},{8,12},{12,14},{14,10},{10,6},{6,2},{2,0},{1,5},{5,9},... | collective-permute-start | bytes 786440 | tf_op jit(solution)/shard_map/ppermute | solution.py:142
  23.1 0.5 collective-permute-start.10
  23.6 0.4 collective-permute-start.11
  24.2 5.0 %collective-permute-done.6.refs_0_ = bf16[256,512]{1,0:T(8,128)(2,1)} collective-permute-done((bf16[256,512]{1,0:T(8,128)(2,1)S(1)}, bf16[256,512]{1,0:T(8,128)(2,1)}, u32[]{:S(2)}, u32[]{:S(2)}) %collective-permute-start.6) | collective-permute-done | bytes 262176 | tf_op jit(solution)/shard_map/ppermute | solution.py:142
  29.2 1.6 %collective-permute-start.7 = (bf16[256,512]{1,0:T(8,128)(2,1)}, bf16[256,512]{1,0:T(8,128)(2,1)}, u32[]{:S(2)}, u32[]{:S(2)}) collective-permute-start(bf16[256,512]{1,0:T(8,128)(2,1)} %collective-permute-done.6.refs_0_), channel_id=1, source_target_pairs={{0,4},{4,8},{8,12},{12,14},{14,10},{10,6},{6,2},{2,0},{1,5},{5,9},... | collective-permute-start | bytes 786440 | tf_op jit(solution)/shard_map/ppermute | solution.py:142
  30.7 4.0 %collective-permute-done.9.refs_1_ = bf16[256,512]{1,0:T(8,128)(2,1)} collective-permute-done((bf16[256,512]{1,0:T(8,128)(2,1)S(1)}, bf16[256,512]{1,0:T(8,128)(2,1)}, u32[]{:S(2)}, u32[]{:S(2)}) %collective-permute-start.9) | collective-permute-done | bytes 262176 | tf_op jit(solution)/shard_map/ppermute | solution.py:142
  34.8 1.6 %collective-permute-start.12 = (bf16[256,512]{1,0:T(8,128)(2,1)}, bf16[256,512]{1,0:T(8,128)(2,1)}, u32[]{:S(2)}, u32[]{:S(2)}) collective-permute-start(bf16[256,512]{1,0:T(8,128)(2,1)} %collective-permute-done.9.refs_1_), channel_id=1, source_target_pairs={{0,4},{4,8},{8,12},{12,14},{14,10},{10,6},{6,2},{2,0},{1,5},{5,9},... | collective-permute-start | bytes 786440 | tf_op jit(solution)/shard_map/ppermute | solution.py:142
  36.4 0.5 collective-permute-start.13
  36.9 0.5 collective-permute-start.14
  37.4 0.7 constant_dynamic-slice_fusion.3
  38.2 5.7 %shard_map.82 = (f32[1024,512]{1,0:T(8,128)S(1)}, f32[8,128]{1,0:T(8,128)}) custom-call(s32[4]{0:T(128)S(1)} %pad_add_fusion.1.places_ref, bf16[512,8192]{1,0:T(8,128)(2,1)} %mine_ref.11, bf16[512,8192]{1,0:T(8,128)(2,1)} %collective-permute-done.5.theirs_ref, bf16[512,512]{1,0:T(8,128)(2,1)S(1)} %get-tuple-element.84.refs_0_, ...), custom_call_target="tpu_custom_call" | custom-call | flops 2147483648 | bytes 4194304 | tf_op jit(solution)/shard_map/pallas_call | solution.py:73
  43.9 5.7 %collective-permute-done.14.refs_7_ = bf16[256,512]{1,0:T(8,128)(2,1)} collective-permute-done((bf16[256,512]{1,0:T(8,128)(2,1)}, bf16[256,512]{1,0:T(8,128)(2,1)}, u32[]{:S(2)}, u32[]{:S(2)}) %collective-permute-start.14) | collective-permute-done | bytes 262176 | tf_op jit(solution)/shard_map/ppermute | solution.py:142
  49.6 0.4 collective-permute-start.18
  50.0 1.6 %collective-permute-start.16 = (bf16[256,512]{1,0:T(8,128)(2,1)}, bf16[256,512]{1,0:T(8,128)(2,1)}, u32[]{:S(2)}, u32[]{:S(2)}) collective-permute-start(bf16[256,512]{1,0:T(8,128)(2,1)} %collective-permute-done.12.refs_5_), channel_id=1, source_target_pairs={{0,4},{4,8},{8,12},{12,14},{14,10},{10,6},{6,2},{2,0},{1,5},{5,9},... | collective-permute-start | bytes 786440 | tf_op jit(solution)/shard_map/ppermute | solution.py:142
  51.6 0.5 collective-permute-start.17
  52.1 1.6 %collective-permute-start.8 = (bf16[256,512]{1,0:T(8,128)(2,1)}, bf16[256,512]{1,0:T(8,128)(2,1)}, u32[]{:S(2)}, u32[]{:S(2)}) collective-permute-start(bf16[256,512]{1,0:T(8,128)(2,1)} %collective-permute-done.7.refs_4_), channel_id=1, source_target_pairs={{0,4},{4,8},{8,12},{12,14},{14,10},{10,6},{6,2},{2,0},{1,5},{5,9},... | collective-permute-start | bytes 786440 | tf_op jit(solution)/shard_map/ppermute | solution.py:142
  53.7 1.1 reshape.83
  54.8 6.0 %shard_map.83 = (f32[1024,512]{1,0:T(8,128)S(1)}, f32[8,128]{1,0:T(8,128)}) custom-call(s32[4]{0:T(128)S(1)} %pad_add_fusion.2.places_ref, bf16[512,8192]{1,0:T(8,128)(2,1)} %mine_ref.11, bf16[512,8192]{1,0:T(8,128)(2,1)} %collective-permute-done.5.theirs_ref, bf16[256,512]{1,0:T(8,128)(2,1)} %collective-permute-done.6.refs_0_, ...), custom_call_target="tpu_custom_call", output_to_operand_aliasing={{0}: (11, {})} | custom-call | flops 2147483648 | bytes 4194304 | tf_op jit(solution)/shard_map/pallas_call | solution.py:73
  60.8 0.5 collective-permute-start.22
  61.3 1.5 %collective-permute-done.17.refs_2_ = bf16[256,512]{1,0:T(8,128)(2,1)} collective-permute-done((bf16[256,512]{1,0:T(8,128)(2,1)}, bf16[256,512]{1,0:T(8,128)(2,1)}, u32[]{:S(2)}, u32[]{:S(2)}) %collective-permute-start.17) | collective-permute-done | bytes 262176 | tf_op jit(solution)/shard_map/ppermute | solution.py:142
  62.8 0.4 collective-permute-start.21
  63.3 1.6 %collective-permute-start.20 = (bf16[256,512]{1,0:T(8,128)(2,1)}, bf16[256,512]{1,0:T(8,128)(2,1)}, u32[]{:S(2)}, u32[]{:S(2)}) collective-permute-start(bf16[256,512]{1,0:T(8,128)(2,1)} %collective-permute-done.16.refs_1_), channel_id=1, source_target_pairs={{0,4},{4,8},{8,12},{12,14},{14,10},{10,6},{6,2},{2,0},{1,5},{5,9},... | collective-permute-start | bytes 786440 | tf_op jit(solution)/shard_map/ppermute | solution.py:142
  64.9 1.5 %collective-permute-start.15 = (bf16[256,512]{1,0:T(8,128)(2,1)}, bf16[256,512]{1,0:T(8,128)(2,1)}, u32[]{:S(2)}, u32[]{:S(2)}) collective-permute-start(bf16[256,512]{1,0:T(8,128)(2,1)} %collective-permute-done.8.refs_0_), channel_id=1, source_target_pairs={{0,4},{4,8},{8,12},{12,14},{14,10},{10,6},{6,2},{2,0},{1,5},{5,9},... | collective-permute-start | bytes 786440 | tf_op jit(solution)/shard_map/ppermute | solution.py:142
  66.5 3.9 %shard_map.84 = (f32[1024,512]{1,0:T(8,128)S(1)}, f32[8,128]{1,0:T(8,128)}) custom-call(s32[2]{0:T(128)S(1)} %pad_add_fusion.3.places_ref, bf16[512,8192]{1,0:T(8,128)(2,1)} %mine_ref.11, bf16[512,8192]{1,0:T(8,128)(2,1)} %collective-permute-done.5.theirs_ref, bf16[256,512]{1,0:T(8,128)(2,1)} %collective-permute-done.8.refs_0_, ...), custom_call_target="tpu_custom_call", output_to_operand_aliasing={{0}: (7, {})} | custom-call | flops 1073741824 | bytes 2097152 | tf_op jit(solution)/shard_map/pallas_call | solution.py:73
  70.4 0.5 collective-permute-start.28
  70.9 5.1 %collective-permute-done.21.refs_2_ = bf16[256,512]{1,0:T(8,128)(2,1)} collective-permute-done((bf16[256,512]{1,0:T(8,128)(2,1)}, bf16[256,512]{1,0:T(8,128)(2,1)}, u32[]{:S(2)}, u32[]{:S(2)}) %collective-permute-start.21) | collective-permute-done | bytes 262176 | tf_op jit(solution)/shard_map/ppermute | solution.py:142
  76.1 0.4 collective-permute-start.26
  76.5 1.6 %collective-permute-start.24 = (bf16[256,512]{1,0:T(8,128)(2,1)}, bf16[256,512]{1,0:T(8,128)(2,1)}, u32[]{:S(2)}, u32[]{:S(2)}) collective-permute-start(bf16[256,512]{1,0:T(8,128)(2,1)} %collective-permute-done.20.refs_1_), channel_id=1, source_target_pairs={{0,4},{4,8},{8,12},{12,14},{14,10},{10,6},{6,2},{2,0},{1,5},{5,9},... | collective-permute-start | bytes 786440 | tf_op jit(solution)/shard_map/ppermute | solution.py:142
  78.1 1.5 %collective-permute-start.19 = (bf16[256,512]{1,0:T(8,128)(2,1)}, bf16[256,512]{1,0:T(8,128)(2,1)}, u32[]{:S(2)}, u32[]{:S(2)}) collective-permute-start(bf16[256,512]{1,0:T(8,128)(2,1)} %collective-permute-done.15.refs_0_), channel_id=1, source_target_pairs={{0,4},{4,8},{8,12},{12,14},{14,10},{10,6},{6,2},{2,0},{1,5},{5,9},... | collective-permute-start | bytes 786440 | tf_op jit(solution)/shard_map/ppermute | solution.py:142
  79.7 3.9 %shard_map.85 = (f32[1024,512]{1,0:T(8,128)S(1)}, f32[8,128]{1,0:T(8,128)}) custom-call(s32[2]{0:T(128)S(1)} %pad_add_fusion.4.places_ref, bf16[512,8192]{1,0:T(8,128)(2,1)} %mine_ref.11, bf16[512,8192]{1,0:T(8,128)(2,1)} %collective-permute-done.5.theirs_ref, bf16[256,512]{1,0:T(8,128)(2,1)} %collective-permute-done.15.refs_0_, ...), custom_call_target="tpu_custom_call", output_to_operand_aliasing={{0}: (7, {})} | custom-call | flops 1073741824 | bytes 2097152 | tf_op jit(solution)/shard_map/pallas_call | solution.py:73
  83.6 0.6 collective-permute-start.29
  84.2 3.1 %collective-permute-done.26.refs_2_ = bf16[256,512]{1,0:T(8,128)(2,1)} collective-permute-done((bf16[256,512]{1,0:T(8,128)(2,1)}, bf16[256,512]{1,0:T(8,128)(2,1)}, u32[]{:S(2)}, u32[]{:S(2)}) %collective-permute-start.26) | collective-permute-done | bytes 262176 | tf_op jit(solution)/shard_map/ppermute | solution.py:142
  87.3 0.4 collective-permute-start.27
  87.7 1.6 %collective-permute-start.25 = (bf16[256,512]{1,0:T(8,128)(2,1)}, bf16[256,512]{1,0:T(8,128)(2,1)}, u32[]{:S(2)}, u32[]{:S(2)}) collective-permute-start(bf16[256,512]{1,0:T(8,128)(2,1)} %collective-permute-done.24.refs_1_), channel_id=1, source_target_pairs={{0,4},{4,8},{8,12},{12,14},{14,10},{10,6},{6,2},{2,0},{1,5},{5,9},... | collective-permute-start | bytes 786440 | tf_op jit(solution)/shard_map/ppermute | solution.py:142
  89.3 1.5 %collective-permute-start.23 = (bf16[256,512]{1,0:T(8,128)(2,1)}, bf16[256,512]{1,0:T(8,128)(2,1)}, u32[]{:S(2)}, u32[]{:S(2)}) collective-permute-start(bf16[256,512]{1,0:T(8,128)(2,1)} %collective-permute-done.19.refs_0_), channel_id=1, source_target_pairs={{0,4},{4,8},{8,12},{12,14},{14,10},{10,6},{6,2},{2,0},{1,5},{5,9},... | collective-permute-start | bytes 786440 | tf_op jit(solution)/shard_map/ppermute | solution.py:142
  91.2 3.9 %shard_map.86 = (f32[1024,512]{1,0:T(8,128)S(1)}, f32[8,128]{1,0:T(8,128)}) custom-call(s32[2]{0:T(128)S(1)} %pad_add_fusion.5.places_ref, bf16[512,8192]{1,0:T(8,128)(2,1)} %mine_ref.11, bf16[512,8192]{1,0:T(8,128)(2,1)} %collective-permute-done.5.theirs_ref, bf16[256,512]{1,0:T(8,128)(2,1)} %collective-permute-done.19.refs_0_, ...), custom_call_target="tpu_custom_call", output_to_operand_aliasing={{0}: (7, {})} | custom-call | flops 1073741824 | bytes 2097152 | tf_op jit(solution)/shard_map/pallas_call | solution.py:73
  95.1 0.5 collective-permute-done.27.refs_2_
  95.6 1.7 %collective-permute-done.23.refs_0_ = bf16[256,512]{1,0:T(8,128)(2,1)} collective-permute-done((bf16[256,512]{1,0:T(8,128)(2,1)}, bf16[256,512]{1,0:T(8,128)(2,1)}, u32[]{:S(2)}, u32[]{:S(2)}) %collective-permute-start.23) | collective-permute-done | bytes 262176 | tf_op jit(solution)/shard_map/ppermute | solution.py:142
  97.2 4.8 %shard_map.87 = (bf16[1024,512]{1,0:T(8,128)(2,1)}, f32[8,128]{1,0:T(8,128)}) custom-call(s32[4]{0:T(128)S(1)} %pad_add_fusion.places_ref, bf16[512,8192]{1,0:T(8,128)(2,1)} %mine_ref.11, bf16[512,8192]{1,0:T(8,128)(2,1)} %collective-permute-done.5.theirs_ref, bf16[256,512]{1,0:T(8,128)(2,1)} %collective-permute-done.23.refs_0_, ...), custom_call_target="tpu_custom_call" | custom-call | flops 1073741824 | bytes 2097152 | tf_op jit(solution)/shard_map/pallas_call | solution.py:73
  102.4 0.8 reshape.89
  103.6 0.7 fusion.17
  104.3 0.7 collective-permute-done.30.got_ref
  105.0 4.7 %shard_map.88 = f32[8,9,8,128]{3,2,1,0:T(8,128)} custom-call(s32[1]{0:T(128)} %bitcast.core_ref, bf16[1024,512]{1,0:T(8,128)(2,1)} %get-tuple-element.78.have_ref, bf16[1024,512]{1,0:T(8,128)(2,1)S(1)} %collective-permute-done.30.got_ref, bf16[512,512]{1,0:T(8,128)(2,1)S(1)} %get-tuple-element.79.key_up_ref, ...), custom_call_target="tpu_custom_call" | custom-call | flops 1342177280 | bytes 2097152 | tf_op jit(solution)/shard_map/pallas_call | solution.py:194
  109.7 4.7 %all-to-all-start = ((f32[8,72,128]{2,1,0:T(8,128)}), f32[8,72,128]{2,1,0:T(8,128)S(1)}, u32[]{:S(2)}, u32[]{:S(2)}) async-start(f32[8,72,128]{2,1,0:T(8,128)} %bitcast.25), calls=%async_computation | async-start | bytes 589824 | tf_op jit(solution)/shard_map/all_to_all | solution.py:288
  115.7 8.6 %all-to-all-done = f32[8,72,128]{2,1,0:T(8,128)S(1)} async-done(((f32[8,72,128]{2,1,0:T(8,128)}), f32[8,72,128]{2,1,0:T(8,128)S(1)}, u32[]{:S(2)}, u32[]{:S(2)}) %all-to-all-start) | async-done | bytes 294944 | tf_op jit(solution)/shard_map/all_to_all | solution.py:288
  124.6 1.5 %collective-permute-start.31 = (bf16[64,128]{1,0:T(8,128)(2,1)S(1)}, bf16[64,128]{1,0:T(8,128)(2,1)S(1)}, u32[]{:S(2)}, u32[]{:S(2)}) collective-permute-start(bf16[64,128]{1,0:T(8,128)(2,1)S(1)} %shard_map.89), channel_id=1, source_target_pairs={{0,2},{2,0},{4,6},{6,4},{8,10},{10,8},{12,14},{14,12},{1,3},{3,1},... | collective-permute-start | bytes 49160 | tf_op jit(solution)/shard_map/ppermute | solution.py:292
  126.2 2.3 %collective-permute-done.31 = bf16[64,128]{1,0:T(8,128)(2,1)S(1)} collective-permute-done((bf16[64,128]{1,0:T(8,128)(2,1)S(1)}, bf16[64,128]{1,0:T(8,128)(2,1)S(1)}, u32[]{:S(2)}, u32[]{:S(2)}) %collective-permute-start.31) | collective-permute-done | bytes 16416 | tf_op jit(solution)/shard_map/ppermute | solution.py:292
  128.4 1.2 collective-permute-start.32
  129.7 1.3 collective-permute-start.33
  131.0 1.9 %collective-permute-start.34 = (bf16[128,128]{1,0:T(8,128)(2,1)S(1)}, bf16[128,128]{1,0:T(8,128)(2,1)S(1)}, u32[]{:S(2)}, u32[]{:S(2)}) collective-permute-start(bf16[128,128]{1,0:T(8,128)(2,1)S(1)} %pad_maximum_fusion.2), channel_id=1, source_target_pairs={{0,4},{2,6},{4,0},{6,2},{8,12},{10,14},{12,8},{14,10},{1,5},{3,7},... | collective-permute-start | bytes 98312 | tf_op jit(solution)/shard_map/ppermute | solution.py:295
  132.9 1.3 collective-permute-done.32
  134.2 0.8 collective-permute-done.33
  135.5 1.3 collective-permute-done.35
  137.1 0.9 reshape.98
  (83 shorter events, 4.1 us)
Async XLA Ops:
  0.0 37.4 %copy-start = (bf16[4,4,8192]{2,1,0:T(4,128)(2,1)S(1)}, bf16[4,4,8192]{2,1,0:T(4,128)(2,1)}, u32[]{:S(2)}) copy-start(bf16[4,4,8192]{2,1,0:T(4,128)(2,1)} %param.14) | copy-start | bytes 786436
  1.3 4.8 %collective-permute-start.2 = (bf16[512,512]{1,0:T(8,128)(2,1)S(1)}, bf16[512,512]{1,0:T(8,128)(2,1)S(1)}, u32[]{:S(2)}, u32[]{:S(2)}) collective-permute-start(bf16[512,512]{1,0:T(8,128)(2,1)S(1)} %get-tuple-element.83), channel_id=1, source_target_pairs={{0,1},{1,0},{2,3},{3,2},{4,5},{5,4},{6,7},{7,6},{8,9},{9,8},{10,11... | collective-permute-start | bytes 1572872 | tf_op jit(solution)/shard_map/ppermute | solution.py:103
  1.9 9.7 %collective-permute-start = (bf16[256,512]{1,0:T(8,128)(2,1)S(1)}, bf16[256,512]{1,0:T(8,128)(2,1)S(1)}, u32[]{:S(2)}, u32[]{:S(2)}) collective-permute-start(bf16[256,512]{1,0:T(8,128)(2,1)S(1)} %get-tuple-element.88), channel_id=1, source_target_pairs={{0,4},{4,8},{8,12},{12,14},{14,10},{10,6},{6,2},{2,0},{1,5},{5,9},... | collective-permute-start | bytes 786440 | tf_op jit(solution)/shard_map/ppermute | solution.py:142
  4.5 12.5 %collective-permute-start.1 = (bf16[256,512]{1,0:T(8,128)(2,1)S(1)}, bf16[256,512]{1,0:T(8,128)(2,1)S(1)}, u32[]{:S(2)}, u32[]{:S(2)}) collective-permute-start(bf16[256,512]{1,0:T(8,128)(2,1)S(1)} %get-tuple-element.87), channel_id=1, source_target_pairs={{0,4},{4,8},{8,12},{12,14},{14,10},{10,6},{6,2},{2,0},{1,5},{5,9},... | collective-permute-start | bytes 786440 | tf_op jit(solution)/shard_map/ppermute | solution.py:142
  6.1 10.9 %collective-permute-start.3 = (bf16[256,512]{1,0:T(8,128)(2,1)S(1)}, bf16[256,512]{1,0:T(8,128)(2,1)S(1)}, u32[]{:S(2)}, u32[]{:S(2)}) collective-permute-start(bf16[256,512]{1,0:T(8,128)(2,1)S(1)} %get-tuple-element.86), channel_id=1, source_target_pairs={{4,0},{8,4},{12,8},{14,12},{10,14},{6,10},{2,6},{0,2},{5,1},{9,5},... | collective-permute-start | bytes 786440 | tf_op jit(solution)/shard_map/ppermute | solution.py:142
  6.6 13.3 %collective-permute-start.4 = (bf16[256,512]{1,0:T(8,128)(2,1)S(1)}, bf16[256,512]{1,0:T(8,128)(2,1)S(1)}, u32[]{:S(2)}, u32[]{:S(2)}) collective-permute-start(bf16[256,512]{1,0:T(8,128)(2,1)S(1)} %get-tuple-element.85), channel_id=1, source_target_pairs={{4,0},{8,4},{12,8},{14,12},{10,14},{6,10},{2,6},{0,2},{5,1},{9,5},... | collective-permute-start | bytes 786440 | tf_op jit(solution)/shard_map/ppermute | solution.py:142
  11.6 26.5 %copy-start.1 = (bf16[256,512]{1,0:T(8,128)(2,1)}, bf16[256,512]{1,0:T(8,128)(2,1)S(1)}, u32[]{:S(2)}) copy-start(bf16[256,512]{1,0:T(8,128)(2,1)S(1)} %collective-permute-done.refs_2_) | copy-start | bytes 786436
  17.0 21.1 %copy-start.2 = (bf16[256,512]{1,0:T(8,128)(2,1)}, bf16[256,512]{1,0:T(8,128)(2,1)S(1)}, u32[]{:S(2)}) copy-start(bf16[256,512]{1,0:T(8,128)(2,1)S(1)} %collective-permute-done.1.refs_3_) | copy-start | bytes 786436
  17.0 21.1 %copy-start.3 = (bf16[256,512]{1,0:T(8,128)(2,1)}, bf16[256,512]{1,0:T(8,128)(2,1)S(1)}, u32[]{:S(2)}) copy-start(bf16[256,512]{1,0:T(8,128)(2,1)S(1)} %collective-permute-done.3.refs_4_) | copy-start | bytes 786436
  20.0 18.2 %copy-start.4 = (bf16[256,512]{1,0:T(8,128)(2,1)}, bf16[256,512]{1,0:T(8,128)(2,1)S(1)}, u32[]{:S(2)}) copy-start(bf16[256,512]{1,0:T(8,128)(2,1)S(1)} %collective-permute-done.4.refs_5_) | copy-start | bytes 786436
  20.0 18.2 %collective-permute-start.5 = (bf16[512,8192]{1,0:T(8,128)(2,1)}, bf16[512,8192]{1,0:T(8,128)(2,1)}, u32[]{:S(2)}, u32[]{:S(2)}) collective-permute-start(bf16[512,8192]{1,0:T(8,128)(2,1)} %mine_ref.11), channel_id=1, source_target_pairs={{0,1},{1,0},{2,3},{3,2},{4,5},{5,4},{6,7},{7,6},{8,9},{9,8},{10,11... | collective-permute-start | bytes 25165832 | tf_op jit(solution)/shard_map/ppermute | solution.py:133
  20.0 9.2 %collective-permute-start.6 = (bf16[256,512]{1,0:T(8,128)(2,1)S(1)}, bf16[256,512]{1,0:T(8,128)(2,1)}, u32[]{:S(2)}, u32[]{:S(2)}) collective-permute-start(bf16[256,512]{1,0:T(8,128)(2,1)S(1)} %collective-permute-done.refs_2_), channel_id=1, source_target_pairs={{0,4},{4,8},{8,12},{12,14},{14,10},{10,6},{6,2},{2,0},{1,5},{5,9},... | collective-permute-start | bytes 786440 | tf_op jit(solution)/shard_map/ppermute | solution.py:142
  21.5 13.2 %collective-permute-start.9 = (bf16[256,512]{1,0:T(8,128)(2,1)S(1)}, bf16[256,512]{1,0:T(8,128)(2,1)}, u32[]{:S(2)}, u32[]{:S(2)}) collective-permute-start(bf16[256,512]{1,0:T(8,128)(2,1)S(1)} %collective-permute-done.1.refs_3_), channel_id=1, source_target_pairs={{0,4},{4,8},{8,12},{12,14},{14,10},{10,6},{6,2},{2,0},{1,5},{5,9},... | collective-permute-start | bytes 786440 | tf_op jit(solution)/shard_map/ppermute | solution.py:142
  23.1 13.3 %collective-permute-start.10 = (bf16[256,512]{1,0:T(8,128)(2,1)S(1)}, bf16[256,512]{1,0:T(8,128)(2,1)}, u32[]{:S(2)}, u32[]{:S(2)}) collective-permute-start(bf16[256,512]{1,0:T(8,128)(2,1)S(1)} %collective-permute-done.3.refs_4_), channel_id=1, source_target_pairs={{4,0},{8,4},{12,8},{14,12},{10,14},{6,10},{2,6},{0,2},{5,1},{9,5},... | collective-permute-start | bytes 786440 | tf_op jit(solution)/shard_map/ppermute | solution.py:142
  23.6 13.4 %collective-permute-start.11 = (bf16[256,512]{1,0:T(8,128)(2,1)S(1)}, bf16[256,512]{1,0:T(8,128)(2,1)}, u32[]{:S(2)}, u32[]{:S(2)}) collective-permute-start(bf16[256,512]{1,0:T(8,128)(2,1)S(1)} %collective-permute-done.4.refs_5_), channel_id=1, source_target_pairs={{4,0},{8,4},{12,8},{14,12},{10,14},{6,10},{2,6},{0,2},{5,1},{9,5},... | collective-permute-start | bytes 786440 | tf_op jit(solution)/shard_map/ppermute | solution.py:142
  29.2 22.9 %collective-permute-start.7 = (bf16[256,512]{1,0:T(8,128)(2,1)}, bf16[256,512]{1,0:T(8,128)(2,1)}, u32[]{:S(2)}, u32[]{:S(2)}) collective-permute-start(bf16[256,512]{1,0:T(8,128)(2,1)} %collective-permute-done.6.refs_0_), channel_id=1, source_target_pairs={{0,4},{4,8},{8,12},{12,14},{14,10},{10,6},{6,2},{2,0},{1,5},{5,9},... | collective-permute-start | bytes 786440 | tf_op jit(solution)/shard_map/ppermute | solution.py:142
  34.8 15.2 %collective-permute-start.12 = (bf16[256,512]{1,0:T(8,128)(2,1)}, bf16[256,512]{1,0:T(8,128)(2,1)}, u32[]{:S(2)}, u32[]{:S(2)}) collective-permute-start(bf16[256,512]{1,0:T(8,128)(2,1)} %collective-permute-done.9.refs_1_), channel_id=1, source_target_pairs={{0,4},{4,8},{8,12},{12,14},{14,10},{10,6},{6,2},{2,0},{1,5},{5,9},... | collective-permute-start | bytes 786440 | tf_op jit(solution)/shard_map/ppermute | solution.py:142
  36.4 15.2 %collective-permute-start.13 = (bf16[256,512]{1,0:T(8,128)(2,1)}, bf16[256,512]{1,0:T(8,128)(2,1)}, u32[]{:S(2)}, u32[]{:S(2)}) collective-permute-start(bf16[256,512]{1,0:T(8,128)(2,1)} %collective-permute-done.10.refs_2_), channel_id=1, source_target_pairs={{4,0},{8,4},{12,8},{14,12},{10,14},{6,10},{2,6},{0,2},{5,1},{9,5},... | collective-permute-start | bytes 786440 | tf_op jit(solution)/shard_map/ppermute | solution.py:142
  36.9 12.6 %collective-permute-start.14 = (bf16[256,512]{1,0:T(8,128)(2,1)}, bf16[256,512]{1,0:T(8,128)(2,1)}, u32[]{:S(2)}, u32[]{:S(2)}) collective-permute-start(bf16[256,512]{1,0:T(8,128)(2,1)} %collective-permute-done.11.refs_3_), channel_id=1, source_target_pairs={{4,0},{8,4},{12,8},{14,12},{10,14},{6,10},{2,6},{0,2},{5,1},{9,5},... | collective-permute-start | bytes 786440 | tf_op jit(solution)/shard_map/ppermute | solution.py:142
  38.2 15.5 %copy-start.5 = (bf16[512,1024]{1,0:T(8,128)(2,1)S(1)}, bf16[512,1024]{1,0:T(8,128)(2,1)}, u32[]{:S(2)}) copy-start(bf16[512,1024]{1,0:T(8,128)(2,1)} %param.12) | copy-start | bytes 3145732
  38.2 15.5 %copy-start.6 = (bf16[512,1024]{1,0:T(8,128)(2,1)S(1)}, bf16[512,1024]{1,0:T(8,128)(2,1)}, u32[]{:S(2)}) copy-start(bf16[512,1024]{1,0:T(8,128)(2,1)} %param.11) | copy-start | bytes 3145732
  49.6 11.3 %collective-permute-start.18 = (bf16[256,512]{1,0:T(8,128)(2,1)}, bf16[256,512]{1,0:T(8,128)(2,1)}, u32[]{:S(2)}, u32[]{:S(2)}) collective-permute-start(bf16[256,512]{1,0:T(8,128)(2,1)} %collective-permute-done.14.refs_7_), channel_id=1, source_target_pairs={{4,0},{8,4},{12,8},{14,12},{10,14},{6,10},{2,6},{0,2},{5,1},{9,5},... | collective-permute-start | bytes 786440 | tf_op jit(solution)/shard_map/ppermute | solution.py:142
  50.0 13.3 %collective-permute-start.16 = (bf16[256,512]{1,0:T(8,128)(2,1)}, bf16[256,512]{1,0:T(8,128)(2,1)}, u32[]{:S(2)}, u32[]{:S(2)}) collective-permute-start(bf16[256,512]{1,0:T(8,128)(2,1)} %collective-permute-done.12.refs_5_), channel_id=1, source_target_pairs={{0,4},{4,8},{8,12},{12,14},{14,10},{10,6},{6,2},{2,0},{1,5},{5,9},... | collective-permute-start | bytes 786440 | tf_op jit(solution)/shard_map/ppermute | solution.py:142
  51.6 11.2 %collective-permute-start.17 = (bf16[256,512]{1,0:T(8,128)(2,1)}, bf16[256,512]{1,0:T(8,128)(2,1)}, u32[]{:S(2)}, u32[]{:S(2)}) collective-permute-start(bf16[256,512]{1,0:T(8,128)(2,1)} %collective-permute-done.13.refs_6_), channel_id=1, source_target_pairs={{4,0},{8,4},{12,8},{14,12},{10,14},{6,10},{2,6},{0,2},{5,1},{9,5},... | collective-permute-start | bytes 786440 | tf_op jit(solution)/shard_map/ppermute | solution.py:142
  52.1 12.8 %collective-permute-start.8 = (bf16[256,512]{1,0:T(8,128)(2,1)}, bf16[256,512]{1,0:T(8,128)(2,1)}, u32[]{:S(2)}, u32[]{:S(2)}) collective-permute-start(bf16[256,512]{1,0:T(8,128)(2,1)} %collective-permute-done.7.refs_4_), channel_id=1, source_target_pairs={{0,4},{4,8},{8,12},{12,14},{14,10},{10,6},{6,2},{2,0},{1,5},{5,9},... | collective-permute-start | bytes 786440 | tf_op jit(solution)/shard_map/ppermute | solution.py:142
  60.8 9.6 %collective-permute-start.22 = (bf16[256,512]{1,0:T(8,128)(2,1)}, bf16[256,512]{1,0:T(8,128)(2,1)}, u32[]{:S(2)}, u32[]{:S(2)}) collective-permute-start(bf16[256,512]{1,0:T(8,128)(2,1)} %collective-permute-done.18.refs_3_), channel_id=1, source_target_pairs={{4,0},{8,4},{12,8},{14,12},{10,14},{6,10},{2,6},{0,2},{5,1},{9,5},... | collective-permute-start | bytes 786440 | tf_op jit(solution)/shard_map/ppermute | solution.py:142
  62.8 13.2 %collective-permute-start.21 = (bf16[256,512]{1,0:T(8,128)(2,1)}, bf16[256,512]{1,0:T(8,128)(2,1)}, u32[]{:S(2)}, u32[]{:S(2)}) collective-permute-start(bf16[256,512]{1,0:T(8,128)(2,1)} %collective-permute-done.17.refs_2_), channel_id=1, source_target_pairs={{4,0},{8,4},{12,8},{14,12},{10,14},{6,10},{2,6},{0,2},{5,1},{9,5},... | collective-permute-start | bytes 786440 | tf_op jit(solution)/shard_map/ppermute | solution.py:142
  63.3 13.2 %collective-permute-start.20 = (bf16[256,512]{1,0:T(8,128)(2,1)}, bf16[256,512]{1,0:T(8,128)(2,1)}, u32[]{:S(2)}, u32[]{:S(2)}) collective-permute-start(bf16[256,512]{1,0:T(8,128)(2,1)} %collective-permute-done.16.refs_1_), channel_id=1, source_target_pairs={{0,4},{4,8},{8,12},{12,14},{14,10},{10,6},{6,2},{2,0},{1,5},{5,9},... | collective-permute-start | bytes 786440 | tf_op jit(solution)/shard_map/ppermute | solution.py:142
  64.9 13.2 %collective-permute-start.15 = (bf16[256,512]{1,0:T(8,128)(2,1)}, bf16[256,512]{1,0:T(8,128)(2,1)}, u32[]{:S(2)}, u32[]{:S(2)}) collective-permute-start(bf16[256,512]{1,0:T(8,128)(2,1)} %collective-permute-done.8.refs_0_), channel_id=1, source_target_pairs={{0,4},{4,8},{8,12},{12,14},{14,10},{10,6},{6,2},{2,0},{1,5},{5,9},... | collective-permute-start | bytes 786440 | tf_op jit(solution)/shard_map/ppermute | solution.py:142
  70.4 13.1 %collective-permute-start.28 = (bf16[256,512]{1,0:T(8,128)(2,1)}, bf16[256,512]{1,0:T(8,128)(2,1)}, u32[]{:S(2)}, u32[]{:S(2)}) collective-permute-start(bf16[256,512]{1,0:T(8,128)(2,1)} %collective-permute-done.22.refs_3_), channel_id=1, source_target_pairs={{4,0},{8,4},{12,8},{14,12},{10,14},{6,10},{2,6},{0,2},{5,1},{9,5},... | collective-permute-start | bytes 786440 | tf_op jit(solution)/shard_map/ppermute | solution.py:142
  76.1 11.2 %collective-permute-start.26 = (bf16[256,512]{1,0:T(8,128)(2,1)}, bf16[256,512]{1,0:T(8,128)(2,1)}, u32[]{:S(2)}, u32[]{:S(2)}) collective-permute-start(bf16[256,512]{1,0:T(8,128)(2,1)} %collective-permute-done.21.refs_2_), channel_id=1, source_target_pairs={{4,0},{8,4},{12,8},{14,12},{10,14},{6,10},{2,6},{0,2},{5,1},{9,5},... | collective-permute-start | bytes 786440 | tf_op jit(solution)/shard_map/ppermute | solution.py:142
  76.5 11.2 %collective-permute-start.24 = (bf16[256,512]{1,0:T(8,128)(2,1)}, bf16[256,512]{1,0:T(8,128)(2,1)}, u32[]{:S(2)}, u32[]{:S(2)}) collective-permute-start(bf16[256,512]{1,0:T(8,128)(2,1)} %collective-permute-done.20.refs_1_), channel_id=1, source_target_pairs={{0,4},{4,8},{8,12},{12,14},{14,10},{10,6},{6,2},{2,0},{1,5},{5,9},... | collective-permute-start | bytes 786440 | tf_op jit(solution)/shard_map/ppermute | solution.py:142
  78.1 11.2 %collective-permute-start.19 = (bf16[256,512]{1,0:T(8,128)(2,1)}, bf16[256,512]{1,0:T(8,128)(2,1)}, u32[]{:S(2)}, u32[]{:S(2)}) collective-permute-start(bf16[256,512]{1,0:T(8,128)(2,1)} %collective-permute-done.15.refs_0_), channel_id=1, source_target_pairs={{0,4},{4,8},{8,12},{12,14},{14,10},{10,6},{6,2},{2,0},{1,5},{5,9},... | collective-permute-start | bytes 786440 | tf_op jit(solution)/shard_map/ppermute | solution.py:142
  79.7 11.2 %copy-start.7 = (s32[4]{0:T(128)S(1)}, s32[4]{0:T(128)}, u32[]{:S(2)}) copy-start(s32[4]{0:T(128)} %param.13) | copy-start | bytes 52
  83.6 11.5 %collective-permute-start.29 = (bf16[256,512]{1,0:T(8,128)(2,1)}, bf16[256,512]{1,0:T(8,128)(2,1)}, u32[]{:S(2)}, u32[]{:S(2)}) collective-permute-start(bf16[256,512]{1,0:T(8,128)(2,1)} %collective-permute-done.28.refs_3_), channel_id=1, source_target_pairs={{4,0},{8,4},{12,8},{14,12},{10,14},{6,10},{2,6},{0,2},{5,1},{9,5},... | collective-permute-start | bytes 786440 | tf_op jit(solution)/shard_map/ppermute | solution.py:142
  87.3 8.3 %collective-permute-start.27 = (bf16[256,512]{1,0:T(8,128)(2,1)}, bf16[256,512]{1,0:T(8,128)(2,1)}, u32[]{:S(2)}, u32[]{:S(2)}) collective-permute-start(bf16[256,512]{1,0:T(8,128)(2,1)} %collective-permute-done.26.refs_2_), channel_id=1, source_target_pairs={{4,0},{8,4},{12,8},{14,12},{10,14},{6,10},{2,6},{0,2},{5,1},{9,5},... | collective-permute-start | bytes 786440 | tf_op jit(solution)/shard_map/ppermute | solution.py:142
  87.7 7.8 %collective-permute-start.25 = (bf16[256,512]{1,0:T(8,128)(2,1)}, bf16[256,512]{1,0:T(8,128)(2,1)}, u32[]{:S(2)}, u32[]{:S(2)}) collective-permute-start(bf16[256,512]{1,0:T(8,128)(2,1)} %collective-permute-done.24.refs_1_), channel_id=1, source_target_pairs={{0,4},{4,8},{8,12},{12,14},{14,10},{10,6},{6,2},{2,0},{1,5},{5,9},... | collective-permute-start | bytes 786440 | tf_op jit(solution)/shard_map/ppermute | solution.py:142
  89.3 7.9 %collective-permute-start.23 = (bf16[256,512]{1,0:T(8,128)(2,1)}, bf16[256,512]{1,0:T(8,128)(2,1)}, u32[]{:S(2)}, u32[]{:S(2)}) collective-permute-start(bf16[256,512]{1,0:T(8,128)(2,1)} %collective-permute-done.19.refs_0_), channel_id=1, source_target_pairs={{0,4},{4,8},{8,12},{12,14},{14,10},{10,6},{6,2},{2,0},{1,5},{5,9},... | collective-permute-start | bytes 786440 | tf_op jit(solution)/shard_map/ppermute | solution.py:142
  102.1 2.9 %collective-permute-start.30 = (bf16[1024,512]{1,0:T(8,128)(2,1)}, bf16[1024,512]{1,0:T(8,128)(2,1)S(1)}, u32[]{:S(2)}, u32[]{:S(2)}) collective-permute-start(bf16[1024,512]{1,0:T(8,128)(2,1)} %get-tuple-element.78.have_ref), channel_id=1, source_target_pairs={{0,1},{1,0},{2,3},{3,2},{4,5},{5,4},{6,7},{7,6},{8,9},{9,8},{10,11... | collective-permute-start | bytes 3145736 | tf_op jit(solution)/shard_map/ppermute | solution.py:261
  109.7 14.6 %all-to-all-start = ((f32[8,72,128]{2,1,0:T(8,128)}), f32[8,72,128]{2,1,0:T(8,128)S(1)}, u32[]{:S(2)}, u32[]{:S(2)}) async-start(f32[8,72,128]{2,1,0:T(8,128)} %bitcast.25), calls=%async_computation | async-start | bytes 589824 | tf_op jit(solution)/shard_map/all_to_all | solution.py:288
  124.6 3.8 %collective-permute-start.31 = (bf16[64,128]{1,0:T(8,128)(2,1)S(1)}, bf16[64,128]{1,0:T(8,128)(2,1)S(1)}, u32[]{:S(2)}, u32[]{:S(2)}) collective-permute-start(bf16[64,128]{1,0:T(8,128)(2,1)S(1)} %shard_map.89), channel_id=1, source_target_pairs={{0,2},{2,0},{4,6},{6,4},{8,10},{10,8},{12,14},{14,12},{1,3},{3,1},... | collective-permute-start | bytes 49160 | tf_op jit(solution)/shard_map/ppermute | solution.py:292
  128.4 5.8 %collective-permute-start.32 = (bf16[128,128]{1,0:T(8,128)(2,1)S(1)}, bf16[128,128]{1,0:T(8,128)(2,1)S(1)}, u32[]{:S(2)}, u32[]{:S(2)}) collective-permute-start(bf16[128,128]{1,0:T(8,128)(2,1)S(1)} %pad_maximum_fusion.2), channel_id=1, source_target_pairs={{0,12},{2,14},{4,8},{6,10},{8,4},{10,6},{12,0},{14,2},{1,13},{3,15... | collective-permute-start | bytes 98312 | tf_op jit(solution)/shard_map/ppermute | solution.py:295
  129.7 5.3 %collective-permute-start.33 = (bf16[128,128]{1,0:T(8,128)(2,1)S(1)}, bf16[128,128]{1,0:T(8,128)(2,1)S(1)}, u32[]{:S(2)}, u32[]{:S(2)}) collective-permute-start(bf16[128,128]{1,0:T(8,128)(2,1)S(1)} %pad_maximum_fusion.2), channel_id=1, source_target_pairs={{0,8},{2,10},{4,12},{6,14},{8,0},{10,2},{12,4},{14,6},{1,9},{3,11}... | collective-permute-start | bytes 98312 | tf_op jit(solution)/shard_map/ppermute | solution.py:295
  131.0 4.2 %collective-permute-start.34 = (bf16[128,128]{1,0:T(8,128)(2,1)S(1)}, bf16[128,128]{1,0:T(8,128)(2,1)S(1)}, u32[]{:S(2)}, u32[]{:S(2)}) collective-permute-start(bf16[128,128]{1,0:T(8,128)(2,1)S(1)} %pad_maximum_fusion.2), channel_id=1, source_target_pairs={{0,4},{2,6},{4,0},{6,2},{8,12},{10,14},{12,8},{14,10},{1,5},{3,7},... | collective-permute-start | bytes 98312 | tf_op jit(solution)/shard_map/ppermute | solution.py:295
  135.4 1.4 %collective-permute-start.35 = (bf16[16,1,4096]{2,0,1:T(8,128)(2,1)S(1)}, bf16[16,1,4096]{2,0,1:T(8,128)(2,1)S(1)}, u32[]{:S(2)}, u32[]{:S(2)}) collective-permute-start(bf16[16,1,4096]{2,0,1:T(8,128)(2,1)S(1)} %reshape.97), channel_id=1, source_target_pairs={{0,1},{1,0},{2,3},{3,2},{4,5},{5,4},{6,7},{7,6},{8,9},{9,8},{10,11... | collective-permute-start | bytes 393224 | tf_op jit(solution)/shard_map/ppermute | solution.py:305

commit v17 on v16

--- a/solution.py
+++ b/solution.py
@@ -143,7 +143,7 @@
         arriving = [(start_of(w, step), held[w * chains : (w + 1) * chains]) for w in range(2)]
         todo += arriving
         if step >= 3:
-            taken = 4 if step in (3, 4) else 2
+            taken = 4 if step in (3, last) else 2
             ready, todo = todo[:taken], todo[taken:]
             total, mark = add_pieces(tokens, theirs, ready, total)
     return add_pieces(tokens, theirs, todo, total, core)[0], early

time: 138 us -> 134 us (0.971)
  waiting for transfers between devices: 54.1 us -> 48.7 us
  starting transfers between devices: 41.8 us -> 43.4 us
    ppermute x28, waiting for transfers between devices: 38.8 us -> 33.4 us  [project(): held[k] = lax.ppermute(held[k], 'chip', ways[k])]
    ppermute x28, starting transfers between devices: 30.4 us -> 32 us  [project(): held[k] = lax.ppermute(held[k], 'chip', ways[k])]
  transfers between devices with their start and end apart: 37 -> 37, of which waited for: 20 -> 18; matrix products, arithmetic and copies ran while one was open for 4% -> 4% of each run, Pallas kernels for 17% -> 18%
where the time goes in v17:
time: 134 us; the launch traced here: 133 us
  waiting for transfers between devices  48.7 us (36%)
  starting transfers between devices  43.4 us (32%)
  Pallas kernels  32.6 us (24%)
  local copies, waits for them, and re-layouts  4.49 us (3%)
  other arithmetic  2.34 us (2%)
  matrix products  1.36 us (1%)
    ppermute x28, waiting for transfers between devices, project(): held[k] = lax.ppermute(held[k], 'chip', ways[k])  33.4 us
    ppermute x28, starting transfers between devices, project(): held[k] = lax.ppermute(held[k], 'chip', ways[k])  32 us
    pallas_call x6, Pallas kernels, add_pieces(): pl.pallas_call(kernel, out_shape=(jax.ShapeDtypeStruct((2 * tok_rows, wid...  27.5 us
    all_to_all x1, waiting for transfers between devices, on_device(): lax.all_to_all(flat, 'chip', split_axis=0, concat_axis=0, tiled=True)  8.6 us
    all_to_all x1, starting transfers between devices, on_device(): lax.all_to_all(flat, 'chip', split_axis=0, concat_axis=0, tiled=True)  4.82 us
    pallas_call x1, Pallas kernels, attend(): pl.pallas_call(kernel, out_shape=jax.ShapeDtypeStruct((chips, blocks + 1,...  4.66 us
    ppermute x3, starting transfers between devices, on_device(): lax.ppermute(couple, 'chip', [(c, c ^ 2 * d) for c in range(chips)])  4.45 us
  transfers between devices with their start and end apart: 37, of which 18 were waited for; matrix products, arithmetic and copies ran while one was open for 4% of the time, Pallas kernels for 18%

profile of v17, /device:TPU:0, one launch (start us, length us, event | category | flops | bytes accessed | tf_op | source)
XLA Modules:
  0.0 133.2 jit_solution(17837389587407527595)
XLA Ops:
  0.0 1.3 broadcast_select_fusion
  1.3 0.5 collective-permute-start.2
  1.9 2.6 %collective-permute-start = (bf16[256,512]{1,0:T(8,128)(2,1)S(1)}, bf16[256,512]{1,0:T(8,128)(2,1)S(1)}, u32[]{:S(2)}, u32[]{:S(2)}) collective-permute-start(bf16[256,512]{1,0:T(8,128)(2,1)S(1)} %get-tuple-element.88), channel_id=1, source_target_pairs={{0,4},{4,8},{8,12},{12,14},{14,10},{10,6},{6,2},{2,0},{1,5},{5,9},... | collective-permute-start | bytes 786440 | tf_op jit(solution)/shard_map/ppermute | solution.py:142
  4.5 1.6 %collective-permute-start.1 = (bf16[256,512]{1,0:T(8,128)(2,1)S(1)}, bf16[256,512]{1,0:T(8,128)(2,1)S(1)}, u32[]{:S(2)}, u32[]{:S(2)}) collective-permute-start(bf16[256,512]{1,0:T(8,128)(2,1)S(1)} %get-tuple-element.87), channel_id=1, source_target_pairs={{0,4},{4,8},{8,12},{12,14},{14,10},{10,6},{6,2},{2,0},{1,5},{5,9},... | collective-permute-start | bytes 786440 | tf_op jit(solution)/shard_map/ppermute | solution.py:142
  6.1 0.5 collective-permute-start.3
  6.6 1.3 collective-permute-start.4
  7.9 3.7 %collective-permute-done.refs_2_ = bf16[256,512]{1,0:T(8,128)(2,1)S(1)} collective-permute-done((bf16[256,512]{1,0:T(8,128)(2,1)S(1)}, bf16[256,512]{1,0:T(8,128)(2,1)S(1)}, u32[]{:S(2)}, u32[]{:S(2)}) %collective-permute-start) | collective-permute-done | bytes 262176 | tf_op jit(solution)/shard_map/ppermute | solution.py:142
  11.6 5.4 %collective-permute-done.1.refs_3_ = bf16[256,512]{1,0:T(8,128)(2,1)S(1)} collective-permute-done((bf16[256,512]{1,0:T(8,128)(2,1)S(1)}, bf16[256,512]{1,0:T(8,128)(2,1)S(1)}, u32[]{:S(2)}, u32[]{:S(2)}) %collective-permute-start.1) | collective-permute-done | bytes 262176 | tf_op jit(solution)/shard_map/ppermute | solution.py:142
  17.1 2.9 %collective-permute-done.4.refs_5_ = bf16[256,512]{1,0:T(8,128)(2,1)S(1)} collective-permute-done((bf16[256,512]{1,0:T(8,128)(2,1)S(1)}, bf16[256,512]{1,0:T(8,128)(2,1)S(1)}, u32[]{:S(2)}, u32[]{:S(2)}) %collective-permute-start.4) | collective-permute-done | bytes 262176 | tf_op jit(solution)/shard_map/ppermute | solution.py:142
  20.0 0.4 collective-permute-start.11
  20.4 1.6 %collective-permute-start.6 = (bf16[256,512]{1,0:T(8,128)(2,1)S(1)}, bf16[256,512]{1,0:T(8,128)(2,1)}, u32[]{:S(2)}, u32[]{:S(2)}) collective-permute-start(bf16[256,512]{1,0:T(8,128)(2,1)S(1)} %collective-permute-done.refs_2_), channel_id=1, source_target_pairs={{0,4},{4,8},{8,12},{12,14},{14,10},{10,6},{6,2},{2,0},{1,5},{5,9},... | collective-permute-start | bytes 786440 | tf_op jit(solution)/shard_map/ppermute | solution.py:142
  22.0 1.6 %collective-permute-start.9 = (bf16[256,512]{1,0:T(8,128)(2,1)S(1)}, bf16[256,512]{1,0:T(8,128)(2,1)}, u32[]{:S(2)}, u32[]{:S(2)}) collective-permute-start(bf16[256,512]{1,0:T(8,128)(2,1)S(1)} %collective-permute-done.1.refs_3_), channel_id=1, source_target_pairs={{0,4},{4,8},{8,12},{12,14},{14,10},{10,6},{6,2},{2,0},{1,5},{5,9},... | collective-permute-start | bytes 786440 | tf_op jit(solution)/shard_map/ppermute | solution.py:142
  23.6 0.4 collective-permute-start.10
  24.1 5.1 %collective-permute-done.11.refs_3_ = bf16[256,512]{1,0:T(8,128)(2,1)} collective-permute-done((bf16[256,512]{1,0:T(8,128)(2,1)S(1)}, bf16[256,512]{1,0:T(8,128)(2,1)}, u32[]{:S(2)}, u32[]{:S(2)}) %collective-permute-start.11) | collective-permute-done | bytes 262176 | tf_op jit(solution)/shard_map/ppermute | solution.py:142
  29.2 0.4 collective-permute-start.15
  29.7 1.6 %collective-permute-start.7 = (bf16[256,512]{1,0:T(8,128)(2,1)}, bf16[256,512]{1,0:T(8,128)(2,1)}, u32[]{:S(2)}, u32[]{:S(2)}) collective-permute-start(bf16[256,512]{1,0:T(8,128)(2,1)} %collective-permute-done.6.refs_0_), channel_id=1, source_target_pairs={{0,4},{4,8},{8,12},{12,14},{14,10},{10,6},{6,2},{2,0},{1,5},{5,9},... | collective-permute-start | bytes 786440 | tf_op jit(solution)/shard_map/ppermute | solution.py:142
  31.2 4.0 %collective-permute-done.9.refs_1_ = bf16[256,512]{1,0:T(8,128)(2,1)} collective-permute-done((bf16[256,512]{1,0:T(8,128)(2,1)S(1)}, bf16[256,512]{1,0:T(8,128)(2,1)}, u32[]{:S(2)}, u32[]{:S(2)}) %collective-permute-start.9) | collective-permute-done | bytes 262176 | tf_op jit(solution)/shard_map/ppermute | solution.py:142
  35.3 1.6 %collective-permute-start.13 = (bf16[256,512]{1,0:T(8,128)(2,1)}, bf16[256,512]{1,0:T(8,128)(2,1)}, u32[]{:S(2)}, u32[]{:S(2)}) collective-permute-start(bf16[256,512]{1,0:T(8,128)(2,1)} %collective-permute-done.9.refs_1_), channel_id=1, source_target_pairs={{0,4},{4,8},{8,12},{12,14},{14,10},{10,6},{6,2},{2,0},{1,5},{5,9},... | collective-permute-start | bytes 786440 | tf_op jit(solution)/shard_map/ppermute | solution.py:142
  36.9 0.4 collective-permute-start.14
  37.4 5.7 %shard_map.82 = (f32[1024,512]{1,0:T(8,128)S(1)}, f32[8,128]{1,0:T(8,128)}) custom-call(s32[4]{0:T(128)S(1)} %pad_add_fusion.1.places_ref, bf16[512,8192]{1,0:T(8,128)(2,1)} %mine_ref.11, bf16[512,8192]{1,0:T(8,128)(2,1)} %collective-permute-done.5.theirs_ref, bf16[512,512]{1,0:T(8,128)(2,1)S(1)} %get-tuple-element.84.refs_0_, ...), custom_call_target="tpu_custom_call" | custom-call | flops 2147483648 | bytes 4194304 | tf_op jit(solution)/shard_map/pallas_call | solution.py:73
  43.1 1.5 %collective-permute-start.19 = (bf16[256,512]{1,0:T(8,128)(2,1)}, bf16[256,512]{1,0:T(8,128)(2,1)}, u32[]{:S(2)}, u32[]{:S(2)}) collective-permute-start(bf16[256,512]{1,0:T(8,128)(2,1)} %collective-permute-done.15.refs_3_), channel_id=1, source_target_pairs={{4,0},{8,4},{12,8},{14,12},{10,14},{6,10},{2,6},{0,2},{5,1},{9,5},... | collective-permute-start | bytes 786440 | tf_op jit(solution)/shard_map/ppermute | solution.py:142
  44.7 1.8 %collective-permute-done.14.refs_2_ = bf16[256,512]{1,0:T(8,128)(2,1)} collective-permute-done((bf16[256,512]{1,0:T(8,128)(2,1)}, bf16[256,512]{1,0:T(8,128)(2,1)}, u32[]{:S(2)}, u32[]{:S(2)}) %collective-permute-start.14) | collective-permute-done | bytes 262176 | tf_op jit(solution)/shard_map/ppermute | solution.py:142
  46.4 2.0 %collective-permute-start.17 = (bf16[256,512]{1,0:T(8,128)(2,1)}, bf16[256,512]{1,0:T(8,128)(2,1)}, u32[]{:S(2)}, u32[]{:S(2)}) collective-permute-start(bf16[256,512]{1,0:T(8,128)(2,1)} %collective-permute-done.13.refs_1_), channel_id=1, source_target_pairs={{0,4},{4,8},{8,12},{12,14},{14,10},{10,6},{6,2},{2,0},{1,5},{5,9},... | collective-permute-start | bytes 786440 | tf_op jit(solution)/shard_map/ppermute | solution.py:142
  48.4 1.6 %collective-permute-start.8 = (bf16[256,512]{1,0:T(8,128)(2,1)}, bf16[256,512]{1,0:T(8,128)(2,1)}, u32[]{:S(2)}, u32[]{:S(2)}) collective-permute-start(bf16[256,512]{1,0:T(8,128)(2,1)} %collective-permute-done.7.refs_0_), channel_id=1, source_target_pairs={{0,4},{4,8},{8,12},{12,14},{14,10},{10,6},{6,2},{2,0},{1,5},{5,9},... | collective-permute-start | bytes 786440 | tf_op jit(solution)/shard_map/ppermute | solution.py:142
  50.2 1.3 constant_dynamic-slice_fusion.1
  51.5 3.9 %shard_map.83 = (f32[1024,512]{1,0:T(8,128)S(1)}, f32[8,128]{1,0:T(8,128)}) custom-call(s32[2]{0:T(128)S(1)} %pad_add_fusion.2.places_ref, bf16[512,8192]{1,0:T(8,128)(2,1)} %mine_ref.11, bf16[512,8192]{1,0:T(8,128)(2,1)} %collective-permute-done.5.theirs_ref, bf16[256,512]{1,0:T(8,128)(2,1)} %collective-permute-done.6.refs_0_, ...), custom_call_target="tpu_custom_call", output_to_operand_aliasing={{0}: (7, {})} | custom-call | flops 1073741824 | bytes 2097152 | tf_op jit(solution)/shard_map/pallas_call | solution.py:73
  55.4 0.5 collective-permute-start.27
  55.9 1.6 %collective-permute-done.18.refs_2_ = bf16[256,512]{1,0:T(8,128)(2,1)} collective-permute-done((bf16[256,512]{1,0:T(8,128)(2,1)}, bf16[256,512]{1,0:T(8,128)(2,1)}, u32[]{:S(2)}, u32[]{:S(2)}) %collective-permute-start.18) | collective-permute-done | bytes 262176 | tf_op jit(solution)/shard_map/ppermute | solution.py:142
  57.5 0.5 collective-permute-start.24
  58.0 1.5 %collective-permute-start.21 = (bf16[256,512]{1,0:T(8,128)(2,1)}, bf16[256,512]{1,0:T(8,128)(2,1)}, u32[]{:S(2)}, u32[]{:S(2)}) collective-permute-start(bf16[256,512]{1,0:T(8,128)(2,1)} %collective-permute-done.17.refs_1_), channel_id=1, source_target_pairs={{0,4},{4,8},{8,12},{12,14},{14,10},{10,6},{6,2},{2,0},{1,5},{5,9},... | collective-permute-start | bytes 786440 | tf_op jit(solution)/shard_map/ppermute | solution.py:142
  59.5 0.7 collective-permute-done.8.refs_0_
  60.2 1.4 %collective-permute-start.12 = (bf16[256,512]{1,0:T(8,128)(2,1)}, bf16[256,512]{1,0:T(8,128)(2,1)}, u32[]{:S(2)}, u32[]{:S(2)}) collective-permute-start(bf16[256,512]{1,0:T(8,128)(2,1)} %collective-permute-done.8.refs_0_), channel_id=1, source_target_pairs={{0,4},{4,8},{8,12},{12,14},{14,10},{10,6},{6,2},{2,0},{1,5},{5,9},... | collective-permute-start | bytes 786440 | tf_op jit(solution)/shard_map/ppermute | solution.py:142
  61.7 3.9 %shard_map.84 = (f32[1024,512]{1,0:T(8,128)S(1)}, f32[8,128]{1,0:T(8,128)}) custom-call(s32[2]{0:T(128)S(1)} %pad_add_fusion.3.places_ref, bf16[512,8192]{1,0:T(8,128)(2,1)} %mine_ref.11, bf16[512,8192]{1,0:T(8,128)(2,1)} %collective-permute-done.5.theirs_ref, bf16[256,512]{1,0:T(8,128)(2,1)} %collective-permute-done.7.refs_0_, ...), custom_call_target="tpu_custom_call", output_to_operand_aliasing={{0}: (7, {})} | custom-call | flops 1073741824 | bytes 2097152 | tf_op jit(solution)/shard_map/pallas_call | solution.py:73
  65.6 1.1 collective-permute-start.28
  66.7 4.0 %collective-permute-done.24.refs_2_ = bf16[256,512]{1,0:T(8,128)(2,1)} collective-permute-done((bf16[256,512]{1,0:T(8,128)(2,1)}, bf16[256,512]{1,0:T(8,128)(2,1)}, u32[]{:S(2)}, u32[]{:S(2)}) %collective-permute-start.24) | collective-permute-done | bytes 262176 | tf_op jit(solution)/shard_map/ppermute | solution.py:142
  70.7 0.4 collective-permute-start.25
  71.1 1.6 %collective-permute-start.22 = (bf16[256,512]{1,0:T(8,128)(2,1)}, bf16[256,512]{1,0:T(8,128)(2,1)}, u32[]{:S(2)}, u32[]{:S(2)}) collective-permute-start(bf16[256,512]{1,0:T(8,128)(2,1)} %collective-permute-done.21.refs_1_), channel_id=1, source_target_pairs={{0,4},{4,8},{8,12},{12,14},{14,10},{10,6},{6,2},{2,0},{1,5},{5,9},... | collective-permute-start | bytes 786440 | tf_op jit(solution)/shard_map/ppermute | solution.py:142
  72.7 1.5 %collective-permute-start.16 = (bf16[256,512]{1,0:T(8,128)(2,1)}, bf16[256,512]{1,0:T(8,128)(2,1)}, u32[]{:S(2)}, u32[]{:S(2)}) collective-permute-start(bf16[256,512]{1,0:T(8,128)(2,1)} %collective-permute-done.12.refs_0_), channel_id=1, source_target_pairs={{0,4},{4,8},{8,12},{12,14},{14,10},{10,6},{6,2},{2,0},{1,5},{5,9},... | collective-permute-start | bytes 786440 | tf_op jit(solution)/shard_map/ppermute | solution.py:142
  74.5 3.9 %shard_map.85 = (f32[1024,512]{1,0:T(8,128)S(1)}, f32[8,128]{1,0:T(8,128)}) custom-call(s32[2]{0:T(128)S(1)} %pad_add_fusion.4.places_ref, bf16[512,8192]{1,0:T(8,128)(2,1)} %mine_ref.11, bf16[512,8192]{1,0:T(8,128)(2,1)} %collective-permute-done.5.theirs_ref, bf16[256,512]{1,0:T(8,128)(2,1)} %collective-permute-done.8.refs_0_, ...), custom_call_target="tpu_custom_call", output_to_operand_aliasing={{0}: (7, {})} | custom-call | flops 1073741824 | bytes 2097152 | tf_op jit(solution)/shard_map/pallas_call | solution.py:73
  78.5 0.6 collective-permute-start.29
  79.0 2.9 %collective-permute-done.25.refs_6_ = bf16[256,512]{1,0:T(8,128)(2,1)} collective-permute-done((bf16[256,512]{1,0:T(8,128)(2,1)}, bf16[256,512]{1,0:T(8,128)(2,1)}, u32[]{:S(2)}, u32[]{:S(2)}) %collective-permute-start.25) | collective-permute-done | bytes 262176 | tf_op jit(solution)/shard_map/ppermute | solution.py:142
  81.9 0.4 collective-permute-start.26
  82.3 1.6 %collective-permute-start.23 = (bf16[256,512]{1,0:T(8,128)(2,1)}, bf16[256,512]{1,0:T(8,128)(2,1)S(1)}, u32[]{:S(2)}, u32[]{:S(2)}) collective-permute-start(bf16[256,512]{1,0:T(8,128)(2,1)} %collective-permute-done.22.refs_5_), channel_id=1, source_target_pairs={{0,4},{4,8},{8,12},{12,14},{14,10},{10,6},{6,2},{2,0},{1,5},{5,9},... | collective-permute-start | bytes 786440 | tf_op jit(solution)/shard_map/ppermute | solution.py:142
  83.9 1.5 %collective-permute-start.20 = (bf16[256,512]{1,0:T(8,128)(2,1)}, bf16[256,512]{1,0:T(8,128)(2,1)S(1)}, u32[]{:S(2)}, u32[]{:S(2)}) collective-permute-start(bf16[256,512]{1,0:T(8,128)(2,1)} %collective-permute-done.16.refs_4_), channel_id=1, source_target_pairs={{0,4},{4,8},{8,12},{12,14},{14,10},{10,6},{6,2},{2,0},{1,5},{5,9},... | collective-permute-start | bytes 786440 | tf_op jit(solution)/shard_map/ppermute | solution.py:142
  85.5 6.0 %shard_map.86 = (f32[1024,512]{1,0:T(8,128)S(1)}, f32[8,128]{1,0:T(8,128)}) custom-call(s32[4]{0:T(128)S(1)} %pad_add_fusion.5.places_ref, bf16[512,8192]{1,0:T(8,128)(2,1)} %mine_ref.11, bf16[512,8192]{1,0:T(8,128)(2,1)} %collective-permute-done.5.theirs_ref, bf16[256,512]{1,0:T(8,128)(2,1)} %collective-permute-done.12.refs_0_, ...), custom_call_target="tpu_custom_call", output_to_operand_aliasing={{0}: (11, {})} | custom-call | flops 2147483648 | bytes 4194304 | tf_op jit(solution)/shard_map/pallas_call | solution.py:73
  91.6 1.4 %collective-permute-done.20.refs_0_ = bf16[256,512]{1,0:T(8,128)(2,1)S(1)} collective-permute-done((bf16[256,512]{1,0:T(8,128)(2,1)}, bf16[256,512]{1,0:T(8,128)(2,1)S(1)}, u32[]{:S(2)}, u32[]{:S(2)}) %collective-permute-start.20) | collective-permute-done | bytes 262176 | tf_op jit(solution)/shard_map/ppermute | solution.py:142
  93.0 4.2 %shard_map.87 = (bf16[1024,512]{1,0:T(8,128)(2,1)}, f32[8,128]{1,0:T(8,128)}) custom-call(s32[4]{0:T(128)S(1)} %pad_add_fusion.places_ref, bf16[512,8192]{1,0:T(8,128)(2,1)} %mine_ref.11, bf16[512,8192]{1,0:T(8,128)(2,1)} %collective-permute-done.5.theirs_ref, bf16[256,512]{1,0:T(8,128)(2,1)S(1)} %collective-permute-done.20.refs_0_, ...), custom_call_target="tpu_custom_call" | custom-call | flops 1073741824 | bytes 2097152 | tf_op jit(solution)/shard_map/pallas_call | solution.py:73
  97.5 0.8 reshape.89
  98.7 0.7 fusion.17
  99.4 0.7 collective-permute-done.30.got_ref
  100.1 4.7 %shard_map.88 = f32[8,9,8,128]{3,2,1,0:T(8,128)} custom-call(s32[1]{0:T(128)} %bitcast.core_ref, bf16[1024,512]{1,0:T(8,128)(2,1)} %get-tuple-element.78.have_ref, bf16[1024,512]{1,0:T(8,128)(2,1)S(1)} %collective-permute-done.30.got_ref, bf16[512,512]{1,0:T(8,128)(2,1)S(1)} %get-tuple-element.79.key_up_ref, ...), custom_call_target="tpu_custom_call" | custom-call | flops 1342177280 | bytes 2097152 | tf_op jit(solution)/shard_map/pallas_call | solution.py:194
  104.8 4.8 %all-to-all-start = ((f32[8,72,128]{2,1,0:T(8,128)}), f32[8,72,128]{2,1,0:T(8,128)S(1)}, u32[]{:S(2)}, u32[]{:S(2)}) async-start(f32[8,72,128]{2,1,0:T(8,128)} %bitcast.25), calls=%async_computation | async-start | bytes 589824 | tf_op jit(solution)/shard_map/all_to_all | solution.py:288
  109.6 0.3 convolution_bitcast_fusion
  110.9 8.6 %all-to-all-done = f32[8,72,128]{2,1,0:T(8,128)S(1)} async-done(((f32[8,72,128]{2,1,0:T(8,128)}), f32[8,72,128]{2,1,0:T(8,128)S(1)}, u32[]{:S(2)}, u32[]{:S(2)}) %all-to-all-start) | async-done | bytes 294944 | tf_op jit(solution)/shard_map/all_to_all | solution.py:288
  119.5 0.4 shard_map.89
  119.8 1.5 %collective-permute-start.31 = (bf16[64,128]{1,0:T(8,128)(2,1)S(1)}, bf16[64,128]{1,0:T(8,128)(2,1)S(1)}, u32[]{:S(2)}, u32[]{:S(2)}) collective-permute-start(bf16[64,128]{1,0:T(8,128)(2,1)S(1)} %shard_map.89), channel_id=1, source_target_pairs={{0,2},{2,0},{4,6},{6,4},{8,10},{10,8},{12,14},{14,12},{1,3},{3,1},... | collective-permute-start | bytes 49160 | tf_op jit(solution)/shard_map/ppermute | solution.py:292
  121.4 2.3 %collective-permute-done.31 = bf16[64,128]{1,0:T(8,128)(2,1)S(1)} collective-permute-done((bf16[64,128]{1,0:T(8,128)(2,1)S(1)}, bf16[64,128]{1,0:T(8,128)(2,1)S(1)}, u32[]{:S(2)}, u32[]{:S(2)}) %collective-permute-start.31) | collective-permute-done | bytes 16416 | tf_op jit(solution)/shard_map/ppermute | solution.py:292
  123.7 1.2 collective-permute-start.32
  124.9 1.3 %collective-permute-start.33 = (bf16[128,128]{1,0:T(8,128)(2,1)S(1)}, bf16[128,128]{1,0:T(8,128)(2,1)S(1)}, u32[]{:S(2)}, u32[]{:S(2)}) collective-permute-start(bf16[128,128]{1,0:T(8,128)(2,1)S(1)} %pad_maximum_fusion.2), channel_id=1, source_target_pairs={{0,8},{2,10},{4,12},{6,14},{8,0},{10,2},{12,4},{14,6},{1,9},{3,11}... | collective-permute-start | bytes 98312 | tf_op jit(solution)/shard_map/ppermute | solution.py:295
  126.3 1.9 %collective-permute-start.34 = (bf16[128,128]{1,0:T(8,128)(2,1)S(1)}, bf16[128,128]{1,0:T(8,128)(2,1)S(1)}, u32[]{:S(2)}, u32[]{:S(2)}) collective-permute-start(bf16[128,128]{1,0:T(8,128)(2,1)S(1)} %pad_maximum_fusion.2), channel_id=1, source_target_pairs={{0,4},{2,6},{4,0},{6,2},{8,12},{10,14},{12,8},{14,10},{1,5},{3,7},... | collective-permute-start | bytes 98312 | tf_op jit(solution)/shard_map/ppermute | solution.py:295
  128.1 1.3 collective-permute-done.32
  129.4 0.8 collective-permute-done.33
  130.7 1.3 %collective-permute-done.35 = bf16[16,1,4096]{2,0,1:T(8,128)(2,1)S(1)} collective-permute-done((bf16[16,1,4096]{2,0,1:T(8,128)(2,1)S(1)}, bf16[16,1,4096]{2,0,1:T(8,128)(2,1)S(1)}, u32[]{:S(2)}, u32[]{:S(2)}) %collective-permute-start.35) | collective-permute-done | bytes 131104 | tf_op jit(solution)/shard_map/ppermute | solution.py:305
  132.4 0.9 reshape.98
  (79 shorter events, 3.4 us)
Async XLA Ops:
  0.0 50.0 %copy-start = (bf16[4,4,8192]{2,1,0:T(4,128)(2,1)S(1)}, bf16[4,4,8192]{2,1,0:T(4,128)(2,1)}, u32[]{:S(2)}) copy-start(bf16[4,4,8192]{2,1,0:T(4,128)(2,1)} %param.14) | copy-start | bytes 786436
  1.3 4.8 %collective-permute-start.2 = (bf16[512,512]{1,0:T(8,128)(2,1)S(1)}, bf16[512,512]{1,0:T(8,128)(2,1)S(1)}, u32[]{:S(2)}, u32[]{:S(2)}) collective-permute-start(bf16[512,512]{1,0:T(8,128)(2,1)S(1)} %get-tuple-element.83), channel_id=1, source_target_pairs={{0,1},{1,0},{2,3},{3,2},{4,5},{5,4},{6,7},{7,6},{8,9},{9,8},{10,11... | collective-permute-start | bytes 1572872 | tf_op jit(solution)/shard_map/ppermute | solution.py:103
  1.9 9.7 %collective-permute-start = (bf16[256,512]{1,0:T(8,128)(2,1)S(1)}, bf16[256,512]{1,0:T(8,128)(2,1)S(1)}, u32[]{:S(2)}, u32[]{:S(2)}) collective-permute-start(bf16[256,512]{1,0:T(8,128)(2,1)S(1)} %get-tuple-element.88), channel_id=1, source_target_pairs={{0,4},{4,8},{8,12},{12,14},{14,10},{10,6},{6,2},{2,0},{1,5},{5,9},... | collective-permute-start | bytes 786440 | tf_op jit(solution)/shard_map/ppermute | solution.py:142
  4.5 12.5 %collective-permute-start.1 = (bf16[256,512]{1,0:T(8,128)(2,1)S(1)}, bf16[256,512]{1,0:T(8,128)(2,1)S(1)}, u32[]{:S(2)}, u32[]{:S(2)}) collective-permute-start(bf16[256,512]{1,0:T(8,128)(2,1)S(1)} %get-tuple-element.87), channel_id=1, source_target_pairs={{0,4},{4,8},{8,12},{12,14},{14,10},{10,6},{6,2},{2,0},{1,5},{5,9},... | collective-permute-start | bytes 786440 | tf_op jit(solution)/shard_map/ppermute | solution.py:142
  6.1 10.9 %collective-permute-start.3 = (bf16[256,512]{1,0:T(8,128)(2,1)S(1)}, bf16[256,512]{1,0:T(8,128)(2,1)S(1)}, u32[]{:S(2)}, u32[]{:S(2)}) collective-permute-start(bf16[256,512]{1,0:T(8,128)(2,1)S(1)} %get-tuple-element.86), channel_id=1, source_target_pairs={{4,0},{8,4},{12,8},{14,12},{10,14},{6,10},{2,6},{0,2},{5,1},{9,5},... | collective-permute-start | bytes 786440 | tf_op jit(solution)/shard_map/ppermute | solution.py:142
  6.6 13.3 %collective-permute-start.4 = (bf16[256,512]{1,0:T(8,128)(2,1)S(1)}, bf16[256,512]{1,0:T(8,128)(2,1)S(1)}, u32[]{:S(2)}, u32[]{:S(2)}) collective-permute-start(bf16[256,512]{1,0:T(8,128)(2,1)S(1)} %get-tuple-element.85), channel_id=1, source_target_pairs={{4,0},{8,4},{12,8},{14,12},{10,14},{6,10},{2,6},{0,2},{5,1},{9,5},... | collective-permute-start | bytes 786440 | tf_op jit(solution)/shard_map/ppermute | solution.py:142
  11.6 25.8 %copy-start.1 = (bf16[256,512]{1,0:T(8,128)(2,1)}, bf16[256,512]{1,0:T(8,128)(2,1)S(1)}, u32[]{:S(2)}) copy-start(bf16[256,512]{1,0:T(8,128)(2,1)S(1)} %collective-permute-done.refs_2_) | copy-start | bytes 786436
  17.0 20.3 %copy-start.2 = (bf16[256,512]{1,0:T(8,128)(2,1)}, bf16[256,512]{1,0:T(8,128)(2,1)S(1)}, u32[]{:S(2)}) copy-start(bf16[256,512]{1,0:T(8,128)(2,1)S(1)} %collective-permute-done.1.refs_3_) | copy-start | bytes 786436
  17.0 20.3 %copy-start.3 = (bf16[256,512]{1,0:T(8,128)(2,1)}, bf16[256,512]{1,0:T(8,128)(2,1)S(1)}, u32[]{:S(2)}) copy-start(bf16[256,512]{1,0:T(8,128)(2,1)S(1)} %collective-permute-done.3.refs_4_) | copy-start | bytes 786436
  20.0 17.4 %copy-start.4 = (bf16[256,512]{1,0:T(8,128)(2,1)}, bf16[256,512]{1,0:T(8,128)(2,1)S(1)}, u32[]{:S(2)}) copy-start(bf16[256,512]{1,0:T(8,128)(2,1)S(1)} %collective-permute-done.4.refs_5_) | copy-start | bytes 786436
  20.0 17.4 %collective-permute-start.5 = (bf16[512,8192]{1,0:T(8,128)(2,1)}, bf16[512,8192]{1,0:T(8,128)(2,1)}, u32[]{:S(2)}, u32[]{:S(2)}) collective-permute-start(bf16[512,8192]{1,0:T(8,128)(2,1)} %mine_ref.11), channel_id=1, source_target_pairs={{0,1},{1,0},{2,3},{3,2},{4,5},{5,4},{6,7},{7,6},{8,9},{9,8},{10,11... | collective-permute-start | bytes 25165832 | tf_op jit(solution)/shard_map/ppermute | solution.py:133
  20.0 9.2 %collective-permute-start.11 = (bf16[256,512]{1,0:T(8,128)(2,1)S(1)}, bf16[256,512]{1,0:T(8,128)(2,1)}, u32[]{:S(2)}, u32[]{:S(2)}) collective-permute-start(bf16[256,512]{1,0:T(8,128)(2,1)S(1)} %collective-permute-done.4.refs_5_), channel_id=1, source_target_pairs={{4,0},{8,4},{12,8},{14,12},{10,14},{6,10},{2,6},{0,2},{5,1},{9,5},... | collective-permute-start | bytes 786440 | tf_op jit(solution)/shard_map/ppermute | solution.py:142
  20.4 9.2 %collective-permute-start.6 = (bf16[256,512]{1,0:T(8,128)(2,1)S(1)}, bf16[256,512]{1,0:T(8,128)(2,1)}, u32[]{:S(2)}, u32[]{:S(2)}) collective-permute-start(bf16[256,512]{1,0:T(8,128)(2,1)S(1)} %collective-permute-done.refs_2_), channel_id=1, source_target_pairs={{0,4},{4,8},{8,12},{12,14},{14,10},{10,6},{6,2},{2,0},{1,5},{5,9},... | collective-permute-start | bytes 786440 | tf_op jit(solution)/shard_map/ppermute | solution.py:142
  22.0 13.3 %collective-permute-start.9 = (bf16[256,512]{1,0:T(8,128)(2,1)S(1)}, bf16[256,512]{1,0:T(8,128)(2,1)}, u32[]{:S(2)}, u32[]{:S(2)}) collective-permute-start(bf16[256,512]{1,0:T(8,128)(2,1)S(1)} %collective-permute-done.1.refs_3_), channel_id=1, source_target_pairs={{0,4},{4,8},{8,12},{12,14},{14,10},{10,6},{6,2},{2,0},{1,5},{5,9},... | collective-permute-start | bytes 786440 | tf_op jit(solution)/shard_map/ppermute | solution.py:142
  23.6 13.3 %collective-permute-start.10 = (bf16[256,512]{1,0:T(8,128)(2,1)S(1)}, bf16[256,512]{1,0:T(8,128)(2,1)}, u32[]{:S(2)}, u32[]{:S(2)}) collective-permute-start(bf16[256,512]{1,0:T(8,128)(2,1)S(1)} %collective-permute-done.3.refs_4_), channel_id=1, source_target_pairs={{4,0},{8,4},{12,8},{14,12},{10,14},{6,10},{2,6},{0,2},{5,1},{9,5},... | collective-permute-start | bytes 786440 | tf_op jit(solution)/shard_map/ppermute | solution.py:142
  29.2 13.9 %collective-permute-start.15 = (bf16[256,512]{1,0:T(8,128)(2,1)}, bf16[256,512]{1,0:T(8,128)(2,1)}, u32[]{:S(2)}, u32[]{:S(2)}) collective-permute-start(bf16[256,512]{1,0:T(8,128)(2,1)} %collective-permute-done.11.refs_3_), channel_id=1, source_target_pairs={{4,0},{8,4},{12,8},{14,12},{10,14},{6,10},{2,6},{0,2},{5,1},{9,5},... | collective-permute-start | bytes 786440 | tf_op jit(solution)/shard_map/ppermute | solution.py:142
  29.7 18.8 %collective-permute-start.7 = (bf16[256,512]{1,0:T(8,128)(2,1)}, bf16[256,512]{1,0:T(8,128)(2,1)}, u32[]{:S(2)}, u32[]{:S(2)}) collective-permute-start(bf16[256,512]{1,0:T(8,128)(2,1)} %collective-permute-done.6.refs_0_), channel_id=1, source_target_pairs={{0,4},{4,8},{8,12},{12,14},{14,10},{10,6},{6,2},{2,0},{1,5},{5,9},... | collective-permute-start | bytes 786440 | tf_op jit(solution)/shard_map/ppermute | solution.py:142
  35.3 11.1 %collective-permute-start.13 = (bf16[256,512]{1,0:T(8,128)(2,1)}, bf16[256,512]{1,0:T(8,128)(2,1)}, u32[]{:S(2)}, u32[]{:S(2)}) collective-permute-start(bf16[256,512]{1,0:T(8,128)(2,1)} %collective-permute-done.9.refs_1_), channel_id=1, source_target_pairs={{0,4},{4,8},{8,12},{12,14},{14,10},{10,6},{6,2},{2,0},{1,5},{5,9},... | collective-permute-start | bytes 786440 | tf_op jit(solution)/shard_map/ppermute | solution.py:142
  36.9 9.6 %collective-permute-start.14 = (bf16[256,512]{1,0:T(8,128)(2,1)}, bf16[256,512]{1,0:T(8,128)(2,1)}, u32[]{:S(2)}, u32[]{:S(2)}) collective-permute-start(bf16[256,512]{1,0:T(8,128)(2,1)} %collective-permute-done.10.refs_2_), channel_id=1, source_target_pairs={{4,0},{8,4},{12,8},{14,12},{10,14},{6,10},{2,6},{0,2},{5,1},{9,5},... | collective-permute-start | bytes 786440 | tf_op jit(solution)/shard_map/ppermute | solution.py:142
  43.1 12.3 %collective-permute-start.19 = (bf16[256,512]{1,0:T(8,128)(2,1)}, bf16[256,512]{1,0:T(8,128)(2,1)}, u32[]{:S(2)}, u32[]{:S(2)}) collective-permute-start(bf16[256,512]{1,0:T(8,128)(2,1)} %collective-permute-done.15.refs_3_), channel_id=1, source_target_pairs={{4,0},{8,4},{12,8},{14,12},{10,14},{6,10},{2,6},{0,2},{5,1},{9,5},... | collective-permute-start | bytes 786440 | tf_op jit(solution)/shard_map/ppermute | solution.py:142
  46.4 11.1 %collective-permute-start.18 = (bf16[256,512]{1,0:T(8,128)(2,1)}, bf16[256,512]{1,0:T(8,128)(2,1)}, u32[]{:S(2)}, u32[]{:S(2)}) collective-permute-start(bf16[256,512]{1,0:T(8,128)(2,1)} %collective-permute-done.14.refs_2_), channel_id=1, source_target_pairs={{4,0},{8,4},{12,8},{14,12},{10,14},{6,10},{2,6},{0,2},{5,1},{9,5},... | collective-permute-start | bytes 786440 | tf_op jit(solution)/shard_map/ppermute | solution.py:142
  46.4 11.6 %collective-permute-start.17 = (bf16[256,512]{1,0:T(8,128)(2,1)}, bf16[256,512]{1,0:T(8,128)(2,1)}, u32[]{:S(2)}, u32[]{:S(2)}) collective-permute-start(bf16[256,512]{1,0:T(8,128)(2,1)} %collective-permute-done.13.refs_1_), channel_id=1, source_target_pairs={{0,4},{4,8},{8,12},{12,14},{14,10},{10,6},{6,2},{2,0},{1,5},{5,9},... | collective-permute-start | bytes 786440 | tf_op jit(solution)/shard_map/ppermute | solution.py:142
  48.4 11.8 %collective-permute-start.8 = (bf16[256,512]{1,0:T(8,128)(2,1)}, bf16[256,512]{1,0:T(8,128)(2,1)}, u32[]{:S(2)}, u32[]{:S(2)}) collective-permute-start(bf16[256,512]{1,0:T(8,128)(2,1)} %collective-permute-done.7.refs_0_), channel_id=1, source_target_pairs={{0,4},{4,8},{8,12},{12,14},{14,10},{10,6},{6,2},{2,0},{1,5},{5,9},... | collective-permute-start | bytes 786440 | tf_op jit(solution)/shard_map/ppermute | solution.py:142
  55.4 10.2 %collective-permute-start.27 = (bf16[256,512]{1,0:T(8,128)(2,1)}, bf16[256,512]{1,0:T(8,128)(2,1)}, u32[]{:S(2)}, u32[]{:S(2)}) collective-permute-start(bf16[256,512]{1,0:T(8,128)(2,1)} %collective-permute-done.19.refs_3_), channel_id=1, source_target_pairs={{4,0},{8,4},{12,8},{14,12},{10,14},{6,10},{2,6},{0,2},{5,1},{9,5},... | collective-permute-start | bytes 786440 | tf_op jit(solution)/shard_map/ppermute | solution.py:142
  57.5 13.2 %collective-permute-start.24 = (bf16[256,512]{1,0:T(8,128)(2,1)}, bf16[256,512]{1,0:T(8,128)(2,1)}, u32[]{:S(2)}, u32[]{:S(2)}) collective-permute-start(bf16[256,512]{1,0:T(8,128)(2,1)} %collective-permute-done.18.refs_2_), channel_id=1, source_target_pairs={{4,0},{8,4},{12,8},{14,12},{10,14},{6,10},{2,6},{0,2},{5,1},{9,5},... | collective-permute-start | bytes 786440 | tf_op jit(solution)/shard_map/ppermute | solution.py:142
  58.0 13.1 %collective-permute-start.21 = (bf16[256,512]{1,0:T(8,128)(2,1)}, bf16[256,512]{1,0:T(8,128)(2,1)}, u32[]{:S(2)}, u32[]{:S(2)}) collective-permute-start(bf16[256,512]{1,0:T(8,128)(2,1)} %collective-permute-done.17.refs_1_), channel_id=1, source_target_pairs={{0,4},{4,8},{8,12},{12,14},{14,10},{10,6},{6,2},{2,0},{1,5},{5,9},... | collective-permute-start | bytes 786440 | tf_op jit(solution)/shard_map/ppermute | solution.py:142
  60.2 12.5 %collective-permute-start.12 = (bf16[256,512]{1,0:T(8,128)(2,1)}, bf16[256,512]{1,0:T(8,128)(2,1)}, u32[]{:S(2)}, u32[]{:S(2)}) collective-permute-start(bf16[256,512]{1,0:T(8,128)(2,1)} %collective-permute-done.8.refs_0_), channel_id=1, source_target_pairs={{0,4},{4,8},{8,12},{12,14},{14,10},{10,6},{6,2},{2,0},{1,5},{5,9},... | collective-permute-start | bytes 786440 | tf_op jit(solution)/shard_map/ppermute | solution.py:142
  61.7 12.6 %copy-start.5 = (s32[4]{0:T(128)S(1)}, s32[4]{0:T(128)}, u32[]{:S(2)}) copy-start(s32[4]{0:T(128)} %param.13) | copy-start | bytes 52
  65.6 12.8 %collective-permute-start.28 = (bf16[256,512]{1,0:T(8,128)(2,1)}, bf16[256,512]{1,0:T(8,128)(2,1)}, u32[]{:S(2)}, u32[]{:S(2)}) collective-permute-start(bf16[256,512]{1,0:T(8,128)(2,1)} %collective-permute-done.27.refs_3_), channel_id=1, source_target_pairs={{4,0},{8,4},{12,8},{14,12},{10,14},{6,10},{2,6},{0,2},{5,1},{9,5},... | collective-permute-start | bytes 786440 | tf_op jit(solution)/shard_map/ppermute | solution.py:142
  70.7 11.2 %collective-permute-start.25 = (bf16[256,512]{1,0:T(8,128)(2,1)}, bf16[256,512]{1,0:T(8,128)(2,1)}, u32[]{:S(2)}, u32[]{:S(2)}) collective-permute-start(bf16[256,512]{1,0:T(8,128)(2,1)} %collective-permute-done.24.refs_2_), channel_id=1, source_target_pairs={{4,0},{8,4},{12,8},{14,12},{10,14},{6,10},{2,6},{0,2},{5,1},{9,5},... | collective-permute-start | bytes 786440 | tf_op jit(solution)/shard_map/ppermute | solution.py:142
  71.1 11.2 %collective-permute-start.22 = (bf16[256,512]{1,0:T(8,128)(2,1)}, bf16[256,512]{1,0:T(8,128)(2,1)}, u32[]{:S(2)}, u32[]{:S(2)}) collective-permute-start(bf16[256,512]{1,0:T(8,128)(2,1)} %collective-permute-done.21.refs_1_), channel_id=1, source_target_pairs={{0,4},{4,8},{8,12},{12,14},{14,10},{10,6},{6,2},{2,0},{1,5},{5,9},... | collective-permute-start | bytes 786440 | tf_op jit(solution)/shard_map/ppermute | solution.py:142
  72.7 11.2 %collective-permute-start.16 = (bf16[256,512]{1,0:T(8,128)(2,1)}, bf16[256,512]{1,0:T(8,128)(2,1)}, u32[]{:S(2)}, u32[]{:S(2)}) collective-permute-start(bf16[256,512]{1,0:T(8,128)(2,1)} %collective-permute-done.12.refs_0_), channel_id=1, source_target_pairs={{0,4},{4,8},{8,12},{12,14},{14,10},{10,6},{6,2},{2,0},{1,5},{5,9},... | collective-permute-start | bytes 786440 | tf_op jit(solution)/shard_map/ppermute | solution.py:142
  78.5 13.1 %collective-permute-start.29 = (bf16[256,512]{1,0:T(8,128)(2,1)}, bf16[256,512]{1,0:T(8,128)(2,1)S(1)}, u32[]{:S(2)}, u32[]{:S(2)}) collective-permute-start(bf16[256,512]{1,0:T(8,128)(2,1)} %collective-permute-done.28.refs_7_), channel_id=1, source_target_pairs={{4,0},{8,4},{12,8},{14,12},{10,14},{6,10},{2,6},{0,2},{5,1},{9,5},... | collective-permute-start | bytes 786440 | tf_op jit(solution)/shard_map/ppermute | solution.py:142
  81.9 9.7 %collective-permute-start.26 = (bf16[256,512]{1,0:T(8,128)(2,1)}, bf16[256,512]{1,0:T(8,128)(2,1)S(1)}, u32[]{:S(2)}, u32[]{:S(2)}) collective-permute-start(bf16[256,512]{1,0:T(8,128)(2,1)} %collective-permute-done.25.refs_6_), channel_id=1, source_target_pairs={{4,0},{8,4},{12,8},{14,12},{10,14},{6,10},{2,6},{0,2},{5,1},{9,5},... | collective-permute-start | bytes 786440 | tf_op jit(solution)/shard_map/ppermute | solution.py:142
  82.3 9.2 %collective-permute-start.23 = (bf16[256,512]{1,0:T(8,128)(2,1)}, bf16[256,512]{1,0:T(8,128)(2,1)S(1)}, u32[]{:S(2)}, u32[]{:S(2)}) collective-permute-start(bf16[256,512]{1,0:T(8,128)(2,1)} %collective-permute-done.22.refs_5_), channel_id=1, source_target_pairs={{0,4},{4,8},{8,12},{12,14},{14,10},{10,6},{6,2},{2,0},{1,5},{5,9},... | collective-permute-start | bytes 786440 | tf_op jit(solution)/shard_map/ppermute | solution.py:142
  83.9 9.0 %collective-permute-start.20 = (bf16[256,512]{1,0:T(8,128)(2,1)}, bf16[256,512]{1,0:T(8,128)(2,1)S(1)}, u32[]{:S(2)}, u32[]{:S(2)}) collective-permute-start(bf16[256,512]{1,0:T(8,128)(2,1)} %collective-permute-done.16.refs_4_), channel_id=1, source_target_pairs={{0,4},{4,8},{8,12},{12,14},{14,10},{10,6},{6,2},{2,0},{1,5},{5,9},... | collective-permute-start | bytes 786440 | tf_op jit(solution)/shard_map/ppermute | solution.py:142
  97.2 2.9 %collective-permute-start.30 = (bf16[1024,512]{1,0:T(8,128)(2,1)}, bf16[1024,512]{1,0:T(8,128)(2,1)S(1)}, u32[]{:S(2)}, u32[]{:S(2)}) collective-permute-start(bf16[1024,512]{1,0:T(8,128)(2,1)} %get-tuple-element.78.have_ref), channel_id=1, source_target_pairs={{0,1},{1,0},{2,3},{3,2},{4,5},{5,4},{6,7},{7,6},{8,9},{9,8},{10,11... | collective-permute-start | bytes 3145736 | tf_op jit(solution)/shard_map/ppermute | solution.py:261
  104.8 14.7 %all-to-all-start = ((f32[8,72,128]{2,1,0:T(8,128)}), f32[8,72,128]{2,1,0:T(8,128)S(1)}, u32[]{:S(2)}, u32[]{:S(2)}) async-start(f32[8,72,128]{2,1,0:T(8,128)} %bitcast.25), calls=%async_computation | async-start | bytes 589824 | tf_op jit(solution)/shard_map/all_to_all | solution.py:288
  119.8 3.8 %collective-permute-start.31 = (bf16[64,128]{1,0:T(8,128)(2,1)S(1)}, bf16[64,128]{1,0:T(8,128)(2,1)S(1)}, u32[]{:S(2)}, u32[]{:S(2)}) collective-permute-start(bf16[64,128]{1,0:T(8,128)(2,1)S(1)} %shard_map.89), channel_id=1, source_target_pairs={{0,2},{2,0},{4,6},{6,4},{8,10},{10,8},{12,14},{14,12},{1,3},{3,1},... | collective-permute-start | bytes 49160 | tf_op jit(solution)/shard_map/ppermute | solution.py:292
  123.7 5.8 %collective-permute-start.32 = (bf16[128,128]{1,0:T(8,128)(2,1)S(1)}, bf16[128,128]{1,0:T(8,128)(2,1)S(1)}, u32[]{:S(2)}, u32[]{:S(2)}) collective-permute-start(bf16[128,128]{1,0:T(8,128)(2,1)S(1)} %pad_maximum_fusion.2), channel_id=1, source_target_pairs={{0,12},{2,14},{4,8},{6,10},{8,4},{10,6},{12,0},{14,2},{1,13},{3,15... | collective-permute-start | bytes 98312 | tf_op jit(solution)/shard_map/ppermute | solution.py:295
  124.9 5.3 %collective-permute-start.33 = (bf16[128,128]{1,0:T(8,128)(2,1)S(1)}, bf16[128,128]{1,0:T(8,128)(2,1)S(1)}, u32[]{:S(2)}, u32[]{:S(2)}) collective-permute-start(bf16[128,128]{1,0:T(8,128)(2,1)S(1)} %pad_maximum_fusion.2), channel_id=1, source_target_pairs={{0,8},{2,10},{4,12},{6,14},{8,0},{10,2},{12,4},{14,6},{1,9},{3,11}... | collective-permute-start | bytes 98312 | tf_op jit(solution)/shard_map/ppermute | solution.py:295
  126.3 4.2 %collective-permute-start.34 = (bf16[128,128]{1,0:T(8,128)(2,1)S(1)}, bf16[128,128]{1,0:T(8,128)(2,1)S(1)}, u32[]{:S(2)}, u32[]{:S(2)}) collective-permute-start(bf16[128,128]{1,0:T(8,128)(2,1)S(1)} %pad_maximum_fusion.2), channel_id=1, source_target_pairs={{0,4},{2,6},{4,0},{6,2},{8,12},{10,14},{12,8},{14,10},{1,5},{3,7},... | collective-permute-start | bytes 98312 | tf_op jit(solution)/shard_map/ppermute | solution.py:295
  130.6 1.4 %collective-permute-start.35 = (bf16[16,1,4096]{2,0,1:T(8,128)(2,1)S(1)}, bf16[16,1,4096]{2,0,1:T(8,128)(2,1)S(1)}, u32[]{:S(2)}, u32[]{:S(2)}) collective-permute-start(bf16[16,1,4096]{2,0,1:T(8,128)(2,1)S(1)} %reshape.97), channel_id=1, source_target_pairs={{0,1},{1,0},{2,3},{3,2},{4,5},{5,4},{6,7},{7,6},{8,9},{9,8},{10,11... | collective-permute-start | bytes 393224 | tf_op jit(solution)/shard_map/ppermute | solution.py:305

commit v18 on v17

--- a/solution.py
+++ b/solution.py
@@ -284,8 +284,7 @@
     fresh_stats = [my_share(x.reshape(rows)).reshape(-1, group).T for x in (fresh_top, fresh_total)]
     fresh_stats = jnp.pad(jnp.concatenate(fresh_stats, 1), ((0, 0), (0, DH - 2 * share // group)))
 
-    flat = sending.reshape(chips, -1, DH)
-    arrived = lax.all_to_all(flat, "chip", split_axis=0, concat_axis=0, tiled=True).reshape(sending.shape)
+    arrived = lax.all_to_all(sending, "chip", split_axis=0, concat_axis=0, tiled=True)
     result = merge(arrived, fresh_stats, fresh_summed)
 
     if chips == 8:

time: 134 us -> 134 us (level)
  no operation moved by 1% of the time
where the time goes in v18:
time: 134 us; the launch traced here: 133 us
  waiting for transfers between devices  48.7 us (36%)
  starting transfers between devices  43.4 us (32%)
  Pallas kernels  32.6 us (24%)
  local copies, waits for them, and re-layouts  4.49 us (3%)
  other arithmetic  2.34 us (2%)
  matrix products  1.36 us (1%)
    ppermute x28, waiting for transfers between devices, project(): held[k] = lax.ppermute(held[k], 'chip', ways[k])  33.4 us
    ppermute x28, starting transfers between devices, project(): held[k] = lax.ppermute(held[k], 'chip', ways[k])  32 us
    pallas_call x6, Pallas kernels, add_pieces(): pl.pallas_call(kernel, out_shape=(jax.ShapeDtypeStruct((2 * tok_rows, wid...  27.5 us
    all_to_all x1, waiting for transfers between devices, on_device(): lax.all_to_all(sending, 'chip', split_axis=0, concat_axis=0, tiled=True)  8.6 us
    all_to_all x1, starting transfers between devices, on_device(): lax.all_to_all(sending, 'chip', split_axis=0, concat_axis=0, tiled=True)  4.82 us
    pallas_call x1, Pallas kernels, attend(): pl.pallas_call(kernel, out_shape=jax.ShapeDtypeStruct((chips, blocks + 1,...  4.66 us
    ppermute x3, starting transfers between devices, on_device(): lax.ppermute(couple, 'chip', [(c, c ^ 2 * d) for c in range(chips)])  4.45 us
  transfers between devices with their start and end apart: 37, of which 18 were waited for; matrix products, arithmetic and copies ran while one was open for 4% of the time, Pallas kernels for 18%

profile of v18, /device:TPU:0, one launch (start us, length us, event | category | flops | bytes accessed | tf_op | source)
XLA Modules:
  0.0 133.2 jit_solution(16936980133816042022)
XLA Ops:
  0.0 1.3 broadcast_select_fusion
  1.3 0.5 collective-permute-start.2
  1.9 2.6 %collective-permute-start = (bf16[256,512]{1,0:T(8,128)(2,1)S(1)}, bf16[256,512]{1,0:T(8,128)(2,1)S(1)}, u32[]{:S(2)}, u32[]{:S(2)}) collective-permute-start(bf16[256,512]{1,0:T(8,128)(2,1)S(1)} %get-tuple-element.88), channel_id=1, source_target_pairs={{0,4},{4,8},{8,12},{12,14},{14,10},{10,6},{6,2},{2,0},{1,5},{5,9},... | collective-permute-start | bytes 786440 | tf_op jit(solution)/shard_map/ppermute | solution.py:142
  4.5 1.6 %collective-permute-start.1 = (bf16[256,512]{1,0:T(8,128)(2,1)S(1)}, bf16[256,512]{1,0:T(8,128)(2,1)S(1)}, u32[]{:S(2)}, u32[]{:S(2)}) collective-permute-start(bf16[256,512]{1,0:T(8,128)(2,1)S(1)} %get-tuple-element.87), channel_id=1, source_target_pairs={{0,4},{4,8},{8,12},{12,14},{14,10},{10,6},{6,2},{2,0},{1,5},{5,9},... | collective-permute-start | bytes 786440 | tf_op jit(solution)/shard_map/ppermute | solution.py:142
  6.1 0.5 collective-permute-start.3
  6.6 1.3 collective-permute-start.4
  7.9 3.7 %collective-permute-done.refs_2_ = bf16[256,512]{1,0:T(8,128)(2,1)S(1)} collective-permute-done((bf16[256,512]{1,0:T(8,128)(2,1)S(1)}, bf16[256,512]{1,0:T(8,128)(2,1)S(1)}, u32[]{:S(2)}, u32[]{:S(2)}) %collective-permute-start) | collective-permute-done | bytes 262176 | tf_op jit(solution)/shard_map/ppermute | solution.py:142
  11.6 5.4 %collective-permute-done.1.refs_3_ = bf16[256,512]{1,0:T(8,128)(2,1)S(1)} collective-permute-done((bf16[256,512]{1,0:T(8,128)(2,1)S(1)}, bf16[256,512]{1,0:T(8,128)(2,1)S(1)}, u32[]{:S(2)}, u32[]{:S(2)}) %collective-permute-start.1) | collective-permute-done | bytes 262176 | tf_op jit(solution)/shard_map/ppermute | solution.py:142
  17.1 2.9 %collective-permute-done.4.refs_5_ = bf16[256,512]{1,0:T(8,128)(2,1)S(1)} collective-permute-done((bf16[256,512]{1,0:T(8,128)(2,1)S(1)}, bf16[256,512]{1,0:T(8,128)(2,1)S(1)}, u32[]{:S(2)}, u32[]{:S(2)}) %collective-permute-start.4) | collective-permute-done | bytes 262176 | tf_op jit(solution)/shard_map/ppermute | solution.py:142
  20.0 0.4 collective-permute-start.11
  20.4 1.6 %collective-permute-start.6 = (bf16[256,512]{1,0:T(8,128)(2,1)S(1)}, bf16[256,512]{1,0:T(8,128)(2,1)}, u32[]{:S(2)}, u32[]{:S(2)}) collective-permute-start(bf16[256,512]{1,0:T(8,128)(2,1)S(1)} %collective-permute-done.refs_2_), channel_id=1, source_target_pairs={{0,4},{4,8},{8,12},{12,14},{14,10},{10,6},{6,2},{2,0},{1,5},{5,9},... | collective-permute-start | bytes 786440 | tf_op jit(solution)/shard_map/ppermute | solution.py:142
  22.0 1.6 %collective-permute-start.9 = (bf16[256,512]{1,0:T(8,128)(2,1)S(1)}, bf16[256,512]{1,0:T(8,128)(2,1)}, u32[]{:S(2)}, u32[]{:S(2)}) collective-permute-start(bf16[256,512]{1,0:T(8,128)(2,1)S(1)} %collective-permute-done.1.refs_3_), channel_id=1, source_target_pairs={{0,4},{4,8},{8,12},{12,14},{14,10},{10,6},{6,2},{2,0},{1,5},{5,9},... | collective-permute-start | bytes 786440 | tf_op jit(solution)/shard_map/ppermute | solution.py:142
  23.6 0.4 collective-permute-start.10
  24.1 5.1 %collective-permute-done.11.refs_3_ = bf16[256,512]{1,0:T(8,128)(2,1)} collective-permute-done((bf16[256,512]{1,0:T(8,128)(2,1)S(1)}, bf16[256,512]{1,0:T(8,128)(2,1)}, u32[]{:S(2)}, u32[]{:S(2)}) %collective-permute-start.11) | collective-permute-done | bytes 262176 | tf_op jit(solution)/shard_map/ppermute | solution.py:142
  29.2 0.4 collective-permute-start.15
  29.7 1.6 %collective-permute-start.7 = (bf16[256,512]{1,0:T(8,128)(2,1)}, bf16[256,512]{1,0:T(8,128)(2,1)}, u32[]{:S(2)}, u32[]{:S(2)}) collective-permute-start(bf16[256,512]{1,0:T(8,128)(2,1)} %collective-permute-done.6.refs_0_), channel_id=1, source_target_pairs={{0,4},{4,8},{8,12},{12,14},{14,10},{10,6},{6,2},{2,0},{1,5},{5,9},... | collective-permute-start | bytes 786440 | tf_op jit(solution)/shard_map/ppermute | solution.py:142
  31.2 4.0 %collective-permute-done.9.refs_1_ = bf16[256,512]{1,0:T(8,128)(2,1)} collective-permute-done((bf16[256,512]{1,0:T(8,128)(2,1)S(1)}, bf16[256,512]{1,0:T(8,128)(2,1)}, u32[]{:S(2)}, u32[]{:S(2)}) %collective-permute-start.9) | collective-permute-done | bytes 262176 | tf_op jit(solution)/shard_map/ppermute | solution.py:142
  35.3 1.6 %collective-permute-start.13 = (bf16[256,512]{1,0:T(8,128)(2,1)}, bf16[256,512]{1,0:T(8,128)(2,1)}, u32[]{:S(2)}, u32[]{:S(2)}) collective-permute-start(bf16[256,512]{1,0:T(8,128)(2,1)} %collective-permute-done.9.refs_1_), channel_id=1, source_target_pairs={{0,4},{4,8},{8,12},{12,14},{14,10},{10,6},{6,2},{2,0},{1,5},{5,9},... | collective-permute-start | bytes 786440 | tf_op jit(solution)/shard_map/ppermute | solution.py:142
  36.9 0.4 collective-permute-start.14
  37.4 5.7 %shard_map.82 = (f32[1024,512]{1,0:T(8,128)S(1)}, f32[8,128]{1,0:T(8,128)}) custom-call(s32[4]{0:T(128)S(1)} %pad_add_fusion.1.places_ref, bf16[512,8192]{1,0:T(8,128)(2,1)} %mine_ref.11, bf16[512,8192]{1,0:T(8,128)(2,1)} %collective-permute-done.5.theirs_ref, bf16[512,512]{1,0:T(8,128)(2,1)S(1)} %get-tuple-element.84.refs_0_, ...), custom_call_target="tpu_custom_call" | custom-call | flops 2147483648 | bytes 4194304 | tf_op jit(solution)/shard_map/pallas_call | solution.py:73
  43.1 1.5 %collective-permute-start.19 = (bf16[256,512]{1,0:T(8,128)(2,1)}, bf16[256,512]{1,0:T(8,128)(2,1)}, u32[]{:S(2)}, u32[]{:S(2)}) collective-permute-start(bf16[256,512]{1,0:T(8,128)(2,1)} %collective-permute-done.15.refs_3_), channel_id=1, source_target_pairs={{4,0},{8,4},{12,8},{14,12},{10,14},{6,10},{2,6},{0,2},{5,1},{9,5},... | collective-permute-start | bytes 786440 | tf_op jit(solution)/shard_map/ppermute | solution.py:142
  44.7 1.8 %collective-permute-done.14.refs_2_ = bf16[256,512]{1,0:T(8,128)(2,1)} collective-permute-done((bf16[256,512]{1,0:T(8,128)(2,1)}, bf16[256,512]{1,0:T(8,128)(2,1)}, u32[]{:S(2)}, u32[]{:S(2)}) %collective-permute-start.14) | collective-permute-done | bytes 262176 | tf_op jit(solution)/shard_map/ppermute | solution.py:142
  46.4 2.0 %collective-permute-start.17 = (bf16[256,512]{1,0:T(8,128)(2,1)}, bf16[256,512]{1,0:T(8,128)(2,1)}, u32[]{:S(2)}, u32[]{:S(2)}) collective-permute-start(bf16[256,512]{1,0:T(8,128)(2,1)} %collective-permute-done.13.refs_1_), channel_id=1, source_target_pairs={{0,4},{4,8},{8,12},{12,14},{14,10},{10,6},{6,2},{2,0},{1,5},{5,9},... | collective-permute-start | bytes 786440 | tf_op jit(solution)/shard_map/ppermute | solution.py:142
  48.4 1.6 %collective-permute-start.8 = (bf16[256,512]{1,0:T(8,128)(2,1)}, bf16[256,512]{1,0:T(8,128)(2,1)}, u32[]{:S(2)}, u32[]{:S(2)}) collective-permute-start(bf16[256,512]{1,0:T(8,128)(2,1)} %collective-permute-done.7.refs_0_), channel_id=1, source_target_pairs={{0,4},{4,8},{8,12},{12,14},{14,10},{10,6},{6,2},{2,0},{1,5},{5,9},... | collective-permute-start | bytes 786440 | tf_op jit(solution)/shard_map/ppermute | solution.py:142
  50.2 1.3 constant_dynamic-slice_fusion.1
  51.5 3.9 %shard_map.83 = (f32[1024,512]{1,0:T(8,128)S(1)}, f32[8,128]{1,0:T(8,128)}) custom-call(s32[2]{0:T(128)S(1)} %pad_add_fusion.2.places_ref, bf16[512,8192]{1,0:T(8,128)(2,1)} %mine_ref.11, bf16[512,8192]{1,0:T(8,128)(2,1)} %collective-permute-done.5.theirs_ref, bf16[256,512]{1,0:T(8,128)(2,1)} %collective-permute-done.6.refs_0_, ...), custom_call_target="tpu_custom_call", output_to_operand_aliasing={{0}: (7, {})} | custom-call | flops 1073741824 | bytes 2097152 | tf_op jit(solution)/shard_map/pallas_call | solution.py:73
  55.4 0.5 collective-permute-start.27
  55.9 1.6 %collective-permute-done.18.refs_2_ = bf16[256,512]{1,0:T(8,128)(2,1)} collective-permute-done((bf16[256,512]{1,0:T(8,128)(2,1)}, bf16[256,512]{1,0:T(8,128)(2,1)}, u32[]{:S(2)}, u32[]{:S(2)}) %collective-permute-start.18) | collective-permute-done | bytes 262176 | tf_op jit(solution)/shard_map/ppermute | solution.py:142
  57.5 0.5 collective-permute-start.24
  58.0 1.5 %collective-permute-start.21 = (bf16[256,512]{1,0:T(8,128)(2,1)}, bf16[256,512]{1,0:T(8,128)(2,1)}, u32[]{:S(2)}, u32[]{:S(2)}) collective-permute-start(bf16[256,512]{1,0:T(8,128)(2,1)} %collective-permute-done.17.refs_1_), channel_id=1, source_target_pairs={{0,4},{4,8},{8,12},{12,14},{14,10},{10,6},{6,2},{2,0},{1,5},{5,9},... | collective-permute-start | bytes 786440 | tf_op jit(solution)/shard_map/ppermute | solution.py:142
  59.5 0.7 collective-permute-done.8.refs_0_
  60.2 1.4 %collective-permute-start.12 = (bf16[256,512]{1,0:T(8,128)(2,1)}, bf16[256,512]{1,0:T(8,128)(2,1)}, u32[]{:S(2)}, u32[]{:S(2)}) collective-permute-start(bf16[256,512]{1,0:T(8,128)(2,1)} %collective-permute-done.8.refs_0_), channel_id=1, source_target_pairs={{0,4},{4,8},{8,12},{12,14},{14,10},{10,6},{6,2},{2,0},{1,5},{5,9},... | collective-permute-start | bytes 786440 | tf_op jit(solution)/shard_map/ppermute | solution.py:142
  61.7 3.9 %shard_map.84 = (f32[1024,512]{1,0:T(8,128)S(1)}, f32[8,128]{1,0:T(8,128)}) custom-call(s32[2]{0:T(128)S(1)} %pad_add_fusion.3.places_ref, bf16[512,8192]{1,0:T(8,128)(2,1)} %mine_ref.11, bf16[512,8192]{1,0:T(8,128)(2,1)} %collective-permute-done.5.theirs_ref, bf16[256,512]{1,0:T(8,128)(2,1)} %collective-permute-done.7.refs_0_, ...), custom_call_target="tpu_custom_call", output_to_operand_aliasing={{0}: (7, {})} | custom-call | flops 1073741824 | bytes 2097152 | tf_op jit(solution)/shard_map/pallas_call | solution.py:73
  65.6 1.1 collective-permute-start.28
  66.7 4.0 %collective-permute-done.24.refs_2_ = bf16[256,512]{1,0:T(8,128)(2,1)} collective-permute-done((bf16[256,512]{1,0:T(8,128)(2,1)}, bf16[256,512]{1,0:T(8,128)(2,1)}, u32[]{:S(2)}, u32[]{:S(2)}) %collective-permute-start.24) | collective-permute-done | bytes 262176 | tf_op jit(solution)/shard_map/ppermute | solution.py:142
  70.7 0.4 collective-permute-start.25
  71.1 1.6 %collective-permute-start.22 = (bf16[256,512]{1,0:T(8,128)(2,1)}, bf16[256,512]{1,0:T(8,128)(2,1)}, u32[]{:S(2)}, u32[]{:S(2)}) collective-permute-start(bf16[256,512]{1,0:T(8,128)(2,1)} %collective-permute-done.21.refs_1_), channel_id=1, source_target_pairs={{0,4},{4,8},{8,12},{12,14},{14,10},{10,6},{6,2},{2,0},{1,5},{5,9},... | collective-permute-start | bytes 786440 | tf_op jit(solution)/shard_map/ppermute | solution.py:142
  72.7 1.5 %collective-permute-start.16 = (bf16[256,512]{1,0:T(8,128)(2,1)}, bf16[256,512]{1,0:T(8,128)(2,1)}, u32[]{:S(2)}, u32[]{:S(2)}) collective-permute-start(bf16[256,512]{1,0:T(8,128)(2,1)} %collective-permute-done.12.refs_0_), channel_id=1, source_target_pairs={{0,4},{4,8},{8,12},{12,14},{14,10},{10,6},{6,2},{2,0},{1,5},{5,9},... | collective-permute-start | bytes 786440 | tf_op jit(solution)/shard_map/ppermute | solution.py:142
  74.5 3.9 %shard_map.85 = (f32[1024,512]{1,0:T(8,128)S(1)}, f32[8,128]{1,0:T(8,128)}) custom-call(s32[2]{0:T(128)S(1)} %pad_add_fusion.4.places_ref, bf16[512,8192]{1,0:T(8,128)(2,1)} %mine_ref.11, bf16[512,8192]{1,0:T(8,128)(2,1)} %collective-permute-done.5.theirs_ref, bf16[256,512]{1,0:T(8,128)(2,1)} %collective-permute-done.8.refs_0_, ...), custom_call_target="tpu_custom_call", output_to_operand_aliasing={{0}: (7, {})} | custom-call | flops 1073741824 | bytes 2097152 | tf_op jit(solution)/shard_map/pallas_call | solution.py:73
  78.5 0.6 collective-permute-start.29
  79.0 2.9 %collective-permute-done.25.refs_6_ = bf16[256,512]{1,0:T(8,128)(2,1)} collective-permute-done((bf16[256,512]{1,0:T(8,128)(2,1)}, bf16[256,512]{1,0:T(8,128)(2,1)}, u32[]{:S(2)}, u32[]{:S(2)}) %collective-permute-start.25) | collective-permute-done | bytes 262176 | tf_op jit(solution)/shard_map/ppermute | solution.py:142
  81.9 0.4 collective-permute-start.26
  82.3 1.6 %collective-permute-start.23 = (bf16[256,512]{1,0:T(8,128)(2,1)}, bf16[256,512]{1,0:T(8,128)(2,1)S(1)}, u32[]{:S(2)}, u32[]{:S(2)}) collective-permute-start(bf16[256,512]{1,0:T(8,128)(2,1)} %collective-permute-done.22.refs_5_), channel_id=1, source_target_pairs={{0,4},{4,8},{8,12},{12,14},{14,10},{10,6},{6,2},{2,0},{1,5},{5,9},... | collective-permute-start | bytes 786440 | tf_op jit(solution)/shard_map/ppermute | solution.py:142
  83.9 1.5 %collective-permute-start.20 = (bf16[256,512]{1,0:T(8,128)(2,1)}, bf16[256,512]{1,0:T(8,128)(2,1)S(1)}, u32[]{:S(2)}, u32[]{:S(2)}) collective-permute-start(bf16[256,512]{1,0:T(8,128)(2,1)} %collective-permute-done.16.refs_4_), channel_id=1, source_target_pairs={{0,4},{4,8},{8,12},{12,14},{14,10},{10,6},{6,2},{2,0},{1,5},{5,9},... | collective-permute-start | bytes 786440 | tf_op jit(solution)/shard_map/ppermute | solution.py:142
  85.5 6.0 %shard_map.86 = (f32[1024,512]{1,0:T(8,128)S(1)}, f32[8,128]{1,0:T(8,128)}) custom-call(s32[4]{0:T(128)S(1)} %pad_add_fusion.5.places_ref, bf16[512,8192]{1,0:T(8,128)(2,1)} %mine_ref.11, bf16[512,8192]{1,0:T(8,128)(2,1)} %collective-permute-done.5.theirs_ref, bf16[256,512]{1,0:T(8,128)(2,1)} %collective-permute-done.12.refs_0_, ...), custom_call_target="tpu_custom_call", output_to_operand_aliasing={{0}: (11, {})} | custom-call | flops 2147483648 | bytes 4194304 | tf_op jit(solution)/shard_map/pallas_call | solution.py:73
  91.6 1.4 %collective-permute-done.20.refs_0_ = bf16[256,512]{1,0:T(8,128)(2,1)S(1)} collective-permute-done((bf16[256,512]{1,0:T(8,128)(2,1)}, bf16[256,512]{1,0:T(8,128)(2,1)S(1)}, u32[]{:S(2)}, u32[]{:S(2)}) %collective-permute-start.20) | collective-permute-done | bytes 262176 | tf_op jit(solution)/shard_map/ppermute | solution.py:142
  93.0 4.2 %shard_map.87 = (bf16[1024,512]{1,0:T(8,128)(2,1)}, f32[8,128]{1,0:T(8,128)}) custom-call(s32[4]{0:T(128)S(1)} %pad_add_fusion.places_ref, bf16[512,8192]{1,0:T(8,128)(2,1)} %mine_ref.11, bf16[512,8192]{1,0:T(8,128)(2,1)} %collective-permute-done.5.theirs_ref, bf16[256,512]{1,0:T(8,128)(2,1)S(1)} %collective-permute-done.20.refs_0_, ...), custom_call_target="tpu_custom_call" | custom-call | flops 1073741824 | bytes 2097152 | tf_op jit(solution)/shard_map/pallas_call | solution.py:73
  97.5 0.8 reshape.81
  98.7 0.7 fusion.17
  99.4 0.7 collective-permute-done.30.got_ref
  100.1 4.7 %shard_map.88 = f32[8,9,8,128]{3,2,1,0:T(8,128)} custom-call(s32[1]{0:T(128)} %bitcast.core_ref, bf16[1024,512]{1,0:T(8,128)(2,1)} %get-tuple-element.78.have_ref, bf16[1024,512]{1,0:T(8,128)(2,1)S(1)} %collective-permute-done.30.got_ref, bf16[512,512]{1,0:T(8,128)(2,1)S(1)} %get-tuple-element.79.key_up_ref, ...), custom_call_target="tpu_custom_call" | custom-call | flops 1342177280 | bytes 2097152 | tf_op jit(solution)/shard_map/pallas_call | solution.py:194
  104.8 4.8 %all-to-all-start = ((f32[8,9,8,128]{3,2,1,0:T(8,128)}), f32[8,9,8,128]{3,2,1,0:T(8,128)S(1)}, u32[]{:S(2)}, u32[]{:S(2)}) async-start(f32[8,9,8,128]{3,2,1,0:T(8,128)} %shard_map.88), calls=%async_computation | async-start | bytes 589824 | tf_op jit(solution)/shard_map/all_to_all | solution.py:287
  109.6 0.3 convolution_bitcast_fusion
  110.9 8.6 %all-to-all-done.arrived_ref = f32[8,9,8,128]{3,2,1,0:T(8,128)S(1)} async-done(((f32[8,9,8,128]{3,2,1,0:T(8,128)}), f32[8,9,8,128]{3,2,1,0:T(8,128)S(1)}, u32[]{:S(2)}, u32[]{:S(2)}) %all-to-all-start) | async-done | bytes 294944 | tf_op jit(solution)/shard_map/all_to_all | solution.py:287
  119.5 0.4 shard_map.89
  119.8 1.5 %collective-permute-start.31 = (bf16[64,128]{1,0:T(8,128)(2,1)S(1)}, bf16[64,128]{1,0:T(8,128)(2,1)S(1)}, u32[]{:S(2)}, u32[]{:S(2)}) collective-permute-start(bf16[64,128]{1,0:T(8,128)(2,1)S(1)} %shard_map.89), channel_id=1, source_target_pairs={{0,2},{2,0},{4,6},{6,4},{8,10},{10,8},{12,14},{14,12},{1,3},{3,1},... | collective-permute-start | bytes 49160 | tf_op jit(solution)/shard_map/ppermute | solution.py:291
  121.4 2.3 %collective-permute-done.31 = bf16[64,128]{1,0:T(8,128)(2,1)S(1)} collective-permute-done((bf16[64,128]{1,0:T(8,128)(2,1)S(1)}, bf16[64,128]{1,0:T(8,128)(2,1)S(1)}, u32[]{:S(2)}, u32[]{:S(2)}) %collective-permute-start.31) | collective-permute-done | bytes 16416 | tf_op jit(solution)/shard_map/ppermute | solution.py:291
  123.7 1.2 collective-permute-start.32
  124.9 1.3 %collective-permute-start.33 = (bf16[128,128]{1,0:T(8,128)(2,1)S(1)}, bf16[128,128]{1,0:T(8,128)(2,1)S(1)}, u32[]{:S(2)}, u32[]{:S(2)}) collective-permute-start(bf16[128,128]{1,0:T(8,128)(2,1)S(1)} %pad_maximum_fusion.2), channel_id=1, source_target_pairs={{0,8},{2,10},{4,12},{6,14},{8,0},{10,2},{12,4},{14,6},{1,9},{3,11}... | collective-permute-start | bytes 98312 | tf_op jit(solution)/shard_map/ppermute | solution.py:294
  126.3 1.9 %collective-permute-start.34 = (bf16[128,128]{1,0:T(8,128)(2,1)S(1)}, bf16[128,128]{1,0:T(8,128)(2,1)S(1)}, u32[]{:S(2)}, u32[]{:S(2)}) collective-permute-start(bf16[128,128]{1,0:T(8,128)(2,1)S(1)} %pad_maximum_fusion.2), channel_id=1, source_target_pairs={{0,4},{2,6},{4,0},{6,2},{8,12},{10,14},{12,8},{14,10},{1,5},{3,7},... | collective-permute-start | bytes 98312 | tf_op jit(solution)/shard_map/ppermute | solution.py:294
  128.1 1.3 collective-permute-done.32
  129.4 0.8 collective-permute-done.33
  130.7 1.3 %collective-permute-done.35 = bf16[16,1,4096]{2,0,1:T(8,128)(2,1)S(1)} collective-permute-done((bf16[16,1,4096]{2,0,1:T(8,128)(2,1)S(1)}, bf16[16,1,4096]{2,0,1:T(8,128)(2,1)S(1)}, u32[]{:S(2)}, u32[]{:S(2)}) %collective-permute-start.35) | collective-permute-done | bytes 131104 | tf_op jit(solution)/shard_map/ppermute | solution.py:304
  132.4 0.9 reshape.90
  (79 shorter events, 3.4 us)
Async XLA Ops:
  0.0 50.0 %copy-start = (bf16[4,4,8192]{2,1,0:T(4,128)(2,1)S(1)}, bf16[4,4,8192]{2,1,0:T(4,128)(2,1)}, u32[]{:S(2)}) copy-start(bf16[4,4,8192]{2,1,0:T(4,128)(2,1)} %param.14) | copy-start | bytes 786436
  1.3 4.8 %collective-permute-start.2 = (bf16[512,512]{1,0:T(8,128)(2,1)S(1)}, bf16[512,512]{1,0:T(8,128)(2,1)S(1)}, u32[]{:S(2)}, u32[]{:S(2)}) collective-permute-start(bf16[512,512]{1,0:T(8,128)(2,1)S(1)} %get-tuple-element.83), channel_id=1, source_target_pairs={{0,1},{1,0},{2,3},{3,2},{4,5},{5,4},{6,7},{7,6},{8,9},{9,8},{10,11... | collective-permute-start | bytes 1572872 | tf_op jit(solution)/shard_map/ppermute | solution.py:103
  1.9 9.7 %collective-permute-start = (bf16[256,512]{1,0:T(8,128)(2,1)S(1)}, bf16[256,512]{1,0:T(8,128)(2,1)S(1)}, u32[]{:S(2)}, u32[]{:S(2)}) collective-permute-start(bf16[256,512]{1,0:T(8,128)(2,1)S(1)} %get-tuple-element.88), channel_id=1, source_target_pairs={{0,4},{4,8},{8,12},{12,14},{14,10},{10,6},{6,2},{2,0},{1,5},{5,9},... | collective-permute-start | bytes 786440 | tf_op jit(solution)/shard_map/ppermute | solution.py:142
  4.5 12.5 %collective-permute-start.1 = (bf16[256,512]{1,0:T(8,128)(2,1)S(1)}, bf16[256,512]{1,0:T(8,128)(2,1)S(1)}, u32[]{:S(2)}, u32[]{:S(2)}) collective-permute-start(bf16[256,512]{1,0:T(8,128)(2,1)S(1)} %get-tuple-element.87), channel_id=1, source_target_pairs={{0,4},{4,8},{8,12},{12,14},{14,10},{10,6},{6,2},{2,0},{1,5},{5,9},... | collective-permute-start | bytes 786440 | tf_op jit(solution)/shard_map/ppermute | solution.py:142
  6.1 10.9 %collective-permute-start.3 = (bf16[256,512]{1,0:T(8,128)(2,1)S(1)}, bf16[256,512]{1,0:T(8,128)(2,1)S(1)}, u32[]{:S(2)}, u32[]{:S(2)}) collective-permute-start(bf16[256,512]{1,0:T(8,128)(2,1)S(1)} %get-tuple-element.86), channel_id=1, source_target_pairs={{4,0},{8,4},{12,8},{14,12},{10,14},{6,10},{2,6},{0,2},{5,1},{9,5},... | collective-permute-start | bytes 786440 | tf_op jit(solution)/shard_map/ppermute | solution.py:142
  6.6 13.3 %collective-permute-start.4 = (bf16[256,512]{1,0:T(8,128)(2,1)S(1)}, bf16[256,512]{1,0:T(8,128)(2,1)S(1)}, u32[]{:S(2)}, u32[]{:S(2)}) collective-permute-start(bf16[256,512]{1,0:T(8,128)(2,1)S(1)} %get-tuple-element.85), channel_id=1, source_target_pairs={{4,0},{8,4},{12,8},{14,12},{10,14},{6,10},{2,6},{0,2},{5,1},{9,5},... | collective-permute-start | bytes 786440 | tf_op jit(solution)/shard_map/ppermute | solution.py:142
  11.6 25.8 %copy-start.1 = (bf16[256,512]{1,0:T(8,128)(2,1)}, bf16[256,512]{1,0:T(8,128)(2,1)S(1)}, u32[]{:S(2)}) copy-start(bf16[256,512]{1,0:T(8,128)(2,1)S(1)} %collective-permute-done.refs_2_) | copy-start | bytes 786436
  17.0 20.3 %copy-start.2 = (bf16[256,512]{1,0:T(8,128)(2,1)}, bf16[256,512]{1,0:T(8,128)(2,1)S(1)}, u32[]{:S(2)}) copy-start(bf16[256,512]{1,0:T(8,128)(2,1)S(1)} %collective-permute-done.1.refs_3_) | copy-start | bytes 786436
  17.0 20.3 %copy-start.3 = (bf16[256,512]{1,0:T(8,128)(2,1)}, bf16[256,512]{1,0:T(8,128)(2,1)S(1)}, u32[]{:S(2)}) copy-start(bf16[256,512]{1,0:T(8,128)(2,1)S(1)} %collective-permute-done.3.refs_4_) | copy-start | bytes 786436
  20.0 17.4 %copy-start.4 = (bf16[256,512]{1,0:T(8,128)(2,1)}, bf16[256,512]{1,0:T(8,128)(2,1)S(1)}, u32[]{:S(2)}) copy-start(bf16[256,512]{1,0:T(8,128)(2,1)S(1)} %collective-permute-done.4.refs_5_) | copy-start | bytes 786436
  20.0 17.4 %collective-permute-start.5 = (bf16[512,8192]{1,0:T(8,128)(2,1)}, bf16[512,8192]{1,0:T(8,128)(2,1)}, u32[]{:S(2)}, u32[]{:S(2)}) collective-permute-start(bf16[512,8192]{1,0:T(8,128)(2,1)} %mine_ref.11), channel_id=1, source_target_pairs={{0,1},{1,0},{2,3},{3,2},{4,5},{5,4},{6,7},{7,6},{8,9},{9,8},{10,11... | collective-permute-start | bytes 25165832 | tf_op jit(solution)/shard_map/ppermute | solution.py:133
  20.0 9.2 %collective-permute-start.11 = (bf16[256,512]{1,0:T(8,128)(2,1)S(1)}, bf16[256,512]{1,0:T(8,128)(2,1)}, u32[]{:S(2)}, u32[]{:S(2)}) collective-permute-start(bf16[256,512]{1,0:T(8,128)(2,1)S(1)} %collective-permute-done.4.refs_5_), channel_id=1, source_target_pairs={{4,0},{8,4},{12,8},{14,12},{10,14},{6,10},{2,6},{0,2},{5,1},{9,5},... | collective-permute-start | bytes 786440 | tf_op jit(solution)/shard_map/ppermute | solution.py:142
  20.4 9.2 %collective-permute-start.6 = (bf16[256,512]{1,0:T(8,128)(2,1)S(1)}, bf16[256,512]{1,0:T(8,128)(2,1)}, u32[]{:S(2)}, u32[]{:S(2)}) collective-permute-start(bf16[256,512]{1,0:T(8,128)(2,1)S(1)} %collective-permute-done.refs_2_), channel_id=1, source_target_pairs={{0,4},{4,8},{8,12},{12,14},{14,10},{10,6},{6,2},{2,0},{1,5},{5,9},... | collective-permute-start | bytes 786440 | tf_op jit(solution)/shard_map/ppermute | solution.py:142
  22.0 13.3 %collective-permute-start.9 = (bf16[256,512]{1,0:T(8,128)(2,1)S(1)}, bf16[256,512]{1,0:T(8,128)(2,1)}, u32[]{:S(2)}, u32[]{:S(2)}) collective-permute-start(bf16[256,512]{1,0:T(8,128)(2,1)S(1)} %collective-permute-done.1.refs_3_), channel_id=1, source_target_pairs={{0,4},{4,8},{8,12},{12,14},{14,10},{10,6},{6,2},{2,0},{1,5},{5,9},... | collective-permute-start | bytes 786440 | tf_op jit(solution)/shard_map/ppermute | solution.py:142
  23.6 13.3 %collective-permute-start.10 = (bf16[256,512]{1,0:T(8,128)(2,1)S(1)}, bf16[256,512]{1,0:T(8,128)(2,1)}, u32[]{:S(2)}, u32[]{:S(2)}) collective-permute-start(bf16[256,512]{1,0:T(8,128)(2,1)S(1)} %collective-permute-done.3.refs_4_), channel_id=1, source_target_pairs={{4,0},{8,4},{12,8},{14,12},{10,14},{6,10},{2,6},{0,2},{5,1},{9,5},... | collective-permute-start | bytes 786440 | tf_op jit(solution)/shard_map/ppermute | solution.py:142
  29.2 13.9 %collective-permute-start.15 = (bf16[256,512]{1,0:T(8,128)(2,1)}, bf16[256,512]{1,0:T(8,128)(2,1)}, u32[]{:S(2)}, u32[]{:S(2)}) collective-permute-start(bf16[256,512]{1,0:T(8,128)(2,1)} %collective-permute-done.11.refs_3_), channel_id=1, source_target_pairs={{4,0},{8,4},{12,8},{14,12},{10,14},{6,10},{2,6},{0,2},{5,1},{9,5},... | collective-permute-start | bytes 786440 | tf_op jit(solution)/shard_map/ppermute | solution.py:142
  29.7 18.8 %collective-permute-start.7 = (bf16[256,512]{1,0:T(8,128)(2,1)}, bf16[256,512]{1,0:T(8,128)(2,1)}, u32[]{:S(2)}, u32[]{:S(2)}) collective-permute-start(bf16[256,512]{1,0:T(8,128)(2,1)} %collective-permute-done.6.refs_0_), channel_id=1, source_target_pairs={{0,4},{4,8},{8,12},{12,14},{14,10},{10,6},{6,2},{2,0},{1,5},{5,9},... | collective-permute-start | bytes 786440 | tf_op jit(solution)/shard_map/ppermute | solution.py:142
  35.3 11.1 %collective-permute-start.13 = (bf16[256,512]{1,0:T(8,128)(2,1)}, bf16[256,512]{1,0:T(8,128)(2,1)}, u32[]{:S(2)}, u32[]{:S(2)}) collective-permute-start(bf16[256,512]{1,0:T(8,128)(2,1)} %collective-permute-done.9.refs_1_), channel_id=1, source_target_pairs={{0,4},{4,8},{8,12},{12,14},{14,10},{10,6},{6,2},{2,0},{1,5},{5,9},... | collective-permute-start | bytes 786440 | tf_op jit(solution)/shard_map/ppermute | solution.py:142
  36.9 9.6 %collective-permute-start.14 = (bf16[256,512]{1,0:T(8,128)(2,1)}, bf16[256,512]{1,0:T(8,128)(2,1)}, u32[]{:S(2)}, u32[]{:S(2)}) collective-permute-start(bf16[256,512]{1,0:T(8,128)(2,1)} %collective-permute-done.10.refs_2_), channel_id=1, source_target_pairs={{4,0},{8,4},{12,8},{14,12},{10,14},{6,10},{2,6},{0,2},{5,1},{9,5},... | collective-permute-start | bytes 786440 | tf_op jit(solution)/shard_map/ppermute | solution.py:142
  43.1 12.3 %collective-permute-start.19 = (bf16[256,512]{1,0:T(8,128)(2,1)}, bf16[256,512]{1,0:T(8,128)(2,1)}, u32[]{:S(2)}, u32[]{:S(2)}) collective-permute-start(bf16[256,512]{1,0:T(8,128)(2,1)} %collective-permute-done.15.refs_3_), channel_id=1, source_target_pairs={{4,0},{8,4},{12,8},{14,12},{10,14},{6,10},{2,6},{0,2},{5,1},{9,5},... | collective-permute-start | bytes 786440 | tf_op jit(solution)/shard_map/ppermute | solution.py:142
  46.4 11.1 %collective-permute-start.18 = (bf16[256,512]{1,0:T(8,128)(2,1)}, bf16[256,512]{1,0:T(8,128)(2,1)}, u32[]{:S(2)}, u32[]{:S(2)}) collective-permute-start(bf16[256,512]{1,0:T(8,128)(2,1)} %collective-permute-done.14.refs_2_), channel_id=1, source_target_pairs={{4,0},{8,4},{12,8},{14,12},{10,14},{6,10},{2,6},{0,2},{5,1},{9,5},... | collective-permute-start | bytes 786440 | tf_op jit(solution)/shard_map/ppermute | solution.py:142
  46.4 11.6 %collective-permute-start.17 = (bf16[256,512]{1,0:T(8,128)(2,1)}, bf16[256,512]{1,0:T(8,128)(2,1)}, u32[]{:S(2)}, u32[]{:S(2)}) collective-permute-start(bf16[256,512]{1,0:T(8,128)(2,1)} %collective-permute-done.13.refs_1_), channel_id=1, source_target_pairs={{0,4},{4,8},{8,12},{12,14},{14,10},{10,6},{6,2},{2,0},{1,5},{5,9},... | collective-permute-start | bytes 786440 | tf_op jit(solution)/shard_map/ppermute | solution.py:142
  48.4 11.8 %collective-permute-start.8 = (bf16[256,512]{1,0:T(8,128)(2,1)}, bf16[256,512]{1,0:T(8,128)(2,1)}, u32[]{:S(2)}, u32[]{:S(2)}) collective-permute-start(bf16[256,512]{1,0:T(8,128)(2,1)} %collective-permute-done.7.refs_0_), channel_id=1, source_target_pairs={{0,4},{4,8},{8,12},{12,14},{14,10},{10,6},{6,2},{2,0},{1,5},{5,9},... | collective-permute-start | bytes 786440 | tf_op jit(solution)/shard_map/ppermute | solution.py:142
  55.4 10.2 %collective-permute-start.27 = (bf16[256,512]{1,0:T(8,128)(2,1)}, bf16[256,512]{1,0:T(8,128)(2,1)}, u32[]{:S(2)}, u32[]{:S(2)}) collective-permute-start(bf16[256,512]{1,0:T(8,128)(2,1)} %collective-permute-done.19.refs_3_), channel_id=1, source_target_pairs={{4,0},{8,4},{12,8},{14,12},{10,14},{6,10},{2,6},{0,2},{5,1},{9,5},... | collective-permute-start | bytes 786440 | tf_op jit(solution)/shard_map/ppermute | solution.py:142
  57.5 13.2 %collective-permute-start.24 = (bf16[256,512]{1,0:T(8,128)(2,1)}, bf16[256,512]{1,0:T(8,128)(2,1)}, u32[]{:S(2)}, u32[]{:S(2)}) collective-permute-start(bf16[256,512]{1,0:T(8,128)(2,1)} %collective-permute-done.18.refs_2_), channel_id=1, source_target_pairs={{4,0},{8,4},{12,8},{14,12},{10,14},{6,10},{2,6},{0,2},{5,1},{9,5},... | collective-permute-start | bytes 786440 | tf_op jit(solution)/shard_map/ppermute | solution.py:142
  58.0 13.1 %collective-permute-start.21 = (bf16[256,512]{1,0:T(8,128)(2,1)}, bf16[256,512]{1,0:T(8,128)(2,1)}, u32[]{:S(2)}, u32[]{:S(2)}) collective-permute-start(bf16[256,512]{1,0:T(8,128)(2,1)} %collective-permute-done.17.refs_1_), channel_id=1, source_target_pairs={{0,4},{4,8},{8,12},{12,14},{14,10},{10,6},{6,2},{2,0},{1,5},{5,9},... | collective-permute-start | bytes 786440 | tf_op jit(solution)/shard_map/ppermute | solution.py:142
  60.2 12.5 %collective-permute-start.12 = (bf16[256,512]{1,0:T(8,128)(2,1)}, bf16[256,512]{1,0:T(8,128)(2,1)}, u32[]{:S(2)}, u32[]{:S(2)}) collective-permute-start(bf16[256,512]{1,0:T(8,128)(2,1)} %collective-permute-done.8.refs_0_), channel_id=1, source_target_pairs={{0,4},{4,8},{8,12},{12,14},{14,10},{10,6},{6,2},{2,0},{1,5},{5,9},... | collective-permute-start | bytes 786440 | tf_op jit(solution)/shard_map/ppermute | solution.py:142
  61.7 12.6 %copy-start.5 = (s32[4]{0:T(128)S(1)}, s32[4]{0:T(128)}, u32[]{:S(2)}) copy-start(s32[4]{0:T(128)} %param.13) | copy-start | bytes 52
  65.6 12.8 %collective-permute-start.28 = (bf16[256,512]{1,0:T(8,128)(2,1)}, bf16[256,512]{1,0:T(8,128)(2,1)}, u32[]{:S(2)}, u32[]{:S(2)}) collective-permute-start(bf16[256,512]{1,0:T(8,128)(2,1)} %collective-permute-done.27.refs_3_), channel_id=1, source_target_pairs={{4,0},{8,4},{12,8},{14,12},{10,14},{6,10},{2,6},{0,2},{5,1},{9,5},... | collective-permute-start | bytes 786440 | tf_op jit(solution)/shard_map/ppermute | solution.py:142
  70.7 11.2 %collective-permute-start.25 = (bf16[256,512]{1,0:T(8,128)(2,1)}, bf16[256,512]{1,0:T(8,128)(2,1)}, u32[]{:S(2)}, u32[]{:S(2)}) collective-permute-start(bf16[256,512]{1,0:T(8,128)(2,1)} %collective-permute-done.24.refs_2_), channel_id=1, source_target_pairs={{4,0},{8,4},{12,8},{14,12},{10,14},{6,10},{2,6},{0,2},{5,1},{9,5},... | collective-permute-start | bytes 786440 | tf_op jit(solution)/shard_map/ppermute | solution.py:142
  71.1 11.2 %collective-permute-start.22 = (bf16[256,512]{1,0:T(8,128)(2,1)}, bf16[256,512]{1,0:T(8,128)(2,1)}, u32[]{:S(2)}, u32[]{:S(2)}) collective-permute-start(bf16[256,512]{1,0:T(8,128)(2,1)} %collective-permute-done.21.refs_1_), channel_id=1, source_target_pairs={{0,4},{4,8},{8,12},{12,14},{14,10},{10,6},{6,2},{2,0},{1,5},{5,9},... | collective-permute-start | bytes 786440 | tf_op jit(solution)/shard_map/ppermute | solution.py:142
  72.7 11.2 %collective-permute-start.16 = (bf16[256,512]{1,0:T(8,128)(2,1)}, bf16[256,512]{1,0:T(8,128)(2,1)}, u32[]{:S(2)}, u32[]{:S(2)}) collective-permute-start(bf16[256,512]{1,0:T(8,128)(2,1)} %collective-permute-done.12.refs_0_), channel_id=1, source_target_pairs={{0,4},{4,8},{8,12},{12,14},{14,10},{10,6},{6,2},{2,0},{1,5},{5,9},... | collective-permute-start | bytes 786440 | tf_op jit(solution)/shard_map/ppermute | solution.py:142
  78.5 13.1 %collective-permute-start.29 = (bf16[256,512]{1,0:T(8,128)(2,1)}, bf16[256,512]{1,0:T(8,128)(2,1)S(1)}, u32[]{:S(2)}, u32[]{:S(2)}) collective-permute-start(bf16[256,512]{1,0:T(8,128)(2,1)} %collective-permute-done.28.refs_7_), channel_id=1, source_target_pairs={{4,0},{8,4},{12,8},{14,12},{10,14},{6,10},{2,6},{0,2},{5,1},{9,5},... | collective-permute-start | bytes 786440 | tf_op jit(solution)/shard_map/ppermute | solution.py:142
  81.9 9.7 %collective-permute-start.26 = (bf16[256,512]{1,0:T(8,128)(2,1)}, bf16[256,512]{1,0:T(8,128)(2,1)S(1)}, u32[]{:S(2)}, u32[]{:S(2)}) collective-permute-start(bf16[256,512]{1,0:T(8,128)(2,1)} %collective-permute-done.25.refs_6_), channel_id=1, source_target_pairs={{4,0},{8,4},{12,8},{14,12},{10,14},{6,10},{2,6},{0,2},{5,1},{9,5},... | collective-permute-start | bytes 786440 | tf_op jit(solution)/shard_map/ppermute | solution.py:142
  82.3 9.2 %collective-permute-start.23 = (bf16[256,512]{1,0:T(8,128)(2,1)}, bf16[256,512]{1,0:T(8,128)(2,1)S(1)}, u32[]{:S(2)}, u32[]{:S(2)}) collective-permute-start(bf16[256,512]{1,0:T(8,128)(2,1)} %collective-permute-done.22.refs_5_), channel_id=1, source_target_pairs={{0,4},{4,8},{8,12},{12,14},{14,10},{10,6},{6,2},{2,0},{1,5},{5,9},... | collective-permute-start | bytes 786440 | tf_op jit(solution)/shard_map/ppermute | solution.py:142
  83.9 9.0 %collective-permute-start.20 = (bf16[256,512]{1,0:T(8,128)(2,1)}, bf16[256,512]{1,0:T(8,128)(2,1)S(1)}, u32[]{:S(2)}, u32[]{:S(2)}) collective-permute-start(bf16[256,512]{1,0:T(8,128)(2,1)} %collective-permute-done.16.refs_4_), channel_id=1, source_target_pairs={{0,4},{4,8},{8,12},{12,14},{14,10},{10,6},{6,2},{2,0},{1,5},{5,9},... | collective-permute-start | bytes 786440 | tf_op jit(solution)/shard_map/ppermute | solution.py:142
  97.2 2.9 %collective-permute-start.30 = (bf16[1024,512]{1,0:T(8,128)(2,1)}, bf16[1024,512]{1,0:T(8,128)(2,1)S(1)}, u32[]{:S(2)}, u32[]{:S(2)}) collective-permute-start(bf16[1024,512]{1,0:T(8,128)(2,1)} %get-tuple-element.78.have_ref), channel_id=1, source_target_pairs={{0,1},{1,0},{2,3},{3,2},{4,5},{5,4},{6,7},{7,6},{8,9},{9,8},{10,11... | collective-permute-start | bytes 3145736 | tf_op jit(solution)/shard_map/ppermute | solution.py:261
  104.8 14.7 %all-to-all-start = ((f32[8,9,8,128]{3,2,1,0:T(8,128)}), f32[8,9,8,128]{3,2,1,0:T(8,128)S(1)}, u32[]{:S(2)}, u32[]{:S(2)}) async-start(f32[8,9,8,128]{3,2,1,0:T(8,128)} %shard_map.88), calls=%async_computation | async-start | bytes 589824 | tf_op jit(solution)/shard_map/all_to_all | solution.py:287
  119.8 3.8 %collective-permute-start.31 = (bf16[64,128]{1,0:T(8,128)(2,1)S(1)}, bf16[64,128]{1,0:T(8,128)(2,1)S(1)}, u32[]{:S(2)}, u32[]{:S(2)}) collective-permute-start(bf16[64,128]{1,0:T(8,128)(2,1)S(1)} %shard_map.89), channel_id=1, source_target_pairs={{0,2},{2,0},{4,6},{6,4},{8,10},{10,8},{12,14},{14,12},{1,3},{3,1},... | collective-permute-start | bytes 49160 | tf_op jit(solution)/shard_map/ppermute | solution.py:291
  123.7 5.8 %collective-permute-start.32 = (bf16[128,128]{1,0:T(8,128)(2,1)S(1)}, bf16[128,128]{1,0:T(8,128)(2,1)S(1)}, u32[]{:S(2)}, u32[]{:S(2)}) collective-permute-start(bf16[128,128]{1,0:T(8,128)(2,1)S(1)} %pad_maximum_fusion.2), channel_id=1, source_target_pairs={{0,12},{2,14},{4,8},{6,10},{8,4},{10,6},{12,0},{14,2},{1,13},{3,15... | collective-permute-start | bytes 98312 | tf_op jit(solution)/shard_map/ppermute | solution.py:294
  124.9 5.3 %collective-permute-start.33 = (bf16[128,128]{1,0:T(8,128)(2,1)S(1)}, bf16[128,128]{1,0:T(8,128)(2,1)S(1)}, u32[]{:S(2)}, u32[]{:S(2)}) collective-permute-start(bf16[128,128]{1,0:T(8,128)(2,1)S(1)} %pad_maximum_fusion.2), channel_id=1, source_target_pairs={{0,8},{2,10},{4,12},{6,14},{8,0},{10,2},{12,4},{14,6},{1,9},{3,11}... | collective-permute-start | bytes 98312 | tf_op jit(solution)/shard_map/ppermute | solution.py:294
  126.3 4.2 %collective-permute-start.34 = (bf16[128,128]{1,0:T(8,128)(2,1)S(1)}, bf16[128,128]{1,0:T(8,128)(2,1)S(1)}, u32[]{:S(2)}, u32[]{:S(2)}) collective-permute-start(bf16[128,128]{1,0:T(8,128)(2,1)S(1)} %pad_maximum_fusion.2), channel_id=1, source_target_pairs={{0,4},{2,6},{4,0},{6,2},{8,12},{10,14},{12,8},{14,10},{1,5},{3,7},... | collective-permute-start | bytes 98312 | tf_op jit(solution)/shard_map/ppermute | solution.py:294
  130.6 1.4 %collective-permute-start.35 = (bf16[16,1,4096]{2,0,1:T(8,128)(2,1)S(1)}, bf16[16,1,4096]{2,0,1:T(8,128)(2,1)S(1)}, u32[]{:S(2)}, u32[]{:S(2)}) collective-permute-start(bf16[16,1,4096]{2,0,1:T(8,128)(2,1)S(1)} %reshape.89), channel_id=1, source_target_pairs={{0,1},{1,0},{2,3},{3,2},{4,5},{5,4},{6,7},{7,6},{8,9},{9,8},{10,11... | collective-permute-start | bytes 393224 | tf_op jit(solution)/shard_map/ppermute | solution.py:304

commit v19 on v18

--- a/solution.py
+++ b/solution.py
@@ -300,7 +300,7 @@
         whole = jnp.concatenate([of(z) for z in range(4)], 0)
     else:
         whole = lax.all_gather(result, "chip", axis=0, tiled=True)
-    whole = whole.reshape(pairs, 1, rows // pairs * DH)
+    whole = whole.reshape(pairs, 1, rows // pairs, DH)
     away = lax.ppermute(whole, "core", SWAP)
     whole = jnp.concatenate([jnp.where(first, whole, away), jnp.where(first, away, whole)], 1)
     return whole.reshape(steps_count, req_count, QH * DH)

time: 134 us -> 133 us (level)
  no operation moved by 1% of the time
where the time goes in v19:
time: 133 us
  waiting for transfers between devices  48.7 us (37%)
  starting transfers between devices  43.4 us (33%)
  Pallas kernels  32.6 us (25%)
  local copies, waits for them, and re-layouts  4.08 us (3%)
  other arithmetic  2.34 us (2%)
  matrix products  1.36 us (1%)
    ppermute x28, waiting for transfers between devices, project(): held[k] = lax.ppermute(held[k], 'chip', ways[k])  33.4 us
    ppermute x28, starting transfers between devices, project(): held[k] = lax.ppermute(held[k], 'chip', ways[k])  32 us
    pallas_call x6, Pallas kernels, add_pieces(): pl.pallas_call(kernel, out_shape=(jax.ShapeDtypeStruct((2 * tok_rows, wid...  27.5 us
    all_to_all x1, waiting for transfers between devices, on_device(): lax.all_to_all(sending, 'chip', split_axis=0, concat_axis=0, tiled=True)  8.6 us
    all_to_all x1, starting transfers between devices, on_device(): lax.all_to_all(sending, 'chip', split_axis=0, concat_axis=0, tiled=True)  4.82 us
    pallas_call x1, Pallas kernels, attend(): pl.pallas_call(kernel, out_shape=jax.ShapeDtypeStruct((chips, blocks + 1,...  4.66 us
    ppermute x3, starting transfers between devices, on_device(): lax.ppermute(couple, 'chip', [(c, c ^ 2 * d) for c in range(chips)])  4.45 us
  transfers between devices with their start and end apart: 37, of which 18 were waited for; matrix products, arithmetic and copies ran while one was open for 4% of the time, Pallas kernels for 18%

profile of v19, /device:TPU:0, one launch (start us, length us, event | category | flops | bytes accessed | tf_op | source)
XLA Modules:
  0.0 132.8 jit_solution(4868060307038710258)
XLA Ops:
  0.0 1.3 broadcast_select_fusion
  1.3 0.5 collective-permute-start.2
  1.9 2.6 %collective-permute-start = (bf16[256,512]{1,0:T(8,128)(2,1)S(1)}, bf16[256,512]{1,0:T(8,128)(2,1)S(1)}, u32[]{:S(2)}, u32[]{:S(2)}) collective-permute-start(bf16[256,512]{1,0:T(8,128)(2,1)S(1)} %get-tuple-element.88), channel_id=1, source_target_pairs={{0,4},{4,8},{8,12},{12,14},{14,10},{10,6},{6,2},{2,0},{1,5},{5,9},... | collective-permute-start | bytes 786440 | tf_op jit(solution)/shard_map/ppermute | solution.py:142
  4.5 1.6 %collective-permute-start.1 = (bf16[256,512]{1,0:T(8,128)(2,1)S(1)}, bf16[256,512]{1,0:T(8,128)(2,1)S(1)}, u32[]{:S(2)}, u32[]{:S(2)}) collective-permute-start(bf16[256,512]{1,0:T(8,128)(2,1)S(1)} %get-tuple-element.87), channel_id=1, source_target_pairs={{0,4},{4,8},{8,12},{12,14},{14,10},{10,6},{6,2},{2,0},{1,5},{5,9},... | collective-permute-start | bytes 786440 | tf_op jit(solution)/shard_map/ppermute | solution.py:142
  6.1 0.5 collective-permute-start.3
  6.6 1.3 collective-permute-start.4
  7.9 3.7 %collective-permute-done.refs_2_ = bf16[256,512]{1,0:T(8,128)(2,1)S(1)} collective-permute-done((bf16[256,512]{1,0:T(8,128)(2,1)S(1)}, bf16[256,512]{1,0:T(8,128)(2,1)S(1)}, u32[]{:S(2)}, u32[]{:S(2)}) %collective-permute-start) | collective-permute-done | bytes 262176 | tf_op jit(solution)/shard_map/ppermute | solution.py:142
  11.6 5.4 %collective-permute-done.1.refs_3_ = bf16[256,512]{1,0:T(8,128)(2,1)S(1)} collective-permute-done((bf16[256,512]{1,0:T(8,128)(2,1)S(1)}, bf16[256,512]{1,0:T(8,128)(2,1)S(1)}, u32[]{:S(2)}, u32[]{:S(2)}) %collective-permute-start.1) | collective-permute-done | bytes 262176 | tf_op jit(solution)/shard_map/ppermute | solution.py:142
  17.1 2.9 %collective-permute-done.4.refs_5_ = bf16[256,512]{1,0:T(8,128)(2,1)S(1)} collective-permute-done((bf16[256,512]{1,0:T(8,128)(2,1)S(1)}, bf16[256,512]{1,0:T(8,128)(2,1)S(1)}, u32[]{:S(2)}, u32[]{:S(2)}) %collective-permute-start.4) | collective-permute-done | bytes 262176 | tf_op jit(solution)/shard_map/ppermute | solution.py:142
  20.0 0.4 collective-permute-start.11
  20.4 1.6 %collective-permute-start.6 = (bf16[256,512]{1,0:T(8,128)(2,1)S(1)}, bf16[256,512]{1,0:T(8,128)(2,1)}, u32[]{:S(2)}, u32[]{:S(2)}) collective-permute-start(bf16[256,512]{1,0:T(8,128)(2,1)S(1)} %collective-permute-done.refs_2_), channel_id=1, source_target_pairs={{0,4},{4,8},{8,12},{12,14},{14,10},{10,6},{6,2},{2,0},{1,5},{5,9},... | collective-permute-start | bytes 786440 | tf_op jit(solution)/shard_map/ppermute | solution.py:142
  22.0 1.6 %collective-permute-start.9 = (bf16[256,512]{1,0:T(8,128)(2,1)S(1)}, bf16[256,512]{1,0:T(8,128)(2,1)}, u32[]{:S(2)}, u32[]{:S(2)}) collective-permute-start(bf16[256,512]{1,0:T(8,128)(2,1)S(1)} %collective-permute-done.1.refs_3_), channel_id=1, source_target_pairs={{0,4},{4,8},{8,12},{12,14},{14,10},{10,6},{6,2},{2,0},{1,5},{5,9},... | collective-permute-start | bytes 786440 | tf_op jit(solution)/shard_map/ppermute | solution.py:142
  23.6 0.4 collective-permute-start.10
  24.1 5.1 %collective-permute-done.11.refs_3_ = bf16[256,512]{1,0:T(8,128)(2,1)} collective-permute-done((bf16[256,512]{1,0:T(8,128)(2,1)S(1)}, bf16[256,512]{1,0:T(8,128)(2,1)}, u32[]{:S(2)}, u32[]{:S(2)}) %collective-permute-start.11) | collective-permute-done | bytes 262176 | tf_op jit(solution)/shard_map/ppermute | solution.py:142
  29.2 0.4 collective-permute-start.15
  29.7 1.6 %collective-permute-start.7 = (bf16[256,512]{1,0:T(8,128)(2,1)}, bf16[256,512]{1,0:T(8,128)(2,1)}, u32[]{:S(2)}, u32[]{:S(2)}) collective-permute-start(bf16[256,512]{1,0:T(8,128)(2,1)} %collective-permute-done.6.refs_0_), channel_id=1, source_target_pairs={{0,4},{4,8},{8,12},{12,14},{14,10},{10,6},{6,2},{2,0},{1,5},{5,9},... | collective-permute-start | bytes 786440 | tf_op jit(solution)/shard_map/ppermute | solution.py:142
  31.2 4.0 %collective-permute-done.9.refs_1_ = bf16[256,512]{1,0:T(8,128)(2,1)} collective-permute-done((bf16[256,512]{1,0:T(8,128)(2,1)S(1)}, bf16[256,512]{1,0:T(8,128)(2,1)}, u32[]{:S(2)}, u32[]{:S(2)}) %collective-permute-start.9) | collective-permute-done | bytes 262176 | tf_op jit(solution)/shard_map/ppermute | solution.py:142
  35.3 1.6 %collective-permute-start.13 = (bf16[256,512]{1,0:T(8,128)(2,1)}, bf16[256,512]{1,0:T(8,128)(2,1)}, u32[]{:S(2)}, u32[]{:S(2)}) collective-permute-start(bf16[256,512]{1,0:T(8,128)(2,1)} %collective-permute-done.9.refs_1_), channel_id=1, source_target_pairs={{0,4},{4,8},{8,12},{12,14},{14,10},{10,6},{6,2},{2,0},{1,5},{5,9},... | collective-permute-start | bytes 786440 | tf_op jit(solution)/shard_map/ppermute | solution.py:142
  36.9 0.4 collective-permute-start.14
  37.4 5.7 %shard_map.82 = (f32[1024,512]{1,0:T(8,128)S(1)}, f32[8,128]{1,0:T(8,128)}) custom-call(s32[4]{0:T(128)S(1)} %pad_add_fusion.1.places_ref, bf16[512,8192]{1,0:T(8,128)(2,1)} %mine_ref.11, bf16[512,8192]{1,0:T(8,128)(2,1)} %collective-permute-done.5.theirs_ref, bf16[512,512]{1,0:T(8,128)(2,1)S(1)} %get-tuple-element.84.refs_0_, ...), custom_call_target="tpu_custom_call" | custom-call | flops 2147483648 | bytes 4194304 | tf_op jit(solution)/shard_map/pallas_call | solution.py:73
  43.1 1.5 %collective-permute-start.19 = (bf16[256,512]{1,0:T(8,128)(2,1)}, bf16[256,512]{1,0:T(8,128)(2,1)}, u32[]{:S(2)}, u32[]{:S(2)}) collective-permute-start(bf16[256,512]{1,0:T(8,128)(2,1)} %collective-permute-done.15.refs_3_), channel_id=1, source_target_pairs={{4,0},{8,4},{12,8},{14,12},{10,14},{6,10},{2,6},{0,2},{5,1},{9,5},... | collective-permute-start | bytes 786440 | tf_op jit(solution)/shard_map/ppermute | solution.py:142
  44.7 1.8 %collective-permute-done.14.refs_2_ = bf16[256,512]{1,0:T(8,128)(2,1)} collective-permute-done((bf16[256,512]{1,0:T(8,128)(2,1)}, bf16[256,512]{1,0:T(8,128)(2,1)}, u32[]{:S(2)}, u32[]{:S(2)}) %collective-permute-start.14) | collective-permute-done | bytes 262176 | tf_op jit(solution)/shard_map/ppermute | solution.py:142
  46.4 2.0 %collective-permute-start.17 = (bf16[256,512]{1,0:T(8,128)(2,1)}, bf16[256,512]{1,0:T(8,128)(2,1)}, u32[]{:S(2)}, u32[]{:S(2)}) collective-permute-start(bf16[256,512]{1,0:T(8,128)(2,1)} %collective-permute-done.13.refs_1_), channel_id=1, source_target_pairs={{0,4},{4,8},{8,12},{12,14},{14,10},{10,6},{6,2},{2,0},{1,5},{5,9},... | collective-permute-start | bytes 786440 | tf_op jit(solution)/shard_map/ppermute | solution.py:142
  48.4 1.6 %collective-permute-start.8 = (bf16[256,512]{1,0:T(8,128)(2,1)}, bf16[256,512]{1,0:T(8,128)(2,1)}, u32[]{:S(2)}, u32[]{:S(2)}) collective-permute-start(bf16[256,512]{1,0:T(8,128)(2,1)} %collective-permute-done.7.refs_0_), channel_id=1, source_target_pairs={{0,4},{4,8},{8,12},{12,14},{14,10},{10,6},{6,2},{2,0},{1,5},{5,9},... | collective-permute-start | bytes 786440 | tf_op jit(solution)/shard_map/ppermute | solution.py:142
  50.2 1.3 constant_dynamic-slice_fusion.1
  51.5 3.9 %shard_map.83 = (f32[1024,512]{1,0:T(8,128)S(1)}, f32[8,128]{1,0:T(8,128)}) custom-call(s32[2]{0:T(128)S(1)} %pad_add_fusion.2.places_ref, bf16[512,8192]{1,0:T(8,128)(2,1)} %mine_ref.11, bf16[512,8192]{1,0:T(8,128)(2,1)} %collective-permute-done.5.theirs_ref, bf16[256,512]{1,0:T(8,128)(2,1)} %collective-permute-done.6.refs_0_, ...), custom_call_target="tpu_custom_call", output_to_operand_aliasing={{0}: (7, {})} | custom-call | flops 1073741824 | bytes 2097152 | tf_op jit(solution)/shard_map/pallas_call | solution.py:73
  55.4 0.5 collective-permute-start.27
  55.9 1.6 %collective-permute-done.18.refs_2_ = bf16[256,512]{1,0:T(8,128)(2,1)} collective-permute-done((bf16[256,512]{1,0:T(8,128)(2,1)}, bf16[256,512]{1,0:T(8,128)(2,1)}, u32[]{:S(2)}, u32[]{:S(2)}) %collective-permute-start.18) | collective-permute-done | bytes 262176 | tf_op jit(solution)/shard_map/ppermute | solution.py:142
  57.5 0.5 collective-permute-start.24
  58.0 1.5 %collective-permute-start.21 = (bf16[256,512]{1,0:T(8,128)(2,1)}, bf16[256,512]{1,0:T(8,128)(2,1)}, u32[]{:S(2)}, u32[]{:S(2)}) collective-permute-start(bf16[256,512]{1,0:T(8,128)(2,1)} %collective-permute-done.17.refs_1_), channel_id=1, source_target_pairs={{0,4},{4,8},{8,12},{12,14},{14,10},{10,6},{6,2},{2,0},{1,5},{5,9},... | collective-permute-start | bytes 786440 | tf_op jit(solution)/shard_map/ppermute | solution.py:142
  59.5 0.7 collective-permute-done.8.refs_0_
  60.2 1.4 %collective-permute-start.12 = (bf16[256,512]{1,0:T(8,128)(2,1)}, bf16[256,512]{1,0:T(8,128)(2,1)}, u32[]{:S(2)}, u32[]{:S(2)}) collective-permute-start(bf16[256,512]{1,0:T(8,128)(2,1)} %collective-permute-done.8.refs_0_), channel_id=1, source_target_pairs={{0,4},{4,8},{8,12},{12,14},{14,10},{10,6},{6,2},{2,0},{1,5},{5,9},... | collective-permute-start | bytes 786440 | tf_op jit(solution)/shard_map/ppermute | solution.py:142
  61.7 3.9 %shard_map.84 = (f32[1024,512]{1,0:T(8,128)S(1)}, f32[8,128]{1,0:T(8,128)}) custom-call(s32[2]{0:T(128)S(1)} %pad_add_fusion.3.places_ref, bf16[512,8192]{1,0:T(8,128)(2,1)} %mine_ref.11, bf16[512,8192]{1,0:T(8,128)(2,1)} %collective-permute-done.5.theirs_ref, bf16[256,512]{1,0:T(8,128)(2,1)} %collective-permute-done.7.refs_0_, ...), custom_call_target="tpu_custom_call", output_to_operand_aliasing={{0}: (7, {})} | custom-call | flops 1073741824 | bytes 2097152 | tf_op jit(solution)/shard_map/pallas_call | solution.py:73
  65.6 1.1 collective-permute-start.28
  66.7 4.0 %collective-permute-done.24.refs_2_ = bf16[256,512]{1,0:T(8,128)(2,1)} collective-permute-done((bf16[256,512]{1,0:T(8,128)(2,1)}, bf16[256,512]{1,0:T(8,128)(2,1)}, u32[]{:S(2)}, u32[]{:S(2)}) %collective-permute-start.24) | collective-permute-done | bytes 262176 | tf_op jit(solution)/shard_map/ppermute | solution.py:142
  70.7 0.4 collective-permute-start.25
  71.1 1.6 %collective-permute-start.22 = (bf16[256,512]{1,0:T(8,128)(2,1)}, bf16[256,512]{1,0:T(8,128)(2,1)}, u32[]{:S(2)}, u32[]{:S(2)}) collective-permute-start(bf16[256,512]{1,0:T(8,128)(2,1)} %collective-permute-done.21.refs_1_), channel_id=1, source_target_pairs={{0,4},{4,8},{8,12},{12,14},{14,10},{10,6},{6,2},{2,0},{1,5},{5,9},... | collective-permute-start | bytes 786440 | tf_op jit(solution)/shard_map/ppermute | solution.py:142
  72.7 1.5 %collective-permute-start.16 = (bf16[256,512]{1,0:T(8,128)(2,1)}, bf16[256,512]{1,0:T(8,128)(2,1)}, u32[]{:S(2)}, u32[]{:S(2)}) collective-permute-start(bf16[256,512]{1,0:T(8,128)(2,1)} %collective-permute-done.12.refs_0_), channel_id=1, source_target_pairs={{0,4},{4,8},{8,12},{12,14},{14,10},{10,6},{6,2},{2,0},{1,5},{5,9},... | collective-permute-start | bytes 786440 | tf_op jit(solution)/shard_map/ppermute | solution.py:142
  74.5 3.9 %shard_map.85 = (f32[1024,512]{1,0:T(8,128)S(1)}, f32[8,128]{1,0:T(8,128)}) custom-call(s32[2]{0:T(128)S(1)} %pad_add_fusion.4.places_ref, bf16[512,8192]{1,0:T(8,128)(2,1)} %mine_ref.11, bf16[512,8192]{1,0:T(8,128)(2,1)} %collective-permute-done.5.theirs_ref, bf16[256,512]{1,0:T(8,128)(2,1)} %collective-permute-done.8.refs_0_, ...), custom_call_target="tpu_custom_call", output_to_operand_aliasing={{0}: (7, {})} | custom-call | flops 1073741824 | bytes 2097152 | tf_op jit(solution)/shard_map/pallas_call | solution.py:73
  78.5 0.6 collective-permute-start.29
  79.0 2.9 %collective-permute-done.25.refs_6_ = bf16[256,512]{1,0:T(8,128)(2,1)} collective-permute-done((bf16[256,512]{1,0:T(8,128)(2,1)}, bf16[256,512]{1,0:T(8,128)(2,1)}, u32[]{:S(2)}, u32[]{:S(2)}) %collective-permute-start.25) | collective-permute-done | bytes 262176 | tf_op jit(solution)/shard_map/ppermute | solution.py:142
  81.9 0.4 collective-permute-start.26
  82.3 1.6 %collective-permute-start.23 = (bf16[256,512]{1,0:T(8,128)(2,1)}, bf16[256,512]{1,0:T(8,128)(2,1)S(1)}, u32[]{:S(2)}, u32[]{:S(2)}) collective-permute-start(bf16[256,512]{1,0:T(8,128)(2,1)} %collective-permute-done.22.refs_5_), channel_id=1, source_target_pairs={{0,4},{4,8},{8,12},{12,14},{14,10},{10,6},{6,2},{2,0},{1,5},{5,9},... | collective-permute-start | bytes 786440 | tf_op jit(solution)/shard_map/ppermute | solution.py:142
  83.9 1.5 %collective-permute-start.20 = (bf16[256,512]{1,0:T(8,128)(2,1)}, bf16[256,512]{1,0:T(8,128)(2,1)S(1)}, u32[]{:S(2)}, u32[]{:S(2)}) collective-permute-start(bf16[256,512]{1,0:T(8,128)(2,1)} %collective-permute-done.16.refs_4_), channel_id=1, source_target_pairs={{0,4},{4,8},{8,12},{12,14},{14,10},{10,6},{6,2},{2,0},{1,5},{5,9},... | collective-permute-start | bytes 786440 | tf_op jit(solution)/shard_map/ppermute | solution.py:142
  85.5 6.0 %shard_map.86 = (f32[1024,512]{1,0:T(8,128)S(1)}, f32[8,128]{1,0:T(8,128)}) custom-call(s32[4]{0:T(128)S(1)} %pad_add_fusion.5.places_ref, bf16[512,8192]{1,0:T(8,128)(2,1)} %mine_ref.11, bf16[512,8192]{1,0:T(8,128)(2,1)} %collective-permute-done.5.theirs_ref, bf16[256,512]{1,0:T(8,128)(2,1)} %collective-permute-done.12.refs_0_, ...), custom_call_target="tpu_custom_call", output_to_operand_aliasing={{0}: (11, {})} | custom-call | flops 2147483648 | bytes 4194304 | tf_op jit(solution)/shard_map/pallas_call | solution.py:73
  91.6 1.4 %collective-permute-done.20.refs_0_ = bf16[256,512]{1,0:T(8,128)(2,1)S(1)} collective-permute-done((bf16[256,512]{1,0:T(8,128)(2,1)}, bf16[256,512]{1,0:T(8,128)(2,1)S(1)}, u32[]{:S(2)}, u32[]{:S(2)}) %collective-permute-start.20) | collective-permute-done | bytes 262176 | tf_op jit(solution)/shard_map/ppermute | solution.py:142
  93.0 4.2 %shard_map.87 = (bf16[1024,512]{1,0:T(8,128)(2,1)}, f32[8,128]{1,0:T(8,128)}) custom-call(s32[4]{0:T(128)S(1)} %pad_add_fusion.places_ref, bf16[512,8192]{1,0:T(8,128)(2,1)} %mine_ref.11, bf16[512,8192]{1,0:T(8,128)(2,1)} %collective-permute-done.5.theirs_ref, bf16[256,512]{1,0:T(8,128)(2,1)S(1)} %collective-permute-done.20.refs_0_, ...), custom_call_target="tpu_custom_call" | custom-call | flops 1073741824 | bytes 2097152 | tf_op jit(solution)/shard_map/pallas_call | solution.py:73
  97.5 0.8 reshape.81
  98.7 0.7 fusion.17
  99.4 0.7 collective-permute-done.30.got_ref
  100.1 4.7 %shard_map.88 = f32[8,9,8,128]{3,2,1,0:T(8,128)} custom-call(s32[1]{0:T(128)} %bitcast.core_ref, bf16[1024,512]{1,0:T(8,128)(2,1)} %get-tuple-element.78.have_ref, bf16[1024,512]{1,0:T(8,128)(2,1)S(1)} %collective-permute-done.30.got_ref, bf16[512,512]{1,0:T(8,128)(2,1)S(1)} %get-tuple-element.79.key_up_ref, ...), custom_call_target="tpu_custom_call" | custom-call | flops 1342177280 | bytes 2097152 | tf_op jit(solution)/shard_map/pallas_call | solution.py:194
  104.8 4.8 %all-to-all-start = ((f32[8,9,8,128]{3,2,1,0:T(8,128)}), f32[8,9,8,128]{3,2,1,0:T(8,128)S(1)}, u32[]{:S(2)}, u32[]{:S(2)}) async-start(f32[8,9,8,128]{3,2,1,0:T(8,128)} %shard_map.88), calls=%async_computation | async-start | bytes 589824 | tf_op jit(solution)/shard_map/all_to_all | solution.py:287
  109.6 0.3 convolution_bitcast_fusion
  110.9 8.6 %all-to-all-done.arrived_ref = f32[8,9,8,128]{3,2,1,0:T(8,128)S(1)} async-done(((f32[8,9,8,128]{3,2,1,0:T(8,128)}), f32[8,9,8,128]{3,2,1,0:T(8,128)S(1)}, u32[]{:S(2)}, u32[]{:S(2)}) %all-to-all-start) | async-done | bytes 294944 | tf_op jit(solution)/shard_map/all_to_all | solution.py:287
  119.5 0.4 shard_map.89
  119.8 1.5 %collective-permute-start.31 = (bf16[64,128]{1,0:T(8,128)(2,1)S(1)}, bf16[64,128]{1,0:T(8,128)(2,1)S(1)}, u32[]{:S(2)}, u32[]{:S(2)}) collective-permute-start(bf16[64,128]{1,0:T(8,128)(2,1)S(1)} %shard_map.89), channel_id=1, source_target_pairs={{0,2},{2,0},{4,6},{6,4},{8,10},{10,8},{12,14},{14,12},{1,3},{3,1},... | collective-permute-start | bytes 49160 | tf_op jit(solution)/shard_map/ppermute | solution.py:291
  121.4 2.3 %collective-permute-done.31 = bf16[64,128]{1,0:T(8,128)(2,1)S(1)} collective-permute-done((bf16[64,128]{1,0:T(8,128)(2,1)S(1)}, bf16[64,128]{1,0:T(8,128)(2,1)S(1)}, u32[]{:S(2)}, u32[]{:S(2)}) %collective-permute-start.31) | collective-permute-done | bytes 16416 | tf_op jit(solution)/shard_map/ppermute | solution.py:291
  123.7 1.2 collective-permute-start.32
  124.9 1.3 %collective-permute-start.33 = (bf16[128,128]{1,0:T(8,128)(2,1)S(1)}, bf16[128,128]{1,0:T(8,128)(2,1)S(1)}, u32[]{:S(2)}, u32[]{:S(2)}) collective-permute-start(bf16[128,128]{1,0:T(8,128)(2,1)S(1)} %pad_maximum_fusion.2), channel_id=1, source_target_pairs={{0,8},{2,10},{4,12},{6,14},{8,0},{10,2},{12,4},{14,6},{1,9},{3,11}... | collective-permute-start | bytes 98312 | tf_op jit(solution)/shard_map/ppermute | solution.py:294
  126.3 1.9 %collective-permute-start.34 = (bf16[128,128]{1,0:T(8,128)(2,1)S(1)}, bf16[128,128]{1,0:T(8,128)(2,1)S(1)}, u32[]{:S(2)}, u32[]{:S(2)}) collective-permute-start(bf16[128,128]{1,0:T(8,128)(2,1)S(1)} %pad_maximum_fusion.2), channel_id=1, source_target_pairs={{0,4},{2,6},{4,0},{6,2},{8,12},{10,14},{12,8},{14,10},{1,5},{3,7},... | collective-permute-start | bytes 98312 | tf_op jit(solution)/shard_map/ppermute | solution.py:294
  128.1 1.3 %collective-permute-done.32 = bf16[128,128]{1,0:T(8,128)(2,1)S(1)} collective-permute-done((bf16[128,128]{1,0:T(8,128)(2,1)S(1)}, bf16[128,128]{1,0:T(8,128)(2,1)S(1)}, u32[]{:S(2)}, u32[]{:S(2)}) %collective-permute-start.32) | collective-permute-done | bytes 32800 | tf_op jit(solution)/shard_map/ppermute | solution.py:294
  129.4 0.8 collective-permute-done.33
  130.6 1.3 %collective-permute-done.35 = bf16[16,1,32,128]{3,2,0,1:T(8,128)(2,1)S(1)} collective-permute-done((bf16[16,1,32,128]{3,2,0,1:T(8,128)(2,1)S(1)}, bf16[16,1,32,128]{3,2,0,1:T(8,128)(2,1)S(1)}, u32[]{:S(2)}, u32[]{:S(2)}) %collective-permute-start.35) | collective-permute-done | bytes 131104 | tf_op jit(solution)/shard_map/ppermute | solution.py:304
  132.0 0.8 reshape.90
  (78 shorter events, 3.1 us)
Async XLA Ops:
  0.0 50.0 %copy-start = (bf16[4,4,8192]{2,1,0:T(4,128)(2,1)S(1)}, bf16[4,4,8192]{2,1,0:T(4,128)(2,1)}, u32[]{:S(2)}) copy-start(bf16[4,4,8192]{2,1,0:T(4,128)(2,1)} %param.14) | copy-start | bytes 786436
  1.3 4.8 %collective-permute-start.2 = (bf16[512,512]{1,0:T(8,128)(2,1)S(1)}, bf16[512,512]{1,0:T(8,128)(2,1)S(1)}, u32[]{:S(2)}, u32[]{:S(2)}) collective-permute-start(bf16[512,512]{1,0:T(8,128)(2,1)S(1)} %get-tuple-element.83), channel_id=1, source_target_pairs={{0,1},{1,0},{2,3},{3,2},{4,5},{5,4},{6,7},{7,6},{8,9},{9,8},{10,11... | collective-permute-start | bytes 1572872 | tf_op jit(solution)/shard_map/ppermute | solution.py:103
  1.9 9.7 %collective-permute-start = (bf16[256,512]{1,0:T(8,128)(2,1)S(1)}, bf16[256,512]{1,0:T(8,128)(2,1)S(1)}, u32[]{:S(2)}, u32[]{:S(2)}) collective-permute-start(bf16[256,512]{1,0:T(8,128)(2,1)S(1)} %get-tuple-element.88), channel_id=1, source_target_pairs={{0,4},{4,8},{8,12},{12,14},{14,10},{10,6},{6,2},{2,0},{1,5},{5,9},... | collective-permute-start | bytes 786440 | tf_op jit(solution)/shard_map/ppermute | solution.py:142
  4.5 12.5 %collective-permute-start.1 = (bf16[256,512]{1,0:T(8,128)(2,1)S(1)}, bf16[256,512]{1,0:T(8,128)(2,1)S(1)}, u32[]{:S(2)}, u32[]{:S(2)}) collective-permute-start(bf16[256,512]{1,0:T(8,128)(2,1)S(1)} %get-tuple-element.87), channel_id=1, source_target_pairs={{0,4},{4,8},{8,12},{12,14},{14,10},{10,6},{6,2},{2,0},{1,5},{5,9},... | collective-permute-start | bytes 786440 | tf_op jit(solution)/shard_map/ppermute | solution.py:142
  6.1 10.9 %collective-permute-start.3 = (bf16[256,512]{1,0:T(8,128)(2,1)S(1)}, bf16[256,512]{1,0:T(8,128)(2,1)S(1)}, u32[]{:S(2)}, u32[]{:S(2)}) collective-permute-start(bf16[256,512]{1,0:T(8,128)(2,1)S(1)} %get-tuple-element.86), channel_id=1, source_target_pairs={{4,0},{8,4},{12,8},{14,12},{10,14},{6,10},{2,6},{0,2},{5,1},{9,5},... | collective-permute-start | bytes 786440 | tf_op jit(solution)/shard_map/ppermute | solution.py:142
  6.6 13.3 %collective-permute-start.4 = (bf16[256,512]{1,0:T(8,128)(2,1)S(1)}, bf16[256,512]{1,0:T(8,128)(2,1)S(1)}, u32[]{:S(2)}, u32[]{:S(2)}) collective-permute-start(bf16[256,512]{1,0:T(8,128)(2,1)S(1)} %get-tuple-element.85), channel_id=1, source_target_pairs={{4,0},{8,4},{12,8},{14,12},{10,14},{6,10},{2,6},{0,2},{5,1},{9,5},... | collective-permute-start | bytes 786440 | tf_op jit(solution)/shard_map/ppermute | solution.py:142
  11.6 25.8 %copy-start.1 = (bf16[256,512]{1,0:T(8,128)(2,1)}, bf16[256,512]{1,0:T(8,128)(2,1)S(1)}, u32[]{:S(2)}) copy-start(bf16[256,512]{1,0:T(8,128)(2,1)S(1)} %collective-permute-done.refs_2_) | copy-start | bytes 786436
  17.0 20.3 %copy-start.2 = (bf16[256,512]{1,0:T(8,128)(2,1)}, bf16[256,512]{1,0:T(8,128)(2,1)S(1)}, u32[]{:S(2)}) copy-start(bf16[256,512]{1,0:T(8,128)(2,1)S(1)} %collective-permute-done.1.refs_3_) | copy-start | bytes 786436
  17.0 20.3 %copy-start.3 = (bf16[256,512]{1,0:T(8,128)(2,1)}, bf16[256,512]{1,0:T(8,128)(2,1)S(1)}, u32[]{:S(2)}) copy-start(bf16[256,512]{1,0:T(8,128)(2,1)S(1)} %collective-permute-done.3.refs_4_) | copy-start | bytes 786436
  20.0 17.4 %copy-start.4 = (bf16[256,512]{1,0:T(8,128)(2,1)}, bf16[256,512]{1,0:T(8,128)(2,1)S(1)}, u32[]{:S(2)}) copy-start(bf16[256,512]{1,0:T(8,128)(2,1)S(1)} %collective-permute-done.4.refs_5_) | copy-start | bytes 786436
  20.0 17.4 %collective-permute-start.5 = (bf16[512,8192]{1,0:T(8,128)(2,1)}, bf16[512,8192]{1,0:T(8,128)(2,1)}, u32[]{:S(2)}, u32[]{:S(2)}) collective-permute-start(bf16[512,8192]{1,0:T(8,128)(2,1)} %mine_ref.11), channel_id=1, source_target_pairs={{0,1},{1,0},{2,3},{3,2},{4,5},{5,4},{6,7},{7,6},{8,9},{9,8},{10,11... | collective-permute-start | bytes 25165832 | tf_op jit(solution)/shard_map/ppermute | solution.py:133
  20.0 9.2 %collective-permute-start.11 = (bf16[256,512]{1,0:T(8,128)(2,1)S(1)}, bf16[256,512]{1,0:T(8,128)(2,1)}, u32[]{:S(2)}, u32[]{:S(2)}) collective-permute-start(bf16[256,512]{1,0:T(8,128)(2,1)S(1)} %collective-permute-done.4.refs_5_), channel_id=1, source_target_pairs={{4,0},{8,4},{12,8},{14,12},{10,14},{6,10},{2,6},{0,2},{5,1},{9,5},... | collective-permute-start | bytes 786440 | tf_op jit(solution)/shard_map/ppermute | solution.py:142
  20.4 9.2 %collective-permute-start.6 = (bf16[256,512]{1,0:T(8,128)(2,1)S(1)}, bf16[256,512]{1,0:T(8,128)(2,1)}, u32[]{:S(2)}, u32[]{:S(2)}) collective-permute-start(bf16[256,512]{1,0:T(8,128)(2,1)S(1)} %collective-permute-done.refs_2_), channel_id=1, source_target_pairs={{0,4},{4,8},{8,12},{12,14},{14,10},{10,6},{6,2},{2,0},{1,5},{5,9},... | collective-permute-start | bytes 786440 | tf_op jit(solution)/shard_map/ppermute | solution.py:142
  22.0 13.3 %collective-permute-start.9 = (bf16[256,512]{1,0:T(8,128)(2,1)S(1)}, bf16[256,512]{1,0:T(8,128)(2,1)}, u32[]{:S(2)}, u32[]{:S(2)}) collective-permute-start(bf16[256,512]{1,0:T(8,128)(2,1)S(1)} %collective-permute-done.1.refs_3_), channel_id=1, source_target_pairs={{0,4},{4,8},{8,12},{12,14},{14,10},{10,6},{6,2},{2,0},{1,5},{5,9},... | collective-permute-start | bytes 786440 | tf_op jit(solution)/shard_map/ppermute | solution.py:142
  23.6 13.3 %collective-permute-start.10 = (bf16[256,512]{1,0:T(8,128)(2,1)S(1)}, bf16[256,512]{1,0:T(8,128)(2,1)}, u32[]{:S(2)}, u32[]{:S(2)}) collective-permute-start(bf16[256,512]{1,0:T(8,128)(2,1)S(1)} %collective-permute-done.3.refs_4_), channel_id=1, source_target_pairs={{4,0},{8,4},{12,8},{14,12},{10,14},{6,10},{2,6},{0,2},{5,1},{9,5},... | collective-permute-start | bytes 786440 | tf_op jit(solution)/shard_map/ppermute | solution.py:142
  29.2 13.9 %collective-permute-start.15 = (bf16[256,512]{1,0:T(8,128)(2,1)}, bf16[256,512]{1,0:T(8,128)(2,1)}, u32[]{:S(2)}, u32[]{:S(2)}) collective-permute-start(bf16[256,512]{1,0:T(8,128)(2,1)} %collective-permute-done.11.refs_3_), channel_id=1, source_target_pairs={{4,0},{8,4},{12,8},{14,12},{10,14},{6,10},{2,6},{0,2},{5,1},{9,5},... | collective-permute-start | bytes 786440 | tf_op jit(solution)/shard_map/ppermute | solution.py:142
  29.7 18.8 %collective-permute-start.7 = (bf16[256,512]{1,0:T(8,128)(2,1)}, bf16[256,512]{1,0:T(8,128)(2,1)}, u32[]{:S(2)}, u32[]{:S(2)}) collective-permute-start(bf16[256,512]{1,0:T(8,128)(2,1)} %collective-permute-done.6.refs_0_), channel_id=1, source_target_pairs={{0,4},{4,8},{8,12},{12,14},{14,10},{10,6},{6,2},{2,0},{1,5},{5,9},... | collective-permute-start | bytes 786440 | tf_op jit(solution)/shard_map/ppermute | solution.py:142
  35.3 11.1 %collective-permute-start.13 = (bf16[256,512]{1,0:T(8,128)(2,1)}, bf16[256,512]{1,0:T(8,128)(2,1)}, u32[]{:S(2)}, u32[]{:S(2)}) collective-permute-start(bf16[256,512]{1,0:T(8,128)(2,1)} %collective-permute-done.9.refs_1_), channel_id=1, source_target_pairs={{0,4},{4,8},{8,12},{12,14},{14,10},{10,6},{6,2},{2,0},{1,5},{5,9},... | collective-permute-start | bytes 786440 | tf_op jit(solution)/shard_map/ppermute | solution.py:142
  36.9 9.6 %collective-permute-start.14 = (bf16[256,512]{1,0:T(8,128)(2,1)}, bf16[256,512]{1,0:T(8,128)(2,1)}, u32[]{:S(2)}, u32[]{:S(2)}) collective-permute-start(bf16[256,512]{1,0:T(8,128)(2,1)} %collective-permute-done.10.refs_2_), channel_id=1, source_target_pairs={{4,0},{8,4},{12,8},{14,12},{10,14},{6,10},{2,6},{0,2},{5,1},{9,5},... | collective-permute-start | bytes 786440 | tf_op jit(solution)/shard_map/ppermute | solution.py:142
  43.1 12.3 %collective-permute-start.19 = (bf16[256,512]{1,0:T(8,128)(2,1)}, bf16[256,512]{1,0:T(8,128)(2,1)}, u32[]{:S(2)}, u32[]{:S(2)}) collective-permute-start(bf16[256,512]{1,0:T(8,128)(2,1)} %collective-permute-done.15.refs_3_), channel_id=1, source_target_pairs={{4,0},{8,4},{12,8},{14,12},{10,14},{6,10},{2,6},{0,2},{5,1},{9,5},... | collective-permute-start | bytes 786440 | tf_op jit(solution)/shard_map/ppermute | solution.py:142
  46.4 11.1 %collective-permute-start.18 = (bf16[256,512]{1,0:T(8,128)(2,1)}, bf16[256,512]{1,0:T(8,128)(2,1)}, u32[]{:S(2)}, u32[]{:S(2)}) collective-permute-start(bf16[256,512]{1,0:T(8,128)(2,1)} %collective-permute-done.14.refs_2_), channel_id=1, source_target_pairs={{4,0},{8,4},{12,8},{14,12},{10,14},{6,10},{2,6},{0,2},{5,1},{9,5},... | collective-permute-start | bytes 786440 | tf_op jit(solution)/shard_map/ppermute | solution.py:142
  46.4 11.6 %collective-permute-start.17 = (bf16[256,512]{1,0:T(8,128)(2,1)}, bf16[256,512]{1,0:T(8,128)(2,1)}, u32[]{:S(2)}, u32[]{:S(2)}) collective-permute-start(bf16[256,512]{1,0:T(8,128)(2,1)} %collective-permute-done.13.refs_1_), channel_id=1, source_target_pairs={{0,4},{4,8},{8,12},{12,14},{14,10},{10,6},{6,2},{2,0},{1,5},{5,9},... | collective-permute-start | bytes 786440 | tf_op jit(solution)/shard_map/ppermute | solution.py:142
  48.4 11.8 %collective-permute-start.8 = (bf16[256,512]{1,0:T(8,128)(2,1)}, bf16[256,512]{1,0:T(8,128)(2,1)}, u32[]{:S(2)}, u32[]{:S(2)}) collective-permute-start(bf16[256,512]{1,0:T(8,128)(2,1)} %collective-permute-done.7.refs_0_), channel_id=1, source_target_pairs={{0,4},{4,8},{8,12},{12,14},{14,10},{10,6},{6,2},{2,0},{1,5},{5,9},... | collective-permute-start | bytes 786440 | tf_op jit(solution)/shard_map/ppermute | solution.py:142
  55.4 10.2 %collective-permute-start.27 = (bf16[256,512]{1,0:T(8,128)(2,1)}, bf16[256,512]{1,0:T(8,128)(2,1)}, u32[]{:S(2)}, u32[]{:S(2)}) collective-permute-start(bf16[256,512]{1,0:T(8,128)(2,1)} %collective-permute-done.19.refs_3_), channel_id=1, source_target_pairs={{4,0},{8,4},{12,8},{14,12},{10,14},{6,10},{2,6},{0,2},{5,1},{9,5},... | collective-permute-start | bytes 786440 | tf_op jit(solution)/shard_map/ppermute | solution.py:142
  57.5 13.2 %collective-permute-start.24 = (bf16[256,512]{1,0:T(8,128)(2,1)}, bf16[256,512]{1,0:T(8,128)(2,1)}, u32[]{:S(2)}, u32[]{:S(2)}) collective-permute-start(bf16[256,512]{1,0:T(8,128)(2,1)} %collective-permute-done.18.refs_2_), channel_id=1, source_target_pairs={{4,0},{8,4},{12,8},{14,12},{10,14},{6,10},{2,6},{0,2},{5,1},{9,5},... | collective-permute-start | bytes 786440 | tf_op jit(solution)/shard_map/ppermute | solution.py:142
  58.0 13.1 %collective-permute-start.21 = (bf16[256,512]{1,0:T(8,128)(2,1)}, bf16[256,512]{1,0:T(8,128)(2,1)}, u32[]{:S(2)}, u32[]{:S(2)}) collective-permute-start(bf16[256,512]{1,0:T(8,128)(2,1)} %collective-permute-done.17.refs_1_), channel_id=1, source_target_pairs={{0,4},{4,8},{8,12},{12,14},{14,10},{10,6},{6,2},{2,0},{1,5},{5,9},... | collective-permute-start | bytes 786440 | tf_op jit(solution)/shard_map/ppermute | solution.py:142
  60.2 12.5 %collective-permute-start.12 = (bf16[256,512]{1,0:T(8,128)(2,1)}, bf16[256,512]{1,0:T(8,128)(2,1)}, u32[]{:S(2)}, u32[]{:S(2)}) collective-permute-start(bf16[256,512]{1,0:T(8,128)(2,1)} %collective-permute-done.8.refs_0_), channel_id=1, source_target_pairs={{0,4},{4,8},{8,12},{12,14},{14,10},{10,6},{6,2},{2,0},{1,5},{5,9},... | collective-permute-start | bytes 786440 | tf_op jit(solution)/shard_map/ppermute | solution.py:142
  61.7 12.6 %copy-start.5 = (s32[4]{0:T(128)S(1)}, s32[4]{0:T(128)}, u32[]{:S(2)}) copy-start(s32[4]{0:T(128)} %param.13) | copy-start | bytes 52
  65.6 12.8 %collective-permute-start.28 = (bf16[256,512]{1,0:T(8,128)(2,1)}, bf16[256,512]{1,0:T(8,128)(2,1)}, u32[]{:S(2)}, u32[]{:S(2)}) collective-permute-start(bf16[256,512]{1,0:T(8,128)(2,1)} %collective-permute-done.27.refs_3_), channel_id=1, source_target_pairs={{4,0},{8,4},{12,8},{14,12},{10,14},{6,10},{2,6},{0,2},{5,1},{9,5},... | collective-permute-start | bytes 786440 | tf_op jit(solution)/shard_map/ppermute | solution.py:142
  70.7 11.2 %collective-permute-start.25 = (bf16[256,512]{1,0:T(8,128)(2,1)}, bf16[256,512]{1,0:T(8,128)(2,1)}, u32[]{:S(2)}, u32[]{:S(2)}) collective-permute-start(bf16[256,512]{1,0:T(8,128)(2,1)} %collective-permute-done.24.refs_2_), channel_id=1, source_target_pairs={{4,0},{8,4},{12,8},{14,12},{10,14},{6,10},{2,6},{0,2},{5,1},{9,5},... | collective-permute-start | bytes 786440 | tf_op jit(solution)/shard_map/ppermute | solution.py:142
  71.1 11.2 %collective-permute-start.22 = (bf16[256,512]{1,0:T(8,128)(2,1)}, bf16[256,512]{1,0:T(8,128)(2,1)}, u32[]{:S(2)}, u32[]{:S(2)}) collective-permute-start(bf16[256,512]{1,0:T(8,128)(2,1)} %collective-permute-done.21.refs_1_), channel_id=1, source_target_pairs={{0,4},{4,8},{8,12},{12,14},{14,10},{10,6},{6,2},{2,0},{1,5},{5,9},... | collective-permute-start | bytes 786440 | tf_op jit(solution)/shard_map/ppermute | solution.py:142
  72.7 11.2 %collective-permute-start.16 = (bf16[256,512]{1,0:T(8,128)(2,1)}, bf16[256,512]{1,0:T(8,128)(2,1)}, u32[]{:S(2)}, u32[]{:S(2)}) collective-permute-start(bf16[256,512]{1,0:T(8,128)(2,1)} %collective-permute-done.12.refs_0_), channel_id=1, source_target_pairs={{0,4},{4,8},{8,12},{12,14},{14,10},{10,6},{6,2},{2,0},{1,5},{5,9},... | collective-permute-start | bytes 786440 | tf_op jit(solution)/shard_map/ppermute | solution.py:142
  78.5 13.1 %collective-permute-start.29 = (bf16[256,512]{1,0:T(8,128)(2,1)}, bf16[256,512]{1,0:T(8,128)(2,1)S(1)}, u32[]{:S(2)}, u32[]{:S(2)}) collective-permute-start(bf16[256,512]{1,0:T(8,128)(2,1)} %collective-permute-done.28.refs_7_), channel_id=1, source_target_pairs={{4,0},{8,4},{12,8},{14,12},{10,14},{6,10},{2,6},{0,2},{5,1},{9,5},... | collective-permute-start | bytes 786440 | tf_op jit(solution)/shard_map/ppermute | solution.py:142
  81.9 9.7 %collective-permute-start.26 = (bf16[256,512]{1,0:T(8,128)(2,1)}, bf16[256,512]{1,0:T(8,128)(2,1)S(1)}, u32[]{:S(2)}, u32[]{:S(2)}) collective-permute-start(bf16[256,512]{1,0:T(8,128)(2,1)} %collective-permute-done.25.refs_6_), channel_id=1, source_target_pairs={{4,0},{8,4},{12,8},{14,12},{10,14},{6,10},{2,6},{0,2},{5,1},{9,5},... | collective-permute-start | bytes 786440 | tf_op jit(solution)/shard_map/ppermute | solution.py:142
  82.3 9.2 %collective-permute-start.23 = (bf16[256,512]{1,0:T(8,128)(2,1)}, bf16[256,512]{1,0:T(8,128)(2,1)S(1)}, u32[]{:S(2)}, u32[]{:S(2)}) collective-permute-start(bf16[256,512]{1,0:T(8,128)(2,1)} %collective-permute-done.22.refs_5_), channel_id=1, source_target_pairs={{0,4},{4,8},{8,12},{12,14},{14,10},{10,6},{6,2},{2,0},{1,5},{5,9},... | collective-permute-start | bytes 786440 | tf_op jit(solution)/shard_map/ppermute | solution.py:142
  83.9 9.0 %collective-permute-start.20 = (bf16[256,512]{1,0:T(8,128)(2,1)}, bf16[256,512]{1,0:T(8,128)(2,1)S(1)}, u32[]{:S(2)}, u32[]{:S(2)}) collective-permute-start(bf16[256,512]{1,0:T(8,128)(2,1)} %collective-permute-done.16.refs_4_), channel_id=1, source_target_pairs={{0,4},{4,8},{8,12},{12,14},{14,10},{10,6},{6,2},{2,0},{1,5},{5,9},... | collective-permute-start | bytes 786440 | tf_op jit(solution)/shard_map/ppermute | solution.py:142
  97.2 2.9 %collective-permute-start.30 = (bf16[1024,512]{1,0:T(8,128)(2,1)}, bf16[1024,512]{1,0:T(8,128)(2,1)S(1)}, u32[]{:S(2)}, u32[]{:S(2)}) collective-permute-start(bf16[1024,512]{1,0:T(8,128)(2,1)} %get-tuple-element.78.have_ref), channel_id=1, source_target_pairs={{0,1},{1,0},{2,3},{3,2},{4,5},{5,4},{6,7},{7,6},{8,9},{9,8},{10,11... | collective-permute-start | bytes 3145736 | tf_op jit(solution)/shard_map/ppermute | solution.py:261
  104.8 14.7 %all-to-all-start = ((f32[8,9,8,128]{3,2,1,0:T(8,128)}), f32[8,9,8,128]{3,2,1,0:T(8,128)S(1)}, u32[]{:S(2)}, u32[]{:S(2)}) async-start(f32[8,9,8,128]{3,2,1,0:T(8,128)} %shard_map.88), calls=%async_computation | async-start | bytes 589824 | tf_op jit(solution)/shard_map/all_to_all | solution.py:287
  119.8 3.8 %collective-permute-start.31 = (bf16[64,128]{1,0:T(8,128)(2,1)S(1)}, bf16[64,128]{1,0:T(8,128)(2,1)S(1)}, u32[]{:S(2)}, u32[]{:S(2)}) collective-permute-start(bf16[64,128]{1,0:T(8,128)(2,1)S(1)} %shard_map.89), channel_id=1, source_target_pairs={{0,2},{2,0},{4,6},{6,4},{8,10},{10,8},{12,14},{14,12},{1,3},{3,1},... | collective-permute-start | bytes 49160 | tf_op jit(solution)/shard_map/ppermute | solution.py:291
  123.7 5.8 %collective-permute-start.32 = (bf16[128,128]{1,0:T(8,128)(2,1)S(1)}, bf16[128,128]{1,0:T(8,128)(2,1)S(1)}, u32[]{:S(2)}, u32[]{:S(2)}) collective-permute-start(bf16[128,128]{1,0:T(8,128)(2,1)S(1)} %pad_maximum_fusion.2), channel_id=1, source_target_pairs={{0,12},{2,14},{4,8},{6,10},{8,4},{10,6},{12,0},{14,2},{1,13},{3,15... | collective-permute-start | bytes 98312 | tf_op jit(solution)/shard_map/ppermute | solution.py:294
  124.9 5.3 %collective-permute-start.33 = (bf16[128,128]{1,0:T(8,128)(2,1)S(1)}, bf16[128,128]{1,0:T(8,128)(2,1)S(1)}, u32[]{:S(2)}, u32[]{:S(2)}) collective-permute-start(bf16[128,128]{1,0:T(8,128)(2,1)S(1)} %pad_maximum_fusion.2), channel_id=1, source_target_pairs={{0,8},{2,10},{4,12},{6,14},{8,0},{10,2},{12,4},{14,6},{1,9},{3,11}... | collective-permute-start | bytes 98312 | tf_op jit(solution)/shard_map/ppermute | solution.py:294
  126.3 4.2 %collective-permute-start.34 = (bf16[128,128]{1,0:T(8,128)(2,1)S(1)}, bf16[128,128]{1,0:T(8,128)(2,1)S(1)}, u32[]{:S(2)}, u32[]{:S(2)}) collective-permute-start(bf16[128,128]{1,0:T(8,128)(2,1)S(1)} %pad_maximum_fusion.2), channel_id=1, source_target_pairs={{0,4},{2,6},{4,0},{6,2},{8,12},{10,14},{12,8},{14,10},{1,5},{3,7},... | collective-permute-start | bytes 98312 | tf_op jit(solution)/shard_map/ppermute | solution.py:294
  130.5 1.4 %collective-permute-start.35 = (bf16[16,1,32,128]{3,2,0,1:T(8,128)(2,1)S(1)}, bf16[16,1,32,128]{3,2,0,1:T(8,128)(2,1)S(1)}, u32[]{:S(2)}, u32[]{:S(2)}) collective-permute-start(bf16[16,1,32,128]{3,2,0,1:T(8,128)(2,1)S(1)} %bitcast.46), channel_id=1, source_target_pairs={{0,1},{1,0},{2,3},{3,2},{4,5},{5,4},{6,7},{7,6},{8,9},{9,8},{10,11... | collective-permute-start | bytes 393224 | tf_op jit(solution)/shard_map/ppermute | solution.py:304
